TPU v7x, 32 devices: a whole 2x2x4 slice. The times are simulated.
32 devices in a mesh: replica: 4 (over y, core), fsdp: 8 (over z, x).
Axes of the slice: x: 2, y: 2, z: 4, core: 2. Of those that a mesh axis runs over, the one named last changes fastest.
Arguments:
- layer_input: bfloat16 [4, 4096, 4096], P('replica', 'fsdp'), may hold values from -36 to 36, as said below
- norm_gain: bfloat16 [4, 4096], P('replica', 'fsdp'), may hold values from 0.099609375 to 1.8984375
- kv_weight: bfloat16 [4, 4096, 1024], P('replica', 'fsdp'), may hold values from -0.09375 to 0.09375
- kv_cotangent: bfloat16 [4, 4096, 1024], P('replica', 'fsdp'), may hold values from -6 to 6
- pseudo_grad: float32 [4, 3072, 1024], P('replica', 'fsdp'), may hold values from -6 to 6
- outer_momentum: float32 [3072, 1024], P('fsdp'), may hold values from -6 to 6
- global_params: float32 [3072, 1024], P('fsdp'), may hold values from -6 to 6
- local_params: bfloat16 [4, 3072, 1024], P('replica', 'fsdp'), may hold values from -6 to 6
Outputs:
- kv_out: bfloat16 [4, 4096, 1024], P('replica', 'fsdp')
- input_grad: bfloat16 [4, 4096, 4096], P('replica', 'fsdp')
- kv_weight_grad: float32 [4, 4096, 1024], P('replica', 'fsdp')
- gain_grad: float32 [4, 4096], P('replica', 'fsdp')
- momentum_new: float32 [3072, 1024], P('fsdp')
- global_new: float32 [3072, 1024], P('fsdp')
- local_new: bfloat16 [4, 3072, 1024], P('replica', 'fsdp')
Inputs may be any that keep to these rules, and one draw needn't show every extreme that they name: `layer_input`: activations of the residual stream.
All inputs are finite; a program needn't handle non-finite values.
Results may differ from a plain program's by a relative error of at most 0.0049.
Values may be sent and summed in bfloat16 or wider, within the bound.
No kernel may reach another device: no remote copies, remote signals or barrier semaphores. Data moves between devices by JAX's collectives and lax.ppermute only.
A program may use at most 128 MiB of HBM per device.

v0:
```python
import math

import jax
import jax.numpy as jnp
from jax import lax
from jax.sharding import PartitionSpec as P

HEAD = 128
SEQ_LEN = 4096


epsilon = 1e-05
rope_base = 500000.0
momentum_rate = 0.9
outer_rate = 0.7
mixing_rate = 0.5


def angles_for(positions, head):
    half = head // 2
    index_f = jnp.arange(half, dtype=jnp.float32)
    inverse = jnp.exp(index_f * (-2.0 * math.log(rope_base) / head))
    angle = positions.astype(jnp.float32)[:, None] * inverse[None, :]
    return (jnp.cos(angle), jnp.sin(angle))


def rotate_keys(keys, cosine, sine, head, sign):
    count = keys.shape[0]
    shaped = keys.reshape(count, -1, head)
    half = head // 2
    first = shaped[:, :, :half]
    second = shaped[:, :, half:]
    cos_b = cosine[:, None, :]
    sin_b = sine[:, None, :] * sign
    out = jnp.concatenate([first * cos_b - second * sin_b, second * cos_b + first * sin_b], axis=2)
    return out.reshape(count, -1)


def forward_piece(normed, weight_piece, gain_piece):
    gain_vals = gain_piece.astype(jnp.float32)
    hidden_piece = (normed * gain_vals[None, :]).astype(jnp.bfloat16)
    key_pre = jnp.dot(hidden_piece, weight_piece, preferred_element_type=jnp.float32)
    return (key_pre, hidden_piece, gain_vals)


def backward_piece(kv_grad, weight_piece):
    product = lax.dot_general(
        kv_grad, weight_piece, (((1,), (1,)), ((), ())), preferred_element_type=jnp.float32
    )
    return product


def local(
    layer_input,
    norm_gain,
    kv_weight,
    kv_cotangent,
    pseudo_grad,
    outer_momentum,
    global_params,
    local_params,
):
    tokens_in = layer_input[0]
    gain_shard = norm_gain[0]
    weight_shard = kv_weight[0]
    cotangent = kv_cotangent[0]
    rows, width = tokens_in.shape
    kvw = weight_shard.shape[1] // 2
    groups = lax.axis_size("fsdp")
    positions = (lax.axis_index("fsdp") * rows + jnp.arange(rows, dtype=jnp.int32)) % SEQ_LEN
    cosine, sine = angles_for(positions, HEAD)
    values = tokens_in.astype(jnp.float32)
    inv_rms = lax.rsqrt(jnp.mean(values * values, axis=-1, keepdims=True) + epsilon)
    normed = values * inv_rms
    key_back = rotate_keys(cotangent[:, :kvw].astype(jnp.float32), cosine, sine, HEAD, -1.0).astype(
        jnp.bfloat16
    )
    kv_grad = jnp.concatenate([key_back, cotangent[:, kvw:]], axis=1)
    key_pre, hidden, gain_full = forward_piece(
        normed,
        lax.all_gather(weight_shard, "fsdp", axis=0, tiled=True),
        lax.all_gather(gain_shard, "fsdp", axis=0, tiled=True),
    )
    hidden_grad = backward_piece(kv_grad, lax.all_gather(weight_shard, "fsdp", axis=0, tiled=True))
    kv_out = jnp.concatenate(
        [rotate_keys(key_pre[:, :kvw], cosine, sine, HEAD, 1.0), key_pre[:, kvw:]], axis=1
    ).astype(jnp.bfloat16)
    scale = 1.0 / math.sqrt(rows * groups)
    gain_product = hidden_grad * normed
    weight_term = (
        lax.dot_general(
            hidden, kv_grad, (((0,), (0,)), ((), ())), preferred_element_type=jnp.float32
        )
        * scale
    )
    gain_term = jnp.sum(gain_product, axis=0) * scale
    weight_grad, gain_grad = (
        lax.psum_scatter(weight_term, "fsdp", scatter_dimension=0, tiled=True),
        lax.psum_scatter(gain_term, "fsdp", scatter_dimension=0, tiled=True),
    )
    normed_grad = hidden_grad * gain_full
    input_grad = (
        inv_rms * (normed_grad - normed * jnp.mean(normed_grad * normed, axis=-1, keepdims=True))
    ).astype(jnp.bfloat16)
    pseudo = pseudo_grad[0]
    replicas = lax.axis_size("replica")
    total = lax.psum(pseudo, "replica")
    average = total / replicas
    momentum_new = momentum_rate * outer_momentum + average
    global_new = global_params - outer_rate * (average + momentum_rate * momentum_new)
    local_new = (
        mixing_rate * local_params[0].astype(jnp.float32) + (1.0 - mixing_rate) * global_new
    ).astype(jnp.bfloat16)
    return (
        kv_out[None],
        input_grad[None],
        weight_grad[None],
        gain_grad[None],
        momentum_new,
        global_new,
        local_new[None],
    )


def solution(mesh):
    in_specs = (
        P("replica", "fsdp", None),
        P("replica", "fsdp"),
        P("replica", "fsdp", None),
        P("replica", "fsdp", None),
        P("replica", "fsdp", None),
        P("fsdp", None),
        P("fsdp", None),
        P("replica", "fsdp", None),
    )
    out_specs = (
        P("replica", "fsdp", None),
        P("replica", "fsdp", None),
        P("replica", "fsdp", None),
        P("replica", "fsdp"),
        P("fsdp", None),
        P("fsdp", None),
        P("replica", "fsdp", None),
    )
    return jax.shard_map(local, mesh=mesh, in_specs=in_specs, out_specs=out_specs, check_vma=False)
```

profile of v0, /device:TPU:8, one launch (start us, length us, event | category | flops | bytes accessed | tf_op | source)
XLA Modules:
  0.0 447.5 jit_solution(2748918201171752788)
XLA Ops:
  8.0 0.0 copy-start.3
  8.0 0.0 all-gather.4.cloned.1.call-start
  8.1 0.7 all-gather.4.cloned.1.call-update
  8.7 0.0 all-reduce.3.cloned.1.call-start
  8.8 0.5 all-reduce.3.cloned.1.call-update
  9.3 0.0 reduce-scatter.2.cloned.1.call-start
  9.4 25.3 %all-gather = bf16[1,4096]{1,0:T(2,128)(2,1)S(1)} all-gather(bf16[1,512]{1,0:T(2,128)(2,1)} %param.9), channel_id=2, replica_groups=mesh['replica'=4,'fsdp'=8] {'fsdp'}, dimensions={1}, use_global_device_ids=true | all-gather | bytes 9216 | tf_op jit(solution)/shard_map/all_gather | solution.py:82
  34.8 3.1 fusion.10
  37.9 0.0 copy-done.3
  37.9 0.9 slice_convert_fusion.1
  38.8 0.4 reshape.172
  39.2 1.8 broadcast_multiply_fusion.1
  41.0 94.3 %all-gather.4.cloned.1.call-done = bf16[1,4096,1024]{2,1,0:T(8,128)(2,1)} async-done(((bf16[1,512,1024]{2,1,0:T(8,128)(2,1)}), bf16[1,4096,1024]{2,1,0:T(8,128)(2,1)}) %all-gather.4.cloned.1.call-update) | async-done | bytes 8388624 | tf_op jit(solution)/shard_map/all_gather | solution.py:81
  135.4 8.2 %fusion.13 = f32[512,1024]{1,0:T(8,128)S(1)} fusion(bf16[1,4096,1024]{2,1,0:T(8,128)(2,1)} %all-gather.4.cloned.1.call-done, bf16[1,512,4096]{2,1,0:T(8,128)(2,1)} %param.8, f32[4096]{0:T(1024)S(1)} %bitcast.40, f32[512]{0:T(512)S(1)} %add_rsqrt_fusion), kind=kOutput, calls=%fused_computation.15 | convolution fusion | flops 4303355904 | bytes 14698496 | tf_op jit(solution)/shard_map/dot_general | solution.py:42
  143.6 0.0 copy-start.2
  143.6 1.3 copy-done.2
  144.9 0.1 slice.33
  145.0 0.4 reshape.167
  145.4 0.0 copy-start
  145.4 0.0 copy-start.5
  145.4 2.7 subtract_convert_fusion
  148.2 1.4 pad_maximum_fusion.4
  149.6 0.1 copy.17
  149.7 0.0 copy-start.7
  149.7 0.0 copy-done
  149.7 0.0 copy-done.5
  149.7 8.3 %broadcast_multiply_fusion = f32[4096,1024]{1,0:T(8,128)} fusion(bf16[1,512,4096]{2,1,0:T(8,128)(2,1)S(1)} %copy-done, f32[4096]{0:T(1024)S(1)} %bitcast.41, f32[512]{0:T(512)S(1)} %add_rsqrt_fusion, bf16[512,512]{1,0:T(8,128)(2,1)S(1)} %copy-done.5, bf16[512,512]{1,0:T(8,128)(2,1)S(1)} %bitcast.38), kind=kOutput, calls=%fused_computation.17 | convolution fusion | flops 4309647360 | bytes 22038528 | tf_op jit(solution)/shard_map/dot_general | solution.py:91
  158.0 0.0 copy-done.7
  158.0 0.0 copy-start.8
  158.0 0.0 copy-start.1
  158.0 0.0 copy-start.4
  158.0 0.0 reduce-scatter.2.cloned.1.call-update
  158.0 0.6 copy-done.8
  158.6 0.6 dynamic-slice
  159.9 0.0 copy-start.6
  159.9 0.0 all-reduce.3.cloned.1.call-done
  159.9 0.0 copy-done.1
  159.9 0.0 copy-done.4
  159.9 4.6 %fusion.20 = (bf16[1,384,1024]{2,1,0:T(8,128)(2,1)}, f32[384,1024]{1,0:T(8,128)}, f32[384,1024]{1,0:T(8,128)}) fusion(bf16[1,384,1024]{2,1,0:T(8,128)(2,1)S(1)} %copy-done.4, f32[384,1024]{1,0:T(8,128)S(1)} %copy-done.1, f32[384,1024]{1,0:T(8,128)} %all-reduce.3.cloned.1.call-done, f32[384,1024]{1,0:T(8,128)} %param.13), kind=kLoop, calls=%fused_computation.31 | loop fusion | flops 4325376 | bytes 9437184 | tf_op jit(solution)/shard_map/broadcast_in_dim | solution.py:121
  164.6 0.2 concatenate.27
  164.8 0.0 copy-done.6
  164.8 13.9 %fusion.9 = (f32[4096]{0:T(1024)S(1)}, f32[512]{0:T(512)S(1)}, f32[512,4096]{1,0:T(8,128)}) fusion(bf16[1,512,4096]{2,1,0:T(8,128)(2,1)} %param.8, f32[512]{0:T(512)S(1)} %add_rsqrt_fusion, f32[4096]{0:T(1024)S(1)} %bitcast.42, bf16[1,4096,1024]{2,1,0:T(8,128)(2,1)} %all-gather.4.cloned.1.call-done, bf16[512,512]{1,0:T(8,128)(2,1)S(1)} %copy-done.6, ...), kind=kOutput, calls=%fused_computation.11 | convolution fusion | flops 4311739904 | bytes 22056960 | tf_op jit(solution)/shard_map/dot_general | solution.py:47
  178.6 35.2 %all-reduce = f32[4096]{0:T(1024)S(1)} all-reduce(f32[4096]{0:T(1024)S(1)} %broadcast_multiply_fusion.2), channel_id=5, replica_groups=mesh['replica'=4,'fsdp'=8] {'fsdp'}, use_global_device_ids=true, to_apply=%region_4.5.clone | all-reduce | flops 4096 | bytes 32768
  213.8 0.7 dynamic-slice.1
  214.5 1.3 fusion.21
  215.8 1.1 pad_maximum_fusion
  216.9 7.3 %fusion.15 = bf16[1,512,4096]{2,1,0:T(8,128)(2,1)} fusion(f32[512,4096]{1,0:T(8,128)} %get-tuple-element.23, bf16[1,512,4096]{2,1,0:T(8,128)(2,1)} %param.8, f32[512]{0:T(512)S(1)} %broadcast_multiply_fusion.3, f32[4096]{0:T(1024)S(1)} %bitcast.43, f32[512]{0:T(512)S(1)} %add_rsqrt_fusion), kind=kLoop, calls=%fused_computation.18 | loop fusion | flops 14680064 | bytes 16797696 | tf_op jit(solution)/shard_map/broadcast_in_dim | solution.py:116
  224.2 215.8 %reduce-scatter.2.cloned.1.call-done = f32[512,1024]{1,0:T(8,128)} async-done(((f32[4096,1024]{1,0:T(8,128)}), f32[512,1024]{1,0:T(8,128)}) %reduce-scatter.2.cloned.1.call-update) | async-done | bytes 2097168 | tf_op jit(solution)/shard_map/reduce_scatter | solution.py:98
  (6 shorter events, 0.1 us)
Async XLA Ops:
  8.0 29.9 %copy-start.3 = (bf16[1,512,1024]{2,1,0:T(8,128)(2,1)S(1)}, bf16[1,512,1024]{2,1,0:T(8,128)(2,1)}, u32[]{:S(2)}) copy-start(bf16[1,512,1024]{2,1,0:T(8,128)(2,1)} %param.11) | copy-start | bytes 3145732
  8.0 127.4 %all-gather.4.cloned.1.call-start = ((), (), s32[]{:S(2)}) async-start(), calls=%async_computation.3 | async-start | bytes 9437184 | tf_op jit(solution)/shard_map/all_gather | solution.py:81
  8.7 151.2 %all-reduce.3.cloned.1.call-start = ((), (), s32[]{:S(2)}) async-start(), calls=%async_computation.2 | async-start | bytes 3145728 | tf_op jit(solution)/shard_map/psum | solution.py:107
  9.3 430.8 %reduce-scatter.2.cloned.1.call-start = ((), (), s32[]{:S(2)}) async-start(), calls=%async_computation.1 | async-start | bytes 18874368 | tf_op jit(solution)/shard_map/reduce_scatter | solution.py:98
  143.6 1.3 copy-start.2
  145.4 4.3 copy-start
  145.4 4.3 copy-start.5
  149.7 8.3 %copy-start.7 = (bf16[64,8,4,128]{3,1,2,0:T(8,128)(2,1)}, bf16[64,8,4,128]{3,1,2,0:T(8,128)(2,1)S(1)}, u32[]{:S(2)}) copy-start(bf16[64,8,4,128]{3,1,2,0:T(8,128)(2,1)S(1)} %copy.17) | copy-start | bytes 1572868
  158.0 0.7 copy-start.8
  158.0 1.9 copy-start.1
  158.0 1.9 copy-start.4
  159.9 4.9 %copy-start.6 = (bf16[512,512]{1,0:T(8,128)(2,1)S(1)}, bf16[512,512]{1,0:T(8,128)(2,1)}, u32[]{:S(2)}) copy-start(bf16[512,512]{1,0:T(8,128)(2,1)} %get-tuple-element.17) | copy-start | bytes 1572868
Sparse Core Ops, SparseCore 0:
  11.0 124.3 all-gather.3
  158.1 281.8 reduce-scatter.1
Sparse Core Ops, SparseCore 1:
  11.7 43.8 all-reduce.2
where the time goes:
time: 451 us; the launch traced here: 448 us
  waiting for transfers between devices  311 us (69%)
  blocking collectives  60.5 us (13%)
  matrix products  30.4 us (7%)
  other arithmetic  23.1 us (5%)
  between operations  16.3 us (4%)
  local copies, waits for them, and re-layouts  5.6 us (1%)
    reduce_scatter x1, waiting for transfers between devices, local(): lax.psum_scatter(weight_term, 'fsdp', scatter_dimension=0, tiled=True)  216 us
    all_gather x1, waiting for transfers between devices, local(): lax.all_gather(weight_shard, 'fsdp', axis=0, tiled=True)  94.3 us
    unnamed x1, blocking collectives  35.2 us
    all_gather x1, blocking collectives, local(): lax.all_gather(gain_shard, 'fsdp', axis=0, tiled=True)  25.3 us
    dot_general x1, matrix products, backward_piece(): lax.dot_general(kv_grad, weight_piece, (((1,), (1,)), ((), ())), preferre...  13.9 us
  transfers between devices with their start and end apart: 3, of which 2 were waited for; matrix products, arithmetic and copies ran while one was open for 13% of the time, Pallas kernels for 0%

commit v1 on v0

--- a/solution.py
+++ b/solution.py
@@ -36,18 +36,127 @@
     return out.reshape(count, -1)
 
 
-def forward_piece(normed, weight_piece, gain_piece):
-    gain_vals = gain_piece.astype(jnp.float32)
-    hidden_piece = (normed * gain_vals[None, :]).astype(jnp.bfloat16)
-    key_pre = jnp.dot(hidden_piece, weight_piece, preferred_element_type=jnp.float32)
-    return (key_pre, hidden_piece, gain_vals)
-
-
-def backward_piece(kv_grad, weight_piece):
-    product = lax.dot_general(
-        kv_grad, weight_piece, (((1,), (1,)), ((), ())), preferred_element_type=jnp.float32
-    )
-    return product
+class Grid:
+    def __init__(self):
+        self.groups = lax.axis_size("fsdp")
+        self.line = self.groups // 2
+        self.me = lax.axis_index("fsdp")
+        self.place = self.me // 2
+        self.side = self.me % 2
+
+    def send(self, value, step, keep):
+        pairs = [
+            (i, i ^ 1 if step == 0 else i + 2 * step) for i in range(self.groups) if keep(i // 2)
+        ]
+        return lax.ppermute(value, "fsdp", pairs)
+
+    def flip(self, value, keep=lambda p: True):
+        return self.send(value, 0, keep)
+
+    def block(self, distance):
+        return (self.place + distance) % self.line
+
+
+def gather_rows(grid, piece):
+    n = grid.groups
+    around = [piece] + [
+        lax.ppermute(piece, "fsdp", [(i, (i - m) % n) for i in range(n)]) for m in range(1, n)
+    ]
+    twice = jnp.stack(around + around)
+    return lax.dynamic_slice_in_dim(twice, (n - grid.me) % n, n, 0).reshape(-1)
+
+
+def scatter_rows(grid, term):
+    n = grid.groups
+    pieces = term.reshape(n, -1)
+    around = lax.dynamic_slice_in_dim(jnp.concatenate([pieces, pieces]), grid.me, n, 0)
+    total = around[0]
+    for m in range(1, n):
+        total = total + lax.ppermute(around[m], "fsdp", [(i, (i + m) % n) for i in range(n)])
+    return total
+
+
+def gather_line(grid, block):
+    last = grid.line - 1
+    up, down = [block], [block]
+    for s in range(1, grid.line):
+        up.append(grid.send(up[-1], 1, lambda p: s - 1 <= p < last))
+        down.append(grid.send(down[-1], -1, lambda p: 1 <= p <= grid.line - s))
+    return up, down
+
+
+def by_distance(grid, up, down):
+    out = [up[0]]
+    for r in range(1, grid.line):
+        out.append(jnp.where(grid.place + r < grid.line, down[r], up[grid.line - r]))
+    return out
+
+
+def gather_weight(grid, weight, split):
+    shard, cols = weight.shape
+    part_a, part_b = weight[:, :split], weight[:, split:]
+    last = grid.line - 1
+    other_b = grid.flip(part_b)
+    up_a, down_a = gather_line(grid, part_a)
+    pair_b = jnp.concatenate(
+        [
+            jnp.where(grid.side == 0, part_b, other_b),
+            jnp.where(grid.side == 0, other_b, part_b),
+        ],
+        axis=0,
+    )
+    up_b, down_b = gather_line(grid, pair_b)
+    own = grid.flip(part_a)
+    up_x, down_x = [own], [own]
+    for s in range(1, grid.line):
+        up_x.append(grid.flip(up_a[s], lambda p: p >= s))
+        down_x.append(grid.flip(down_a[s], lambda p: p <= last - s))
+    near = by_distance(grid, up_a, down_a)
+    far = by_distance(grid, up_x, down_x)
+    both = by_distance(grid, up_b, down_b)
+    whole = jnp.zeros((grid.groups * shard, cols), weight.dtype)
+    for r in range(grid.line):
+        base = grid.block(r) * 2 * shard
+        whole = lax.dynamic_update_slice(whole, near[r], (base + grid.side * shard, 0))
+        whole = lax.dynamic_update_slice(whole, far[r], (base + (1 - grid.side) * shard, 0))
+        whole = lax.dynamic_update_slice(whole, both[r], (base, split))
+    return whole
+
+
+def scatter_line(grid, terms):
+    half = jnp.bfloat16
+    up = down = None
+    for s in range(grid.line - 1, 0, -1):
+        mine_up, mine_down = terms(s), terms(grid.line - s)
+        if up is not None:
+            mine_up = mine_up + up.astype(jnp.float32)
+            mine_down = mine_down + down.astype(jnp.float32)
+        up = grid.send(mine_up.astype(half), 1, lambda p: p + s < grid.line)
+        down = grid.send(mine_down.astype(half), -1, lambda p: p >= s)
+    return terms(0) + up.astype(jnp.float32) + down.astype(jnp.float32)
+
+
+def scatter_weight(grid, term, shard, split):
+    cols = term.shape[1]
+
+    def cut(r, side, first, last, count):
+        start = grid.block(r) * 2 * shard + side * shard
+        return lax.dynamic_slice(term, (start, first), (count * shard, last - first))
+
+    order = []
+    for s in range(grid.line - 1, 0, -1):
+        order += [r for r in (s, grid.line - s) if r not in order]
+    order.append(0)
+    paired = {}
+    for r in order:
+        theirs = cut(r, 1 - grid.side, 0, split, 1).astype(jnp.bfloat16)
+        paired[r] = cut(r, grid.side, 0, split, 1) + grid.flip(theirs).astype(jnp.float32)
+    grad_a = scatter_line(grid, lambda r: paired[r])
+    pair_b = scatter_line(grid, lambda r: cut(r, 0, split, cols, 2))
+    mine = lax.dynamic_slice(pair_b, (grid.side * shard, 0), (shard, cols - split))
+    theirs = lax.dynamic_slice(pair_b, ((1 - grid.side) * shard, 0), (shard, cols - split))
+    grad_b = mine + grid.flip(theirs.astype(jnp.bfloat16)).astype(jnp.float32)
+    return jnp.concatenate([grad_a, grad_b], axis=1)
 
 
 def local(
@@ -60,52 +169,55 @@
     global_params,
     local_params,
 ):
+    grid = Grid()
     tokens_in = layer_input[0]
     gain_shard = norm_gain[0]
     weight_shard = kv_weight[0]
     cotangent = kv_cotangent[0]
     rows, width = tokens_in.shape
-    kvw = weight_shard.shape[1] // 2
-    groups = lax.axis_size("fsdp")
-    positions = (lax.axis_index("fsdp") * rows + jnp.arange(rows, dtype=jnp.int32)) % SEQ_LEN
+    shard, cols = weight_shard.shape
+    kvw = cols // 2
+    split = cols * 5 // 8
+    weight = gather_weight(grid, weight_shard, split)
+    gain_full = gather_rows(grid, gain_shard).astype(jnp.float32)
+
+    positions = (grid.me * rows + jnp.arange(rows, dtype=jnp.int32)) % SEQ_LEN
     cosine, sine = angles_for(positions, HEAD)
     values = tokens_in.astype(jnp.float32)
     inv_rms = lax.rsqrt(jnp.mean(values * values, axis=-1, keepdims=True) + epsilon)
     normed = values * inv_rms
+    hidden = (normed * gain_full[None, :]).astype(jnp.bfloat16)
     key_back = rotate_keys(cotangent[:, :kvw].astype(jnp.float32), cosine, sine, HEAD, -1.0).astype(
         jnp.bfloat16
     )
     kv_grad = jnp.concatenate([key_back, cotangent[:, kvw:]], axis=1)
-    key_pre, hidden, gain_full = forward_piece(
-        normed,
-        lax.all_gather(weight_shard, "fsdp", axis=0, tiled=True),
-        lax.all_gather(gain_shard, "fsdp", axis=0, tiled=True),
-    )
-    hidden_grad = backward_piece(kv_grad, lax.all_gather(weight_shard, "fsdp", axis=0, tiled=True))
-    kv_out = jnp.concatenate(
-        [rotate_keys(key_pre[:, :kvw], cosine, sine, HEAD, 1.0), key_pre[:, kvw:]], axis=1
-    ).astype(jnp.bfloat16)
-    scale = 1.0 / math.sqrt(rows * groups)
-    gain_product = hidden_grad * normed
+    scale = 1.0 / math.sqrt(rows * grid.groups)
     weight_term = (
         lax.dot_general(
             hidden, kv_grad, (((0,), (0,)), ((), ())), preferred_element_type=jnp.float32
         )
         * scale
     )
+    weight_grad = scatter_weight(grid, weight_term, shard, split)
+
+    key_pre = jnp.dot(hidden, weight, preferred_element_type=jnp.float32)
+    kv_out = jnp.concatenate(
+        [rotate_keys(key_pre[:, :kvw], cosine, sine, HEAD, 1.0), key_pre[:, kvw:]], axis=1
+    ).astype(jnp.bfloat16)
+    hidden_grad = lax.dot_general(
+        kv_grad, weight, (((1,), (1,)), ((), ())), preferred_element_type=jnp.float32
+    )
+    gain_product = hidden_grad * normed
     gain_term = jnp.sum(gain_product, axis=0) * scale
-    weight_grad, gain_grad = (
-        lax.psum_scatter(weight_term, "fsdp", scatter_dimension=0, tiled=True),
-        lax.psum_scatter(gain_term, "fsdp", scatter_dimension=0, tiled=True),
-    )
+    gain_grad = scatter_rows(grid, gain_term)
     normed_grad = hidden_grad * gain_full
     input_grad = (
         inv_rms * (normed_grad - normed * jnp.mean(normed_grad * normed, axis=-1, keepdims=True))
     ).astype(jnp.bfloat16)
+
     pseudo = pseudo_grad[0]
     replicas = lax.axis_size("replica")
-    total = lax.psum(pseudo, "replica")
-    average = total / replicas
+    average = lax.psum(pseudo, "replica") / replicas
     momentum_new = momentum_rate * outer_momentum + average
     global_new = global_params - outer_rate * (average + momentum_rate * momentum_new)
     local_new = (

time: 451 us -> 382 us (0.85)
  waiting for transfers between devices: 311 us -> 116 us
  starting transfers between devices: 0.12 us -> 132 us
  blocking collectives: 60.5 us -> 0 us
  other arithmetic: 23.1 us -> 61.9 us
  local copies, waits for them, and re-layouts: 5.6 us -> 28.2 us
  matrix products: 30.4 us -> 23.4 us
    reduce_scatter x1 -> x0, waiting for transfers between devices: 216 us -> none  [local(): lax.psum_scatter(weight_term, 'fsdp', scatter_dimension=0, tiled=True)]
    ppermute x0 -> x51, starting transfers between devices: none -> 132 us  [the longest x37 80.6 us: send(): return lax.ppermute(value, 'fsdp', pairs)]
    all_gather x1 -> x0, waiting for transfers between devices: 94.3 us -> none  [local(): lax.all_gather(weight_shard, 'fsdp', axis=0, tiled=True)]
    ppermute x0 -> x51, waiting for transfers between devices: none -> 93.3 us  [the longest x37 55.7 us: send(): return lax.ppermute(value, 'fsdp', pairs)]
    unnamed x1 -> x0, blocking collectives: 35.2 us -> none
    all_gather x1 -> x0, blocking collectives: 25.3 us -> none  [local(): lax.all_gather(gain_shard, 'fsdp', axis=0, tiled=True)]
    psum x1, waiting for transfers between devices: 0.03 us -> 22.3 us  [local(): average = lax.psum(pseudo, 'replica') / replicas]
    convert_element_type x1 -> x8, other arithmetic: 0.02 us -> 19.1 us  [the longest x5 13.3 us: scatter_line(): up = grid.send(mine_up.astype(half), 1, lambda p: p + s < grid.line)]
  transfers between devices with their start and end apart: 3 -> 52, of which waited for: 2 -> 18; matrix products, arithmetic and copies ran while one was open for 13% -> 21% of each run, Pallas kernels for 0% -> 0%
where the time goes in v1:
time: 382 us; the launch traced here: 376 us
  starting transfers between devices  132 us (35%)
  waiting for transfers between devices  116 us (30%)
  other arithmetic  61.9 us (16%)
  local copies, waits for them, and re-layouts  28.2 us (7%)
  matrix products  23.4 us (6%)
  between operations  14.9 us (4%)
    ppermute x37, starting transfers between devices, send(): return lax.ppermute(value, 'fsdp', pairs)  80.6 us
    ppermute x37, waiting for transfers between devices, send(): return lax.ppermute(value, 'fsdp', pairs)  55.7 us
    ppermute x7, starting transfers between devices, scatter_rows(): lax.ppermute(around[m], 'fsdp', [(i, (i + m) % n) for i in range(n)])  29.3 us
    ppermute x7, waiting for transfers between devices, gather_rows(): lax.ppermute(piece, 'fsdp', [(i, (i - m) % n) for i in range(n)])  28.7 us
    psum x1, waiting for transfers between devices, local(): average = lax.psum(pseudo, 'replica') / replicas  22.3 us
    ppermute x7, starting transfers between devices, gather_rows(): lax.ppermute(piece, 'fsdp', [(i, (i - m) % n) for i in range(n)])  22.2 us
    convert_element_type x5, other arithmetic, scatter_line(): up = grid.send(mine_up.astype(half), 1, lambda p: p + s < grid.line)  13.3 us
    dot_general x1, matrix products, local(): lax.dot_general(kv_grad, weight, (((1,), (1,)), ((), ())), preferred_elem...  11.6 us
  transfers between devices with their start and end apart: 52, of which 18 were waited for; matrix products, arithmetic and copies ran while one was open for 21% of the time, Pallas kernels for 0%

profile of v1, /device:TPU:8, one launch (start us, length us, event | category | flops | bytes accessed | tf_op | source)
XLA Modules:
  0.0 376.2 jit_solution(4728979881289830508)
XLA Ops:
  9.8 4.3 %broadcast_in_dim.10 = bf16[4096,1024]{1,0:T(8,128)(2,1)} broadcast(bf16[]{:T(256)} %constant.127.clone.1), dimensions={} | broadcast | bytes 8388610 | tf_op jit(solution)/shard_map/broadcast_in_dim | solution.py:117
  15.9 3.5 collective-permute-start.10
  20.4 12.8 %collective-permute-done.7 = bf16[512,640]{1,0:T(8,128)(2,1)S(1)} collective-permute-done((bf16[512,640]{1,0:T(8,128)(2,1)}, bf16[512,640]{1,0:T(8,128)(2,1)S(1)}, u32[]{:S(2)}, u32[]{:S(2)}) %collective-permute-start.7) | collective-permute-done | bytes 655392 | tf_op jit(solution)/shard_map/ppermute | solution.py:51
  35.3 3.5 collective-permute-start.16
  38.8 4.2 %collective-permute-start.11 = (bf16[512,640]{1,0:T(8,128)(2,1)S(1)}, bf16[512,640]{1,0:T(8,128)(2,1)}, u32[]{:S(2)}, u32[]{:S(2)}) collective-permute-start(bf16[512,640]{1,0:T(8,128)(2,1)S(1)} %collective-permute-done.10), channel_id=1, source_target_pairs={{2,4},{3,5},{4,6},{5,7},{10,12},{11,13},{12,14},{13,15},{18,20},{1... | collective-permute-start | bytes 1966088 | tf_op jit(solution)/shard_map/ppermute | solution.py:51
  45.5 3.9 %collective-permute-start.1 = (bf16[512]{0:T(512)(128)(2,1)}, bf16[512]{0:T(512)(128)(2,1)S(1)}, u32[]{:S(2)}, u32[]{:S(2)}) collective-permute-start(bf16[512]{0:T(512)(128)(2,1)} %reduce), channel_id=1, source_target_pairs={{0,6},{1,7},{2,0},{3,1},{4,2},{5,3},{6,4},{7,5},{8,14},{9,15},{10,... | collective-permute-start | bytes 3080 | tf_op jit(solution)/shard_map/ppermute | solution.py:63
  49.4 8.7 %collective-permute-done = bf16[512]{0:T(512)(128)(2,1)S(1)} collective-permute-done((bf16[512]{0:T(512)(128)(2,1)}, bf16[512]{0:T(512)(128)(2,1)S(1)}, u32[]{:S(2)}, u32[]{:S(2)}) %collective-permute-start) | collective-permute-done | bytes 1056 | tf_op jit(solution)/shard_map/ppermute | solution.py:63
  60.3 3.7 collective-permute-start.3
  64.0 4.9 %collective-permute-done.2 = bf16[512]{0:T(512)(128)(2,1)S(1)} collective-permute-done((bf16[512]{0:T(512)(128)(2,1)}, bf16[512]{0:T(512)(128)(2,1)S(1)}, u32[]{:S(2)}, u32[]{:S(2)}) %collective-permute-start.2) | collective-permute-done | bytes 1056 | tf_op jit(solution)/shard_map/ppermute | solution.py:63
  72.4 6.1 %collective-permute-start.17 = (bf16[1024,384]{1,0:T(8,128)(2,1)}, bf16[1024,384]{1,0:T(8,128)(2,1)}, u32[]{:S(2)}, u32[]{:S(2)}) collective-permute-start(bf16[1024,384]{1,0:T(8,128)(2,1)} %collective-permute-done.16), channel_id=1, source_target_pairs={{2,4},{3,5},{4,6},{5,7},{10,12},{11,13},{12,14},{13,15},{18,20},{1... | collective-permute-start | bytes 2359304 | tf_op jit(solution)/shard_map/ppermute | solution.py:51
  78.4 3.1 fusion.10
  84.7 7.9 %collective-permute-done.4 = bf16[512]{0:T(512)(128)(2,1)} collective-permute-done((bf16[512]{0:T(512)(128)(2,1)}, bf16[512]{0:T(512)(128)(2,1)}, u32[]{:S(2)}, u32[]{:S(2)}) %collective-permute-start.4) | collective-permute-done | bytes 1056 | tf_op jit(solution)/shard_map/ppermute | solution.py:63
  92.6 11.6 %collective-permute-start.5 = (bf16[512]{0:T(512)(128)(2,1)}, bf16[512]{0:T(512)(128)(2,1)S(1)}, u32[]{:S(2)}, u32[]{:S(2)}) collective-permute-start(bf16[512]{0:T(512)(128)(2,1)} %reduce), channel_id=1, source_target_pairs={{0,2},{1,3},{2,4},{3,5},{4,6},{5,7},{6,0},{7,1},{8,10},{9,11},{10,... | collective-permute-start | bytes 3080 | tf_op jit(solution)/shard_map/ppermute | solution.py:63
  106.2 5.8 %collective-permute-done.6 = bf16[512]{0:T(512)(128)(2,1)S(1)} collective-permute-done((bf16[512]{0:T(512)(128)(2,1)}, bf16[512]{0:T(512)(128)(2,1)S(1)}, u32[]{:S(2)}, u32[]{:S(2)}) %collective-permute-start.6) | collective-permute-done | bytes 1056 | tf_op jit(solution)/shard_map/ppermute | solution.py:63
  117.6 4.5 %collective-permute-start.22 = (bf16[1024,384]{1,0:T(8,128)(2,1)}, bf16[1024,384]{1,0:T(8,128)(2,1)S(1)}, u32[]{:S(2)}, u32[]{:S(2)}) collective-permute-start(bf16[1024,384]{1,0:T(8,128)(2,1)} %collective-permute-done.15), channel_id=1, source_target_pairs={{2,0},{3,1},{4,2},{5,3},{10,8},{11,9},{12,10},{13,11},{18,16},{19,... | collective-permute-start | bytes 2359304 | tf_op jit(solution)/shard_map/ppermute | solution.py:51
  129.9 3.4 collective-permute-start.20
  136.2 12.3 %collective-permute-done.23 = bf16[512,640]{1,0:T(8,128)(2,1)S(1)} collective-permute-done((bf16[512,640]{1,0:T(8,128)(2,1)}, bf16[512,640]{1,0:T(8,128)(2,1)S(1)}, u32[]{:S(2)}, u32[]{:S(2)}) %collective-permute-start.23) | collective-permute-done | bytes 655392 | tf_op jit(solution)/shard_map/ppermute | solution.py:51
  148.5 3.3 collective-permute-start.25
  152.5 4.5 %collective-permute-start.26 = (bf16[1024,384]{1,0:T(8,128)(2,1)S(1)}, bf16[1024,384]{1,0:T(8,128)(2,1)S(1)}, u32[]{:S(2)}, u32[]{:S(2)}) collective-permute-start(bf16[1024,384]{1,0:T(8,128)(2,1)S(1)} %collective-permute-done.22), channel_id=1, source_target_pairs={{2,0},{3,1},{10,8},{11,9},{18,16},{19,17},{26,24},{27,25}} | collective-permute-start | bytes 2359304 | tf_op jit(solution)/shard_map/ppermute | solution.py:51
  157.0 2.3 select_dynamic-update-slice_fusion.2
  167.5 2.2 select_dynamic-update-slice_fusion
  169.7 7.0 %fusion.15 = f32[512,1024]{1,0:T(8,128)S(1)} fusion(bf16[4096,1024]{1,0:T(8,128)(2,1)} %select_dynamic-update-slice_fusion, bf16[1,512,4096]{2,1,0:T(8,128)(2,1)S(1)} %copy-done.1, f32[4096]{0:T(1024)S(1)} %bitcast.49, f32[512]{0:T(512)S(1)} %add_rsqrt_fusion), kind=kOutput, calls=%fused_computation.40 | convolution fusion | flops 4303355904 | bytes 14698496 | tf_op jit(solution)/shard_map/dot_general | solution.py:203
  178.5 2.7 subtract_convert_fusion
  182.8 4.7 %broadcast_multiply_fusion = f32[4096,1024]{0,1:T(8,128)S(1)} fusion(bf16[1,512,4096]{2,1,0:T(8,128)(2,1)S(1)} %copy-done.2, f32[4096]{0:T(1024)S(1)} %bitcast.50, f32[512]{0:T(512)S(1)} %add_rsqrt_fusion, bf16[512,512]{1,0:T(8,128)(2,1)S(1)} %copy-done.12, bf16[512,512]{1,0:T(8,128)(2,1)S(1)} %bitcast.47), kind=kOutput, calls=%fused_computation.13 | convolution fusion | flops 4309647360 | bytes 22038528 | tf_op jit(solution)/shard_map/dot_general | solution.py:196
  187.6 5.8 %copy-done = f32[4096,1024]{0,1:T(8,128)} copy-done((f32[4096,1024]{0,1:T(8,128)}, f32[4096,1024]{0,1:T(8,128)S(1)}, u32[]{:S(2)}) %copy-start) | copy-done | bytes 16777240
  195.8 3.3 dynamic-slice_convert_fusion
  202.0 9.8 %collective-permute-done.30 = bf16[512,640]{0,1:T(8,128)(2,1)S(1)} collective-permute-done((bf16[512,640]{0,1:T(8,128)(2,1)}, bf16[512,640]{0,1:T(8,128)(2,1)S(1)}, u32[]{:S(2)}, u32[]{:S(2)}) %collective-permute-start.30) | collective-permute-done | bytes 655392 | tf_op jit(solution)/shard_map/ppermute | solution.py:51
  211.8 2.4 fusion.18
  215.4 22.3 %all-reduce.2.cloned.1.call-done = f32[384,1024]{1,0:T(8,128)} async-done(((f32[384,1024]{1,0:T(8,128)}), f32[384,1024]{1,0:T(8,128)}) %all-reduce.2.cloned.1.call-update) | async-done | bytes 1572880 | tf_op jit(solution)/shard_map/psum | solution.py:220
  237.8 4.8 %fusion.19 = (bf16[1,384,1024]{2,1,0:T(8,128)(2,1)}, f32[384,1024]{1,0:T(8,128)}, f32[384,1024]{1,0:T(8,128)}) fusion(bf16[1,384,1024]{2,1,0:T(8,128)(2,1)} %param.15, f32[384,1024]{1,0:T(8,128)S(1)} %copy-done.7, f32[384,1024]{1,0:T(8,128)} %all-reduce.2.cloned.1.call-done, f32[384,1024]{1,0:T(8,128)} %param.13), kind=kLoop, calls=%fused_computation.50 | loop fusion | flops 4325376 | bytes 9437184 | tf_op jit(solution)/shard_map/broadcast_in_dim | solution.py:233
  245.0 2.8 add_convert_fusion.3
  247.8 4.1 %collective-permute-start.38 = (bf16[1024,384]{0,1:T(8,128)(2,1)}, bf16[1024,384]{0,1:T(8,128)(2,1)S(1)}, u32[]{:S(2)}, u32[]{:S(2)}) collective-permute-start(bf16[1024,384]{0,1:T(8,128)(2,1)} %add_convert_fusion.3), channel_id=1, source_target_pairs={{0,2},{1,3},{2,4},{3,5},{8,10},{9,11},{10,12},{11,13},{16,18},{17,... | collective-permute-start | bytes 2359304 | tf_op jit(solution)/shard_map/ppermute | solution.py:51
  251.9 2.7 add_convert_fusion.7
  256.5 11.6 %fusion.9 = (f32[4096]{0:T(1024)S(1)}, f32[512]{0:T(512)S(1)}, f32[512,4096]{1,0:T(8,128)}) fusion(bf16[1,512,4096]{2,1,0:T(8,128)(2,1)S(1)} %copy-done.3, f32[512]{0:T(512)S(1)} %add_rsqrt_fusion, f32[4096]{0:T(1024)S(1)} %bitcast.51, bf16[4096,1024]{1,0:T(8,128)(2,1)} %select_dynamic-update-slice_fusion, bf16[512,512]{1,0:T(8,128)(2,1)S(1)} %copy-done.13, ...), kind=kOutput, calls=%fused_computation.11 | convolution fusion | flops 4311739904 | bytes 22056960 | tf_op jit(solution)/shard_map/dot_general | solution.py:207
  270.3 2.6 add_convert_fusion.2
  274.4 8.4 %collective-permute-done.32 = bf16[512,640]{0,1:T(8,128)(2,1)} collective-permute-done((bf16[512,640]{0,1:T(8,128)(2,1)}, bf16[512,640]{0,1:T(8,128)(2,1)}, u32[]{:S(2)}, u32[]{:S(2)}) %collective-permute-start.32) | collective-permute-done | bytes 655392 | tf_op jit(solution)/shard_map/ppermute | solution.py:51
  282.9 2.9 add_convert_fusion.6
  286.7 6.5 %collective-permute-start.49 = (f32[512]{0:T(512)S(1)}, f32[512]{0:T(512)S(1)}, u32[]{:S(2)}, u32[]{:S(2)}) collective-permute-start(f32[512]{0:T(512)S(1)} %bitcast.59), channel_id=1, source_target_pairs={{0,6},{1,7},{2,0},{3,1},{4,2},{5,3},{6,4},{7,5},{8,14},{9,15},{10,... | collective-permute-start | bytes 6152 | tf_op jit(solution)/shard_map/ppermute | solution.py:75
  296.8 4.0 %collective-permute-start.42 = (bf16[1024,384]{0,1:T(8,128)(2,1)S(1)}, bf16[1024,384]{0,1:T(8,128)(2,1)S(1)}, u32[]{:S(2)}, u32[]{:S(2)}) collective-permute-start(bf16[1024,384]{0,1:T(8,128)(2,1)S(1)} %add_convert_fusion), channel_id=1, source_target_pairs={{2,0},{3,1},{4,2},{5,3},{6,4},{7,5},{10,8},{11,9},{12,10},{13,11},... | collective-permute-start | bytes 2359304 | tf_op jit(solution)/shard_map/ppermute | solution.py:51
  303.7 4.1 %fusion.11 = bf16[1,512,4096]{2,1,0:T(8,128)(2,1)} fusion(f32[512,4096]{1,0:T(8,128)S(1)} %copy-done.5, bf16[1,512,4096]{2,1,0:T(8,128)(2,1)S(1)} %copy-done.4, f32[512]{0:T(512)S(1)} %broadcast_multiply_fusion.3, f32[4096]{0:T(1024)S(1)} %bitcast.52, f32[512]{0:T(512)S(1)} %add_rsqrt_fusion), kind=kLoop, calls=%fused_computation.14 | loop fusion | flops 14680064 | bytes 16797696 | tf_op jit(solution)/shard_map/broadcast_in_dim | solution.py:228
  307.8 4.3 %collective-permute-done.39 = bf16[1024,384]{0,1:T(8,128)(2,1)S(1)} collective-permute-done((bf16[1024,384]{0,1:T(8,128)(2,1)S(1)}, bf16[1024,384]{0,1:T(8,128)(2,1)S(1)}, u32[]{:S(2)}, u32[]{:S(2)}) %collective-permute-start.39) | collective-permute-done | bytes 786464 | tf_op jit(solution)/shard_map/ppermute | solution.py:51
  312.1 6.9 %collective-permute-start.48 = (f32[512]{0:T(512)S(1)}, f32[512]{0:T(512)S(1)}, u32[]{:S(2)}, u32[]{:S(2)}) collective-permute-start(f32[512]{0:T(512)S(1)} %bitcast.58), channel_id=1, source_target_pairs={{0,5},{1,6},{2,7},{3,0},{4,1},{5,2},{6,3},{7,4},{8,13},{9,14},{10,... | collective-permute-start | bytes 6152 | tf_op jit(solution)/shard_map/ppermute | solution.py:75
  319.1 6.6 %collective-permute-start.47 = (f32[512]{0:T(512)S(1)}, f32[512]{0:T(512)S(1)}, u32[]{:S(2)}, u32[]{:S(2)}) collective-permute-start(f32[512]{0:T(512)S(1)} %bitcast.57), channel_id=1, source_target_pairs={{0,4},{1,5},{2,6},{3,7},{4,0},{5,1},{6,2},{7,3},{8,12},{9,13},{10,... | collective-permute-start | bytes 6152 | tf_op jit(solution)/shard_map/ppermute | solution.py:75
  329.8 8.7 %collective-permute-start.46 = (f32[512]{0:T(512)S(1)}, f32[512]{0:T(512)S(1)}, u32[]{:S(2)}, u32[]{:S(2)}) collective-permute-start(f32[512]{0:T(512)S(1)} %bitcast.56), channel_id=1, source_target_pairs={{0,3},{1,4},{2,5},{3,6},{4,7},{5,0},{6,1},{7,2},{8,11},{9,12},{10,... | collective-permute-start | bytes 6152 | tf_op jit(solution)/shard_map/ppermute | solution.py:75
  338.5 2.5 add_convert_fusion.4
  345.1 4.7 %collective-permute-start.36 = (bf16[512,640]{0,1:T(8,128)(2,1)}, bf16[512,640]{0,1:T(8,128)(2,1)}, u32[]{:S(2)}, u32[]{:S(2)}) collective-permute-start(bf16[512,640]{0,1:T(8,128)(2,1)} %add_convert_fusion.4), channel_id=1, source_target_pairs={{2,0},{3,1},{4,2},{5,3},{6,4},{7,5},{10,8},{11,9},{12,10},{13,11},... | collective-permute-start | bytes 1966088 | tf_op jit(solution)/shard_map/ppermute | solution.py:51
  353.0 8.9 %collective-permute-done.44 = f32[512]{0:T(512)S(1)} collective-permute-done((f32[512]{0:T(512)S(1)}, f32[512]{0:T(512)S(1)}, u32[]{:S(2)}, u32[]{:S(2)}) %collective-permute-start.44) | collective-permute-done | bytes 2080 | tf_op jit(solution)/shard_map/ppermute | solution.py:75
  365.1 2.3 convert_add_fusion.2
  (167 shorter events, 87.6 us)
Async XLA Ops:
  7.2 230.6 %all-reduce.2.cloned.1.call-start = ((), (), s32[]{:S(2)}) async-start(), calls=%async_computation | async-start | bytes 3145728 | tf_op jit(solution)/shard_map/psum | solution.py:220
  8.3 12.1 %collective-permute-start.8 = (bf16[512,384]{1,0:T(8,128)(2,1)S(1)}, bf16[512,384]{1,0:T(8,128)(2,1)S(1)}, u32[]{:S(2)}, u32[]{:S(2)}) collective-permute-start(bf16[512,384]{1,0:T(8,128)(2,1)S(1)} %slice.74), channel_id=1, source_target_pairs={{0,1},{1,0},{2,3},{3,2},{4,5},{5,4},{6,7},{7,6},{8,9},{9,8},{10,11... | collective-permute-start | bytes 1179656 | tf_op jit(solution)/shard_map/ppermute | solution.py:51
  15.3 17.9 %collective-permute-start.7 = (bf16[512,640]{1,0:T(8,128)(2,1)}, bf16[512,640]{1,0:T(8,128)(2,1)S(1)}, u32[]{:S(2)}, u32[]{:S(2)}) collective-permute-start(bf16[512,640]{1,0:T(8,128)(2,1)} %get-tuple-element.37), channel_id=1, source_target_pairs={{0,1},{1,0},{2,3},{3,2},{4,5},{5,4},{6,7},{7,6},{8,9},{9,8},{10,11... | collective-permute-start | bytes 1966088 | tf_op jit(solution)/shard_map/ppermute | solution.py:51
  15.9 22.9 %collective-permute-start.10 = (bf16[512,640]{1,0:T(8,128)(2,1)}, bf16[512,640]{1,0:T(8,128)(2,1)S(1)}, u32[]{:S(2)}, u32[]{:S(2)}) collective-permute-start(bf16[512,640]{1,0:T(8,128)(2,1)} %get-tuple-element.37), channel_id=1, source_target_pairs={{0,2},{1,3},{2,4},{3,5},{4,6},{5,7},{8,10},{9,11},{10,12},{11,13},... | collective-permute-start | bytes 1966088 | tf_op jit(solution)/shard_map/ppermute | solution.py:51
  35.3 37.1 %collective-permute-start.16 = (bf16[1024,384]{1,0:T(8,128)(2,1)S(1)}, bf16[1024,384]{1,0:T(8,128)(2,1)}, u32[]{:S(2)}, u32[]{:S(2)}) collective-permute-start(bf16[1024,384]{1,0:T(8,128)(2,1)S(1)} %get-tuple-element.39), channel_id=1, source_target_pairs={{0,2},{1,3},{2,4},{3,5},{4,6},{5,7},{8,10},{9,11},{10,12},{11,13},... | collective-permute-start | bytes 2359304 | tf_op jit(solution)/shard_map/ppermute | solution.py:51
  38.8 32.0 %collective-permute-start.11 = (bf16[512,640]{1,0:T(8,128)(2,1)S(1)}, bf16[512,640]{1,0:T(8,128)(2,1)}, u32[]{:S(2)}, u32[]{:S(2)}) collective-permute-start(bf16[512,640]{1,0:T(8,128)(2,1)S(1)} %collective-permute-done.10), channel_id=1, source_target_pairs={{2,4},{3,5},{4,6},{5,7},{10,12},{11,13},{12,14},{13,15},{18,20},{1... | collective-permute-start | bytes 1966088 | tf_op jit(solution)/shard_map/ppermute | solution.py:51
  43.0 61.1 %collective-permute-start.9 = (bf16[512,640]{1,0:T(8,128)(2,1)}, bf16[512,640]{1,0:T(8,128)(2,1)}, u32[]{:S(2)}, u32[]{:S(2)}) collective-permute-start(bf16[512,640]{1,0:T(8,128)(2,1)} %get-tuple-element.37), channel_id=1, source_target_pairs={{2,0},{3,1},{4,2},{5,3},{6,4},{7,5},{10,8},{11,9},{12,10},{13,11},... | collective-permute-start | bytes 1966088 | tf_op jit(solution)/shard_map/ppermute | solution.py:51
  45.5 12.6 %collective-permute-start = (bf16[512]{0:T(512)(128)(2,1)}, bf16[512]{0:T(512)(128)(2,1)S(1)}, u32[]{:S(2)}, u32[]{:S(2)}) collective-permute-start(bf16[512]{0:T(512)(128)(2,1)} %reduce), channel_id=1, source_target_pairs={{0,7},{1,0},{2,1},{3,2},{4,3},{5,4},{6,5},{7,6},{8,15},{9,8},{10,9... | collective-permute-start | bytes 3080 | tf_op jit(solution)/shard_map/ppermute | solution.py:63
  45.5 14.7 %collective-permute-start.1 = (bf16[512]{0:T(512)(128)(2,1)}, bf16[512]{0:T(512)(128)(2,1)S(1)}, u32[]{:S(2)}, u32[]{:S(2)}) collective-permute-start(bf16[512]{0:T(512)(128)(2,1)} %reduce), channel_id=1, source_target_pairs={{0,6},{1,7},{2,0},{3,1},{4,2},{5,3},{6,4},{7,5},{8,14},{9,15},{10,... | collective-permute-start | bytes 3080 | tf_op jit(solution)/shard_map/ppermute | solution.py:63
  60.3 21.2 %collective-permute-start.3 = (bf16[512]{0:T(512)(128)(2,1)}, bf16[512]{0:T(512)(128)(2,1)S(1)}, u32[]{:S(2)}, u32[]{:S(2)}) collective-permute-start(bf16[512]{0:T(512)(128)(2,1)} %reduce), channel_id=1, source_target_pairs={{0,4},{1,5},{2,6},{3,7},{4,0},{5,1},{6,2},{7,3},{8,12},{9,13},{10,... | collective-permute-start | bytes 3080 | tf_op jit(solution)/shard_map/ppermute | solution.py:63
  68.9 48.7 %collective-permute-start.15 = (bf16[1024,384]{1,0:T(8,128)(2,1)S(1)}, bf16[1024,384]{1,0:T(8,128)(2,1)}, u32[]{:S(2)}, u32[]{:S(2)}) collective-permute-start(bf16[1024,384]{1,0:T(8,128)(2,1)S(1)} %get-tuple-element.39), channel_id=1, source_target_pairs={{2,0},{3,1},{4,2},{5,3},{6,4},{7,5},{10,8},{11,9},{12,10},{13,11},... | collective-permute-start | bytes 2359304 | tf_op jit(solution)/shard_map/ppermute | solution.py:51
  70.8 43.0 %collective-permute-start.12 = (bf16[512,640]{1,0:T(8,128)(2,1)}, bf16[512,640]{1,0:T(8,128)(2,1)}, u32[]{:S(2)}, u32[]{:S(2)}) collective-permute-start(bf16[512,640]{1,0:T(8,128)(2,1)} %collective-permute-done.11), channel_id=1, source_target_pairs={{4,6},{5,7},{12,14},{13,15},{20,22},{21,23},{28,30},{29,31}} | collective-permute-start | bytes 1966088 | tf_op jit(solution)/shard_map/ppermute | solution.py:51
  72.4 49.7 %collective-permute-start.17 = (bf16[1024,384]{1,0:T(8,128)(2,1)}, bf16[1024,384]{1,0:T(8,128)(2,1)}, u32[]{:S(2)}, u32[]{:S(2)}) collective-permute-start(bf16[1024,384]{1,0:T(8,128)(2,1)} %collective-permute-done.16), channel_id=1, source_target_pairs={{2,4},{3,5},{4,6},{5,7},{10,12},{11,13},{12,14},{13,15},{18,20},{1... | collective-permute-start | bytes 2359304 | tf_op jit(solution)/shard_map/ppermute | solution.py:51
  81.5 11.0 %collective-permute-start.4 = (bf16[512]{0:T(512)(128)(2,1)}, bf16[512]{0:T(512)(128)(2,1)}, u32[]{:S(2)}, u32[]{:S(2)}) collective-permute-start(bf16[512]{0:T(512)(128)(2,1)} %reduce), channel_id=1, source_target_pairs={{0,3},{1,4},{2,5},{3,6},{4,7},{5,0},{6,1},{7,2},{8,11},{9,12},{10,... | collective-permute-start | bytes 3080 | tf_op jit(solution)/shard_map/ppermute | solution.py:63
  92.6 13.5 %collective-permute-start.5 = (bf16[512]{0:T(512)(128)(2,1)}, bf16[512]{0:T(512)(128)(2,1)S(1)}, u32[]{:S(2)}, u32[]{:S(2)}) collective-permute-start(bf16[512]{0:T(512)(128)(2,1)} %reduce), channel_id=1, source_target_pairs={{0,2},{1,3},{2,4},{3,5},{4,6},{5,7},{6,0},{7,1},{8,10},{9,11},{10,... | collective-permute-start | bytes 3080 | tf_op jit(solution)/shard_map/ppermute | solution.py:63
  104.1 22.2 %collective-permute-start.19 = (bf16[512,640]{1,0:T(8,128)(2,1)}, bf16[512,640]{1,0:T(8,128)(2,1)}, u32[]{:S(2)}, u32[]{:S(2)}) collective-permute-start(bf16[512,640]{1,0:T(8,128)(2,1)} %collective-permute-done.9), channel_id=1, source_target_pairs={{2,0},{3,1},{4,2},{5,3},{10,8},{11,9},{12,10},{13,11},{18,16},{19,... | collective-permute-start | bytes 1966088 | tf_op jit(solution)/shard_map/ppermute | solution.py:51
  111.9 17.9 %collective-permute-start.13 = (bf16[512,640]{1,0:T(8,128)(2,1)}, bf16[512,640]{1,0:T(8,128)(2,1)}, u32[]{:S(2)}, u32[]{:S(2)}) collective-permute-start(bf16[512,640]{1,0:T(8,128)(2,1)} %collective-permute-done.9), channel_id=1, source_target_pairs={{0,1},{1,0},{2,3},{3,2},{4,5},{5,4},{8,9},{9,8},{10,11},{11,10},{1... | collective-permute-start | bytes 1966088 | tf_op jit(solution)/shard_map/ppermute | solution.py:51
  113.9 19.4 %collective-permute-start.14 = (bf16[512,640]{1,0:T(8,128)(2,1)}, bf16[512,640]{1,0:T(8,128)(2,1)}, u32[]{:S(2)}, u32[]{:S(2)}) collective-permute-start(bf16[512,640]{1,0:T(8,128)(2,1)} %collective-permute-done.12), channel_id=1, source_target_pairs={{6,7},{7,6},{14,15},{15,14},{22,23},{23,22},{30,31},{31,30}} | collective-permute-start | bytes 1966088 | tf_op jit(solution)/shard_map/ppermute | solution.py:51
  117.6 34.1 %collective-permute-start.22 = (bf16[1024,384]{1,0:T(8,128)(2,1)}, bf16[1024,384]{1,0:T(8,128)(2,1)S(1)}, u32[]{:S(2)}, u32[]{:S(2)}) collective-permute-start(bf16[1024,384]{1,0:T(8,128)(2,1)} %collective-permute-done.15), channel_id=1, source_target_pairs={{2,0},{3,1},{4,2},{5,3},{10,8},{11,9},{12,10},{13,11},{18,16},{19,... | collective-permute-start | bytes 2359304 | tf_op jit(solution)/shard_map/ppermute | solution.py:51
  122.1 30.3 %collective-permute-start.18 = (bf16[1024,384]{1,0:T(8,128)(2,1)}, bf16[1024,384]{1,0:T(8,128)(2,1)S(1)}, u32[]{:S(2)}, u32[]{:S(2)}) collective-permute-start(bf16[1024,384]{1,0:T(8,128)(2,1)} %collective-permute-done.17), channel_id=1, source_target_pairs={{4,6},{5,7},{12,14},{13,15},{20,22},{21,23},{28,30},{29,31}} | collective-permute-start | bytes 2359304 | tf_op jit(solution)/shard_map/ppermute | solution.py:51
  126.4 22.1 %collective-permute-start.23 = (bf16[512,640]{1,0:T(8,128)(2,1)}, bf16[512,640]{1,0:T(8,128)(2,1)S(1)}, u32[]{:S(2)}, u32[]{:S(2)}) collective-permute-start(bf16[512,640]{1,0:T(8,128)(2,1)} %collective-permute-done.19), channel_id=1, source_target_pairs={{2,0},{3,1},{10,8},{11,9},{18,16},{19,17},{26,24},{27,25}} | collective-permute-start | bytes 1966088 | tf_op jit(solution)/shard_map/ppermute | solution.py:51
  129.9 31.6 %collective-permute-start.20 = (bf16[512,640]{1,0:T(8,128)(2,1)}, bf16[512,640]{1,0:T(8,128)(2,1)S(1)}, u32[]{:S(2)}, u32[]{:S(2)}) collective-permute-start(bf16[512,640]{1,0:T(8,128)(2,1)} %collective-permute-done.19), channel_id=1, source_target_pairs={{0,1},{1,0},{2,3},{3,2},{8,9},{9,8},{10,11},{11,10},{16,17},{17,16... | collective-permute-start | bytes 1966088 | tf_op jit(solution)/shard_map/ppermute | solution.py:51
  133.3 28.2 %collective-permute-start.21 = (bf16[512,640]{1,0:T(8,128)(2,1)}, bf16[512,640]{1,0:T(8,128)(2,1)S(1)}, u32[]{:S(2)}, u32[]{:S(2)}) collective-permute-start(bf16[512,640]{1,0:T(8,128)(2,1)} %collective-permute-done.11), channel_id=1, source_target_pairs={{4,5},{5,4},{6,7},{7,6},{12,13},{13,12},{14,15},{15,14},{20,21},{2... | collective-permute-start | bytes 1966088 | tf_op jit(solution)/shard_map/ppermute | solution.py:51
  148.5 16.2 %collective-permute-start.25 = (bf16[512,640]{1,0:T(8,128)(2,1)}, bf16[512,640]{1,0:T(8,128)(2,1)S(1)}, u32[]{:S(2)}, u32[]{:S(2)}) collective-permute-start(bf16[512,640]{1,0:T(8,128)(2,1)} %copy-done.10), channel_id=1, source_target_pairs={{2,3},{3,2},{4,5},{5,4},{6,7},{7,6},{10,11},{11,10},{12,13},{13,12... | collective-permute-start | bytes 1966088 | tf_op jit(solution)/shard_map/ppermute | solution.py:51
  151.8 12.9 %collective-permute-start.24 = (bf16[512,640]{1,0:T(8,128)(2,1)S(1)}, bf16[512,640]{1,0:T(8,128)(2,1)S(1)}, u32[]{:S(2)}, u32[]{:S(2)}) collective-permute-start(bf16[512,640]{1,0:T(8,128)(2,1)S(1)} %collective-permute-done.23), channel_id=1, source_target_pairs={{0,1},{1,0},{8,9},{9,8},{16,17},{17,16},{24,25},{25,24}} | collective-permute-start | bytes 1966088 | tf_op jit(solution)/shard_map/ppermute | solution.py:51
  152.5 15.0 %collective-permute-start.26 = (bf16[1024,384]{1,0:T(8,128)(2,1)S(1)}, bf16[1024,384]{1,0:T(8,128)(2,1)S(1)}, u32[]{:S(2)}, u32[]{:S(2)}) collective-permute-start(bf16[1024,384]{1,0:T(8,128)(2,1)S(1)} %collective-permute-done.22), channel_id=1, source_target_pairs={{2,0},{3,1},{10,8},{11,9},{18,16},{19,17},{26,24},{27,25}} | collective-permute-start | bytes 2359304 | tf_op jit(solution)/shard_map/ppermute | solution.py:51
  195.1 16.7 %collective-permute-start.30 = (bf16[512,640]{0,1:T(8,128)(2,1)}, bf16[512,640]{0,1:T(8,128)(2,1)S(1)}, u32[]{:S(2)}, u32[]{:S(2)}) collective-permute-start(bf16[512,640]{0,1:T(8,128)(2,1)} %get-tuple-element.22), channel_id=1, source_target_pairs={{0,1},{1,0},{2,3},{3,2},{4,5},{5,4},{6,7},{7,6},{8,9},{9,8},{10,11... | collective-permute-start | bytes 1966088 | tf_op jit(solution)/shard_map/ppermute | solution.py:51
  199.1 45.9 %collective-permute-start.37 = (bf16[1024,384]{0,1:T(8,128)(2,1)}, bf16[1024,384]{0,1:T(8,128)(2,1)}, u32[]{:S(2)}, u32[]{:S(2)}) collective-permute-start(bf16[1024,384]{0,1:T(8,128)(2,1)} %get-tuple-element.27), channel_id=1, source_target_pairs={{0,2},{1,3},{8,10},{9,11},{16,18},{17,19},{24,26},{25,27}} | collective-permute-start | bytes 2359304 | tf_op jit(solution)/shard_map/ppermute | solution.py:51
  200.6 51.3 %collective-permute-start.29 = (bf16[512,640]{0,1:T(8,128)(2,1)}, bf16[512,640]{0,1:T(8,128)(2,1)S(1)}, u32[]{:S(2)}, u32[]{:S(2)}) collective-permute-start(bf16[512,640]{0,1:T(8,128)(2,1)} %get-tuple-element.23), channel_id=1, source_target_pairs={{0,1},{1,0},{2,3},{3,2},{4,5},{5,4},{6,7},{7,6},{8,9},{9,8},{10,11... | collective-permute-start | bytes 1966088 | tf_op jit(solution)/shard_map/ppermute | solution.py:51
  214.1 37.7 %collective-permute-start.31 = (bf16[512,640]{0,1:T(8,128)(2,1)}, bf16[512,640]{0,1:T(8,128)(2,1)}, u32[]{:S(2)}, u32[]{:S(2)}) collective-permute-start(bf16[512,640]{0,1:T(8,128)(2,1)} %fusion.18), channel_id=1, source_target_pairs={{0,2},{1,3},{8,10},{9,11},{16,18},{17,19},{24,26},{25,27}} | collective-permute-start | bytes 1966088 | tf_op jit(solution)/shard_map/ppermute | solution.py:51
  242.6 25.5 %collective-permute-start.40 = (bf16[1024,384]{0,1:T(8,128)(2,1)}, bf16[1024,384]{0,1:T(8,128)(2,1)S(1)}, u32[]{:S(2)}, u32[]{:S(2)}) collective-permute-start(bf16[1024,384]{0,1:T(8,128)(2,1)} %get-tuple-element.28), channel_id=1, source_target_pairs={{6,4},{7,5},{14,12},{15,13},{22,20},{23,21},{30,28},{31,29}} | collective-permute-start | bytes 2359304 | tf_op jit(solution)/shard_map/ppermute | solution.py:51
  243.4 31.0 %collective-permute-start.28 = (bf16[512,640]{0,1:T(8,128)(2,1)}, bf16[512,640]{0,1:T(8,128)(2,1)}, u32[]{:S(2)}, u32[]{:S(2)}) collective-permute-start(bf16[512,640]{0,1:T(8,128)(2,1)} %get-tuple-element.24), channel_id=1, source_target_pairs={{0,1},{1,0},{2,3},{3,2},{4,5},{5,4},{6,7},{7,6},{8,9},{9,8},{10,11... | collective-permute-start | bytes 1966088 | tf_op jit(solution)/shard_map/ppermute | solution.py:51
  247.8 22.6 %collective-permute-start.38 = (bf16[1024,384]{0,1:T(8,128)(2,1)}, bf16[1024,384]{0,1:T(8,128)(2,1)S(1)}, u32[]{:S(2)}, u32[]{:S(2)}) collective-permute-start(bf16[1024,384]{0,1:T(8,128)(2,1)} %add_convert_fusion.3), channel_id=1, source_target_pairs={{0,2},{1,3},{2,4},{3,5},{8,10},{9,11},{10,12},{11,13},{16,18},{17,... | collective-permute-start | bytes 2359304 | tf_op jit(solution)/shard_map/ppermute | solution.py:51
  254.5 28.3 %collective-permute-start.32 = (bf16[512,640]{0,1:T(8,128)(2,1)}, bf16[512,640]{0,1:T(8,128)(2,1)}, u32[]{:S(2)}, u32[]{:S(2)}) collective-permute-start(bf16[512,640]{0,1:T(8,128)(2,1)} %add_convert_fusion.7), channel_id=1, source_target_pairs={{0,2},{1,3},{2,4},{3,5},{8,10},{9,11},{10,12},{11,13},{16,18},{17,... | collective-permute-start | bytes 1966088 | tf_op jit(solution)/shard_map/ppermute | solution.py:51
  273.0 22.1 %collective-permute-start.41 = (bf16[1024,384]{0,1:T(8,128)(2,1)S(1)}, bf16[1024,384]{0,1:T(8,128)(2,1)S(1)}, u32[]{:S(2)}, u32[]{:S(2)}) collective-permute-start(bf16[1024,384]{0,1:T(8,128)(2,1)S(1)} %get-tuple-element.26), channel_id=1, source_target_pairs={{4,2},{5,3},{6,4},{7,5},{12,10},{13,11},{14,12},{15,13},{20,18},{2... | collective-permute-start | bytes 2359304 | tf_op jit(solution)/shard_map/ppermute | solution.py:51
  285.7 15.0 %collective-permute-start.34 = (bf16[512,640]{0,1:T(8,128)(2,1)S(1)}, bf16[512,640]{0,1:T(8,128)(2,1)S(1)}, u32[]{:S(2)}, u32[]{:S(2)}) collective-permute-start(bf16[512,640]{0,1:T(8,128)(2,1)S(1)} %get-tuple-element.20), channel_id=1, source_target_pairs={{6,4},{7,5},{14,12},{15,13},{22,20},{23,21},{30,28},{31,29}} | collective-permute-start | bytes 1966088 | tf_op jit(solution)/shard_map/ppermute | solution.py:51
  286.6 54.4 %collective-permute-start.50 = (f32[512]{0:T(512)S(1)}, f32[512]{0:T(512)S(1)}, u32[]{:S(2)}, u32[]{:S(2)}) collective-permute-start(f32[512]{0:T(512)S(1)} %bitcast.60), channel_id=1, source_target_pairs={{0,7},{1,0},{2,1},{3,2},{4,3},{5,4},{6,5},{7,6},{8,15},{9,8},{10,9... | collective-permute-start | bytes 6152 | tf_op jit(solution)/shard_map/ppermute | solution.py:75
  286.7 54.9 %collective-permute-start.49 = (f32[512]{0:T(512)S(1)}, f32[512]{0:T(512)S(1)}, u32[]{:S(2)}, u32[]{:S(2)}) collective-permute-start(f32[512]{0:T(512)S(1)} %bitcast.59), channel_id=1, source_target_pairs={{0,6},{1,7},{2,0},{3,1},{4,2},{5,3},{6,4},{7,5},{8,14},{9,15},{10,... | collective-permute-start | bytes 6152 | tf_op jit(solution)/shard_map/ppermute | solution.py:75
  293.1 19.0 %collective-permute-start.39 = (bf16[1024,384]{0,1:T(8,128)(2,1)S(1)}, bf16[1024,384]{0,1:T(8,128)(2,1)S(1)}, u32[]{:S(2)}, u32[]{:S(2)}) collective-permute-start(bf16[1024,384]{0,1:T(8,128)(2,1)S(1)} %get-tuple-element.25), channel_id=1, source_target_pairs={{0,2},{1,3},{2,4},{3,5},{4,6},{5,7},{8,10},{9,11},{10,12},{11,13},... | collective-permute-start | bytes 2359304 | tf_op jit(solution)/shard_map/ppermute | solution.py:51
  296.8 22.4 %collective-permute-start.42 = (bf16[1024,384]{0,1:T(8,128)(2,1)S(1)}, bf16[1024,384]{0,1:T(8,128)(2,1)S(1)}, u32[]{:S(2)}, u32[]{:S(2)}) collective-permute-start(bf16[1024,384]{0,1:T(8,128)(2,1)S(1)} %add_convert_fusion), channel_id=1, source_target_pairs={{2,0},{3,1},{4,2},{5,3},{6,4},{7,5},{10,8},{11,9},{12,10},{13,11},... | collective-permute-start | bytes 2359304 | tf_op jit(solution)/shard_map/ppermute | solution.py:51
  302.4 27.5 %collective-permute-start.35 = (bf16[512,640]{0,1:T(8,128)(2,1)S(1)}, bf16[512,640]{0,1:T(8,128)(2,1)S(1)}, u32[]{:S(2)}, u32[]{:S(2)}) collective-permute-start(bf16[512,640]{0,1:T(8,128)(2,1)S(1)} %add_convert_fusion.5), channel_id=1, source_target_pairs={{4,2},{5,3},{6,4},{7,5},{12,10},{13,11},{14,12},{15,13},{20,18},{2... | collective-permute-start | bytes 1966088 | tf_op jit(solution)/shard_map/ppermute | solution.py:51
  312.1 29.5 %collective-permute-start.48 = (f32[512]{0:T(512)S(1)}, f32[512]{0:T(512)S(1)}, u32[]{:S(2)}, u32[]{:S(2)}) collective-permute-start(f32[512]{0:T(512)S(1)} %bitcast.58), channel_id=1, source_target_pairs={{0,5},{1,6},{2,7},{3,0},{4,1},{5,2},{6,3},{7,4},{8,13},{9,14},{10,... | collective-permute-start | bytes 6152 | tf_op jit(solution)/shard_map/ppermute | solution.py:75
  319.1 24.4 %collective-permute-start.47 = (f32[512]{0:T(512)S(1)}, f32[512]{0:T(512)S(1)}, u32[]{:S(2)}, u32[]{:S(2)}) collective-permute-start(f32[512]{0:T(512)S(1)} %bitcast.57), channel_id=1, source_target_pairs={{0,4},{1,5},{2,6},{3,7},{4,0},{5,1},{6,2},{7,3},{8,12},{9,13},{10,... | collective-permute-start | bytes 6152 | tf_op jit(solution)/shard_map/ppermute | solution.py:75
  329.8 15.3 %collective-permute-start.46 = (f32[512]{0:T(512)S(1)}, f32[512]{0:T(512)S(1)}, u32[]{:S(2)}, u32[]{:S(2)}) collective-permute-start(f32[512]{0:T(512)S(1)} %bitcast.56), channel_id=1, source_target_pairs={{0,3},{1,4},{2,5},{3,6},{4,7},{5,0},{6,1},{7,2},{8,11},{9,12},{10,... | collective-permute-start | bytes 6152 | tf_op jit(solution)/shard_map/ppermute | solution.py:75
  341.0 24.0 %collective-permute-start.27 = (bf16[512,640]{0,1:T(8,128)(2,1)}, bf16[512,640]{0,1:T(8,128)(2,1)}, u32[]{:S(2)}, u32[]{:S(2)}) collective-permute-start(bf16[512,640]{0,1:T(8,128)(2,1)} %get-tuple-element.21), channel_id=1, source_target_pairs={{0,1},{1,0},{2,3},{3,2},{4,5},{5,4},{6,7},{7,6},{8,9},{9,8},{10,11... | collective-permute-start | bytes 1966088 | tf_op jit(solution)/shard_map/ppermute | solution.py:51
  341.6 23.5 %collective-permute-start.33 = (bf16[512,640]{0,1:T(8,128)(2,1)}, bf16[512,640]{0,1:T(8,128)(2,1)}, u32[]{:S(2)}, u32[]{:S(2)}) collective-permute-start(bf16[512,640]{0,1:T(8,128)(2,1)} %get-tuple-element.19), channel_id=1, source_target_pairs={{0,2},{1,3},{2,4},{3,5},{4,6},{5,7},{8,10},{9,11},{10,12},{11,13},... | collective-permute-start | bytes 1966088 | tf_op jit(solution)/shard_map/ppermute | solution.py:51
  343.5 20.4 %collective-permute-start.43 = (bf16[512,384]{0,1:T(8,128)(2,1)}, bf16[512,384]{0,1:T(8,128)(2,1)}, u32[]{:S(2)}, u32[]{:S(2)}) collective-permute-start(bf16[512,384]{0,1:T(8,128)(2,1)} %dynamic-slice_convert_fusion.6), channel_id=1, source_target_pairs={{0,1},{1,0},{2,3},{3,2},{4,5},{5,4},{6,7},{7,6},{8,9},{9,8},{10,11... | collective-permute-start | bytes 1179656 | tf_op jit(solution)/shard_map/ppermute | solution.py:51
  345.1 20.0 %collective-permute-start.36 = (bf16[512,640]{0,1:T(8,128)(2,1)}, bf16[512,640]{0,1:T(8,128)(2,1)}, u32[]{:S(2)}, u32[]{:S(2)}) collective-permute-start(bf16[512,640]{0,1:T(8,128)(2,1)} %add_convert_fusion.4), channel_id=1, source_target_pairs={{2,0},{3,1},{4,2},{5,3},{6,4},{7,5},{10,8},{11,9},{12,10},{13,11},... | collective-permute-start | bytes 1966088 | tf_op jit(solution)/shard_map/ppermute | solution.py:51
  (25 other events, 423.5 us)
Sparse Core Ops, SparseCore 0:
  195.9 41.7 all-reduce.1

commit v2 on v0

v2 whole, which is shorter than its diff:
```python
import functools
import math

import jax
import jax.numpy as jnp
from jax import lax
from jax.experimental import pallas as pl
from jax.experimental.pallas import tpu as pltpu
from jax.sharding import PartitionSpec as P

HEAD = 128
SEQ_LEN = 4096
PAD = 16


epsilon = 1e-05
rope_base = 500000.0
momentum_rate = 0.9
outer_rate = 0.7
mixing_rate = 0.5

f32, bf16 = jnp.float32, jnp.bfloat16


class Ring:
    def __init__(self):
        self.count = lax.axis_size("fsdp")
        self.half = self.count // 2
        walk = list(range(0, self.count, 2)) + list(range(self.count - 1, 0, -2))
        after = walk[1:] + walk[:1]
        self.right = list(zip(walk, after))
        self.left = list(zip(after, walk))
        self.me = lax.axis_index("fsdp")
        self.spot = jnp.where(
            self.me % 2 == 0, self.me // 2, self.count - 1 - self.me // 2
        )

    def devices_at(self, distances):
        spot = (self.spot + self.count + jnp.array(distances, jnp.int32)) % self.count
        return jnp.where(spot < self.half, 2 * spot, 2 * (self.count - 1 - spot) + 1)

    def to_right(self, value):
        return lax.ppermute(value, "fsdp", self.right)

    def to_left(self, value):
        return lax.ppermute(value, "fsdp", self.left)


def rope_tables(positions):
    half = HEAD // 2
    index_f = jnp.arange(half, dtype=f32)
    inverse = jnp.exp(index_f * (-2.0 * math.log(rope_base) / HEAD))
    angle = positions.astype(f32)[:, None] * inverse[None, :]
    cosine, sine = jnp.cos(angle), jnp.sin(angle)
    return jnp.concatenate([cosine, cosine], axis=1), jnp.concatenate([-sine, sine], axis=1)


def first_kernel(scale, at, x, cotangent, cosine, sine, kv_grad, inv, far, near):
    step = pl.program_id(0)
    width = x.shape[1]
    shard = far.shape[0]
    kvw = cotangent.shape[1] // 2

    @pl.when(step == 0)
    def _():
        total = jnp.zeros((x.shape[0], HEAD), f32)
        for c in range(0, width, HEAD):
            part = x[:, c : c + HEAD].astype(f32)
            total = total + part * part
        mean = jnp.sum(total, axis=1, keepdims=True) / width
        inv[...] = jnp.broadcast_to(lax.rsqrt(mean + epsilon), inv.shape)
        for c in range(0, kvw, HEAD):
            part = cotangent[:, c : c + HEAD].astype(f32)
            turned = pltpu.roll(part, HEAD // 2, 1)
            kv_grad[:, c : c + HEAD] = (part * cosine[...] - turned * sine[...]).astype(bf16)
        kv_grad[:, kvw:] = cotangent[:, kvw:]

    block = x[:, pl.ds(pl.multiple_of(at[step] * shard, shard), shard)]
    normed = (block.astype(f32) * inv[:, :1]).astype(bf16)
    term = (
        lax.dot_general(normed, kv_grad[...], (((0,), (0,)), ((), ())), preferred_element_type=f32)
        * scale
    )

    @pl.when(step == 0)
    def _():
        far[...] = term.astype(bf16)

    @pl.when(step > 0)
    def _():
        near[0] = term


def first_part(ring, tokens_in, cotangent, cosine, sine, shard, scale):
    rows, width = tokens_in.shape
    cols = cotangent.shape[1]
    order = [ring.half]
    for d in range(ring.half - 1, 0, -1):
        order += [d, -d]
    order.append(0)
    n = ring.count
    fixed = lambda k, at: (0, 0)
    return pl.pallas_call(
        functools.partial(first_kernel, scale),
        grid_spec=pltpu.PrefetchScalarGridSpec(
            num_scalar_prefetch=1,
            grid=(n,),
            in_specs=[
                pl.BlockSpec((rows, width), fixed),
                pl.BlockSpec((rows, cols), fixed),
                pl.BlockSpec((rows, HEAD), fixed),
                pl.BlockSpec((rows, HEAD), fixed),
            ],
            out_specs=[
                pl.BlockSpec((rows, cols), fixed),
                pl.BlockSpec((rows, HEAD), fixed),
                pl.BlockSpec((shard, cols), fixed),
                pl.BlockSpec((1, shard, cols), lambda k, at: (jnp.maximum(k - 1, 0), 0, 0)),
            ],
        ),
        out_shape=[
            jax.ShapeDtypeStruct((rows, cols), bf16),
            jax.ShapeDtypeStruct((rows, HEAD), f32),
            jax.ShapeDtypeStruct((shard, cols), bf16),
            jax.ShapeDtypeStruct((n - 1, shard, cols), f32),
        ],
        compiler_params=pltpu.CompilerParams(vmem_limit_bytes=40 * 2**20),
        cost_estimate=pl.CostEstimate(
            flops=2 * rows * width * cols,
            bytes_accessed=2 * rows * width + 4 * width * cols,
            transcendentals=0,
        ),
        name="norm_and_weight_terms",
    )(ring.devices_at(order), tokens_in, cotangent, cosine, sine)


def second_kernel(n, at, x, kv_grad, inv, cosine, sine, *refs):
    blocks, refs = refs[: n + 1], refs[n + 1 :]
    kv_out, input_grad, xs, ws, ng, pre, out, x_sem, w_sem, o_sem = refs
    rows, width = x.shape
    shard = xs.shape[2]
    cols = pre.shape[1]
    kvw = cols // 2
    cut = shard // 2

    def columns(k):
        return pl.ds(pl.multiple_of(at[k] * shard, shard), shard)

    def x_copy(k):
        return pltpu.make_async_copy(x.at[:, columns(k)], xs.at[k], x_sem.at[k])

    def o_copy(k):
        return pltpu.make_async_copy(out.at[k], input_grad.at[:, columns(k)], o_sem.at[k])

    for k in range(n):
        x_copy(k).start()
        if k < n - 1:
            pltpu.make_async_copy(blocks[k], ws.at[k], w_sem.at[k]).start()
        else:
            pltpu.make_async_copy(blocks[k], ws.at[k, :cut], w_sem.at[k]).start()
            pltpu.make_async_copy(blocks[k + 1], ws.at[k, cut:], w_sem.at[k]).start()

    pre[...] = jnp.zeros_like(pre)

    def gather(k, total):
        x_copy(k).wait()
        pltpu.make_async_copy(ws.at[k], ws.at[k], w_sem.at[k]).wait()
        weight = ws[k, :shard, :]
        gain = ws[k, shard : shard + PAD, :shard].astype(f32)[:1]
        normed = xs[k].astype(f32) * inv[:, :1]
        hidden = (normed * gain).astype(bf16)
        pre[...] += jnp.dot(hidden, weight, preferred_element_type=f32)
        grad = (
            lax.dot_general(
                kv_grad[...], weight, (((1,), (1,)), ((), ())), preferred_element_type=f32
            )
            * gain
        )
        ng[k] = grad
        product = grad * normed
        for c in range(0, shard, HEAD):
            total = total + product[:, c : c + HEAD]
        return total

    total = lax.fori_loop(0, n, gather, jnp.zeros((rows, HEAD), f32))
    mean = jnp.sum(total, axis=1, keepdims=True) / width

    def finish(k, carry):
        scale = inv[:, :1]
        normed = xs[k].astype(f32) * scale
        out[k] = (scale * (ng[k] - normed * mean)).astype(bf16)
        o_copy(k).start()
        return carry

    lax.fori_loop(0, n, finish, 0)
    for c in range(0, kvw, HEAD):
        part = pre[:, c : c + HEAD]
        turned = pltpu.roll(part, HEAD // 2, 1)
        kv_out[:, c : c + HEAD] = (part * cosine[...] + turned * sine[...]).astype(bf16)
    kv_out[:, kvw:] = pre[:, kvw:].astype(bf16)

    def drain(k, carry):
        o_copy(k).wait()
        return carry

    lax.fori_loop(0, n, drain, 0)


def second_part(ring, tokens_in, kv_grad, inv, cosine, sine, blocks, shard):
    rows, width = tokens_in.shape
    cols = kv_grad.shape[1]
    n = ring.count
    order = [0]
    for d in range(1, ring.half):
        order += [-d, d]
    order.append(ring.half)
    whole = pl.BlockSpec(memory_space=pltpu.VMEM)
    there = pl.BlockSpec(memory_space=pl.ANY)
    return pl.pallas_call(
        functools.partial(second_kernel, n),
        in_specs=[pl.BlockSpec(memory_space=pltpu.SMEM), there]
        + [whole] * 4
        + [there] * len(blocks),
        out_specs=[whole, there],
        out_shape=[
            jax.ShapeDtypeStruct((rows, cols), bf16),
            jax.ShapeDtypeStruct((rows, width), bf16),
        ],
        scratch_shapes=[
            pltpu.VMEM((n, rows, shard), bf16),
            pltpu.VMEM((n, shard + PAD, cols), bf16),
            pltpu.VMEM((n, rows, shard), f32),
            pltpu.VMEM((rows, cols), f32),
            pltpu.VMEM((n, rows, shard), bf16),
            pltpu.SemaphoreType.DMA((n,)),
            pltpu.SemaphoreType.DMA((n,)),
            pltpu.SemaphoreType.DMA((n,)),
        ],
        compiler_params=pltpu.CompilerParams(vmem_limit_bytes=48 * 2**20),
        cost_estimate=pl.CostEstimate(
            flops=4 * rows * width * cols,
            bytes_accessed=4 * rows * width + 2 * width * cols,
            transcendentals=0,
        ),
        name="project_and_input_grad",
    )(ring.devices_at(order), tokens_in, kv_grad, inv, cosine, sine, *blocks)


def gather_blocks(ring, own, cut):
    blocks = [own]
    from_left = from_right = own
    for d in range(1, ring.half):
        from_left, from_right = ring.to_right(from_left), ring.to_left(from_right)
        blocks += [from_left, from_right]
    blocks += [ring.to_right(from_left[:cut]), ring.to_left(from_right[cut:])]
    return blocks


def scatter_terms(ring, far, near, cut):
    rest = far.shape[0] - cut
    from_left = ring.to_right(far[:cut]).astype(f32)
    from_right = ring.to_left(far[cut:]).astype(f32)
    from_left = jnp.pad(from_left, ((0, rest), (0, 0)))
    from_right = jnp.pad(from_right, ((cut, 0), (0, 0)))
    for k in range(0, 2 * (ring.half - 1), 2):
        from_left = ring.to_right((near[k] + from_left).astype(bf16)).astype(f32)
        from_right = ring.to_left((near[k + 1] + from_right).astype(bf16)).astype(f32)
    return near[-1] + from_left + from_right


def local(
    layer_input,
    norm_gain,
    kv_weight,
    kv_cotangent,
    pseudo_grad,
    outer_momentum,
    global_params,
    local_params,
):
    ring = Ring()
    tokens_in = layer_input[0]
    gain_shard = norm_gain[0]
    weight_shard = kv_weight[0]
    cotangent = kv_cotangent[0]
    rows, width = tokens_in.shape
    shard, cols = weight_shard.shape

    gain_rows = jnp.pad(gain_shard[None, :], ((0, PAD - 1), (0, cols - shard)))
    own = jnp.concatenate([weight_shard, gain_rows], axis=0)
    blocks = gather_blocks(ring, own, shard // 2)

    positions = (ring.me * rows + jnp.arange(rows, dtype=jnp.int32)) % SEQ_LEN
    cosine, sine = rope_tables(positions)
    scale = 1.0 / math.sqrt(rows * ring.count)
    kv_grad, inv, far, near = first_part(
        ring, tokens_in, cotangent, cosine, sine, shard, scale
    )
    term = scatter_terms(ring, far, near, shard // 2)
    weight_grad = term * gain_shard.astype(f32)[:, None]
    gain_grad = jnp.sum(term * weight_shard.astype(f32), axis=1)

    replicas = lax.axis_size("replica")
    average = lax.psum(pseudo_grad[0], "replica") / replicas
    momentum_new = momentum_rate * outer_momentum + average
    global_new = global_params - outer_rate * (average + momentum_rate * momentum_new)
    local_new = (
        mixing_rate * local_params[0].astype(f32) + (1.0 - mixing_rate) * global_new
    ).astype(bf16)

    kv_out, input_grad = second_part(
        ring, tokens_in, kv_grad, inv, cosine, sine, blocks, shard
    )
    return (
        kv_out[None],
        input_grad[None],
        weight_grad[None],
        gain_grad[None],
        momentum_new,
        global_new,
        local_new[None],
    )


def solution(mesh):
    in_specs = (
        P("replica", "fsdp", None),
        P("replica", "fsdp"),
        P("replica", "fsdp", None),
        P("replica", "fsdp", None),
        P("replica", "fsdp", None),
        P("fsdp", None),
        P("fsdp", None),
        P("replica", "fsdp", None),
    )
    out_specs = (
        P("replica", "fsdp", None),
        P("replica", "fsdp", None),
        P("replica", "fsdp", None),
        P("replica", "fsdp"),
        P("fsdp", None),
        P("fsdp", None),
        P("replica", "fsdp", None),
    )
    return jax.shard_map(local, mesh=mesh, in_specs=in_specs, out_specs=out_specs, check_vma=False)
```

time: 451 us -> 230 us (0.51)
  waiting for transfers between devices: 311 us -> 135 us
  blocking collectives: 60.5 us -> 0 us
  matrix products: 30.4 us -> 0 us
  Pallas kernels: 0 us -> 28.6 us
  starting transfers between devices: 0.12 us -> 17 us
    reduce_scatter x1 -> x0, waiting for transfers between devices: 216 us -> none  [local(): lax.psum_scatter(weight_term, 'fsdp', scatter_dimension=0, tiled=True)]
    ppermute x0 -> x16, waiting for transfers between devices: none -> 135 us  [the longest x8 89.7 us: to_right(): return lax.ppermute(value, 'fsdp', self.right)]
    all_gather x1 -> x0, waiting for transfers between devices: 94.3 us -> none  [local(): lax.all_gather(weight_shard, 'fsdp', axis=0, tiled=True)]
    unnamed x1 -> x0, blocking collectives: 35.2 us -> none
    dot_general x3 -> x0, matrix products: 30.4 us -> none  [the longest x1 13.9 us: backward_piece(): lax.dot_general(kv_grad, weight_piece, (((1,), (1,)), ((), ())), preferre...]
    pallas_call x0 -> x2, Pallas kernels: none -> 28.6 us  [the longest x1 16.6 us: second_part(): pl.pallas_call(functools.partial(second_kernel, n), in_specs=[pl.BlockSpe...]
    all_gather x1 -> x0, blocking collectives: 25.3 us -> none  [local(): lax.all_gather(gain_shard, 'fsdp', axis=0, tiled=True)]
    ppermute x0 -> x16, starting transfers between devices: none -> 17 us  [the longest x8 13.3 us: to_right(): return lax.ppermute(value, 'fsdp', self.right)]
  transfers between devices with their start and end apart: 3 -> 17, of which waited for: 2 -> 10; matrix products, arithmetic and copies ran while one was open for 13% -> 9% of each run, Pallas kernels for 0% -> 7%
where the time goes in v2:
time: 230 us; the launch traced here: 227 us
  waiting for transfers between devices  135 us (59%)
  Pallas kernels  28.6 us (12%)
  other arithmetic  26.2 us (11%)
  starting transfers between devices  17 us (7%)
  between operations  14.2 us (6%)
  local copies, waits for them, and re-layouts  6.11 us (3%)
    ppermute x8, waiting for transfers between devices, to_right(): return lax.ppermute(value, 'fsdp', self.right)  89.7 us
    ppermute x8, waiting for transfers between devices, to_left(): return lax.ppermute(value, 'fsdp', self.left)  45.7 us
    pallas_call x1, Pallas kernels, second_part(): pl.pallas_call(functools.partial(second_kernel, n), in_specs=[pl.BlockSpe...  16.6 us
    ppermute x8, starting transfers between devices, to_right(): return lax.ppermute(value, 'fsdp', self.right)  13.3 us
    pallas_call x1, Pallas kernels, first_part(): pl.pallas_call(functools.partial(first_kernel, scale), grid_spec=pltpu.Pr...  12 us
    convert_element_type x3, other arithmetic, scatter_terms(): from_left = ring.to_right((near[k] + from_left).astype(bf16)).astype(f32)  7.66 us
    convert_element_type x2, other arithmetic, scatter_terms(): (near[k + 1] + from_right).astype(bf16)  6.18 us
    broadcast_in_dim x1, other arithmetic, local(): local_new[None]  5.6 us
  transfers between devices with their start and end apart: 17, of which 10 were waited for; matrix products, arithmetic and copies ran while one was open for 9% of the time, Pallas kernels for 7%

profile of v2, /device:TPU:8, one launch (start us, length us, event | category | flops | bytes accessed | tf_op | source)
XLA Modules:
  0.0 227.5 jit_solution(9264631135942378599)
XLA Ops:
  7.2 0.0 all-reduce.5.cloned.1.call-start
  7.3 0.7 compare_select_fusion.4.at
  8.0 1.0 fusion.12
  9.0 0.2 pad_maximum_fusion
  9.3 0.0 copy-start
  9.3 2.2 copy-done
  11.4 12.0 %norm_and_weight_terms.1 = (bf16[512,1024]{1,0:T(8,128)(2,1)S(1)}, f32[512,128]{1,0:T(8,128)S(1)}, bf16[512,1024]{1,0:T(8,128)(2,1)S(1)}, f32[7,512,1024]{2,1,0:T(8,128)}) custom-call(s32[8]{0:T(128)S(1)} %compare_select_fusion.4.at, bf16[512,4096]{1,0:T(8,128)(2,1)S(1)} %bitcast.49, bf16[512,1024]{1,0:T(8,128)(2,1)S(1)} %bitcast.50, ...), custom_call_target="tpu_custom_call" | custom-call | flops 4294967296 | bytes 20971520 | tf_op jit(solution)/shard_map/norm_and_weight_terms/pallas_call | solution.py:103
  23.4 0.1 fusion.17
  23.5 0.0 copy-start.6
  23.5 0.0 copy-start.8
  23.5 1.6 collective-permute-start.8
  25.2 12.1 %collective-permute-done.8 = bf16[256,1024]{1,0:T(8,128)(2,1)S(1)} collective-permute-done((bf16[256,1024]{1,0:T(8,128)(2,1)S(1)}, bf16[256,1024]{1,0:T(8,128)(2,1)S(1)}, u32[]{:S(2)}, u32[]{:S(2)}) %collective-permute-start.8) | collective-permute-done | bytes 524320 | tf_op jit(solution)/shard_map/ppermute | solution.py:43
  37.3 1.8 fusion.4
  39.1 1.6 collective-permute-start.9
  40.7 0.1 fusion.10.refs_0_
  40.8 0.5 collective-permute-start.1
  41.3 1.6 collective-permute-start
  42.9 22.4 %collective-permute-done.9 = bf16[512,1024]{1,0:T(8,128)(2,1)S(1)} collective-permute-done((bf16[512,1024]{1,0:T(8,128)(2,1)S(1)}, bf16[512,1024]{1,0:T(8,128)(2,1)S(1)}, u32[]{:S(2)}, u32[]{:S(2)}) %collective-permute-start.9) | collective-permute-done | bytes 1048608 | tf_op jit(solution)/shard_map/ppermute | solution.py:43
  65.3 2.0 fusion.5
  67.2 1.6 collective-permute-start.10
  68.9 0.4 collective-permute-start.12
  69.3 0.2 collective-permute-start.3
  69.5 18.9 %collective-permute-done.refs_1_ = bf16[528,1024]{1,0:T(8,128)(2,1)S(1)} collective-permute-done((bf16[528,1024]{1,0:T(8,128)(2,1)S(1)}, bf16[528,1024]{1,0:T(8,128)(2,1)S(1)}, u32[]{:S(2)}, u32[]{:S(2)}) %collective-permute-start) | collective-permute-done | bytes 1081376 | tf_op jit(solution)/shard_map/ppermute | solution.py:43
  88.4 1.6 collective-permute-start.2
  90.0 20.9 %collective-permute-done.10 = bf16[512,1024]{1,0:T(8,128)(2,1)S(1)} collective-permute-done((bf16[512,1024]{1,0:T(8,128)(2,1)S(1)}, bf16[512,1024]{1,0:T(8,128)(2,1)S(1)}, u32[]{:S(2)}, u32[]{:S(2)}) %collective-permute-start.10) | collective-permute-done | bytes 1048608 | tf_op jit(solution)/shard_map/ppermute | solution.py:43
  110.9 3.9 %fusion.6 = (bf16[512,1024]{1,0:T(8,128)(2,1)}, bf16[512,1024]{1,0:T(8,128)(2,1)S(1)}) fusion(bf16[512,1024]{1,0:T(8,128)(2,1)S(1)} %collective-permute-done.10, f32[7,512,1024]{2,1,0:T(8,128)} %get-tuple-element.17, bf16[256,1024]{1,0:T(8,128)(2,1)S(1)} %collective-permute-done.12), kind=kLoop, calls=%fused_computation.13 | loop fusion | flops 3145728 | bytes 7864320 | tf_op jit(solution)/shard_map/convert_element_type | solution.py:266
  114.8 0.2 collective-permute-start.13
  115.0 1.7 collective-permute-start.5
  116.7 15.4 %collective-permute-done.2.refs_3_ = bf16[528,1024]{1,0:T(8,128)(2,1)} collective-permute-done((bf16[528,1024]{1,0:T(8,128)(2,1)S(1)}, bf16[528,1024]{1,0:T(8,128)(2,1)}, u32[]{:S(2)}, u32[]{:S(2)}) %collective-permute-start.2) | collective-permute-done | bytes 1081376 | tf_op jit(solution)/shard_map/ppermute | solution.py:43
  132.1 1.6 collective-permute-start.4
  133.7 7.2 %collective-permute-done.13 = bf16[512,1024]{1,0:T(8,128)(2,1)S(1)} collective-permute-done((bf16[512,1024]{1,0:T(8,128)(2,1)S(1)}, bf16[512,1024]{1,0:T(8,128)(2,1)S(1)}, u32[]{:S(2)}, u32[]{:S(2)}) %collective-permute-start.13) | collective-permute-done | bytes 1048608 | tf_op jit(solution)/shard_map/ppermute | solution.py:46
  140.9 2.9 %fusion.2 = bf16[512,1024]{1,0:T(8,128)(2,1)} fusion(bf16[512,1024]{1,0:T(8,128)(2,1)S(1)} %collective-permute-done.13, f32[7,512,1024]{2,1,0:T(8,128)} %get-tuple-element.17), kind=kLoop, calls=%fused_computation.5 | loop fusion | flops 1572864 | bytes 4194304 | tf_op jit(solution)/shard_map/convert_element_type | solution.py:267
  143.8 0.2 collective-permute-start.14
  144.0 0.0 all-reduce.5.cloned.1.call-update
  144.0 1.9 collective-permute-start.11
  145.9 18.2 %collective-permute-done.5.refs_6_ = bf16[528,1024]{1,0:T(8,128)(2,1)} collective-permute-done((bf16[528,1024]{1,0:T(8,128)(2,1)}, bf16[528,1024]{1,0:T(8,128)(2,1)}, u32[]{:S(2)}, u32[]{:S(2)}) %collective-permute-start.5) | collective-permute-done | bytes 1081376 | tf_op jit(solution)/shard_map/ppermute | solution.py:46
  164.1 1.9 slice.45
  166.0 0.2 collective-permute-start.7
  166.2 1.9 slice.44
  168.1 1.8 collective-permute-start.6
  170.0 16.6 %collective-permute-done.14 = bf16[512,1024]{1,0:T(8,128)(2,1)} collective-permute-done((bf16[512,1024]{1,0:T(8,128)(2,1)}, bf16[512,1024]{1,0:T(8,128)(2,1)}, u32[]{:S(2)}, u32[]{:S(2)}) %collective-permute-start.14) | collective-permute-done | bytes 1048608 | tf_op jit(solution)/shard_map/ppermute | solution.py:46
  186.6 3.3 %fusion.3 = bf16[512,1024]{1,0:T(8,128)(2,1)} fusion(bf16[512,1024]{1,0:T(8,128)(2,1)} %collective-permute-done.14, f32[7,512,1024]{2,1,0:T(8,128)} %get-tuple-element.17), kind=kLoop, calls=%fused_computation.7 | loop fusion | flops 1572864 | bytes 4194304 | tf_op jit(solution)/shard_map/convert_element_type | solution.py:267
  189.9 0.2 collective-permute-start.15
  190.1 5.6 %fusion.11 = (bf16[1,384,1024]{2,1,0:T(8,128)(2,1)}, f32[384,1024]{1,0:T(8,128)}, f32[384,1024]{1,0:T(8,128)}) fusion(bf16[1,384,1024]{2,1,0:T(8,128)(2,1)} %param.17, f32[384,1024]{1,0:T(8,128)} %param.16, f32[384,1024]{1,0:T(8,128)} %all-reduce.5.cloned.1.call-done, f32[384,1024]{1,0:T(8,128)} %param.15), kind=kLoop, calls=%fused_computation.24 | loop fusion | flops 4325376 | bytes 9437184 | tf_op jit(solution)/shard_map/broadcast_in_dim | solution.py:321
  195.7 2.8 %collective-permute-done.7.refs_8_ = bf16[272,1024]{1,0:T(8,128)(2,1)S(1)} collective-permute-done((bf16[272,1024]{1,0:T(8,128)(2,1)}, bf16[272,1024]{1,0:T(8,128)(2,1)S(1)}, u32[]{:S(2)}, u32[]{:S(2)}) %collective-permute-start.7) | collective-permute-done | bytes 557088 | tf_op jit(solution)/shard_map/ppermute | solution.py:46
  198.4 16.6 %project_and_input_grad.1 = (bf16[512,1024]{1,0:T(8,128)(2,1)}, bf16[512,4096]{1,0:T(8,128)(2,1)}) custom-call(s32[8]{0:T(128)S(1)} %compare_select_fusion.5.at, bf16[512,4096]{1,0:T(8,128)(2,1)} %bitcast.48, bf16[512,1024]{1,0:T(8,128)(2,1)S(1)} %copy-done.5, f32[512,128]{1,0:T(8,128)S(1)} %get-tuple-element.14.inv, ...), custom_call_target="tpu_custom_call" | custom-call | flops 8589934592 | bytes 16777216 | tf_op jit(solution)/shard_map/project_and_input_grad/pallas_call | solution.py:219
  215.0 0.9 collective-permute-done.15
  216.0 4.7 %multiply_reduce_fusion = (f32[512]{0:T(512)}, f32[1,512,1024]{2,1,0:T(8,128)}) fusion(bf16[512,1024]{1,0:T(8,128)(2,1)} %collective-permute-done.15, bf16[512,1024]{1,0:T(8,128)(2,1)} %collective-permute-done.11, f32[7,512,1024]{2,1,0:T(8,128)} %get-tuple-element.17, bf16[1,512,1024]{2,1,0:T(8,128)(2,1)S(1)} %copy-done.7, f32[512]{0:T(512)S(1)} %bitcast.53), kind=kLoop, calls=%fused_computation.16 | loop fusion | flops 4193792 | bytes 7344128 | tf_op jit(solution)/shard_map/reduce_sum | solution.py:301
  (27 shorter events, 0.1 us)
Async XLA Ops:
  7.2 2.1 copy-start.3
  7.2 182.9 %all-reduce.5.cloned.1.call-start = ((), (), s32[]{:S(2)}) async-start(), calls=%async_computation | async-start | bytes 3145728 | tf_op jit(solution)/shard_map/psum | solution.py:304
  9.3 2.2 copy-start
  23.4 15.7 %copy-start.4 = (bf16[512,1024]{1,0:T(8,128)(2,1)}, bf16[512,1024]{1,0:T(8,128)(2,1)S(1)}, u32[]{:S(2)}) copy-start(bf16[512,1024]{1,0:T(8,128)(2,1)S(1)} %get-tuple-element.13.kv_grad) | copy-start | bytes 3145732
  23.5 17.2 %copy-start.6 = (bf16[1,512,1024]{2,1,0:T(8,128)(2,1)S(1)}, bf16[1,512,1024]{2,1,0:T(8,128)(2,1)}, u32[]{:S(2)}) copy-start(bf16[1,512,1024]{2,1,0:T(8,128)(2,1)} %param.12) | copy-start | bytes 3145732
  23.5 17.2 %copy-start.8 = (bf16[1,512]{1,0:T(2,128)(2,1)S(1)}, bf16[1,512]{1,0:T(2,128)(2,1)}, u32[]{:S(2)}) copy-start(bf16[1,512]{1,0:T(2,128)(2,1)} %param.11) | copy-start | bytes 3076
  23.5 13.7 %collective-permute-start.8 = (bf16[256,1024]{1,0:T(8,128)(2,1)S(1)}, bf16[256,1024]{1,0:T(8,128)(2,1)S(1)}, u32[]{:S(2)}, u32[]{:S(2)}) collective-permute-start(bf16[256,1024]{1,0:T(8,128)(2,1)S(1)} %get-tuple-element.26), channel_id=1, source_target_pairs={{0,2},{2,4},{4,6},{6,7},{7,5},{5,3},{3,1},{1,0},{8,10},{10,12},{12... | collective-permute-start | bytes 1572872 | tf_op jit(solution)/shard_map/ppermute | solution.py:43
  39.1 26.1 %collective-permute-start.9 = (bf16[512,1024]{1,0:T(8,128)(2,1)S(1)}, bf16[512,1024]{1,0:T(8,128)(2,1)S(1)}, u32[]{:S(2)}, u32[]{:S(2)}) collective-permute-start(bf16[512,1024]{1,0:T(8,128)(2,1)S(1)} %fusion.4), channel_id=1, source_target_pairs={{0,2},{2,4},{4,6},{6,7},{7,5},{5,3},{3,1},{1,0},{8,10},{10,12},{12... | collective-permute-start | bytes 3145736 | tf_op jit(solution)/shard_map/ppermute | solution.py:43
  40.8 28.5 %collective-permute-start.1 = (bf16[528,1024]{1,0:T(8,128)(2,1)S(1)}, bf16[528,1024]{1,0:T(8,128)(2,1)S(1)}, u32[]{:S(2)}, u32[]{:S(2)}) collective-permute-start(bf16[528,1024]{1,0:T(8,128)(2,1)S(1)} %fusion.10.refs_0_), channel_id=1, source_target_pairs={{2,0},{4,2},{6,4},{7,6},{5,7},{3,5},{1,3},{0,1},{10,8},{12,10},{14... | collective-permute-start | bytes 3244040 | tf_op jit(solution)/shard_map/ppermute | solution.py:46
  41.3 47.1 %collective-permute-start = (bf16[528,1024]{1,0:T(8,128)(2,1)S(1)}, bf16[528,1024]{1,0:T(8,128)(2,1)S(1)}, u32[]{:S(2)}, u32[]{:S(2)}) collective-permute-start(bf16[528,1024]{1,0:T(8,128)(2,1)S(1)} %fusion.10.refs_0_), channel_id=1, source_target_pairs={{0,2},{2,4},{4,6},{6,7},{7,5},{5,3},{3,1},{1,0},{8,10},{10,12},{12... | collective-permute-start | bytes 3244040 | tf_op jit(solution)/shard_map/ppermute | solution.py:43
  67.2 43.7 %collective-permute-start.10 = (bf16[512,1024]{1,0:T(8,128)(2,1)S(1)}, bf16[512,1024]{1,0:T(8,128)(2,1)S(1)}, u32[]{:S(2)}, u32[]{:S(2)}) collective-permute-start(bf16[512,1024]{1,0:T(8,128)(2,1)S(1)} %fusion.5), channel_id=1, source_target_pairs={{0,2},{2,4},{4,6},{6,7},{7,5},{5,3},{3,1},{1,0},{8,10},{10,12},{12... | collective-permute-start | bytes 3145736 | tf_op jit(solution)/shard_map/ppermute | solution.py:43
  68.9 21.1 %collective-permute-start.12 = (bf16[256,1024]{1,0:T(8,128)(2,1)S(1)}, bf16[256,1024]{1,0:T(8,128)(2,1)S(1)}, u32[]{:S(2)}, u32[]{:S(2)}) collective-permute-start(bf16[256,1024]{1,0:T(8,128)(2,1)S(1)} %get-tuple-element.27), channel_id=1, source_target_pairs={{2,0},{4,2},{6,4},{7,6},{5,7},{3,5},{1,3},{0,1},{10,8},{12,10},{14... | collective-permute-start | bytes 1572872 | tf_op jit(solution)/shard_map/ppermute | solution.py:46
  69.3 45.6 %collective-permute-start.3 = (bf16[528,1024]{1,0:T(8,128)(2,1)S(1)}, bf16[528,1024]{1,0:T(8,128)(2,1)}, u32[]{:S(2)}, u32[]{:S(2)}) collective-permute-start(bf16[528,1024]{1,0:T(8,128)(2,1)S(1)} %collective-permute-done.1.refs_2_), channel_id=1, source_target_pairs={{2,0},{4,2},{6,4},{7,6},{5,7},{3,5},{1,3},{0,1},{10,8},{12,10},{14... | collective-permute-start | bytes 3244040 | tf_op jit(solution)/shard_map/ppermute | solution.py:46
  88.4 26.3 %copy-start.1 = (bf16[528,1024]{1,0:T(8,128)(2,1)}, bf16[528,1024]{1,0:T(8,128)(2,1)S(1)}, u32[]{:S(2)}) copy-start(bf16[528,1024]{1,0:T(8,128)(2,1)S(1)} %collective-permute-done.refs_1_) | copy-start | bytes 3244036
  88.4 43.7 %collective-permute-start.2 = (bf16[528,1024]{1,0:T(8,128)(2,1)S(1)}, bf16[528,1024]{1,0:T(8,128)(2,1)}, u32[]{:S(2)}, u32[]{:S(2)}) collective-permute-start(bf16[528,1024]{1,0:T(8,128)(2,1)S(1)} %collective-permute-done.refs_1_), channel_id=1, source_target_pairs={{0,2},{2,4},{4,6},{6,7},{7,5},{5,3},{3,1},{1,0},{8,10},{10,12},{12... | collective-permute-start | bytes 3244040 | tf_op jit(solution)/shard_map/ppermute | solution.py:43
  114.8 29.2 %copy-start.9 = (s32[8]{0:T(128)S(1)}, s32[8]{0:T(128)}, u32[]{:S(2)}) copy-start(s32[8]{0:T(128)} %constant.94.clone) | copy-start | bytes 100
  114.8 26.1 %collective-permute-start.13 = (bf16[512,1024]{1,0:T(8,128)(2,1)S(1)}, bf16[512,1024]{1,0:T(8,128)(2,1)S(1)}, u32[]{:S(2)}, u32[]{:S(2)}) collective-permute-start(bf16[512,1024]{1,0:T(8,128)(2,1)S(1)} %get-tuple-element.25), channel_id=1, source_target_pairs={{2,0},{4,2},{6,4},{7,6},{5,7},{3,5},{1,3},{0,1},{10,8},{12,10},{14... | collective-permute-start | bytes 3145736 | tf_op jit(solution)/shard_map/ppermute | solution.py:46
  115.0 49.2 %collective-permute-start.5 = (bf16[528,1024]{1,0:T(8,128)(2,1)}, bf16[528,1024]{1,0:T(8,128)(2,1)}, u32[]{:S(2)}, u32[]{:S(2)}) collective-permute-start(bf16[528,1024]{1,0:T(8,128)(2,1)} %collective-permute-done.3.refs_4_), channel_id=1, source_target_pairs={{2,0},{4,2},{6,4},{7,6},{5,7},{3,5},{1,3},{0,1},{10,8},{12,10},{14... | collective-permute-start | bytes 3244040 | tf_op jit(solution)/shard_map/ppermute | solution.py:46
  132.1 34.1 %collective-permute-start.4 = (bf16[528,1024]{1,0:T(8,128)(2,1)}, bf16[528,1024]{1,0:T(8,128)(2,1)}, u32[]{:S(2)}, u32[]{:S(2)}) collective-permute-start(bf16[528,1024]{1,0:T(8,128)(2,1)} %collective-permute-done.2.refs_3_), channel_id=1, source_target_pairs={{0,2},{2,4},{4,6},{6,7},{7,5},{5,3},{3,1},{1,0},{8,10},{10,12},{12... | collective-permute-start | bytes 3244040 | tf_op jit(solution)/shard_map/ppermute | solution.py:43
  143.8 42.8 %collective-permute-start.14 = (bf16[512,1024]{1,0:T(8,128)(2,1)}, bf16[512,1024]{1,0:T(8,128)(2,1)}, u32[]{:S(2)}, u32[]{:S(2)}) collective-permute-start(bf16[512,1024]{1,0:T(8,128)(2,1)} %fusion.2), channel_id=1, source_target_pairs={{2,0},{4,2},{6,4},{7,6},{5,7},{3,5},{1,3},{0,1},{10,8},{12,10},{14... | collective-permute-start | bytes 3145736 | tf_op jit(solution)/shard_map/ppermute | solution.py:46
  144.0 71.0 %collective-permute-start.11 = (bf16[512,1024]{1,0:T(8,128)(2,1)}, bf16[512,1024]{1,0:T(8,128)(2,1)}, u32[]{:S(2)}, u32[]{:S(2)}) collective-permute-start(bf16[512,1024]{1,0:T(8,128)(2,1)} %get-tuple-element.24), channel_id=1, source_target_pairs={{0,2},{2,4},{4,6},{6,7},{7,5},{5,3},{3,1},{1,0},{8,10},{10,12},{12... | collective-permute-start | bytes 3145736 | tf_op jit(solution)/shard_map/ppermute | solution.py:43
  166.0 32.4 %collective-permute-start.7 = (bf16[272,1024]{1,0:T(8,128)(2,1)}, bf16[272,1024]{1,0:T(8,128)(2,1)S(1)}, u32[]{:S(2)}, u32[]{:S(2)}) collective-permute-start(bf16[272,1024]{1,0:T(8,128)(2,1)} %slice.45), channel_id=1, source_target_pairs={{2,0},{4,2},{6,4},{7,6},{5,7},{3,5},{1,3},{0,1},{10,8},{12,10},{14... | collective-permute-start | bytes 1671176 | tf_op jit(solution)/shard_map/ppermute | solution.py:46
  168.1 27.5 %collective-permute-start.6 = (bf16[256,1024]{1,0:T(8,128)(2,1)}, bf16[256,1024]{1,0:T(8,128)(2,1)}, u32[]{:S(2)}, u32[]{:S(2)}) collective-permute-start(bf16[256,1024]{1,0:T(8,128)(2,1)} %slice.44), channel_id=1, source_target_pairs={{0,2},{2,4},{4,6},{6,7},{7,5},{5,3},{3,1},{1,0},{8,10},{10,12},{12... | collective-permute-start | bytes 1572872 | tf_op jit(solution)/shard_map/ppermute | solution.py:43
  189.9 26.1 %collective-permute-start.15 = (bf16[512,1024]{1,0:T(8,128)(2,1)}, bf16[512,1024]{1,0:T(8,128)(2,1)}, u32[]{:S(2)}, u32[]{:S(2)}) collective-permute-start(bf16[512,1024]{1,0:T(8,128)(2,1)} %fusion.3), channel_id=1, source_target_pairs={{2,0},{4,2},{6,4},{7,6},{5,7},{3,5},{1,3},{0,1},{10,8},{12,10},{14... | collective-permute-start | bytes 3145736 | tf_op jit(solution)/shard_map/ppermute | solution.py:46
  190.1 8.4 %copy-start.2 = (bf16[528,1024]{1,0:T(8,128)(2,1)S(1)}, bf16[528,1024]{1,0:T(8,128)(2,1)}, u32[]{:S(2)}) copy-start(bf16[528,1024]{1,0:T(8,128)(2,1)} %copy-done.1) | copy-start | bytes 3244036
  190.1 8.4 %copy-start.5 = (bf16[512,1024]{1,0:T(8,128)(2,1)S(1)}, bf16[512,1024]{1,0:T(8,128)(2,1)}, u32[]{:S(2)}) copy-start(bf16[512,1024]{1,0:T(8,128)(2,1)} %copy-done.4) | copy-start | bytes 3145732
  198.4 17.5 %copy-start.7 = (bf16[1,512,1024]{2,1,0:T(8,128)(2,1)S(1)}, bf16[1,512,1024]{2,1,0:T(8,128)(2,1)}, u32[]{:S(2)}) copy-start(bf16[1,512,1024]{2,1,0:T(8,128)(2,1)} %param.12) | copy-start | bytes 3145732
Sparse Core Ops, SparseCore 0:
  144.1 44.3 all-reduce.4

commit v3 on v2

--- a/solution.py
+++ b/solution.py
@@ -46,6 +46,10 @@
         return lax.ppermute(value, "fsdp", self.left)
 
 
+def after(value, *others):
+    return lax.optimization_barrier((value, others))[0]
+
+
 def rope_tables(positions):
     half = HEAD // 2
     index_f = jnp.arange(half, dtype=f32)
@@ -55,10 +59,10 @@
     return jnp.concatenate([cosine, cosine], axis=1), jnp.concatenate([-sine, sine], axis=1)
 
 
-def first_kernel(scale, at, x, cotangent, cosine, sine, kv_grad, inv, far, near):
+def first_kernel(scale, at, x, cotangent, cosine, sine, kv_grad, inv, top, bottom, near):
     step = pl.program_id(0)
     width = x.shape[1]
-    shard = far.shape[0]
+    shard, cut = near.shape[1], top.shape[0]
     kvw = cotangent.shape[1] // 2
 
     @pl.when(step == 0)
@@ -84,7 +88,8 @@
 
     @pl.when(step == 0)
     def _():
-        far[...] = term.astype(bf16)
+        top[...] = term[:cut].astype(bf16)
+        bottom[...] = term[cut:].astype(bf16)
 
     @pl.when(step > 0)
     def _():
@@ -114,14 +119,16 @@
             out_specs=[
                 pl.BlockSpec((rows, cols), fixed),
                 pl.BlockSpec((rows, HEAD), fixed),
-                pl.BlockSpec((shard, cols), fixed),
+                pl.BlockSpec((shard // 2, cols), fixed),
+                pl.BlockSpec((shard - shard // 2, cols), fixed),
                 pl.BlockSpec((1, shard, cols), lambda k, at: (jnp.maximum(k - 1, 0), 0, 0)),
             ],
         ),
         out_shape=[
             jax.ShapeDtypeStruct((rows, cols), bf16),
             jax.ShapeDtypeStruct((rows, HEAD), f32),
-            jax.ShapeDtypeStruct((shard, cols), bf16),
+            jax.ShapeDtypeStruct((shard // 2, cols), bf16),
+            jax.ShapeDtypeStruct((shard - shard // 2, cols), bf16),
             jax.ShapeDtypeStruct((n - 1, shard, cols), f32),
         ],
         compiler_params=pltpu.CompilerParams(vmem_limit_bytes=40 * 2**20),
@@ -246,25 +253,40 @@
     )(ring.devices_at(order), tokens_in, kv_grad, inv, cosine, sine, *blocks)
 
 
-def gather_blocks(ring, own, cut):
+def replica_sum(value):
+    replicas = lax.axis_size("replica")
+    if replicas & (replicas - 1):
+        return lax.psum(value, "replica")
+    step = 1
+    while step < replicas:
+        pairs = [(r, r ^ step) for r in range(replicas)]
+        value = value + lax.ppermute(value, "replica", pairs)
+        step *= 2
+    return value
+
+
+def gather_blocks(ring, own, cut, other):
     blocks = [own]
     from_left = from_right = own
     for d in range(1, ring.half):
         from_left, from_right = ring.to_right(from_left), ring.to_left(from_right)
         blocks += [from_left, from_right]
+    from_left, from_right = after(from_left, other), after(from_right, other)
     blocks += [ring.to_right(from_left[:cut]), ring.to_left(from_right[cut:])]
     return blocks
 
 
-def scatter_terms(ring, far, near, cut):
-    rest = far.shape[0] - cut
-    from_left = ring.to_right(far[:cut]).astype(f32)
-    from_right = ring.to_left(far[cut:]).astype(f32)
-    from_left = jnp.pad(from_left, ((0, rest), (0, 0)))
-    from_right = jnp.pad(from_right, ((cut, 0), (0, 0)))
+def scatter_terms(ring, top, bottom, near):
+    cut, rest = top.shape[0], bottom.shape[0]
+    from_left, from_right = ring.to_right(top), ring.to_left(bottom)
     for k in range(0, 2 * (ring.half - 1), 2):
-        from_left = ring.to_right((near[k] + from_left).astype(bf16)).astype(f32)
-        from_right = ring.to_left((near[k + 1] + from_right).astype(bf16)).astype(f32)
+        from_left, from_right = lax.optimization_barrier((from_left, from_right))
+        if k == 0:
+            from_left = jnp.pad(from_left, ((0, rest), (0, 0)))
+            from_right = jnp.pad(from_right, ((cut, 0), (0, 0)))
+        from_left = ring.to_right((near[k] + from_left.astype(f32)).astype(bf16))
+        from_right = ring.to_left((near[k + 1] + from_right.astype(f32)).astype(bf16))
+    from_left, from_right = from_left.astype(f32), from_right.astype(f32)
     return near[-1] + from_left + from_right
 
 
@@ -288,20 +310,22 @@
 
     gain_rows = jnp.pad(gain_shard[None, :], ((0, PAD - 1), (0, cols - shard)))
     own = jnp.concatenate([weight_shard, gain_rows], axis=0)
-    blocks = gather_blocks(ring, own, shard // 2)
+    total = replica_sum(pseudo_grad[0])
+    blocks = gather_blocks(ring, own, shard // 2, total)
 
     positions = (ring.me * rows + jnp.arange(rows, dtype=jnp.int32)) % SEQ_LEN
     cosine, sine = rope_tables(positions)
     scale = 1.0 / math.sqrt(rows * ring.count)
-    kv_grad, inv, far, near = first_part(
+    kv_grad, inv, top, bottom, near = first_part(
         ring, tokens_in, cotangent, cosine, sine, shard, scale
     )
-    term = scatter_terms(ring, far, near, shard // 2)
+    top, bottom = after((top, bottom), blocks[1], blocks[2])
+    term = scatter_terms(ring, top, bottom, near)
     weight_grad = term * gain_shard.astype(f32)[:, None]
     gain_grad = jnp.sum(term * weight_shard.astype(f32), axis=1)
 
     replicas = lax.axis_size("replica")
-    average = lax.psum(pseudo_grad[0], "replica") / replicas
+    average = total / replicas
     momentum_new = momentum_rate * outer_momentum + average
     global_new = global_params - outer_rate * (average + momentum_rate * momentum_new)
     local_new = (

time: 230 us -> 174 us (0.76)
  waiting for transfers between devices: 135 us -> 102 us
  between operations: 14.2 us -> 0.87 us
  other arithmetic: 26.2 us -> 20.5 us
  local copies, waits for them, and re-layouts: 6.11 us -> 2.32 us
    ppermute x8, waiting for transfers between devices: 89.7 us -> 62.1 us  [to_right(): return lax.ppermute(value, 'fsdp', self.right)]
    ppermute x8, waiting for transfers between devices: 45.7 us -> 40.1 us  [to_left(): return lax.ppermute(value, 'fsdp', self.left)]
    convert_element_type x5 -> x3, other arithmetic: 13.8 us -> 8.91 us  [the longest x2 5.83 us: scatter_terms(): (near[k + 1] + from_right.astype(f32)).astype(bf16)]
    slice x2, local copies, waits for them, and re-layouts: 3.82 us -> 0.07 us  [gather_blocks(): blocks += [ring.to_right(from_left[:cut]), ring.to_left(from_right[cut:])]]
    broadcast_in_dim x1, other arithmetic: 5.6 us -> 2.69 us  [local(): local_new[None]]
  transfers between devices with their start and end apart: 17 -> 18, of which waited for: 10 -> 14; matrix products, arithmetic and copies ran while one was open for 9% -> 9% of each run, Pallas kernels for 7% -> 17%
where the time goes in v3:
time: 174 us; the launch traced here: 172 us
  waiting for transfers between devices  102 us (59%)
  Pallas kernels  28.6 us (16%)
  other arithmetic  20.5 us (12%)
  starting transfers between devices  18.1 us (10%)
  local copies, waits for them, and re-layouts  2.32 us (1%)
    ppermute x8, waiting for transfers between devices, to_right(): return lax.ppermute(value, 'fsdp', self.right)  62.1 us
    ppermute x8, waiting for transfers between devices, to_left(): return lax.ppermute(value, 'fsdp', self.left)  40.1 us
    pallas_call x1, Pallas kernels, second_part(): pl.pallas_call(functools.partial(second_kernel, n), in_specs=[pl.BlockSpe...  16.5 us
    ppermute x8, starting transfers between devices, to_right(): return lax.ppermute(value, 'fsdp', self.right)  12.7 us
    pallas_call x1, Pallas kernels, first_part(): pl.pallas_call(functools.partial(first_kernel, scale), grid_spec=pltpu.Pr...  12 us
    convert_element_type x2, other arithmetic, scatter_terms(): (near[k + 1] + from_right.astype(f32)).astype(bf16)  5.83 us
    reduce_sum x1, other arithmetic, local(): gain_grad = jnp.sum(term * weight_shard.astype(f32), axis=1)  4.09 us
    ppermute x8, starting transfers between devices, to_left(): return lax.ppermute(value, 'fsdp', self.left)  3.85 us
  transfers between devices with their start and end apart: 18, of which 14 were waited for; matrix products, arithmetic and copies ran while one was open for 9% of the time, Pallas kernels for 17%

profile of v3, /device:TPU:8, one launch (start us, length us, event | category | flops | bytes accessed | tf_op | source)
XLA Modules:
  0.0 172.5 jit_solution(5613661069029629021)
XLA Ops:
  0.6 0.0 copy-start.12
  0.6 1.3 fusion.10.refs_0_
  2.0 1.6 collective-permute-start
  3.6 0.4 collective-permute-start.1
  4.1 0.0 copy-start.1
  4.1 1.0 fusion.12
  5.1 0.2 pad_maximum_fusion
  5.4 0.0 copy-start
  5.4 2.2 %copy-done = bf16[1,512,4096]{2,1,0:T(8,128)(2,1)S(1)} copy-done((bf16[1,512,4096]{2,1,0:T(8,128)(2,1)S(1)}, bf16[1,512,4096]{2,1,0:T(8,128)(2,1)}, u32[]{:S(2)}) %copy-start) | copy-done | bytes 4194328
  7.5 12.0 %norm_and_weight_terms.1 = (bf16[512,1024]{1,0:T(8,128)(2,1)S(1)}, f32[512,128]{1,0:T(8,128)S(1)}, bf16[256,1024]{1,0:T(8,128)(2,1)S(1)}, bf16[256,1024]{1,0:T(8,128)(2,1)S(1)}, f32[7,512,1024]{2,1,0:T(8,128)}) custom-call(s32[8]{0:T(128)S(1)} %compare_select_fusion.4.at, bf16[512,4096]{1,0:T(8,128)(2,1)S(1)} %bitcast.50, bf16[512,1024]{1,0:T(8,128)(2,1)S(1)} %bitcast.51, ...), custom_call_target="tpu_custom_call" | custom-call | flops 4294967296 | bytes 20971520 | tf_op jit(solution)/shard_map/norm_and_weight_terms/pallas_call | solution.py:108
  19.6 8.0 %collective-permute-done.refs_1_ = bf16[528,1024]{1,0:T(8,128)(2,1)S(1)} collective-permute-done((bf16[528,1024]{1,0:T(8,128)(2,1)S(1)}, bf16[528,1024]{1,0:T(8,128)(2,1)S(1)}, u32[]{:S(2)}, u32[]{:S(2)}) %collective-permute-start) | collective-permute-done | bytes 1081376 | tf_op jit(solution)/shard_map/ppermute | solution.py:43
  27.6 1.3 collective-permute-done.1.refs_2_
  28.9 1.6 collective-permute-start.10
  30.5 0.4 collective-permute-start.11
  30.9 0.4 collective-permute-start.3
  31.4 1.6 collective-permute-start.2
  33.0 10.8 %collective-permute-done.10 = bf16[256,1024]{1,0:T(8,128)(2,1)S(1)} collective-permute-done((bf16[256,1024]{1,0:T(8,128)(2,1)S(1)}, bf16[256,1024]{1,0:T(8,128)(2,1)S(1)}, u32[]{:S(2)}, u32[]{:S(2)}) %collective-permute-start.10) | collective-permute-done | bytes 524320 | tf_op jit(solution)/shard_map/ppermute | solution.py:43
  43.8 1.6 collective-permute-done.11
  45.4 2.8 %fusion.3 = (bf16[512,1024]{1,0:T(8,128)(2,1)S(1)}, bf16[512,1024]{1,0:T(8,128)(2,1)S(1)}) fusion(f32[7,512,1024]{2,1,0:T(8,128)} %get-tuple-element.30, bf16[256,1024]{1,0:T(8,128)(2,1)S(1)} %collective-permute-done.11, bf16[256,1024]{1,0:T(8,128)(2,1)S(1)} %collective-permute-done.10), kind=kLoop, calls=%fused_computation.7 | loop fusion | flops 3145728 | bytes 7340032 | tf_op jit(solution)/shard_map/convert_element_type | solution.py:288
  48.2 1.6 collective-permute-start.12
  49.7 0.5 collective-permute-start.13
  50.3 2.2 %bitcast_add_fusion.7 = f32[384,1024]{1,0:T(8,128)S(1)} fusion(f32[384,1024]{1,0:T(8,128)} %collective-permute-done.6, f32[1,384,1024]{2,1,0:T(8,128)} %param.14), kind=kLoop, calls=%fused_computation.46 | loop fusion | flops 393216 | bytes 4718592 | tf_op jit(solution)/shard_map/add | solution.py:263
  52.5 0.0 copy-start.5
  52.5 1.6 collective-permute-start.7
  54.1 14.4 %collective-permute-done.3.refs_4_ = bf16[528,1024]{1,0:T(8,128)(2,1)S(1)} collective-permute-done((bf16[528,1024]{1,0:T(8,128)(2,1)S(1)}, bf16[528,1024]{1,0:T(8,128)(2,1)S(1)}, u32[]{:S(2)}, u32[]{:S(2)}) %collective-permute-start.3) | collective-permute-done | bytes 1081376 | tf_op jit(solution)/shard_map/ppermute | solution.py:46
  68.5 0.4 collective-permute-start.5
  69.0 1.6 collective-permute-start.4
  70.6 18.9 %collective-permute-done.12 = bf16[512,1024]{1,0:T(8,128)(2,1)S(1)} collective-permute-done((bf16[512,1024]{1,0:T(8,128)(2,1)S(1)}, bf16[512,1024]{1,0:T(8,128)(2,1)S(1)}, u32[]{:S(2)}, u32[]{:S(2)}) %collective-permute-start.12) | collective-permute-done | bytes 1048608 | tf_op jit(solution)/shard_map/ppermute | solution.py:43
  89.4 1.6 collective-permute-done.13
  91.0 3.0 %fusion.2 = (bf16[512,1024]{1,0:T(8,128)(2,1)S(1)}, bf16[512,1024]{1,0:T(8,128)(2,1)S(1)}) fusion(bf16[512,1024]{1,0:T(8,128)(2,1)S(1)} %collective-permute-done.13, f32[7,512,1024]{2,1,0:T(8,128)} %get-tuple-element.30, bf16[512,1024]{1,0:T(8,128)(2,1)S(1)} %collective-permute-done.12), kind=kLoop, calls=%fused_computation.5 | loop fusion | flops 3145728 | bytes 8388608 | tf_op jit(solution)/shard_map/convert_element_type | solution.py:288
  94.1 1.6 collective-permute-start.14
  95.6 0.5 collective-permute-start.15
  96.2 2.7 %fusion.11 = (bf16[1,384,1024]{2,1,0:T(8,128)(2,1)}, f32[384,1024]{1,0:T(8,128)}, f32[384,1024]{1,0:T(8,128)}) fusion(bf16[1,384,1024]{2,1,0:T(8,128)(2,1)S(1)} %copy-done.5, f32[384,1024]{1,0:T(8,128)S(1)} %copy-done.3, f32[384,1024]{1,0:T(8,128)S(1)} %copy-done.4, f32[384,1024]{1,0:T(8,128)S(1)} %bitcast_add_fusion.7, ...), kind=kLoop, calls=%fused_computation.24 | loop fusion | flops 4718592 | bytes 11010048 | tf_op jit(solution)/shard_map/broadcast_in_dim | solution.py:345
  98.8 15.3 %collective-permute-done.5.refs_6_ = bf16[528,1024]{1,0:T(8,128)(2,1)S(1)} collective-permute-done((bf16[528,1024]{1,0:T(8,128)(2,1)S(1)}, bf16[528,1024]{1,0:T(8,128)(2,1)S(1)}, u32[]{:S(2)}, u32[]{:S(2)}) %collective-permute-start.5) | collective-permute-done | bytes 1081376 | tf_op jit(solution)/shard_map/ppermute | solution.py:46
  114.2 0.5 collective-permute-start.9
  114.8 0.0 copy-start.11
  114.8 1.6 collective-permute-start.8
  116.4 18.7 %collective-permute-done.14 = bf16[512,1024]{1,0:T(8,128)(2,1)S(1)} collective-permute-done((bf16[512,1024]{1,0:T(8,128)(2,1)S(1)}, bf16[512,1024]{1,0:T(8,128)(2,1)S(1)}, u32[]{:S(2)}, u32[]{:S(2)}) %collective-permute-start.14) | collective-permute-done | bytes 1048608 | tf_op jit(solution)/shard_map/ppermute | solution.py:43
  135.1 1.6 collective-permute-done.15
  136.6 3.1 %fusion.6 = (bf16[512,1024]{1,0:T(8,128)(2,1)S(1)}, bf16[512,1024]{1,0:T(8,128)(2,1)S(1)}) fusion(bf16[512,1024]{1,0:T(8,128)(2,1)S(1)} %collective-permute-done.14, f32[7,512,1024]{2,1,0:T(8,128)} %get-tuple-element.30, bf16[512,1024]{1,0:T(8,128)(2,1)S(1)} %collective-permute-done.15), kind=kLoop, calls=%fused_computation.13 | loop fusion | flops 3145728 | bytes 8388608 | tf_op jit(solution)/shard_map/convert_element_type | solution.py:287
  139.8 1.6 collective-permute-start.16
  141.3 0.5 collective-permute-start.17
  141.9 4.4 %collective-permute-done.8.refs_7_ = bf16[256,1024]{1,0:T(8,128)(2,1)S(1)} collective-permute-done((bf16[256,1024]{1,0:T(8,128)(2,1)S(1)}, bf16[256,1024]{1,0:T(8,128)(2,1)S(1)}, u32[]{:S(2)}, u32[]{:S(2)}) %collective-permute-start.8) | collective-permute-done | bytes 524320 | tf_op jit(solution)/shard_map/ppermute | solution.py:43
  146.3 2.3 %collective-permute-done.9.refs_8_ = bf16[272,1024]{1,0:T(8,128)(2,1)S(1)} collective-permute-done((bf16[272,1024]{1,0:T(8,128)(2,1)S(1)}, bf16[272,1024]{1,0:T(8,128)(2,1)S(1)}, u32[]{:S(2)}, u32[]{:S(2)}) %collective-permute-start.9) | collective-permute-done | bytes 557088 | tf_op jit(solution)/shard_map/ppermute | solution.py:46
  148.6 16.5 %project_and_input_grad.1 = (bf16[512,1024]{1,0:T(8,128)(2,1)}, bf16[512,4096]{1,0:T(8,128)(2,1)}) custom-call(s32[8]{0:T(128)S(1)} %compare_select_fusion.5.at, bf16[512,4096]{1,0:T(8,128)(2,1)} %bitcast.49, bf16[512,1024]{1,0:T(8,128)(2,1)S(1)} %get-tuple-element.24.kv_grad, f32[512,128]{1,0:T(8,128)S(1)} %get-tuple-element.25.inv, ...), custom_call_target="tpu_custom_call" | custom-call | flops 8589934592 | bytes 16777216 | tf_op jit(solution)/shard_map/project_and_input_grad/pallas_call | solution.py:226
  165.1 1.2 collective-permute-done.16
  166.4 2.0 %collective-permute-done.17 = bf16[512,1024]{1,0:T(8,128)(2,1)S(1)} collective-permute-done((bf16[512,1024]{1,0:T(8,128)(2,1)S(1)}, bf16[512,1024]{1,0:T(8,128)(2,1)S(1)}, u32[]{:S(2)}, u32[]{:S(2)}) %collective-permute-start.17) | collective-permute-done | bytes 1048608 | tf_op jit(solution)/shard_map/ppermute | solution.py:46
  168.4 4.1 %multiply_reduce_fusion = (f32[512]{0:T(512)}, f32[1,512,1024]{2,1,0:T(8,128)}) fusion(bf16[512,1024]{1,0:T(8,128)(2,1)S(1)} %collective-permute-done.17, bf16[512,1024]{1,0:T(8,128)(2,1)S(1)} %collective-permute-done.16, f32[7,512,1024]{2,1,0:T(8,128)} %get-tuple-element.30, bf16[1,512,1024]{2,1,0:T(8,128)(2,1)S(1)} %copy-done.2, f32[512]{0:T(512)S(1)} %bitcast.53), kind=kLoop, calls=%fused_computation.16 | loop fusion | flops 4193792 | bytes 7344128 | tf_op jit(solution)/shard_map/reduce_sum | solution.py:325
  (32 shorter events, 0.2 us)
Async XLA Ops:
  0.6 4.5 %copy-start.12 = (s32[8]{0:T(128)S(1)}, s32[8]{0:T(128)}, u32[]{:S(2)}) copy-start(s32[8]{0:T(128)} %constant.91.clone) | copy-start | bytes 100
  2.0 25.7 %collective-permute-start = (bf16[528,1024]{1,0:T(8,128)(2,1)S(1)}, bf16[528,1024]{1,0:T(8,128)(2,1)S(1)}, u32[]{:S(2)}, u32[]{:S(2)}) collective-permute-start(bf16[528,1024]{1,0:T(8,128)(2,1)S(1)} %fusion.10.refs_0_), channel_id=1, source_target_pairs={{0,2},{2,4},{4,6},{6,7},{7,5},{5,3},{3,1},{1,0},{8,10},{10,12},{12... | collective-permute-start | bytes 3244040 | tf_op jit(solution)/shard_map/ppermute | solution.py:43
  3.6 25.3 %collective-permute-start.1 = (bf16[528,1024]{1,0:T(8,128)(2,1)S(1)}, bf16[528,1024]{1,0:T(8,128)(2,1)S(1)}, u32[]{:S(2)}, u32[]{:S(2)}) collective-permute-start(bf16[528,1024]{1,0:T(8,128)(2,1)S(1)} %fusion.10.refs_0_), channel_id=1, source_target_pairs={{2,0},{4,2},{6,4},{7,6},{5,7},{3,5},{1,3},{0,1},{10,8},{12,10},{14... | collective-permute-start | bytes 3244040 | tf_op jit(solution)/shard_map/ppermute | solution.py:46
  4.0 46.2 %collective-permute-start.6 = (f32[384,1024]{1,0:T(8,128)}, f32[384,1024]{1,0:T(8,128)}, u32[]{:S(2)}, u32[]{:S(2)}) collective-permute-start(f32[384,1024]{1,0:T(8,128)} %bitcast.3), channel_id=1, source_target_pairs={{0,8},{8,0},{16,24},{24,16},{1,9},{9,1},{17,25},{25,17},{2,10},{10... | collective-permute-start | bytes 4718600 | tf_op jit(solution)/shard_map/ppermute | solution.py:263
  4.1 1.3 copy-start.1
  5.4 2.2 %copy-start = (bf16[1,512,4096]{2,1,0:T(8,128)(2,1)S(1)}, bf16[1,512,4096]{2,1,0:T(8,128)(2,1)}, u32[]{:S(2)}) copy-start(bf16[1,512,4096]{2,1,0:T(8,128)(2,1)} %param.10) | copy-start | bytes 12582916
  28.9 14.9 %collective-permute-start.10 = (bf16[256,1024]{1,0:T(8,128)(2,1)S(1)}, bf16[256,1024]{1,0:T(8,128)(2,1)S(1)}, u32[]{:S(2)}, u32[]{:S(2)}) collective-permute-start(bf16[256,1024]{1,0:T(8,128)(2,1)S(1)} %get-tuple-element.33), channel_id=1, source_target_pairs={{0,2},{2,4},{4,6},{6,7},{7,5},{5,3},{3,1},{1,0},{8,10},{10,12},{12... | collective-permute-start | bytes 1572872 | tf_op jit(solution)/shard_map/ppermute | solution.py:43
  30.5 14.9 %collective-permute-start.11 = (bf16[256,1024]{1,0:T(8,128)(2,1)S(1)}, bf16[256,1024]{1,0:T(8,128)(2,1)S(1)}, u32[]{:S(2)}, u32[]{:S(2)}) collective-permute-start(bf16[256,1024]{1,0:T(8,128)(2,1)S(1)} %get-tuple-element.34), channel_id=1, source_target_pairs={{2,0},{4,2},{6,4},{7,6},{5,7},{3,5},{1,3},{0,1},{10,8},{12,10},{14... | collective-permute-start | bytes 1572872 | tf_op jit(solution)/shard_map/ppermute | solution.py:46
  30.9 37.6 %collective-permute-start.3 = (bf16[528,1024]{1,0:T(8,128)(2,1)S(1)}, bf16[528,1024]{1,0:T(8,128)(2,1)S(1)}, u32[]{:S(2)}, u32[]{:S(2)}) collective-permute-start(bf16[528,1024]{1,0:T(8,128)(2,1)S(1)} %collective-permute-done.1.refs_2_), channel_id=1, source_target_pairs={{2,0},{4,2},{6,4},{7,6},{5,7},{3,5},{1,3},{0,1},{10,8},{12,10},{14... | collective-permute-start | bytes 3244040 | tf_op jit(solution)/shard_map/ppermute | solution.py:46
  31.4 37.6 %collective-permute-start.2 = (bf16[528,1024]{1,0:T(8,128)(2,1)S(1)}, bf16[528,1024]{1,0:T(8,128)(2,1)S(1)}, u32[]{:S(2)}, u32[]{:S(2)}) collective-permute-start(bf16[528,1024]{1,0:T(8,128)(2,1)S(1)} %collective-permute-done.refs_1_), channel_id=1, source_target_pairs={{0,2},{2,4},{4,6},{6,7},{7,5},{5,3},{3,1},{1,0},{8,10},{10,12},{12... | collective-permute-start | bytes 3244040 | tf_op jit(solution)/shard_map/ppermute | solution.py:43
  48.2 41.3 %collective-permute-start.12 = (bf16[512,1024]{1,0:T(8,128)(2,1)S(1)}, bf16[512,1024]{1,0:T(8,128)(2,1)S(1)}, u32[]{:S(2)}, u32[]{:S(2)}) collective-permute-start(bf16[512,1024]{1,0:T(8,128)(2,1)S(1)} %get-tuple-element.52), channel_id=1, source_target_pairs={{0,2},{2,4},{4,6},{6,7},{7,5},{5,3},{3,1},{1,0},{8,10},{10,12},{12... | collective-permute-start | bytes 3145736 | tf_op jit(solution)/shard_map/ppermute | solution.py:43
  49.7 41.3 %collective-permute-start.13 = (bf16[512,1024]{1,0:T(8,128)(2,1)S(1)}, bf16[512,1024]{1,0:T(8,128)(2,1)S(1)}, u32[]{:S(2)}, u32[]{:S(2)}) collective-permute-start(bf16[512,1024]{1,0:T(8,128)(2,1)S(1)} %get-tuple-element.51), channel_id=1, source_target_pairs={{2,0},{4,2},{6,4},{7,6},{5,7},{3,5},{1,3},{0,1},{10,8},{12,10},{14... | collective-permute-start | bytes 3145736 | tf_op jit(solution)/shard_map/ppermute | solution.py:46
  52.5 43.7 %copy-start.3 = (f32[384,1024]{1,0:T(8,128)S(1)}, f32[384,1024]{1,0:T(8,128)}, u32[]{:S(2)}) copy-start(f32[384,1024]{1,0:T(8,128)} %param.16) | copy-start | bytes 4718596
  52.5 43.7 %copy-start.4 = (f32[384,1024]{1,0:T(8,128)S(1)}, f32[384,1024]{1,0:T(8,128)}, u32[]{:S(2)}) copy-start(f32[384,1024]{1,0:T(8,128)} %param.15) | copy-start | bytes 4718596
  52.5 43.7 %copy-start.5 = (bf16[1,384,1024]{2,1,0:T(8,128)(2,1)S(1)}, bf16[1,384,1024]{2,1,0:T(8,128)(2,1)}, u32[]{:S(2)}) copy-start(bf16[1,384,1024]{2,1,0:T(8,128)(2,1)} %param.17) | copy-start | bytes 2359300
  52.5 43.6 %collective-permute-start.7 = (f32[384,1024]{1,0:T(8,128)S(1)}, f32[384,1024]{1,0:T(8,128)S(1)}, u32[]{:S(2)}, u32[]{:S(2)}) collective-permute-start(f32[384,1024]{1,0:T(8,128)S(1)} %bitcast_add_fusion.7), channel_id=1, source_target_pairs={{0,16},{8,24},{16,0},{24,8},{1,17},{9,25},{17,1},{25,9},{2,18},{10... | collective-permute-start | bytes 4718600 | tf_op jit(solution)/shard_map/ppermute | solution.py:263
  68.5 25.5 %copy-start.9 = (bf16[528,1024]{1,0:T(8,128)(2,1)}, bf16[528,1024]{1,0:T(8,128)(2,1)S(1)}, u32[]{:S(2)}) copy-start(bf16[528,1024]{1,0:T(8,128)(2,1)S(1)} %collective-permute-done.3.refs_4_) | copy-start | bytes 3244036
  68.5 45.6 %collective-permute-start.5 = (bf16[528,1024]{1,0:T(8,128)(2,1)S(1)}, bf16[528,1024]{1,0:T(8,128)(2,1)S(1)}, u32[]{:S(2)}, u32[]{:S(2)}) collective-permute-start(bf16[528,1024]{1,0:T(8,128)(2,1)S(1)} %collective-permute-done.3.refs_4_), channel_id=1, source_target_pairs={{2,0},{4,2},{6,4},{7,6},{5,7},{3,5},{1,3},{0,1},{10,8},{12,10},{14... | collective-permute-start | bytes 3244040 | tf_op jit(solution)/shard_map/ppermute | solution.py:46
  69.0 25.1 %copy-start.10 = (bf16[528,1024]{1,0:T(8,128)(2,1)}, bf16[528,1024]{1,0:T(8,128)(2,1)S(1)}, u32[]{:S(2)}) copy-start(bf16[528,1024]{1,0:T(8,128)(2,1)S(1)} %collective-permute-done.2.refs_3_) | copy-start | bytes 3244036
  69.0 45.7 %collective-permute-start.4 = (bf16[528,1024]{1,0:T(8,128)(2,1)S(1)}, bf16[528,1024]{1,0:T(8,128)(2,1)S(1)}, u32[]{:S(2)}, u32[]{:S(2)}) collective-permute-start(bf16[528,1024]{1,0:T(8,128)(2,1)S(1)} %collective-permute-done.2.refs_3_), channel_id=1, source_target_pairs={{0,2},{2,4},{4,6},{6,7},{7,5},{5,3},{3,1},{1,0},{8,10},{10,12},{12... | collective-permute-start | bytes 3244040 | tf_op jit(solution)/shard_map/ppermute | solution.py:43
  94.1 41.0 %collective-permute-start.14 = (bf16[512,1024]{1,0:T(8,128)(2,1)S(1)}, bf16[512,1024]{1,0:T(8,128)(2,1)S(1)}, u32[]{:S(2)}, u32[]{:S(2)}) collective-permute-start(bf16[512,1024]{1,0:T(8,128)(2,1)S(1)} %get-tuple-element.50), channel_id=1, source_target_pairs={{0,2},{2,4},{4,6},{6,7},{7,5},{5,3},{3,1},{1,0},{8,10},{10,12},{12... | collective-permute-start | bytes 3145736 | tf_op jit(solution)/shard_map/ppermute | solution.py:43
  95.6 41.0 %collective-permute-start.15 = (bf16[512,1024]{1,0:T(8,128)(2,1)S(1)}, bf16[512,1024]{1,0:T(8,128)(2,1)S(1)}, u32[]{:S(2)}, u32[]{:S(2)}) collective-permute-start(bf16[512,1024]{1,0:T(8,128)(2,1)S(1)} %get-tuple-element.49), channel_id=1, source_target_pairs={{2,0},{4,2},{6,4},{7,6},{5,7},{3,5},{1,3},{0,1},{10,8},{12,10},{14... | collective-permute-start | bytes 3145736 | tf_op jit(solution)/shard_map/ppermute | solution.py:46
  114.2 25.6 %copy-start.6 = (bf16[528,1024]{1,0:T(8,128)(2,1)}, bf16[528,1024]{1,0:T(8,128)(2,1)S(1)}, u32[]{:S(2)}) copy-start(bf16[528,1024]{1,0:T(8,128)(2,1)S(1)} %collective-permute-done.5.refs_6_) | copy-start | bytes 3244036
  114.2 34.4 %collective-permute-start.9 = (bf16[272,1024]{1,0:T(8,128)(2,1)S(1)}, bf16[272,1024]{1,0:T(8,128)(2,1)S(1)}, u32[]{:S(2)}, u32[]{:S(2)}) collective-permute-start(bf16[272,1024]{1,0:T(8,128)(2,1)S(1)} %slice.28), channel_id=1, source_target_pairs={{2,0},{4,2},{6,4},{7,6},{5,7},{3,5},{1,3},{0,1},{10,8},{12,10},{14... | collective-permute-start | bytes 1671176 | tf_op jit(solution)/shard_map/ppermute | solution.py:46
  114.7 25.0 %copy-start.7 = (bf16[528,1024]{1,0:T(8,128)(2,1)}, bf16[528,1024]{1,0:T(8,128)(2,1)S(1)}, u32[]{:S(2)}) copy-start(bf16[528,1024]{1,0:T(8,128)(2,1)S(1)} %collective-permute-done.4.refs_5_) | copy-start | bytes 3244036
  114.8 27.1 %copy-start.8 = (bf16[1,512]{1,0:T(2,128)(2,1)S(1)}, bf16[1,512]{1,0:T(2,128)(2,1)}, u32[]{:S(2)}) copy-start(bf16[1,512]{1,0:T(2,128)(2,1)} %param.11) | copy-start | bytes 3076
  114.8 27.1 %copy-start.11 = (s32[8]{0:T(128)S(1)}, s32[8]{0:T(128)}, u32[]{:S(2)}) copy-start(s32[8]{0:T(128)} %constant.92.clone) | copy-start | bytes 100
  114.8 31.5 %collective-permute-start.8 = (bf16[256,1024]{1,0:T(8,128)(2,1)S(1)}, bf16[256,1024]{1,0:T(8,128)(2,1)S(1)}, u32[]{:S(2)}, u32[]{:S(2)}) collective-permute-start(bf16[256,1024]{1,0:T(8,128)(2,1)S(1)} %slice.27), channel_id=1, source_target_pairs={{0,2},{2,4},{4,6},{6,7},{7,5},{5,3},{3,1},{1,0},{8,10},{10,12},{12... | collective-permute-start | bytes 1572872 | tf_op jit(solution)/shard_map/ppermute | solution.py:43
  139.8 26.6 %collective-permute-start.16 = (bf16[512,1024]{1,0:T(8,128)(2,1)S(1)}, bf16[512,1024]{1,0:T(8,128)(2,1)S(1)}, u32[]{:S(2)}, u32[]{:S(2)}) collective-permute-start(bf16[512,1024]{1,0:T(8,128)(2,1)S(1)} %get-tuple-element.47), channel_id=1, source_target_pairs={{0,2},{2,4},{4,6},{6,7},{7,5},{5,3},{3,1},{1,0},{8,10},{10,12},{12... | collective-permute-start | bytes 3145736 | tf_op jit(solution)/shard_map/ppermute | solution.py:43
  141.3 27.1 %collective-permute-start.17 = (bf16[512,1024]{1,0:T(8,128)(2,1)S(1)}, bf16[512,1024]{1,0:T(8,128)(2,1)S(1)}, u32[]{:S(2)}, u32[]{:S(2)}) collective-permute-start(bf16[512,1024]{1,0:T(8,128)(2,1)S(1)} %get-tuple-element.48), channel_id=1, source_target_pairs={{2,0},{4,2},{6,4},{7,6},{5,7},{3,5},{1,3},{0,1},{10,8},{12,10},{14... | collective-permute-start | bytes 3145736 | tf_op jit(solution)/shard_map/ppermute | solution.py:46
  148.6 19.8 %copy-start.2 = (bf16[1,512,1024]{2,1,0:T(8,128)(2,1)S(1)}, bf16[1,512,1024]{2,1,0:T(8,128)(2,1)}, u32[]{:S(2)}) copy-start(bf16[1,512,1024]{2,1,0:T(8,128)(2,1)} %param.12) | copy-start | bytes 3145732

commit v4 on v3

--- a/solution.py
+++ b/solution.py
@@ -22,28 +22,27 @@
 f32, bf16 = jnp.float32, jnp.bfloat16
 
 
-class Ring:
+class Plane:
     def __init__(self):
         self.count = lax.axis_size("fsdp")
-        self.half = self.count // 2
-        walk = list(range(0, self.count, 2)) + list(range(self.count - 1, 0, -2))
-        after = walk[1:] + walk[:1]
-        self.right = list(zip(walk, after))
-        self.left = list(zip(after, walk))
+        self.line = self.count // 2
         self.me = lax.axis_index("fsdp")
-        self.spot = jnp.where(
-            self.me % 2 == 0, self.me // 2, self.count - 1 - self.me // 2
-        )
-
-    def devices_at(self, distances):
-        spot = (self.spot + self.count + jnp.array(distances, jnp.int32)) % self.count
-        return jnp.where(spot < self.half, 2 * spot, 2 * (self.count - 1 - spot) + 1)
-
-    def to_right(self, value):
-        return lax.ppermute(value, "fsdp", self.right)
-
-    def to_left(self, value):
-        return lax.ppermute(value, "fsdp", self.left)
+        self.place, self.side = self.me // 2, self.me % 2
+
+    def device(self, distance, other):
+        return (self.place + distance) % self.line * 2 + (self.side + other) % 2
+
+    def up(self, value, first, last):
+        pairs = [(2 * p + i, 2 * p + 2 + i) for p in range(first, last + 1) for i in range(2)]
+        return lax.ppermute(value, "fsdp", pairs)
+
+    def down(self, value, first, last):
+        pairs = [(2 * p + i, 2 * p - 2 + i) for p in range(first, last + 1) for i in range(2)]
+        return lax.ppermute(value, "fsdp", pairs)
+
+    def flip(self, value, first, last):
+        pairs = [(2 * p + i, 2 * p + 1 - i) for p in range(first, last + 1) for i in range(2)]
+        return lax.ppermute(value, "fsdp", pairs)
 
 
 def after(value, *others):
@@ -59,10 +58,11 @@
     return jnp.concatenate([cosine, cosine], axis=1), jnp.concatenate([-sine, sine], axis=1)
 
 
-def first_kernel(scale, at, x, cotangent, cosine, sine, kv_grad, inv, top, bottom, near):
+def first_kernel(scale, line, at, x, cotangent, cosine, sine, kv_grad, inv, near_a, near_b, *far_a):
     step = pl.program_id(0)
     width = x.shape[1]
-    shard, cut = near.shape[1], top.shape[0]
+    cut, rest = near_a.shape[1], near_b.shape[2]
+    shard = cut + rest
     kvw = cotangent.shape[1] // 2
 
     @pl.when(step == 0)
@@ -85,31 +85,30 @@
         lax.dot_general(normed, kv_grad[...], (((0,), (0,)), ((), ())), preferred_element_type=f32)
         * scale
     )
-
-    @pl.when(step == 0)
+    near_b[0, 0] = term[cut:]
+
+    @pl.when(step % 2 == 0)
     def _():
-        top[...] = term[:cut].astype(bf16)
-        bottom[...] = term[cut:].astype(bf16)
-
-    @pl.when(step > 0)
-    def _():
-        near[0] = term
-
-
-def first_part(ring, tokens_in, cotangent, cosine, sine, shard, scale):
+        near_a[0] = term[:cut]
+
+    for j in range(line):
+
+        @pl.when(step == 2 * j + 1)
+        def _(j=j):
+            far_a[j][...] = term[:cut].astype(bf16)
+
+
+def first_part(plane, tokens_in, cotangent, cosine, sine, shard, cut, distances, scale):
     rows, width = tokens_in.shape
     cols = cotangent.shape[1]
-    order = [ring.half]
-    for d in range(ring.half - 1, 0, -1):
-        order += [d, -d]
-    order.append(0)
-    n = ring.count
+    line, rest = plane.line, shard - cut
+    at = jnp.stack([plane.device(r, e) for r in distances for e in range(2)]).astype(jnp.int32)
     fixed = lambda k, at: (0, 0)
-    return pl.pallas_call(
-        functools.partial(first_kernel, scale),
+    outs = pl.pallas_call(
+        functools.partial(first_kernel, scale, line),
         grid_spec=pltpu.PrefetchScalarGridSpec(
             num_scalar_prefetch=1,
-            grid=(n,),
+            grid=(2 * line,),
             in_specs=[
                 pl.BlockSpec((rows, width), fixed),
                 pl.BlockSpec((rows, cols), fixed),
@@ -119,18 +118,18 @@
             out_specs=[
                 pl.BlockSpec((rows, cols), fixed),
                 pl.BlockSpec((rows, HEAD), fixed),
-                pl.BlockSpec((shard // 2, cols), fixed),
-                pl.BlockSpec((shard - shard // 2, cols), fixed),
-                pl.BlockSpec((1, shard, cols), lambda k, at: (jnp.maximum(k - 1, 0), 0, 0)),
-            ],
+                pl.BlockSpec((1, cut, cols), lambda k, at: (k // 2, 0, 0)),
+                pl.BlockSpec((1, 1, rest, cols), lambda k, at: (k // 2, k % 2, 0, 0)),
+            ]
+            + [pl.BlockSpec((cut, cols), fixed)] * line,
         ),
         out_shape=[
             jax.ShapeDtypeStruct((rows, cols), bf16),
             jax.ShapeDtypeStruct((rows, HEAD), f32),
-            jax.ShapeDtypeStruct((shard // 2, cols), bf16),
-            jax.ShapeDtypeStruct((shard - shard // 2, cols), bf16),
-            jax.ShapeDtypeStruct((n - 1, shard, cols), f32),
-        ],
+            jax.ShapeDtypeStruct((line, cut, cols), f32),
+            jax.ShapeDtypeStruct((line, 2, rest, cols), f32),
+        ]
+        + [jax.ShapeDtypeStruct((cut, cols), bf16)] * line,
         compiler_params=pltpu.CompilerParams(vmem_limit_bytes=40 * 2**20),
         cost_estimate=pl.CostEstimate(
             flops=2 * rows * width * cols,
@@ -138,17 +137,26 @@
             transcendentals=0,
         ),
         name="norm_and_weight_terms",
-    )(ring.devices_at(order), tokens_in, cotangent, cosine, sine)
-
-
-def second_kernel(n, at, x, kv_grad, inv, cosine, sine, *refs):
-    blocks, refs = refs[: n + 1], refs[n + 1 :]
-    kv_out, input_grad, xs, ws, ng, pre, out, x_sem, w_sem, o_sem = refs
+    )(at, tokens_in, cotangent, cosine, sine)
+    kv_grad, inv, near_a, near_b, *far_a = outs
+    place = {r: j for j, r in enumerate(distances)}
+    near_a = {r: near_a[j] for r, j in place.items()}
+    near_b = {r: near_b[j].reshape(2 * rest, cols) for r, j in place.items()}
+    return kv_grad, inv, near_a, near_b, {r: far_a[j] for r, j in place.items()}
+
+
+def second_kernel(line, at, x, kv_grad, inv, cosine, sine, *refs):
+    n = 2 * line
+    own_a, own_x, own_b = refs[:3]
+    up_a, down_a, up_x, down_x, up_b, down_b = [
+        (None,) + refs[3 + i * (line - 1) : 3 + (i + 1) * (line - 1)] for i in range(6)
+    ]
+    kv_out, input_grad, xs, ws, ng, pre, out, x_sem, w_sem, o_sem = refs[3 + 6 * (line - 1) :]
     rows, width = x.shape
     shard = xs.shape[2]
     cols = pre.shape[1]
     kvw = cols // 2
-    cut = shard // 2
+    cut, rest = own_a.shape[0], own_b.shape[0] // 2
 
     def columns(k):
         return pl.ds(pl.multiple_of(at[k] * shard, shard), shard)
@@ -159,13 +167,28 @@
     def o_copy(k):
         return pltpu.make_async_copy(out.at[k], input_grad.at[:, columns(k)], o_sem.at[k])
 
-    for k in range(n):
-        x_copy(k).start()
-        if k < n - 1:
-            pltpu.make_async_copy(blocks[k], ws.at[k], w_sem.at[k]).start()
+    def w_start(k, near, far, both):
+        for e, part in enumerate((near, far)):
+            sem = w_sem.at[k + e]
+            pltpu.make_async_copy(part, ws.at[k + e, :cut], sem).start()
+            half = both.at[e * rest : (e + 1) * rest]
+            pltpu.make_async_copy(half, ws.at[k + e, cut:], sem).start()
+
+    for r in range(line):
+        x_copy(2 * r).start()
+        x_copy(2 * r + 1).start()
+        if r == 0:
+            w_start(0, own_a, own_x, own_b)
         else:
-            pltpu.make_async_copy(blocks[k], ws.at[k, :cut], w_sem.at[k]).start()
-            pltpu.make_async_copy(blocks[k + 1], ws.at[k, cut:], w_sem.at[k]).start()
+            above = at[n] + r < line
+
+            @pl.when(above)
+            def _():
+                w_start(2 * r, down_a[r], down_x[r], down_b[r])
+
+            @pl.when(jnp.logical_not(above))
+            def _():
+                w_start(2 * r, up_a[line - r], up_x[line - r], up_b[line - r])
 
     pre[...] = jnp.zeros_like(pre)
 
@@ -213,18 +236,15 @@
     lax.fori_loop(0, n, drain, 0)
 
 
-def second_part(ring, tokens_in, kv_grad, inv, cosine, sine, blocks, shard):
+def second_part(plane, tokens_in, kv_grad, inv, cosine, sine, blocks, shard):
     rows, width = tokens_in.shape
     cols = kv_grad.shape[1]
-    n = ring.count
-    order = [0]
-    for d in range(1, ring.half):
-        order += [-d, d]
-    order.append(ring.half)
+    n = plane.count
+    at = [plane.device(r, e) for r in range(plane.line) for e in range(2)] + [plane.place]
     whole = pl.BlockSpec(memory_space=pltpu.VMEM)
     there = pl.BlockSpec(memory_space=pl.ANY)
     return pl.pallas_call(
-        functools.partial(second_kernel, n),
+        functools.partial(second_kernel, plane.line),
         in_specs=[pl.BlockSpec(memory_space=pltpu.SMEM), there]
         + [whole] * 4
         + [there] * len(blocks),
@@ -250,7 +270,7 @@
             transcendentals=0,
         ),
         name="project_and_input_grad",
-    )(ring.devices_at(order), tokens_in, kv_grad, inv, cosine, sine, *blocks)
+    )(jnp.stack(at).astype(jnp.int32), tokens_in, kv_grad, inv, cosine, sine, *blocks)
 
 
 def replica_sum(value):
@@ -265,29 +285,52 @@
     return value
 
 
-def gather_blocks(ring, own, cut, other):
-    blocks = [own]
-    from_left = from_right = own
-    for d in range(1, ring.half):
-        from_left, from_right = ring.to_right(from_left), ring.to_left(from_right)
-        blocks += [from_left, from_right]
-    from_left, from_right = after(from_left, other), after(from_right, other)
-    blocks += [ring.to_right(from_left[:cut]), ring.to_left(from_right[cut:])]
-    return blocks
-
-
-def scatter_terms(ring, top, bottom, near):
-    cut, rest = top.shape[0], bottom.shape[0]
-    from_left, from_right = ring.to_right(top), ring.to_left(bottom)
-    for k in range(0, 2 * (ring.half - 1), 2):
-        from_left, from_right = lax.optimization_barrier((from_left, from_right))
-        if k == 0:
-            from_left = jnp.pad(from_left, ((0, rest), (0, 0)))
-            from_right = jnp.pad(from_right, ((cut, 0), (0, 0)))
-        from_left = ring.to_right((near[k] + from_left.astype(f32)).astype(bf16))
-        from_right = ring.to_left((near[k + 1] + from_right.astype(f32)).astype(bf16))
-    from_left, from_right = from_left.astype(f32), from_right.astype(f32)
-    return near[-1] + from_left + from_right
+def gather_a(plane, own):
+    last = plane.line - 1
+    up, down = [own], [own]
+    up_x, down_x = [plane.flip(own, 0, last)], [None]
+    for s in range(1, plane.line):
+        up.append(plane.up(up[-1], s - 1, last - 1))
+        down.append(plane.down(down[-1], 1, last - s + 1))
+        up[s], down[s] = lax.optimization_barrier((up[s], down[s]))
+        up_x.append(plane.flip(up[s], s, last))
+        down_x.append(plane.flip(down[s], 0, last - s))
+    return up, down, up_x, down_x
+
+
+def gather_b(plane, own):
+    last = plane.line - 1
+    pair = jnp.concatenate([own, plane.flip(own, 0, last)], axis=0)
+    up, down = [pair], [pair]
+    for s in range(1, plane.line):
+        up.append(plane.up(up[-1], s - 1, last - 1))
+        down.append(plane.down(down[-1], 1, last - s + 1))
+        up[s], down[s] = lax.optimization_barrier((up[s], down[s]))
+    return up, down
+
+
+def scatter_line(plane, terms):
+    last = plane.line - 1
+    up, down = [], []
+    for s in range(last, 0, -1):
+        up = plane.up(sum(terms(s) + up).astype(bf16), 0, last - s)
+        down = plane.down(sum(terms(plane.line - s) + down).astype(bf16), s, last)
+        up, down = lax.optimization_barrier((up, down))
+        up, down = [up.astype(f32)], [down.astype(f32)]
+    return sum(terms(0) + up + down)
+
+
+def scatter_a(plane, near, far, distances):
+    last = plane.line - 1
+    other = {r: plane.flip(far[r], 0, last) for r in distances}
+    return scatter_line(plane, lambda r: [near[r], other[r].astype(f32)])
+
+
+def scatter_b(plane, near):
+    both = scatter_line(plane, lambda r: [near[r]])
+    rest = both.shape[0] // 2
+    other = plane.flip(both[rest:].astype(bf16), 0, plane.line - 1)
+    return both[:rest] + other.astype(f32)
 
 
 def local(
@@ -300,27 +343,39 @@
     global_params,
     local_params,
 ):
-    ring = Ring()
+    plane = Plane()
     tokens_in = layer_input[0]
     gain_shard = norm_gain[0]
     weight_shard = kv_weight[0]
     cotangent = kv_cotangent[0]
     rows, width = tokens_in.shape
     shard, cols = weight_shard.shape
-
+    cut = shard * 5 // 8 // PAD * PAD
+
+    total = replica_sum(pseudo_grad[0])
     gain_rows = jnp.pad(gain_shard[None, :], ((0, PAD - 1), (0, cols - shard)))
-    own = jnp.concatenate([weight_shard, gain_rows], axis=0)
-    total = replica_sum(pseudo_grad[0])
-    blocks = gather_blocks(ring, own, shard // 2, total)
-
-    positions = (ring.me * rows + jnp.arange(rows, dtype=jnp.int32)) % SEQ_LEN
+    own_a = weight_shard[:cut]
+    own_b = jnp.concatenate([weight_shard[cut:], gain_rows], axis=0)
+    up_a, down_a, up_x, down_x = gather_a(plane, own_a)
+    up_b, down_b = gather_b(plane, own_b)
+    blocks = [own_a, up_x[0], up_b[0]]
+    for part in (up_a, down_a, up_x, down_x, up_b, down_b):
+        blocks += part[1:]
+
+    positions = (plane.me * rows + jnp.arange(rows, dtype=jnp.int32)) % SEQ_LEN
     cosine, sine = rope_tables(positions)
-    scale = 1.0 / math.sqrt(rows * ring.count)
-    kv_grad, inv, top, bottom, near = first_part(
-        ring, tokens_in, cotangent, cosine, sine, shard, scale
-    )
-    top, bottom = after((top, bottom), blocks[1], blocks[2])
-    term = scatter_terms(ring, top, bottom, near)
+    scale = 1.0 / math.sqrt(rows * plane.count)
+    distances = []
+    for s in range(plane.line - 1, 0, -1):
+        distances += [s, plane.line - s]
+    distances = list(dict.fromkeys(distances)) + [0]
+    kv_grad, inv, near_a, near_b, far_a = first_part(
+        plane, tokens_in, cotangent, cosine, sine, shard, cut, distances, scale
+    )
+    (far_a, near_b) = after((far_a, near_b), up_a[1], down_a[1])
+    term_a = scatter_a(plane, near_a, far_a, distances)
+    term_b = scatter_b(plane, near_b)
+    term = jnp.concatenate([term_a, term_b], axis=0)
     weight_grad = term * gain_shard.astype(f32)[:, None]
     gain_grad = jnp.sum(term * weight_shard.astype(f32), axis=1)
 
@@ -333,7 +388,7 @@
     ).astype(bf16)
 
     kv_out, input_grad = second_part(
-        ring, tokens_in, kv_grad, inv, cosine, sine, blocks, shard
+        plane, tokens_in, kv_grad, inv, cosine, sine, blocks, shard
     )
     return (
         kv_out[None],

time: 174 us -> 248 us (1.43)
  starting transfers between devices: 18.1 us -> 91.2 us
  waiting for transfers between devices: 102 us -> 91.3 us
  local copies, waits for them, and re-layouts: 2.32 us -> 11.8 us
    ppermute x16 -> x37, starting transfers between devices: 16.5 us -> 89.5 us  [the longest x12 47.8 us: up(): return lax.ppermute(value, 'fsdp', pairs)]
    ppermute x16 -> x37, waiting for transfers between devices: 102 us -> 91.3 us  [the longest x13 67.2 us: flip(): return lax.ppermute(value, 'fsdp', pairs)]
    slice x2 -> x4, local copies, waits for them, and re-layouts: 0.07 us -> 7.31 us  [the longest x1 5.1 us: first_part(): near_b = {r: near_b[j].reshape(2 * rest, cols) for r, j in place.items()}]
    reduce_sum x1, other arithmetic: 4.09 us -> 0.88 us  [local(): gain_grad = jnp.sum(term * weight_shard.astype(f32), axis=1)]
    convert_element_type x3 -> x8, other arithmetic: 8.91 us -> 6.94 us  [the longest x6 6.58 us: scatter_line(): down = plane.down(sum(terms(plane.line - s) + down).astype(bf16), s, last)]
  transfers between devices with their start and end apart: 18 -> 39, of which waited for: 14 -> 11; matrix products, arithmetic and copies ran while one was open for 9% -> 10% of each run, Pallas kernels for 17% -> 12%
where the time goes in v4:
time: 248 us; the launch traced here: 245 us
  waiting for transfers between devices  91.3 us (37%)
  starting transfers between devices  91.2 us (37%)
  Pallas kernels  29.4 us (12%)
  other arithmetic  20.1 us (8%)
  local copies, waits for them, and re-layouts  11.8 us (5%)
    ppermute x13, waiting for transfers between devices, flip(): return lax.ppermute(value, 'fsdp', pairs)  67.2 us
    ppermute x12, starting transfers between devices, up(): return lax.ppermute(value, 'fsdp', pairs)  47.8 us
    ppermute x12, waiting for transfers between devices, down(): return lax.ppermute(value, 'fsdp', pairs)  21.5 us
    ppermute x13, starting transfers between devices, flip(): return lax.ppermute(value, 'fsdp', pairs)  21 us
    ppermute x12, starting transfers between devices, down(): return lax.ppermute(value, 'fsdp', pairs)  20.7 us
    pallas_call x1, Pallas kernels, second_part(): pl.pallas_call(functools.partial(second_kernel, plane.line), in_specs=[pl...  17.8 us
    pallas_call x1, Pallas kernels, first_part(): pl.pallas_call(functools.partial(first_kernel, scale, line), grid_spec=pl...  11.7 us
    convert_element_type x6, other arithmetic, scatter_line(): down = plane.down(sum(terms(plane.line - s) + down).astype(bf16), s, last)  6.58 us
  transfers between devices with their start and end apart: 39, of which 11 were waited for; matrix products, arithmetic and copies ran while one was open for 10% of the time, Pallas kernels for 12%

profile of v4, /device:TPU:8, one launch (start us, length us, event | category | flops | bytes accessed | tf_op | source)
XLA Modules:
  0.0 245.5 jit_solution(670966894372284003)
XLA Ops:
  1.8 3.5 %collective-permute-start.2 = (bf16[320,1024]{1,0:T(8,128)(2,1)S(1)}, bf16[320,1024]{1,0:T(8,128)(2,1)S(1)}, u32[]{:S(2)}, u32[]{:S(2)}) collective-permute-start(bf16[320,1024]{1,0:T(8,128)(2,1)S(1)} %slice_bitcast_fusion.refs_0_), channel_id=1, source_target_pairs={{0,2},{1,3},{2,4},{3,5},{4,6},{5,7},{8,10},{9,11},{10,12},{11,13},... | collective-permute-start | bytes 1966088 | tf_op jit(solution)/shard_map/ppermute | solution.py:37
  5.3 2.4 collective-permute-start.3
  7.7 1.6 collective-permute-start
  13.7 19.2 %collective-permute-done.1 = bf16[208,1024]{1,0:T(8,128)(2,1)} collective-permute-done((bf16[208,1024]{1,0:T(8,128)(2,1)}, bf16[208,1024]{1,0:T(8,128)(2,1)}, u32[]{:S(2)}, u32[]{:S(2)}) %collective-permute-start.1) | collective-permute-done | bytes 426016 | tf_op jit(solution)/shard_map/ppermute | solution.py:45
  34.0 3.4 %collective-permute-start.14 = (bf16[416,1024]{1,0:T(8,128)(2,1)S(1)}, bf16[416,1024]{1,0:T(8,128)(2,1)S(1)}, u32[]{:S(2)}, u32[]{:S(2)}) collective-permute-start(bf16[416,1024]{1,0:T(8,128)(2,1)S(1)} %pad_maximum_fusion.refs_2_), channel_id=1, source_target_pairs={{0,2},{1,3},{2,4},{3,5},{4,6},{5,7},{8,10},{9,11},{10,12},{11,13},... | collective-permute-start | bytes 2555912 | tf_op jit(solution)/shard_map/ppermute | solution.py:37
  37.4 2.2 copy-done
  39.6 11.7 %norm_and_weight_terms.1 = (bf16[512,1024]{1,0:T(8,128)(2,1)S(1)}, f32[512,128]{1,0:T(8,128)S(1)}, f32[4,320,1024]{2,1,0:T(8,128)}, f32[4,2,192,1024]{3,2,1,0:T(...) custom-call(s32[8]{0:T(128)S(1)} %stack.51.at, ...), custom_call_target="tpu_custom_call" | custom-call | flops 4294967296 | bytes 20971520 | tf_op jit(solution)/shard_map/norm_and_weight_terms/pallas_call | solution.py:107
  51.3 2.5 collective-permute-start.15
  53.8 5.1 %fusion.11 = (f32[1,2,192,1024]{3,2,1,0:T(8,128)S(1)}, f32[1,2,192,1024]{3,2,1,0:T(8,128)S(1)}, f32[1,2,192,1024]{3,2,1,0:T(8,128)S(1)}, f32[1,2,192,1024]{3,2,1,0:T(8,128)}) fusion(f32[4,2,192,1024]{3,2,1,0:T(8,128)} %get-tuple-element.70), kind=kLoop, calls=%fused_computation.45 | loop fusion | bytes 12582912 | tf_op jit(solution)/shard_map/slice | solution.py:144
  58.9 1.6 collective-permute-start.21
  61.0 1.5 collective-permute-start.22
  62.5 3.4 %collective-permute-start.4 = (bf16[320,1024]{1,0:T(8,128)(2,1)S(1)}, bf16[320,1024]{1,0:T(8,128)(2,1)S(1)}, u32[]{:S(2)}, u32[]{:S(2)}) collective-permute-start(bf16[320,1024]{1,0:T(8,128)(2,1)S(1)} %collective-permute-done.2.refs_3_), channel_id=1, source_target_pairs={{2,4},{3,5},{4,6},{5,7},{10,12},{11,13},{12,14},{13,15},{18,20},{1... | collective-permute-start | bytes 1966088 | tf_op jit(solution)/shard_map/ppermute | solution.py:37
  65.9 6.2 %collective-permute-done.15.refs_18_ = bf16[416,1024]{1,0:T(8,128)(2,1)S(1)} collective-permute-done((bf16[416,1024]{1,0:T(8,128)(2,1)S(1)}, bf16[416,1024]{1,0:T(8,128)(2,1)S(1)}, u32[]{:S(2)}, u32[]{:S(2)}) %collective-permute-start.15) | collective-permute-done | bytes 852000 | tf_op jit(solution)/shard_map/ppermute | solution.py:41
  72.1 2.4 collective-permute-start.5
  74.7 2.0 collective-permute-done.21
  78.0 12.8 %collective-permute-done.23 = bf16[320,1024]{1,0:T(8,128)(2,1)S(1)} collective-permute-done((bf16[320,1024]{1,0:T(8,128)(2,1)S(1)}, bf16[320,1024]{1,0:T(8,128)(2,1)S(1)}, u32[]{:S(2)}, u32[]{:S(2)}) %collective-permute-start.23) | collective-permute-done | bytes 655392 | tf_op jit(solution)/shard_map/ppermute | solution.py:45
  90.7 3.4 %collective-permute-start.11 = (bf16[320,1024]{1,0:T(8,128)(2,1)S(1)}, bf16[320,1024]{1,0:T(8,128)(2,1)S(1)}, u32[]{:S(2)}, u32[]{:S(2)}) collective-permute-start(bf16[320,1024]{1,0:T(8,128)(2,1)S(1)} %collective-permute-done.3.refs_6_), channel_id=1, source_target_pairs={{0,1},{1,0},{2,3},{3,2},{4,5},{5,4},{8,9},{9,8},{10,11},{11,10},{1... | collective-permute-start | bytes 1966088 | tf_op jit(solution)/shard_map/ppermute | solution.py:45
  94.2 10.5 %collective-permute-done.22 = bf16[320,1024]{1,0:T(8,128)(2,1)S(1)} collective-permute-done((bf16[320,1024]{1,0:T(8,128)(2,1)S(1)}, bf16[320,1024]{1,0:T(8,128)(2,1)S(1)}, u32[]{:S(2)}, u32[]{:S(2)}) %collective-permute-start.22) | collective-permute-done | bytes 655392 | tf_op jit(solution)/shard_map/ppermute | solution.py:45
  107.4 8.1 %collective-permute-done.11.refs_12_ = bf16[320,1024]{1,0:T(8,128)(2,1)S(1)} collective-permute-done((bf16[320,1024]{1,0:T(8,128)(2,1)S(1)}, bf16[320,1024]{1,0:T(8,128)(2,1)S(1)}, u32[]{:S(2)}, u32[]{:S(2)}) %collective-permute-start.11) | collective-permute-done | bytes 655392 | tf_op jit(solution)/shard_map/ppermute | solution.py:45
  115.6 4.3 %collective-permute-start.16 = (bf16[416,1024]{1,0:T(8,128)(2,1)S(1)}, bf16[416,1024]{1,0:T(8,128)(2,1)}, u32[]{:S(2)}, u32[]{:S(2)}) collective-permute-start(bf16[416,1024]{1,0:T(8,128)(2,1)S(1)} %collective-permute-done.14.refs_15_), channel_id=1, source_target_pairs={{2,4},{3,5},{4,6},{5,7},{10,12},{11,13},{12,14},{13,15},{18,20},{1... | collective-permute-start | bytes 2555912 | tf_op jit(solution)/shard_map/ppermute | solution.py:37
  119.9 1.9 collective-permute-start.17
  122.5 2.6 %collective-permute-done.24 = bf16[320,1024]{1,0:T(8,128)(2,1)S(1)} collective-permute-done((bf16[320,1024]{1,0:T(8,128)(2,1)S(1)}, bf16[320,1024]{1,0:T(8,128)(2,1)S(1)}, u32[]{:S(2)}, u32[]{:S(2)}) %collective-permute-start.24) | collective-permute-done | bytes 655392 | tf_op jit(solution)/shard_map/ppermute | solution.py:37
  126.4 15.2 %collective-permute-start.32 = (bf16[384,1024]{1,0:T(8,128)(2,1)S(1)}, bf16[384,1024]{1,0:T(8,128)(2,1)S(1)}, u32[]{:S(2)}, u32[]{:S(2)}) collective-permute-start(bf16[384,1024]{1,0:T(8,128)(2,1)S(1)} %get-tuple-element.105), channel_id=1, source_target_pairs={{0,2},{1,3},{2,4},{3,5},{8,10},{9,11},{10,12},{11,13},{16,18},{17,... | collective-permute-start | bytes 2359304 | tf_op jit(solution)/shard_map/ppermute | solution.py:37
  142.9 1.3 collective-permute-start.7
  144.2 1.6 collective-permute-start.18
  145.8 2.2 collective-permute-start.19
  148.0 1.6 add_convert_fusion.6
  149.6 9.7 %collective-permute-done.7.refs_8_ = bf16[320,1024]{1,0:T(8,128)(2,1)S(1)} collective-permute-done((bf16[320,1024]{1,0:T(8,128)(2,1)S(1)}, bf16[320,1024]{1,0:T(8,128)(2,1)S(1)}, u32[]{:S(2)}, u32[]{:S(2)}) %collective-permute-start.7) | collective-permute-done | bytes 655392 | tf_op jit(solution)/shard_map/ppermute | solution.py:41
  159.3 3.4 %collective-permute-start.8 = (bf16[320,1024]{1,0:T(8,128)(2,1)S(1)}, bf16[320,1024]{1,0:T(8,128)(2,1)}, u32[]{:S(2)}, u32[]{:S(2)}) collective-permute-start(bf16[320,1024]{1,0:T(8,128)(2,1)S(1)} %collective-permute-done.2.refs_3_), channel_id=1, source_target_pairs={{2,3},{3,2},{4,5},{5,4},{6,7},{7,6},{10,11},{11,10},{12,13},{13,12... | collective-permute-start | bytes 1966088 | tf_op jit(solution)/shard_map/ppermute | solution.py:45
  162.7 1.9 collective-permute-start.26
  164.7 1.3 collective-permute-start.27
  166.1 2.4 bitcast_add_fusion.4
  168.9 9.5 %collective-permute-done.8.refs_9_ = bf16[320,1024]{1,0:T(8,128)(2,1)} collective-permute-done((bf16[320,1024]{1,0:T(8,128)(2,1)S(1)}, bf16[320,1024]{1,0:T(8,128)(2,1)}, u32[]{:S(2)}, u32[]{:S(2)}) %collective-permute-start.8) | collective-permute-done | bytes 655392 | tf_op jit(solution)/shard_map/ppermute | solution.py:45
  178.4 3.3 %collective-permute-start.12 = (bf16[320,1024]{1,0:T(8,128)(2,1)S(1)}, bf16[320,1024]{1,0:T(8,128)(2,1)}, u32[]{:S(2)}, u32[]{:S(2)}) collective-permute-start(bf16[320,1024]{1,0:T(8,128)(2,1)S(1)} %copy-done.7), channel_id=1, source_target_pairs={{0,1},{1,0},{2,3},{3,2},{8,9},{9,8},{10,11},{11,10},{16,17},{17,16... | collective-permute-start | bytes 1966088 | tf_op jit(solution)/shard_map/ppermute | solution.py:45
  182.5 1.7 collective-permute-start.38
  186.1 3.7 %add_convert_fusion.4 = (bf16[320,1024]{1,0:T(8,128)(2,1)S(1)}, bf16[320,1024]{1,0:T(8,128)(2,1)}) fusion(bf16[320,1024]{1,0:T(8,128)(2,1)} %collective-permute-done.27, bf16[320,1024]{1,0:T(8,128)(2,1)S(1)} %copy-done.25, f32[4,320,1024]{2,1,0:T(8,128)} %get-tuple-element.65, bf16[320,1024]{1,0:T(8,128)(2,1)} %collective-permute-done.26, ...), kind=kLoop, calls=%fused_computation.20 | loop fusion | flops 3276800 | bytes 6553600 | tf_op jit(solution)/shard_map/convert_element_type | solution.py:317
  189.8 5.1 %collective-permute-done.12.refs_13_ = bf16[320,1024]{1,0:T(8,128)(2,1)} collective-permute-done((bf16[320,1024]{1,0:T(8,128)(2,1)S(1)}, bf16[320,1024]{1,0:T(8,128)(2,1)}, u32[]{:S(2)}, u32[]{:S(2)}) %collective-permute-start.12) | collective-permute-done | bytes 655392 | tf_op jit(solution)/shard_map/ppermute | solution.py:45
  194.9 1.4 collective-permute-start.20
  196.3 1.9 collective-permute-start.35
  198.2 3.9 %collective-permute-start.34 = (bf16[384,1024]{1,0:T(8,128)(2,1)S(1)}, bf16[384,1024]{1,0:T(8,128)(2,1)S(1)}, u32[]{:S(2)}, u32[]{:S(2)}) collective-permute-start(bf16[384,1024]{1,0:T(8,128)(2,1)S(1)} %add_convert_fusion.1), channel_id=1, source_target_pairs={{0,2},{1,3},{2,4},{3,5},{4,6},{5,7},{8,10},{9,11},{10,12},{11,13},... | collective-permute-start | bytes 2359304 | tf_op jit(solution)/shard_map/ppermute | solution.py:37
  202.2 7.3 %collective-permute-start.28 = (bf16[320,1024]{1,0:T(8,128)(2,1)}, bf16[320,1024]{1,0:T(8,128)(2,1)}, u32[]{:S(2)}, u32[]{:S(2)}) collective-permute-start(bf16[320,1024]{1,0:T(8,128)(2,1)} %get-tuple-element.101), channel_id=1, source_target_pairs={{0,2},{1,3},{2,4},{3,5},{4,6},{5,7},{8,10},{9,11},{10,12},{11,13},... | collective-permute-start | bytes 1966088 | tf_op jit(solution)/shard_map/ppermute | solution.py:37
  209.5 17.8 %project_and_input_grad.1 = (bf16[512,1024]{1,0:T(8,128)(2,1)}, bf16[512,4096]{1,0:T(8,128)(2,1)}) custom-call(s32[9]{0:T(128)S(1)} %stack.50.at, bf16[512,4096]{1,0:T(8,128)(2,1)} %bitcast.59, bf16[512,1024]{1,0:T(8,128)(2,1)} %copy-done.12, f32[512,128]{1,0:T(8,128)S(1)} %get-tuple-element.50.inv, f32[512,128]{1,0:T(8,128)S(1)} %get-tuple-element.109.cosine, ...), custom_call_target="tpu_custom_call" | custom-call | flops 8589934592 | bytes 16777216 | tf_op jit(solution)/shard_map/project_and_input_grad/pallas_call | solution.py:246
  227.3 2.1 collective-permute-start.29
  229.9 1.5 collective-permute-start.36
  231.4 2.9 %fusion.7 = (bf16[1,384,1024]{2,1,0:T(8,128)(2,1)}, f32[384,1024]{1,0:T(8,128)}, f32[384,1024]{1,0:T(8,128)}) fusion(bf16[1,384,1024]{2,1,0:T(8,128)(2,1)S(1)} %copy-done.35, f32[384,1024]{1,0:T(8,128)S(1)} %copy-done.28, f32[384,1024]{1,0:T(8,128)S(1)} %bitcast_add_fusion.4, f32[384,1024]{1,0:T(8,128)S(1)} %collective-permute-done.38, ...), kind=kLoop, calls=%fused_computation.27 | loop fusion | flops 4718592 | bytes 11010048 | tf_op jit(solution)/shard_map/broadcast_in_dim | solution.py:400
  234.3 5.6 %collective-permute-done.29 = bf16[320,1024]{1,0:T(8,128)(2,1)S(1)} collective-permute-done((bf16[320,1024]{1,0:T(8,128)(2,1)S(1)}, bf16[320,1024]{1,0:T(8,128)(2,1)S(1)}, u32[]{:S(2)}, u32[]{:S(2)}) %collective-permute-start.29) | collective-permute-done | bytes 655392 | tf_op jit(solution)/shard_map/ppermute | solution.py:41
  239.9 1.9 fusion.4
  244.0 1.5 maximum_multiply_fusion
  (147 shorter events, 20.1 us)
Async XLA Ops:
  1.8 57.1 %collective-permute-start.2 = (bf16[320,1024]{1,0:T(8,128)(2,1)S(1)}, bf16[320,1024]{1,0:T(8,128)(2,1)S(1)}, u32[]{:S(2)}, u32[]{:S(2)}) collective-permute-start(bf16[320,1024]{1,0:T(8,128)(2,1)S(1)} %slice_bitcast_fusion.refs_0_), channel_id=1, source_target_pairs={{0,2},{1,3},{2,4},{3,5},{4,6},{5,7},{8,10},{9,11},{10,12},{11,13},... | collective-permute-start | bytes 1966088 | tf_op jit(solution)/shard_map/ppermute | solution.py:37
  5.3 53.6 %collective-permute-start.3 = (bf16[320,1024]{1,0:T(8,128)(2,1)S(1)}, bf16[320,1024]{1,0:T(8,128)(2,1)S(1)}, u32[]{:S(2)}, u32[]{:S(2)}) collective-permute-start(bf16[320,1024]{1,0:T(8,128)(2,1)S(1)} %slice_bitcast_fusion.refs_0_), channel_id=1, source_target_pairs={{2,0},{3,1},{4,2},{5,3},{6,4},{7,5},{10,8},{11,9},{12,10},{13,11},... | collective-permute-start | bytes 1966088 | tf_op jit(solution)/shard_map/ppermute | solution.py:41
  7.7 53.3 %collective-permute-start = (bf16[320,1024]{1,0:T(8,128)(2,1)S(1)}, bf16[320,1024]{1,0:T(8,128)(2,1)S(1)}, u32[]{:S(2)}, u32[]{:S(2)}) collective-permute-start(bf16[320,1024]{1,0:T(8,128)(2,1)S(1)} %slice_bitcast_fusion.refs_0_), channel_id=1, source_target_pairs={{0,1},{1,0},{2,3},{3,2},{4,5},{5,4},{6,7},{7,6},{8,9},{9,8},{10,11... | collective-permute-start | bytes 1966088 | tf_op jit(solution)/shard_map/ppermute | solution.py:45
  11.8 21.1 %collective-permute-start.1 = (bf16[208,1024]{1,0:T(8,128)(2,1)}, bf16[208,1024]{1,0:T(8,128)(2,1)}, u32[]{:S(2)}, u32[]{:S(2)}) collective-permute-start(bf16[208,1024]{1,0:T(8,128)(2,1)} %pad_maximum_fusion.1), channel_id=1, source_target_pairs={{0,1},{1,0},{2,3},{3,2},{4,5},{5,4},{6,7},{7,6},{8,9},{9,8},{10,11... | collective-permute-start | bytes 1277960 | tf_op jit(solution)/shard_map/ppermute | solution.py:45
  13.5 24.0 %copy-start.1 = (bf16[1,512,1024]{2,1,0:T(8,128)(2,1)S(1)}, bf16[1,512,1024]{2,1,0:T(8,128)(2,1)}, u32[]{:S(2)}) copy-start(bf16[1,512,1024]{2,1,0:T(8,128)(2,1)} %param.11) | copy-start | bytes 3145732
  34.0 28.6 %collective-permute-start.14 = (bf16[416,1024]{1,0:T(8,128)(2,1)S(1)}, bf16[416,1024]{1,0:T(8,128)(2,1)S(1)}, u32[]{:S(2)}, u32[]{:S(2)}) collective-permute-start(bf16[416,1024]{1,0:T(8,128)(2,1)S(1)} %pad_maximum_fusion.refs_2_), channel_id=1, source_target_pairs={{0,2},{1,3},{2,4},{3,5},{4,6},{5,7},{8,10},{9,11},{10,12},{11,13},... | collective-permute-start | bytes 2555912 | tf_op jit(solution)/shard_map/ppermute | solution.py:37
  51.3 20.8 %collective-permute-start.15 = (bf16[416,1024]{1,0:T(8,128)(2,1)S(1)}, bf16[416,1024]{1,0:T(8,128)(2,1)S(1)}, u32[]{:S(2)}, u32[]{:S(2)}) collective-permute-start(bf16[416,1024]{1,0:T(8,128)(2,1)S(1)} %pad_maximum_fusion.refs_2_), channel_id=1, source_target_pairs={{2,0},{3,1},{4,2},{5,3},{6,4},{7,5},{10,8},{11,9},{12,10},{13,11},... | collective-permute-start | bytes 2555912 | tf_op jit(solution)/shard_map/ppermute | solution.py:41
  53.8 51.8 %copy-start.17 = (f32[4,320,1024]{2,1,0:T(8,128)S(1)}, f32[4,320,1024]{2,1,0:T(8,128)}, u32[]{:S(2)}) copy-start(f32[4,320,1024]{2,1,0:T(8,128)} %get-tuple-element.65) | copy-start | bytes 15728644
  58.9 35.3 %copy-start.13 = (f32[1,2,192,1024]{3,2,1,0:T(8,128)}, f32[1,2,192,1024]{3,2,1,0:T(8,128)S(1)}, u32[]{:S(2)}) copy-start(f32[1,2,192,1024]{3,2,1,0:T(8,128)S(1)} %get-tuple-element.96) | copy-start | bytes 4718596
  58.9 35.3 %copy-start.15 = (f32[1,2,192,1024]{3,2,1,0:T(8,128)}, f32[1,2,192,1024]{3,2,1,0:T(8,128)S(1)}, u32[]{:S(2)}) copy-start(f32[1,2,192,1024]{3,2,1,0:T(8,128)S(1)} %get-tuple-element.94) | copy-start | bytes 4718596
  58.9 17.7 %collective-permute-start.21 = (bf16[320,1024]{1,0:T(8,128)(2,1)S(1)}, bf16[320,1024]{1,0:T(8,128)(2,1)S(1)}, u32[]{:S(2)}, u32[]{:S(2)}) collective-permute-start(bf16[320,1024]{1,0:T(8,128)(2,1)S(1)} %get-tuple-element.72), channel_id=1, source_target_pairs={{0,1},{1,0},{2,3},{3,2},{4,5},{5,4},{6,7},{7,6},{8,9},{9,8},{10,11... | collective-permute-start | bytes 1966088 | tf_op jit(solution)/shard_map/ppermute | solution.py:45
  60.5 30.2 %collective-permute-start.23 = (bf16[320,1024]{1,0:T(8,128)(2,1)S(1)}, bf16[320,1024]{1,0:T(8,128)(2,1)S(1)}, u32[]{:S(2)}, u32[]{:S(2)}) collective-permute-start(bf16[320,1024]{1,0:T(8,128)(2,1)S(1)} %get-tuple-element.74), channel_id=1, source_target_pairs={{0,1},{1,0},{2,3},{3,2},{4,5},{5,4},{6,7},{7,6},{8,9},{9,8},{10,11... | collective-permute-start | bytes 1966088 | tf_op jit(solution)/shard_map/ppermute | solution.py:45
  61.0 43.7 %collective-permute-start.22 = (bf16[320,1024]{1,0:T(8,128)(2,1)S(1)}, bf16[320,1024]{1,0:T(8,128)(2,1)S(1)}, u32[]{:S(2)}, u32[]{:S(2)}) collective-permute-start(bf16[320,1024]{1,0:T(8,128)(2,1)S(1)} %get-tuple-element.73), channel_id=1, source_target_pairs={{0,1},{1,0},{2,3},{3,2},{4,5},{5,4},{6,7},{7,6},{8,9},{9,8},{10,11... | collective-permute-start | bytes 1966088 | tf_op jit(solution)/shard_map/ppermute | solution.py:45
  62.5 53.0 %copy-start.37 = (bf16[416,1024]{1,0:T(8,128)(2,1)}, bf16[416,1024]{1,0:T(8,128)(2,1)S(1)}, u32[]{:S(2)}) copy-start(bf16[416,1024]{1,0:T(8,128)(2,1)S(1)} %collective-permute-done.14.refs_15_) | copy-start | bytes 2555908
  62.5 42.9 %collective-permute-start.4 = (bf16[320,1024]{1,0:T(8,128)(2,1)S(1)}, bf16[320,1024]{1,0:T(8,128)(2,1)S(1)}, u32[]{:S(2)}, u32[]{:S(2)}) collective-permute-start(bf16[320,1024]{1,0:T(8,128)(2,1)S(1)} %collective-permute-done.2.refs_3_), channel_id=1, source_target_pairs={{2,4},{3,5},{4,6},{5,7},{10,12},{11,13},{12,14},{13,15},{18,20},{1... | collective-permute-start | bytes 1966088 | tf_op jit(solution)/shard_map/ppermute | solution.py:37
  72.1 47.7 %copy-start.38 = (bf16[416,1024]{1,0:T(8,128)(2,1)}, bf16[416,1024]{1,0:T(8,128)(2,1)S(1)}, u32[]{:S(2)}) copy-start(bf16[416,1024]{1,0:T(8,128)(2,1)S(1)} %collective-permute-done.15.refs_18_) | copy-start | bytes 2555908
  72.1 34.0 %collective-permute-start.5 = (bf16[320,1024]{1,0:T(8,128)(2,1)S(1)}, bf16[320,1024]{1,0:T(8,128)(2,1)S(1)}, u32[]{:S(2)}, u32[]{:S(2)}) collective-permute-start(bf16[320,1024]{1,0:T(8,128)(2,1)S(1)} %collective-permute-done.3.refs_6_), channel_id=1, source_target_pairs={{2,0},{3,1},{4,2},{5,3},{10,8},{11,9},{12,10},{13,11},{18,16},{19,... | collective-permute-start | bytes 1966088 | tf_op jit(solution)/shard_map/ppermute | solution.py:41
  74.7 30.8 %copy-start.26 = (f32[1,384,1024]{2,1,0:T(8,128)S(1)}, f32[1,384,1024]{2,1,0:T(8,128)}, u32[]{:S(2)}) copy-start(f32[1,384,1024]{2,1,0:T(8,128)} %param.12) | copy-start | bytes 4718596
  76.7 29.4 %copy-start.22 = (bf16[320,1024]{1,0:T(8,128)(2,1)}, bf16[320,1024]{1,0:T(8,128)(2,1)S(1)}, u32[]{:S(2)}) copy-start(bf16[320,1024]{1,0:T(8,128)(2,1)S(1)} %collective-permute-done.21) | copy-start | bytes 1966084
  76.7 43.2 %collective-permute-start.30 = (bf16[384,1024]{1,0:T(8,128)(2,1)S(1)}, bf16[384,1024]{1,0:T(8,128)(2,1)S(1)}, u32[]{:S(2)}, u32[]{:S(2)}) collective-permute-start(bf16[384,1024]{1,0:T(8,128)(2,1)S(1)} %convert_element_type.142), channel_id=1, source_target_pairs={{0,2},{1,3},{8,10},{9,11},{16,18},{17,19},{24,26},{25,27}} | collective-permute-start | bytes 2359304 | tf_op jit(solution)/shard_map/ppermute | solution.py:37
  90.7 24.8 %collective-permute-start.11 = (bf16[320,1024]{1,0:T(8,128)(2,1)S(1)}, bf16[320,1024]{1,0:T(8,128)(2,1)S(1)}, u32[]{:S(2)}, u32[]{:S(2)}) collective-permute-start(bf16[320,1024]{1,0:T(8,128)(2,1)S(1)} %collective-permute-done.3.refs_6_), channel_id=1, source_target_pairs={{0,1},{1,0},{2,3},{3,2},{4,5},{5,4},{8,9},{9,8},{10,11},{11,10},{1... | collective-permute-start | bytes 1966088 | tf_op jit(solution)/shard_map/ppermute | solution.py:45
  104.8 17.0 %collective-permute-start.31 = (bf16[384,1024]{1,0:T(8,128)(2,1)S(1)}, bf16[384,1024]{1,0:T(8,128)(2,1)S(1)}, u32[]{:S(2)}, u32[]{:S(2)}) collective-permute-start(bf16[384,1024]{1,0:T(8,128)(2,1)S(1)} %convert_element_type.143), channel_id=1, source_target_pairs={{6,4},{7,5},{14,12},{15,13},{22,20},{23,21},{30,28},{31,29}} | collective-permute-start | bytes 2359304 | tf_op jit(solution)/shard_map/ppermute | solution.py:41
  105.5 38.7 %collective-permute-start.37 = (f32[384,1024]{1,0:T(8,128)S(1)}, f32[384,1024]{1,0:T(8,128)S(1)}, u32[]{:S(2)}, u32[]{:S(2)}) collective-permute-start(f32[384,1024]{1,0:T(8,128)S(1)} %bitcast.70), channel_id=1, source_target_pairs={{0,8},{8,0},{16,24},{24,16},{1,9},{9,1},{17,25},{25,17},{2,10},{10... | collective-permute-start | bytes 4718600 | tf_op jit(solution)/shard_map/ppermute | solution.py:283
  106.1 36.7 %copy-start.6 = (bf16[320,1024]{1,0:T(8,128)(2,1)}, bf16[320,1024]{1,0:T(8,128)(2,1)S(1)}, u32[]{:S(2)}) copy-start(bf16[320,1024]{1,0:T(8,128)(2,1)S(1)} %collective-permute-done.5.refs_7_) | copy-start | bytes 1966084
  106.1 19.0 %collective-permute-start.24 = (bf16[320,1024]{1,0:T(8,128)(2,1)S(1)}, bf16[320,1024]{1,0:T(8,128)(2,1)S(1)}, u32[]{:S(2)}, u32[]{:S(2)}) collective-permute-start(bf16[320,1024]{1,0:T(8,128)(2,1)S(1)} %get-tuple-element.103), channel_id=1, source_target_pairs={{0,2},{1,3},{8,10},{9,11},{16,18},{17,19},{24,26},{25,27}} | collective-permute-start | bytes 1966088 | tf_op jit(solution)/shard_map/ppermute | solution.py:37
  115.6 26.0 %collective-permute-start.16 = (bf16[416,1024]{1,0:T(8,128)(2,1)S(1)}, bf16[416,1024]{1,0:T(8,128)(2,1)}, u32[]{:S(2)}, u32[]{:S(2)}) collective-permute-start(bf16[416,1024]{1,0:T(8,128)(2,1)S(1)} %collective-permute-done.14.refs_15_), channel_id=1, source_target_pairs={{2,4},{3,5},{4,6},{5,7},{10,12},{11,13},{12,14},{13,15},{18,20},{1... | collective-permute-start | bytes 2555912 | tf_op jit(solution)/shard_map/ppermute | solution.py:37
  119.9 23.0 %collective-permute-start.17 = (bf16[416,1024]{1,0:T(8,128)(2,1)S(1)}, bf16[416,1024]{1,0:T(8,128)(2,1)}, u32[]{:S(2)}, u32[]{:S(2)}) collective-permute-start(bf16[416,1024]{1,0:T(8,128)(2,1)S(1)} %collective-permute-done.15.refs_18_), channel_id=1, source_target_pairs={{2,0},{3,1},{4,2},{5,3},{10,8},{11,9},{12,10},{13,11},{18,16},{19,... | collective-permute-start | bytes 2555912 | tf_op jit(solution)/shard_map/ppermute | solution.py:41
  121.8 4.5 %collective-permute-start.25 = (bf16[320,1024]{1,0:T(8,128)(2,1)S(1)}, bf16[320,1024]{1,0:T(8,128)(2,1)S(1)}, u32[]{:S(2)}, u32[]{:S(2)}) collective-permute-start(bf16[320,1024]{1,0:T(8,128)(2,1)S(1)} %get-tuple-element.102), channel_id=1, source_target_pairs={{6,4},{7,5},{14,12},{15,13},{22,20},{23,21},{30,28},{31,29}} | collective-permute-start | bytes 1966088 | tf_op jit(solution)/shard_map/ppermute | solution.py:41
  125.1 20.7 %collective-permute-start.6 = (bf16[320,1024]{1,0:T(8,128)(2,1)S(1)}, bf16[320,1024]{1,0:T(8,128)(2,1)S(1)}, u32[]{:S(2)}, u32[]{:S(2)}) collective-permute-start(bf16[320,1024]{1,0:T(8,128)(2,1)S(1)} %collective-permute-done.4.refs_4_), channel_id=1, source_target_pairs={{4,6},{5,7},{12,14},{13,15},{20,22},{21,23},{28,30},{29,31}} | collective-permute-start | bytes 1966088 | tf_op jit(solution)/shard_map/ppermute | solution.py:37
  126.4 36.3 %collective-permute-start.32 = (bf16[384,1024]{1,0:T(8,128)(2,1)S(1)}, bf16[384,1024]{1,0:T(8,128)(2,1)S(1)}, u32[]{:S(2)}, u32[]{:S(2)}) collective-permute-start(bf16[384,1024]{1,0:T(8,128)(2,1)S(1)} %get-tuple-element.105), channel_id=1, source_target_pairs={{0,2},{1,3},{2,4},{3,5},{8,10},{9,11},{10,12},{11,13},{16,18},{17,... | collective-permute-start | bytes 2359304 | tf_op jit(solution)/shard_map/ppermute | solution.py:37
  141.5 23.1 %collective-permute-start.33 = (bf16[384,1024]{1,0:T(8,128)(2,1)S(1)}, bf16[384,1024]{1,0:T(8,128)(2,1)S(1)}, u32[]{:S(2)}, u32[]{:S(2)}) collective-permute-start(bf16[384,1024]{1,0:T(8,128)(2,1)S(1)} %get-tuple-element.104), channel_id=1, source_target_pairs={{4,2},{5,3},{6,4},{7,5},{12,10},{13,11},{14,12},{15,13},{20,18},{2... | collective-permute-start | bytes 2359304 | tf_op jit(solution)/shard_map/ppermute | solution.py:41
  142.9 16.5 %collective-permute-start.7 = (bf16[320,1024]{1,0:T(8,128)(2,1)S(1)}, bf16[320,1024]{1,0:T(8,128)(2,1)S(1)}, u32[]{:S(2)}, u32[]{:S(2)}) collective-permute-start(bf16[320,1024]{1,0:T(8,128)(2,1)S(1)} %collective-permute-done.5.refs_7_), channel_id=1, source_target_pairs={{2,0},{3,1},{10,8},{11,9},{18,16},{19,17},{26,24},{27,25}} | collective-permute-start | bytes 1966088 | tf_op jit(solution)/shard_map/ppermute | solution.py:41
  144.2 40.0 %collective-permute-start.18 = (bf16[416,1024]{1,0:T(8,128)(2,1)}, bf16[416,1024]{1,0:T(8,128)(2,1)}, u32[]{:S(2)}, u32[]{:S(2)}) collective-permute-start(bf16[416,1024]{1,0:T(8,128)(2,1)} %collective-permute-done.16.refs_16_), channel_id=1, source_target_pairs={{4,6},{5,7},{12,14},{13,15},{20,22},{21,23},{28,30},{29,31}} | collective-permute-start | bytes 2555912 | tf_op jit(solution)/shard_map/ppermute | solution.py:37
  145.8 39.1 %collective-permute-start.19 = (bf16[416,1024]{1,0:T(8,128)(2,1)}, bf16[416,1024]{1,0:T(8,128)(2,1)}, u32[]{:S(2)}, u32[]{:S(2)}) collective-permute-start(bf16[416,1024]{1,0:T(8,128)(2,1)} %collective-permute-done.17.refs_19_), channel_id=1, source_target_pairs={{2,0},{3,1},{10,8},{11,9},{18,16},{19,17},{26,24},{27,25}} | collective-permute-start | bytes 2555912 | tf_op jit(solution)/shard_map/ppermute | solution.py:41
  159.3 19.1 %collective-permute-start.8 = (bf16[320,1024]{1,0:T(8,128)(2,1)S(1)}, bf16[320,1024]{1,0:T(8,128)(2,1)}, u32[]{:S(2)}, u32[]{:S(2)}) collective-permute-start(bf16[320,1024]{1,0:T(8,128)(2,1)S(1)} %collective-permute-done.2.refs_3_), channel_id=1, source_target_pairs={{2,3},{3,2},{4,5},{5,4},{6,7},{7,6},{10,11},{11,10},{12,13},{13,12... | collective-permute-start | bytes 1966088 | tf_op jit(solution)/shard_map/ppermute | solution.py:45
  162.7 19.1 %collective-permute-start.26 = (bf16[320,1024]{1,0:T(8,128)(2,1)}, bf16[320,1024]{1,0:T(8,128)(2,1)}, u32[]{:S(2)}, u32[]{:S(2)}) collective-permute-start(bf16[320,1024]{1,0:T(8,128)(2,1)} %get-tuple-element.99), channel_id=1, source_target_pairs={{0,2},{1,3},{2,4},{3,5},{8,10},{9,11},{10,12},{11,13},{16,18},{17,... | collective-permute-start | bytes 1966088 | tf_op jit(solution)/shard_map/ppermute | solution.py:37
  164.7 17.8 %collective-permute-start.27 = (bf16[320,1024]{1,0:T(8,128)(2,1)}, bf16[320,1024]{1,0:T(8,128)(2,1)}, u32[]{:S(2)}, u32[]{:S(2)}) collective-permute-start(bf16[320,1024]{1,0:T(8,128)(2,1)} %get-tuple-element.98), channel_id=1, source_target_pairs={{4,2},{5,3},{6,4},{7,5},{12,10},{13,11},{14,12},{15,13},{20,18},{2... | collective-permute-start | bytes 1966088 | tf_op jit(solution)/shard_map/ppermute | solution.py:41
  178.4 16.4 %collective-permute-start.12 = (bf16[320,1024]{1,0:T(8,128)(2,1)S(1)}, bf16[320,1024]{1,0:T(8,128)(2,1)}, u32[]{:S(2)}, u32[]{:S(2)}) collective-permute-start(bf16[320,1024]{1,0:T(8,128)(2,1)S(1)} %copy-done.7), channel_id=1, source_target_pairs={{0,1},{1,0},{2,3},{3,2},{8,9},{9,8},{10,11},{11,10},{16,17},{17,16... | collective-permute-start | bytes 1966088 | tf_op jit(solution)/shard_map/ppermute | solution.py:45
  181.8 14.5 %collective-permute-start.9 = (bf16[320,1024]{1,0:T(8,128)(2,1)S(1)}, bf16[320,1024]{1,0:T(8,128)(2,1)S(1)}, u32[]{:S(2)}, u32[]{:S(2)}) collective-permute-start(bf16[320,1024]{1,0:T(8,128)(2,1)S(1)} %copy-done.5), channel_id=1, source_target_pairs={{4,5},{5,4},{6,7},{7,6},{12,13},{13,12},{14,15},{15,14},{20,21},{2... | collective-permute-start | bytes 1966088 | tf_op jit(solution)/shard_map/ppermute | solution.py:45
  182.5 48.9 %collective-permute-start.38 = (f32[384,1024]{1,0:T(8,128)S(1)}, f32[384,1024]{1,0:T(8,128)S(1)}, u32[]{:S(2)}, u32[]{:S(2)}) collective-permute-start(f32[384,1024]{1,0:T(8,128)S(1)} %bitcast_add_fusion.4), channel_id=1, source_target_pairs={{0,16},{8,24},{16,0},{24,8},{1,17},{9,25},{17,1},{25,9},{2,18},{10... | collective-permute-start | bytes 4718600 | tf_op jit(solution)/shard_map/ppermute | solution.py:283
  184.2 14.0 %collective-permute-start.10 = (bf16[320,1024]{1,0:T(8,128)(2,1)S(1)}, bf16[320,1024]{1,0:T(8,128)(2,1)S(1)}, u32[]{:S(2)}, u32[]{:S(2)}) collective-permute-start(bf16[320,1024]{1,0:T(8,128)(2,1)S(1)} %copy-done.9), channel_id=1, source_target_pairs={{6,7},{7,6},{14,15},{15,14},{22,23},{23,22},{30,31},{31,30}} | collective-permute-start | bytes 1966088 | tf_op jit(solution)/shard_map/ppermute | solution.py:45
  184.9 17.2 %collective-permute-start.13 = (bf16[320,1024]{1,0:T(8,128)(2,1)S(1)}, bf16[320,1024]{1,0:T(8,128)(2,1)S(1)}, u32[]{:S(2)}, u32[]{:S(2)}) collective-permute-start(bf16[320,1024]{1,0:T(8,128)(2,1)S(1)} %copy-done.11), channel_id=1, source_target_pairs={{0,1},{1,0},{8,9},{9,8},{16,17},{17,16},{24,25},{25,24}} | collective-permute-start | bytes 1966088 | tf_op jit(solution)/shard_map/ppermute | solution.py:45
  194.9 45.1 %collective-permute-start.20 = (bf16[320,1024]{1,0:T(8,128)(2,1)S(1)}, bf16[320,1024]{1,0:T(8,128)(2,1)S(1)}, u32[]{:S(2)}, u32[]{:S(2)}) collective-permute-start(bf16[320,1024]{1,0:T(8,128)(2,1)S(1)} %copy-done.3), channel_id=1, source_target_pairs={{0,1},{1,0},{2,3},{3,2},{4,5},{5,4},{6,7},{7,6},{8,9},{9,8},{10,11... | collective-permute-start | bytes 1966088 | tf_op jit(solution)/shard_map/ppermute | solution.py:45
  196.3 31.0 %collective-permute-start.35 = (bf16[384,1024]{1,0:T(8,128)(2,1)S(1)}, bf16[384,1024]{1,0:T(8,128)(2,1)S(1)}, u32[]{:S(2)}, u32[]{:S(2)}) collective-permute-start(bf16[384,1024]{1,0:T(8,128)(2,1)S(1)} %add_convert_fusion), channel_id=1, source_target_pairs={{2,0},{3,1},{4,2},{5,3},{6,4},{7,5},{10,8},{11,9},{12,10},{13,11},... | collective-permute-start | bytes 2359304 | tf_op jit(solution)/shard_map/ppermute | solution.py:41
  198.2 31.2 %collective-permute-start.34 = (bf16[384,1024]{1,0:T(8,128)(2,1)S(1)}, bf16[384,1024]{1,0:T(8,128)(2,1)S(1)}, u32[]{:S(2)}, u32[]{:S(2)}) collective-permute-start(bf16[384,1024]{1,0:T(8,128)(2,1)S(1)} %add_convert_fusion.1), channel_id=1, source_target_pairs={{0,2},{1,3},{2,4},{3,5},{4,6},{5,7},{8,10},{9,11},{10,12},{11,13},... | collective-permute-start | bytes 2359304 | tf_op jit(solution)/shard_map/ppermute | solution.py:37
  202.2 32.2 %collective-permute-start.28 = (bf16[320,1024]{1,0:T(8,128)(2,1)}, bf16[320,1024]{1,0:T(8,128)(2,1)}, u32[]{:S(2)}, u32[]{:S(2)}) collective-permute-start(bf16[320,1024]{1,0:T(8,128)(2,1)} %get-tuple-element.101), channel_id=1, source_target_pairs={{0,2},{1,3},{2,4},{3,5},{4,6},{5,7},{8,10},{9,11},{10,12},{11,13},... | collective-permute-start | bytes 1966088 | tf_op jit(solution)/shard_map/ppermute | solution.py:37
  227.3 12.6 %collective-permute-start.29 = (bf16[320,1024]{1,0:T(8,128)(2,1)S(1)}, bf16[320,1024]{1,0:T(8,128)(2,1)S(1)}, u32[]{:S(2)}, u32[]{:S(2)}) collective-permute-start(bf16[320,1024]{1,0:T(8,128)(2,1)S(1)} %get-tuple-element.100), channel_id=1, source_target_pairs={{2,0},{3,1},{4,2},{5,3},{6,4},{7,5},{10,8},{11,9},{12,10},{13,11},... | collective-permute-start | bytes 1966088 | tf_op jit(solution)/shard_map/ppermute | solution.py:41
  229.9 12.0 %collective-permute-start.36 = (bf16[192,1024]{1,0:T(8,128)(2,1)S(1)}, bf16[192,1024]{1,0:T(8,128)(2,1)S(1)}, u32[]{:S(2)}, u32[]{:S(2)}) collective-permute-start(bf16[192,1024]{1,0:T(8,128)(2,1)S(1)} %slice.79), channel_id=1, source_target_pairs={{0,1},{1,0},{2,3},{3,2},{4,5},{5,4},{6,7},{7,6},{8,9},{9,8},{10,11... | collective-permute-start | bytes 1179656 | tf_op jit(solution)/shard_map/ppermute | solution.py:45
  (34 other events, 335.1 us)

commit v5 on v3

--- a/solution.py
+++ b/solution.py
@@ -10,7 +10,6 @@
 
 HEAD = 128
 SEQ_LEN = 4096
-PAD = 16
 
 
 epsilon = 1e-05
@@ -39,11 +38,26 @@
         spot = (self.spot + self.count + jnp.array(distances, jnp.int32)) % self.count
         return jnp.where(spot < self.half, 2 * spot, 2 * (self.count - 1 - spot) + 1)
 
-    def to_right(self, value):
-        return lax.ppermute(value, "fsdp", self.right)
-
-    def to_left(self, value):
-        return lax.ppermute(value, "fsdp", self.left)
+    def to_right(self, value, skip=()):
+        return lax.ppermute(value, "fsdp", [p for p in self.right if p[0] not in skip])
+
+    def to_left(self, value, skip=()):
+        return lax.ppermute(value, "fsdp", [p for p in self.left if p[0] not in skip])
+
+
+class Plane(Ring):
+    first, second = (2, 5), (4, 3)
+    chords = [(2, 3), (3, 2), (4, 5), (5, 4)]
+    inward = [(0, 2), (6, 4), (7, 5), (1, 3)]
+    outward = [(2, 0), (4, 6), (5, 7), (3, 1)]
+
+    def __init__(self):
+        super().__init__()
+        self.is_first = (self.me == 2) | (self.me == 5)
+        self.is_second = (self.me == 4) | (self.me == 3)
+
+    def send(self, value, pairs):
+        return lax.ppermute(value, "fsdp", pairs)
 
 
 def after(value, *others):
@@ -59,10 +73,10 @@
     return jnp.concatenate([cosine, cosine], axis=1), jnp.concatenate([-sine, sine], axis=1)
 
 
-def first_kernel(scale, at, x, cotangent, cosine, sine, kv_grad, inv, top, bottom, near):
+def first_kernel(scale, at, x, cotangent, cosine, sine, kv_grad, inv, far, near):
     step = pl.program_id(0)
     width = x.shape[1]
-    shard, cut = near.shape[1], top.shape[0]
+    shard = far.shape[0]
     kvw = cotangent.shape[1] // 2
 
     @pl.when(step == 0)
@@ -88,8 +102,7 @@
 
     @pl.when(step == 0)
     def _():
-        top[...] = term[:cut].astype(bf16)
-        bottom[...] = term[cut:].astype(bf16)
+        far[...] = term.astype(bf16)
 
     @pl.when(step > 0)
     def _():
@@ -119,16 +132,14 @@
             out_specs=[
                 pl.BlockSpec((rows, cols), fixed),
                 pl.BlockSpec((rows, HEAD), fixed),
-                pl.BlockSpec((shard // 2, cols), fixed),
-                pl.BlockSpec((shard - shard // 2, cols), fixed),
+                pl.BlockSpec((shard, cols), fixed),
                 pl.BlockSpec((1, shard, cols), lambda k, at: (jnp.maximum(k - 1, 0), 0, 0)),
             ],
         ),
         out_shape=[
             jax.ShapeDtypeStruct((rows, cols), bf16),
             jax.ShapeDtypeStruct((rows, HEAD), f32),
-            jax.ShapeDtypeStruct((shard // 2, cols), bf16),
-            jax.ShapeDtypeStruct((shard - shard // 2, cols), bf16),
+            jax.ShapeDtypeStruct((shard, cols), bf16),
             jax.ShapeDtypeStruct((n - 1, shard, cols), f32),
         ],
         compiler_params=pltpu.CompilerParams(vmem_limit_bytes=40 * 2**20),
@@ -141,14 +152,13 @@
     )(ring.devices_at(order), tokens_in, cotangent, cosine, sine)
 
 
-def second_kernel(n, at, x, kv_grad, inv, cosine, sine, *refs):
-    blocks, refs = refs[: n + 1], refs[n + 1 :]
+def second_kernel(plan, at, x, kv_grad, inv, cosine, sine, *refs):
+    n = len(plan)
+    blocks, refs = refs[:-10], refs[-10:]
     kv_out, input_grad, xs, ws, ng, pre, out, x_sem, w_sem, o_sem = refs
     rows, width = x.shape
     shard = xs.shape[2]
-    cols = pre.shape[1]
-    kvw = cols // 2
-    cut = shard // 2
+    kvw = pre.shape[1] // 2
 
     def columns(k):
         return pl.ds(pl.multiple_of(at[k] * shard, shard), shard)
@@ -161,27 +171,26 @@
 
     for k in range(n):
         x_copy(k).start()
-        if k < n - 1:
-            pltpu.make_async_copy(blocks[k], ws.at[k], w_sem.at[k]).start()
-        else:
-            pltpu.make_async_copy(blocks[k], ws.at[k, :cut], w_sem.at[k]).start()
-            pltpu.make_async_copy(blocks[k + 1], ws.at[k, cut:], w_sem.at[k]).start()
+        for flag, block, start, stop in plan[k]:
+            copy = pltpu.make_async_copy(blocks[block], ws.at[k, start:stop], w_sem.at[k])
+            if flag is None:
+                copy.start()
+            else:
+
+                @pl.when(at[n + flag] == 1)
+                def _(copy=copy):
+                    copy.start()
 
     pre[...] = jnp.zeros_like(pre)
 
     def gather(k, total):
         x_copy(k).wait()
         pltpu.make_async_copy(ws.at[k], ws.at[k], w_sem.at[k]).wait()
-        weight = ws[k, :shard, :]
-        gain = ws[k, shard : shard + PAD, :shard].astype(f32)[:1]
+        weight = ws[k]
         normed = xs[k].astype(f32) * inv[:, :1]
-        hidden = (normed * gain).astype(bf16)
-        pre[...] += jnp.dot(hidden, weight, preferred_element_type=f32)
-        grad = (
-            lax.dot_general(
-                kv_grad[...], weight, (((1,), (1,)), ((), ())), preferred_element_type=f32
-            )
-            * gain
+        pre[...] += jnp.dot(normed.astype(bf16), weight, preferred_element_type=f32)
+        grad = lax.dot_general(
+            kv_grad[...], weight, (((1,), (1,)), ((), ())), preferred_element_type=f32
         )
         ng[k] = grad
         product = grad * normed
@@ -213,7 +222,7 @@
     lax.fori_loop(0, n, drain, 0)
 
 
-def second_part(ring, tokens_in, kv_grad, inv, cosine, sine, blocks, shard):
+def second_part(ring, tokens_in, kv_grad, inv, cosine, sine, blocks, plan, flags, shard):
     rows, width = tokens_in.shape
     cols = kv_grad.shape[1]
     n = ring.count
@@ -221,10 +230,11 @@
     for d in range(1, ring.half):
         order += [-d, d]
     order.append(ring.half)
+    at = jnp.concatenate([ring.devices_at(order).astype(jnp.int32), flags.astype(jnp.int32)])
     whole = pl.BlockSpec(memory_space=pltpu.VMEM)
     there = pl.BlockSpec(memory_space=pl.ANY)
     return pl.pallas_call(
-        functools.partial(second_kernel, n),
+        functools.partial(second_kernel, plan),
         in_specs=[pl.BlockSpec(memory_space=pltpu.SMEM), there]
         + [whole] * 4
         + [there] * len(blocks),
@@ -235,7 +245,7 @@
         ],
         scratch_shapes=[
             pltpu.VMEM((n, rows, shard), bf16),
-            pltpu.VMEM((n, shard + PAD, cols), bf16),
+            pltpu.VMEM((n, shard, cols), bf16),
             pltpu.VMEM((n, rows, shard), f32),
             pltpu.VMEM((rows, cols), f32),
             pltpu.VMEM((n, rows, shard), bf16),
@@ -250,7 +260,7 @@
             transcendentals=0,
         ),
         name="project_and_input_grad",
-    )(ring.devices_at(order), tokens_in, kv_grad, inv, cosine, sine, *blocks)
+    )(at, tokens_in, kv_grad, inv, cosine, sine, *blocks)
 
 
 def replica_sum(value):
@@ -265,29 +275,77 @@
     return value
 
 
-def gather_blocks(ring, own, cut, other):
+def exchange_ring(ring, own, far, near, pseudo):
+    total = replica_sum(pseudo)
+    shard, cut = own.shape[0], own.shape[0] // 2
     blocks = [own]
     from_left = from_right = own
     for d in range(1, ring.half):
         from_left, from_right = ring.to_right(from_left), ring.to_left(from_right)
         blocks += [from_left, from_right]
-    from_left, from_right = after(from_left, other), after(from_right, other)
+    from_left, from_right = after((from_left, from_right), total)
     blocks += [ring.to_right(from_left[:cut]), ring.to_left(from_right[cut:])]
-    return blocks
-
-
-def scatter_terms(ring, top, bottom, near):
-    cut, rest = top.shape[0], bottom.shape[0]
-    from_left, from_right = ring.to_right(top), ring.to_left(bottom)
+    last = len(blocks) - 2
+    plan = [((None, k, 0, shard),) for k in range(last)]
+    plan.append(((None, last, 0, cut), (None, last + 1, cut, shard)))
+
+    far = after(far, blocks[1], blocks[2])
+    from_left, from_right = ring.to_right(far[:cut]), ring.to_left(far[cut:])
     for k in range(0, 2 * (ring.half - 1), 2):
         from_left, from_right = lax.optimization_barrier((from_left, from_right))
         if k == 0:
-            from_left = jnp.pad(from_left, ((0, rest), (0, 0)))
+            from_left = jnp.pad(from_left, ((0, shard - cut), (0, 0)))
             from_right = jnp.pad(from_right, ((cut, 0), (0, 0)))
         from_left = ring.to_right((near[k] + from_left.astype(f32)).astype(bf16))
         from_right = ring.to_left((near[k + 1] + from_right.astype(f32)).astype(bf16))
-    from_left, from_right = from_left.astype(f32), from_right.astype(f32)
-    return near[-1] + from_left + from_right
+    term = near[-1] + from_left.astype(f32) + from_right.astype(f32)
+    return blocks, plan, jnp.zeros((1,), jnp.int32), term, total
+
+
+def exchange_plane(plane, own, far, near, pseudo):
+    first, second = plane.first, plane.second
+    left1, right1 = plane.to_right(own), plane.to_left(own)
+    partner = plane.send(own, plane.chords)
+    left1, right1, partner = lax.optimization_barrier((left1, right1, partner))
+    left2, right2 = plane.to_right(left1), plane.to_left(right1)
+    far_inner = plane.send(jnp.where(plane.is_second, left1, right1), plane.chords)
+    total = replica_sum(after(pseudo, left1, right1))
+    left2, right2 = lax.optimization_barrier((left2, right2))
+    far = after(far, left2, right2)
+    left3, right3 = plane.to_right(left2, (0, 7)), plane.to_left(right2, (6, 1))
+    from_outer = plane.send(far, plane.inward)
+    left3, right3, from_outer, far_inner, far = lax.optimization_barrier(
+        (left3, right3, from_outer, far_inner, far)
+    )
+    far_outer = plane.send(jnp.where(plane.is_second, left3, right3), plane.outward)
+    from_inner = plane.send(far, plane.chords)
+    from_outer = from_outer.astype(f32)
+    sum_r = plane.to_right((near[0] + from_outer).astype(bf16), second)
+    sum_l = plane.to_left((near[1] + from_outer).astype(bf16), first)
+    sum_r, sum_l, far_outer, from_inner, total = lax.optimization_barrier(
+        (sum_r, sum_l, far_outer, from_inner, total)
+    )
+    for_partner = after(jnp.where(plane.is_first, near[1], near[0]).astype(bf16), sum_r)
+    from_partner = plane.send(for_partner, plane.chords)
+    sum_r = plane.to_right((near[2] + sum_r.astype(f32)).astype(bf16))
+    sum_l = plane.to_left((near[3] + sum_l.astype(f32)).astype(bf16))
+    sum_r, sum_l = lax.optimization_barrier((sum_r, sum_l))
+    from_inner = from_inner.astype(f32)
+    more_r = near[4] + jnp.where(plane.is_first, from_inner, 0.0)
+    more_l = near[5] + jnp.where(plane.is_second, from_inner, 0.0)
+    sum_r = plane.to_right((more_r + sum_r.astype(f32)).astype(bf16))
+    sum_l = plane.to_left((more_l + sum_l.astype(f32)).astype(bf16))
+    term = near[6] + from_partner.astype(f32) + sum_r.astype(f32) + sum_l.astype(f32)
+
+    blocks = [own, left1, right1, left2, right2, left3, right3, partner, far_inner, far_outer]
+    shard = own.shape[0]
+    plan = [((None, k, 0, shard),) for k in range(5)]
+    plan.append(((0, 7, 0, shard), (1, 5, 0, shard)))
+    plan.append(((2, 7, 0, shard), (3, 6, 0, shard)))
+    plan.append(((4, 8, 0, shard), (5, 9, 0, shard)))
+    inner = plane.is_first | plane.is_second
+    flags = [plane.is_first, ~plane.is_first, plane.is_second, ~plane.is_second, inner, ~inner]
+    return blocks, plan, jnp.stack(flags), term, total
 
 
 def local(
@@ -300,29 +358,27 @@
     global_params,
     local_params,
 ):
-    ring = Ring()
+    small = lax.axis_size("fsdp") == 8
+    ring = Plane() if small else Ring()
     tokens_in = layer_input[0]
-    gain_shard = norm_gain[0]
+    gain_shard = norm_gain[0].astype(f32)[:, None]
     weight_shard = kv_weight[0]
     cotangent = kv_cotangent[0]
     rows, width = tokens_in.shape
     shard, cols = weight_shard.shape
 
-    gain_rows = jnp.pad(gain_shard[None, :], ((0, PAD - 1), (0, cols - shard)))
-    own = jnp.concatenate([weight_shard, gain_rows], axis=0)
-    total = replica_sum(pseudo_grad[0])
-    blocks = gather_blocks(ring, own, shard // 2, total)
-
+    weight_f = weight_shard.astype(f32)
+    own = (weight_f * gain_shard).astype(bf16)
     positions = (ring.me * rows + jnp.arange(rows, dtype=jnp.int32)) % SEQ_LEN
     cosine, sine = rope_tables(positions)
     scale = 1.0 / math.sqrt(rows * ring.count)
-    kv_grad, inv, top, bottom, near = first_part(
+    kv_grad, inv, far, near = first_part(
         ring, tokens_in, cotangent, cosine, sine, shard, scale
     )
-    top, bottom = after((top, bottom), blocks[1], blocks[2])
-    term = scatter_terms(ring, top, bottom, near)
-    weight_grad = term * gain_shard.astype(f32)[:, None]
-    gain_grad = jnp.sum(term * weight_shard.astype(f32), axis=1)
+    exchange = exchange_plane if small else exchange_ring
+    blocks, plan, flags, term, total = exchange(ring, own, far, near, pseudo_grad[0])
+    weight_grad = term * gain_shard
+    gain_grad = jnp.sum(term * weight_f, axis=1)
 
     replicas = lax.axis_size("replica")
     average = total / replicas
@@ -333,7 +389,7 @@
     ).astype(bf16)
 
     kv_out, input_grad = second_part(
-        ring, tokens_in, kv_grad, inv, cosine, sine, blocks, shard
+        ring, tokens_in, kv_grad, inv, cosine, sine, blocks, plan, flags, shard
     )
     return (
         kv_out[None],

time: 174 us -> 176 us (1.011); the launches traced: 172 us -> 172 us
  waiting for transfers between devices: 102 us -> 76.4 us
  starting transfers between devices: 18.1 us -> 38.4 us
  other arithmetic: 20.5 us -> 25.8 us
    ppermute x16 -> x18, waiting for transfers between devices: 102 us -> 76.4 us  [the longest x6 35.3 us: to_right(): lax.ppermute(value, 'fsdp', [p for p in self.right if p[0] not in skip])]
    ppermute x16 -> x18, starting transfers between devices: 16.5 us -> 36.7 us  [the longest x6 16.1 us: send(): return lax.ppermute(value, 'fsdp', pairs)]
    convert_element_type x4 -> x7, other arithmetic: 8.91 us -> 15.8 us  [the longest x1 4.31 us: exchange_plane(): sum_l = plane.to_left((near[3] + sum_l.astype(f32)).astype(bf16))]
  transfers between devices with their start and end apart: 18 -> 20, of which waited for: 14 -> 13; matrix products, arithmetic and copies ran while one was open for 9% -> 9% of each run, Pallas kernels for 17% -> 17%
where the time goes in v5:
time: 176 us; the launch traced here: 172 us
  waiting for transfers between devices  76.4 us (43%)
  starting transfers between devices  38.4 us (22%)
  Pallas kernels  28.5 us (16%)
  other arithmetic  25.8 us (15%)
  local copies, waits for them, and re-layouts  2.38 us (1%)
    ppermute x6, waiting for transfers between devices, to_right(): lax.ppermute(value, 'fsdp', [p for p in self.right if p[0] not in skip])  35.3 us
    ppermute x6, waiting for transfers between devices, send(): return lax.ppermute(value, 'fsdp', pairs)  27.3 us
    pallas_call x1, Pallas kernels, second_part(): pl.pallas_call(functools.partial(second_kernel, plan), in_specs=[pl.Block...  16.6 us
    ppermute x6, starting transfers between devices, send(): return lax.ppermute(value, 'fsdp', pairs)  16.1 us
    ppermute x6, waiting for transfers between devices, to_left(): lax.ppermute(value, 'fsdp', [p for p in self.left if p[0] not in skip])  13.8 us
    pallas_call x1, Pallas kernels, first_part(): pl.pallas_call(functools.partial(first_kernel, scale), grid_spec=pltpu.Pr...  11.9 us
    ppermute x6, starting transfers between devices, to_right(): lax.ppermute(value, 'fsdp', [p for p in self.right if p[0] not in skip])  10.9 us
    ppermute x6, starting transfers between devices, to_left(): lax.ppermute(value, 'fsdp', [p for p in self.left if p[0] not in skip])  9.7 us
  transfers between devices with their start and end apart: 20, of which 13 were waited for; matrix products, arithmetic and copies ran while one was open for 9% of the time, Pallas kernels for 17%

profile of v5, /device:TPU:8, one launch (start us, length us, event | category | flops | bytes accessed | tf_op | source)
XLA Modules:
  0.0 172.5 jit_solution(11548067156220185860)
XLA Ops:
  0.6 0.7 convert_element_type.113
  1.3 1.5 fusion.8.refs_0_
  2.8 1.6 collective-permute-start
  4.4 0.4 collective-permute-start.1
  4.9 3.4 %collective-permute-start.2 = (bf16[512,1024]{1,0:T(8,128)(2,1)S(1)}, bf16[512,1024]{1,0:T(8,128)(2,1)}, u32[]{:S(2)}, u32[]{:S(2)}) collective-permute-start(bf16[512,1024]{1,0:T(8,128)(2,1)S(1)} %fusion.8.refs_0_), channel_id=1, source_target_pairs={{2,3},{3,2},{4,5},{5,4},{10,11},{11,10},{12,13},{13,12},{18,19},{1... | collective-permute-start | bytes 3145736 | tf_op jit(solution)/shard_map/ppermute | solution.py:60
  8.3 1.0 fusion.18
  9.3 18.4 %collective-permute-done.refs_1_ = bf16[512,1024]{1,0:T(8,128)(2,1)S(1)} collective-permute-done((bf16[512,1024]{1,0:T(8,128)(2,1)S(1)}, bf16[512,1024]{1,0:T(8,128)(2,1)S(1)}, u32[]{:S(2)}, u32[]{:S(2)}) %collective-permute-start) | collective-permute-done | bytes 1048608 | tf_op jit(solution)/shard_map/ppermute | solution.py:42
  27.8 1.3 collective-permute-done.1.refs_2_
  29.0 2.2 %collective-permute-done.2.refs_7_ = bf16[512,1024]{1,0:T(8,128)(2,1)} collective-permute-done((bf16[512,1024]{1,0:T(8,128)(2,1)S(1)}, bf16[512,1024]{1,0:T(8,128)(2,1)}, u32[]{:S(2)}, u32[]{:S(2)}) %collective-permute-start.2) | collective-permute-done | bytes 1048608 | tf_op jit(solution)/shard_map/ppermute | solution.py:60
  31.2 1.6 collective-permute-start.3
  32.8 0.4 collective-permute-start.4
  33.2 0.2 pad_maximum_fusion
  33.6 2.2 %copy-done.2 = bf16[1,512,4096]{2,1,0:T(8,128)(2,1)S(1)} copy-done((bf16[1,512,4096]{2,1,0:T(8,128)(2,1)S(1)}, bf16[1,512,4096]{2,1,0:T(8,128)(2,1)}, u32[]{:S(2)}) %copy-start.2) | copy-done | bytes 4194328
  35.8 11.9 %norm_and_weight_terms.1 = (bf16[512,1024]{1,0:T(8,128)(2,1)S(1)}, f32[512,128]{1,0:T(8,128)S(1)}, bf16[512,1024]{1,0:T(8,128)(2,1)S(1)}, f32[7,512,1024]{2,1,0:T(8,128)}) custom-call(s32[8]{0:T(128)S(1)} %compare_select_fusion.4.at, bf16[512,4096]{1,0:T(8,128)(2,1)S(1)} %bitcast.55, bf16[512,1024]{1,0:T(8,128)(2,1)S(1)} %bitcast.56, ...), custom_call_target="tpu_custom_call" | custom-call | flops 4294967296 | bytes 20971520 | tf_op jit(solution)/shard_map/norm_and_weight_terms/pallas_call | solution.py:121
  47.6 0.1 broadcast_select_fusion.1
  47.8 3.7 %collective-permute-start.8 = (bf16[512,1024]{1,0:T(8,128)(2,1)S(1)}, bf16[512,1024]{1,0:T(8,128)(2,1)S(1)}, u32[]{:S(2)}, u32[]{:S(2)}) collective-permute-start(bf16[512,1024]{1,0:T(8,128)(2,1)S(1)} %broadcast_select_fusion.1), channel_id=1, source_target_pairs={{2,3},{3,2},{4,5},{5,4},{10,11},{11,10},{12,13},{13,12},{18,19},{1... | collective-permute-start | bytes 3145736 | tf_op jit(solution)/shard_map/ppermute | solution.py:60
  51.4 3.2 %collective-permute-done.3.refs_3_ = bf16[512,1024]{1,0:T(8,128)(2,1)S(1)} collective-permute-done((bf16[512,1024]{1,0:T(8,128)(2,1)S(1)}, bf16[512,1024]{1,0:T(8,128)(2,1)S(1)}, u32[]{:S(2)}, u32[]{:S(2)}) %collective-permute-start.3) | collective-permute-done | bytes 1048608 | tf_op jit(solution)/shard_map/ppermute | solution.py:42
  54.6 1.3 collective-permute-done.4.refs_4_
  55.9 1.3 collective-permute-start.7
  57.2 2.3 %collective-permute-start.5 = (bf16[512,1024]{1,0:T(8,128)(2,1)S(1)}, bf16[512,1024]{1,0:T(8,128)(2,1)S(1)}, u32[]{:S(2)}, u32[]{:S(2)}) collective-permute-start(bf16[512,1024]{1,0:T(8,128)(2,1)S(1)} %collective-permute-done.3.refs_3_), channel_id=1, source_target_pairs={{2,4},{4,6},{6,7},{5,3},{3,1},{1,0},{10,12},{12,14},{14,15},{13,11... | collective-permute-start | bytes 3145736 | tf_op jit(solution)/shard_map/ppermute | solution.py:42
  59.5 3.6 %collective-permute-start.6 = (bf16[512,1024]{1,0:T(8,128)(2,1)S(1)}, bf16[512,1024]{1,0:T(8,128)(2,1)S(1)}, u32[]{:S(2)}, u32[]{:S(2)}) collective-permute-start(bf16[512,1024]{1,0:T(8,128)(2,1)S(1)} %collective-permute-done.4.refs_4_), channel_id=1, source_target_pairs={{2,0},{4,2},{7,6},{5,7},{3,5},{0,1},{10,8},{12,10},{15,14},{13,15}... | collective-permute-start | bytes 3145736 | tf_op jit(solution)/shard_map/ppermute | solution.py:45
  63.1 0.3 add.118
  63.5 1.6 collective-permute-start.14
  65.0 10.4 %collective-permute-done.8.refs_8_ = bf16[512,1024]{1,0:T(8,128)(2,1)S(1)} collective-permute-done((bf16[512,1024]{1,0:T(8,128)(2,1)S(1)}, bf16[512,1024]{1,0:T(8,128)(2,1)S(1)}, u32[]{:S(2)}, u32[]{:S(2)}) %collective-permute-start.8) | collective-permute-done | bytes 1048608 | tf_op jit(solution)/shard_map/ppermute | solution.py:60
  75.5 4.5 %collective-permute-done.7 = bf16[512,1024]{1,0:T(8,128)(2,1)S(1)} collective-permute-done((bf16[512,1024]{1,0:T(8,128)(2,1)S(1)}, bf16[512,1024]{1,0:T(8,128)(2,1)S(1)}, u32[]{:S(2)}, u32[]{:S(2)}) %collective-permute-start.7) | collective-permute-done | bytes 1048608 | tf_op jit(solution)/shard_map/ppermute | solution.py:60
  80.0 3.6 %collective-permute-done.6.refs_6_ = bf16[512,1024]{1,0:T(8,128)(2,1)S(1)} collective-permute-done((bf16[512,1024]{1,0:T(8,128)(2,1)S(1)}, bf16[512,1024]{1,0:T(8,128)(2,1)S(1)}, u32[]{:S(2)}, u32[]{:S(2)}) %collective-permute-start.6) | collective-permute-done | bytes 1048608 | tf_op jit(solution)/shard_map/ppermute | solution.py:45
  83.7 3.4 %collective-permute-start.11 = (bf16[512,1024]{1,0:T(8,128)(2,1)S(1)}, bf16[512,1024]{1,0:T(8,128)(2,1)S(1)}, u32[]{:S(2)}, u32[]{:S(2)}) collective-permute-start(bf16[512,1024]{1,0:T(8,128)(2,1)S(1)} %broadcast_select_fusion), channel_id=1, source_target_pairs={{2,0},{4,6},{5,7},{3,1},{10,8},{12,14},{13,15},{11,9},{18,16},{20,... | collective-permute-start | bytes 3145736 | tf_op jit(solution)/shard_map/ppermute | solution.py:60
  87.1 2.9 %fusion.1 = (bf16[512,1024]{1,0:T(8,128)(2,1)S(1)}, bf16[512,1024]{1,0:T(8,128)(2,1)S(1)}) fusion(bf16[512,1024]{1,0:T(8,128)(2,1)S(1)} %collective-permute-done.7, f32[7,512,1024]{2,1,0:T(8,128)} %get-tuple-element.45), kind=kLoop, calls=%fused_computation.7 | loop fusion | flops 2621440 | bytes 7340032 | tf_op jit(solution)/shard_map/convert_element_type | solution.py:324
  90.1 1.3 collective-permute-start.10
  91.4 4.9 %collective-permute-start.9 = (bf16[512,1024]{1,0:T(8,128)(2,1)S(1)}, bf16[512,1024]{1,0:T(8,128)(2,1)S(1)}, u32[]{:S(2)}, u32[]{:S(2)}) collective-permute-start(bf16[512,1024]{1,0:T(8,128)(2,1)S(1)} %get-tuple-element.67), channel_id=1, source_target_pairs={{0,2},{2,4},{6,7},{7,5},{5,3},{1,0},{8,10},{10,12},{14,15},{15,13}... | collective-permute-start | bytes 3145736 | tf_op jit(solution)/shard_map/ppermute | solution.py:42
  96.3 1.9 %collective-permute-start.12 = (bf16[512,1024]{1,0:T(8,128)(2,1)S(1)}, bf16[512,1024]{1,0:T(8,128)(2,1)}, u32[]{:S(2)}, u32[]{:S(2)}) collective-permute-start(bf16[512,1024]{1,0:T(8,128)(2,1)S(1)} %get-tuple-element.47), channel_id=1, source_target_pairs={{2,3},{3,2},{4,5},{5,4},{10,11},{11,10},{12,13},{13,12},{18,19},{1... | collective-permute-start | bytes 3145736 | tf_op jit(solution)/shard_map/ppermute | solution.py:60
  98.2 1.4 add.119
  99.7 5.9 %collective-permute-done.11.refs_9_ = bf16[512,1024]{1,0:T(8,128)(2,1)S(1)} collective-permute-done((bf16[512,1024]{1,0:T(8,128)(2,1)S(1)}, bf16[512,1024]{1,0:T(8,128)(2,1)S(1)}, u32[]{:S(2)}, u32[]{:S(2)}) %collective-permute-start.11) | collective-permute-done | bytes 1048608 | tf_op jit(solution)/shard_map/ppermute | solution.py:60
  105.6 7.6 %collective-permute-done.10 = bf16[512,1024]{1,0:T(8,128)(2,1)S(1)} collective-permute-done((bf16[512,1024]{1,0:T(8,128)(2,1)S(1)}, bf16[512,1024]{1,0:T(8,128)(2,1)S(1)}, u32[]{:S(2)}, u32[]{:S(2)}) %collective-permute-start.10) | collective-permute-done | bytes 1048608 | tf_op jit(solution)/shard_map/ppermute | solution.py:45
  113.2 1.2 collective-permute-done.9
  114.4 4.2 %collective-permute-done.12 = bf16[512,1024]{1,0:T(8,128)(2,1)} collective-permute-done((bf16[512,1024]{1,0:T(8,128)(2,1)S(1)}, bf16[512,1024]{1,0:T(8,128)(2,1)}, u32[]{:S(2)}, u32[]{:S(2)}) %collective-permute-start.12) | collective-permute-done | bytes 1048608 | tf_op jit(solution)/shard_map/ppermute | solution.py:60
  118.6 4.3 %fusion.10 = (bf16[512,1024]{1,0:T(8,128)(2,1)}, bf16[512,1024]{1,0:T(8,128)(2,1)}) fusion(bf16[512,1024]{1,0:T(8,128)(2,1)S(1)} %collective-permute-done.10, f32[7,512,1024]{2,1,0:T(8,128)} %get-tuple-element.45, bf16[512,1024]{1,0:T(8,128)(2,1)S(1)} %collective-permute-done.9), kind=kLoop, calls=%fused_computation.17 | loop fusion | flops 3145728 | bytes 8388608 | tf_op jit(solution)/shard_map/convert_element_type | solution.py:331
  122.9 0.1 collective-permute-start.16
  123.0 1.9 %collective-permute-start.17 = (bf16[512,1024]{1,0:T(8,128)(2,1)}, bf16[512,1024]{1,0:T(8,128)(2,1)}, u32[]{:S(2)}, u32[]{:S(2)}) collective-permute-start(bf16[512,1024]{1,0:T(8,128)(2,1)} %get-tuple-element.68), channel_id=1, source_target_pairs={{2,0},{4,2},{6,4},{7,6},{5,7},{3,5},{1,3},{0,1},{10,8},{12,10},{14... | collective-permute-start | bytes 3145736 | tf_op jit(solution)/shard_map/ppermute | solution.py:45
  125.1 2.4 %fusion.14 = bf16[512,1024]{1,0:T(8,128)(2,1)S(1)} fusion(f32[7,512,1024]{2,1,0:T(8,128)} %get-tuple-element.45, pred[]{:T(512)} %or.9), kind=kLoop, calls=%fused_computation.24 | loop fusion | flops 524288 | bytes 3145729 | tf_op jit(solution)/shard_map/convert_element_type | solution.py:328
  127.6 2.5 %collective-permute-start.15 = (bf16[512,1024]{1,0:T(8,128)(2,1)S(1)}, bf16[512,1024]{1,0:T(8,128)(2,1)S(1)}, u32[]{:S(2)}, u32[]{:S(2)}) collective-permute-start(bf16[512,1024]{1,0:T(8,128)(2,1)S(1)} %fusion.14), channel_id=1, source_target_pairs={{2,3},{3,2},{4,5},{5,4},{10,11},{11,10},{12,13},{13,12},{18,19},{1... | collective-permute-start | bytes 3145736 | tf_op jit(solution)/shard_map/ppermute | solution.py:60
  130.1 12.5 %collective-permute-done.16 = bf16[512,1024]{1,0:T(8,128)(2,1)} collective-permute-done((bf16[512,1024]{1,0:T(8,128)(2,1)}, bf16[512,1024]{1,0:T(8,128)(2,1)}, u32[]{:S(2)}, u32[]{:S(2)}) %collective-permute-start.16) | collective-permute-done | bytes 1048608 | tf_op jit(solution)/shard_map/ppermute | solution.py:42
  142.6 4.0 %fusion.4 = (bf16[512,1024]{1,0:T(8,128)(2,1)S(1)}, bf16[512,1024]{1,0:T(8,128)(2,1)S(1)}) fusion(bf16[512,1024]{1,0:T(8,128)(2,1)} %collective-permute-done.12, bf16[512,1024]{1,0:T(8,128)(2,1)} %collective-permute-done.16, f32[7,512,1024]{2,1,0:T(8,128)} %get-tuple-element.45, pred[]{:T(512)} %or.9, bf16[512,1024]{1,0:T(8,128)(2,1)} %collective-permute-done.17, ...), kind=kLoop, calls=%fused_computation.10 | loop fusion | flops 5767168 | bytes 9437186 | tf_op jit(solution)/shard_map/convert_element_type | solution.py:336
  146.7 0.3 collective-permute-start.18
  147.0 2.0 %collective-permute-start.19 = (bf16[512,1024]{1,0:T(8,128)(2,1)S(1)}, bf16[512,1024]{1,0:T(8,128)(2,1)S(1)}, u32[]{:S(2)}, u32[]{:S(2)}) collective-permute-start(bf16[512,1024]{1,0:T(8,128)(2,1)S(1)} %get-tuple-element.65), channel_id=1, source_target_pairs={{2,0},{4,2},{6,4},{7,6},{5,7},{3,5},{1,3},{0,1},{10,8},{12,10},{14... | collective-permute-start | bytes 3145736 | tf_op jit(solution)/shard_map/ppermute | solution.py:45
  149.0 2.6 %fusion.17 = (bf16[1,384,1024]{2,1,0:T(8,128)(2,1)}, f32[384,1024]{1,0:T(8,128)}, f32[384,1024]{1,0:T(8,128)}) fusion(bf16[1,384,1024]{2,1,0:T(8,128)(2,1)S(1)} %copy-done.17, f32[384,1024]{1,0:T(8,128)S(1)} %copy-done.12, f32[384,1024]{1,0:T(8,128)S(1)} %copy-done.10, f32[384,1024]{1,0:T(8,128)S(1)} %copy-done.13), kind=kLoop, calls=%fused_computation.33 | loop fusion | flops 4325376 | bytes 9437184 | tf_op jit(solution)/shard_map/broadcast_in_dim | solution.py:401
  151.6 16.6 %project_and_input_grad.1 = (bf16[512,1024]{1,0:T(8,128)(2,1)}, bf16[512,4096]{1,0:T(8,128)(2,1)}) custom-call(s32[14]{0:T(128)S(1)} %pad_add_fusion.at, bf16[512,4096]{1,0:T(8,128)(2,1)} %bitcast.54, bf16[512,1024]{1,0:T(8,128)(2,1)S(1)} %copy-done.7, f32[512,128]{1,0:T(8,128)S(1)} %copy-done.9, f32[512,128]{1,0:T(8,128)S(1)} %get-tuple-element.73.cosine, ...), custom_call_target="tpu_custom_call" | custom-call | flops 8589934592 | bytes 16777216 | tf_op jit(solution)/shard_map/project_and_input_grad/pallas_call | solution.py:236
  168.3 4.2 %fusion.9 = (f32[512]{0:T(512)}, f32[1,512,1024]{2,1,0:T(8,128)}) fusion(bf16[1,512,1024]{2,1,0:T(8,128)(2,1)S(1)} %copy-done.11, bf16[512,1024]{1,0:T(8,128)(2,1)S(1)} %collective-permute-done.19, bf16[512,1024]{1,0:T(8,128)(2,1)S(1)} %collective-permute-done.18, bf16[512,1024]{1,0:T(8,128)(2,1)S(1)} %collective-permute-done.15, ...), kind=kLoop, calls=%fused_computation.15 | loop fusion | flops 5242368 | bytes 8392704 | tf_op jit(solution)/shard_map/reduce_sum | solution.py:381
  (61 shorter events, 0.6 us)
Async XLA Ops:
  1.3 32.1 %copy-start.22 = (s32[8]{0:T(128)S(1)}, s32[8]{0:T(128)}, u32[]{:S(2)}) copy-start(s32[8]{0:T(128)} %constant.94.clone) | copy-start | bytes 100
  2.8 25.0 %collective-permute-start = (bf16[512,1024]{1,0:T(8,128)(2,1)S(1)}, bf16[512,1024]{1,0:T(8,128)(2,1)S(1)}, u32[]{:S(2)}, u32[]{:S(2)}) collective-permute-start(bf16[512,1024]{1,0:T(8,128)(2,1)S(1)} %fusion.8.refs_0_), channel_id=1, source_target_pairs={{0,2},{2,4},{4,6},{6,7},{7,5},{5,3},{3,1},{1,0},{8,10},{10,12},{12... | collective-permute-start | bytes 3145736 | tf_op jit(solution)/shard_map/ppermute | solution.py:42
  4.4 24.6 %collective-permute-start.1 = (bf16[512,1024]{1,0:T(8,128)(2,1)S(1)}, bf16[512,1024]{1,0:T(8,128)(2,1)S(1)}, u32[]{:S(2)}, u32[]{:S(2)}) collective-permute-start(bf16[512,1024]{1,0:T(8,128)(2,1)S(1)} %fusion.8.refs_0_), channel_id=1, source_target_pairs={{2,0},{4,2},{6,4},{7,6},{5,7},{3,5},{1,3},{0,1},{10,8},{12,10},{14... | collective-permute-start | bytes 3145736 | tf_op jit(solution)/shard_map/ppermute | solution.py:45
  4.9 26.3 %collective-permute-start.2 = (bf16[512,1024]{1,0:T(8,128)(2,1)S(1)}, bf16[512,1024]{1,0:T(8,128)(2,1)}, u32[]{:S(2)}, u32[]{:S(2)}) collective-permute-start(bf16[512,1024]{1,0:T(8,128)(2,1)S(1)} %fusion.8.refs_0_), channel_id=1, source_target_pairs={{2,3},{3,2},{4,5},{5,4},{10,11},{11,10},{12,13},{13,12},{18,19},{1... | collective-permute-start | bytes 3145736 | tf_op jit(solution)/shard_map/ppermute | solution.py:60
  8.3 25.3 %copy-start.3 = (bf16[1,512,1024]{2,1,0:T(8,128)(2,1)S(1)}, bf16[1,512,1024]{2,1,0:T(8,128)(2,1)}, u32[]{:S(2)}) copy-start(bf16[1,512,1024]{2,1,0:T(8,128)(2,1)} %param.13) | copy-start | bytes 3145732
  31.2 23.4 %collective-permute-start.3 = (bf16[512,1024]{1,0:T(8,128)(2,1)S(1)}, bf16[512,1024]{1,0:T(8,128)(2,1)S(1)}, u32[]{:S(2)}, u32[]{:S(2)}) collective-permute-start(bf16[512,1024]{1,0:T(8,128)(2,1)S(1)} %collective-permute-done.refs_1_), channel_id=1, source_target_pairs={{0,2},{2,4},{4,6},{6,7},{7,5},{5,3},{3,1},{1,0},{8,10},{10,12},{12... | collective-permute-start | bytes 3145736 | tf_op jit(solution)/shard_map/ppermute | solution.py:42
  32.8 23.1 %collective-permute-start.4 = (bf16[512,1024]{1,0:T(8,128)(2,1)S(1)}, bf16[512,1024]{1,0:T(8,128)(2,1)S(1)}, u32[]{:S(2)}, u32[]{:S(2)}) collective-permute-start(bf16[512,1024]{1,0:T(8,128)(2,1)S(1)} %collective-permute-done.1.refs_2_), channel_id=1, source_target_pairs={{2,0},{4,2},{6,4},{7,6},{5,7},{3,5},{1,3},{0,1},{10,8},{12,10},{14... | collective-permute-start | bytes 3145736 | tf_op jit(solution)/shard_map/ppermute | solution.py:45
  33.4 14.2 %copy-start = (f32[512,128]{1,0:T(8,128)}, f32[512,128]{1,0:T(8,128)S(1)}, u32[]{:S(2)}) copy-start(f32[512,128]{1,0:T(8,128)S(1)} %get-tuple-element.74.sine) | copy-start | bytes 786436
  33.5 29.6 %collective-permute-start.13 = (f32[384,1024]{1,0:T(8,128)}, f32[384,1024]{1,0:T(8,128)S(1)}, u32[]{:S(2)}, u32[]{:S(2)}) collective-permute-start(f32[384,1024]{1,0:T(8,128)} %bitcast.57), channel_id=1, source_target_pairs={{0,8},{8,0},{16,24},{24,16},{1,9},{9,1},{17,25},{25,17},{2,10},{10... | collective-permute-start | bytes 4718600 | tf_op jit(solution)/shard_map/ppermute | solution.py:273
  33.6 2.2 %copy-start.2 = (bf16[1,512,4096]{2,1,0:T(8,128)(2,1)S(1)}, bf16[1,512,4096]{2,1,0:T(8,128)(2,1)}, u32[]{:S(2)}) copy-start(bf16[1,512,4096]{2,1,0:T(8,128)(2,1)} %param.10) | copy-start | bytes 12582916
  47.6 15.8 %copy-start.6 = (bf16[512,1024]{1,0:T(8,128)(2,1)}, bf16[512,1024]{1,0:T(8,128)(2,1)S(1)}, u32[]{:S(2)}) copy-start(bf16[512,1024]{1,0:T(8,128)(2,1)S(1)} %get-tuple-element.33.kv_grad) | copy-start | bytes 3145732
  47.6 15.8 %copy-start.8 = (f32[512,128]{1,0:T(8,128)}, f32[512,128]{1,0:T(8,128)S(1)}, u32[]{:S(2)}) copy-start(f32[512,128]{1,0:T(8,128)S(1)} %get-tuple-element.34.inv) | copy-start | bytes 786436
  47.6 15.5 %copy-start.14 = (f32[1,384,1024]{2,1,0:T(8,128)S(1)}, f32[1,384,1024]{2,1,0:T(8,128)}, u32[]{:S(2)}) copy-start(f32[1,384,1024]{2,1,0:T(8,128)} %param.14) | copy-start | bytes 4718596
  47.8 27.7 %collective-permute-start.8 = (bf16[512,1024]{1,0:T(8,128)(2,1)S(1)}, bf16[512,1024]{1,0:T(8,128)(2,1)S(1)}, u32[]{:S(2)}, u32[]{:S(2)}) collective-permute-start(bf16[512,1024]{1,0:T(8,128)(2,1)S(1)} %broadcast_select_fusion.1), channel_id=1, source_target_pairs={{2,3},{3,2},{4,5},{5,4},{10,11},{11,10},{12,13},{13,12},{18,19},{1... | collective-permute-start | bytes 3145736 | tf_op jit(solution)/shard_map/ppermute | solution.py:60
  54.6 8.8 %copy-start.4 = (bf16[512,1024]{1,0:T(8,128)(2,1)}, bf16[512,1024]{1,0:T(8,128)(2,1)S(1)}, u32[]{:S(2)}) copy-start(bf16[512,1024]{1,0:T(8,128)(2,1)S(1)} %collective-permute-done.3.refs_3_) | copy-start | bytes 3145732
  55.9 7.5 %copy-start.18 = (bf16[512,1024]{1,0:T(8,128)(2,1)}, bf16[512,1024]{1,0:T(8,128)(2,1)S(1)}, u32[]{:S(2)}) copy-start(bf16[512,1024]{1,0:T(8,128)(2,1)S(1)} %collective-permute-done.4.refs_4_) | copy-start | bytes 3145732
  55.9 24.1 %collective-permute-start.7 = (bf16[512,1024]{1,0:T(8,128)(2,1)S(1)}, bf16[512,1024]{1,0:T(8,128)(2,1)S(1)}, u32[]{:S(2)}, u32[]{:S(2)}) collective-permute-start(bf16[512,1024]{1,0:T(8,128)(2,1)S(1)} %get-tuple-element.47), channel_id=1, source_target_pairs={{0,2},{6,4},{7,5},{1,3},{8,10},{14,12},{15,13},{9,11},{16,18},{22,... | collective-permute-start | bytes 3145736 | tf_op jit(solution)/shard_map/ppermute | solution.py:60
  57.2 22.8 %collective-permute-start.5 = (bf16[512,1024]{1,0:T(8,128)(2,1)S(1)}, bf16[512,1024]{1,0:T(8,128)(2,1)S(1)}, u32[]{:S(2)}, u32[]{:S(2)}) collective-permute-start(bf16[512,1024]{1,0:T(8,128)(2,1)S(1)} %collective-permute-done.3.refs_3_), channel_id=1, source_target_pairs={{2,4},{4,6},{6,7},{5,3},{3,1},{1,0},{10,12},{12,14},{14,15},{13,11... | collective-permute-start | bytes 3145736 | tf_op jit(solution)/shard_map/ppermute | solution.py:42
  59.5 24.1 %collective-permute-start.6 = (bf16[512,1024]{1,0:T(8,128)(2,1)S(1)}, bf16[512,1024]{1,0:T(8,128)(2,1)S(1)}, u32[]{:S(2)}, u32[]{:S(2)}) collective-permute-start(bf16[512,1024]{1,0:T(8,128)(2,1)S(1)} %collective-permute-done.4.refs_4_), channel_id=1, source_target_pairs={{2,0},{4,2},{7,6},{5,7},{3,5},{0,1},{10,8},{12,10},{15,14},{13,15}... | collective-permute-start | bytes 3145736 | tf_op jit(solution)/shard_map/ppermute | solution.py:45
  63.5 34.8 %collective-permute-start.14 = (f32[384,1024]{1,0:T(8,128)S(1)}, f32[384,1024]{1,0:T(8,128)S(1)}, u32[]{:S(2)}, u32[]{:S(2)}) collective-permute-start(f32[384,1024]{1,0:T(8,128)S(1)} %add.118), channel_id=1, source_target_pairs={{0,16},{8,24},{16,0},{24,8},{1,17},{9,25},{17,1},{25,9},{2,18},{10... | collective-permute-start | bytes 4718600 | tf_op jit(solution)/shard_map/ppermute | solution.py:273
  75.5 14.6 %copy-start.19 = (bf16[512,1024]{1,0:T(8,128)(2,1)}, bf16[512,1024]{1,0:T(8,128)(2,1)S(1)}, u32[]{:S(2)}) copy-start(bf16[512,1024]{1,0:T(8,128)(2,1)S(1)} %collective-permute-done.8.refs_8_) | copy-start | bytes 3145732
  80.0 10.0 %copy-start.15 = (bf16[512,1024]{1,0:T(8,128)(2,1)}, bf16[512,1024]{1,0:T(8,128)(2,1)S(1)}, u32[]{:S(2)}) copy-start(bf16[512,1024]{1,0:T(8,128)(2,1)S(1)} %collective-permute-done.5.refs_5_) | copy-start | bytes 3145732
  83.6 6.5 %copy-start.16 = (bf16[512,1024]{1,0:T(8,128)(2,1)}, bf16[512,1024]{1,0:T(8,128)(2,1)S(1)}, u32[]{:S(2)}) copy-start(bf16[512,1024]{1,0:T(8,128)(2,1)S(1)} %collective-permute-done.6.refs_6_) | copy-start | bytes 3145732
  83.7 21.9 %collective-permute-start.11 = (bf16[512,1024]{1,0:T(8,128)(2,1)S(1)}, bf16[512,1024]{1,0:T(8,128)(2,1)S(1)}, u32[]{:S(2)}, u32[]{:S(2)}) collective-permute-start(bf16[512,1024]{1,0:T(8,128)(2,1)S(1)} %broadcast_select_fusion), channel_id=1, source_target_pairs={{2,0},{4,6},{5,7},{3,1},{10,8},{12,14},{13,15},{11,9},{18,16},{20,... | collective-permute-start | bytes 3145736 | tf_op jit(solution)/shard_map/ppermute | solution.py:60
  90.1 23.1 %collective-permute-start.10 = (bf16[512,1024]{1,0:T(8,128)(2,1)S(1)}, bf16[512,1024]{1,0:T(8,128)(2,1)S(1)}, u32[]{:S(2)}, u32[]{:S(2)}) collective-permute-start(bf16[512,1024]{1,0:T(8,128)(2,1)S(1)} %get-tuple-element.66), channel_id=1, source_target_pairs={{4,2},{6,4},{7,6},{3,5},{1,3},{0,1},{12,10},{14,12},{15,14},{11,13... | collective-permute-start | bytes 3145736 | tf_op jit(solution)/shard_map/ppermute | solution.py:45
  91.4 23.0 %collective-permute-start.9 = (bf16[512,1024]{1,0:T(8,128)(2,1)S(1)}, bf16[512,1024]{1,0:T(8,128)(2,1)S(1)}, u32[]{:S(2)}, u32[]{:S(2)}) collective-permute-start(bf16[512,1024]{1,0:T(8,128)(2,1)S(1)} %get-tuple-element.67), channel_id=1, source_target_pairs={{0,2},{2,4},{6,7},{7,5},{5,3},{1,0},{8,10},{10,12},{14,15},{15,13}... | collective-permute-start | bytes 3145736 | tf_op jit(solution)/shard_map/ppermute | solution.py:42
  96.3 22.3 %collective-permute-start.12 = (bf16[512,1024]{1,0:T(8,128)(2,1)S(1)}, bf16[512,1024]{1,0:T(8,128)(2,1)}, u32[]{:S(2)}, u32[]{:S(2)}) collective-permute-start(bf16[512,1024]{1,0:T(8,128)(2,1)S(1)} %get-tuple-element.47), channel_id=1, source_target_pairs={{2,3},{3,2},{4,5},{5,4},{10,11},{11,10},{12,13},{13,12},{18,19},{1... | collective-permute-start | bytes 3145736 | tf_op jit(solution)/shard_map/ppermute | solution.py:60
  99.6 25.4 %copy-start.21 = (s32[8]{0:T(128)S(1)}, s32[8]{0:T(128)}, u32[]{:S(2)}) copy-start(s32[8]{0:T(128)} %constant.95.clone) | copy-start | bytes 100
  105.6 17.3 %copy-start.20 = (bf16[512,1024]{1,0:T(8,128)(2,1)}, bf16[512,1024]{1,0:T(8,128)(2,1)S(1)}, u32[]{:S(2)}) copy-start(bf16[512,1024]{1,0:T(8,128)(2,1)S(1)} %collective-permute-done.11.refs_9_) | copy-start | bytes 3145732
  122.9 19.7 %collective-permute-start.16 = (bf16[512,1024]{1,0:T(8,128)(2,1)}, bf16[512,1024]{1,0:T(8,128)(2,1)}, u32[]{:S(2)}, u32[]{:S(2)}) collective-permute-start(bf16[512,1024]{1,0:T(8,128)(2,1)} %get-tuple-element.69), channel_id=1, source_target_pairs={{0,2},{2,4},{4,6},{6,7},{7,5},{5,3},{3,1},{1,0},{8,10},{10,12},{12... | collective-permute-start | bytes 3145736 | tf_op jit(solution)/shard_map/ppermute | solution.py:42
  123.0 19.6 %collective-permute-start.17 = (bf16[512,1024]{1,0:T(8,128)(2,1)}, bf16[512,1024]{1,0:T(8,128)(2,1)}, u32[]{:S(2)}, u32[]{:S(2)}) collective-permute-start(bf16[512,1024]{1,0:T(8,128)(2,1)} %get-tuple-element.68), channel_id=1, source_target_pairs={{2,0},{4,2},{6,4},{7,6},{5,7},{3,5},{1,3},{0,1},{10,8},{12,10},{14... | collective-permute-start | bytes 3145736 | tf_op jit(solution)/shard_map/ppermute | solution.py:45
  127.6 21.4 %copy-start.10 = (f32[384,1024]{1,0:T(8,128)S(1)}, f32[384,1024]{1,0:T(8,128)}, u32[]{:S(2)}) copy-start(f32[384,1024]{1,0:T(8,128)} %add.119) | copy-start | bytes 4718596
  127.6 21.4 %copy-start.12 = (f32[384,1024]{1,0:T(8,128)S(1)}, f32[384,1024]{1,0:T(8,128)}, u32[]{:S(2)}) copy-start(f32[384,1024]{1,0:T(8,128)} %param.16) | copy-start | bytes 4718596
  127.6 21.4 %copy-start.13 = (f32[384,1024]{1,0:T(8,128)S(1)}, f32[384,1024]{1,0:T(8,128)}, u32[]{:S(2)}) copy-start(f32[384,1024]{1,0:T(8,128)} %param.15) | copy-start | bytes 4718596
  127.6 21.4 %copy-start.17 = (bf16[1,384,1024]{2,1,0:T(8,128)(2,1)S(1)}, bf16[1,384,1024]{2,1,0:T(8,128)(2,1)}, u32[]{:S(2)}) copy-start(bf16[1,384,1024]{2,1,0:T(8,128)(2,1)} %param.17) | copy-start | bytes 2359300
  127.6 40.6 %collective-permute-start.15 = (bf16[512,1024]{1,0:T(8,128)(2,1)S(1)}, bf16[512,1024]{1,0:T(8,128)(2,1)S(1)}, u32[]{:S(2)}, u32[]{:S(2)}) collective-permute-start(bf16[512,1024]{1,0:T(8,128)(2,1)S(1)} %fusion.14), channel_id=1, source_target_pairs={{2,3},{3,2},{4,5},{5,4},{10,11},{11,10},{12,13},{13,12},{18,19},{1... | collective-permute-start | bytes 3145736 | tf_op jit(solution)/shard_map/ppermute | solution.py:60
  146.7 21.6 %collective-permute-start.18 = (bf16[512,1024]{1,0:T(8,128)(2,1)S(1)}, bf16[512,1024]{1,0:T(8,128)(2,1)S(1)}, u32[]{:S(2)}, u32[]{:S(2)}) collective-permute-start(bf16[512,1024]{1,0:T(8,128)(2,1)S(1)} %get-tuple-element.64), channel_id=1, source_target_pairs={{0,2},{2,4},{4,6},{6,7},{7,5},{5,3},{3,1},{1,0},{8,10},{10,12},{12... | collective-permute-start | bytes 3145736 | tf_op jit(solution)/shard_map/ppermute | solution.py:42
  147.0 4.6 %copy-start.1 = (f32[512,128]{1,0:T(8,128)S(1)}, f32[512,128]{1,0:T(8,128)}, u32[]{:S(2)}) copy-start(f32[512,128]{1,0:T(8,128)} %copy-done) | copy-start | bytes 786436
  147.0 4.6 %copy-start.5 = (bf16[512,1024]{1,0:T(8,128)(2,1)S(1)}, bf16[512,1024]{1,0:T(8,128)(2,1)}, u32[]{:S(2)}) copy-start(bf16[512,1024]{1,0:T(8,128)(2,1)} %copy-done.4) | copy-start | bytes 3145732
  147.0 4.6 %copy-start.7 = (bf16[512,1024]{1,0:T(8,128)(2,1)S(1)}, bf16[512,1024]{1,0:T(8,128)(2,1)}, u32[]{:S(2)}) copy-start(bf16[512,1024]{1,0:T(8,128)(2,1)} %copy-done.6) | copy-start | bytes 3145732
  147.0 4.6 %copy-start.9 = (f32[512,128]{1,0:T(8,128)S(1)}, f32[512,128]{1,0:T(8,128)}, u32[]{:S(2)}) copy-start(f32[512,128]{1,0:T(8,128)} %copy-done.8) | copy-start | bytes 786436
  147.0 21.2 %collective-permute-start.19 = (bf16[512,1024]{1,0:T(8,128)(2,1)S(1)}, bf16[512,1024]{1,0:T(8,128)(2,1)S(1)}, u32[]{:S(2)}, u32[]{:S(2)}) collective-permute-start(bf16[512,1024]{1,0:T(8,128)(2,1)S(1)} %get-tuple-element.65), channel_id=1, source_target_pairs={{2,0},{4,2},{6,4},{7,6},{5,7},{3,5},{1,3},{0,1},{10,8},{12,10},{14... | collective-permute-start | bytes 3145736 | tf_op jit(solution)/shard_map/ppermute | solution.py:45
  151.6 16.7 %copy-start.11 = (bf16[1,512,1024]{2,1,0:T(8,128)(2,1)S(1)}, bf16[1,512,1024]{2,1,0:T(8,128)(2,1)}, u32[]{:S(2)}) copy-start(bf16[1,512,1024]{2,1,0:T(8,128)(2,1)} %param.12) | copy-start | bytes 3145732

commit v6 on v5

--- a/solution.py
+++ b/solution.py
@@ -38,26 +38,20 @@
         spot = (self.spot + self.count + jnp.array(distances, jnp.int32)) % self.count
         return jnp.where(spot < self.half, 2 * spot, 2 * (self.count - 1 - spot) + 1)
 
-    def to_right(self, value, skip=()):
-        return lax.ppermute(value, "fsdp", [p for p in self.right if p[0] not in skip])
-
-    def to_left(self, value, skip=()):
-        return lax.ppermute(value, "fsdp", [p for p in self.left if p[0] not in skip])
+    def to_right(self, value):
+        return lax.ppermute(value, "fsdp", self.right)
+
+    def to_left(self, value):
+        return lax.ppermute(value, "fsdp", self.left)
 
 
 class Plane(Ring):
-    first, second = (2, 5), (4, 3)
-    chords = [(2, 3), (3, 2), (4, 5), (5, 4)]
-    inward = [(0, 2), (6, 4), (7, 5), (1, 3)]
-    outward = [(2, 0), (4, 6), (5, 7), (3, 1)]
-
     def __init__(self):
         super().__init__()
-        self.is_first = (self.me == 2) | (self.me == 5)
-        self.is_second = (self.me == 4) | (self.me == 3)
-
-    def send(self, value, pairs):
-        return lax.ppermute(value, "fsdp", pairs)
+        self.at = [self.spot % 4 == i for i in range(4)]
+
+    def over_chord(self, value):
+        return lax.ppermute(value, "fsdp", [(2, 3), (3, 2), (4, 5), (5, 4)])
 
 
 def after(value, *others):
@@ -265,18 +259,24 @@
 
 def replica_sum(value):
     replicas = lax.axis_size("replica")
-    if replicas & (replicas - 1):
-        return lax.psum(value, "replica")
-    step = 1
-    while step < replicas:
-        pairs = [(r, r ^ step) for r in range(replicas)]
-        value = value + lax.ppermute(value, "replica", pairs)
-        step *= 2
-    return value
+    if replicas != 4:
+        total = lax.psum(value, "replica")
+        return total, total
+    swap = lambda v, step: lax.ppermute(v, "replica", [(r, r ^ step) for r in range(4)])
+    odd = lax.axis_index("replica") % 2
+    half = value.shape[0] // 2
+    mine = lax.dynamic_slice_in_dim(value, odd * half, half, 0)
+    theirs = lax.dynamic_slice_in_dim(value, (1 - odd) * half, half, 0)
+    came = swap(theirs, 1)
+    mine = mine + came
+    mine = mine + swap(mine, 2)
+    theirs = swap(mine, 1)
+    low, high = jnp.where(odd == 0, mine, theirs), jnp.where(odd == 0, theirs, mine)
+    return (low, high), came
 
 
 def exchange_ring(ring, own, far, near, pseudo):
-    total = replica_sum(pseudo)
+    total, came = replica_sum(pseudo)
     shard, cut = own.shape[0], own.shape[0] // 2
     blocks = [own]
     from_left = from_right = own
@@ -303,49 +303,94 @@
 
 
 def exchange_plane(plane, own, far, near, pseudo):
-    first, second = plane.first, plane.second
-    left1, right1 = plane.to_right(own), plane.to_left(own)
-    partner = plane.send(own, plane.chords)
-    left1, right1, partner = lax.optimization_barrier((left1, right1, partner))
-    left2, right2 = plane.to_right(left1), plane.to_left(right1)
-    far_inner = plane.send(jnp.where(plane.is_second, left1, right1), plane.chords)
-    total = replica_sum(after(pseudo, left1, right1))
-    left2, right2 = lax.optimization_barrier((left2, right2))
-    far = after(far, left2, right2)
-    left3, right3 = plane.to_right(left2, (0, 7)), plane.to_left(right2, (6, 1))
-    from_outer = plane.send(far, plane.inward)
-    left3, right3, from_outer, far_inner, far = lax.optimization_barrier(
-        (left3, right3, from_outer, far_inner, far)
-    )
-    far_outer = plane.send(jnp.where(plane.is_second, left3, right3), plane.outward)
-    from_inner = plane.send(far, plane.chords)
-    from_outer = from_outer.astype(f32)
-    sum_r = plane.to_right((near[0] + from_outer).astype(bf16), second)
-    sum_l = plane.to_left((near[1] + from_outer).astype(bf16), first)
-    sum_r, sum_l, far_outer, from_inner, total = lax.optimization_barrier(
-        (sum_r, sum_l, far_outer, from_inner, total)
-    )
-    for_partner = after(jnp.where(plane.is_first, near[1], near[0]).astype(bf16), sum_r)
-    from_partner = plane.send(for_partner, plane.chords)
-    sum_r = plane.to_right((near[2] + sum_r.astype(f32)).astype(bf16))
-    sum_l = plane.to_left((near[3] + sum_l.astype(f32)).astype(bf16))
-    sum_r, sum_l = lax.optimization_barrier((sum_r, sum_l))
-    from_inner = from_inner.astype(f32)
-    more_r = near[4] + jnp.where(plane.is_first, from_inner, 0.0)
-    more_l = near[5] + jnp.where(plane.is_second, from_inner, 0.0)
-    sum_r = plane.to_right((more_r + sum_r.astype(f32)).astype(bf16))
-    sum_l = plane.to_left((more_l + sum_l.astype(f32)).astype(bf16))
-    term = near[6] + from_partner.astype(f32) + sum_r.astype(f32) + sum_l.astype(f32)
-
-    blocks = [own, left1, right1, left2, right2, left3, right3, partner, far_inner, far_outer]
-    shard = own.shape[0]
-    plan = [((None, k, 0, shard),) for k in range(5)]
-    plan.append(((0, 7, 0, shard), (1, 5, 0, shard)))
-    plan.append(((2, 7, 0, shard), (3, 6, 0, shard)))
-    plan.append(((4, 8, 0, shard), (5, 9, 0, shard)))
-    inner = plane.is_first | plane.is_second
-    flags = [plane.is_first, ~plane.is_first, plane.is_second, ~plane.is_second, inner, ~inner]
-    return blocks, plan, jnp.stack(flags), term, total
+    shard, cols = own.shape
+    at0, at1, at2, at3 = plane.at
+    zero = jnp.zeros((), f32)
+    pieces = [(0, shard // 2), (shard // 2, shard)]
+    halves = range(2)
+    wide = lambda v: v.astype(f32)
+    pick = jnp.where
+    sent = [own]
+
+    def part(value, h):
+        return value[pieces[h][0] : pieces[h][1]]
+
+    def ring(to_right, to_left):
+        sent[0] = to_right, to_left
+        return lax.optimization_barrier((plane.to_right(to_right), plane.to_left(to_left)))
+
+    def later(*values):
+        return after(values, sent[0])
+
+    one = [ring(*later(part(own, h), part(own, h))) for h in halves]
+    total, came = replica_sum(pseudo)
+    one[0], far, came = lax.optimization_barrier((one[0], far, came))
+    two = [ring(*later(*one[h])) for h in halves]
+    two[1], total = lax.optimization_barrier((two[1], total))
+    partner = plane.over_chord(after(own, total))
+    three = []
+    for h in halves:
+        left, right = later(*two[h])
+        terms = part(far, h)
+        three.append(ring(pick(at0, terms, left), pick(at3, terms, right)))
+    three[1], partner = lax.optimization_barrier((three[1], partner))
+    from_inner = plane.over_chord(after(far, partner))
+    four = []
+    for h in halves:
+        left, right = later(*three[h])
+        to_right = wide(part(near[0], h)) + pick(at1, wide(left), zero)
+        to_left = wide(part(near[1], h)) + pick(at2, wide(right), zero)
+        four.append(
+            ring(
+                pick(at2, left, to_right.astype(bf16)),
+                pick(at1, right, to_left.astype(bf16)),
+            )
+        )
+    four[1], from_inner = lax.optimization_barrier((four[1], from_inner))
+    join = jnp.concatenate([pick(at2, *one[h]) for h in halves])
+    far_inner = plane.over_chord(after(join, from_inner))
+    five = []
+    for h in halves:
+        left, right = later(*four[h])
+        to_right = part(near[2], h) + pick(at3, zero, wide(left))
+        to_left = part(near[3], h) + pick(at0, zero, wide(right))
+        five.append(ring(to_right.astype(bf16), to_left.astype(bf16)))
+    five[1], far_inner = lax.optimization_barrier((five[1], far_inner))
+    for_partner = pick(at1, near[1], near[0]).astype(bf16)
+    from_partner = plane.over_chord(after(for_partner, far_inner))
+    six = []
+    for h in halves:
+        left, right = later(*five[h])
+        chord = wide(part(from_inner, h))
+        to_right = part(near[4], h) + wide(left) + pick(at1, chord, zero)
+        to_left = part(near[5], h) + wide(right) + pick(at2, chord, zero)
+        six.append(ring(to_right.astype(bf16), to_left.astype(bf16)))
+    term = [
+        part(near[6], h) + wide(part(from_partner, h)) + wide(six[h][0]) + wide(six[h][1])
+        for h in halves
+    ]
+
+    blocks = [own, partner, far_inner]
+    plan = [[(None, 0, 0, shard)]]
+
+    def add(flag, arrays):
+        entry = []
+        for (start, stop), array in zip(pieces, arrays):
+            entry.append((flag, len(blocks), start, stop))
+            blocks.append(array)
+        return entry
+
+    for step in (one, two):
+        for way in range(2):
+            plan.append(add(None, [step[h][way] for h in halves]))
+    for way in range(2):
+        plan.append([(way, 1, 0, shard)] + add(2 + way, [three[h][way] for h in halves]))
+    plan.append([(4, 2, 0, shard)])
+    for way in range(2):
+        plan[-1] += add(5 + way, [four[h][way] for h in halves])
+    flags = [at1, at2, ~at1, ~at2, at1 | at2, at3, at0]
+    plan = tuple(tuple(entry) for entry in plan)
+    return blocks, plan, jnp.stack(flags), jnp.concatenate(term), total
 
 
 def local(
@@ -367,8 +412,7 @@
     rows, width = tokens_in.shape
     shard, cols = weight_shard.shape
 
-    weight_f = weight_shard.astype(f32)
-    own = (weight_f * gain_shard).astype(bf16)
+    own = (weight_shard.astype(f32) * gain_shard).astype(bf16)
     positions = (ring.me * rows + jnp.arange(rows, dtype=jnp.int32)) % SEQ_LEN
     cosine, sine = rope_tables(positions)
     scale = 1.0 / math.sqrt(rows * ring.count)
@@ -378,10 +422,11 @@
     exchange = exchange_plane if small else exchange_ring
     blocks, plan, flags, term, total = exchange(ring, own, far, near, pseudo_grad[0])
     weight_grad = term * gain_shard
-    gain_grad = jnp.sum(term * weight_f, axis=1)
-
-    replicas = lax.axis_size("replica")
-    average = total / replicas
+    gain_grad = jnp.sum(term * weight_shard.astype(f32), axis=1)
+
+    if isinstance(total, tuple):
+        total = jnp.concatenate(total)
+    average = total / lax.axis_size("replica")
     momentum_new = momentum_rate * outer_momentum + average
     global_new = global_params - outer_rate * (average + momentum_rate * momentum_new)
     local_new = (

time: 176 us -> 189 us (1.074)
  other arithmetic: 25.8 us -> 42.2 us
  local copies, waits for them, and re-layouts: 2.38 us -> 6.07 us
  waiting for transfers between devices: 76.4 us -> 72.8 us
  starting transfers between devices: 38.4 us -> 35.6 us
    select_n x2 -> x6, other arithmetic: 0.22 us -> 10.4 us  [the longest x2 5.25 us: exchange_plane(): pick(at1, right, to_left.astype(bf16))]
    add x2 -> x3, other arithmetic: 1.66 us -> 7.18 us  [the longest x1 2.68 us: exchange_plane(): part(near[6], h) + wide(part(from_partner, h)) + wide(six[h][0])]
    ppermute x20 -> x31, waiting for transfers between devices: 76.4 us -> 72.8 us  [the longest x12 50.8 us: to_right(): return lax.ppermute(value, 'fsdp', self.right)]
    reduce_sum x1, other arithmetic: 4.23 us -> 0.88 us  [local(): gain_grad = jnp.sum(term * weight_shard.astype(f32), axis=1)]
    ppermute x20 -> x31, starting transfers between devices: 38.4 us -> 35.6 us  [the longest x12 18 us: to_right(): return lax.ppermute(value, 'fsdp', self.right)]
    broadcast_in_dim x1, other arithmetic: 2.55 us -> 5.27 us  [local(): local_new[None]]
    dynamic_slice x0 -> x1, local copies, waits for them, and re-layouts: none -> 2.18 us  [replica_sum(): theirs = lax.dynamic_slice_in_dim(value, (1 - odd) * half, half, 0)]
    convert_element_type x5 -> x6, other arithmetic: 15.1 us -> 13.8 us  [the longest x2 5.3 us: exchange_plane(): six.append(ring(to_right.astype(bf16), to_left.astype(bf16)))]
  transfers between devices with their start and end apart: 20 -> 31, of which waited for: 13 -> 18; matrix products, arithmetic and copies ran while one was open for 9% -> 18% of each run, Pallas kernels for 17% -> 16%
where the time goes in v6:
time: 189 us; the launch traced here: 187 us
  waiting for transfers between devices  72.8 us (39%)
  other arithmetic  42.2 us (22%)
  starting transfers between devices  35.6 us (19%)
  Pallas kernels  29.5 us (16%)
  local copies, waits for them, and re-layouts  6.07 us (3%)
    ppermute x12, waiting for transfers between devices, to_right(): return lax.ppermute(value, 'fsdp', self.right)  50.8 us
    ppermute x12, waiting for transfers between devices, to_left(): return lax.ppermute(value, 'fsdp', self.left)  19.1 us
    ppermute x12, starting transfers between devices, to_right(): return lax.ppermute(value, 'fsdp', self.right)  18 us
    pallas_call x1, Pallas kernels, second_part(): pl.pallas_call(functools.partial(second_kernel, plan), in_specs=[pl.Block...  17.6 us
    pallas_call x1, Pallas kernels, first_part(): pl.pallas_call(functools.partial(first_kernel, scale), grid_spec=pltpu.Pr...  11.9 us
    ppermute x4, starting transfers between devices, over_chord(): return lax.ppermute(value, 'fsdp', [(2, 3), (3, 2), (4, 5), (5, 4)])  9.37 us
    ppermute x12, starting transfers between devices, to_left(): return lax.ppermute(value, 'fsdp', self.left)  6.74 us
    convert_element_type x2, other arithmetic, exchange_plane(): six.append(ring(to_right.astype(bf16), to_left.astype(bf16)))  5.3 us
  transfers between devices with their start and end apart: 31, of which 18 were waited for; matrix products, arithmetic and copies ran while one was open for 18% of the time, Pallas kernels for 16%

profile of v6, /device:TPU:8, one launch (start us, length us, event | category | flops | bytes accessed | tf_op | source)
XLA Modules:
  0.0 187.2 jit_solution(21247929494425153)
XLA Ops:
  0.7 2.2 %dynamic-slice_bitcast_fusion = f32[192,1024]{1,0:T(8,128)} fusion(f32[1,384,1024]{2,1,0:T(8,128)} %param.14, s32[]{:T(128)S(6)} %select_n.196), kind=kLoop, calls=%fused_computation.58 | loop fusion | bytes 1572868 | tf_op jit(solution)/shard_map/dynamic_slice | solution.py:269
  5.8 1.6 collective-permute-start
  7.8 1.6 collective-permute-start.3
  11.2 2.1 %bitcast_add_fusion.14 = f32[192,1024]{1,0:T(8,128)} fusion(f32[192,1024]{1,0:T(8,128)} %collective-permute-done.2, f32[1,384,1024]{2,1,0:T(8,128)S(1)} %copy-done.14, s32[]{:T(128)S(6)} %select_n.198), kind=kLoop, calls=%fused_computation.57 | loop fusion | flops 196608 | bytes 2359300 | tf_op jit(solution)/shard_map/add | solution.py:271
  13.4 1.5 collective-permute-start.7
  14.9 11.9 %norm_and_weight_terms.1 = (bf16[512,1024]{1,0:T(8,128)(2,1)S(1)}, f32[512,128]{1,0:T(8,128)S(1)}, bf16[512,1024]{1,0:T(8,128)(2,1)S(1)}, f32[7,512,1024]{2,1,0:T(8,128)}) custom-call(s32[8]{0:T(128)S(1)} %compare_select_fusion.4.at, bf16[512,4096]{1,0:T(8,128)(2,1)S(1)} %bitcast.99, bf16[512,1024]{1,0:T(8,128)(2,1)S(1)} %bitcast.100, ...), custom_call_target="tpu_custom_call" | custom-call | flops 4294967296 | bytes 20971520 | tf_op jit(solution)/shard_map/norm_and_weight_terms/pallas_call | solution.py:115
  28.9 1.6 collective-permute-start.9
  30.5 1.6 collective-permute-done.3.refs_4_
  32.1 1.6 collective-permute-done.4.refs_6_
  33.7 1.6 collective-permute-start.5
  35.7 9.1 %collective-permute-done.10.refs_9_ = bf16[256,1024]{1,0:T(8,128)(2,1)S(1)} collective-permute-done((bf16[256,1024]{1,0:T(8,128)(2,1)}, bf16[256,1024]{1,0:T(8,128)(2,1)S(1)}, u32[]{:S(2)}, u32[]{:S(2)}) %collective-permute-start.10) | collective-permute-done | bytes 524320 | tf_op jit(solution)/shard_map/ppermute | solution.py:45
  44.8 2.4 %add.169 = f32[192,1024]{1,0:T(8,128)} add(f32[192,1024]{1,0:T(8,128)} %bitcast_add_fusion.14, f32[192,1024]{1,0:T(8,128)} %collective-permute-done.7) | non-fusion elementwise | flops 196608 | bytes 2359296 | tf_op jit(solution)/shard_map/add | solution.py:272
  48.2 1.6 collective-permute-start.14
  50.3 4.9 %collective-permute-done.5.refs_8_ = bf16[256,1024]{1,0:T(8,128)(2,1)S(1)} collective-permute-done((bf16[256,1024]{1,0:T(8,128)(2,1)}, bf16[256,1024]{1,0:T(8,128)(2,1)S(1)}, u32[]{:S(2)}, u32[]{:S(2)}) %collective-permute-start.5) | collective-permute-done | bytes 524320 | tf_op jit(solution)/shard_map/ppermute | solution.py:42
  56.0 9.3 %collective-permute-done.14.refs_11_ = bf16[256,1024]{1,0:T(8,128)(2,1)} collective-permute-done((bf16[256,1024]{1,0:T(8,128)(2,1)}, bf16[256,1024]{1,0:T(8,128)(2,1)}, u32[]{:S(2)}, u32[]{:S(2)}) %collective-permute-start.14) | collective-permute-done | bytes 524320 | tf_op jit(solution)/shard_map/ppermute | solution.py:42
  66.7 2.7 %broadcast_select_fusion.6 = (f32[192,1024]{1,0:T(8,128)}, f32[192,1024]{1,0:T(8,128)}) fusion(f32[192,1024]{1,0:T(8,128)} %collective-permute-done.8, f32[192,1024]{1,0:T(8,128)} %add.169, pred[]{:T(512)S(6)} %eq.36), kind=kLoop, calls=%fused_computation.65 | loop fusion | flops 393216 | bytes 3145729 | tf_op jit(solution)/shard_map/jit(_where)/select_n | solution.py:274
  69.4 2.3 %collective-permute-start.13 = (bf16[512,1024]{1,0:T(8,128)(2,1)S(1)}, bf16[512,1024]{1,0:T(8,128)(2,1)S(1)}, u32[]{:S(2)}, u32[]{:S(2)}) collective-permute-start(bf16[512,1024]{1,0:T(8,128)(2,1)S(1)} %copy-done.10), channel_id=1, source_target_pairs={{2,3},{3,2},{4,5},{5,4},{10,11},{11,10},{12,13},{13,12},{18,19},{1... | collective-permute-start | bytes 3145736 | tf_op jit(solution)/shard_map/ppermute | solution.py:54
  71.8 2.7 %fusion.26 = (bf16[256,1024]{1,0:T(8,128)(2,1)S(1)}, bf16[256,1024]{1,0:T(8,128)(2,1)S(1)}) fusion(bf16[256,1024]{1,0:T(8,128)(2,1)} %collective-permute-done.15.refs_13_, f32[7,512,1024]{2,1,0:T(8,128)} %get-tuple-element.115, pred[]{:T(512)} %eq.32, pred[]{:T(512)} %eq.33, bf16[256,1024]{1,0:T(8,128)(2,1)} %collective-permute-done.14.refs_11_), kind=kLoop, calls=%fused_computation.53 | loop fusion | flops 2621440 | bytes 4194306 | tf_op jit(solution)/shard_map/jit(_where)/select_n | solution.py:346
  74.5 1.6 collective-permute-start.19
  76.6 1.6 collective-permute-start.11
  78.6 10.8 %collective-permute-done.19.refs_15_ = bf16[256,1024]{1,0:T(8,128)(2,1)S(1)} collective-permute-done((bf16[256,1024]{1,0:T(8,128)(2,1)S(1)}, bf16[256,1024]{1,0:T(8,128)(2,1)S(1)}, u32[]{:S(2)}, u32[]{:S(2)}) %collective-permute-start.19) | collective-permute-done | bytes 524320 | tf_op jit(solution)/shard_map/ppermute | solution.py:42
  89.4 1.6 collective-permute-done.20.refs_17_
  91.0 7.8 %collective-permute-done.11.refs_12_ = bf16[256,1024]{1,0:T(8,128)(2,1)S(1)} collective-permute-done((bf16[256,1024]{1,0:T(8,128)(2,1)S(1)}, bf16[256,1024]{1,0:T(8,128)(2,1)S(1)}, u32[]{:S(2)}, u32[]{:S(2)}) %collective-permute-start.11) | collective-permute-done | bytes 524320 | tf_op jit(solution)/shard_map/ppermute | solution.py:42
  100.1 2.5 %fusion.28 = (bf16[256,1024]{1,0:T(8,128)(2,1)S(1)}, bf16[256,1024]{1,0:T(8,128)(2,1)S(1)}) fusion(bf16[256,1024]{1,0:T(8,128)(2,1)S(1)} %collective-permute-done.12.refs_14_, f32[7,512,1024]{2,1,0:T(8,128)} %get-tuple-element.115, pred[]{:T(512)} %eq.32, pred[]{:T(512)} %eq.33, bf16[256,1024]{1,0:T(8,128)(2,1)S(1)} %collective-permute-done.11.refs_12_), kind=kLoop, calls=%fused_computation.55 | loop fusion | flops 2621440 | bytes 4194306 | tf_op jit(solution)/shard_map/jit(_where)/select_n | solution.py:346
  103.2 1.6 collective-permute-start.17
  104.7 2.5 %collective-permute-start.18 = (bf16[512,1024]{1,0:T(8,128)(2,1)S(1)}, bf16[512,1024]{1,0:T(8,128)(2,1)S(1)}, u32[]{:S(2)}, u32[]{:S(2)}) collective-permute-start(bf16[512,1024]{1,0:T(8,128)(2,1)S(1)} %get-tuple-element.126), channel_id=1, source_target_pairs={{2,3},{3,2},{4,5},{5,4},{10,11},{11,10},{12,13},{13,12},{18,19},{1... | collective-permute-start | bytes 3145736 | tf_op jit(solution)/shard_map/ppermute | solution.py:54
  107.2 1.9 %fusion.18 = (bf16[256,1024]{1,0:T(8,128)(2,1)S(1)}, bf16[256,1024]{1,0:T(8,128)(2,1)S(1)}) fusion(bf16[256,1024]{1,0:T(8,128)(2,1)S(1)} %collective-permute-done.20.refs_17_, f32[7,512,1024]{2,1,0:T(8,128)} %get-tuple-element.115, pred[]{:T(512)} %eq.35, bf16[256,1024]{1,0:T(8,128)(2,1)S(1)} %collective-permute-done.19.refs_15_, pred[]{:T(512)} %eq.34), kind=kLoop, calls=%fused_computation.39 | loop fusion | flops 2097152 | bytes 4194306 | tf_op jit(solution)/shard_map/convert_element_type | solution.py:357
  109.1 1.6 collective-permute-start.25
  111.2 3.4 %fusion.12 = bf16[512,1024]{1,0:T(8,128)(2,1)} fusion(f32[7,512,1024]{2,1,0:T(8,128)} %get-tuple-element.115, pred[]{:T(512)} %eq.32), kind=kLoop, calls=%fused_computation.24 | loop fusion | flops 524288 | bytes 3145729 | tf_op jit(solution)/shard_map/convert_element_type | solution.py:359
  114.6 1.3 broadcast_select_fusion
  116.9 8.7 %collective-permute-done.25 = bf16[256,1024]{1,0:T(8,128)(2,1)S(1)} collective-permute-done((bf16[256,1024]{1,0:T(8,128)(2,1)S(1)}, bf16[256,1024]{1,0:T(8,128)(2,1)S(1)}, u32[]{:S(2)}, u32[]{:S(2)}) %collective-permute-start.25) | collective-permute-done | bytes 524320 | tf_op jit(solution)/shard_map/ppermute | solution.py:42
  126.2 2.9 %collective-permute-done.18 = bf16[512,1024]{1,0:T(8,128)(2,1)S(1)} collective-permute-done((bf16[512,1024]{1,0:T(8,128)(2,1)S(1)}, bf16[512,1024]{1,0:T(8,128)(2,1)S(1)}, u32[]{:S(2)}, u32[]{:S(2)}) %collective-permute-start.18) | collective-permute-done | bytes 1048608 | tf_op jit(solution)/shard_map/ppermute | solution.py:54
  129.0 2.7 %collective-permute-start.23 = (bf16[512,1024]{1,0:T(8,128)(2,1)}, bf16[512,1024]{1,0:T(8,128)(2,1)}, u32[]{:S(2)}, u32[]{:S(2)}) collective-permute-start(bf16[512,1024]{1,0:T(8,128)(2,1)} %pad_maximum_fusion), channel_id=1, source_target_pairs={{2,3},{3,2},{4,5},{5,4},{10,11},{11,10},{12,13},{13,12},{18,19},{1... | collective-permute-start | bytes 3145736 | tf_op jit(solution)/shard_map/ppermute | solution.py:54
  131.8 3.0 %fusion.17 = (bf16[256,1024]{1,0:T(8,128)(2,1)}, bf16[256,1024]{1,0:T(8,128)(2,1)}) fusion(bf16[256,1024]{1,0:T(8,128)(2,1)S(1)} %collective-permute-done.17.refs_18_, f32[7,512,1024]{2,1,0:T(8,128)} %get-tuple-element.115, pred[]{:T(512)} %eq.35, bf16[256,1024]{1,0:T(8,128)(2,1)S(1)} %collective-permute-done.16.refs_16_, pred[]{:T(512)} %eq.34), kind=kLoop, calls=%fused_computation.37 | loop fusion | flops 2097152 | bytes 4194306 | tf_op jit(solution)/shard_map/convert_element_type | solution.py:357
  134.8 1.6 collective-permute-start.21
  136.8 3.0 %fusion.7 = (bf16[256,1024]{1,0:T(8,128)(2,1)}, bf16[256,1024]{1,0:T(8,128)(2,1)}) fusion(bf16[256,1024]{1,0:T(8,128)(2,1)S(1)} %collective-permute-done.26, f32[7,512,1024]{2,1,0:T(8,128)} %get-tuple-element.115, pred[]{:T(512)} %eq.33, bf16[512,1024]{1,0:T(8,128)(2,1)S(1)} %collective-permute-done.18, pred[]{:T(512)} %eq.32, ...), kind=kLoop, calls=%fused_computation.19 | loop fusion | flops 2883584 | bytes 4718594 | tf_op jit(solution)/shard_map/convert_element_type | solution.py:367
  139.8 1.6 collective-permute-start.27
  142.1 5.3 %fusion.29 = (bf16[1,384,1024]{2,1,0:T(8,128)(2,1)}, f32[384,1024]{1,0:T(8,128)}, f32[384,1024]{1,0:T(8,128)}) fusion(bf16[1,384,1024]{2,1,0:T(8,128)(2,1)} %param.17, f32[384,1024]{1,0:T(8,128)} %param.16, f32[192,1024]{1,0:T(8,128)S(1)} %copy-done.13, f32[192,1024]{1,0:T(8,128)} %get-tuple-element.111, f32[384,1024]{1,0:T(8,128)} %param.15), kind=kLoop, calls=%fused_computation.56 | loop fusion | flops 4718592 | bytes 9437184 | tf_op jit(solution)/shard_map/broadcast_in_dim | solution.py:446
  147.3 2.6 %collective-permute-done.21 = bf16[256,1024]{1,0:T(8,128)(2,1)} collective-permute-done((bf16[256,1024]{1,0:T(8,128)(2,1)}, bf16[256,1024]{1,0:T(8,128)(2,1)}, u32[]{:S(2)}, u32[]{:S(2)}) %collective-permute-start.21) | collective-permute-done | bytes 524320 | tf_op jit(solution)/shard_map/ppermute | solution.py:42
  149.9 1.6 collective-permute-done.22
  151.5 5.1 %collective-permute-done.27 = bf16[256,1024]{1,0:T(8,128)(2,1)} collective-permute-done((bf16[256,1024]{1,0:T(8,128)(2,1)}, bf16[256,1024]{1,0:T(8,128)(2,1)}, u32[]{:S(2)}, u32[]{:S(2)}) %collective-permute-start.27) | collective-permute-done | bytes 524320 | tf_op jit(solution)/shard_map/ppermute | solution.py:42
  156.6 1.3 collective-permute-done.28
  157.9 1.9 %collective-permute-start.24 = (bf16[512,1024]{1,0:T(8,128)(2,1)S(1)}, bf16[512,1024]{1,0:T(8,128)(2,1)S(1)}, u32[]{:S(2)}, u32[]{:S(2)}) collective-permute-start(bf16[512,1024]{1,0:T(8,128)(2,1)S(1)} %copy-done.17), channel_id=1, source_target_pairs={{2,3},{3,2},{4,5},{5,4},{10,11},{11,10},{12,13},{13,12},{18,19},{1... | collective-permute-start | bytes 3145736 | tf_op jit(solution)/shard_map/ppermute | solution.py:54
  159.8 2.3 %fusion.11 = (bf16[256,1024]{1,0:T(8,128)(2,1)S(1)}, bf16[256,1024]{1,0:T(8,128)(2,1)S(1)}) fusion(bf16[256,1024]{1,0:T(8,128)(2,1)} %collective-permute-done.22, f32[7,512,1024]{2,1,0:T(8,128)} %get-tuple-element.115, pred[]{:T(512)} %eq.33, bf16[512,1024]{1,0:T(8,128)(2,1)S(1)} %copy-done.16, pred[]{:T(512)} %eq.32, ...), kind=kLoop, calls=%fused_computation.23 | loop fusion | flops 2883584 | bytes 4718594 | tf_op jit(solution)/shard_map/convert_element_type | solution.py:367
  162.1 1.6 collective-permute-start.29
  164.4 17.6 %project_and_input_grad.1 = (bf16[512,1024]{1,0:T(8,128)(2,1)}, bf16[512,4096]{1,0:T(8,128)(2,1)}) custom-call(s32[15]{0:T(128)S(1)} %pad_add_fusion.at, bf16[512,4096]{1,0:T(8,128)(2,1)} %bitcast.98, bf16[512,1024]{1,0:T(8,128)(2,1)} %copy-done.6, f32[512,128]{1,0:T(8,128)S(1)} %copy-done.8, f32[512,128]{1,0:T(8,128)S(1)} %copy-done.3, ...), custom_call_target="tpu_custom_call" | custom-call | flops 8589934592 | bytes 16777216 | tf_op jit(solution)/shard_map/project_and_input_grad/pallas_call | solution.py:230
  182.1 2.7 %fusion.16 = (f32[256,1024]{1,0:T(8,128)S(1)}, f32[256,1024]{1,0:T(8,128)S(1)}) fusion(bf16[256,1024]{1,0:T(8,128)(2,1)} %collective-permute-done.28, bf16[256,1024]{1,0:T(8,128)(2,1)} %collective-permute-done.27, f32[7,512,1024]{2,1,0:T(8,128)} %get-tuple-element.115, bf16[512,1024]{1,0:T(8,128)(2,1)S(1)} %collective-permute-done.24, ...), kind=kLoop, calls=%fused_computation.35 | loop fusion | flops 3145728 | bytes 7340032 | tf_op jit(solution)/shard_map/add | solution.py:369
  185.7 1.5 maximum_multiply_fusion
  (100 shorter events, 18.9 us)
Async XLA Ops:
  2.8 8.4 %collective-permute-start.2 = (f32[192,1024]{1,0:T(8,128)}, f32[192,1024]{1,0:T(8,128)}, u32[]{:S(2)}, u32[]{:S(2)}) collective-permute-start(f32[192,1024]{1,0:T(8,128)} %dynamic-slice_bitcast_fusion), channel_id=1, source_target_pairs={{0,8},{8,0},{16,24},{24,16},{1,9},{9,1},{17,25},{25,17},{2,10},{10... | collective-permute-start | bytes 2359304 | tf_op jit(solution)/shard_map/ppermute | solution.py:265
  3.5 7.7 %copy-start.14 = (f32[1,384,1024]{2,1,0:T(8,128)S(1)}, f32[1,384,1024]{2,1,0:T(8,128)}, u32[]{:S(2)}) copy-start(f32[1,384,1024]{2,1,0:T(8,128)} %param.14) | copy-start | bytes 4718596
  4.8 6.4 %copy-start.25 = (s32[8]{0:T(128)S(1)}, s32[8]{0:T(128)}, u32[]{:S(2)}) copy-start(s32[8]{0:T(128)} %constant.120.clone) | copy-start | bytes 100
  4.8 10.1 %copy-start.5 = (bf16[1,512,1024]{2,1,0:T(8,128)(2,1)S(1)}, bf16[1,512,1024]{2,1,0:T(8,128)(2,1)}, u32[]{:S(2)}) copy-start(bf16[1,512,1024]{2,1,0:T(8,128)(2,1)} %param.13) | copy-start | bytes 3145732
  5.8 22.7 %collective-permute-start = (bf16[256,1024]{1,0:T(8,128)(2,1)}, bf16[256,1024]{1,0:T(8,128)(2,1)}, u32[]{:S(2)}, u32[]{:S(2)}) collective-permute-start(bf16[256,1024]{1,0:T(8,128)(2,1)} %get-tuple-element.84), channel_id=1, source_target_pairs={{0,2},{2,4},{4,6},{6,7},{7,5},{5,3},{3,1},{1,0},{8,10},{10,12},{12... | collective-permute-start | bytes 1572872 | tf_op jit(solution)/shard_map/ppermute | solution.py:42
  7.4 21.1 %collective-permute-start.1 = (bf16[256,1024]{1,0:T(8,128)(2,1)}, bf16[256,1024]{1,0:T(8,128)(2,1)}, u32[]{:S(2)}, u32[]{:S(2)}) collective-permute-start(bf16[256,1024]{1,0:T(8,128)(2,1)} %get-tuple-element.84), channel_id=1, source_target_pairs={{2,0},{4,2},{6,4},{7,6},{5,7},{3,5},{1,3},{0,1},{10,8},{12,10},{14... | collective-permute-start | bytes 1572872 | tf_op jit(solution)/shard_map/ppermute | solution.py:45
  7.8 24.2 %collective-permute-start.3 = (bf16[256,1024]{1,0:T(8,128)(2,1)}, bf16[256,1024]{1,0:T(8,128)(2,1)}, u32[]{:S(2)}, u32[]{:S(2)}) collective-permute-start(bf16[256,1024]{1,0:T(8,128)(2,1)} %get-tuple-element.90), channel_id=1, source_target_pairs={{0,2},{2,4},{4,6},{6,7},{7,5},{5,3},{3,1},{1,0},{8,10},{10,12},{12... | collective-permute-start | bytes 1572872 | tf_op jit(solution)/shard_map/ppermute | solution.py:42
  9.4 24.3 %collective-permute-start.4 = (bf16[256,1024]{1,0:T(8,128)(2,1)}, bf16[256,1024]{1,0:T(8,128)(2,1)}, u32[]{:S(2)}, u32[]{:S(2)}) collective-permute-start(bf16[256,1024]{1,0:T(8,128)(2,1)} %get-tuple-element.90), channel_id=1, source_target_pairs={{2,0},{4,2},{6,4},{7,6},{5,7},{3,5},{1,3},{0,1},{10,8},{12,10},{14... | collective-permute-start | bytes 1572872 | tf_op jit(solution)/shard_map/ppermute | solution.py:45
  11.0 15.7 %copy-start.2 = (f32[512,128]{1,0:T(8,128)}, f32[512,128]{1,0:T(8,128)S(1)}, u32[]{:S(2)}) copy-start(f32[512,128]{1,0:T(8,128)S(1)} %pad_maximum_fusion.1.cosine) | copy-start | bytes 786436
  13.4 31.5 %collective-permute-start.7 = (f32[192,1024]{1,0:T(8,128)}, f32[192,1024]{1,0:T(8,128)}, u32[]{:S(2)}, u32[]{:S(2)}) collective-permute-start(f32[192,1024]{1,0:T(8,128)} %bitcast_add_fusion.14), channel_id=1, source_target_pairs={{0,16},{8,24},{16,0},{24,8},{1,17},{9,25},{17,1},{25,9},{2,18},{10... | collective-permute-start | bytes 2359304 | tf_op jit(solution)/shard_map/ppermute | solution.py:265
  28.5 16.3 %collective-permute-start.10 = (bf16[256,1024]{1,0:T(8,128)(2,1)}, bf16[256,1024]{1,0:T(8,128)(2,1)S(1)}, u32[]{:S(2)}, u32[]{:S(2)}) collective-permute-start(bf16[256,1024]{1,0:T(8,128)(2,1)} %collective-permute-done.1.refs_5_), channel_id=1, source_target_pairs={{2,0},{4,2},{6,4},{7,6},{5,7},{3,5},{1,3},{0,1},{10,8},{12,10},{14... | collective-permute-start | bytes 1572872 | tf_op jit(solution)/shard_map/ppermute | solution.py:45
  28.9 15.9 %collective-permute-start.9 = (bf16[256,1024]{1,0:T(8,128)(2,1)}, bf16[256,1024]{1,0:T(8,128)(2,1)S(1)}, u32[]{:S(2)}, u32[]{:S(2)}) collective-permute-start(bf16[256,1024]{1,0:T(8,128)(2,1)} %collective-permute-done.refs_3_), channel_id=1, source_target_pairs={{0,2},{2,4},{4,6},{6,7},{7,5},{5,3},{3,1},{1,0},{8,10},{10,12},{12... | collective-permute-start | bytes 1572872 | tf_op jit(solution)/shard_map/ppermute | solution.py:42
  33.7 21.5 %collective-permute-start.5 = (bf16[256,1024]{1,0:T(8,128)(2,1)}, bf16[256,1024]{1,0:T(8,128)(2,1)S(1)}, u32[]{:S(2)}, u32[]{:S(2)}) collective-permute-start(bf16[256,1024]{1,0:T(8,128)(2,1)} %collective-permute-done.3.refs_4_), channel_id=1, source_target_pairs={{0,2},{2,4},{4,6},{6,7},{7,5},{5,3},{3,1},{1,0},{8,10},{10,12},{12... | collective-permute-start | bytes 1572872 | tf_op jit(solution)/shard_map/ppermute | solution.py:42
  35.3 20.8 %collective-permute-start.6 = (bf16[256,1024]{1,0:T(8,128)(2,1)}, bf16[256,1024]{1,0:T(8,128)(2,1)S(1)}, u32[]{:S(2)}, u32[]{:S(2)}) collective-permute-start(bf16[256,1024]{1,0:T(8,128)(2,1)} %collective-permute-done.4.refs_6_), channel_id=1, source_target_pairs={{2,0},{4,2},{6,4},{7,6},{5,7},{3,5},{1,3},{0,1},{10,8},{12,10},{14... | collective-permute-start | bytes 1572872 | tf_op jit(solution)/shard_map/ppermute | solution.py:45
  47.2 19.5 %collective-permute-start.8 = (f32[192,1024]{1,0:T(8,128)}, f32[192,1024]{1,0:T(8,128)}, u32[]{:S(2)}, u32[]{:S(2)}) collective-permute-start(f32[192,1024]{1,0:T(8,128)} %add.169), channel_id=1, source_target_pairs={{0,8},{8,0},{16,24},{24,16},{1,9},{9,1},{17,25},{25,17},{2,10},{10... | collective-permute-start | bytes 2359304 | tf_op jit(solution)/shard_map/ppermute | solution.py:265
  48.2 17.1 %collective-permute-start.14 = (bf16[256,1024]{1,0:T(8,128)(2,1)}, bf16[256,1024]{1,0:T(8,128)(2,1)}, u32[]{:S(2)}, u32[]{:S(2)}) collective-permute-start(bf16[256,1024]{1,0:T(8,128)(2,1)} %get-tuple-element.177), channel_id=1, source_target_pairs={{0,2},{2,4},{4,6},{6,7},{7,5},{5,3},{3,1},{1,0},{8,10},{10,12},{12... | collective-permute-start | bytes 1572872 | tf_op jit(solution)/shard_map/ppermute | solution.py:42
  49.8 16.9 %collective-permute-start.15 = (bf16[256,1024]{1,0:T(8,128)(2,1)}, bf16[256,1024]{1,0:T(8,128)(2,1)}, u32[]{:S(2)}, u32[]{:S(2)}) collective-permute-start(bf16[256,1024]{1,0:T(8,128)(2,1)} %get-tuple-element.176), channel_id=1, source_target_pairs={{2,0},{4,2},{6,4},{7,6},{5,7},{3,5},{1,3},{0,1},{10,8},{12,10},{14... | collective-permute-start | bytes 1572872 | tf_op jit(solution)/shard_map/ppermute | solution.py:45
  50.3 19.1 %copy-start.10 = (bf16[512,1024]{1,0:T(8,128)(2,1)S(1)}, bf16[512,1024]{1,0:T(8,128)(2,1)}, u32[]{:S(2)}) copy-start(bf16[512,1024]{1,0:T(8,128)(2,1)} %copy-done.9) | copy-start | bytes 3145732
  69.4 30.7 %collective-permute-start.13 = (bf16[512,1024]{1,0:T(8,128)(2,1)S(1)}, bf16[512,1024]{1,0:T(8,128)(2,1)S(1)}, u32[]{:S(2)}, u32[]{:S(2)}) collective-permute-start(bf16[512,1024]{1,0:T(8,128)(2,1)S(1)} %copy-done.10), channel_id=1, source_target_pairs={{2,3},{3,2},{4,5},{5,4},{10,11},{11,10},{12,13},{13,12},{18,19},{1... | collective-permute-start | bytes 3145736 | tf_op jit(solution)/shard_map/ppermute | solution.py:54
  74.5 14.9 %collective-permute-start.19 = (bf16[256,1024]{1,0:T(8,128)(2,1)S(1)}, bf16[256,1024]{1,0:T(8,128)(2,1)S(1)}, u32[]{:S(2)}, u32[]{:S(2)}) collective-permute-start(bf16[256,1024]{1,0:T(8,128)(2,1)S(1)} %get-tuple-element.171), channel_id=1, source_target_pairs={{0,2},{2,4},{4,6},{6,7},{7,5},{5,3},{3,1},{1,0},{8,10},{10,12},{12... | collective-permute-start | bytes 1572872 | tf_op jit(solution)/shard_map/ppermute | solution.py:42
  76.1 14.9 %collective-permute-start.20 = (bf16[256,1024]{1,0:T(8,128)(2,1)S(1)}, bf16[256,1024]{1,0:T(8,128)(2,1)S(1)}, u32[]{:S(2)}, u32[]{:S(2)}) collective-permute-start(bf16[256,1024]{1,0:T(8,128)(2,1)S(1)} %get-tuple-element.170), channel_id=1, source_target_pairs={{2,0},{4,2},{6,4},{7,6},{5,7},{3,5},{1,3},{0,1},{10,8},{12,10},{14... | collective-permute-start | bytes 1572872 | tf_op jit(solution)/shard_map/ppermute | solution.py:45
  76.6 22.2 %collective-permute-start.11 = (bf16[256,1024]{1,0:T(8,128)(2,1)S(1)}, bf16[256,1024]{1,0:T(8,128)(2,1)S(1)}, u32[]{:S(2)}, u32[]{:S(2)}) collective-permute-start(bf16[256,1024]{1,0:T(8,128)(2,1)S(1)} %get-tuple-element.175), channel_id=1, source_target_pairs={{0,2},{2,4},{4,6},{6,7},{7,5},{5,3},{3,1},{1,0},{8,10},{10,12},{12... | collective-permute-start | bytes 1572872 | tf_op jit(solution)/shard_map/ppermute | solution.py:42
  78.2 21.9 %collective-permute-start.12 = (bf16[256,1024]{1,0:T(8,128)(2,1)S(1)}, bf16[256,1024]{1,0:T(8,128)(2,1)S(1)}, u32[]{:S(2)}, u32[]{:S(2)}) collective-permute-start(bf16[256,1024]{1,0:T(8,128)(2,1)S(1)} %get-tuple-element.174), channel_id=1, source_target_pairs={{2,0},{4,2},{6,4},{7,6},{5,7},{3,5},{1,3},{0,1},{10,8},{12,10},{14... | collective-permute-start | bytes 1572872 | tf_op jit(solution)/shard_map/ppermute | solution.py:45
  89.4 17.7 %copy-start.18 = (bf16[256,1024]{1,0:T(8,128)(2,1)}, bf16[256,1024]{1,0:T(8,128)(2,1)S(1)}, u32[]{:S(2)}) copy-start(bf16[256,1024]{1,0:T(8,128)(2,1)S(1)} %collective-permute-done.19.refs_15_) | copy-start | bytes 1572868
  91.0 16.2 %copy-start.19 = (bf16[256,1024]{1,0:T(8,128)(2,1)}, bf16[256,1024]{1,0:T(8,128)(2,1)S(1)}, u32[]{:S(2)}) copy-start(bf16[256,1024]{1,0:T(8,128)(2,1)S(1)} %collective-permute-done.20.refs_17_) | copy-start | bytes 1572868
  102.6 23.5 %collective-permute-start.16 = (bf16[256,1024]{1,0:T(8,128)(2,1)S(1)}, bf16[256,1024]{1,0:T(8,128)(2,1)S(1)}, u32[]{:S(2)}, u32[]{:S(2)}) collective-permute-start(bf16[256,1024]{1,0:T(8,128)(2,1)S(1)} %get-tuple-element.169), channel_id=1, source_target_pairs={{0,2},{2,4},{4,6},{6,7},{7,5},{5,3},{3,1},{1,0},{8,10},{10,12},{12... | collective-permute-start | bytes 1572872 | tf_op jit(solution)/shard_map/ppermute | solution.py:42
  103.2 23.0 %collective-permute-start.17 = (bf16[256,1024]{1,0:T(8,128)(2,1)S(1)}, bf16[256,1024]{1,0:T(8,128)(2,1)S(1)}, u32[]{:S(2)}, u32[]{:S(2)}) collective-permute-start(bf16[256,1024]{1,0:T(8,128)(2,1)S(1)} %get-tuple-element.168), channel_id=1, source_target_pairs={{2,0},{4,2},{6,4},{7,6},{5,7},{3,5},{1,3},{0,1},{10,8},{12,10},{14... | collective-permute-start | bytes 1572872 | tf_op jit(solution)/shard_map/ppermute | solution.py:45
  104.7 24.3 %collective-permute-start.18 = (bf16[512,1024]{1,0:T(8,128)(2,1)S(1)}, bf16[512,1024]{1,0:T(8,128)(2,1)S(1)}, u32[]{:S(2)}, u32[]{:S(2)}) collective-permute-start(bf16[512,1024]{1,0:T(8,128)(2,1)S(1)} %get-tuple-element.126), channel_id=1, source_target_pairs={{2,3},{3,2},{4,5},{5,4},{10,11},{11,10},{12,13},{13,12},{18,19},{1... | collective-permute-start | bytes 3145736 | tf_op jit(solution)/shard_map/ppermute | solution.py:54
  109.1 16.5 %collective-permute-start.25 = (bf16[256,1024]{1,0:T(8,128)(2,1)S(1)}, bf16[256,1024]{1,0:T(8,128)(2,1)S(1)}, u32[]{:S(2)}, u32[]{:S(2)}) collective-permute-start(bf16[256,1024]{1,0:T(8,128)(2,1)S(1)} %get-tuple-element.167), channel_id=1, source_target_pairs={{0,2},{2,4},{4,6},{6,7},{7,5},{5,3},{3,1},{1,0},{8,10},{10,12},{12... | collective-permute-start | bytes 1572872 | tf_op jit(solution)/shard_map/ppermute | solution.py:42
  110.8 15.4 %collective-permute-start.26 = (bf16[256,1024]{1,0:T(8,128)(2,1)S(1)}, bf16[256,1024]{1,0:T(8,128)(2,1)S(1)}, u32[]{:S(2)}, u32[]{:S(2)}) collective-permute-start(bf16[256,1024]{1,0:T(8,128)(2,1)S(1)} %get-tuple-element.166), channel_id=1, source_target_pairs={{2,0},{4,2},{6,4},{7,6},{5,7},{3,5},{1,3},{0,1},{10,8},{12,10},{14... | collective-permute-start | bytes 1572872 | tf_op jit(solution)/shard_map/ppermute | solution.py:45
  126.2 8.6 %copy-start.21 = (bf16[256,1024]{1,0:T(8,128)(2,1)}, bf16[256,1024]{1,0:T(8,128)(2,1)S(1)}, u32[]{:S(2)}) copy-start(bf16[256,1024]{1,0:T(8,128)(2,1)S(1)} %collective-permute-done.16.refs_16_) | copy-start | bytes 1572868
  126.2 8.6 %copy-start.22 = (bf16[256,1024]{1,0:T(8,128)(2,1)}, bf16[256,1024]{1,0:T(8,128)(2,1)S(1)}, u32[]{:S(2)}) copy-start(bf16[256,1024]{1,0:T(8,128)(2,1)S(1)} %collective-permute-done.17.refs_18_) | copy-start | bytes 1572868
  129.0 7.8 %copy-start.15 = (bf16[512,1024]{1,0:T(8,128)(2,1)}, bf16[512,1024]{1,0:T(8,128)(2,1)S(1)}, u32[]{:S(2)}) copy-start(bf16[512,1024]{1,0:T(8,128)(2,1)S(1)} %collective-permute-done.18) | copy-start | bytes 3145732
  129.0 28.9 %collective-permute-start.23 = (bf16[512,1024]{1,0:T(8,128)(2,1)}, bf16[512,1024]{1,0:T(8,128)(2,1)}, u32[]{:S(2)}, u32[]{:S(2)}) collective-permute-start(bf16[512,1024]{1,0:T(8,128)(2,1)} %pad_maximum_fusion), channel_id=1, source_target_pairs={{2,3},{3,2},{4,5},{5,4},{10,11},{11,10},{12,13},{13,12},{18,19},{1... | collective-permute-start | bytes 3145736 | tf_op jit(solution)/shard_map/ppermute | solution.py:54
  134.8 15.2 %collective-permute-start.21 = (bf16[256,1024]{1,0:T(8,128)(2,1)}, bf16[256,1024]{1,0:T(8,128)(2,1)}, u32[]{:S(2)}, u32[]{:S(2)}) collective-permute-start(bf16[256,1024]{1,0:T(8,128)(2,1)} %get-tuple-element.165), channel_id=1, source_target_pairs={{0,2},{2,4},{4,6},{6,7},{7,5},{5,3},{3,1},{1,0},{8,10},{10,12},{12... | collective-permute-start | bytes 1572872 | tf_op jit(solution)/shard_map/ppermute | solution.py:42
  136.4 5.5 %copy-start.24 = (s32[8]{0:T(128)S(1)}, s32[8]{0:T(128)}, u32[]{:S(2)}) copy-start(s32[8]{0:T(128)} %constant.121.clone) | copy-start | bytes 100
  136.4 5.7 %copy-start.13 = (f32[192,1024]{1,0:T(8,128)S(1)}, f32[192,1024]{1,0:T(8,128)}, u32[]{:S(2)}) copy-start(f32[192,1024]{1,0:T(8,128)} %get-tuple-element.112) | copy-start | bytes 2359300
  136.4 15.2 %collective-permute-start.22 = (bf16[256,1024]{1,0:T(8,128)(2,1)}, bf16[256,1024]{1,0:T(8,128)(2,1)}, u32[]{:S(2)}, u32[]{:S(2)}) collective-permute-start(bf16[256,1024]{1,0:T(8,128)(2,1)} %get-tuple-element.164), channel_id=1, source_target_pairs={{2,0},{4,2},{6,4},{7,6},{5,7},{3,5},{1,3},{0,1},{10,8},{12,10},{14... | collective-permute-start | bytes 1572872 | tf_op jit(solution)/shard_map/ppermute | solution.py:45
  139.8 16.8 %collective-permute-start.27 = (bf16[256,1024]{1,0:T(8,128)(2,1)}, bf16[256,1024]{1,0:T(8,128)(2,1)}, u32[]{:S(2)}, u32[]{:S(2)}) collective-permute-start(bf16[256,1024]{1,0:T(8,128)(2,1)} %get-tuple-element.163), channel_id=1, source_target_pairs={{0,2},{2,4},{4,6},{6,7},{7,5},{5,3},{3,1},{1,0},{8,10},{10,12},{12... | collective-permute-start | bytes 1572872 | tf_op jit(solution)/shard_map/ppermute | solution.py:42
  141.4 16.5 %collective-permute-start.28 = (bf16[256,1024]{1,0:T(8,128)(2,1)}, bf16[256,1024]{1,0:T(8,128)(2,1)}, u32[]{:S(2)}, u32[]{:S(2)}) collective-permute-start(bf16[256,1024]{1,0:T(8,128)(2,1)} %get-tuple-element.162), channel_id=1, source_target_pairs={{2,0},{4,2},{6,4},{7,6},{5,7},{3,5},{1,3},{0,1},{10,8},{12,10},{14... | collective-permute-start | bytes 1572872 | tf_op jit(solution)/shard_map/ppermute | solution.py:45
  142.1 15.9 %copy-start.17 = (bf16[512,1024]{1,0:T(8,128)(2,1)S(1)}, bf16[512,1024]{1,0:T(8,128)(2,1)}, u32[]{:S(2)}) copy-start(bf16[512,1024]{1,0:T(8,128)(2,1)} %fusion.12) | copy-start | bytes 3145732
  142.1 17.8 %copy-start.16 = (bf16[512,1024]{1,0:T(8,128)(2,1)S(1)}, bf16[512,1024]{1,0:T(8,128)(2,1)}, u32[]{:S(2)}) copy-start(bf16[512,1024]{1,0:T(8,128)(2,1)} %copy-done.15) | copy-start | bytes 3145732
  147.3 17.1 %copy-start.1 = (bf16[256,1024]{1,0:T(8,128)(2,1)S(1)}, bf16[256,1024]{1,0:T(8,128)(2,1)}, u32[]{:S(2)}) copy-start(bf16[256,1024]{1,0:T(8,128)(2,1)} %copy-done) | copy-start | bytes 1572868
  147.3 17.1 %copy-start.3 = (f32[512,128]{1,0:T(8,128)S(1)}, f32[512,128]{1,0:T(8,128)}, u32[]{:S(2)}) copy-start(f32[512,128]{1,0:T(8,128)} %copy-done.2) | copy-start | bytes 786436
  147.3 17.1 %copy-start.8 = (f32[512,128]{1,0:T(8,128)S(1)}, f32[512,128]{1,0:T(8,128)}, u32[]{:S(2)}) copy-start(f32[512,128]{1,0:T(8,128)} %copy-done.7) | copy-start | bytes 786436
  157.9 24.2 %collective-permute-start.24 = (bf16[512,1024]{1,0:T(8,128)(2,1)S(1)}, bf16[512,1024]{1,0:T(8,128)(2,1)S(1)}, u32[]{:S(2)}, u32[]{:S(2)}) collective-permute-start(bf16[512,1024]{1,0:T(8,128)(2,1)S(1)} %copy-done.17), channel_id=1, source_target_pairs={{2,3},{3,2},{4,5},{5,4},{10,11},{11,10},{12,13},{13,12},{18,19},{1... | collective-permute-start | bytes 3145736 | tf_op jit(solution)/shard_map/ppermute | solution.py:54
  162.1 19.9 %collective-permute-start.29 = (bf16[256,1024]{1,0:T(8,128)(2,1)S(1)}, bf16[256,1024]{1,0:T(8,128)(2,1)S(1)}, u32[]{:S(2)}, u32[]{:S(2)}) collective-permute-start(bf16[256,1024]{1,0:T(8,128)(2,1)S(1)} %get-tuple-element.161), channel_id=1, source_target_pairs={{0,2},{2,4},{4,6},{6,7},{7,5},{5,3},{3,1},{1,0},{8,10},{10,12},{12... | collective-permute-start | bytes 1572872 | tf_op jit(solution)/shard_map/ppermute | solution.py:42
  163.7 18.4 %collective-permute-start.30 = (bf16[256,1024]{1,0:T(8,128)(2,1)S(1)}, bf16[256,1024]{1,0:T(8,128)(2,1)S(1)}, u32[]{:S(2)}, u32[]{:S(2)}) collective-permute-start(bf16[256,1024]{1,0:T(8,128)(2,1)S(1)} %get-tuple-element.160), channel_id=1, source_target_pairs={{2,0},{4,2},{6,4},{7,6},{5,7},{3,5},{1,3},{0,1},{10,8},{12,10},{14... | collective-permute-start | bytes 1572872 | tf_op jit(solution)/shard_map/ppermute | solution.py:45
  (9 other events, 22.3 us)

commit v7 on v6

--- a/solution.py
+++ b/solution.py
@@ -277,7 +277,9 @@
 
 def exchange_ring(ring, own, far, near, pseudo):
     total, came = replica_sum(pseudo)
-    shard, cut = own.shape[0], own.shape[0] // 2
+    cut = own[0].shape[0]
+    own = jnp.concatenate(own)
+    shard = own.shape[0]
     blocks = [own]
     from_left = from_right = own
     for d in range(1, ring.half):
@@ -303,75 +305,63 @@
 
 
 def exchange_plane(plane, own, far, near, pseudo):
-    shard, cols = own.shape
+    shard = 2 * own[0].shape[0]
     at0, at1, at2, at3 = plane.at
     zero = jnp.zeros((), f32)
     pieces = [(0, shard // 2), (shard // 2, shard)]
     halves = range(2)
     wide = lambda v: v.astype(f32)
     pick = jnp.where
-    sent = [own]
+    sent, crossed = [own], [own]
 
     def part(value, h):
         return value[pieces[h][0] : pieces[h][1]]
 
-    def ring(to_right, to_left):
-        sent[0] = to_right, to_left
-        return lax.optimization_barrier((plane.to_right(to_right), plane.to_left(to_left)))
-
     def later(*values):
         return after(values, sent[0])
 
-    one = [ring(*later(part(own, h), part(own, h))) for h in halves]
-    total, came = replica_sum(pseudo)
+    def links(to_right, to_left, chord=None):
+        sent[0] = to_right, to_left
+        came = [plane.to_right(to_right), plane.to_left(to_left)]
+        if chord is not None:
+            came.append(plane.over_chord(after(chord, sent[0], crossed[0])))
+            crossed[0] = came[-1]
+        return lax.optimization_barrier(came)
+
+    one = [links(*later(own[h], own[h])) for h in halves]
+    total, came = replica_sum(after(pseudo, sent[0]))
     one[0], far, came = lax.optimization_barrier((one[0], far, came))
-    two = [ring(*later(*one[h])) for h in halves]
-    two[1], total = lax.optimization_barrier((two[1], total))
-    partner = plane.over_chord(after(own, total))
+    two = [links(*later(*one[h])) for h in halves]
+    two[0], total = lax.optimization_barrier((two[0], total))
     three = []
     for h in halves:
         left, right = later(*two[h])
         terms = part(far, h)
-        three.append(ring(pick(at0, terms, left), pick(at3, terms, right)))
-    three[1], partner = lax.optimization_barrier((three[1], partner))
-    from_inner = plane.over_chord(after(far, partner))
+        three.append(links(pick(at0, terms, left), pick(at3, terms, right), own[h]))
     four = []
     for h in halves:
-        left, right = later(*three[h])
+        left, right, _ = later(*three[h])
         to_right = wide(part(near[0], h)) + pick(at1, wide(left), zero)
         to_left = wide(part(near[1], h)) + pick(at2, wide(right), zero)
-        four.append(
-            ring(
-                pick(at2, left, to_right.astype(bf16)),
-                pick(at1, right, to_left.astype(bf16)),
-            )
-        )
-    four[1], from_inner = lax.optimization_barrier((four[1], from_inner))
-    join = jnp.concatenate([pick(at2, *one[h]) for h in halves])
-    far_inner = plane.over_chord(after(join, from_inner))
+        to_right = pick(at2, left, to_right.astype(bf16))
+        to_left = pick(at1, right, to_left.astype(bf16))
+        four.append(links(to_right, to_left, pick(at2, *one[h])))
     five = []
     for h in halves:
-        left, right = later(*four[h])
+        left, right, _ = later(*four[h])
         to_right = part(near[2], h) + pick(at3, zero, wide(left))
         to_left = part(near[3], h) + pick(at0, zero, wide(right))
-        five.append(ring(to_right.astype(bf16), to_left.astype(bf16)))
-    five[1], far_inner = lax.optimization_barrier((five[1], far_inner))
-    for_partner = pick(at1, near[1], near[0]).astype(bf16)
-    from_partner = plane.over_chord(after(for_partner, far_inner))
+        five.append(links(to_right.astype(bf16), to_left.astype(bf16), part(far, h)))
     six = []
     for h in halves:
-        left, right = later(*five[h])
-        chord = wide(part(from_inner, h))
-        to_right = part(near[4], h) + wide(left) + pick(at1, chord, zero)
-        to_left = part(near[5], h) + wide(right) + pick(at2, chord, zero)
-        six.append(ring(to_right.astype(bf16), to_left.astype(bf16)))
-    term = [
-        part(near[6], h) + wide(part(from_partner, h)) + wide(six[h][0]) + wide(six[h][1])
-        for h in halves
-    ]
-
-    blocks = [own, partner, far_inner]
-    plan = [[(None, 0, 0, shard)]]
+        left, right, chord = later(*five[h])
+        to_right = part(near[4], h) + wide(left) + pick(at1, wide(chord), zero)
+        to_left = part(near[5], h) + wide(right) + pick(at2, wide(chord), zero)
+        for_partner = part(pick(at1, near[1], near[0]).astype(bf16), h)
+        six.append(links(to_right.astype(bf16), to_left.astype(bf16), for_partner))
+    term = [part(near[6], h) + sum(wide(came) for came in six[h]) for h in halves]
+
+    blocks, plan = [], []
 
     def add(flag, arrays):
         entry = []
@@ -380,12 +370,15 @@
             blocks.append(array)
         return entry
 
+    plan.append(add(None, own))
     for step in (one, two):
         for way in range(2):
             plan.append(add(None, [step[h][way] for h in halves]))
+    partner = add(0, [three[h][2] for h in halves])
     for way in range(2):
-        plan.append([(way, 1, 0, shard)] + add(2 + way, [three[h][way] for h in halves]))
-    plan.append([(4, 2, 0, shard)])
+        entry = [(way, *rest) for _, *rest in partner]
+        plan.append(entry + add(2 + way, [three[h][way] for h in halves]))
+    plan.append(add(4, [four[h][2] for h in halves]))
     for way in range(2):
         plan[-1] += add(5 + way, [four[h][way] for h in halves])
     flags = [at1, at2, ~at1, ~at2, at1 | at2, at3, at0]
@@ -412,7 +405,11 @@
     rows, width = tokens_in.shape
     shard, cols = weight_shard.shape
 
-    own = (weight_shard.astype(f32) * gain_shard).astype(bf16)
+    cut = shard // 2
+    own = [
+        (weight_shard[rows].astype(f32) * gain_shard[rows]).astype(bf16)
+        for rows in (slice(0, cut), slice(cut, shard))
+    ]
     positions = (ring.me * rows + jnp.arange(rows, dtype=jnp.int32)) % SEQ_LEN
     cosine, sine = rope_tables(positions)
     scale = 1.0 / math.sqrt(rows * ring.count)

time: 189 us -> 182 us (0.963)
  starting transfers between devices: 35.6 us -> 45.4 us
  waiting for transfers between devices: 72.8 us -> 63.9 us
  other arithmetic: 42.2 us -> 37.8 us
  local copies, waits for them, and re-layouts: 6.07 us -> 3.88 us
    ppermute x12, waiting for transfers between devices: 50.8 us -> 13.3 us  [to_right(): return lax.ppermute(value, 'fsdp', self.right)]
    ppermute x4 -> x8, waiting for transfers between devices: 2.86 us -> 25.7 us  [over_chord(): return lax.ppermute(value, 'fsdp', [(2, 3), (3, 2), (4, 5), (5, 4)])]
    ppermute x3, waiting for transfers between devices: 0.01 us -> 16 us  [replica_sum(): lax.ppermute(v, 'replica', [(r, r ^ step) for r in range(4)])]
    ppermute x12, waiting for transfers between devices: 19.1 us -> 8.94 us  [to_left(): return lax.ppermute(value, 'fsdp', self.left)]
    ppermute x4 -> x8, starting transfers between devices: 9.37 us -> 19.2 us  [over_chord(): return lax.ppermute(value, 'fsdp', [(2, 3), (3, 2), (4, 5), (5, 4)])]
    broadcast_in_dim x1, other arithmetic: 5.27 us -> 2.5 us  [local(): local_new[None]]
    select_n x5, other arithmetic: 7.7 us -> 10.4 us  [the longest x2 6.09 us: exchange_plane(): to_left = pick(at1, right, to_left.astype(bf16))]
  transfers between devices with their start and end apart: 31 -> 35, of which waited for: 18 -> 15; matrix products, arithmetic and copies ran while one was open for 18% -> 18% of each run, Pallas kernels for 16% -> 16%
where the time goes in v7:
time: 182 us; the launch traced here: 181 us
  waiting for transfers between devices  63.9 us (35%)
  starting transfers between devices  45.4 us (25%)
  other arithmetic  37.8 us (21%)
  Pallas kernels  29.2 us (16%)
  local copies, waits for them, and re-layouts  3.88 us (2%)
    ppermute x8, waiting for transfers between devices, over_chord(): return lax.ppermute(value, 'fsdp', [(2, 3), (3, 2), (4, 5), (5, 4)])  25.7 us
    ppermute x12, starting transfers between devices, to_right(): return lax.ppermute(value, 'fsdp', self.right)  19.5 us
    ppermute x8, starting transfers between devices, over_chord(): return lax.ppermute(value, 'fsdp', [(2, 3), (3, 2), (4, 5), (5, 4)])  19.2 us
    pallas_call x1, Pallas kernels, second_part(): pl.pallas_call(functools.partial(second_kernel, plan), in_specs=[pl.Block...  17.4 us
    ppermute x3, waiting for transfers between devices, replica_sum(): lax.ppermute(v, 'replica', [(r, r ^ step) for r in range(4)])  16 us
    ppermute x12, waiting for transfers between devices, to_right(): return lax.ppermute(value, 'fsdp', self.right)  13.3 us
    pallas_call x1, Pallas kernels, first_part(): pl.pallas_call(functools.partial(first_kernel, scale), grid_spec=pltpu.Pr...  11.8 us
    ppermute x12, waiting for transfers between devices, to_left(): return lax.ppermute(value, 'fsdp', self.left)  8.94 us
  transfers between devices with their start and end apart: 35, of which 15 were waited for; matrix products, arithmetic and copies ran while one was open for 18% of the time, Pallas kernels for 16%

profile of v7, /device:TPU:8, one launch (start us, length us, event | category | flops | bytes accessed | tf_op | source)
XLA Modules:
  0.0 181.4 jit_solution(2150063467860331639)
XLA Ops:
  4.1 1.6 collective-permute-start
  6.2 1.6 collective-permute-start.3
  9.5 1.6 collective-permute-start.7
  12.4 16.0 %collective-permute-done.7 = f32[192,1024]{1,0:T(8,128)S(1)} collective-permute-done((f32[192,1024]{1,0:T(8,128)S(1)}, f32[192,1024]{1,0:T(8,128)S(1)}, u32[]{:S(2)}, u32[]{:S(2)}) %collective-permute-start.7) | collective-permute-done | bytes 786464 | tf_op jit(solution)/shard_map/ppermute | solution.py:265
  29.4 11.8 %norm_and_weight_terms.1 = (bf16[512,1024]{1,0:T(8,128)(2,1)S(1)}, f32[512,128]{1,0:T(8,128)S(1)}, bf16[512,1024]{1,0:T(8,128)(2,1)S(1)}, f32[7,512,1024]{2,1,0:T(8,128)}) custom-call(s32[8]{0:T(128)S(1)} %compare_select_fusion.4.at, bf16[512,4096]{1,0:T(8,128)(2,1)S(1)} %bitcast.97, bf16[512,1024]{1,0:T(8,128)(2,1)S(1)} %bitcast.98, ...), custom_call_target="tpu_custom_call" | custom-call | flops 4294967296 | bytes 20971520 | tf_op jit(solution)/shard_map/norm_and_weight_terms/pallas_call | solution.py:115
  42.9 1.6 collective-permute-start.5
  45.3 1.7 collective-permute-start.9
  47.0 10.9 %collective-permute-done.5.refs_6_ = bf16[256,1024]{1,0:T(8,128)(2,1)S(1)} collective-permute-done((bf16[256,1024]{1,0:T(8,128)(2,1)}, bf16[256,1024]{1,0:T(8,128)(2,1)S(1)}, u32[]{:S(2)}, u32[]{:S(2)}) %collective-permute-start.5) | collective-permute-done | bytes 524320 | tf_op jit(solution)/shard_map/ppermute | solution.py:42
  57.9 1.6 collective-permute-done.6.refs_8_
  59.5 2.7 %broadcast_select_fusion.6 = (f32[192,1024]{1,0:T(8,128)}, f32[192,1024]{1,0:T(8,128)}) fusion(f32[192,1024]{1,0:T(8,128)} %collective-permute-done.8, f32[192,1024]{1,0:T(8,128)} %add.169, pred[]{:T(512)S(6)} %eq.36), kind=kLoop, calls=%fused_computation.62 | loop fusion | flops 393216 | bytes 3145729 | tf_op jit(solution)/shard_map/jit(_where)/select_n | solution.py:274
  63.6 2.3 %collective-permute-start.13 = (bf16[256,1024]{1,0:T(8,128)(2,1)S(1)}, bf16[256,1024]{1,0:T(8,128)(2,1)}, u32[]{:S(2)}, u32[]{:S(2)}) collective-permute-start(bf16[256,1024]{1,0:T(8,128)(2,1)S(1)} %get-tuple-element.114.refs_0_), channel_id=1, source_target_pairs={{2,3},{3,2},{4,5},{5,4},{10,11},{11,10},{12,13},{13,12},{18,19},{1... | collective-permute-start | bytes 1572872 | tf_op jit(solution)/shard_map/ppermute | solution.py:54
  65.9 4.2 %collective-permute-done.10.refs_9_ = bf16[256,1024]{1,0:T(8,128)(2,1)} collective-permute-done((bf16[256,1024]{1,0:T(8,128)(2,1)}, bf16[256,1024]{1,0:T(8,128)(2,1)}, u32[]{:S(2)}, u32[]{:S(2)}) %collective-permute-start.10) | collective-permute-done | bytes 524320 | tf_op jit(solution)/shard_map/ppermute | solution.py:45
  70.1 1.6 collective-permute-start.11
  73.4 4.8 %collective-permute-done.13.refs_10_ = bf16[256,1024]{1,0:T(8,128)(2,1)} collective-permute-done((bf16[256,1024]{1,0:T(8,128)(2,1)S(1)}, bf16[256,1024]{1,0:T(8,128)(2,1)}, u32[]{:S(2)}, u32[]{:S(2)}) %collective-permute-start.13) | collective-permute-done | bytes 524320 | tf_op jit(solution)/shard_map/ppermute | solution.py:54
  78.2 2.3 %collective-permute-start.16 = (bf16[256,1024]{1,0:T(8,128)(2,1)S(1)}, bf16[256,1024]{1,0:T(8,128)(2,1)S(1)}, u32[]{:S(2)}, u32[]{:S(2)}) collective-permute-start(bf16[256,1024]{1,0:T(8,128)(2,1)S(1)} %get-tuple-element.118.refs_1_), channel_id=1, source_target_pairs={{2,3},{3,2},{4,5},{5,4},{10,11},{11,10},{12,13},{13,12},{18,19},{1... | collective-permute-start | bytes 1572872 | tf_op jit(solution)/shard_map/ppermute | solution.py:54
  81.6 1.6 collective-permute-start.14
  83.7 1.5 collective-permute-done.11.refs_12_
  86.4 2.9 %fusion.22 = (bf16[256,1024]{1,0:T(8,128)(2,1)S(1)}, bf16[256,1024]{1,0:T(8,128)(2,1)}) fusion(bf16[256,1024]{1,0:T(8,128)(2,1)S(1)} %collective-permute-done.12.refs_14_, f32[7,512,1024]{2,1,0:T(8,128)} %get-tuple-element.125, pred[]{:T(512)} %eq.32, pred[]{:T(512)} %eq.33, bf16[256,1024]{1,0:T(8,128)(2,1)S(1)} %collective-permute-done.11.refs_12_), kind=kLoop, calls=%fused_computation.49 | loop fusion | flops 2621440 | bytes 4194306 | tf_op jit(solution)/shard_map/jit(_where)/select_n | solution.py:347
  89.3 2.5 %collective-permute-done.16.refs_11_ = bf16[256,1024]{1,0:T(8,128)(2,1)S(1)} collective-permute-done((bf16[256,1024]{1,0:T(8,128)(2,1)S(1)}, bf16[256,1024]{1,0:T(8,128)(2,1)S(1)}, u32[]{:S(2)}, u32[]{:S(2)}) %collective-permute-start.16) | collective-permute-done | bytes 524320 | tf_op jit(solution)/shard_map/ppermute | solution.py:54
  91.8 2.3 %collective-permute-start.19 = (bf16[256,1024]{1,0:T(8,128)(2,1)S(1)}, bf16[256,1024]{1,0:T(8,128)(2,1)S(1)}, u32[]{:S(2)}, u32[]{:S(2)}) collective-permute-start(bf16[256,1024]{1,0:T(8,128)(2,1)S(1)} %broadcast_select_fusion.1), channel_id=1, source_target_pairs={{2,3},{3,2},{4,5},{5,4},{10,11},{11,10},{12,13},{13,12},{18,19},{1... | collective-permute-start | bytes 1572872 | tf_op jit(solution)/shard_map/ppermute | solution.py:54
  94.1 1.9 %broadcast_select_fusion = bf16[256,1024]{1,0:T(8,128)(2,1)} fusion(bf16[256,1024]{1,0:T(8,128)(2,1)} %collective-permute-done.3.refs_3_, bf16[256,1024]{1,0:T(8,128)(2,1)} %collective-permute-done.4.refs_5_, pred[]{:T(512)} %eq.33), kind=kLoop, calls=%fused_computation.56 | loop fusion | flops 262144 | bytes 1572865 | tf_op jit(solution)/shard_map/jit(_where)/select_n | solution.py:348
  96.0 1.6 collective-permute-start.17
  98.1 3.2 %fusion.24 = (bf16[256,1024]{1,0:T(8,128)(2,1)S(1)}, bf16[256,1024]{1,0:T(8,128)(2,1)}) fusion(bf16[256,1024]{1,0:T(8,128)(2,1)S(1)} %collective-permute-done.15.refs_15_, f32[7,512,1024]{2,1,0:T(8,128)} %get-tuple-element.125, pred[]{:T(512)} %eq.32, pred[]{:T(512)} %eq.33, bf16[256,1024]{1,0:T(8,128)(2,1)S(1)} %collective-permute-done.14.refs_13_), kind=kLoop, calls=%fused_computation.51 | loop fusion | flops 2621440 | bytes 4194306 | tf_op jit(solution)/shard_map/jit(_where)/select_n | solution.py:347
  101.3 3.2 %collective-permute-done.19.refs_16_ = bf16[256,1024]{1,0:T(8,128)(2,1)S(1)} collective-permute-done((bf16[256,1024]{1,0:T(8,128)(2,1)S(1)}, bf16[256,1024]{1,0:T(8,128)(2,1)S(1)}, u32[]{:S(2)}, u32[]{:S(2)}) %collective-permute-start.19) | collective-permute-done | bytes 524320 | tf_op jit(solution)/shard_map/ppermute | solution.py:54
  104.5 2.4 %collective-permute-start.22 = (bf16[256,1024]{1,0:T(8,128)(2,1)}, bf16[256,1024]{1,0:T(8,128)(2,1)}, u32[]{:S(2)}, u32[]{:S(2)}) collective-permute-start(bf16[256,1024]{1,0:T(8,128)(2,1)} %broadcast_select_fusion), channel_id=1, source_target_pairs={{2,3},{3,2},{4,5},{5,4},{10,11},{11,10},{12,13},{13,12},{18,19},{1... | collective-permute-start | bytes 1572872 | tf_op jit(solution)/shard_map/ppermute | solution.py:54
  107.1 1.6 collective-permute-start.20
  109.1 2.2 %fusion.15 = (bf16[256,1024]{1,0:T(8,128)(2,1)S(1)}, bf16[256,1024]{1,0:T(8,128)(2,1)S(1)}) fusion(bf16[256,1024]{1,0:T(8,128)(2,1)} %collective-permute-done.18.refs_20_, f32[7,512,1024]{2,1,0:T(8,128)} %get-tuple-element.125, pred[]{:T(512)} %eq.35, bf16[256,1024]{1,0:T(8,128)(2,1)} %collective-permute-done.17.refs_18_, pred[]{:T(512)} %eq.34), kind=kLoop, calls=%fused_computation.35 | loop fusion | flops 2097152 | bytes 4194306 | tf_op jit(solution)/shard_map/convert_element_type | solution.py:354
  111.3 5.4 %collective-permute-done.22.refs_17_ = bf16[256,1024]{1,0:T(8,128)(2,1)} collective-permute-done((bf16[256,1024]{1,0:T(8,128)(2,1)}, bf16[256,1024]{1,0:T(8,128)(2,1)}, u32[]{:S(2)}, u32[]{:S(2)}) %collective-permute-start.22) | collective-permute-done | bytes 524320 | tf_op jit(solution)/shard_map/ppermute | solution.py:54
  116.8 2.4 %collective-permute-start.25 = (bf16[256,1024]{1,0:T(8,128)(2,1)S(1)}, bf16[256,1024]{1,0:T(8,128)(2,1)S(1)}, u32[]{:S(2)}, u32[]{:S(2)}) collective-permute-start(bf16[256,1024]{1,0:T(8,128)(2,1)S(1)} %copy-done.20), channel_id=1, source_target_pairs={{2,3},{3,2},{4,5},{5,4},{10,11},{11,10},{12,13},{13,12},{18,19},{1... | collective-permute-start | bytes 1572872 | tf_op jit(solution)/shard_map/ppermute | solution.py:54
  119.1 2.4 %select_convert_fusion = bf16[1,512,1024]{2,1,0:T(8,128)(2,1)S(1)} fusion(f32[7,512,1024]{2,1,0:T(8,128)} %get-tuple-element.125, pred[]{:T(512)} %eq.32), kind=kLoop, calls=%fused_computation.3 | loop fusion | flops 524288 | bytes 3145729 | tf_op jit(solution)/shard_map/convert_element_type | solution.py:360
  121.6 1.7 collective-permute-start.23
  123.7 2.3 %fusion.13 = (bf16[256,1024]{1,0:T(8,128)(2,1)S(1)}, bf16[256,1024]{1,0:T(8,128)(2,1)S(1)}) fusion(bf16[256,1024]{1,0:T(8,128)(2,1)S(1)} %collective-permute-done.21.refs_21_, f32[7,512,1024]{2,1,0:T(8,128)} %get-tuple-element.125, pred[]{:T(512)} %eq.35, bf16[256,1024]{1,0:T(8,128)(2,1)S(1)} %collective-permute-done.20.refs_19_, pred[]{:T(512)} %eq.34), kind=kLoop, calls=%fused_computation.31 | loop fusion | flops 2097152 | bytes 4194306 | tf_op jit(solution)/shard_map/convert_element_type | solution.py:354
  126.0 3.2 %collective-permute-done.25 = bf16[256,1024]{1,0:T(8,128)(2,1)S(1)} collective-permute-done((bf16[256,1024]{1,0:T(8,128)(2,1)S(1)}, bf16[256,1024]{1,0:T(8,128)(2,1)S(1)}, u32[]{:S(2)}, u32[]{:S(2)}) %collective-permute-start.25) | collective-permute-done | bytes 524320 | tf_op jit(solution)/shard_map/ppermute | solution.py:54
  129.2 2.4 %collective-permute-start.28 = (bf16[256,1024]{1,0:T(8,128)(2,1)S(1)}, bf16[256,1024]{1,0:T(8,128)(2,1)S(1)}, u32[]{:S(2)}, u32[]{:S(2)}) collective-permute-start(bf16[256,1024]{1,0:T(8,128)(2,1)S(1)} %copy-done.17), channel_id=1, source_target_pairs={{2,3},{3,2},{4,5},{5,4},{10,11},{11,10},{12,13},{13,12},{18,19},{1... | collective-permute-start | bytes 1572872 | tf_op jit(solution)/shard_map/ppermute | solution.py:54
  131.7 1.7 collective-permute-start.30
  134.7 1.9 %collective-permute-done.24 = bf16[256,1024]{1,0:T(8,128)(2,1)S(1)} collective-permute-done((bf16[256,1024]{1,0:T(8,128)(2,1)S(1)}, bf16[256,1024]{1,0:T(8,128)(2,1)S(1)}, u32[]{:S(2)}, u32[]{:S(2)}) %collective-permute-start.24) | collective-permute-done | bytes 524320 | tf_op jit(solution)/shard_map/ppermute | solution.py:45
  136.7 2.0 %fusion.6 = (bf16[256,1024]{1,0:T(8,128)(2,1)S(1)}, bf16[256,1024]{1,0:T(8,128)(2,1)S(1)}) fusion(bf16[256,1024]{1,0:T(8,128)(2,1)S(1)} %collective-permute-done.25, bf16[256,1024]{1,0:T(8,128)(2,1)S(1)} %collective-permute-done.24, f32[7,512,1024]{2,1,0:T(8,128)} %get-tuple-element.125, pred[]{:T(512)} %eq.33, pred[]{:T(512)} %eq.32, ...), kind=kLoop, calls=%fused_computation.17 | loop fusion | flops 2883584 | bytes 4718594 | tf_op jit(solution)/shard_map/convert_element_type | solution.py:361
  138.7 3.6 %collective-permute-done.28 = bf16[256,1024]{1,0:T(8,128)(2,1)S(1)} collective-permute-done((bf16[256,1024]{1,0:T(8,128)(2,1)S(1)}, bf16[256,1024]{1,0:T(8,128)(2,1)S(1)}, u32[]{:S(2)}, u32[]{:S(2)}) %collective-permute-start.28) | collective-permute-done | bytes 524320 | tf_op jit(solution)/shard_map/ppermute | solution.py:54
  142.3 2.5 %collective-permute-start.29 = (bf16[256,1024]{1,0:T(8,128)(2,1)S(1)}, bf16[256,1024]{1,0:T(8,128)(2,1)S(1)}, u32[]{:S(2)}, u32[]{:S(2)}) collective-permute-start(bf16[256,1024]{1,0:T(8,128)(2,1)S(1)} %get-tuple-element.151), channel_id=1, source_target_pairs={{2,3},{3,2},{4,5},{5,4},{10,11},{11,10},{12,13},{13,12},{18,19},{1... | collective-permute-start | bytes 1572872 | tf_op jit(solution)/shard_map/ppermute | solution.py:54
  144.9 2.5 %fusion.25 = (bf16[1,384,1024]{2,1,0:T(8,128)(2,1)}, f32[384,1024]{1,0:T(8,128)}, f32[384,1024]{1,0:T(8,128)}) fusion(bf16[1,384,1024]{2,1,0:T(8,128)(2,1)S(1)} %copy-done.12, f32[384,1024]{1,0:T(8,128)S(1)} %copy-done.10, f32[192,1024]{1,0:T(8,128)S(1)} %copy-done.8, f32[192,1024]{1,0:T(8,128)S(1)} %copy-done.9, f32[384,1024]{1,0:T(8,128)S(1)} %copy-done.11), kind=kLoop, calls=%fused_computation.52 | loop fusion | flops 4718592 | bytes 9437184 | tf_op jit(solution)/shard_map/broadcast_in_dim | solution.py:443
  147.4 1.6 collective-permute-start.26
  149.4 2.0 %fusion.10 = (bf16[256,1024]{1,0:T(8,128)(2,1)S(1)}, bf16[256,1024]{1,0:T(8,128)(2,1)S(1)}) fusion(bf16[256,1024]{1,0:T(8,128)(2,1)S(1)} %collective-permute-done.28, bf16[256,1024]{1,0:T(8,128)(2,1)S(1)} %collective-permute-done.31, f32[7,512,1024]{2,1,0:T(8,128)} %get-tuple-element.125, pred[]{:T(512)} %eq.33, pred[]{:T(512)} %eq.32, ...), kind=kLoop, calls=%fused_computation.21 | loop fusion | flops 2883584 | bytes 4718594 | tf_op jit(solution)/shard_map/convert_element_type | solution.py:361
  151.5 1.6 collective-permute-start.32
  153.6 3.0 %collective-permute-done.29 = bf16[256,1024]{1,0:T(8,128)(2,1)S(1)} collective-permute-done((bf16[256,1024]{1,0:T(8,128)(2,1)S(1)}, bf16[256,1024]{1,0:T(8,128)(2,1)S(1)}, u32[]{:S(2)}, u32[]{:S(2)}) %collective-permute-start.29) | collective-permute-done | bytes 524320 | tf_op jit(solution)/shard_map/ppermute | solution.py:54
  156.6 2.6 %collective-permute-start.34 = (bf16[256,1024]{1,0:T(8,128)(2,1)S(1)}, bf16[256,1024]{1,0:T(8,128)(2,1)S(1)}, u32[]{:S(2)}, u32[]{:S(2)}) collective-permute-start(bf16[256,1024]{1,0:T(8,128)(2,1)S(1)} %get-tuple-element.161), channel_id=1, source_target_pairs={{2,3},{3,2},{4,5},{5,4},{10,11},{11,10},{12,13},{13,12},{18,19},{1... | collective-permute-start | bytes 1572872 | tf_op jit(solution)/shard_map/ppermute | solution.py:54
  159.2 17.4 %project_and_input_grad.1 = (bf16[512,1024]{1,0:T(8,128)(2,1)}, bf16[512,4096]{1,0:T(8,128)(2,1)}) custom-call(s32[15]{0:T(128)S(1)} %pad_add_fusion.at, bf16[512,4096]{1,0:T(8,128)(2,1)} %bitcast.96, bf16[512,1024]{1,0:T(8,128)(2,1)} %copy-done.4, f32[512,128]{1,0:T(8,128)S(1)} %copy-done.6, f32[512,128]{1,0:T(8,128)S(1)} %get-tuple-element.201.cosine, ...), custom_call_target="tpu_custom_call" | custom-call | flops 8589934592 | bytes 16777216 | tf_op jit(solution)/shard_map/project_and_input_grad/pallas_call | solution.py:230
  176.6 2.4 %bitcast_add_fusion.9 = (f32[256,1024]{1,0:T(8,128)S(1)}, f32[256,1024]{1,0:T(8,128)S(1)}) fusion(bf16[256,1024]{1,0:T(8,128)(2,1)S(1)} %collective-permute-done.29, bf16[256,1024]{1,0:T(8,128)(2,1)S(1)} %collective-permute-done.27, bf16[256,1024]{1,0:T(8,128)(2,1)S(1)} %collective-permute-done.26, f32[7,512,1024]{2,1,0:T(8,128)} %get-tuple-element.125, ...), kind=kLoop, calls=%fused_computation.39 | loop fusion | flops 3145728 | bytes 7340032 | tf_op jit(solution)/shard_map/add | solution.py:362
  179.9 1.5 maximum_multiply_fusion
  (108 shorter events, 20.9 us)
Async XLA Ops:
  4.0 4.2 %collective-permute-start.2 = (f32[192,1024]{1,0:T(8,128)S(1)}, f32[192,1024]{1,0:T(8,128)S(1)}, u32[]{:S(2)}, u32[]{:S(2)}) collective-permute-start(f32[192,1024]{1,0:T(8,128)S(1)} %constant_dynamic-slice_fusion), channel_id=1, source_target_pairs={{0,8},{8,0},{16,24},{24,16},{1,9},{9,1},{17,25},{25,17},{2,10},{10... | collective-permute-start | bytes 2359304 | tf_op jit(solution)/shard_map/ppermute | solution.py:265
  4.1 38.9 %collective-permute-start = (bf16[256,1024]{1,0:T(8,128)(2,1)S(1)}, bf16[256,1024]{1,0:T(8,128)(2,1)}, u32[]{:S(2)}, u32[]{:S(2)}) collective-permute-start(bf16[256,1024]{1,0:T(8,128)(2,1)S(1)} %get-tuple-element.114.refs_0_), channel_id=1, source_target_pairs={{0,2},{2,4},{4,6},{6,7},{7,5},{5,3},{3,1},{1,0},{8,10},{10,12},{12... | collective-permute-start | bytes 1572872 | tf_op jit(solution)/shard_map/ppermute | solution.py:42
  5.7 37.2 %collective-permute-start.1 = (bf16[256,1024]{1,0:T(8,128)(2,1)S(1)}, bf16[256,1024]{1,0:T(8,128)(2,1)}, u32[]{:S(2)}, u32[]{:S(2)}) collective-permute-start(bf16[256,1024]{1,0:T(8,128)(2,1)S(1)} %get-tuple-element.114.refs_0_), channel_id=1, source_target_pairs={{2,0},{4,2},{6,4},{7,6},{5,7},{3,5},{1,3},{0,1},{10,8},{12,10},{14... | collective-permute-start | bytes 1572872 | tf_op jit(solution)/shard_map/ppermute | solution.py:45
  6.2 38.8 %collective-permute-start.3 = (bf16[256,1024]{1,0:T(8,128)(2,1)S(1)}, bf16[256,1024]{1,0:T(8,128)(2,1)}, u32[]{:S(2)}, u32[]{:S(2)}) collective-permute-start(bf16[256,1024]{1,0:T(8,128)(2,1)S(1)} %get-tuple-element.118.refs_1_), channel_id=1, source_target_pairs={{0,2},{2,4},{4,6},{6,7},{7,5},{5,3},{3,1},{1,0},{8,10},{10,12},{12... | collective-permute-start | bytes 1572872 | tf_op jit(solution)/shard_map/ppermute | solution.py:42
  7.7 37.2 %collective-permute-start.4 = (bf16[256,1024]{1,0:T(8,128)(2,1)S(1)}, bf16[256,1024]{1,0:T(8,128)(2,1)}, u32[]{:S(2)}, u32[]{:S(2)}) collective-permute-start(bf16[256,1024]{1,0:T(8,128)(2,1)S(1)} %get-tuple-element.118.refs_1_), channel_id=1, source_target_pairs={{2,0},{4,2},{6,4},{7,6},{5,7},{3,5},{1,3},{0,1},{10,8},{12,10},{14... | collective-permute-start | bytes 1572872 | tf_op jit(solution)/shard_map/ppermute | solution.py:45
  8.2 21.2 %copy-start.3 = (bf16[1,512,1024]{2,1,0:T(8,128)(2,1)S(1)}, bf16[1,512,1024]{2,1,0:T(8,128)(2,1)}, u32[]{:S(2)}) copy-start(bf16[1,512,1024]{2,1,0:T(8,128)(2,1)} %param.13) | copy-start | bytes 3145732
  9.5 18.8 %collective-permute-start.7 = (f32[192,1024]{1,0:T(8,128)S(1)}, f32[192,1024]{1,0:T(8,128)S(1)}, u32[]{:S(2)}, u32[]{:S(2)}) collective-permute-start(f32[192,1024]{1,0:T(8,128)S(1)} %dynamic-slice_add_fusion), channel_id=1, source_target_pairs={{0,16},{8,24},{16,0},{24,8},{1,17},{9,25},{17,1},{25,9},{2,18},{10... | collective-permute-start | bytes 2359304 | tf_op jit(solution)/shard_map/ppermute | solution.py:265
  11.2 18.2 %copy-start.2 = (bf16[1,512,4096]{2,1,0:T(8,128)(2,1)S(1)}, bf16[1,512,4096]{2,1,0:T(8,128)(2,1)}, u32[]{:S(2)}) copy-start(bf16[1,512,4096]{2,1,0:T(8,128)(2,1)} %param.10) | copy-start | bytes 12582916
  12.4 28.8 %copy-start = (f32[512,128]{1,0:T(8,128)}, f32[512,128]{1,0:T(8,128)S(1)}, u32[]{:S(2)}) copy-start(f32[512,128]{1,0:T(8,128)S(1)} %get-tuple-element.202.sine) | copy-start | bytes 786436
  29.4 30.1 %collective-permute-start.8 = (f32[192,1024]{1,0:T(8,128)}, f32[192,1024]{1,0:T(8,128)}, u32[]{:S(2)}, u32[]{:S(2)}) collective-permute-start(f32[192,1024]{1,0:T(8,128)} %add.169), channel_id=1, source_target_pairs={{0,8},{8,0},{16,24},{24,16},{1,9},{9,1},{17,25},{25,17},{2,10},{10... | collective-permute-start | bytes 2359304 | tf_op jit(solution)/shard_map/ppermute | solution.py:265
  42.9 14.9 %collective-permute-start.5 = (bf16[256,1024]{1,0:T(8,128)(2,1)}, bf16[256,1024]{1,0:T(8,128)(2,1)S(1)}, u32[]{:S(2)}, u32[]{:S(2)}) collective-permute-start(bf16[256,1024]{1,0:T(8,128)(2,1)} %collective-permute-done.refs_2_), channel_id=1, source_target_pairs={{0,2},{2,4},{4,6},{6,7},{7,5},{5,3},{3,1},{1,0},{8,10},{10,12},{12... | collective-permute-start | bytes 1572872 | tf_op jit(solution)/shard_map/ppermute | solution.py:42
  44.5 15.0 %collective-permute-start.6 = (bf16[256,1024]{1,0:T(8,128)(2,1)}, bf16[256,1024]{1,0:T(8,128)(2,1)S(1)}, u32[]{:S(2)}, u32[]{:S(2)}) collective-permute-start(bf16[256,1024]{1,0:T(8,128)(2,1)} %collective-permute-done.1.refs_4_), channel_id=1, source_target_pairs={{2,0},{4,2},{6,4},{7,6},{5,7},{3,5},{1,3},{0,1},{10,8},{12,10},{14... | collective-permute-start | bytes 1572872 | tf_op jit(solution)/shard_map/ppermute | solution.py:45
  45.0 25.1 %collective-permute-start.10 = (bf16[256,1024]{1,0:T(8,128)(2,1)}, bf16[256,1024]{1,0:T(8,128)(2,1)}, u32[]{:S(2)}, u32[]{:S(2)}) collective-permute-start(bf16[256,1024]{1,0:T(8,128)(2,1)} %collective-permute-done.4.refs_5_), channel_id=1, source_target_pairs={{2,0},{4,2},{6,4},{7,6},{5,7},{3,5},{1,3},{0,1},{10,8},{12,10},{14... | collective-permute-start | bytes 1572872 | tf_op jit(solution)/shard_map/ppermute | solution.py:45
  45.3 24.8 %collective-permute-start.9 = (bf16[256,1024]{1,0:T(8,128)(2,1)}, bf16[256,1024]{1,0:T(8,128)(2,1)}, u32[]{:S(2)}, u32[]{:S(2)}) collective-permute-start(bf16[256,1024]{1,0:T(8,128)(2,1)} %collective-permute-done.3.refs_3_), channel_id=1, source_target_pairs={{0,2},{2,4},{4,6},{6,7},{7,5},{5,3},{3,1},{1,0},{8,10},{10,12},{12... | collective-permute-start | bytes 1572872 | tf_op jit(solution)/shard_map/ppermute | solution.py:42
  63.6 14.6 %collective-permute-start.13 = (bf16[256,1024]{1,0:T(8,128)(2,1)S(1)}, bf16[256,1024]{1,0:T(8,128)(2,1)}, u32[]{:S(2)}, u32[]{:S(2)}) collective-permute-start(bf16[256,1024]{1,0:T(8,128)(2,1)S(1)} %get-tuple-element.114.refs_0_), channel_id=1, source_target_pairs={{2,3},{3,2},{4,5},{5,4},{10,11},{11,10},{12,13},{13,12},{18,19},{1... | collective-permute-start | bytes 1572872 | tf_op jit(solution)/shard_map/ppermute | solution.py:54
  70.1 15.1 %collective-permute-start.11 = (bf16[256,1024]{1,0:T(8,128)(2,1)}, bf16[256,1024]{1,0:T(8,128)(2,1)S(1)}, u32[]{:S(2)}, u32[]{:S(2)}) collective-permute-start(bf16[256,1024]{1,0:T(8,128)(2,1)} %get-tuple-element.189), channel_id=1, source_target_pairs={{0,2},{2,4},{4,6},{6,7},{7,5},{5,3},{3,1},{1,0},{8,10},{10,12},{12... | collective-permute-start | bytes 1572872 | tf_op jit(solution)/shard_map/ppermute | solution.py:42
  71.7 14.7 %collective-permute-start.12 = (bf16[256,1024]{1,0:T(8,128)(2,1)}, bf16[256,1024]{1,0:T(8,128)(2,1)S(1)}, u32[]{:S(2)}, u32[]{:S(2)}) collective-permute-start(bf16[256,1024]{1,0:T(8,128)(2,1)} %get-tuple-element.190), channel_id=1, source_target_pairs={{2,0},{4,2},{6,4},{7,6},{5,7},{3,5},{1,3},{0,1},{10,8},{12,10},{14... | collective-permute-start | bytes 1572872 | tf_op jit(solution)/shard_map/ppermute | solution.py:45
  78.2 13.6 %collective-permute-start.16 = (bf16[256,1024]{1,0:T(8,128)(2,1)S(1)}, bf16[256,1024]{1,0:T(8,128)(2,1)S(1)}, u32[]{:S(2)}, u32[]{:S(2)}) collective-permute-start(bf16[256,1024]{1,0:T(8,128)(2,1)S(1)} %get-tuple-element.118.refs_1_), channel_id=1, source_target_pairs={{2,3},{3,2},{4,5},{5,4},{10,11},{11,10},{12,13},{13,12},{18,19},{1... | collective-permute-start | bytes 1572872 | tf_op jit(solution)/shard_map/ppermute | solution.py:54
  81.6 16.4 %collective-permute-start.14 = (bf16[256,1024]{1,0:T(8,128)(2,1)S(1)}, bf16[256,1024]{1,0:T(8,128)(2,1)S(1)}, u32[]{:S(2)}, u32[]{:S(2)}) collective-permute-start(bf16[256,1024]{1,0:T(8,128)(2,1)S(1)} %get-tuple-element.193), channel_id=1, source_target_pairs={{0,2},{2,4},{4,6},{6,7},{7,5},{5,3},{3,1},{1,0},{8,10},{10,12},{12... | collective-permute-start | bytes 1572872 | tf_op jit(solution)/shard_map/ppermute | solution.py:42
  83.3 14.8 %collective-permute-start.15 = (bf16[256,1024]{1,0:T(8,128)(2,1)S(1)}, bf16[256,1024]{1,0:T(8,128)(2,1)S(1)}, u32[]{:S(2)}, u32[]{:S(2)}) collective-permute-start(bf16[256,1024]{1,0:T(8,128)(2,1)S(1)} %get-tuple-element.192), channel_id=1, source_target_pairs={{2,0},{4,2},{6,4},{7,6},{5,7},{3,5},{1,3},{0,1},{10,8},{12,10},{14... | collective-permute-start | bytes 1572872 | tf_op jit(solution)/shard_map/ppermute | solution.py:45
  91.8 12.7 %collective-permute-start.19 = (bf16[256,1024]{1,0:T(8,128)(2,1)S(1)}, bf16[256,1024]{1,0:T(8,128)(2,1)S(1)}, u32[]{:S(2)}, u32[]{:S(2)}) collective-permute-start(bf16[256,1024]{1,0:T(8,128)(2,1)S(1)} %broadcast_select_fusion.1), channel_id=1, source_target_pairs={{2,3},{3,2},{4,5},{5,4},{10,11},{11,10},{12,13},{13,12},{18,19},{1... | collective-permute-start | bytes 1572872 | tf_op jit(solution)/shard_map/ppermute | solution.py:54
  96.0 10.8 %copy-start.24 = (s32[8]{0:T(128)S(1)}, s32[8]{0:T(128)}, u32[]{:S(2)}) copy-start(s32[8]{0:T(128)} %constant.119.clone) | copy-start | bytes 100
  96.0 10.8 %copy-start.21 = (bf16[1,512]{1,0:T(2,128)(2,1)S(1)}, bf16[1,512]{1,0:T(2,128)(2,1)}, u32[]{:S(2)}) copy-start(bf16[1,512]{1,0:T(2,128)(2,1)} %param.11) | copy-start | bytes 3076
  96.0 13.1 %collective-permute-start.17 = (bf16[256,1024]{1,0:T(8,128)(2,1)}, bf16[256,1024]{1,0:T(8,128)(2,1)}, u32[]{:S(2)}, u32[]{:S(2)}) collective-permute-start(bf16[256,1024]{1,0:T(8,128)(2,1)} %get-tuple-element.183), channel_id=1, source_target_pairs={{0,2},{2,4},{4,6},{6,7},{7,5},{5,3},{3,1},{1,0},{8,10},{10,12},{12... | collective-permute-start | bytes 1572872 | tf_op jit(solution)/shard_map/ppermute | solution.py:42
  97.7 11.5 %collective-permute-start.18 = (bf16[256,1024]{1,0:T(8,128)(2,1)S(1)}, bf16[256,1024]{1,0:T(8,128)(2,1)}, u32[]{:S(2)}, u32[]{:S(2)}) collective-permute-start(bf16[256,1024]{1,0:T(8,128)(2,1)S(1)} %get-tuple-element.182), channel_id=1, source_target_pairs={{2,0},{4,2},{6,4},{7,6},{5,7},{3,5},{1,3},{0,1},{10,8},{12,10},{14... | collective-permute-start | bytes 1572872 | tf_op jit(solution)/shard_map/ppermute | solution.py:45
  104.5 12.3 %collective-permute-start.22 = (bf16[256,1024]{1,0:T(8,128)(2,1)}, bf16[256,1024]{1,0:T(8,128)(2,1)}, u32[]{:S(2)}, u32[]{:S(2)}) collective-permute-start(bf16[256,1024]{1,0:T(8,128)(2,1)} %broadcast_select_fusion), channel_id=1, source_target_pairs={{2,3},{3,2},{4,5},{5,4},{10,11},{11,10},{12,13},{13,12},{18,19},{1... | collective-permute-start | bytes 1572872 | tf_op jit(solution)/shard_map/ppermute | solution.py:54
  107.1 9.7 %copy-start.20 = (bf16[256,1024]{1,0:T(8,128)(2,1)S(1)}, bf16[256,1024]{1,0:T(8,128)(2,1)}, u32[]{:S(2)}) copy-start(bf16[256,1024]{1,0:T(8,128)(2,1)} %get-tuple-element.141) | copy-start | bytes 1572868
  107.1 16.5 %collective-permute-start.20 = (bf16[256,1024]{1,0:T(8,128)(2,1)}, bf16[256,1024]{1,0:T(8,128)(2,1)S(1)}, u32[]{:S(2)}, u32[]{:S(2)}) collective-permute-start(bf16[256,1024]{1,0:T(8,128)(2,1)} %get-tuple-element.181), channel_id=1, source_target_pairs={{0,2},{2,4},{4,6},{6,7},{7,5},{5,3},{3,1},{1,0},{8,10},{10,12},{12... | collective-permute-start | bytes 1572872 | tf_op jit(solution)/shard_map/ppermute | solution.py:42
  108.7 14.9 %collective-permute-start.21 = (bf16[256,1024]{1,0:T(8,128)(2,1)S(1)}, bf16[256,1024]{1,0:T(8,128)(2,1)S(1)}, u32[]{:S(2)}, u32[]{:S(2)}) collective-permute-start(bf16[256,1024]{1,0:T(8,128)(2,1)S(1)} %get-tuple-element.180), channel_id=1, source_target_pairs={{2,0},{4,2},{6,4},{7,6},{5,7},{3,5},{1,3},{0,1},{10,8},{12,10},{14... | collective-permute-start | bytes 1572872 | tf_op jit(solution)/shard_map/ppermute | solution.py:45
  116.8 12.4 %collective-permute-start.25 = (bf16[256,1024]{1,0:T(8,128)(2,1)S(1)}, bf16[256,1024]{1,0:T(8,128)(2,1)S(1)}, u32[]{:S(2)}, u32[]{:S(2)}) collective-permute-start(bf16[256,1024]{1,0:T(8,128)(2,1)S(1)} %copy-done.20), channel_id=1, source_target_pairs={{2,3},{3,2},{4,5},{5,4},{10,11},{11,10},{12,13},{13,12},{18,19},{1... | collective-permute-start | bytes 1572872 | tf_op jit(solution)/shard_map/ppermute | solution.py:54
  121.6 13.2 %collective-permute-start.23 = (bf16[256,1024]{1,0:T(8,128)(2,1)S(1)}, bf16[256,1024]{1,0:T(8,128)(2,1)S(1)}, u32[]{:S(2)}, u32[]{:S(2)}) collective-permute-start(bf16[256,1024]{1,0:T(8,128)(2,1)S(1)} %get-tuple-element.179), channel_id=1, source_target_pairs={{0,2},{2,4},{4,6},{6,7},{7,5},{5,3},{3,1},{1,0},{8,10},{10,12},{12... | collective-permute-start | bytes 1572872 | tf_op jit(solution)/shard_map/ppermute | solution.py:42
  123.2 13.4 %collective-permute-start.24 = (bf16[256,1024]{1,0:T(8,128)(2,1)S(1)}, bf16[256,1024]{1,0:T(8,128)(2,1)S(1)}, u32[]{:S(2)}, u32[]{:S(2)}) collective-permute-start(bf16[256,1024]{1,0:T(8,128)(2,1)S(1)} %get-tuple-element.178), channel_id=1, source_target_pairs={{2,0},{4,2},{6,4},{7,6},{5,7},{3,5},{1,3},{0,1},{10,8},{12,10},{14... | collective-permute-start | bytes 1572872 | tf_op jit(solution)/shard_map/ppermute | solution.py:45
  129.2 13.2 %collective-permute-start.28 = (bf16[256,1024]{1,0:T(8,128)(2,1)S(1)}, bf16[256,1024]{1,0:T(8,128)(2,1)S(1)}, u32[]{:S(2)}, u32[]{:S(2)}) collective-permute-start(bf16[256,1024]{1,0:T(8,128)(2,1)S(1)} %copy-done.17), channel_id=1, source_target_pairs={{2,3},{3,2},{4,5},{5,4},{10,11},{11,10},{12,13},{13,12},{18,19},{1... | collective-permute-start | bytes 1572872 | tf_op jit(solution)/shard_map/ppermute | solution.py:54
  131.6 13.3 %copy-start.12 = (bf16[1,384,1024]{2,1,0:T(8,128)(2,1)S(1)}, bf16[1,384,1024]{2,1,0:T(8,128)(2,1)}, u32[]{:S(2)}) copy-start(bf16[1,384,1024]{2,1,0:T(8,128)(2,1)} %param.17) | copy-start | bytes 2359300
  131.7 13.2 %copy-start.8 = (f32[192,1024]{1,0:T(8,128)S(1)}, f32[192,1024]{1,0:T(8,128)}, u32[]{:S(2)}) copy-start(f32[192,1024]{1,0:T(8,128)} %get-tuple-element.166) | copy-start | bytes 2359300
  131.7 13.2 %copy-start.9 = (f32[192,1024]{1,0:T(8,128)S(1)}, f32[192,1024]{1,0:T(8,128)}, u32[]{:S(2)}) copy-start(f32[192,1024]{1,0:T(8,128)} %get-tuple-element.165) | copy-start | bytes 2359300
  131.7 13.2 %copy-start.10 = (f32[384,1024]{1,0:T(8,128)S(1)}, f32[384,1024]{1,0:T(8,128)}, u32[]{:S(2)}) copy-start(f32[384,1024]{1,0:T(8,128)} %param.16) | copy-start | bytes 4718596
  131.7 13.2 %copy-start.11 = (f32[384,1024]{1,0:T(8,128)S(1)}, f32[384,1024]{1,0:T(8,128)}, u32[]{:S(2)}) copy-start(f32[384,1024]{1,0:T(8,128)} %param.15) | copy-start | bytes 4718596
  131.7 17.7 %collective-permute-start.30 = (bf16[256,1024]{1,0:T(8,128)(2,1)S(1)}, bf16[256,1024]{1,0:T(8,128)(2,1)S(1)}, u32[]{:S(2)}, u32[]{:S(2)}) collective-permute-start(bf16[256,1024]{1,0:T(8,128)(2,1)S(1)} %get-tuple-element.177), channel_id=1, source_target_pairs={{0,2},{2,4},{4,6},{6,7},{7,5},{5,3},{3,1},{1,0},{8,10},{10,12},{12... | collective-permute-start | bytes 1572872 | tf_op jit(solution)/shard_map/ppermute | solution.py:42
  133.4 16.0 %collective-permute-start.31 = (bf16[256,1024]{1,0:T(8,128)(2,1)S(1)}, bf16[256,1024]{1,0:T(8,128)(2,1)S(1)}, u32[]{:S(2)}, u32[]{:S(2)}) collective-permute-start(bf16[256,1024]{1,0:T(8,128)(2,1)S(1)} %get-tuple-element.176), channel_id=1, source_target_pairs={{2,0},{4,2},{6,4},{7,6},{5,7},{3,5},{1,3},{0,1},{10,8},{12,10},{14... | collective-permute-start | bytes 1572872 | tf_op jit(solution)/shard_map/ppermute | solution.py:45
  142.3 14.3 %collective-permute-start.29 = (bf16[256,1024]{1,0:T(8,128)(2,1)S(1)}, bf16[256,1024]{1,0:T(8,128)(2,1)S(1)}, u32[]{:S(2)}, u32[]{:S(2)}) collective-permute-start(bf16[256,1024]{1,0:T(8,128)(2,1)S(1)} %get-tuple-element.151), channel_id=1, source_target_pairs={{2,3},{3,2},{4,5},{5,4},{10,11},{11,10},{12,13},{13,12},{18,19},{1... | collective-permute-start | bytes 1572872 | tf_op jit(solution)/shard_map/ppermute | solution.py:54
  147.4 11.8 %copy-start.1 = (f32[512,128]{1,0:T(8,128)S(1)}, f32[512,128]{1,0:T(8,128)}, u32[]{:S(2)}) copy-start(f32[512,128]{1,0:T(8,128)} %copy-done) | copy-start | bytes 786436
  147.4 11.8 %copy-start.6 = (f32[512,128]{1,0:T(8,128)S(1)}, f32[512,128]{1,0:T(8,128)}, u32[]{:S(2)}) copy-start(f32[512,128]{1,0:T(8,128)} %copy-done.5) | copy-start | bytes 786436
  147.4 29.2 %collective-permute-start.26 = (bf16[256,1024]{1,0:T(8,128)(2,1)S(1)}, bf16[256,1024]{1,0:T(8,128)(2,1)S(1)}, u32[]{:S(2)}, u32[]{:S(2)}) collective-permute-start(bf16[256,1024]{1,0:T(8,128)(2,1)S(1)} %get-tuple-element.173), channel_id=1, source_target_pairs={{0,2},{2,4},{4,6},{6,7},{7,5},{5,3},{3,1},{1,0},{8,10},{10,12},{12... | collective-permute-start | bytes 1572872 | tf_op jit(solution)/shard_map/ppermute | solution.py:42
  149.0 27.6 %collective-permute-start.27 = (bf16[256,1024]{1,0:T(8,128)(2,1)S(1)}, bf16[256,1024]{1,0:T(8,128)(2,1)S(1)}, u32[]{:S(2)}, u32[]{:S(2)}) collective-permute-start(bf16[256,1024]{1,0:T(8,128)(2,1)S(1)} %get-tuple-element.172), channel_id=1, source_target_pairs={{2,0},{4,2},{6,4},{7,6},{5,7},{3,5},{1,3},{0,1},{10,8},{12,10},{14... | collective-permute-start | bytes 1572872 | tf_op jit(solution)/shard_map/ppermute | solution.py:45
  151.5 25.1 %collective-permute-start.32 = (bf16[256,1024]{1,0:T(8,128)(2,1)S(1)}, bf16[256,1024]{1,0:T(8,128)(2,1)S(1)}, u32[]{:S(2)}, u32[]{:S(2)}) collective-permute-start(bf16[256,1024]{1,0:T(8,128)(2,1)S(1)} %get-tuple-element.171), channel_id=1, source_target_pairs={{0,2},{2,4},{4,6},{6,7},{7,5},{5,3},{3,1},{1,0},{8,10},{10,12},{12... | collective-permute-start | bytes 1572872 | tf_op jit(solution)/shard_map/ppermute | solution.py:42
  153.1 23.5 %collective-permute-start.33 = (bf16[256,1024]{1,0:T(8,128)(2,1)S(1)}, bf16[256,1024]{1,0:T(8,128)(2,1)S(1)}, u32[]{:S(2)}, u32[]{:S(2)}) collective-permute-start(bf16[256,1024]{1,0:T(8,128)(2,1)S(1)} %get-tuple-element.170), channel_id=1, source_target_pairs={{2,0},{4,2},{6,4},{7,6},{5,7},{3,5},{1,3},{0,1},{10,8},{12,10},{14... | collective-permute-start | bytes 1572872 | tf_op jit(solution)/shard_map/ppermute | solution.py:45
  156.6 20.0 %collective-permute-start.34 = (bf16[256,1024]{1,0:T(8,128)(2,1)S(1)}, bf16[256,1024]{1,0:T(8,128)(2,1)S(1)}, u32[]{:S(2)}, u32[]{:S(2)}) collective-permute-start(bf16[256,1024]{1,0:T(8,128)(2,1)S(1)} %get-tuple-element.161), channel_id=1, source_target_pairs={{2,3},{3,2},{4,5},{5,4},{10,11},{11,10},{12,13},{13,12},{18,19},{1... | collective-permute-start | bytes 1572872 | tf_op jit(solution)/shard_map/ppermute | solution.py:54
  (13 other events, 48.8 us)

commit v8 on v7

--- a/solution.py
+++ b/solution.py
@@ -146,6 +146,64 @@
     )(ring.devices_at(order), tokens_in, cotangent, cosine, sine)
 
 
+def last_kernel(count, own, weight, gain, *refs):
+    came, (weight_grad, gain_grad) = refs[:count], refs[-2:]
+    term = own[0]
+    for ref in came:
+        term = term + ref[...].astype(f32)
+    product = term * weight[...].astype(f32)
+    rows, cols = product.shape
+    lanes = product[:, :HEAD]
+    for c in range(HEAD, cols, HEAD):
+        lanes = lanes + product[:, c : c + HEAD]
+    gain_grad[...] = jnp.sum(lanes.T, axis=0, keepdims=True)
+    gains = jnp.broadcast_to(gain[...].astype(f32), (8, rows)).T
+    weight_grad[0] = term * gains[:, :1]
+
+
+def last_part(near, weight, gain, sums):
+    shard, cols = weight.shape
+    many = len(sums)
+    tile = HEAD
+    tiles = shard // many // tile
+    outs = None
+    for h, came in enumerate(sums):
+        row = lambda i, h=h: h * tiles + i
+        specs = [
+            pl.BlockSpec((1, tile, cols), lambda i, row=row: (near.shape[0] - 1, row(i), 0)),
+            pl.BlockSpec((tile, cols), lambda i, row=row: (row(i), 0)),
+            pl.BlockSpec((1, tile), lambda i, row=row: (0, row(i))),
+        ]
+        specs += [pl.BlockSpec((tile, cols), lambda i: (i, 0))] * len(came)
+        operands = [near, weight, gain, *came]
+        if outs is not None:
+            specs += [pl.BlockSpec(memory_space=pl.ANY)] * 2
+        outs = pl.pallas_call(
+            functools.partial(last_kernel, len(came)),
+            grid=(tiles,),
+            in_specs=specs,
+            out_specs=[
+                pl.BlockSpec((1, tile, cols), lambda i, row=row: (0, row(i), 0)),
+                pl.BlockSpec((1, tile), lambda i, row=row: (0, row(i))),
+            ],
+            out_shape=[
+                jax.ShapeDtypeStruct((1, shard, cols), f32),
+                jax.ShapeDtypeStruct((1, shard), f32),
+            ],
+            input_output_aliases=(
+                {} if outs is None else {len(operands): 0, len(operands) + 1: 1}
+            ),
+            compiler_params=pltpu.CompilerParams(vmem_limit_bytes=16 * 2**20),
+            cost_estimate=pl.CostEstimate(
+                flops=shard // many * cols * 8,
+                bytes_accessed=shard // many * cols * 14,
+                transcendentals=0,
+            ),
+            name="sum_of_terms",
+        )(*operands, *(outs or ()))
+    return outs
+
+
 def second_kernel(plan, at, x, kv_grad, inv, cosine, sine, *refs):
     n = len(plan)
     blocks, refs = refs[:-10], refs[-10:]
@@ -257,7 +315,7 @@
     )(at, tokens_in, kv_grad, inv, cosine, sine, *blocks)
 
 
-def replica_sum(value):
+def replica_sum(value, other):
     replicas = lax.axis_size("replica")
     if replicas != 4:
         total = lax.psum(value, "replica")
@@ -269,17 +327,15 @@
     theirs = lax.dynamic_slice_in_dim(value, (1 - odd) * half, half, 0)
     came = swap(theirs, 1)
     mine = mine + came
-    mine = mine + swap(mine, 2)
+    mine = mine + after(swap(mine, 2), other)
     theirs = swap(mine, 1)
     low, high = jnp.where(odd == 0, mine, theirs), jnp.where(odd == 0, theirs, mine)
     return (low, high), came
 
 
 def exchange_ring(ring, own, far, near, pseudo):
-    total, came = replica_sum(pseudo)
-    cut = own[0].shape[0]
-    own = jnp.concatenate(own)
-    shard = own.shape[0]
+    total, _ = replica_sum(pseudo, far)
+    shard, cut = own.shape[0], own.shape[0] // 2
     blocks = [own]
     from_left = from_right = own
     for d in range(1, ring.half):
@@ -300,12 +356,12 @@
             from_right = jnp.pad(from_right, ((cut, 0), (0, 0)))
         from_left = ring.to_right((near[k] + from_left.astype(f32)).astype(bf16))
         from_right = ring.to_left((near[k + 1] + from_right.astype(f32)).astype(bf16))
-    term = near[-1] + from_left.astype(f32) + from_right.astype(f32)
-    return blocks, plan, jnp.zeros((1,), jnp.int32), term, total
+    sums = [(from_left, from_right)]
+    return blocks, plan, jnp.zeros((1,), jnp.int32), sums, total
 
 
 def exchange_plane(plane, own, far, near, pseudo):
-    shard = 2 * own[0].shape[0]
+    shard = own.shape[0]
     at0, at1, at2, at3 = plane.at
     zero = jnp.zeros((), f32)
     pieces = [(0, shard // 2), (shard // 2, shard)]
@@ -328,38 +384,40 @@
             crossed[0] = came[-1]
         return lax.optimization_barrier(came)
 
-    one = [links(*later(own[h], own[h])) for h in halves]
-    total, came = replica_sum(after(pseudo, sent[0]))
-    one[0], far, came = lax.optimization_barrier((one[0], far, came))
+    first = links(own, own)
+    total, came = replica_sum(after(pseudo, own), far)
+    first, far, came = lax.optimization_barrier((first, far, came))
+    one = [[part(came, h) for came in first] for h in halves]
     two = [links(*later(*one[h])) for h in halves]
     two[0], total = lax.optimization_barrier((two[0], total))
+    chords = [part(own, h) for h in halves] + [pick(at2, *one[h]) for h in halves] + [part(far, h) for h in halves]
+    chords += [part(pick(at1, near[1], near[0]).astype(bf16), h) for h in halves]
     three = []
     for h in halves:
         left, right = later(*two[h])
         terms = part(far, h)
-        three.append(links(pick(at0, terms, left), pick(at3, terms, right), own[h]))
+        three.append(links(pick(at0, terms, left), pick(at3, terms, right), chords[h]))
     four = []
     for h in halves:
-        left, right, _ = later(*three[h])
+        left, right = later(*three[h][:2])
         to_right = wide(part(near[0], h)) + pick(at1, wide(left), zero)
         to_left = wide(part(near[1], h)) + pick(at2, wide(right), zero)
         to_right = pick(at2, left, to_right.astype(bf16))
         to_left = pick(at1, right, to_left.astype(bf16))
-        four.append(links(to_right, to_left, pick(at2, *one[h])))
+        four.append(links(to_right, to_left, chords[2 + h]))
     five = []
     for h in halves:
-        left, right, _ = later(*four[h])
+        left, right = later(*four[h][:2])
         to_right = part(near[2], h) + pick(at3, zero, wide(left))
         to_left = part(near[3], h) + pick(at0, zero, wide(right))
-        five.append(links(to_right.astype(bf16), to_left.astype(bf16), part(far, h)))
+        five.append(links(to_right.astype(bf16), to_left.astype(bf16), chords[4 + h]))
     six = []
     for h in halves:
         left, right, chord = later(*five[h])
-        to_right = part(near[4], h) + wide(left) + pick(at1, wide(chord), zero)
-        to_left = part(near[5], h) + wide(right) + pick(at2, wide(chord), zero)
-        for_partner = part(pick(at1, near[1], near[0]).astype(bf16), h)
-        six.append(links(to_right.astype(bf16), to_left.astype(bf16), for_partner))
-    term = [part(near[6], h) + sum(wide(came) for came in six[h]) for h in halves]
+        chord = wide(chord)
+        to_right = part(near[4], h) + wide(left) + pick(at1, chord, zero)
+        to_left = part(near[5], h) + wide(right) + pick(at2, chord, zero)
+        six.append(links(to_right.astype(bf16), to_left.astype(bf16), chords[6 + h]))
 
     blocks, plan = [], []
 
@@ -370,10 +428,11 @@
             blocks.append(array)
         return entry
 
-    plan.append(add(None, own))
-    for step in (one, two):
-        for way in range(2):
-            plan.append(add(None, [step[h][way] for h in halves]))
+    for array in (own, *first):
+        plan.append([(None, len(blocks), 0, shard)])
+        blocks.append(array)
+    for way in range(2):
+        plan.append(add(None, [two[h][way] for h in halves]))
     partner = add(0, [three[h][2] for h in halves])
     for way in range(2):
         entry = [(way, *rest) for _, *rest in partner]
@@ -383,7 +442,7 @@
         plan[-1] += add(5 + way, [four[h][way] for h in halves])
     flags = [at1, at2, ~at1, ~at2, at1 | at2, at3, at0]
     plan = tuple(tuple(entry) for entry in plan)
-    return blocks, plan, jnp.stack(flags), jnp.concatenate(term), total
+    return blocks, plan, jnp.stack(flags), six, total
 
 
 def local(
@@ -405,11 +464,7 @@
     rows, width = tokens_in.shape
     shard, cols = weight_shard.shape
 
-    cut = shard // 2
-    own = [
-        (weight_shard[rows].astype(f32) * gain_shard[rows]).astype(bf16)
-        for rows in (slice(0, cut), slice(cut, shard))
-    ]
+    own = (weight_shard.astype(f32) * gain_shard).astype(bf16)
     positions = (ring.me * rows + jnp.arange(rows, dtype=jnp.int32)) % SEQ_LEN
     cosine, sine = rope_tables(positions)
     scale = 1.0 / math.sqrt(rows * ring.count)
@@ -417,9 +472,10 @@
         ring, tokens_in, cotangent, cosine, sine, shard, scale
     )
     exchange = exchange_plane if small else exchange_ring
-    blocks, plan, flags, term, total = exchange(ring, own, far, near, pseudo_grad[0])
-    weight_grad = term * gain_shard
-    gain_grad = jnp.sum(term * weight_shard.astype(f32), axis=1)
+    blocks, plan, flags, sums, total = exchange(
+        ring, own, far, near, pseudo_grad[0]
+    )
+    weight_grad, gain_grad = last_part(near, weight_shard, norm_gain, sums)
 
     if isinstance(total, tuple):
         total = jnp.concatenate(total)
@@ -436,8 +492,8 @@
     return (
         kv_out[None],
         input_grad[None],
-        weight_grad[None],
-        gain_grad[None],
+        weight_grad,
+        gain_grad,
         momentum_new,
         global_new,
         local_new[None],

time: 182 us -> 182 us (level)
  waiting for transfers between devices: 63.9 us -> 46.2 us
  starting transfers between devices: 45.4 us -> 53.1 us
  local copies, waits for them, and re-layouts: 3.88 us -> 11.5 us
  Pallas kernels: 29.2 us -> 32.4 us
    ppermute x3, waiting for transfers between devices: 16 us -> 0.18 us  [replica_sum(): lax.ppermute(v, 'replica', [(r, r ^ step) for r in range(4)])]
    ppermute x8, starting transfers between devices: 19.2 us -> 28.8 us  [over_chord(): return lax.ppermute(value, 'fsdp', [(2, 3), (3, 2), (4, 5), (5, 4)])]
    unnamed x52 -> x54, local copies, waits for them, and re-layouts: 1.81 us -> 9.15 us
    ppermute x12 -> x11, waiting for transfers between devices: 13.3 us -> 8.84 us  [to_right(): return lax.ppermute(value, 'fsdp', self.right)]
    convert_element_type x2 -> x4, other arithmetic: 4.49 us -> 8.55 us  [exchange_plane(): to_left.astype(bf16)]
    ppermute x12 -> x11, starting transfers between devices: 5.05 us -> 1.61 us  [to_left(): return lax.ppermute(value, 'fsdp', self.left)]
    convert_element_type x4 -> x2, other arithmetic: 7.9 us -> 4.84 us  [the longest x1 2.43 us: local(): own = (weight_shard.astype(f32) * gain_shard).astype(bf16)]
    pallas_call x0 -> x2, Pallas kernels: none -> 2.75 us  [last_part(): pl.pallas_call(functools.partial(last_kernel, len(came)), grid=(tiles,),...]
  transfers between devices with their start and end apart: 35 -> 33, of which waited for: 15 -> 14; matrix products, arithmetic and copies ran while one was open for 18% -> 18% of each run, Pallas kernels for 16% -> 17%
where the time goes in v8:
time: 182 us; the launch traced here: 181 us
  starting transfers between devices  53.1 us (29%)
  waiting for transfers between devices  46.2 us (25%)
  other arithmetic  36.5 us (20%)
  Pallas kernels  32.4 us (18%)
  local copies, waits for them, and re-layouts  11.5 us (6%)
    ppermute x8, starting transfers between devices, over_chord(): return lax.ppermute(value, 'fsdp', [(2, 3), (3, 2), (4, 5), (5, 4)])  28.8 us
    ppermute x8, waiting for transfers between devices, over_chord(): return lax.ppermute(value, 'fsdp', [(2, 3), (3, 2), (4, 5), (5, 4)])  27.8 us
    ppermute x11, starting transfers between devices, to_right(): return lax.ppermute(value, 'fsdp', self.right)  21.1 us
    pallas_call x1, Pallas kernels, second_part(): pl.pallas_call(functools.partial(second_kernel, plan), in_specs=[pl.Block...  17.8 us
    pallas_call x1, Pallas kernels, first_part(): pl.pallas_call(functools.partial(first_kernel, scale), grid_spec=pltpu.Pr...  11.9 us
    ppermute x11, waiting for transfers between devices, to_left(): return lax.ppermute(value, 'fsdp', self.left)  9.41 us
    unnamed x54, local copies, waits for them, and re-layouts  9.15 us
    ppermute x11, waiting for transfers between devices, to_right(): return lax.ppermute(value, 'fsdp', self.right)  8.84 us
  transfers between devices with their start and end apart: 33, of which 14 were waited for; matrix products, arithmetic and copies ran while one was open for 18% of the time, Pallas kernels for 17%

profile of v8, /device:TPU:8, one launch (start us, length us, event | category | flops | bytes accessed | tf_op | source)
XLA Modules:
  0.0 180.9 jit_solution(17887102105441095274)
XLA Ops:
  1.5 2.4 %multiply_convert_fusion.refs_0_ = bf16[512,1024]{1,0:T(8,128)(2,1)} fusion(f32[512]{0:T(512)S(1)} %bitcast.87, bf16[1,512,1024]{2,1,0:T(8,128)(2,1)} %param.12), kind=kLoop, calls=%fused_computation.1 | loop fusion | flops 1572864 | bytes 2099200 | tf_op jit(solution)/shard_map/convert_element_type | solution.py:467
  4.1 2.0 %collective-permute-start = (bf16[512,1024]{1,0:T(8,128)(2,1)}, bf16[512,1024]{1,0:T(8,128)(2,1)}, u32[]{:S(2)}, u32[]{:S(2)}) collective-permute-start(bf16[512,1024]{1,0:T(8,128)(2,1)} %multiply_convert_fusion.refs_0_), channel_id=1, source_target_pairs={{0,2},{2,4},{4,6},{6,7},{7,5},{5,3},{3,1},{1,0},{8,10},{10,12},{12... | collective-permute-start | bytes 3145736 | tf_op jit(solution)/shard_map/ppermute | solution.py:42
  7.3 1.5 collective-permute-start.5
  10.1 2.3 %copy-done.5 = bf16[1,512,4096]{2,1,0:T(8,128)(2,1)S(1)} copy-done((bf16[1,512,4096]{2,1,0:T(8,128)(2,1)S(1)}, bf16[1,512,4096]{2,1,0:T(8,128)(2,1)}, u32[]{:S(2)}) %copy-start.5) | copy-done | bytes 4194328
  12.4 11.9 %norm_and_weight_terms.1 = (bf16[512,1024]{1,0:T(8,128)(2,1)S(1)}, f32[512,128]{1,0:T(8,128)S(1)}, bf16[512,1024]{1,0:T(8,128)(2,1)S(1)}, f32[7,512,1024]{2,1,0:T(8,128)}) custom-call(s32[8]{0:T(128)S(1)} %compare_select_fusion.4.at, bf16[512,4096]{1,0:T(8,128)(2,1)S(1)} %bitcast.83, bf16[512,1024]{1,0:T(8,128)(2,1)S(1)} %bitcast.84, ...), custom_call_target="tpu_custom_call" | custom-call | flops 4294967296 | bytes 20971520 | tf_op jit(solution)/shard_map/norm_and_weight_terms/pallas_call | solution.py:115
  24.3 5.7 %collective-permute-done.1.refs_2_ = bf16[512,1024]{1,0:T(8,128)(2,1)} collective-permute-done((bf16[512,1024]{1,0:T(8,128)(2,1)}, bf16[512,1024]{1,0:T(8,128)(2,1)}, u32[]{:S(2)}, u32[]{:S(2)}) %collective-permute-start.1) | collective-permute-done | bytes 1048608 | tf_op jit(solution)/shard_map/ppermute | solution.py:45
  29.9 2.4 %add.151 = f32[192,1024]{1,0:T(8,128)} add(f32[192,1024]{1,0:T(8,128)} %dynamic-slice_add_fusion, f32[192,1024]{1,0:T(8,128)} %collective-permute-done.5) | non-fusion elementwise | flops 196608 | bytes 2359296 | tf_op jit(solution)/shard_map/add | solution.py:330
  32.3 3.2 %broadcast_select_fusion = (bf16[256,1024]{1,0:T(8,128)(2,1)}, bf16[256,1024]{1,0:T(8,128)(2,1)}, bf16[256,1024]{1,0:T(8,128)(2,1)}, bf16[256,1024]{1,0:T(8,128)...) fusion(pred[]{:T(512)} %eq.33, bf16[512,1024]{1,0:T(8,128)(2,1)} %collective-permute-done.1.refs_2_, ...), kind=kLoop, calls=%fused_computation.48 | loop fusion | flops 524288 | bytes 5242881 | tf_op jit(solution)/shard_map/jit(_where)/select_n | solution.py:393
  35.5 1.8 collective-permute-start.3
  37.6 2.1 %fusion.29 = (bf16[256,1024]{1,0:T(8,128)(2,1)}, bf16[256,1024]{1,0:T(8,128)(2,1)S(1)}) fusion(bf16[512,1024]{1,0:T(8,128)(2,1)} %multiply_convert_fusion.refs_0_), kind=kLoop, calls=%fused_computation.80 | loop fusion | bytes 2097152 | tf_op jit(solution)/shard_map/slice | solution.py:374
  39.8 1.7 collective-permute-start.7
  41.8 8.7 %collective-permute-done.3.refs_3_ = bf16[256,1024]{1,0:T(8,128)(2,1)S(1)} collective-permute-done((bf16[256,1024]{1,0:T(8,128)(2,1)}, bf16[256,1024]{1,0:T(8,128)(2,1)S(1)}, u32[]{:S(2)}, u32[]{:S(2)}) %collective-permute-start.3) | collective-permute-done | bytes 524320 | tf_op jit(solution)/shard_map/ppermute | solution.py:42
  50.5 1.8 collective-permute-done.4.refs_5_
  52.3 2.7 %broadcast_select_fusion.6 = (f32[192,1024]{1,0:T(8,128)}, f32[192,1024]{1,0:T(8,128)}) fusion(f32[192,1024]{1,0:T(8,128)} %collective-permute-done.6, f32[192,1024]{1,0:T(8,128)} %add.151, pred[]{:T(512)S(6)} %eq.36), kind=kLoop, calls=%fused_computation.54 | loop fusion | flops 393216 | bytes 3145729 | tf_op jit(solution)/shard_map/jit(_where)/select_n | solution.py:332
  55.0 1.4 fusion.28
  56.4 3.4 %collective-permute-start.11 = (bf16[256,1024]{1,0:T(8,128)(2,1)S(1)}, bf16[256,1024]{1,0:T(8,128)(2,1)S(1)}, u32[]{:S(2)}, u32[]{:S(2)}) collective-permute-start(bf16[256,1024]{1,0:T(8,128)(2,1)S(1)} %get-tuple-element.108), channel_id=1, source_target_pairs={{2,3},{3,2},{4,5},{5,4},{10,11},{11,10},{12,13},{13,12},{18,19},{1... | collective-permute-start | bytes 1572872 | tf_op jit(solution)/shard_map/ppermute | solution.py:54
  59.8 1.6 collective-permute-start.9
  64.2 6.7 %collective-permute-done.11.refs_7_ = bf16[256,1024]{1,0:T(8,128)(2,1)S(1)} collective-permute-done((bf16[256,1024]{1,0:T(8,128)(2,1)S(1)}, bf16[256,1024]{1,0:T(8,128)(2,1)S(1)}, u32[]{:S(2)}, u32[]{:S(2)}) %collective-permute-start.11) | collective-permute-done | bytes 524320 | tf_op jit(solution)/shard_map/ppermute | solution.py:54
  71.7 3.5 %collective-permute-start.14 = (bf16[256,1024]{1,0:T(8,128)(2,1)}, bf16[256,1024]{1,0:T(8,128)(2,1)}, u32[]{:S(2)}, u32[]{:S(2)}) collective-permute-start(bf16[256,1024]{1,0:T(8,128)(2,1)} %get-tuple-element.112), channel_id=1, source_target_pairs={{2,3},{3,2},{4,5},{5,4},{10,11},{11,10},{12,13},{13,12},{18,19},{1... | collective-permute-start | bytes 1572872 | tf_op jit(solution)/shard_map/ppermute | solution.py:54
  75.3 2.0 %collective-permute-start.12 = (bf16[256,1024]{1,0:T(8,128)(2,1)}, bf16[256,1024]{1,0:T(8,128)(2,1)S(1)}, u32[]{:S(2)}, u32[]{:S(2)}) collective-permute-start(bf16[256,1024]{1,0:T(8,128)(2,1)} %get-tuple-element.197), channel_id=1, source_target_pairs={{0,2},{2,4},{4,6},{6,7},{7,5},{5,3},{3,1},{1,0},{8,10},{10,12},{12... | collective-permute-start | bytes 1572872 | tf_op jit(solution)/shard_map/ppermute | solution.py:42
  77.3 3.7 %fusion.19 = (bf16[256,1024]{1,0:T(8,128)(2,1)}, bf16[256,1024]{1,0:T(8,128)(2,1)}) fusion(bf16[256,1024]{1,0:T(8,128)(2,1)} %collective-permute-done.10.refs_11_, f32[7,512,1024]{2,1,0:T(8,128)} %get-tuple-element.119.own, pred[]{:T(512)} %eq.32, pred[]{:T(512)} %eq.33, bf16[256,1024]{1,0:T(8,128)(2,1)} %collective-permute-done.9.refs_9_), kind=kLoop, calls=%fused_computation.41 | loop fusion | flops 2621440 | bytes 4194306 | tf_op jit(solution)/shard_map/jit(_where)/select_n | solution.py:406
  81.0 4.6 %collective-permute-done.14.refs_8_ = bf16[256,1024]{1,0:T(8,128)(2,1)} collective-permute-done((bf16[256,1024]{1,0:T(8,128)(2,1)}, bf16[256,1024]{1,0:T(8,128)(2,1)}, u32[]{:S(2)}, u32[]{:S(2)}) %collective-permute-start.14) | collective-permute-done | bytes 524320 | tf_op jit(solution)/shard_map/ppermute | solution.py:54
  85.6 3.8 %collective-permute-start.17 = (bf16[256,1024]{1,0:T(8,128)(2,1)S(1)}, bf16[256,1024]{1,0:T(8,128)(2,1)S(1)}, u32[]{:S(2)}, u32[]{:S(2)}) collective-permute-start(bf16[256,1024]{1,0:T(8,128)(2,1)S(1)} %copy-done.22), channel_id=1, source_target_pairs={{2,3},{3,2},{4,5},{5,4},{10,11},{11,10},{12,13},{13,12},{18,19},{1... | collective-permute-start | bytes 1572872 | tf_op jit(solution)/shard_map/ppermute | solution.py:54
  89.5 2.0 %collective-permute-start.15 = (bf16[256,1024]{1,0:T(8,128)(2,1)}, bf16[256,1024]{1,0:T(8,128)(2,1)}, u32[]{:S(2)}, u32[]{:S(2)}) collective-permute-start(bf16[256,1024]{1,0:T(8,128)(2,1)} %get-tuple-element.179), channel_id=1, source_target_pairs={{0,2},{2,4},{4,6},{6,7},{7,5},{5,3},{3,1},{1,0},{8,10},{10,12},{12... | collective-permute-start | bytes 1572872 | tf_op jit(solution)/shard_map/ppermute | solution.py:42
  91.5 2.9 %fusion.21 = (bf16[256,1024]{1,0:T(8,128)(2,1)}, bf16[256,1024]{1,0:T(8,128)(2,1)}) fusion(bf16[256,1024]{1,0:T(8,128)(2,1)S(1)} %collective-permute-done.13.refs_12_, f32[7,512,1024]{2,1,0:T(8,128)} %get-tuple-element.119.own, pred[]{:T(512)} %eq.32, pred[]{:T(512)} %eq.33, bf16[256,1024]{1,0:T(8,128)(2,1)S(1)} %collective-permute-done.12.refs_10_), kind=kLoop, calls=%fused_computation.43 | loop fusion | flops 2621440 | bytes 4194306 | tf_op jit(solution)/shard_map/jit(_where)/select_n | solution.py:406
  94.4 4.2 %collective-permute-done.17.refs_13_ = bf16[256,1024]{1,0:T(8,128)(2,1)S(1)} collective-permute-done((bf16[256,1024]{1,0:T(8,128)(2,1)S(1)}, bf16[256,1024]{1,0:T(8,128)(2,1)S(1)}, u32[]{:S(2)}, u32[]{:S(2)}) %collective-permute-start.17) | collective-permute-done | bytes 524320 | tf_op jit(solution)/shard_map/ppermute | solution.py:54
  99.4 3.6 %collective-permute-start.20 = (bf16[256,1024]{1,0:T(8,128)(2,1)}, bf16[256,1024]{1,0:T(8,128)(2,1)}, u32[]{:S(2)}, u32[]{:S(2)}) collective-permute-start(bf16[256,1024]{1,0:T(8,128)(2,1)} %get-tuple-element.125), channel_id=1, source_target_pairs={{2,3},{3,2},{4,5},{5,4},{10,11},{11,10},{12,13},{13,12},{18,19},{1... | collective-permute-start | bytes 1572872 | tf_op jit(solution)/shard_map/ppermute | solution.py:54
  103.3 2.0 %collective-permute-start.18 = (bf16[256,1024]{1,0:T(8,128)(2,1)}, bf16[256,1024]{1,0:T(8,128)(2,1)S(1)}, u32[]{:S(2)}, u32[]{:S(2)}) collective-permute-start(bf16[256,1024]{1,0:T(8,128)(2,1)} %get-tuple-element.177), channel_id=1, source_target_pairs={{0,2},{2,4},{4,6},{6,7},{7,5},{5,3},{3,1},{1,0},{8,10},{10,12},{12... | collective-permute-start | bytes 1572872 | tf_op jit(solution)/shard_map/ppermute | solution.py:42
  105.3 2.2 %fusion.11 = (bf16[256,1024]{1,0:T(8,128)(2,1)S(1)}, bf16[256,1024]{1,0:T(8,128)(2,1)S(1)}) fusion(bf16[256,1024]{1,0:T(8,128)(2,1)} %collective-permute-done.16.refs_17_, f32[7,512,1024]{2,1,0:T(8,128)} %get-tuple-element.119.own, pred[]{:T(512)} %eq.35, bf16[256,1024]{1,0:T(8,128)(2,1)} %collective-permute-done.15.refs_15_, pred[]{:T(512)} %eq.34), kind=kLoop, calls=%fused_computation.26 | loop fusion | flops 2097152 | bytes 4194306 | tf_op jit(solution)/shard_map/convert_element_type | solution.py:413
  107.5 4.2 %collective-permute-done.20.refs_14_ = bf16[256,1024]{1,0:T(8,128)(2,1)} collective-permute-done((bf16[256,1024]{1,0:T(8,128)(2,1)}, bf16[256,1024]{1,0:T(8,128)(2,1)}, u32[]{:S(2)}, u32[]{:S(2)}) %collective-permute-start.20) | collective-permute-done | bytes 524320 | tf_op jit(solution)/shard_map/ppermute | solution.py:54
  111.8 3.6 %collective-permute-start.23 = (bf16[256,1024]{1,0:T(8,128)(2,1)S(1)}, bf16[256,1024]{1,0:T(8,128)(2,1)S(1)}, u32[]{:S(2)}, u32[]{:S(2)}) collective-permute-start(bf16[256,1024]{1,0:T(8,128)(2,1)S(1)} %copy-done.21), channel_id=1, source_target_pairs={{2,3},{3,2},{4,5},{5,4},{10,11},{11,10},{12,13},{13,12},{18,19},{1... | collective-permute-start | bytes 1572872 | tf_op jit(solution)/shard_map/ppermute | solution.py:54
  115.4 2.4 %select_convert_fusion = bf16[1,512,1024]{2,1,0:T(8,128)(2,1)S(1)} fusion(f32[7,512,1024]{2,1,0:T(8,128)} %get-tuple-element.119.own, pred[]{:T(512)} %eq.32), kind=kLoop, calls=%fused_computation | loop fusion | flops 524288 | bytes 3145729 | tf_op jit(solution)/shard_map/convert_element_type | solution.py:394
  117.9 2.0 %collective-permute-start.25 = (bf16[256,1024]{1,0:T(8,128)(2,1)S(1)}, bf16[256,1024]{1,0:T(8,128)(2,1)S(1)}, u32[]{:S(2)}, u32[]{:S(2)}) collective-permute-start(bf16[256,1024]{1,0:T(8,128)(2,1)S(1)} %get-tuple-element.175), channel_id=1, source_target_pairs={{0,2},{2,4},{4,6},{6,7},{7,5},{5,3},{3,1},{1,0},{8,10},{10,12},{12... | collective-permute-start | bytes 1572872 | tf_op jit(solution)/shard_map/ppermute | solution.py:42
  119.9 2.3 %fusion.10 = (bf16[256,1024]{1,0:T(8,128)(2,1)S(1)}, bf16[256,1024]{1,0:T(8,128)(2,1)S(1)}) fusion(bf16[256,1024]{1,0:T(8,128)(2,1)S(1)} %collective-permute-done.19.refs_18_, f32[7,512,1024]{2,1,0:T(8,128)} %get-tuple-element.119.own, pred[]{:T(512)} %eq.35, bf16[256,1024]{1,0:T(8,128)(2,1)S(1)} %collective-permute-done.18.refs_16_, pred[]{:T(512)} %eq.34), kind=kLoop, calls=%fused_computation.24 | loop fusion | flops 2097152 | bytes 4194306 | tf_op jit(solution)/shard_map/convert_element_type | solution.py:413
  122.3 1.9 %collective-permute-done.23 = bf16[256,1024]{1,0:T(8,128)(2,1)S(1)} collective-permute-done((bf16[256,1024]{1,0:T(8,128)(2,1)S(1)}, bf16[256,1024]{1,0:T(8,128)(2,1)S(1)}, u32[]{:S(2)}, u32[]{:S(2)}) %collective-permute-start.23) | collective-permute-done | bytes 524320 | tf_op jit(solution)/shard_map/ppermute | solution.py:54
  124.2 3.6 %collective-permute-start.24 = (bf16[256,1024]{1,0:T(8,128)(2,1)S(1)}, bf16[256,1024]{1,0:T(8,128)(2,1)S(1)}, u32[]{:S(2)}, u32[]{:S(2)}) collective-permute-start(bf16[256,1024]{1,0:T(8,128)(2,1)S(1)} %copy-done.18), channel_id=1, source_target_pairs={{2,3},{3,2},{4,5},{5,4},{10,11},{11,10},{12,13},{13,12},{18,19},{1... | collective-permute-start | bytes 1572872 | tf_op jit(solution)/shard_map/ppermute | solution.py:54
  128.0 2.0 %collective-permute-start.21 = (bf16[256,1024]{1,0:T(8,128)(2,1)S(1)}, bf16[256,1024]{1,0:T(8,128)(2,1)S(1)}, u32[]{:S(2)}, u32[]{:S(2)}) collective-permute-start(bf16[256,1024]{1,0:T(8,128)(2,1)S(1)} %get-tuple-element.173), channel_id=1, source_target_pairs={{0,2},{2,4},{4,6},{6,7},{7,5},{5,3},{3,1},{1,0},{8,10},{10,12},{12... | collective-permute-start | bytes 1572872 | tf_op jit(solution)/shard_map/ppermute | solution.py:42
  130.9 2.0 %fusion.5 = (bf16[256,1024]{1,0:T(8,128)(2,1)S(1)}, bf16[256,1024]{1,0:T(8,128)(2,1)S(1)}) fusion(bf16[256,1024]{1,0:T(8,128)(2,1)S(1)} %collective-permute-done.23, bf16[256,1024]{1,0:T(8,128)(2,1)S(1)} %collective-permute-done.26, f32[7,512,1024]{2,1,0:T(8,128)} %get-tuple-element.119.own, pred[]{:T(512)} %eq.33, pred[]{:T(512)} %eq.32, ...), kind=kLoop, calls=%fused_computation.15 | loop fusion | flops 2883584 | bytes 4718594 | tf_op jit(solution)/shard_map/convert_element_type | solution.py:420
  132.9 4.3 %collective-permute-done.24 = bf16[256,1024]{1,0:T(8,128)(2,1)S(1)} collective-permute-done((bf16[256,1024]{1,0:T(8,128)(2,1)S(1)}, bf16[256,1024]{1,0:T(8,128)(2,1)S(1)}, u32[]{:S(2)}, u32[]{:S(2)}) %collective-permute-start.24) | collective-permute-done | bytes 524320 | tf_op jit(solution)/shard_map/ppermute | solution.py:54
  137.3 3.6 %collective-permute-start.29 = (bf16[256,1024]{1,0:T(8,128)(2,1)S(1)}, bf16[256,1024]{1,0:T(8,128)(2,1)S(1)}, u32[]{:S(2)}, u32[]{:S(2)}) collective-permute-start(bf16[256,1024]{1,0:T(8,128)(2,1)S(1)} %get-tuple-element.151), channel_id=1, source_target_pairs={{2,3},{3,2},{4,5},{5,4},{10,11},{11,10},{12,13},{13,12},{18,19},{1... | collective-permute-start | bytes 1572872 | tf_op jit(solution)/shard_map/ppermute | solution.py:54
  140.9 2.5 %fusion.22 = (bf16[1,384,1024]{2,1,0:T(8,128)(2,1)}, f32[384,1024]{1,0:T(8,128)}, f32[384,1024]{1,0:T(8,128)}) fusion(bf16[1,384,1024]{2,1,0:T(8,128)(2,1)S(1)} %copy-done.17, f32[384,1024]{1,0:T(8,128)S(1)} %copy-done.14, f32[192,1024]{1,0:T(8,128)S(1)} %copy-done.12, f32[192,1024]{1,0:T(8,128)S(1)} %copy-done.13, f32[384,1024]{1,0:T(8,128)S(1)} %copy-done.15), kind=kLoop, calls=%fused_computation.44 | loop fusion | flops 4718592 | bytes 9437184 | tf_op jit(solution)/shard_map/broadcast_in_dim | solution.py:499
  143.5 2.0 %collective-permute-start.31 = (bf16[256,1024]{1,0:T(8,128)(2,1)S(1)}, bf16[256,1024]{1,0:T(8,128)(2,1)S(1)}, u32[]{:S(2)}, u32[]{:S(2)}) collective-permute-start(bf16[256,1024]{1,0:T(8,128)(2,1)S(1)} %get-tuple-element.171), channel_id=1, source_target_pairs={{0,2},{2,4},{4,6},{6,7},{7,5},{5,3},{3,1},{1,0},{8,10},{10,12},{12... | collective-permute-start | bytes 1572872 | tf_op jit(solution)/shard_map/ppermute | solution.py:42
  145.5 2.0 %fusion.9 = (bf16[256,1024]{1,0:T(8,128)(2,1)S(1)}, bf16[256,1024]{1,0:T(8,128)(2,1)S(1)}) fusion(bf16[256,1024]{1,0:T(8,128)(2,1)S(1)} %collective-permute-done.24, bf16[256,1024]{1,0:T(8,128)(2,1)S(1)} %collective-permute-done.22, f32[7,512,1024]{2,1,0:T(8,128)} %get-tuple-element.119.own, pred[]{:T(512)} %eq.33, pred[]{:T(512)} %eq.32, ...), kind=kLoop, calls=%fused_computation.19 | loop fusion | flops 2883584 | bytes 4718594 | tf_op jit(solution)/shard_map/convert_element_type | solution.py:420
  147.8 1.8 collective-permute-start.27
  149.6 1.8 %collective-permute-done.29.refs_2_ = bf16[256,1024]{1,0:T(8,128)(2,1)S(1)} collective-permute-done((bf16[256,1024]{1,0:T(8,128)(2,1)S(1)}, bf16[256,1024]{1,0:T(8,128)(2,1)S(1)}, u32[]{:S(2)}, u32[]{:S(2)}) %collective-permute-start.29) | collective-permute-done | bytes 524320 | tf_op jit(solution)/shard_map/ppermute | solution.py:54
  151.4 3.6 %collective-permute-start.30 = (bf16[256,1024]{1,0:T(8,128)(2,1)S(1)}, bf16[256,1024]{1,0:T(8,128)(2,1)S(1)}, u32[]{:S(2)}, u32[]{:S(2)}) collective-permute-start(bf16[256,1024]{1,0:T(8,128)(2,1)S(1)} %get-tuple-element.152), channel_id=1, source_target_pairs={{2,3},{3,2},{4,5},{5,4},{10,11},{11,10},{12,13},{13,12},{18,19},{1... | collective-permute-start | bytes 1572872 | tf_op jit(solution)/shard_map/ppermute | solution.py:54
  155.1 17.8 %project_and_input_grad.1 = (bf16[512,1024]{1,0:T(8,128)(2,1)}, bf16[512,4096]{1,0:T(8,128)(2,1)}) custom-call(s32[15]{0:T(128)S(1)} %pad_add_fusion.at, bf16[512,4096]{1,0:T(8,128)(2,1)} %bitcast.82, bf16[512,1024]{1,0:T(8,128)(2,1)} %copy-done.9, f32[512,128]{1,0:T(8,128)S(1)} %copy-done.11, f32[512,128]{1,0:T(8,128)S(1)} %get-tuple-element.201.cosine, ...), custom_call_target="tpu_custom_call" | custom-call | flops 8589934592 | bytes 16777216 | tf_op jit(solution)/shard_map/project_and_input_grad/pallas_call | solution.py:288
  173.0 5.2 %copy-done = f32[7,512,1024]{2,1,0:T(8,128)S(1)} copy-done((f32[7,512,1024]{2,1,0:T(8,128)S(1)}, f32[7,512,1024]{2,1,0:T(8,128)}, u32[]{:S(2)}) %copy-start) | copy-done | bytes 14680088
  (104 shorter events, 12.8 us)
Async XLA Ops:
  4.0 2.4 %collective-permute-start.2 = (f32[192,1024]{1,0:T(8,128)S(1)}, f32[192,1024]{1,0:T(8,128)S(1)}, u32[]{:S(2)}, u32[]{:S(2)}) collective-permute-start(f32[192,1024]{1,0:T(8,128)S(1)} %constant_dynamic-slice_fusion), channel_id=1, source_target_pairs={{0,8},{8,0},{16,24},{24,16},{1,9},{9,1},{17,25},{25,17},{2,10},{10... | collective-permute-start | bytes 2359304 | tf_op jit(solution)/shard_map/ppermute | solution.py:323
  4.1 25.9 %collective-permute-start.1 = (bf16[512,1024]{1,0:T(8,128)(2,1)}, bf16[512,1024]{1,0:T(8,128)(2,1)}, u32[]{:S(2)}, u32[]{:S(2)}) collective-permute-start(bf16[512,1024]{1,0:T(8,128)(2,1)} %multiply_convert_fusion.refs_0_), channel_id=1, source_target_pairs={{2,0},{4,2},{6,4},{7,6},{5,7},{3,5},{1,3},{0,1},{10,8},{12,10},{14... | collective-permute-start | bytes 3145736 | tf_op jit(solution)/shard_map/ppermute | solution.py:45
  4.1 25.8 %collective-permute-start = (bf16[512,1024]{1,0:T(8,128)(2,1)}, bf16[512,1024]{1,0:T(8,128)(2,1)}, u32[]{:S(2)}, u32[]{:S(2)}) collective-permute-start(bf16[512,1024]{1,0:T(8,128)(2,1)} %multiply_convert_fusion.refs_0_), channel_id=1, source_target_pairs={{0,2},{2,4},{4,6},{6,7},{7,5},{5,3},{3,1},{1,0},{8,10},{10,12},{12... | collective-permute-start | bytes 3145736 | tf_op jit(solution)/shard_map/ppermute | solution.py:42
  7.3 22.6 %collective-permute-start.5 = (f32[192,1024]{1,0:T(8,128)}, f32[192,1024]{1,0:T(8,128)}, u32[]{:S(2)}, u32[]{:S(2)}) collective-permute-start(f32[192,1024]{1,0:T(8,128)} %dynamic-slice_add_fusion), channel_id=1, source_target_pairs={{0,16},{8,24},{16,0},{24,8},{1,17},{9,25},{17,1},{25,9},{2,18},{10... | collective-permute-start | bytes 2359304 | tf_op jit(solution)/shard_map/ppermute | solution.py:323
  10.1 14.2 %copy-start.2 = (f32[512,128]{1,0:T(8,128)}, f32[512,128]{1,0:T(8,128)S(1)}, u32[]{:S(2)}) copy-start(f32[512,128]{1,0:T(8,128)S(1)} %get-tuple-element.202.sine) | copy-start | bytes 786436
  24.2 11.3 %copy-start.9 = (bf16[512,1024]{1,0:T(8,128)(2,1)}, bf16[512,1024]{1,0:T(8,128)(2,1)S(1)}, u32[]{:S(2)}) copy-start(bf16[512,1024]{1,0:T(8,128)(2,1)S(1)} %get-tuple-element.86.kv_grad) | copy-start | bytes 3145732
  24.3 11.3 %copy-start.10 = (f32[512,128]{1,0:T(8,128)}, f32[512,128]{1,0:T(8,128)S(1)}, u32[]{:S(2)}) copy-start(f32[512,128]{1,0:T(8,128)S(1)} %get-tuple-element.87.inv) | copy-start | bytes 786436
  32.3 20.0 %collective-permute-start.6 = (f32[192,1024]{1,0:T(8,128)}, f32[192,1024]{1,0:T(8,128)}, u32[]{:S(2)}, u32[]{:S(2)}) collective-permute-start(f32[192,1024]{1,0:T(8,128)} %add.151), channel_id=1, source_target_pairs={{0,8},{8,0},{16,24},{24,16},{1,9},{9,1},{17,25},{25,17},{2,10},{10... | collective-permute-start | bytes 2359304 | tf_op jit(solution)/shard_map/ppermute | solution.py:323
  35.5 15.0 %collective-permute-start.3 = (bf16[256,1024]{1,0:T(8,128)(2,1)}, bf16[256,1024]{1,0:T(8,128)(2,1)S(1)}, u32[]{:S(2)}, u32[]{:S(2)}) collective-permute-start(bf16[256,1024]{1,0:T(8,128)(2,1)} %get-tuple-element.94), channel_id=1, source_target_pairs={{0,2},{2,4},{4,6},{6,7},{7,5},{5,3},{3,1},{1,0},{8,10},{10,12},{12... | collective-permute-start | bytes 1572872 | tf_op jit(solution)/shard_map/ppermute | solution.py:42
  37.3 15.0 %collective-permute-start.4 = (bf16[256,1024]{1,0:T(8,128)(2,1)}, bf16[256,1024]{1,0:T(8,128)(2,1)S(1)}, u32[]{:S(2)}, u32[]{:S(2)}) collective-permute-start(bf16[256,1024]{1,0:T(8,128)(2,1)} %get-tuple-element.95), channel_id=1, source_target_pairs={{2,0},{4,2},{6,4},{7,6},{5,7},{3,5},{1,3},{0,1},{10,8},{12,10},{14... | collective-permute-start | bytes 1572872 | tf_op jit(solution)/shard_map/ppermute | solution.py:45
  39.8 22.2 %collective-permute-start.7 = (bf16[256,1024]{1,0:T(8,128)(2,1)}, bf16[256,1024]{1,0:T(8,128)(2,1)S(1)}, u32[]{:S(2)}, u32[]{:S(2)}) collective-permute-start(bf16[256,1024]{1,0:T(8,128)(2,1)} %get-tuple-element.100), channel_id=1, source_target_pairs={{0,2},{2,4},{4,6},{6,7},{7,5},{5,3},{3,1},{1,0},{8,10},{10,12},{12... | collective-permute-start | bytes 1572872 | tf_op jit(solution)/shard_map/ppermute | solution.py:42
  41.5 21.6 %collective-permute-start.8 = (bf16[256,1024]{1,0:T(8,128)(2,1)S(1)}, bf16[256,1024]{1,0:T(8,128)(2,1)S(1)}, u32[]{:S(2)}, u32[]{:S(2)}) collective-permute-start(bf16[256,1024]{1,0:T(8,128)(2,1)S(1)} %copy-done.23), channel_id=1, source_target_pairs={{2,0},{4,2},{6,4},{7,6},{5,7},{3,5},{1,3},{0,1},{10,8},{12,10},{14... | collective-permute-start | bytes 1572872 | tf_op jit(solution)/shard_map/ppermute | solution.py:45
  56.4 14.4 %collective-permute-start.11 = (bf16[256,1024]{1,0:T(8,128)(2,1)S(1)}, bf16[256,1024]{1,0:T(8,128)(2,1)S(1)}, u32[]{:S(2)}, u32[]{:S(2)}) collective-permute-start(bf16[256,1024]{1,0:T(8,128)(2,1)S(1)} %get-tuple-element.108), channel_id=1, source_target_pairs={{2,3},{3,2},{4,5},{5,4},{10,11},{11,10},{12,13},{13,12},{18,19},{1... | collective-permute-start | bytes 1572872 | tf_op jit(solution)/shard_map/ppermute | solution.py:54
  59.8 17.5 %collective-permute-start.9 = (bf16[256,1024]{1,0:T(8,128)(2,1)}, bf16[256,1024]{1,0:T(8,128)(2,1)}, u32[]{:S(2)}, u32[]{:S(2)}) collective-permute-start(bf16[256,1024]{1,0:T(8,128)(2,1)} %get-tuple-element.187), channel_id=1, source_target_pairs={{0,2},{2,4},{4,6},{6,7},{7,5},{5,3},{3,1},{1,0},{8,10},{10,12},{12... | collective-permute-start | bytes 1572872 | tf_op jit(solution)/shard_map/ppermute | solution.py:42
  61.5 15.8 %collective-permute-start.10 = (bf16[256,1024]{1,0:T(8,128)(2,1)}, bf16[256,1024]{1,0:T(8,128)(2,1)}, u32[]{:S(2)}, u32[]{:S(2)}) collective-permute-start(bf16[256,1024]{1,0:T(8,128)(2,1)} %get-tuple-element.188), channel_id=1, source_target_pairs={{2,0},{4,2},{6,4},{7,6},{5,7},{3,5},{1,3},{0,1},{10,8},{12,10},{14... | collective-permute-start | bytes 1572872 | tf_op jit(solution)/shard_map/ppermute | solution.py:45
  71.7 14.0 %collective-permute-start.14 = (bf16[256,1024]{1,0:T(8,128)(2,1)}, bf16[256,1024]{1,0:T(8,128)(2,1)}, u32[]{:S(2)}, u32[]{:S(2)}) collective-permute-start(bf16[256,1024]{1,0:T(8,128)(2,1)} %get-tuple-element.112), channel_id=1, source_target_pairs={{2,3},{3,2},{4,5},{5,4},{10,11},{11,10},{12,13},{13,12},{18,19},{1... | collective-permute-start | bytes 1572872 | tf_op jit(solution)/shard_map/ppermute | solution.py:54
  75.2 16.3 %collective-permute-start.13 = (bf16[256,1024]{1,0:T(8,128)(2,1)}, bf16[256,1024]{1,0:T(8,128)(2,1)S(1)}, u32[]{:S(2)}, u32[]{:S(2)}) collective-permute-start(bf16[256,1024]{1,0:T(8,128)(2,1)} %get-tuple-element.196), channel_id=1, source_target_pairs={{2,0},{4,2},{6,4},{7,6},{5,7},{3,5},{1,3},{0,1},{10,8},{12,10},{14... | collective-permute-start | bytes 1572872 | tf_op jit(solution)/shard_map/ppermute | solution.py:45
  75.3 16.2 %collective-permute-start.12 = (bf16[256,1024]{1,0:T(8,128)(2,1)}, bf16[256,1024]{1,0:T(8,128)(2,1)S(1)}, u32[]{:S(2)}, u32[]{:S(2)}) collective-permute-start(bf16[256,1024]{1,0:T(8,128)(2,1)} %get-tuple-element.197), channel_id=1, source_target_pairs={{0,2},{2,4},{4,6},{6,7},{7,5},{5,3},{3,1},{1,0},{8,10},{10,12},{12... | collective-permute-start | bytes 1572872 | tf_op jit(solution)/shard_map/ppermute | solution.py:42
  85.6 17.4 %copy-start.25 = (s32[8]{0:T(128)S(1)}, s32[8]{0:T(128)}, u32[]{:S(2)}) copy-start(s32[8]{0:T(128)} %constant.119.clone) | copy-start | bytes 100
  85.6 13.0 %collective-permute-start.17 = (bf16[256,1024]{1,0:T(8,128)(2,1)S(1)}, bf16[256,1024]{1,0:T(8,128)(2,1)S(1)}, u32[]{:S(2)}, u32[]{:S(2)}) collective-permute-start(bf16[256,1024]{1,0:T(8,128)(2,1)S(1)} %copy-done.22), channel_id=1, source_target_pairs={{2,3},{3,2},{4,5},{5,4},{10,11},{11,10},{12,13},{13,12},{18,19},{1... | collective-permute-start | bytes 1572872 | tf_op jit(solution)/shard_map/ppermute | solution.py:54
  89.4 15.9 %collective-permute-start.16 = (bf16[256,1024]{1,0:T(8,128)(2,1)}, bf16[256,1024]{1,0:T(8,128)(2,1)}, u32[]{:S(2)}, u32[]{:S(2)}) collective-permute-start(bf16[256,1024]{1,0:T(8,128)(2,1)} %get-tuple-element.178), channel_id=1, source_target_pairs={{2,0},{4,2},{6,4},{7,6},{5,7},{3,5},{1,3},{0,1},{10,8},{12,10},{14... | collective-permute-start | bytes 1572872 | tf_op jit(solution)/shard_map/ppermute | solution.py:45
  89.5 15.9 %collective-permute-start.15 = (bf16[256,1024]{1,0:T(8,128)(2,1)}, bf16[256,1024]{1,0:T(8,128)(2,1)}, u32[]{:S(2)}, u32[]{:S(2)}) collective-permute-start(bf16[256,1024]{1,0:T(8,128)(2,1)} %get-tuple-element.179), channel_id=1, source_target_pairs={{0,2},{2,4},{4,6},{6,7},{7,5},{5,3},{3,1},{1,0},{8,10},{10,12},{12... | collective-permute-start | bytes 1572872 | tf_op jit(solution)/shard_map/ppermute | solution.py:42
  99.4 12.3 %collective-permute-start.20 = (bf16[256,1024]{1,0:T(8,128)(2,1)}, bf16[256,1024]{1,0:T(8,128)(2,1)}, u32[]{:S(2)}, u32[]{:S(2)}) collective-permute-start(bf16[256,1024]{1,0:T(8,128)(2,1)} %get-tuple-element.125), channel_id=1, source_target_pairs={{2,3},{3,2},{4,5},{5,4},{10,11},{11,10},{12,13},{13,12},{18,19},{1... | collective-permute-start | bytes 1572872 | tf_op jit(solution)/shard_map/ppermute | solution.py:54
  103.3 8.5 %copy-start.21 = (bf16[256,1024]{1,0:T(8,128)(2,1)S(1)}, bf16[256,1024]{1,0:T(8,128)(2,1)}, u32[]{:S(2)}) copy-start(bf16[256,1024]{1,0:T(8,128)(2,1)} %get-tuple-element.137) | copy-start | bytes 1572868
  103.3 16.6 %collective-permute-start.19 = (bf16[256,1024]{1,0:T(8,128)(2,1)}, bf16[256,1024]{1,0:T(8,128)(2,1)S(1)}, u32[]{:S(2)}, u32[]{:S(2)}) collective-permute-start(bf16[256,1024]{1,0:T(8,128)(2,1)} %get-tuple-element.176), channel_id=1, source_target_pairs={{2,0},{4,2},{6,4},{7,6},{5,7},{3,5},{1,3},{0,1},{10,8},{12,10},{14... | collective-permute-start | bytes 1572872 | tf_op jit(solution)/shard_map/ppermute | solution.py:45
  103.3 16.6 %collective-permute-start.18 = (bf16[256,1024]{1,0:T(8,128)(2,1)}, bf16[256,1024]{1,0:T(8,128)(2,1)S(1)}, u32[]{:S(2)}, u32[]{:S(2)}) collective-permute-start(bf16[256,1024]{1,0:T(8,128)(2,1)} %get-tuple-element.177), channel_id=1, source_target_pairs={{0,2},{2,4},{4,6},{6,7},{7,5},{5,3},{3,1},{1,0},{8,10},{10,12},{12... | collective-permute-start | bytes 1572872 | tf_op jit(solution)/shard_map/ppermute | solution.py:42
  111.8 12.4 %collective-permute-start.23 = (bf16[256,1024]{1,0:T(8,128)(2,1)S(1)}, bf16[256,1024]{1,0:T(8,128)(2,1)S(1)}, u32[]{:S(2)}, u32[]{:S(2)}) collective-permute-start(bf16[256,1024]{1,0:T(8,128)(2,1)S(1)} %copy-done.21), channel_id=1, source_target_pairs={{2,3},{3,2},{4,5},{5,4},{10,11},{11,10},{12,13},{13,12},{18,19},{1... | collective-permute-start | bytes 1572872 | tf_op jit(solution)/shard_map/ppermute | solution.py:54
  117.8 13.0 %collective-permute-start.26 = (bf16[256,1024]{1,0:T(8,128)(2,1)S(1)}, bf16[256,1024]{1,0:T(8,128)(2,1)S(1)}, u32[]{:S(2)}, u32[]{:S(2)}) collective-permute-start(bf16[256,1024]{1,0:T(8,128)(2,1)S(1)} %get-tuple-element.174), channel_id=1, source_target_pairs={{2,0},{4,2},{6,4},{7,6},{5,7},{3,5},{1,3},{0,1},{10,8},{12,10},{14... | collective-permute-start | bytes 1572872 | tf_op jit(solution)/shard_map/ppermute | solution.py:45
  117.9 13.0 %collective-permute-start.25 = (bf16[256,1024]{1,0:T(8,128)(2,1)S(1)}, bf16[256,1024]{1,0:T(8,128)(2,1)S(1)}, u32[]{:S(2)}, u32[]{:S(2)}) collective-permute-start(bf16[256,1024]{1,0:T(8,128)(2,1)S(1)} %get-tuple-element.175), channel_id=1, source_target_pairs={{0,2},{2,4},{4,6},{6,7},{7,5},{5,3},{3,1},{1,0},{8,10},{10,12},{12... | collective-permute-start | bytes 1572872 | tf_op jit(solution)/shard_map/ppermute | solution.py:42
  124.2 13.1 %collective-permute-start.24 = (bf16[256,1024]{1,0:T(8,128)(2,1)S(1)}, bf16[256,1024]{1,0:T(8,128)(2,1)S(1)}, u32[]{:S(2)}, u32[]{:S(2)}) collective-permute-start(bf16[256,1024]{1,0:T(8,128)(2,1)S(1)} %copy-done.18), channel_id=1, source_target_pairs={{2,3},{3,2},{4,5},{5,4},{10,11},{11,10},{12,13},{13,12},{18,19},{1... | collective-permute-start | bytes 1572872 | tf_op jit(solution)/shard_map/ppermute | solution.py:54
  127.8 13.1 %copy-start.17 = (bf16[1,384,1024]{2,1,0:T(8,128)(2,1)S(1)}, bf16[1,384,1024]{2,1,0:T(8,128)(2,1)}, u32[]{:S(2)}) copy-start(bf16[1,384,1024]{2,1,0:T(8,128)(2,1)} %param.17) | copy-start | bytes 2359300
  127.9 13.0 %copy-start.12 = (f32[192,1024]{1,0:T(8,128)S(1)}, f32[192,1024]{1,0:T(8,128)}, u32[]{:S(2)}) copy-start(f32[192,1024]{1,0:T(8,128)} %get-tuple-element.164) | copy-start | bytes 2359300
  127.9 13.0 %copy-start.13 = (f32[192,1024]{1,0:T(8,128)S(1)}, f32[192,1024]{1,0:T(8,128)}, u32[]{:S(2)}) copy-start(f32[192,1024]{1,0:T(8,128)} %get-tuple-element.163) | copy-start | bytes 2359300
  127.9 13.0 %copy-start.14 = (f32[384,1024]{1,0:T(8,128)S(1)}, f32[384,1024]{1,0:T(8,128)}, u32[]{:S(2)}) copy-start(f32[384,1024]{1,0:T(8,128)} %param.16) | copy-start | bytes 4718596
  127.9 13.0 %copy-start.15 = (f32[384,1024]{1,0:T(8,128)S(1)}, f32[384,1024]{1,0:T(8,128)}, u32[]{:S(2)}) copy-start(f32[384,1024]{1,0:T(8,128)} %param.15) | copy-start | bytes 4718596
  127.9 17.6 %collective-permute-start.22 = (bf16[256,1024]{1,0:T(8,128)(2,1)S(1)}, bf16[256,1024]{1,0:T(8,128)(2,1)S(1)}, u32[]{:S(2)}, u32[]{:S(2)}) collective-permute-start(bf16[256,1024]{1,0:T(8,128)(2,1)S(1)} %get-tuple-element.172), channel_id=1, source_target_pairs={{2,0},{4,2},{6,4},{7,6},{5,7},{3,5},{1,3},{0,1},{10,8},{12,10},{14... | collective-permute-start | bytes 1572872 | tf_op jit(solution)/shard_map/ppermute | solution.py:45
  128.0 17.5 %collective-permute-start.21 = (bf16[256,1024]{1,0:T(8,128)(2,1)S(1)}, bf16[256,1024]{1,0:T(8,128)(2,1)S(1)}, u32[]{:S(2)}, u32[]{:S(2)}) collective-permute-start(bf16[256,1024]{1,0:T(8,128)(2,1)S(1)} %get-tuple-element.173), channel_id=1, source_target_pairs={{0,2},{2,4},{4,6},{6,7},{7,5},{5,3},{3,1},{1,0},{8,10},{10,12},{12... | collective-permute-start | bytes 1572872 | tf_op jit(solution)/shard_map/ppermute | solution.py:42
  137.3 14.2 %collective-permute-start.29 = (bf16[256,1024]{1,0:T(8,128)(2,1)S(1)}, bf16[256,1024]{1,0:T(8,128)(2,1)S(1)}, u32[]{:S(2)}, u32[]{:S(2)}) collective-permute-start(bf16[256,1024]{1,0:T(8,128)(2,1)S(1)} %get-tuple-element.151), channel_id=1, source_target_pairs={{2,3},{3,2},{4,5},{5,4},{10,11},{11,10},{12,13},{13,12},{18,19},{1... | collective-permute-start | bytes 1572872 | tf_op jit(solution)/shard_map/ppermute | solution.py:54
  143.4 11.6 %copy-start.3 = (f32[512,128]{1,0:T(8,128)S(1)}, f32[512,128]{1,0:T(8,128)}, u32[]{:S(2)}) copy-start(f32[512,128]{1,0:T(8,128)} %copy-done.2) | copy-start | bytes 786436
  143.5 11.6 %copy-start.8 = (bf16[256,1024]{1,0:T(8,128)(2,1)S(1)}, bf16[256,1024]{1,0:T(8,128)(2,1)}, u32[]{:S(2)}) copy-start(bf16[256,1024]{1,0:T(8,128)(2,1)} %copy-done.7) | copy-start | bytes 1572868
  143.5 11.6 %copy-start.11 = (f32[512,128]{1,0:T(8,128)S(1)}, f32[512,128]{1,0:T(8,128)}, u32[]{:S(2)}) copy-start(f32[512,128]{1,0:T(8,128)} %copy-done.10) | copy-start | bytes 786436
  143.5 29.5 %collective-permute-start.32 = (bf16[256,1024]{1,0:T(8,128)(2,1)S(1)}, bf16[256,1024]{1,0:T(8,128)(2,1)S(1)}, u32[]{:S(2)}, u32[]{:S(2)}) collective-permute-start(bf16[256,1024]{1,0:T(8,128)(2,1)S(1)} %get-tuple-element.170), channel_id=1, source_target_pairs={{2,0},{4,2},{6,4},{7,6},{5,7},{3,5},{1,3},{0,1},{10,8},{12,10},{14... | collective-permute-start | bytes 1572872 | tf_op jit(solution)/shard_map/ppermute | solution.py:45
  143.5 29.5 %collective-permute-start.31 = (bf16[256,1024]{1,0:T(8,128)(2,1)S(1)}, bf16[256,1024]{1,0:T(8,128)(2,1)S(1)}, u32[]{:S(2)}, u32[]{:S(2)}) collective-permute-start(bf16[256,1024]{1,0:T(8,128)(2,1)S(1)} %get-tuple-element.171), channel_id=1, source_target_pairs={{0,2},{2,4},{4,6},{6,7},{7,5},{5,3},{3,1},{1,0},{8,10},{10,12},{12... | collective-permute-start | bytes 1572872 | tf_op jit(solution)/shard_map/ppermute | solution.py:42
  147.5 32.0 %collective-permute-start.28 = (bf16[256,1024]{1,0:T(8,128)(2,1)S(1)}, bf16[256,1024]{1,0:T(8,128)(2,1)S(1)}, u32[]{:S(2)}, u32[]{:S(2)}) collective-permute-start(bf16[256,1024]{1,0:T(8,128)(2,1)S(1)} %get-tuple-element.168), channel_id=1, source_target_pairs={{2,0},{4,2},{6,4},{7,6},{5,7},{3,5},{1,3},{0,1},{10,8},{12,10},{14... | collective-permute-start | bytes 1572872 | tf_op jit(solution)/shard_map/ppermute | solution.py:45
  147.8 31.7 %collective-permute-start.27 = (bf16[256,1024]{1,0:T(8,128)(2,1)S(1)}, bf16[256,1024]{1,0:T(8,128)(2,1)S(1)}, u32[]{:S(2)}, u32[]{:S(2)}) collective-permute-start(bf16[256,1024]{1,0:T(8,128)(2,1)S(1)} %get-tuple-element.169), channel_id=1, source_target_pairs={{0,2},{2,4},{4,6},{6,7},{7,5},{5,3},{3,1},{1,0},{8,10},{10,12},{12... | collective-permute-start | bytes 1572872 | tf_op jit(solution)/shard_map/ppermute | solution.py:42
  151.4 28.1 %collective-permute-start.30 = (bf16[256,1024]{1,0:T(8,128)(2,1)S(1)}, bf16[256,1024]{1,0:T(8,128)(2,1)S(1)}, u32[]{:S(2)}, u32[]{:S(2)}) collective-permute-start(bf16[256,1024]{1,0:T(8,128)(2,1)S(1)} %get-tuple-element.152), channel_id=1, source_target_pairs={{2,3},{3,2},{4,5},{5,4},{10,11},{11,10},{12,13},{13,12},{18,19},{1... | collective-permute-start | bytes 1572872 | tf_op jit(solution)/shard_map/ppermute | solution.py:54
  155.1 17.8 %copy-start.1 = (bf16[1,512,1024]{2,1,0:T(8,128)(2,1)S(1)}, bf16[1,512,1024]{2,1,0:T(8,128)(2,1)}, u32[]{:S(2)}) copy-start(bf16[1,512,1024]{2,1,0:T(8,128)(2,1)} %param.12) | copy-start | bytes 3145732
  155.1 17.8 %copy-start.4 = (bf16[1,512]{1,0:T(2,128)(2,1)S(1)}, bf16[1,512]{1,0:T(2,128)(2,1)}, u32[]{:S(2)}) copy-start(bf16[1,512]{1,0:T(2,128)(2,1)} %gain.3) | copy-start | bytes 3076
  (12 other events, 41.1 us)

commit v9 on v8

--- a/solution.py
+++ b/solution.py
@@ -315,26 +315,22 @@
     )(at, tokens_in, kv_grad, inv, cosine, sine, *blocks)
 
 
-def replica_sum(value, other):
-    replicas = lax.axis_size("replica")
-    if replicas != 4:
-        total = lax.psum(value, "replica")
-        return total, total
+def replica_pairs(value, odd):
     swap = lambda v, step: lax.ppermute(v, "replica", [(r, r ^ step) for r in range(4)])
-    odd = lax.axis_index("replica") % 2
     half = value.shape[0] // 2
     mine = lax.dynamic_slice_in_dim(value, odd * half, half, 0)
     theirs = lax.dynamic_slice_in_dim(value, (1 - odd) * half, half, 0)
-    came = swap(theirs, 1)
-    mine = mine + came
-    mine = mine + after(swap(mine, 2), other)
-    theirs = swap(mine, 1)
-    low, high = jnp.where(odd == 0, mine, theirs), jnp.where(odd == 0, theirs, mine)
-    return (low, high), came
+    mine = mine + swap(theirs, 1)
+    return mine, swap(mine, 2)
+
+
+def replica_halves(mine, odd):
+    theirs = lax.ppermute(mine, "replica", [(r, r ^ 1) for r in range(4)])
+    return jnp.where(odd, theirs, mine), jnp.where(odd, mine, theirs)
 
 
 def exchange_ring(ring, own, far, near, pseudo):
-    total, _ = replica_sum(pseudo, far)
+    total = lax.psum(pseudo, "replica")
     shard, cut = own.shape[0], own.shape[0] // 2
     blocks = [own]
     from_left = from_right = own
@@ -368,7 +364,7 @@
     halves = range(2)
     wide = lambda v: v.astype(f32)
     pick = jnp.where
-    sent, crossed = [own], [own]
+    sent = [own]
 
     def part(value, h):
         return value[pieces[h][0] : pieces[h][1]]
@@ -376,48 +372,64 @@
     def later(*values):
         return after(values, sent[0])
 
-    def links(to_right, to_left, chord=None):
+    def ring(to_right, to_left):
         sent[0] = to_right, to_left
-        came = [plane.to_right(to_right), plane.to_left(to_left)]
-        if chord is not None:
-            came.append(plane.over_chord(after(chord, sent[0], crossed[0])))
-            crossed[0] = came[-1]
-        return lax.optimization_barrier(came)
-
-    first = links(own, own)
-    total, came = replica_sum(after(pseudo, own), far)
-    first, far, came = lax.optimization_barrier((first, far, came))
-    one = [[part(came, h) for came in first] for h in halves]
-    two = [links(*later(*one[h])) for h in halves]
-    two[0], total = lax.optimization_barrier((two[0], total))
-    chords = [part(own, h) for h in halves] + [pick(at2, *one[h]) for h in halves] + [part(far, h) for h in halves]
-    chords += [part(pick(at1, near[1], near[0]).astype(bf16), h) for h in halves]
+        return lax.optimization_barrier([plane.to_right(to_right), plane.to_left(to_left)])
+
+    def chord(value, *others):
+        return plane.over_chord(after(value, sent[0], *others))
+
+    first = ring(own, own)
+    partner = chord(own)
+    odd = lax.axis_index("replica") % 2 == 1
+    sum_over = lax.axis_size("replica") == 4
+    if sum_over:
+        mine, came = replica_pairs(after(pseudo, own), odd.astype(jnp.int32))
+    else:
+        came = total = lax.psum(pseudo, "replica")
+    first, partner, far, came = lax.optimization_barrier((first, partner, far, came))
+    one = [[part(side, h) for side in first] for h in halves]
+    two = [ring(*later(*one[0]))]
+    if sum_over:
+        total = replica_halves(mine + came, odd)
+    one[1], total = lax.optimization_barrier((one[1], total))
+    two.append(ring(*later(*one[1])))
+    from_inner = chord(far, total)
     three = []
     for h in halves:
         left, right = later(*two[h])
         terms = part(far, h)
-        three.append(links(pick(at0, terms, left), pick(at3, terms, right), chords[h]))
+        three.append(ring(pick(at0, terms, left), pick(at3, terms, right)))
+    three[0], from_inner = lax.optimization_barrier((three[0], from_inner))
     four = []
     for h in halves:
-        left, right = later(*three[h][:2])
+        left, right = later(*three[h])
         to_right = wide(part(near[0], h)) + pick(at1, wide(left), zero)
         to_left = wide(part(near[1], h)) + pick(at2, wide(right), zero)
         to_right = pick(at2, left, to_right.astype(bf16))
         to_left = pick(at1, right, to_left.astype(bf16))
-        four.append(links(to_right, to_left, chords[2 + h]))
+        four.append(ring(to_right, to_left))
+        if h == 0:
+            join = jnp.concatenate([pick(at2, *one[g]) for g in halves])
+            far_inner = chord(join, from_inner)
     five = []
     for h in halves:
-        left, right = later(*four[h][:2])
+        if h == 1:
+            four[1], far_inner = lax.optimization_barrier((four[1], far_inner))
+        left, right = later(*four[h])
         to_right = part(near[2], h) + pick(at3, zero, wide(left))
         to_left = part(near[3], h) + pick(at0, zero, wide(right))
-        five.append(links(to_right.astype(bf16), to_left.astype(bf16), chords[4 + h]))
-    six = []
+        five.append(ring(to_right.astype(bf16), to_left.astype(bf16)))
+    six, from_partner = [], []
     for h in halves:
-        left, right, chord = later(*five[h])
-        chord = wide(chord)
-        to_right = part(near[4], h) + wide(left) + pick(at1, chord, zero)
-        to_left = part(near[5], h) + wide(right) + pick(at2, chord, zero)
-        six.append(links(to_right.astype(bf16), to_left.astype(bf16), chords[6 + h]))
+        for_partner = pick(at1, part(near[1], h), part(near[0], h)).astype(bf16)
+        from_partner.append(chord(for_partner, far_inner, *from_partner))
+        left, right = later(*five[h])
+        over = wide(part(from_inner, h))
+        to_right = part(near[4], h) + wide(left) + pick(at1, over, zero)
+        to_left = part(near[5], h) + wide(right) + pick(at2, over, zero)
+        six.append(ring(to_right.astype(bf16), to_left.astype(bf16)))
+    sums = [(*six[h], from_partner[h]) for h in halves]
 
     blocks, plan = [], []
 
@@ -428,21 +440,21 @@
             blocks.append(array)
         return entry
 
-    for array in (own, *first):
+    for array in (own, *first, partner):
         plan.append([(None, len(blocks), 0, shard)])
         blocks.append(array)
+    plan.pop()
     for way in range(2):
         plan.append(add(None, [two[h][way] for h in halves]))
-    partner = add(0, [three[h][2] for h in halves])
     for way in range(2):
-        entry = [(way, *rest) for _, *rest in partner]
-        plan.append(entry + add(2 + way, [three[h][way] for h in halves]))
-    plan.append(add(4, [four[h][2] for h in halves]))
+        plan.append([(way, 3, 0, shard)] + add(2 + way, [three[h][way] for h in halves]))
+    plan.append([(4, len(blocks), 0, shard)])
+    blocks.append(far_inner)
     for way in range(2):
         plan[-1] += add(5 + way, [four[h][way] for h in halves])
     flags = [at1, at2, ~at1, ~at2, at1 | at2, at3, at0]
     plan = tuple(tuple(entry) for entry in plan)
-    return blocks, plan, jnp.stack(flags), six, total
+    return blocks, plan, jnp.stack(flags), sums, total
 
 
 def local(

time: 182 us -> 181 us (level)
  waiting for transfers between devices: 46.2 us -> 60.4 us
  starting transfers between devices: 53.1 us -> 40 us
  local copies, waits for them, and re-layouts: 11.5 us -> 8.39 us
    ppermute x11, waiting for transfers between devices: 9.41 us -> 42.5 us  [to_left(): return lax.ppermute(value, 'fsdp', self.left)]
    ppermute x8 -> x5, waiting for transfers between devices: 27.8 us -> 3.36 us  [over_chord(): return lax.ppermute(value, 'fsdp', [(2, 3), (3, 2), (4, 5), (5, 4)])]
    ppermute x8 -> x5, starting transfers between devices: 28.8 us -> 15.8 us  [over_chord(): return lax.ppermute(value, 'fsdp', [(2, 3), (3, 2), (4, 5), (5, 4)])]
    ppermute x11, waiting for transfers between devices: 8.84 us -> 14.5 us  [to_right(): return lax.ppermute(value, 'fsdp', self.right)]
    ppermute x11, starting transfers between devices: 21.1 us -> 15.8 us  [to_right(): return lax.ppermute(value, 'fsdp', self.right)]
    ppermute x11, starting transfers between devices: 1.61 us -> 6.79 us  [to_left(): return lax.ppermute(value, 'fsdp', self.left)]
    convert_element_type x5, other arithmetic: 11 us -> 14.2 us  [the longest x1 5.56 us: exchange_plane(): for_partner = pick(at1, part(near[1], h), part(near[0], h)).astype(bf16)]
    select_n x2 -> x1, other arithmetic: 6.62 us -> 3.64 us  [exchange_plane(): to_left = pick(at1, right, to_left.astype(bf16))]
  transfers between devices with their start and end apart: 33 -> 30, of which waited for: 14 -> 16; matrix products, arithmetic and copies ran while one was open for 18% -> 16% of each run, Pallas kernels for 17% -> 17%
where the time goes in v9:
time: 181 us
  waiting for transfers between devices  60.4 us (33%)
  starting transfers between devices  40 us (22%)
  other arithmetic  38.3 us (21%)
  Pallas kernels  32.3 us (18%)
  local copies, waits for them, and re-layouts  8.39 us (5%)
    ppermute x11, waiting for transfers between devices, to_left(): return lax.ppermute(value, 'fsdp', self.left)  42.5 us
    pallas_call x1, Pallas kernels, second_part(): pl.pallas_call(functools.partial(second_kernel, plan), in_specs=[pl.Block...  17.7 us
    ppermute x5, starting transfers between devices, over_chord(): return lax.ppermute(value, 'fsdp', [(2, 3), (3, 2), (4, 5), (5, 4)])  15.8 us
    ppermute x11, starting transfers between devices, to_right(): return lax.ppermute(value, 'fsdp', self.right)  15.8 us
    ppermute x11, waiting for transfers between devices, to_right(): return lax.ppermute(value, 'fsdp', self.right)  14.5 us
    pallas_call x1, Pallas kernels, first_part(): pl.pallas_call(functools.partial(first_kernel, scale), grid_spec=pltpu.Pr...  11.9 us
    unnamed x42, local copies, waits for them, and re-layouts  8.22 us
    ppermute x11, starting transfers between devices, to_left(): return lax.ppermute(value, 'fsdp', self.left)  6.79 us
  transfers between devices with their start and end apart: 30, of which 16 were waited for; matrix products, arithmetic and copies ran while one was open for 16% of the time, Pallas kernels for 17%

profile of v9, /device:TPU:8, one launch (start us, length us, event | category | flops | bytes accessed | tf_op | source)
XLA Modules:
  0.0 180.5 jit_solution(14061604594732175410)
XLA Ops:
  1.5 2.4 %multiply_convert_fusion.refs_0_ = bf16[512,1024]{1,0:T(8,128)(2,1)} fusion(f32[512]{0:T(512)S(1)} %bitcast.91, bf16[1,512,1024]{2,1,0:T(8,128)(2,1)} %param.12), kind=kLoop, calls=%fused_computation | loop fusion | flops 1572864 | bytes 2099200 | tf_op jit(solution)/shard_map/convert_element_type | solution.py:479
  4.1 2.0 %collective-permute-start = (bf16[512,1024]{1,0:T(8,128)(2,1)}, bf16[512,1024]{1,0:T(8,128)(2,1)}, u32[]{:S(2)}, u32[]{:S(2)}) collective-permute-start(bf16[512,1024]{1,0:T(8,128)(2,1)} %multiply_convert_fusion.refs_0_), channel_id=1, source_target_pairs={{0,2},{2,4},{4,6},{6,7},{7,5},{5,3},{3,1},{1,0},{8,10},{10,12},{12... | collective-permute-start | bytes 3145736 | tf_op jit(solution)/shard_map/ppermute | solution.py:42
  6.1 3.4 %collective-permute-start.2 = (bf16[512,1024]{1,0:T(8,128)(2,1)}, bf16[512,1024]{1,0:T(8,128)(2,1)}, u32[]{:S(2)}, u32[]{:S(2)}) collective-permute-start(bf16[512,1024]{1,0:T(8,128)(2,1)} %multiply_convert_fusion.refs_0_), channel_id=1, source_target_pairs={{2,3},{3,2},{4,5},{5,4},{10,11},{11,10},{12,13},{13,12},{18,19},{1... | collective-permute-start | bytes 3145736 | tf_op jit(solution)/shard_map/ppermute | solution.py:54
  10.6 1.5 collective-permute-start.4
  13.4 2.3 %copy-done.5 = bf16[1,512,4096]{2,1,0:T(8,128)(2,1)S(1)} copy-done((bf16[1,512,4096]{2,1,0:T(8,128)(2,1)S(1)}, bf16[1,512,4096]{2,1,0:T(8,128)(2,1)}, u32[]{:S(2)}) %copy-start.5) | copy-done | bytes 4194328
  15.6 11.9 %norm_and_weight_terms.1 = (bf16[512,1024]{1,0:T(8,128)(2,1)S(1)}, f32[512,128]{1,0:T(8,128)S(1)}, bf16[512,1024]{1,0:T(8,128)(2,1)S(1)}, f32[7,512,1024]{2,1,0:T(8,128)}) custom-call(s32[8]{0:T(128)S(1)} %compare_select_fusion.4.at, bf16[512,4096]{1,0:T(8,128)(2,1)S(1)} %bitcast.87, bf16[512,1024]{1,0:T(8,128)(2,1)S(1)} %bitcast.88, ...), custom_call_target="tpu_custom_call" | custom-call | flops 4294967296 | bytes 20971520 | tf_op jit(solution)/shard_map/norm_and_weight_terms/pallas_call | solution.py:115
  28.2 1.7 collective-permute-done.1.refs_2_
  29.9 3.3 %collective-permute-done.2.refs_3_ = bf16[512,1024]{1,0:T(8,128)(2,1)} collective-permute-done((bf16[512,1024]{1,0:T(8,128)(2,1)}, bf16[512,1024]{1,0:T(8,128)(2,1)}, u32[]{:S(2)}, u32[]{:S(2)}) %collective-permute-start.2) | collective-permute-done | bytes 1048608 | tf_op jit(solution)/shard_map/ppermute | solution.py:54
  33.3 2.4 %add.148 = f32[192,1024]{1,0:T(8,128)} add(f32[192,1024]{1,0:T(8,128)} %dynamic-slice_add_fusion, f32[192,1024]{1,0:T(8,128)} %collective-permute-done.4) | non-fusion elementwise | flops 196608 | bytes 2359296 | tf_op jit(solution)/shard_map/add | solution.py:394
  35.7 3.0 %broadcast_select_fusion.1 = (bf16[256,1024]{1,0:T(8,128)(2,1)}, bf16[256,1024]{1,0:T(8,128)(2,1)}, bf16[256,1024]{1,0:T(8,128)(2,1)}, bf16[256,1024]{1,0:T(8,128)(2,1)}, bf16[256,1024]{1,0:T(8,128)(2,1)}) fusion(pred[]{:T(512)} %eq.32, bf16[512,1024]{1,0:T(8,128)(2,1)} %collective-permute-done.1.refs_2_, bf16[512,1024]{1,0:T(8,128)(2,1)} %collective-permute-done.refs_1_), kind=kLoop, calls=%fused_computation.51 | loop fusion | flops 262144 | bytes 4718593 | tf_op jit(solution)/shard_map/jit(_where)/select_n | solution.py:413
  38.7 1.6 collective-permute-start.5
  40.7 2.7 %broadcast_select_fusion.6 = (f32[192,1024]{1,0:T(8,128)}, f32[192,1024]{1,0:T(8,128)}) fusion(f32[192,1024]{1,0:T(8,128)} %add.148, f32[192,1024]{1,0:T(8,128)} %collective-permute-done.7, pred[]{:T(512)S(6)} %eq.35), kind=kLoop, calls=%fused_computation.56 | loop fusion | flops 393216 | bytes 3145729 | tf_op jit(solution)/shard_map/jit(_where)/select_n | solution.py:329
  43.4 1.6 collective-permute-start.8
  45.5 8.2 %collective-permute-done.5.refs_4_ = bf16[256,1024]{1,0:T(8,128)(2,1)S(1)} collective-permute-done((bf16[256,1024]{1,0:T(8,128)(2,1)}, bf16[256,1024]{1,0:T(8,128)(2,1)S(1)}, u32[]{:S(2)}, u32[]{:S(2)}) %collective-permute-start.5) | collective-permute-done | bytes 524320 | tf_op jit(solution)/shard_map/ppermute | solution.py:42
  53.6 1.6 collective-permute-done.6.refs_6_
  55.2 1.9 %collective-permute-start.12 = (bf16[512,1024]{1,0:T(8,128)(2,1)S(1)}, bf16[512,1024]{1,0:T(8,128)(2,1)}, u32[]{:S(2)}, u32[]{:S(2)}) collective-permute-start(bf16[512,1024]{1,0:T(8,128)(2,1)S(1)} %get-tuple-element.108), channel_id=1, source_target_pairs={{2,3},{3,2},{4,5},{5,4},{10,11},{11,10},{12,13},{13,12},{18,19},{1... | collective-permute-start | bytes 3145736 | tf_op jit(solution)/shard_map/ppermute | solution.py:54
  58.4 1.9 %collective-permute-start.10 = (bf16[256,1024]{1,0:T(8,128)(2,1)}, bf16[256,1024]{1,0:T(8,128)(2,1)}, u32[]{:S(2)}, u32[]{:S(2)}) collective-permute-start(bf16[256,1024]{1,0:T(8,128)(2,1)} %get-tuple-element.180), channel_id=1, source_target_pairs={{0,2},{2,4},{4,6},{6,7},{7,5},{5,3},{3,1},{1,0},{8,10},{10,12},{12... | collective-permute-start | bytes 1572872 | tf_op jit(solution)/shard_map/ppermute | solution.py:42
  60.2 4.6 %collective-permute-done.8.refs_5_ = bf16[256,1024]{1,0:T(8,128)(2,1)S(1)} collective-permute-done((bf16[256,1024]{1,0:T(8,128)(2,1)}, bf16[256,1024]{1,0:T(8,128)(2,1)S(1)}, u32[]{:S(2)}, u32[]{:S(2)}) %collective-permute-start.8) | collective-permute-done | bytes 524320 | tf_op jit(solution)/shard_map/ppermute | solution.py:42
  64.9 1.6 collective-permute-done.9.refs_7_
  66.5 1.1 broadcast_select_fusion.2
  68.0 1.6 collective-permute-start.13
  69.6 1.2 broadcast_select_fusion
  71.8 6.0 %collective-permute-done.11.refs_10_ = bf16[256,1024]{1,0:T(8,128)(2,1)} collective-permute-done((bf16[256,1024]{1,0:T(8,128)(2,1)}, bf16[256,1024]{1,0:T(8,128)(2,1)}, u32[]{:S(2)}, u32[]{:S(2)}) %collective-permute-start.11) | collective-permute-done | bytes 524320 | tf_op jit(solution)/shard_map/ppermute | solution.py:45
  77.8 10.5 %collective-permute-done.14.refs_11_ = bf16[256,1024]{1,0:T(8,128)(2,1)} collective-permute-done((bf16[256,1024]{1,0:T(8,128)(2,1)}, bf16[256,1024]{1,0:T(8,128)(2,1)}, u32[]{:S(2)}, u32[]{:S(2)}) %collective-permute-start.14) | collective-permute-done | bytes 524320 | tf_op jit(solution)/shard_map/ppermute | solution.py:45
  88.4 3.6 %fusion.21 = (bf16[256,1024]{1,0:T(8,128)(2,1)}, bf16[256,1024]{1,0:T(8,128)(2,1)}) fusion(bf16[256,1024]{1,0:T(8,128)(2,1)} %collective-permute-done.11.refs_10_, f32[7,512,1024]{2,1,0:T(8,128)} %get-tuple-element.116.own, pred[]{:T(512)} %eq.31, pred[]{:T(512)} %eq.32, bf16[256,1024]{1,0:T(8,128)(2,1)} %collective-permute-done.10.refs_8_), kind=kLoop, calls=%fused_computation.45 | loop fusion | flops 2621440 | bytes 4194306 | tf_op jit(solution)/shard_map/jit(_where)/select_n | solution.py:410
  92.5 1.6 collective-permute-start.18
  94.0 2.1 %collective-permute-start.17 = (bf16[512,1024]{1,0:T(8,128)(2,1)}, bf16[512,1024]{1,0:T(8,128)(2,1)}, u32[]{:S(2)}, u32[]{:S(2)}) collective-permute-start(bf16[512,1024]{1,0:T(8,128)(2,1)} %pad_maximum_fusion), channel_id=1, source_target_pairs={{2,3},{3,2},{4,5},{5,4},{10,11},{11,10},{12,13},{13,12},{18,19},{1... | collective-permute-start | bytes 3145736 | tf_op jit(solution)/shard_map/ppermute | solution.py:54
  96.2 5.6 %fusion.18 = (bf16[256,1024]{1,0:T(8,128)(2,1)}, bf16[256,1024]{1,0:T(8,128)(2,1)}, bf16[256,1024]{1,0:T(8,128)(2,1)}, bf16[256,1024]{1,0:T(8,128)(2,1)}) fusion(f32[7,512,1024]{2,1,0:T(8,128)} %get-tuple-element.116.own, pred[]{:T(512)} %eq.31, bf16[256,1024]{1,0:T(8,128)(2,1)} %collective-permute-done.14.refs_11_, pred[]{:T(512)} %eq.32, ...), kind=kLoop, calls=%fused_computation.41 | loop fusion | flops 3145728 | bytes 7340034 | tf_op jit(solution)/shard_map/convert_element_type | solution.py:425
  101.8 2.0 %collective-permute-start.15 = (bf16[256,1024]{1,0:T(8,128)(2,1)}, bf16[256,1024]{1,0:T(8,128)(2,1)S(1)}, u32[]{:S(2)}, u32[]{:S(2)}) collective-permute-start(bf16[256,1024]{1,0:T(8,128)(2,1)} %get-tuple-element.163), channel_id=1, source_target_pairs={{0,2},{2,4},{4,6},{6,7},{7,5},{5,3},{3,1},{1,0},{8,10},{10,12},{12... | collective-permute-start | bytes 1572872 | tf_op jit(solution)/shard_map/ppermute | solution.py:42
  104.0 3.2 %collective-permute-done.19.refs_15_ = bf16[256,1024]{1,0:T(8,128)(2,1)} collective-permute-done((bf16[256,1024]{1,0:T(8,128)(2,1)}, bf16[256,1024]{1,0:T(8,128)(2,1)}, u32[]{:S(2)}, u32[]{:S(2)}) %collective-permute-start.19) | collective-permute-done | bytes 524320 | tf_op jit(solution)/shard_map/ppermute | solution.py:45
  107.5 9.3 %collective-permute-done.16.refs_16_ = bf16[256,1024]{1,0:T(8,128)(2,1)} collective-permute-done((bf16[256,1024]{1,0:T(8,128)(2,1)}, bf16[256,1024]{1,0:T(8,128)(2,1)}, u32[]{:S(2)}, u32[]{:S(2)}) %collective-permute-start.16) | collective-permute-done | bytes 524320 | tf_op jit(solution)/shard_map/ppermute | solution.py:45
  116.9 2.2 %fusion.11 = (bf16[256,1024]{1,0:T(8,128)(2,1)S(1)}, bf16[256,1024]{1,0:T(8,128)(2,1)S(1)}) fusion(bf16[256,1024]{1,0:T(8,128)(2,1)} %collective-permute-done.19.refs_15_, f32[7,512,1024]{2,1,0:T(8,128)} %get-tuple-element.116.own, pred[]{:T(512)} %eq.34, bf16[256,1024]{1,0:T(8,128)(2,1)S(1)} %collective-permute-done.18.refs_13_, pred[]{:T(512)} %eq.33), kind=kLoop, calls=%fused_computation.26 | loop fusion | flops 2097152 | bytes 4194306 | tf_op jit(solution)/shard_map/convert_element_type | solution.py:422
  119.7 1.5 collective-permute-start.22
  121.2 2.0 %fusion.10 = (bf16[256,1024]{1,0:T(8,128)(2,1)S(1)}, bf16[256,1024]{1,0:T(8,128)(2,1)S(1)}) fusion(bf16[256,1024]{1,0:T(8,128)(2,1)} %collective-permute-done.16.refs_16_, f32[7,512,1024]{2,1,0:T(8,128)} %get-tuple-element.116.own, pred[]{:T(512)} %eq.34, bf16[256,1024]{1,0:T(8,128)(2,1)S(1)} %collective-permute-done.15.refs_14_, pred[]{:T(512)} %eq.33), kind=kLoop, calls=%fused_computation.24 | loop fusion | flops 2097152 | bytes 4194306 | tf_op jit(solution)/shard_map/convert_element_type | solution.py:422
  124.2 1.2 collective-permute-start.20
  125.4 3.9 %collective-permute-start.26 = (bf16[256,1024]{1,0:T(8,128)(2,1)S(1)}, bf16[256,1024]{1,0:T(8,128)(2,1)S(1)}, u32[]{:S(2)}, u32[]{:S(2)}) collective-permute-start(bf16[256,1024]{1,0:T(8,128)(2,1)S(1)} %copy-done.18), channel_id=1, source_target_pairs={{2,3},{3,2},{4,5},{5,4},{10,11},{11,10},{12,13},{13,12},{18,19},{1... | collective-permute-start | bytes 1572872 | tf_op jit(solution)/shard_map/ppermute | solution.py:54
  129.3 2.5 %fusion.24 = (bf16[1,384,1024]{2,1,0:T(8,128)(2,1)}, f32[384,1024]{1,0:T(8,128)}, f32[384,1024]{1,0:T(8,128)}) fusion(bf16[1,384,1024]{2,1,0:T(8,128)(2,1)S(1)} %copy-done.16, f32[384,1024]{1,0:T(8,128)S(1)} %copy-done.13, f32[192,1024]{1,0:T(8,128)S(1)} %copy-done.10, f32[192,1024]{1,0:T(8,128)S(1)} %copy-done.11, f32[384,1024]{1,0:T(8,128)S(1)} %copy-done.14), kind=kLoop, calls=%fused_computation.48 | loop fusion | flops 4718592 | bytes 9437184 | tf_op jit(solution)/shard_map/broadcast_in_dim | solution.py:511
  131.8 2.2 %collective-permute-done.23 = bf16[256,1024]{1,0:T(8,128)(2,1)S(1)} collective-permute-done((bf16[256,1024]{1,0:T(8,128)(2,1)S(1)}, bf16[256,1024]{1,0:T(8,128)(2,1)S(1)}, u32[]{:S(2)}, u32[]{:S(2)}) %collective-permute-start.23) | collective-permute-done | bytes 524320 | tf_op jit(solution)/shard_map/ppermute | solution.py:45
  134.7 2.1 %fusion.5 = (bf16[256,1024]{1,0:T(8,128)(2,1)S(1)}, bf16[256,1024]{1,0:T(8,128)(2,1)S(1)}) fusion(bf16[256,1024]{1,0:T(8,128)(2,1)S(1)} %collective-permute-done.23, f32[7,512,1024]{2,1,0:T(8,128)} %get-tuple-element.116.own, pred[]{:T(512)} %eq.32, bf16[512,1024]{1,0:T(8,128)(2,1)} %collective-permute-done.12, pred[]{:T(512)} %eq.31, ...), kind=kLoop, calls=%fused_computation.14 | loop fusion | flops 2883584 | bytes 4718594 | tf_op jit(solution)/shard_map/convert_element_type | solution.py:431
  136.8 1.6 collective-permute-start.29
  138.9 6.3 %collective-permute-done.21 = bf16[256,1024]{1,0:T(8,128)(2,1)S(1)} collective-permute-done((bf16[256,1024]{1,0:T(8,128)(2,1)S(1)}, bf16[256,1024]{1,0:T(8,128)(2,1)S(1)}, u32[]{:S(2)}, u32[]{:S(2)}) %collective-permute-start.21) | collective-permute-done | bytes 524320 | tf_op jit(solution)/shard_map/ppermute | solution.py:45
  145.9 2.2 %fusion.9 = (bf16[256,1024]{1,0:T(8,128)(2,1)S(1)}, bf16[256,1024]{1,0:T(8,128)(2,1)S(1)}) fusion(bf16[256,1024]{1,0:T(8,128)(2,1)S(1)} %collective-permute-done.21, f32[7,512,1024]{2,1,0:T(8,128)} %get-tuple-element.116.own, pred[]{:T(512)} %eq.32, bf16[512,1024]{1,0:T(8,128)(2,1)} %collective-permute-done.12, pred[]{:T(512)} %eq.31, ...), kind=kLoop, calls=%fused_computation.18 | loop fusion | flops 2883584 | bytes 4718594 | tf_op jit(solution)/shard_map/convert_element_type | solution.py:431
  148.1 1.6 collective-permute-start.25
  150.2 4.5 %collective-permute-start.27 = (bf16[256,1024]{1,0:T(8,128)(2,1)S(1)}, bf16[256,1024]{1,0:T(8,128)(2,1)S(1)}, u32[]{:S(2)}, u32[]{:S(2)}) collective-permute-start(bf16[256,1024]{1,0:T(8,128)(2,1)S(1)} %copy-done.17), channel_id=1, source_target_pairs={{2,3},{3,2},{4,5},{5,4},{10,11},{11,10},{12,13},{13,12},{18,19},{1... | collective-permute-start | bytes 1572872 | tf_op jit(solution)/shard_map/ppermute | solution.py:54
  154.8 17.7 %project_and_input_grad.1 = (bf16[512,1024]{1,0:T(8,128)(2,1)}, bf16[512,4096]{1,0:T(8,128)(2,1)}) custom-call(s32[15]{0:T(128)S(1)} %pad_add_fusion.at, bf16[512,4096]{1,0:T(8,128)(2,1)} %bitcast.86, bf16[512,1024]{1,0:T(8,128)(2,1)} %copy-done.7, f32[512,128]{1,0:T(8,128)S(1)} %copy-done.9, f32[512,128]{1,0:T(8,128)S(1)} %get-tuple-element.184.cosine, ...), custom_call_target="tpu_custom_call" | custom-call | flops 8589934592 | bytes 16777216 | tf_op jit(solution)/shard_map/project_and_input_grad/pallas_call | solution.py:288
  172.6 5.2 %copy-done = f32[7,512,1024]{2,1,0:T(8,128)S(1)} copy-done((f32[7,512,1024]{2,1,0:T(8,128)S(1)}, f32[7,512,1024]{2,1,0:T(8,128)}, u32[]{:S(2)}) %copy-start) | copy-done | bytes 14680088
  177.8 1.3 sum_of_terms.2
  179.2 1.4 sum_of_terms.3
  (85 shorter events, 12.6 us)
Async XLA Ops:
  0.6 3.3 %copy-start.15 = (f32[1,384,1024]{2,1,0:T(8,128)S(1)}, f32[1,384,1024]{2,1,0:T(8,128)}, u32[]{:S(2)}) copy-start(f32[1,384,1024]{2,1,0:T(8,128)} %param.14) | copy-start | bytes 4718596
  4.0 5.6 %collective-permute-start.3 = (f32[192,1024]{1,0:T(8,128)S(1)}, f32[192,1024]{1,0:T(8,128)S(1)}, u32[]{:S(2)}, u32[]{:S(2)}) collective-permute-start(f32[192,1024]{1,0:T(8,128)S(1)} %constant_dynamic-slice_fusion), channel_id=1, source_target_pairs={{0,8},{8,0},{16,24},{24,16},{1,9},{9,1},{17,25},{25,17},{2,10},{10... | collective-permute-start | bytes 2359304 | tf_op jit(solution)/shard_map/ppermute | solution.py:319
  4.1 25.9 %collective-permute-start.1 = (bf16[512,1024]{1,0:T(8,128)(2,1)}, bf16[512,1024]{1,0:T(8,128)(2,1)}, u32[]{:S(2)}, u32[]{:S(2)}) collective-permute-start(bf16[512,1024]{1,0:T(8,128)(2,1)} %multiply_convert_fusion.refs_0_), channel_id=1, source_target_pairs={{2,0},{4,2},{6,4},{7,6},{5,7},{3,5},{1,3},{0,1},{10,8},{12,10},{14... | collective-permute-start | bytes 3145736 | tf_op jit(solution)/shard_map/ppermute | solution.py:45
  4.1 25.8 %collective-permute-start = (bf16[512,1024]{1,0:T(8,128)(2,1)}, bf16[512,1024]{1,0:T(8,128)(2,1)}, u32[]{:S(2)}, u32[]{:S(2)}) collective-permute-start(bf16[512,1024]{1,0:T(8,128)(2,1)} %multiply_convert_fusion.refs_0_), channel_id=1, source_target_pairs={{0,2},{2,4},{4,6},{6,7},{7,5},{5,3},{3,1},{1,0},{8,10},{10,12},{12... | collective-permute-start | bytes 3145736 | tf_op jit(solution)/shard_map/ppermute | solution.py:42
  6.1 27.1 %collective-permute-start.2 = (bf16[512,1024]{1,0:T(8,128)(2,1)}, bf16[512,1024]{1,0:T(8,128)(2,1)}, u32[]{:S(2)}, u32[]{:S(2)}) collective-permute-start(bf16[512,1024]{1,0:T(8,128)(2,1)} %multiply_convert_fusion.refs_0_), channel_id=1, source_target_pairs={{2,3},{3,2},{4,5},{5,4},{10,11},{11,10},{12,13},{13,12},{18,19},{1... | collective-permute-start | bytes 3145736 | tf_op jit(solution)/shard_map/ppermute | solution.py:54
  10.6 2.8 %copy-start.20 = (s32[8]{0:T(128)S(1)}, s32[8]{0:T(128)}, u32[]{:S(2)}) copy-start(s32[8]{0:T(128)} %constant.120.clone) | copy-start | bytes 100
  10.6 2.8 %copy-start.6 = (bf16[1,512,1024]{2,1,0:T(8,128)(2,1)S(1)}, bf16[1,512,1024]{2,1,0:T(8,128)(2,1)}, u32[]{:S(2)}) copy-start(bf16[1,512,1024]{2,1,0:T(8,128)(2,1)} %param.13) | copy-start | bytes 3145732
  10.6 22.7 %collective-permute-start.4 = (f32[192,1024]{1,0:T(8,128)}, f32[192,1024]{1,0:T(8,128)}, u32[]{:S(2)}, u32[]{:S(2)}) collective-permute-start(f32[192,1024]{1,0:T(8,128)} %dynamic-slice_add_fusion), channel_id=1, source_target_pairs={{0,16},{8,24},{16,0},{24,8},{1,17},{9,25},{17,1},{25,9},{2,18},{10... | collective-permute-start | bytes 2359304 | tf_op jit(solution)/shard_map/ppermute | solution.py:319
  13.3 14.2 %copy-start.2 = (f32[512,128]{1,0:T(8,128)}, f32[512,128]{1,0:T(8,128)S(1)}, u32[]{:S(2)}) copy-start(f32[512,128]{1,0:T(8,128)S(1)} %get-tuple-element.185.sine) | copy-start | bytes 786436
  28.2 10.5 %copy-start.7 = (bf16[512,1024]{1,0:T(8,128)(2,1)}, bf16[512,1024]{1,0:T(8,128)(2,1)S(1)}, u32[]{:S(2)}) copy-start(bf16[512,1024]{1,0:T(8,128)(2,1)S(1)} %get-tuple-element.80.kv_grad) | copy-start | bytes 3145732
  35.7 5.1 %collective-permute-start.7 = (f32[192,1024]{1,0:T(8,128)}, f32[192,1024]{1,0:T(8,128)}, u32[]{:S(2)}, u32[]{:S(2)}) collective-permute-start(f32[192,1024]{1,0:T(8,128)} %add.148), channel_id=1, source_target_pairs={{0,8},{8,0},{16,24},{24,16},{1,9},{9,1},{17,25},{25,17},{2,10},{10... | collective-permute-start | bytes 2359304 | tf_op jit(solution)/shard_map/ppermute | solution.py:328
  38.7 14.9 %collective-permute-start.5 = (bf16[256,1024]{1,0:T(8,128)(2,1)}, bf16[256,1024]{1,0:T(8,128)(2,1)S(1)}, u32[]{:S(2)}, u32[]{:S(2)}) collective-permute-start(bf16[256,1024]{1,0:T(8,128)(2,1)} %get-tuple-element.90), channel_id=1, source_target_pairs={{0,2},{2,4},{4,6},{6,7},{7,5},{5,3},{3,1},{1,0},{8,10},{10,12},{12... | collective-permute-start | bytes 1572872 | tf_op jit(solution)/shard_map/ppermute | solution.py:42
  40.3 15.0 %collective-permute-start.6 = (bf16[256,1024]{1,0:T(8,128)(2,1)}, bf16[256,1024]{1,0:T(8,128)(2,1)S(1)}, u32[]{:S(2)}, u32[]{:S(2)}) collective-permute-start(bf16[256,1024]{1,0:T(8,128)(2,1)} %get-tuple-element.91), channel_id=1, source_target_pairs={{2,0},{4,2},{6,4},{7,6},{5,7},{3,5},{1,3},{0,1},{10,8},{12,10},{14... | collective-permute-start | bytes 1572872 | tf_op jit(solution)/shard_map/ppermute | solution.py:45
  43.4 21.4 %collective-permute-start.8 = (bf16[256,1024]{1,0:T(8,128)(2,1)}, bf16[256,1024]{1,0:T(8,128)(2,1)S(1)}, u32[]{:S(2)}, u32[]{:S(2)}) collective-permute-start(bf16[256,1024]{1,0:T(8,128)(2,1)} %get-tuple-element.96), channel_id=1, source_target_pairs={{0,2},{2,4},{4,6},{6,7},{7,5},{5,3},{3,1},{1,0},{8,10},{10,12},{12... | collective-permute-start | bytes 1572872 | tf_op jit(solution)/shard_map/ppermute | solution.py:42
  45.0 21.5 %collective-permute-start.9 = (bf16[256,1024]{1,0:T(8,128)(2,1)}, bf16[256,1024]{1,0:T(8,128)(2,1)S(1)}, u32[]{:S(2)}, u32[]{:S(2)}) collective-permute-start(bf16[256,1024]{1,0:T(8,128)(2,1)} %get-tuple-element.97), channel_id=1, source_target_pairs={{2,0},{4,2},{6,4},{7,6},{5,7},{3,5},{1,3},{0,1},{10,8},{12,10},{14... | collective-permute-start | bytes 1572872 | tf_op jit(solution)/shard_map/ppermute | solution.py:45
  55.2 33.1 %collective-permute-start.12 = (bf16[512,1024]{1,0:T(8,128)(2,1)S(1)}, bf16[512,1024]{1,0:T(8,128)(2,1)}, u32[]{:S(2)}, u32[]{:S(2)}) collective-permute-start(bf16[512,1024]{1,0:T(8,128)(2,1)S(1)} %get-tuple-element.108), channel_id=1, source_target_pairs={{2,3},{3,2},{4,5},{5,4},{10,11},{11,10},{12,13},{13,12},{18,19},{1... | collective-permute-start | bytes 3145736 | tf_op jit(solution)/shard_map/ppermute | solution.py:54
  58.2 19.6 %collective-permute-start.11 = (bf16[256,1024]{1,0:T(8,128)(2,1)}, bf16[256,1024]{1,0:T(8,128)(2,1)}, u32[]{:S(2)}, u32[]{:S(2)}) collective-permute-start(bf16[256,1024]{1,0:T(8,128)(2,1)} %get-tuple-element.179), channel_id=1, source_target_pairs={{2,0},{4,2},{6,4},{7,6},{5,7},{3,5},{1,3},{0,1},{10,8},{12,10},{14... | collective-permute-start | bytes 1572872 | tf_op jit(solution)/shard_map/ppermute | solution.py:45
  58.4 19.4 %collective-permute-start.10 = (bf16[256,1024]{1,0:T(8,128)(2,1)}, bf16[256,1024]{1,0:T(8,128)(2,1)}, u32[]{:S(2)}, u32[]{:S(2)}) collective-permute-start(bf16[256,1024]{1,0:T(8,128)(2,1)} %get-tuple-element.180), channel_id=1, source_target_pairs={{0,2},{2,4},{4,6},{6,7},{7,5},{5,3},{3,1},{1,0},{8,10},{10,12},{12... | collective-permute-start | bytes 1572872 | tf_op jit(solution)/shard_map/ppermute | solution.py:42
  67.6 20.8 %collective-permute-start.14 = (bf16[256,1024]{1,0:T(8,128)(2,1)}, bf16[256,1024]{1,0:T(8,128)(2,1)}, u32[]{:S(2)}, u32[]{:S(2)}) collective-permute-start(bf16[256,1024]{1,0:T(8,128)(2,1)} %get-tuple-element.177), channel_id=1, source_target_pairs={{2,0},{4,2},{6,4},{7,6},{5,7},{3,5},{1,3},{0,1},{10,8},{12,10},{14... | collective-permute-start | bytes 1572872 | tf_op jit(solution)/shard_map/ppermute | solution.py:45
  68.0 20.3 %collective-permute-start.13 = (bf16[256,1024]{1,0:T(8,128)(2,1)}, bf16[256,1024]{1,0:T(8,128)(2,1)}, u32[]{:S(2)}, u32[]{:S(2)}) collective-permute-start(bf16[256,1024]{1,0:T(8,128)(2,1)} %get-tuple-element.178), channel_id=1, source_target_pairs={{0,2},{2,4},{4,6},{6,7},{7,5},{5,3},{3,1},{1,0},{8,10},{10,12},{12... | collective-permute-start | bytes 1572872 | tf_op jit(solution)/shard_map/ppermute | solution.py:42
  92.0 15.2 %collective-permute-start.19 = (bf16[256,1024]{1,0:T(8,128)(2,1)}, bf16[256,1024]{1,0:T(8,128)(2,1)}, u32[]{:S(2)}, u32[]{:S(2)}) collective-permute-start(bf16[256,1024]{1,0:T(8,128)(2,1)} %get-tuple-element.168), channel_id=1, source_target_pairs={{2,0},{4,2},{6,4},{7,6},{5,7},{3,5},{1,3},{0,1},{10,8},{12,10},{14... | collective-permute-start | bytes 1572872 | tf_op jit(solution)/shard_map/ppermute | solution.py:45
  92.5 11.4 %copy-start.19 = (s32[8]{0:T(128)S(1)}, s32[8]{0:T(128)}, u32[]{:S(2)}) copy-start(s32[8]{0:T(128)} %constant.121.clone) | copy-start | bytes 100
  92.5 15.1 %collective-permute-start.18 = (bf16[256,1024]{1,0:T(8,128)(2,1)}, bf16[256,1024]{1,0:T(8,128)(2,1)S(1)}, u32[]{:S(2)}, u32[]{:S(2)}) collective-permute-start(bf16[256,1024]{1,0:T(8,128)(2,1)} %get-tuple-element.169), channel_id=1, source_target_pairs={{0,2},{2,4},{4,6},{6,7},{7,5},{5,3},{3,1},{1,0},{8,10},{10,12},{12... | collective-permute-start | bytes 1572872 | tf_op jit(solution)/shard_map/ppermute | solution.py:42
  94.0 27.2 %collective-permute-start.17 = (bf16[512,1024]{1,0:T(8,128)(2,1)}, bf16[512,1024]{1,0:T(8,128)(2,1)}, u32[]{:S(2)}, u32[]{:S(2)}) collective-permute-start(bf16[512,1024]{1,0:T(8,128)(2,1)} %pad_maximum_fusion), channel_id=1, source_target_pairs={{2,3},{3,2},{4,5},{5,4},{10,11},{11,10},{12,13},{13,12},{18,19},{1... | collective-permute-start | bytes 3145736 | tf_op jit(solution)/shard_map/ppermute | solution.py:54
  101.8 15.0 %collective-permute-start.16 = (bf16[256,1024]{1,0:T(8,128)(2,1)}, bf16[256,1024]{1,0:T(8,128)(2,1)}, u32[]{:S(2)}, u32[]{:S(2)}) collective-permute-start(bf16[256,1024]{1,0:T(8,128)(2,1)} %get-tuple-element.162), channel_id=1, source_target_pairs={{2,0},{4,2},{6,4},{7,6},{5,7},{3,5},{1,3},{0,1},{10,8},{12,10},{14... | collective-permute-start | bytes 1572872 | tf_op jit(solution)/shard_map/ppermute | solution.py:45
  101.8 15.1 %collective-permute-start.15 = (bf16[256,1024]{1,0:T(8,128)(2,1)}, bf16[256,1024]{1,0:T(8,128)(2,1)S(1)}, u32[]{:S(2)}, u32[]{:S(2)}) collective-permute-start(bf16[256,1024]{1,0:T(8,128)(2,1)} %get-tuple-element.163), channel_id=1, source_target_pairs={{0,2},{2,4},{4,6},{6,7},{7,5},{5,3},{3,1},{1,0},{8,10},{10,12},{12... | collective-permute-start | bytes 1572872 | tf_op jit(solution)/shard_map/ppermute | solution.py:42
  116.9 8.5 %copy-start.18 = (bf16[256,1024]{1,0:T(8,128)(2,1)S(1)}, bf16[256,1024]{1,0:T(8,128)(2,1)}, u32[]{:S(2)}) copy-start(bf16[256,1024]{1,0:T(8,128)(2,1)} %get-tuple-element.145) | copy-start | bytes 1572868
  116.9 12.4 %copy-start.14 = (f32[384,1024]{1,0:T(8,128)S(1)}, f32[384,1024]{1,0:T(8,128)}, u32[]{:S(2)}) copy-start(f32[384,1024]{1,0:T(8,128)} %param.15) | copy-start | bytes 4718596
  119.1 14.9 %collective-permute-start.23 = (bf16[256,1024]{1,0:T(8,128)(2,1)S(1)}, bf16[256,1024]{1,0:T(8,128)(2,1)S(1)}, u32[]{:S(2)}, u32[]{:S(2)}) collective-permute-start(bf16[256,1024]{1,0:T(8,128)(2,1)S(1)} %get-tuple-element.166), channel_id=1, source_target_pairs={{2,0},{4,2},{6,4},{7,6},{5,7},{3,5},{1,3},{0,1},{10,8},{12,10},{14... | collective-permute-start | bytes 1572872 | tf_op jit(solution)/shard_map/ppermute | solution.py:45
  119.7 9.5 %copy-start.10 = (f32[192,1024]{1,0:T(8,128)S(1)}, f32[192,1024]{1,0:T(8,128)}, u32[]{:S(2)}) copy-start(f32[192,1024]{1,0:T(8,128)} %get-tuple-element.107) | copy-start | bytes 2359300
  119.7 9.5 %copy-start.11 = (f32[192,1024]{1,0:T(8,128)S(1)}, f32[192,1024]{1,0:T(8,128)}, u32[]{:S(2)}) copy-start(f32[192,1024]{1,0:T(8,128)} %get-tuple-element.106) | copy-start | bytes 2359300
  119.7 9.5 %copy-start.13 = (f32[384,1024]{1,0:T(8,128)S(1)}, f32[384,1024]{1,0:T(8,128)}, u32[]{:S(2)}) copy-start(f32[384,1024]{1,0:T(8,128)} %param.16) | copy-start | bytes 4718596
  119.7 9.5 %copy-start.16 = (bf16[1,384,1024]{2,1,0:T(8,128)(2,1)S(1)}, bf16[1,384,1024]{2,1,0:T(8,128)(2,1)}, u32[]{:S(2)}) copy-start(bf16[1,384,1024]{2,1,0:T(8,128)(2,1)} %param.17) | copy-start | bytes 2359300
  119.7 14.9 %collective-permute-start.22 = (bf16[256,1024]{1,0:T(8,128)(2,1)S(1)}, bf16[256,1024]{1,0:T(8,128)(2,1)S(1)}, u32[]{:S(2)}, u32[]{:S(2)}) collective-permute-start(bf16[256,1024]{1,0:T(8,128)(2,1)S(1)} %get-tuple-element.167), channel_id=1, source_target_pairs={{0,2},{2,4},{4,6},{6,7},{7,5},{5,3},{3,1},{1,0},{8,10},{10,12},{12... | collective-permute-start | bytes 1572872 | tf_op jit(solution)/shard_map/ppermute | solution.py:42
  123.3 22.0 %collective-permute-start.21 = (bf16[256,1024]{1,0:T(8,128)(2,1)S(1)}, bf16[256,1024]{1,0:T(8,128)(2,1)S(1)}, u32[]{:S(2)}, u32[]{:S(2)}) collective-permute-start(bf16[256,1024]{1,0:T(8,128)(2,1)S(1)} %get-tuple-element.164), channel_id=1, source_target_pairs={{2,0},{4,2},{6,4},{7,6},{5,7},{3,5},{1,3},{0,1},{10,8},{12,10},{14... | collective-permute-start | bytes 1572872 | tf_op jit(solution)/shard_map/ppermute | solution.py:45
  124.2 21.7 %collective-permute-start.20 = (bf16[256,1024]{1,0:T(8,128)(2,1)S(1)}, bf16[256,1024]{1,0:T(8,128)(2,1)S(1)}, u32[]{:S(2)}, u32[]{:S(2)}) collective-permute-start(bf16[256,1024]{1,0:T(8,128)(2,1)S(1)} %get-tuple-element.165), channel_id=1, source_target_pairs={{0,2},{2,4},{4,6},{6,7},{7,5},{5,3},{3,1},{1,0},{8,10},{10,12},{12... | collective-permute-start | bytes 1572872 | tf_op jit(solution)/shard_map/ppermute | solution.py:42
  125.4 20.5 %collective-permute-start.26 = (bf16[256,1024]{1,0:T(8,128)(2,1)S(1)}, bf16[256,1024]{1,0:T(8,128)(2,1)S(1)}, u32[]{:S(2)}, u32[]{:S(2)}) collective-permute-start(bf16[256,1024]{1,0:T(8,128)(2,1)S(1)} %copy-done.18), channel_id=1, source_target_pairs={{2,3},{3,2},{4,5},{5,4},{10,11},{11,10},{12,13},{13,12},{18,19},{1... | collective-permute-start | bytes 1572872 | tf_op jit(solution)/shard_map/ppermute | solution.py:54
  136.8 35.8 %collective-permute-start.29 = (bf16[256,1024]{1,0:T(8,128)(2,1)S(1)}, bf16[256,1024]{1,0:T(8,128)(2,1)S(1)}, u32[]{:S(2)}, u32[]{:S(2)}) collective-permute-start(bf16[256,1024]{1,0:T(8,128)(2,1)S(1)} %get-tuple-element.158), channel_id=1, source_target_pairs={{2,0},{4,2},{6,4},{7,6},{5,7},{3,5},{1,3},{0,1},{10,8},{12,10},{14... | collective-permute-start | bytes 1572872 | tf_op jit(solution)/shard_map/ppermute | solution.py:45
  138.4 34.2 %collective-permute-start.28 = (bf16[256,1024]{1,0:T(8,128)(2,1)S(1)}, bf16[256,1024]{1,0:T(8,128)(2,1)S(1)}, u32[]{:S(2)}, u32[]{:S(2)}) collective-permute-start(bf16[256,1024]{1,0:T(8,128)(2,1)S(1)} %get-tuple-element.159), channel_id=1, source_target_pairs={{0,2},{2,4},{4,6},{6,7},{7,5},{5,3},{3,1},{1,0},{8,10},{10,12},{12... | collective-permute-start | bytes 1572872 | tf_op jit(solution)/shard_map/ppermute | solution.py:42
  145.9 4.3 %copy-start.17 = (bf16[256,1024]{1,0:T(8,128)(2,1)S(1)}, bf16[256,1024]{1,0:T(8,128)(2,1)}, u32[]{:S(2)}) copy-start(bf16[256,1024]{1,0:T(8,128)(2,1)} %get-tuple-element.146) | copy-start | bytes 1572868
  145.9 8.9 %copy-start.3 = (f32[512,128]{1,0:T(8,128)S(1)}, f32[512,128]{1,0:T(8,128)}, u32[]{:S(2)}) copy-start(f32[512,128]{1,0:T(8,128)} %copy-done.2) | copy-start | bytes 786436
  145.9 8.9 %copy-start.9 = (f32[512,128]{1,0:T(8,128)S(1)}, f32[512,128]{1,0:T(8,128)}, u32[]{:S(2)}) copy-start(f32[512,128]{1,0:T(8,128)} %copy-done.8) | copy-start | bytes 786436
  148.1 31.0 %collective-permute-start.25 = (bf16[256,1024]{1,0:T(8,128)(2,1)S(1)}, bf16[256,1024]{1,0:T(8,128)(2,1)S(1)}, u32[]{:S(2)}, u32[]{:S(2)}) collective-permute-start(bf16[256,1024]{1,0:T(8,128)(2,1)S(1)} %get-tuple-element.156), channel_id=1, source_target_pairs={{2,0},{4,2},{6,4},{7,6},{5,7},{3,5},{1,3},{0,1},{10,8},{12,10},{14... | collective-permute-start | bytes 1572872 | tf_op jit(solution)/shard_map/ppermute | solution.py:45
  149.7 29.4 %collective-permute-start.24 = (bf16[256,1024]{1,0:T(8,128)(2,1)S(1)}, bf16[256,1024]{1,0:T(8,128)(2,1)S(1)}, u32[]{:S(2)}, u32[]{:S(2)}) collective-permute-start(bf16[256,1024]{1,0:T(8,128)(2,1)S(1)} %get-tuple-element.157), channel_id=1, source_target_pairs={{0,2},{2,4},{4,6},{6,7},{7,5},{5,3},{3,1},{1,0},{8,10},{10,12},{12... | collective-permute-start | bytes 1572872 | tf_op jit(solution)/shard_map/ppermute | solution.py:42
  150.2 28.9 %collective-permute-start.27 = (bf16[256,1024]{1,0:T(8,128)(2,1)S(1)}, bf16[256,1024]{1,0:T(8,128)(2,1)S(1)}, u32[]{:S(2)}, u32[]{:S(2)}) collective-permute-start(bf16[256,1024]{1,0:T(8,128)(2,1)S(1)} %copy-done.17), channel_id=1, source_target_pairs={{2,3},{3,2},{4,5},{5,4},{10,11},{11,10},{12,13},{13,12},{18,19},{1... | collective-permute-start | bytes 1572872 | tf_op jit(solution)/shard_map/ppermute | solution.py:54
  154.8 17.8 %copy-start.1 = (bf16[1,512,1024]{2,1,0:T(8,128)(2,1)S(1)}, bf16[1,512,1024]{2,1,0:T(8,128)(2,1)}, u32[]{:S(2)}) copy-start(bf16[1,512,1024]{2,1,0:T(8,128)(2,1)} %param.12) | copy-start | bytes 3145732
  154.8 17.8 %copy-start.4 = (bf16[1,512]{1,0:T(2,128)(2,1)S(1)}, bf16[1,512]{1,0:T(2,128)(2,1)}, u32[]{:S(2)}) copy-start(bf16[1,512]{1,0:T(2,128)(2,1)} %gain.3) | copy-start | bytes 3076
  172.6 5.2 %copy-start = (f32[7,512,1024]{2,1,0:T(8,128)S(1)}, f32[7,512,1024]{2,1,0:T(8,128)}, u32[]{:S(2)}) copy-start(f32[7,512,1024]{2,1,0:T(8,128)} %get-tuple-element.116.own) | copy-start | bytes 44040196
  (3 other events, 4.2 us)

commit v10 on v9

--- a/solution.py
+++ b/solution.py
@@ -11,6 +11,8 @@
 HEAD = 128
 SEQ_LEN = 4096
 
+
+FLAGS = 7
 
 epsilon = 1e-05
 rope_base = 500000.0
@@ -67,7 +69,7 @@
     return jnp.concatenate([cosine, cosine], axis=1), jnp.concatenate([-sine, sine], axis=1)
 
 
-def first_kernel(scale, at, x, cotangent, cosine, sine, kv_grad, inv, far, near):
+def first_kernel(scale, at, x, cotangent, cosine, sine, kv_grad, inv, far, near, last):
     step = pl.program_id(0)
     width = x.shape[1]
     shard = far.shape[0]
@@ -98,9 +100,13 @@
     def _():
         far[...] = term.astype(bf16)
 
-    @pl.when(step > 0)
+    @pl.when((step > 0) & (step < pl.num_programs(0) - 1))
     def _():
         near[0] = term
+
+    @pl.when(step == pl.num_programs(0) - 1)
+    def _():
+        last[...] = term
 
 
 def first_part(ring, tokens_in, cotangent, cosine, sine, shard, scale):
@@ -127,14 +133,16 @@
                 pl.BlockSpec((rows, cols), fixed),
                 pl.BlockSpec((rows, HEAD), fixed),
                 pl.BlockSpec((shard, cols), fixed),
-                pl.BlockSpec((1, shard, cols), lambda k, at: (jnp.maximum(k - 1, 0), 0, 0)),
+                pl.BlockSpec((1, shard, cols), lambda k, at: (jnp.clip(k - 1, 0, n - 3), 0, 0)),
+                pl.BlockSpec((shard, cols), fixed),
             ],
         ),
         out_shape=[
             jax.ShapeDtypeStruct((rows, cols), bf16),
             jax.ShapeDtypeStruct((rows, HEAD), f32),
             jax.ShapeDtypeStruct((shard, cols), bf16),
-            jax.ShapeDtypeStruct((n - 1, shard, cols), f32),
+            jax.ShapeDtypeStruct((n - 2, shard, cols), f32),
+            jax.ShapeDtypeStruct((shard, cols), f32),
         ],
         compiler_params=pltpu.CompilerParams(vmem_limit_bytes=40 * 2**20),
         cost_estimate=pl.CostEstimate(
@@ -148,7 +156,7 @@
 
 def last_kernel(count, own, weight, gain, *refs):
     came, (weight_grad, gain_grad) = refs[:count], refs[-2:]
-    term = own[0]
+    term = own[...]
     for ref in came:
         term = term + ref[...].astype(f32)
     product = term * weight[...].astype(f32)
@@ -161,7 +169,7 @@
     weight_grad[0] = term * gains[:, :1]
 
 
-def last_part(near, weight, gain, sums):
+def last_part(own, weight, gain, sums):
     shard, cols = weight.shape
     many = len(sums)
     tile = HEAD
@@ -170,12 +178,12 @@
     for h, came in enumerate(sums):
         row = lambda i, h=h: h * tiles + i
         specs = [
-            pl.BlockSpec((1, tile, cols), lambda i, row=row: (near.shape[0] - 1, row(i), 0)),
+            pl.BlockSpec((tile, cols), lambda i, row=row: (row(i), 0)),
             pl.BlockSpec((tile, cols), lambda i, row=row: (row(i), 0)),
             pl.BlockSpec((1, tile), lambda i, row=row: (0, row(i))),
         ]
         specs += [pl.BlockSpec((tile, cols), lambda i: (i, 0))] * len(came)
-        operands = [near, weight, gain, *came]
+        operands = [own, weight, gain, *came]
         if outs is not None:
             specs += [pl.BlockSpec(memory_space=pl.ANY)] * 2
         outs = pl.pallas_call(
@@ -204,63 +212,105 @@
     return outs
 
 
-def second_kernel(plan, at, x, kv_grad, inv, cosine, sine, *refs):
-    n = len(plan)
-    blocks, refs = refs[:-10], refs[-10:]
-    kv_out, input_grad, xs, ws, ng, pre, out, x_sem, w_sem, o_sem = refs
+def part_kernel(plan, before, finish, at, x, kv_grad, inv, cosine, sine, *refs):
+    here = len(plan)
+    done = sum(before)
+    n = done + here
+    total_at = len(refs) - (8 if not finish else 9)
+    blocks, refs = refs[:total_at], refs[total_at:]
+    if before:
+        pre0, sums0, *grads0 = blocks[: 2 + len(before)]
+        blocks = blocks[2 + len(before) :]
+    if finish:
+        kv_out, input_grad, xs, ws, ng, pre, x_sem, w_sem, g_sem = refs
+    else:
+        pre, sums, grads, xs, ws, x_sem, w_sem, g_sem = refs
     rows, width = x.shape
     shard = xs.shape[2]
     kvw = pre.shape[1] // 2
+    held = range(n) if finish else range(done, n)
+    base = held[0]
 
     def columns(k):
         return pl.ds(pl.multiple_of(at[k] * shard, shard), shard)
 
     def x_copy(k):
-        return pltpu.make_async_copy(x.at[:, columns(k)], xs.at[k], x_sem.at[k])
+        return pltpu.make_async_copy(x.at[:, columns(k)], xs.at[k - base], x_sem.at[k - base])
 
     def o_copy(k):
-        return pltpu.make_async_copy(out.at[k], input_grad.at[:, columns(k)], o_sem.at[k])
-
-    for k in range(n):
+        return pltpu.make_async_copy(xs.at[k], input_grad.at[:, columns(k)], x_sem.at[k])
+
+    for k in range(done, n):
         x_copy(k).start()
-        for flag, block, start, stop in plan[k]:
-            copy = pltpu.make_async_copy(blocks[block], ws.at[k, start:stop], w_sem.at[k])
+        for flag, block, start, stop in plan[k - done]:
+            slot = k - done
+            copy = pltpu.make_async_copy(blocks[block], ws.at[slot, start:stop], w_sem.at[slot])
             if flag is None:
                 copy.start()
             else:
 
-                @pl.when(at[n + flag] == 1)
+                @pl.when(at[at.shape[0] - FLAGS + flag] == 1)
                 def _(copy=copy):
                     copy.start()
 
-    pre[...] = jnp.zeros_like(pre)
-
-    def gather(k, total):
+    if before:
+        pre[...] = pre0[...]
+        start = sums0[...]
+    else:
+        pre[...] = jnp.zeros_like(pre)
+        start = jnp.zeros((rows, HEAD), f32)
+    loads = []
+    if finish:
+        slot = 0
+        for j, count in enumerate(before):
+            loads.append(
+                pltpu.make_async_copy(grads0[j], ng.at[slot : slot + count], g_sem.at[j])
+            )
+            slot += count
+        for load in loads:
+            load.start()
+        for k in range(done):
+            x_copy(k).start()
+
+    def gather(i, total):
+        k = done + i
         x_copy(k).wait()
-        pltpu.make_async_copy(ws.at[k], ws.at[k], w_sem.at[k]).wait()
-        weight = ws[k]
-        normed = xs[k].astype(f32) * inv[:, :1]
+        pltpu.make_async_copy(ws.at[i], ws.at[i], w_sem.at[i]).wait()
+        weight = ws[i]
+        normed = xs[k - base].astype(f32) * inv[:, :1]
         pre[...] += jnp.dot(normed.astype(bf16), weight, preferred_element_type=f32)
         grad = lax.dot_general(
             kv_grad[...], weight, (((1,), (1,)), ((), ())), preferred_element_type=f32
         )
-        ng[k] = grad
+        if finish:
+            ng[k] = grad
+        else:
+            grads[i] = grad
         product = grad * normed
         for c in range(0, shard, HEAD):
             total = total + product[:, c : c + HEAD]
         return total
 
-    total = lax.fori_loop(0, n, gather, jnp.zeros((rows, HEAD), f32))
+    total = lax.fori_loop(0, here, gather, start)
+    if not finish:
+        sums[...] = total
+        return
     mean = jnp.sum(total, axis=1, keepdims=True) / width
-
-    def finish(k, carry):
+    for load in loads:
+        load.wait()
+
+    def write(k, carry):
+        @pl.when(k < done)
+        def _():
+            x_copy(k).wait()
+
         scale = inv[:, :1]
         normed = xs[k].astype(f32) * scale
-        out[k] = (scale * (ng[k] - normed * mean)).astype(bf16)
+        xs[k] = (scale * (ng[k] - normed * mean)).astype(bf16)
         o_copy(k).start()
         return carry
 
-    lax.fori_loop(0, n, finish, 0)
+    lax.fori_loop(0, n, write, 0)
     for c in range(0, kvw, HEAD):
         part = pre[:, c : c + HEAD]
         turned = pltpu.roll(part, HEAD // 2, 1)
@@ -274,45 +324,57 @@
     lax.fori_loop(0, n, drain, 0)
 
 
-def second_part(ring, tokens_in, kv_grad, inv, cosine, sine, blocks, plan, flags, shard):
+def project_part(at, tokens_in, kv_grad, inv, cosine, sine, blocks, plan, carry, before, finish):
     rows, width = tokens_in.shape
     cols = kv_grad.shape[1]
-    n = ring.count
-    order = [0]
-    for d in range(1, ring.half):
-        order += [-d, d]
-    order.append(ring.half)
-    at = jnp.concatenate([ring.devices_at(order).astype(jnp.int32), flags.astype(jnp.int32)])
+    here = len(plan)
+    n = sum(before) + here
+    used = sorted({entry[1] for entries in plan for entry in entries})
+    plan = tuple(
+        tuple((flag, used.index(block), *rest) for flag, block, *rest in entries)
+        for entries in plan
+    )
+    blocks = [blocks[i] for i in used]
+    shard = plan[0][0][3] if len(plan[0]) == 1 else max(entry[3] for entry in plan[0])
     whole = pl.BlockSpec(memory_space=pltpu.VMEM)
     there = pl.BlockSpec(memory_space=pl.ANY)
-    return pl.pallas_call(
-        functools.partial(second_kernel, plan),
-        in_specs=[pl.BlockSpec(memory_space=pltpu.SMEM), there]
-        + [whole] * 4
-        + [there] * len(blocks),
-        out_specs=[whole, there],
-        out_shape=[
+    in_specs = [pl.BlockSpec(memory_space=pltpu.SMEM), there] + [whole] * 4
+    in_specs += [whole, whole][: 2 if before else 0] + [there] * (len(before) + len(blocks))
+    slots = n if finish else here
+    scratch = [
+        pltpu.VMEM((slots, rows, shard), bf16),
+        pltpu.VMEM((here, shard, cols), bf16),
+    ]
+    if finish:
+        scratch += [pltpu.VMEM((n, rows, shard), f32), pltpu.VMEM((rows, cols), f32)]
+        out_specs = [whole, there]
+        out_shape = [
             jax.ShapeDtypeStruct((rows, cols), bf16),
             jax.ShapeDtypeStruct((rows, width), bf16),
-        ],
-        scratch_shapes=[
-            pltpu.VMEM((n, rows, shard), bf16),
-            pltpu.VMEM((n, shard, cols), bf16),
-            pltpu.VMEM((n, rows, shard), f32),
-            pltpu.VMEM((rows, cols), f32),
-            pltpu.VMEM((n, rows, shard), bf16),
-            pltpu.SemaphoreType.DMA((n,)),
-            pltpu.SemaphoreType.DMA((n,)),
-            pltpu.SemaphoreType.DMA((n,)),
-        ],
+        ]
+    else:
+        out_specs = [whole] * 3
+        out_shape = [
+            jax.ShapeDtypeStruct((rows, cols), f32),
+            jax.ShapeDtypeStruct((rows, HEAD), f32),
+            jax.ShapeDtypeStruct((here, rows, shard), f32),
+        ]
+    scratch += [pltpu.SemaphoreType.DMA((slots,)), pltpu.SemaphoreType.DMA((here,))]
+    scratch += [pltpu.SemaphoreType.DMA((max(len(before), 1),))]
+    return pl.pallas_call(
+        functools.partial(part_kernel, plan, tuple(before), finish),
+        in_specs=in_specs,
+        out_specs=out_specs,
+        out_shape=out_shape,
+        scratch_shapes=scratch,
         compiler_params=pltpu.CompilerParams(vmem_limit_bytes=48 * 2**20),
         cost_estimate=pl.CostEstimate(
-            flops=4 * rows * width * cols,
-            bytes_accessed=4 * rows * width + 2 * width * cols,
+            flops=4 * rows * shard * here * cols,
+            bytes_accessed=4 * rows * width + 2 * shard * here * cols,
             transcendentals=0,
         ),
-        name="project_and_input_grad",
-    )(at, tokens_in, kv_grad, inv, cosine, sine, *blocks)
+        name="project_last" if finish else "project_first",
+    )(at, tokens_in, kv_grad, inv, cosine, sine, *carry, *blocks)
 
 
 def replica_pairs(value, odd):
@@ -329,7 +391,7 @@
     return jnp.where(odd, theirs, mine), jnp.where(odd, mine, theirs)
 
 
-def exchange_ring(ring, own, far, near, pseudo):
+def exchange_ring(ring, own, far, near, pseudo, project):
     total = lax.psum(pseudo, "replica")
     shard, cut = own.shape[0], own.shape[0] // 2
     blocks = [own]
@@ -353,10 +415,14 @@
         from_left = ring.to_right((near[k] + from_left.astype(f32)).astype(bf16))
         from_right = ring.to_left((near[k + 1] + from_right.astype(f32)).astype(bf16))
     sums = [(from_left, from_right)]
-    return blocks, plan, jnp.zeros((1,), jnp.int32), sums, total
-
-
-def exchange_plane(plane, own, far, near, pseudo):
+    return project(blocks, tuple(plan), (), (), True), sums, total
+
+
+ORDER = {"sum": (0, 1), "inner": (3, 8), "far": (0, 5), "partner0": (4, None), "partner1": (6, None), "first": (2, 4)}
+CHAIN = True
+
+
+def exchange_plane(plane, own, far, near, pseudo, project):
     shard = own.shape[0]
     at0, at1, at2, at3 = plane.at
     zero = jnp.zeros((), f32)
@@ -364,97 +430,99 @@
     halves = range(2)
     wide = lambda v: v.astype(f32)
     pick = jnp.where
-    sent = [own]
+    sent, crossed, beside = [own], [own], {}
 
     def part(value, h):
         return value[pieces[h][0] : pieces[h][1]]
 
-    def later(*values):
-        return after(values, sent[0])
-
-    def ring(to_right, to_left):
+    def chord(value):
+        crossed[0] = plane.over_chord(after(value, sent[0], crossed[0] if CHAIN else own))
+        return crossed[0]
+
+    def ring(step, to_right, to_left):
         sent[0] = to_right, to_left
-        return lax.optimization_barrier([plane.to_right(to_right), plane.to_left(to_left)])
-
-    def chord(value, *others):
-        return plane.over_chord(after(value, sent[0], *others))
-
-    first = ring(own, own)
+        came = lax.optimization_barrier([plane.to_right(to_right), plane.to_left(to_left)])
+        for name, (begin, _) in ORDER.items():
+            if begin == step:
+                beside[name] = tasks[name]()
+        return came
+
+    def later(step, *values):
+        names = [name for name, (_, end) in ORDER.items() if end == step]
+        awaited = [beside[name] for name in names]
+        values, awaited = lax.optimization_barrier((after(values, sent[0]), awaited))
+        beside.update(zip(names, awaited))
+        return values
+
+    def for_partner(h):
+        return pick(at1, part(near[1], h), part(near[0], h)).astype(bf16)
+
+    def first_blocks():
+        gated = after(blocks[0], sent[0])
+        return project([gated, *blocks[1:]], plan[:5], (), (), False)
+
+    tasks = {
+        "sum": lambda: replica_halves(after(mine, sent[0]) + came, odd),
+        "far": lambda: chord(pick(at2, *first)),
+        "inner": lambda: chord(far),
+        "partner0": lambda: chord(for_partner(0)),
+        "partner1": lambda: chord(for_partner(1)),
+        "first": first_blocks,
+    }
+
+    first = ring(None, own, own)
     partner = chord(own)
     odd = lax.axis_index("replica") % 2 == 1
-    sum_over = lax.axis_size("replica") == 4
-    if sum_over:
+    if lax.axis_size("replica") == 4:
         mine, came = replica_pairs(after(pseudo, own), odd.astype(jnp.int32))
     else:
-        came = total = lax.psum(pseudo, "replica")
+        came = lax.psum(pseudo, "replica")
+        tasks["sum"] = lambda: came
     first, partner, far, came = lax.optimization_barrier((first, partner, far, came))
-    one = [[part(side, h) for side in first] for h in halves]
-    two = [ring(*later(*one[0]))]
-    if sum_over:
-        total = replica_halves(mine + came, odd)
-    one[1], total = lax.optimization_barrier((one[1], total))
-    two.append(ring(*later(*one[1])))
-    from_inner = chord(far, total)
+    two = [ring(0, *(part(side, 0) for side in first))]
+    two.append(ring(1, *(part(side, 1) for side in later(1, *first))))
+    blocks = [own, *first, *(two[h][way] for way in range(2) for h in halves)]
+    plan = [((None, k, 0, shard),) for k in range(3)]
+    plan += [tuple((None, 3 + 2 * way + h, *pieces[h]) for h in halves) for way in range(2)]
     three = []
     for h in halves:
-        left, right = later(*two[h])
+        left, right = later(2 + h, *two[h])
         terms = part(far, h)
-        three.append(ring(pick(at0, terms, left), pick(at3, terms, right)))
-    three[0], from_inner = lax.optimization_barrier((three[0], from_inner))
+        three.append(ring(2 + h, pick(at0, terms, left), pick(at3, terms, right)))
     four = []
     for h in halves:
-        left, right = later(*three[h])
+        left, right = later(4 + h, *three[h])
         to_right = wide(part(near[0], h)) + pick(at1, wide(left), zero)
         to_left = wide(part(near[1], h)) + pick(at2, wide(right), zero)
         to_right = pick(at2, left, to_right.astype(bf16))
         to_left = pick(at1, right, to_left.astype(bf16))
-        four.append(ring(to_right, to_left))
-        if h == 0:
-            join = jnp.concatenate([pick(at2, *one[g]) for g in halves])
-            far_inner = chord(join, from_inner)
+        four.append(ring(4 + h, to_right, to_left))
     five = []
     for h in halves:
-        if h == 1:
-            four[1], far_inner = lax.optimization_barrier((four[1], far_inner))
-        left, right = later(*four[h])
+        left, right = later(6 + h, *four[h])
         to_right = part(near[2], h) + pick(at3, zero, wide(left))
         to_left = part(near[3], h) + pick(at0, zero, wide(right))
-        five.append(ring(to_right.astype(bf16), to_left.astype(bf16)))
-    six, from_partner = [], []
+        five.append(ring(6 + h, to_right.astype(bf16), to_left.astype(bf16)))
+    six = []
     for h in halves:
-        for_partner = pick(at1, part(near[1], h), part(near[0], h)).astype(bf16)
-        from_partner.append(chord(for_partner, far_inner, *from_partner))
-        left, right = later(*five[h])
-        over = wide(part(from_inner, h))
+        left, right = later(8 + h, *five[h])
+        over = wide(part(beside["inner"], h))
         to_right = part(near[4], h) + wide(left) + pick(at1, over, zero)
         to_left = part(near[5], h) + wide(right) + pick(at2, over, zero)
-        six.append(ring(to_right.astype(bf16), to_left.astype(bf16)))
-    sums = [(*six[h], from_partner[h]) for h in halves]
-
-    blocks, plan = [], []
-
-    def add(flag, arrays):
-        entry = []
-        for (start, stop), array in zip(pieces, arrays):
-            entry.append((flag, len(blocks), start, stop))
-            blocks.append(array)
-        return entry
-
-    for array in (own, *first, partner):
-        plan.append([(None, len(blocks), 0, shard)])
-        blocks.append(array)
-    plan.pop()
-    for way in range(2):
-        plan.append(add(None, [two[h][way] for h in halves]))
-    for way in range(2):
-        plan.append([(way, 3, 0, shard)] + add(2 + way, [three[h][way] for h in halves]))
-    plan.append([(4, len(blocks), 0, shard)])
-    blocks.append(far_inner)
-    for way in range(2):
-        plan[-1] += add(5 + way, [four[h][way] for h in halves])
-    flags = [at1, at2, ~at1, ~at2, at1 | at2, at3, at0]
-    plan = tuple(tuple(entry) for entry in plan)
-    return blocks, plan, jnp.stack(flags), sums, total
+        six.append(ring(8 + h, to_right.astype(bf16), to_left.astype(bf16)))
+    sums = [(*six[h], beside["partner%d" % h]) for h in halves]
+
+    blocks = [partner, beside["far"]] + [
+        steps[h][way] for steps in (three, four) for way in range(2) for h in halves
+    ]
+    ways = lambda flag, at: tuple((flag, at + h, *pieces[h]) for h in halves)
+    plan = (
+        ((0, 0, 0, shard), *ways(2, 2)),
+        ((1, 0, 0, shard), *ways(3, 4)),
+        ((4, 1, 0, shard), *ways(5, 6), *ways(6, 8)),
+    )
+    outs = project(blocks, plan, beside["first"], (5,), True)
+    return outs, sums, beside["sum"]
 
 
 def local(
@@ -480,14 +548,26 @@
     positions = (ring.me * rows + jnp.arange(rows, dtype=jnp.int32)) % SEQ_LEN
     cosine, sine = rope_tables(positions)
     scale = 1.0 / math.sqrt(rows * ring.count)
-    kv_grad, inv, far, near = first_part(
+    kv_grad, inv, far, near, last = first_part(
         ring, tokens_in, cotangent, cosine, sine, shard, scale
     )
+    order = [0]
+    for d in range(1, ring.half):
+        order += [-d, d]
+    order.append(ring.half)
+    at = [ring.devices_at(order).astype(jnp.int32)]
+    if small:
+        at0, at1, at2, at3 = ring.at
+        flags = [at1, at2, ~at1, ~at2, at1 | at2, at3, at0]
+        at.append(jnp.stack(flags).astype(jnp.int32))
+    at = jnp.concatenate(at)
+
+    def project(*args):
+        return project_part(at, tokens_in, kv_grad, inv, cosine, sine, *args)
+
     exchange = exchange_plane if small else exchange_ring
-    blocks, plan, flags, sums, total = exchange(
-        ring, own, far, near, pseudo_grad[0]
-    )
-    weight_grad, gain_grad = last_part(near, weight_shard, norm_gain, sums)
+    (kv_out, input_grad), sums, total = exchange(ring, own, far, near, pseudo_grad[0], project)
+    weight_grad, gain_grad = last_part(last, weight_shard, norm_gain, sums)
 
     if isinstance(total, tuple):
         total = jnp.concatenate(total)
@@ -498,9 +578,6 @@
         mixing_rate * local_params[0].astype(f32) + (1.0 - mixing_rate) * global_new
     ).astype(bf16)
 
-    kv_out, input_grad = second_part(
-        ring, tokens_in, kv_grad, inv, cosine, sine, blocks, plan, flags, shard
-    )
     return (
         kv_out[None],
         input_grad[None],

time: 181 us -> 161 us (0.89)
  waiting for transfers between devices: 60.4 us -> 42.2 us
  other arithmetic: 38.3 us -> 27.2 us
  Pallas kernels: 32.3 us -> 37.9 us
  starting transfers between devices: 40 us -> 42.3 us
    ppermute x11, waiting for transfers between devices: 14.5 us -> 0.28 us  [to_right(): return lax.ppermute(value, 'fsdp', self.right)]
    ppermute x11, waiting for transfers between devices: 42.5 us -> 36.7 us  [to_left(): return lax.ppermute(value, 'fsdp', self.left)]
    pallas_call x1 -> x2, Pallas kernels: 17.7 us -> 23.1 us  [project_part(): pl.pallas_call(functools.partial(part_kernel, plan, tuple(before), finish...]
    slice x0 -> x4, local copies, waits for them, and re-layouts: none -> 5.19 us  [part(): return value[pieces[h][0]:pieces[h][1]]]
    select_n x4 -> x3, other arithmetic: 6.34 us -> 1.51 us  [the longest x1 1.34 us: exchange_plane(): pick(at2, *first)]
    unnamed x42 -> x30, local copies, waits for them, and re-layouts: 8.22 us -> 3.47 us
    convert_element_type x6, other arithmetic: 14.2 us -> 11.7 us  [the longest x2 4.07 us: exchange_plane(): six.append(ring(8 + h, to_right.astype(bf16), to_left.astype(bf16)))]
    ppermute x5, starting transfers between devices: 15.8 us -> 18.1 us  [over_chord(): return lax.ppermute(value, 'fsdp', [(2, 3), (3, 2), (4, 5), (5, 4)])]
  transfers between devices with their start and end apart: 30 -> 30, of which waited for: 16 -> 13; matrix products, arithmetic and copies ran while one was open for 16% -> 15% of each run, Pallas kernels for 17% -> 23%
where the time goes in v10:
time: 161 us
  starting transfers between devices  42.3 us (26%)
  waiting for transfers between devices  42.2 us (26%)
  Pallas kernels  37.9 us (24%)
  other arithmetic  27.2 us (17%)
  local copies, waits for them, and re-layouts  9.72 us (6%)
    ppermute x11, waiting for transfers between devices, to_left(): return lax.ppermute(value, 'fsdp', self.left)  36.7 us
    pallas_call x2, Pallas kernels, project_part(): pl.pallas_call(functools.partial(part_kernel, plan, tuple(before), finish...  23.1 us
    ppermute x5, starting transfers between devices, over_chord(): return lax.ppermute(value, 'fsdp', [(2, 3), (3, 2), (4, 5), (5, 4)])  18.1 us
    ppermute x11, starting transfers between devices, to_right(): return lax.ppermute(value, 'fsdp', self.right)  17.5 us
    pallas_call x1, Pallas kernels, first_part(): pl.pallas_call(functools.partial(first_kernel, scale), grid_spec=pltpu.Pr...  12 us
    ppermute x11, starting transfers between devices, to_left(): return lax.ppermute(value, 'fsdp', self.left)  5.27 us
    ppermute x5, waiting for transfers between devices, over_chord(): return lax.ppermute(value, 'fsdp', [(2, 3), (3, 2), (4, 5), (5, 4)])  5.24 us
    slice x4, local copies, waits for them, and re-layouts, part(): return value[pieces[h][0]:pieces[h][1]]  5.19 us
  transfers between devices with their start and end apart: 30, of which 13 were waited for; matrix products, arithmetic and copies ran while one was open for 15% of the time, Pallas kernels for 23%

profile of v10, /device:TPU:8, one launch (start us, length us, event | category | flops | bytes accessed | tf_op | source)
XLA Modules:
  0.0 160.5 jit_solution(12705177596868833635)
XLA Ops:
  1.5 2.4 %multiply_convert_fusion.refs_0_ = bf16[512,1024]{1,0:T(8,128)(2,1)} fusion(f32[512]{0:T(512)S(1)} %bitcast.92, bf16[1,512,1024]{2,1,0:T(8,128)(2,1)} %param.12), kind=kLoop, calls=%fused_computation | loop fusion | flops 1572864 | bytes 2099200 | tf_op jit(solution)/shard_map/convert_element_type | solution.py:547
  4.9 2.0 %collective-permute-start = (bf16[512,1024]{1,0:T(8,128)(2,1)}, bf16[512,1024]{1,0:T(8,128)(2,1)}, u32[]{:S(2)}, u32[]{:S(2)}) collective-permute-start(bf16[512,1024]{1,0:T(8,128)(2,1)} %multiply_convert_fusion.refs_0_), channel_id=1, source_target_pairs={{0,2},{2,4},{4,6},{6,7},{7,5},{5,3},{3,1},{1,0},{8,10},{10,12},{12... | collective-permute-start | bytes 3145736 | tf_op jit(solution)/shard_map/ppermute | solution.py:44
  6.9 3.4 %collective-permute-start.2 = (bf16[512,1024]{1,0:T(8,128)(2,1)}, bf16[512,1024]{1,0:T(8,128)(2,1)}, u32[]{:S(2)}, u32[]{:S(2)}) collective-permute-start(bf16[512,1024]{1,0:T(8,128)(2,1)} %multiply_convert_fusion.refs_0_), channel_id=1, source_target_pairs={{2,3},{3,2},{4,5},{5,4},{10,11},{11,10},{12,13},{13,12},{18,19},{1... | collective-permute-start | bytes 3145736 | tf_op jit(solution)/shard_map/ppermute | solution.py:56
  11.3 1.5 collective-permute-start.4
  14.1 2.2 %copy-done.1 = bf16[1,512,4096]{2,1,0:T(8,128)(2,1)S(1)} copy-done((bf16[1,512,4096]{2,1,0:T(8,128)(2,1)S(1)}, bf16[1,512,4096]{2,1,0:T(8,128)(2,1)}, u32[]{:S(2)}) %copy-start.1) | copy-done | bytes 4194328
  16.3 1.2 copy-done.7
  17.5 12.0 %norm_and_weight_terms.1 = (bf16[512,1024]{1,0:T(8,128)(2,1)S(1)}, f32[512,128]{1,0:T(8,128)S(1)}, bf16[512,1024]{1,0:T(8,128)(2,1)S(1)}, f32[6,512,1024]{2,1,0:T(8,128)}, f32[512,1024]{1,0:T(8,128)S(1)}) custom-call(s32[8]{0:T(128)S(1)} %compare_select_fusion.4.at, bf16[512,4096]{1,0:T(8,128)(2,1)S(1)} %bitcast.88, bf16[512,1024]{1,0:T(8,128)(2,1)S(1)} %bitcast.89, ...), custom_call_target="tpu_custom_call" | custom-call | flops 4294967296 | bytes 20971520 | tf_op jit(solution)/shard_map/norm_and_weight_terms/pallas_call | solution.py:121
  29.6 1.2 collective-permute-done.1.refs_2_
  30.7 3.3 %collective-permute-done.2.refs_3_ = bf16[512,1024]{1,0:T(8,128)(2,1)} collective-permute-done((bf16[512,1024]{1,0:T(8,128)(2,1)}, bf16[512,1024]{1,0:T(8,128)(2,1)}, u32[]{:S(2)}, u32[]{:S(2)}) %collective-permute-start.2) | collective-permute-done | bytes 1048608 | tf_op jit(solution)/shard_map/ppermute | solution.py:56
  34.1 1.1 slice.129
  35.2 1.9 %slice.130 = bf16[256,1024]{1,0:T(8,128)(2,1)} slice(bf16[512,1024]{1,0:T(8,128)(2,1)} %collective-permute-done.1.refs_2_), slice={[0:256], [0:1024]} | slice | bytes 1048576 | tf_op jit(solution)/shard_map/slice | solution.py:436
  37.0 2.4 %add.148 = f32[192,1024]{1,0:T(8,128)} add(f32[192,1024]{1,0:T(8,128)} %dynamic-slice_add_fusion, f32[192,1024]{1,0:T(8,128)} %collective-permute-done.4) | non-fusion elementwise | flops 196608 | bytes 2359296 | tf_op jit(solution)/shard_map/add | solution.py:465
  39.6 2.0 %collective-permute-start.5 = (bf16[256,1024]{1,0:T(8,128)(2,1)S(1)}, bf16[256,1024]{1,0:T(8,128)(2,1)S(1)}, u32[]{:S(2)}, u32[]{:S(2)}) collective-permute-start(bf16[256,1024]{1,0:T(8,128)(2,1)S(1)} %slice.129), channel_id=1, source_target_pairs={{0,2},{2,4},{4,6},{6,7},{7,5},{5,3},{3,1},{1,0},{8,10},{10,12},{12... | collective-permute-start | bytes 1572872 | tf_op jit(solution)/shard_map/ppermute | solution.py:44
  41.6 1.3 broadcast_select_fusion
  43.0 3.4 %collective-permute-start.14 = (bf16[512,1024]{1,0:T(8,128)(2,1)S(1)}, bf16[512,1024]{1,0:T(8,128)(2,1)S(1)}, u32[]{:S(2)}, u32[]{:S(2)}) collective-permute-start(bf16[512,1024]{1,0:T(8,128)(2,1)S(1)} %broadcast_select_fusion), channel_id=1, source_target_pairs={{2,3},{3,2},{4,5},{5,4},{10,11},{11,10},{12,13},{13,12},{18,19},{1... | collective-permute-start | bytes 3145736 | tf_op jit(solution)/shard_map/ppermute | solution.py:56
  46.4 1.6 broadcast_select_fusion.5
  48.0 1.2 slice.131
  49.2 1.1 slice.132
  50.3 2.0 %collective-permute-start.10 = (bf16[256,1024]{1,0:T(8,128)(2,1)S(1)}, bf16[256,1024]{1,0:T(8,128)(2,1)S(1)}, u32[]{:S(2)}, u32[]{:S(2)}) collective-permute-start(bf16[256,1024]{1,0:T(8,128)(2,1)S(1)} %slice.131), channel_id=1, source_target_pairs={{0,2},{2,4},{4,6},{6,7},{7,5},{5,3},{3,1},{1,0},{8,10},{10,12},{12... | collective-permute-start | bytes 1572872 | tf_op jit(solution)/shard_map/ppermute | solution.py:44
  52.4 2.1 %collective-permute-done.6.refs_5_ = bf16[256,1024]{1,0:T(8,128)(2,1)S(1)} collective-permute-done((bf16[256,1024]{1,0:T(8,128)(2,1)}, bf16[256,1024]{1,0:T(8,128)(2,1)S(1)}, u32[]{:S(2)}, u32[]{:S(2)}) %collective-permute-start.6) | collective-permute-done | bytes 524320 | tf_op jit(solution)/shard_map/ppermute | solution.py:47
  54.7 1.3 collective-permute-start.9
  56.7 9.0 %collective-permute-done.11.refs_6_ = bf16[256,1024]{1,0:T(8,128)(2,1)S(1)} collective-permute-done((bf16[256,1024]{1,0:T(8,128)(2,1)S(1)}, bf16[256,1024]{1,0:T(8,128)(2,1)S(1)}, u32[]{:S(2)}, u32[]{:S(2)}) %collective-permute-start.11) | collective-permute-done | bytes 524320 | tf_op jit(solution)/shard_map/ppermute | solution.py:47
  65.9 1.3 collective-permute-start.13
  68.0 1.9 %collective-permute-done.14.refs_4_ = bf16[512,1024]{1,0:T(8,128)(2,1)S(1)} collective-permute-done((bf16[512,1024]{1,0:T(8,128)(2,1)S(1)}, bf16[512,1024]{1,0:T(8,128)(2,1)S(1)}, u32[]{:S(2)}, u32[]{:S(2)}) %collective-permute-start.14) | collective-permute-done | bytes 1048608 | tf_op jit(solution)/shard_map/ppermute | solution.py:56
  69.8 3.4 %collective-permute-start.23 = (bf16[512,1024]{1,0:T(8,128)(2,1)S(1)}, bf16[512,1024]{1,0:T(8,128)(2,1)S(1)}, u32[]{:S(2)}, u32[]{:S(2)}) collective-permute-start(bf16[512,1024]{1,0:T(8,128)(2,1)S(1)} %copy-done.5), channel_id=1, source_target_pairs={{2,3},{3,2},{4,5},{5,4},{10,11},{11,10},{12,13},{13,12},{18,19},{1... | collective-permute-start | bytes 3145736 | tf_op jit(solution)/shard_map/ppermute | solution.py:56
  73.3 11.5 %project_first.1 = (f32[512,1024]{1,0:T(8,128)}, f32[512,128]{1,0:T(8,128)S(1)}, f32[5,512,512]{2,1,0:T(8,128)}) custom-call(s32[15]{0:T(128)S(1)} %pad_add_fusion.at, bf16[512,4096]{1,0:T(8,128)(2,1)} %bitcast.86, bf16[512,1024]{1,0:T(8,128)(2,1)S(1)} %copy-done.3, f32[512,128]{1,0:T(8,128)S(1)} %get-tuple-element.100.inv, ...), custom_call_target="tpu_custom_call" | custom-call | flops 5368709120 | bytes 13631488 | tf_op jit(solution)/shard_map/project_first/pallas_call | solution.py:364
  84.8 2.0 %fusion.21 = (bf16[256,1024]{1,0:T(8,128)(2,1)S(1)}, bf16[256,1024]{1,0:T(8,128)(2,1)S(1)}) fusion(bf16[256,1024]{1,0:T(8,128)(2,1)S(1)} %collective-permute-done.9.refs_7_, f32[6,512,1024]{2,1,0:T(8,128)} %get-tuple-element.142, pred[]{:T(512)} %eq.31, pred[]{:T(512)} %eq.32, bf16[256,1024]{1,0:T(8,128)(2,1)S(1)} %collective-permute-done.8.refs_5_), kind=kLoop, calls=%fused_computation.45 | loop fusion | flops 2621440 | bytes 4194306 | tf_op jit(solution)/shard_map/jit(_where)/select_n | solution.py:498
  86.8 2.0 %collective-permute-start.15 = (bf16[256,1024]{1,0:T(8,128)(2,1)S(1)}, bf16[256,1024]{1,0:T(8,128)(2,1)S(1)}, u32[]{:S(2)}, u32[]{:S(2)}) collective-permute-start(bf16[256,1024]{1,0:T(8,128)(2,1)S(1)} %get-tuple-element.207), channel_id=1, source_target_pairs={{0,2},{2,4},{4,6},{6,7},{7,5},{5,3},{3,1},{1,0},{8,10},{10,12},{12... | collective-permute-start | bytes 1572872 | tf_op jit(solution)/shard_map/ppermute | solution.py:44
  88.8 3.8 %fusion.18 = (bf16[256,1024]{1,0:T(8,128)(2,1)S(1)}, bf16[256,1024]{1,0:T(8,128)(2,1)S(1)}, bf16[256,1024]{1,0:T(8,128)(2,1)S(1)}, bf16[256,1024]{1,0:T(8,128)(2,1)S(1)}) fusion(f32[6,512,1024]{2,1,0:T(8,128)} %get-tuple-element.142, pred[]{:T(512)} %eq.31, bf16[256,1024]{1,0:T(8,128)(2,1)S(1)} %collective-permute-done.13.refs_8_, pred[]{:T(512)} %eq.32, ...), kind=kLoop, calls=%fused_computation.40 | loop fusion | flops 3145728 | bytes 7340034 | tf_op jit(solution)/shard_map/convert_element_type | solution.py:458
  93.4 1.3 collective-permute-start.17
  94.6 7.0 %collective-permute-done.16.refs_11_ = bf16[256,1024]{1,0:T(8,128)(2,1)S(1)} collective-permute-done((bf16[256,1024]{1,0:T(8,128)(2,1)S(1)}, bf16[256,1024]{1,0:T(8,128)(2,1)S(1)}, u32[]{:S(2)}, u32[]{:S(2)}) %collective-permute-start.16) | collective-permute-done | bytes 524320 | tf_op jit(solution)/shard_map/ppermute | solution.py:47
  101.7 1.9 %fusion.11 = (bf16[256,1024]{1,0:T(8,128)(2,1)S(1)}, bf16[256,1024]{1,0:T(8,128)(2,1)S(1)}) fusion(bf16[256,1024]{1,0:T(8,128)(2,1)S(1)} %collective-permute-done.16.refs_11_, f32[6,512,1024]{2,1,0:T(8,128)} %get-tuple-element.142, pred[]{:T(512)} %eq.34, bf16[256,1024]{1,0:T(8,128)(2,1)S(1)} %collective-permute-done.15.refs_9_, pred[]{:T(512)} %eq.33), kind=kLoop, calls=%fused_computation.25 | loop fusion | flops 2097152 | bytes 4194306 | tf_op jit(solution)/shard_map/convert_element_type | solution.py:505
  104.2 1.5 collective-permute-start.21
  105.7 7.2 %collective-permute-done.18.refs_12_ = bf16[256,1024]{1,0:T(8,128)(2,1)S(1)} collective-permute-done((bf16[256,1024]{1,0:T(8,128)(2,1)S(1)}, bf16[256,1024]{1,0:T(8,128)(2,1)S(1)}, u32[]{:S(2)}, u32[]{:S(2)}) %collective-permute-start.18) | collective-permute-done | bytes 524320 | tf_op jit(solution)/shard_map/ppermute | solution.py:47
  112.9 1.9 %fusion.10 = (bf16[256,1024]{1,0:T(8,128)(2,1)S(1)}, bf16[256,1024]{1,0:T(8,128)(2,1)S(1)}) fusion(bf16[256,1024]{1,0:T(8,128)(2,1)S(1)} %collective-permute-done.18.refs_12_, f32[6,512,1024]{2,1,0:T(8,128)} %get-tuple-element.142, pred[]{:T(512)} %eq.34, bf16[256,1024]{1,0:T(8,128)(2,1)S(1)} %collective-permute-done.17.refs_10_, pred[]{:T(512)} %eq.33), kind=kLoop, calls=%fused_computation.23 | loop fusion | flops 2097152 | bytes 4194306 | tf_op jit(solution)/shard_map/convert_element_type | solution.py:505
  115.4 1.5 collective-permute-start.19
  116.9 7.2 %collective-permute-done.22 = bf16[256,1024]{1,0:T(8,128)(2,1)S(1)} collective-permute-done((bf16[256,1024]{1,0:T(8,128)(2,1)S(1)}, bf16[256,1024]{1,0:T(8,128)(2,1)S(1)}, u32[]{:S(2)}, u32[]{:S(2)}) %collective-permute-start.22) | collective-permute-done | bytes 524320 | tf_op jit(solution)/shard_map/ppermute | solution.py:47
  124.2 4.0 %collective-permute-start.26 = (bf16[256,1024]{1,0:T(8,128)(2,1)S(1)}, bf16[256,1024]{1,0:T(8,128)(2,1)S(1)}, u32[]{:S(2)}, u32[]{:S(2)}) collective-permute-start(bf16[256,1024]{1,0:T(8,128)(2,1)S(1)} %get-tuple-element.181), channel_id=1, source_target_pairs={{2,3},{3,2},{4,5},{5,4},{10,11},{11,10},{12,13},{13,12},{18,19},{1... | collective-permute-start | bytes 1572872 | tf_op jit(solution)/shard_map/ppermute | solution.py:56
  128.1 2.0 %fusion.5 = (bf16[256,1024]{1,0:T(8,128)(2,1)S(1)}, bf16[256,1024]{1,0:T(8,128)(2,1)S(1)}) fusion(bf16[256,1024]{1,0:T(8,128)(2,1)S(1)} %collective-permute-done.22, f32[6,512,1024]{2,1,0:T(8,128)} %get-tuple-element.142, pred[]{:T(512)} %eq.32, bf16[512,1024]{1,0:T(8,128)(2,1)S(1)} %collective-permute-done.23, pred[]{:T(512)} %eq.31, ...), kind=kLoop, calls=%fused_computation.14 | loop fusion | flops 2883584 | bytes 4718594 | tf_op jit(solution)/shard_map/convert_element_type | solution.py:512
  130.3 2.0 %collective-permute-start.28 = (bf16[256,1024]{1,0:T(8,128)(2,1)S(1)}, bf16[256,1024]{1,0:T(8,128)(2,1)S(1)}, u32[]{:S(2)}, u32[]{:S(2)}) collective-permute-start(bf16[256,1024]{1,0:T(8,128)(2,1)S(1)} %get-tuple-element.197), channel_id=1, source_target_pairs={{0,2},{2,4},{4,6},{6,7},{7,5},{5,3},{3,1},{1,0},{8,10},{10,12},{12... | collective-permute-start | bytes 1572872 | tf_op jit(solution)/shard_map/ppermute | solution.py:44
  132.3 3.1 %collective-permute-done.20 = bf16[256,1024]{1,0:T(8,128)(2,1)S(1)} collective-permute-done((bf16[256,1024]{1,0:T(8,128)(2,1)S(1)}, bf16[256,1024]{1,0:T(8,128)(2,1)S(1)}, u32[]{:S(2)}, u32[]{:S(2)}) %collective-permute-start.20) | collective-permute-done | bytes 524320 | tf_op jit(solution)/shard_map/ppermute | solution.py:47
  135.4 2.0 %fusion.9 = (bf16[256,1024]{1,0:T(8,128)(2,1)S(1)}, bf16[256,1024]{1,0:T(8,128)(2,1)S(1)}) fusion(bf16[256,1024]{1,0:T(8,128)(2,1)S(1)} %collective-permute-done.20, f32[6,512,1024]{2,1,0:T(8,128)} %get-tuple-element.142, pred[]{:T(512)} %eq.32, bf16[512,1024]{1,0:T(8,128)(2,1)S(1)} %collective-permute-done.23, pred[]{:T(512)} %eq.31, ...), kind=kLoop, calls=%fused_computation.18 | loop fusion | flops 2883584 | bytes 4718594 | tf_op jit(solution)/shard_map/convert_element_type | solution.py:512
  138.0 1.5 collective-permute-start.24
  139.5 4.0 %collective-permute-start.27 = (bf16[256,1024]{1,0:T(8,128)(2,1)S(1)}, bf16[256,1024]{1,0:T(8,128)(2,1)S(1)}, u32[]{:S(2)}, u32[]{:S(2)}) collective-permute-start(bf16[256,1024]{1,0:T(8,128)(2,1)S(1)} %get-tuple-element.182), channel_id=1, source_target_pairs={{2,3},{3,2},{4,5},{5,4},{10,11},{11,10},{12,13},{13,12},{18,19},{1... | collective-permute-start | bytes 1572872 | tf_op jit(solution)/shard_map/ppermute | solution.py:56
  143.5 2.5 %fusion.24 = (bf16[1,384,1024]{2,1,0:T(8,128)(2,1)}, f32[384,1024]{1,0:T(8,128)}, f32[384,1024]{1,0:T(8,128)}) fusion(bf16[1,384,1024]{2,1,0:T(8,128)(2,1)S(1)} %copy-done.12, f32[384,1024]{1,0:T(8,128)S(1)} %copy-done.8, f32[192,1024]{1,0:T(8,128)S(1)} %get-tuple-element.190, f32[192,1024]{1,0:T(8,128)S(1)} %get-tuple-element.189, f32[384,1024]{1,0:T(8,128)S(1)} %copy-done.9), kind=kLoop, calls=%fused_computation.48 | loop fusion | flops 4718592 | bytes 9437184 | tf_op jit(solution)/shard_map/broadcast_in_dim | solution.py:588
  146.0 11.6 %project_last.1 = (bf16[512,1024]{1,0:T(8,128)(2,1)}, bf16[512,4096]{1,0:T(8,128)(2,1)}) custom-call(s32[15]{0:T(128)S(1)} %pad_add_fusion.at, bf16[512,4096]{1,0:T(8,128)(2,1)} %bitcast.87, bf16[512,1024]{1,0:T(8,128)(2,1)} %copy-done.2, f32[512,128]{1,0:T(8,128)S(1)} %get-tuple-element.100.inv, f32[512,128]{1,0:T(8,128)S(1)} %get-tuple-element.217.cosine, ...), custom_call_target="tpu_custom_call" | custom-call | flops 3221225472 | bytes 11534336 | tf_op jit(solution)/shard_map/project_last/pallas_call | solution.py:364
  157.7 1.4 sum_of_terms.2
  159.1 1.4 sum_of_terms.3
  (76 shorter events, 8.9 us)
Async XLA Ops:
  0.6 3.3 %copy-start.10 = (f32[1,384,1024]{2,1,0:T(8,128)S(1)}, f32[1,384,1024]{2,1,0:T(8,128)}, u32[]{:S(2)}) copy-start(f32[1,384,1024]{2,1,0:T(8,128)} %param.14) | copy-start | bytes 4718596
  4.9 5.5 %collective-permute-start.3 = (f32[192,1024]{1,0:T(8,128)}, f32[192,1024]{1,0:T(8,128)S(1)}, u32[]{:S(2)}, u32[]{:S(2)}) collective-permute-start(f32[192,1024]{1,0:T(8,128)} %constant_dynamic-slice_fusion), channel_id=1, source_target_pairs={{0,8},{8,0},{16,24},{24,16},{1,9},{9,1},{17,25},{25,17},{2,10},{10... | collective-permute-start | bytes 2359304 | tf_op jit(solution)/shard_map/ppermute | solution.py:381
  4.9 25.9 %collective-permute-start.1 = (bf16[512,1024]{1,0:T(8,128)(2,1)}, bf16[512,1024]{1,0:T(8,128)(2,1)}, u32[]{:S(2)}, u32[]{:S(2)}) collective-permute-start(bf16[512,1024]{1,0:T(8,128)(2,1)} %multiply_convert_fusion.refs_0_), channel_id=1, source_target_pairs={{2,0},{4,2},{6,4},{7,6},{5,7},{3,5},{1,3},{0,1},{10,8},{12,10},{14... | collective-permute-start | bytes 3145736 | tf_op jit(solution)/shard_map/ppermute | solution.py:47
  4.9 25.9 %collective-permute-start = (bf16[512,1024]{1,0:T(8,128)(2,1)}, bf16[512,1024]{1,0:T(8,128)(2,1)}, u32[]{:S(2)}, u32[]{:S(2)}) collective-permute-start(bf16[512,1024]{1,0:T(8,128)(2,1)} %multiply_convert_fusion.refs_0_), channel_id=1, source_target_pairs={{0,2},{2,4},{4,6},{6,7},{7,5},{5,3},{3,1},{1,0},{8,10},{10,12},{12... | collective-permute-start | bytes 3145736 | tf_op jit(solution)/shard_map/ppermute | solution.py:44
  6.9 27.2 %collective-permute-start.2 = (bf16[512,1024]{1,0:T(8,128)(2,1)}, bf16[512,1024]{1,0:T(8,128)(2,1)}, u32[]{:S(2)}, u32[]{:S(2)}) collective-permute-start(bf16[512,1024]{1,0:T(8,128)(2,1)} %multiply_convert_fusion.refs_0_), channel_id=1, source_target_pairs={{2,3},{3,2},{4,5},{5,4},{10,11},{11,10},{12,13},{13,12},{18,19},{1... | collective-permute-start | bytes 3145736 | tf_op jit(solution)/shard_map/ppermute | solution.py:56
  11.3 2.8 %copy-start.14 = (s32[8]{0:T(128)S(1)}, s32[8]{0:T(128)}, u32[]{:S(2)}) copy-start(s32[8]{0:T(128)} %constant.120.clone) | copy-start | bytes 100
  11.3 22.8 %collective-permute-start.4 = (f32[192,1024]{1,0:T(8,128)}, f32[192,1024]{1,0:T(8,128)}, u32[]{:S(2)}, u32[]{:S(2)}) collective-permute-start(f32[192,1024]{1,0:T(8,128)} %dynamic-slice_add_fusion), channel_id=1, source_target_pairs={{0,16},{8,24},{16,0},{24,8},{1,17},{9,25},{17,1},{25,9},{2,18},{10... | collective-permute-start | bytes 2359304 | tf_op jit(solution)/shard_map/ppermute | solution.py:381
  14.1 2.2 %copy-start.1 = (bf16[1,512,4096]{2,1,0:T(8,128)(2,1)S(1)}, bf16[1,512,4096]{2,1,0:T(8,128)(2,1)}, u32[]{:S(2)}) copy-start(bf16[1,512,4096]{2,1,0:T(8,128)(2,1)} %param.10) | copy-start | bytes 12582916
  16.3 1.2 copy-start.7
  29.6 9.8 %copy-start.2 = (bf16[512,1024]{1,0:T(8,128)(2,1)}, bf16[512,1024]{1,0:T(8,128)(2,1)S(1)}, u32[]{:S(2)}) copy-start(bf16[512,1024]{1,0:T(8,128)(2,1)S(1)} %get-tuple-element.99.kv_grad) | copy-start | bytes 3145732
  29.6 9.8 %copy-start.4 = (bf16[512,1024]{1,0:T(8,128)(2,1)}, bf16[512,1024]{1,0:T(8,128)(2,1)S(1)}, u32[]{:S(2)}) copy-start(bf16[512,1024]{1,0:T(8,128)(2,1)S(1)} %get-tuple-element.171) | copy-start | bytes 3145732
  39.4 7.0 %collective-permute-start.7 = (f32[192,1024]{1,0:T(8,128)}, f32[192,1024]{1,0:T(8,128)}, u32[]{:S(2)}, u32[]{:S(2)}) collective-permute-start(f32[192,1024]{1,0:T(8,128)} %add.148), channel_id=1, source_target_pairs={{0,8},{8,0},{16,24},{24,16},{1,9},{9,1},{17,25},{25,17},{2,10},{10... | collective-permute-start | bytes 2359304 | tf_op jit(solution)/shard_map/ppermute | solution.py:390
  39.6 15.0 %collective-permute-start.6 = (bf16[256,1024]{1,0:T(8,128)(2,1)}, bf16[256,1024]{1,0:T(8,128)(2,1)S(1)}, u32[]{:S(2)}, u32[]{:S(2)}) collective-permute-start(bf16[256,1024]{1,0:T(8,128)(2,1)} %slice.130), channel_id=1, source_target_pairs={{2,0},{4,2},{6,4},{7,6},{5,7},{3,5},{1,3},{0,1},{10,8},{12,10},{14... | collective-permute-start | bytes 1572872 | tf_op jit(solution)/shard_map/ppermute | solution.py:47
  39.6 14.9 %collective-permute-start.5 = (bf16[256,1024]{1,0:T(8,128)(2,1)S(1)}, bf16[256,1024]{1,0:T(8,128)(2,1)S(1)}, u32[]{:S(2)}, u32[]{:S(2)}) collective-permute-start(bf16[256,1024]{1,0:T(8,128)(2,1)S(1)} %slice.129), channel_id=1, source_target_pairs={{0,2},{2,4},{4,6},{6,7},{7,5},{5,3},{3,1},{1,0},{8,10},{10,12},{12... | collective-permute-start | bytes 1572872 | tf_op jit(solution)/shard_map/ppermute | solution.py:44
  43.0 26.9 %collective-permute-start.14 = (bf16[512,1024]{1,0:T(8,128)(2,1)S(1)}, bf16[512,1024]{1,0:T(8,128)(2,1)S(1)}, u32[]{:S(2)}, u32[]{:S(2)}) collective-permute-start(bf16[512,1024]{1,0:T(8,128)(2,1)S(1)} %broadcast_select_fusion), channel_id=1, source_target_pairs={{2,3},{3,2},{4,5},{5,4},{10,11},{11,10},{12,13},{13,12},{18,19},{1... | collective-permute-start | bytes 3145736 | tf_op jit(solution)/shard_map/ppermute | solution.py:56
  48.0 4.4 %copy-start.13 = (s32[8]{0:T(128)S(1)}, s32[8]{0:T(128)}, u32[]{:S(2)}) copy-start(s32[8]{0:T(128)} %constant.121.clone) | copy-start | bytes 100
  48.0 6.6 %copy-start.5 = (bf16[512,1024]{1,0:T(8,128)(2,1)S(1)}, bf16[512,1024]{1,0:T(8,128)(2,1)}, u32[]{:S(2)}) copy-start(bf16[512,1024]{1,0:T(8,128)(2,1)} %copy-done.4) | copy-start | bytes 3145732
  50.2 15.5 %collective-permute-start.11 = (bf16[256,1024]{1,0:T(8,128)(2,1)S(1)}, bf16[256,1024]{1,0:T(8,128)(2,1)S(1)}, u32[]{:S(2)}, u32[]{:S(2)}) collective-permute-start(bf16[256,1024]{1,0:T(8,128)(2,1)S(1)} %slice.132), channel_id=1, source_target_pairs={{2,0},{4,2},{6,4},{7,6},{5,7},{3,5},{1,3},{0,1},{10,8},{12,10},{14... | collective-permute-start | bytes 1572872 | tf_op jit(solution)/shard_map/ppermute | solution.py:47
  50.3 15.5 %collective-permute-start.10 = (bf16[256,1024]{1,0:T(8,128)(2,1)S(1)}, bf16[256,1024]{1,0:T(8,128)(2,1)S(1)}, u32[]{:S(2)}, u32[]{:S(2)}) collective-permute-start(bf16[256,1024]{1,0:T(8,128)(2,1)S(1)} %slice.131), channel_id=1, source_target_pairs={{0,2},{2,4},{4,6},{6,7},{7,5},{5,3},{3,1},{1,0},{8,10},{10,12},{12... | collective-permute-start | bytes 1572872 | tf_op jit(solution)/shard_map/ppermute | solution.py:44
  54.6 18.6 %copy-start.3 = (bf16[512,1024]{1,0:T(8,128)(2,1)S(1)}, bf16[512,1024]{1,0:T(8,128)(2,1)}, u32[]{:S(2)}) copy-start(bf16[512,1024]{1,0:T(8,128)(2,1)} %copy-done.2) | copy-start | bytes 3145732
  54.7 30.1 %collective-permute-start.9 = (bf16[256,1024]{1,0:T(8,128)(2,1)S(1)}, bf16[256,1024]{1,0:T(8,128)(2,1)S(1)}, u32[]{:S(2)}, u32[]{:S(2)}) collective-permute-start(bf16[256,1024]{1,0:T(8,128)(2,1)S(1)} %get-tuple-element.212), channel_id=1, source_target_pairs={{2,0},{4,2},{6,4},{7,6},{5,7},{3,5},{1,3},{0,1},{10,8},{12,10},{14... | collective-permute-start | bytes 1572872 | tf_op jit(solution)/shard_map/ppermute | solution.py:47
  56.0 28.8 %collective-permute-start.8 = (bf16[256,1024]{1,0:T(8,128)(2,1)S(1)}, bf16[256,1024]{1,0:T(8,128)(2,1)S(1)}, u32[]{:S(2)}, u32[]{:S(2)}) collective-permute-start(bf16[256,1024]{1,0:T(8,128)(2,1)S(1)} %get-tuple-element.213), channel_id=1, source_target_pairs={{0,2},{2,4},{4,6},{6,7},{7,5},{5,3},{3,1},{1,0},{8,10},{10,12},{12... | collective-permute-start | bytes 1572872 | tf_op jit(solution)/shard_map/ppermute | solution.py:44
  65.9 22.9 %collective-permute-start.13 = (bf16[256,1024]{1,0:T(8,128)(2,1)S(1)}, bf16[256,1024]{1,0:T(8,128)(2,1)S(1)}, u32[]{:S(2)}, u32[]{:S(2)}) collective-permute-start(bf16[256,1024]{1,0:T(8,128)(2,1)S(1)} %get-tuple-element.210), channel_id=1, source_target_pairs={{2,0},{4,2},{6,4},{7,6},{5,7},{3,5},{1,3},{0,1},{10,8},{12,10},{14... | collective-permute-start | bytes 1572872 | tf_op jit(solution)/shard_map/ppermute | solution.py:47
  67.2 21.6 %collective-permute-start.12 = (bf16[256,1024]{1,0:T(8,128)(2,1)S(1)}, bf16[256,1024]{1,0:T(8,128)(2,1)S(1)}, u32[]{:S(2)}, u32[]{:S(2)}) collective-permute-start(bf16[256,1024]{1,0:T(8,128)(2,1)S(1)} %get-tuple-element.211), channel_id=1, source_target_pairs={{0,2},{2,4},{4,6},{6,7},{7,5},{5,3},{3,1},{1,0},{8,10},{10,12},{12... | collective-permute-start | bytes 1572872 | tf_op jit(solution)/shard_map/ppermute | solution.py:44
  69.8 14.9 %copy-start.11 = (bf16[512,1024]{1,0:T(8,128)(2,1)}, bf16[512,1024]{1,0:T(8,128)(2,1)S(1)}, u32[]{:S(2)}) copy-start(bf16[512,1024]{1,0:T(8,128)(2,1)S(1)} %collective-permute-done.14.refs_4_) | copy-start | bytes 3145732
  69.8 54.3 %collective-permute-start.23 = (bf16[512,1024]{1,0:T(8,128)(2,1)S(1)}, bf16[512,1024]{1,0:T(8,128)(2,1)S(1)}, u32[]{:S(2)}, u32[]{:S(2)}) collective-permute-start(bf16[512,1024]{1,0:T(8,128)(2,1)S(1)} %copy-done.5), channel_id=1, source_target_pairs={{2,3},{3,2},{4,5},{5,4},{10,11},{11,10},{12,13},{13,12},{18,19},{1... | collective-permute-start | bytes 3145736 | tf_op jit(solution)/shard_map/ppermute | solution.py:56
  86.7 14.9 %collective-permute-start.16 = (bf16[256,1024]{1,0:T(8,128)(2,1)S(1)}, bf16[256,1024]{1,0:T(8,128)(2,1)S(1)}, u32[]{:S(2)}, u32[]{:S(2)}) collective-permute-start(bf16[256,1024]{1,0:T(8,128)(2,1)S(1)} %get-tuple-element.206), channel_id=1, source_target_pairs={{2,0},{4,2},{6,4},{7,6},{5,7},{3,5},{1,3},{0,1},{10,8},{12,10},{14... | collective-permute-start | bytes 1572872 | tf_op jit(solution)/shard_map/ppermute | solution.py:47
  86.8 14.9 %collective-permute-start.15 = (bf16[256,1024]{1,0:T(8,128)(2,1)S(1)}, bf16[256,1024]{1,0:T(8,128)(2,1)S(1)}, u32[]{:S(2)}, u32[]{:S(2)}) collective-permute-start(bf16[256,1024]{1,0:T(8,128)(2,1)S(1)} %get-tuple-element.207), channel_id=1, source_target_pairs={{0,2},{2,4},{4,6},{6,7},{7,5},{5,3},{3,1},{1,0},{8,10},{10,12},{12... | collective-permute-start | bytes 1572872 | tf_op jit(solution)/shard_map/ppermute | solution.py:44
  92.6 20.3 %collective-permute-start.18 = (bf16[256,1024]{1,0:T(8,128)(2,1)S(1)}, bf16[256,1024]{1,0:T(8,128)(2,1)S(1)}, u32[]{:S(2)}, u32[]{:S(2)}) collective-permute-start(bf16[256,1024]{1,0:T(8,128)(2,1)S(1)} %get-tuple-element.200), channel_id=1, source_target_pairs={{2,0},{4,2},{6,4},{7,6},{5,7},{3,5},{1,3},{0,1},{10,8},{12,10},{14... | collective-permute-start | bytes 1572872 | tf_op jit(solution)/shard_map/ppermute | solution.py:47
  93.4 19.6 %collective-permute-start.17 = (bf16[256,1024]{1,0:T(8,128)(2,1)S(1)}, bf16[256,1024]{1,0:T(8,128)(2,1)S(1)}, u32[]{:S(2)}, u32[]{:S(2)}) collective-permute-start(bf16[256,1024]{1,0:T(8,128)(2,1)S(1)} %get-tuple-element.201), channel_id=1, source_target_pairs={{0,2},{2,4},{4,6},{6,7},{7,5},{5,3},{3,1},{1,0},{8,10},{10,12},{12... | collective-permute-start | bytes 1572872 | tf_op jit(solution)/shard_map/ppermute | solution.py:44
  103.6 20.5 %collective-permute-start.22 = (bf16[256,1024]{1,0:T(8,128)(2,1)S(1)}, bf16[256,1024]{1,0:T(8,128)(2,1)S(1)}, u32[]{:S(2)}, u32[]{:S(2)}) collective-permute-start(bf16[256,1024]{1,0:T(8,128)(2,1)S(1)} %get-tuple-element.204), channel_id=1, source_target_pairs={{2,0},{4,2},{6,4},{7,6},{5,7},{3,5},{1,3},{0,1},{10,8},{12,10},{14... | collective-permute-start | bytes 1572872 | tf_op jit(solution)/shard_map/ppermute | solution.py:47
  104.2 20.0 %collective-permute-start.21 = (bf16[256,1024]{1,0:T(8,128)(2,1)S(1)}, bf16[256,1024]{1,0:T(8,128)(2,1)S(1)}, u32[]{:S(2)}, u32[]{:S(2)}) collective-permute-start(bf16[256,1024]{1,0:T(8,128)(2,1)S(1)} %get-tuple-element.205), channel_id=1, source_target_pairs={{0,2},{2,4},{4,6},{6,7},{7,5},{5,3},{3,1},{1,0},{8,10},{10,12},{12... | collective-permute-start | bytes 1572872 | tf_op jit(solution)/shard_map/ppermute | solution.py:44
  114.9 20.5 %collective-permute-start.20 = (bf16[256,1024]{1,0:T(8,128)(2,1)S(1)}, bf16[256,1024]{1,0:T(8,128)(2,1)S(1)}, u32[]{:S(2)}, u32[]{:S(2)}) collective-permute-start(bf16[256,1024]{1,0:T(8,128)(2,1)S(1)} %get-tuple-element.202), channel_id=1, source_target_pairs={{2,0},{4,2},{6,4},{7,6},{5,7},{3,5},{1,3},{0,1},{10,8},{12,10},{14... | collective-permute-start | bytes 1572872 | tf_op jit(solution)/shard_map/ppermute | solution.py:47
  115.4 20.0 %collective-permute-start.19 = (bf16[256,1024]{1,0:T(8,128)(2,1)S(1)}, bf16[256,1024]{1,0:T(8,128)(2,1)S(1)}, u32[]{:S(2)}, u32[]{:S(2)}) collective-permute-start(bf16[256,1024]{1,0:T(8,128)(2,1)S(1)} %get-tuple-element.203), channel_id=1, source_target_pairs={{0,2},{2,4},{4,6},{6,7},{7,5},{5,3},{3,1},{1,0},{8,10},{10,12},{12... | collective-permute-start | bytes 1572872 | tf_op jit(solution)/shard_map/ppermute | solution.py:44
  124.2 15.4 %collective-permute-start.26 = (bf16[256,1024]{1,0:T(8,128)(2,1)S(1)}, bf16[256,1024]{1,0:T(8,128)(2,1)S(1)}, u32[]{:S(2)}, u32[]{:S(2)}) collective-permute-start(bf16[256,1024]{1,0:T(8,128)(2,1)S(1)} %get-tuple-element.181), channel_id=1, source_target_pairs={{2,3},{3,2},{4,5},{5,4},{10,11},{11,10},{12,13},{13,12},{18,19},{1... | collective-permute-start | bytes 1572872 | tf_op jit(solution)/shard_map/ppermute | solution.py:56
  130.2 27.5 %collective-permute-start.29 = (bf16[256,1024]{1,0:T(8,128)(2,1)S(1)}, bf16[256,1024]{1,0:T(8,128)(2,1)S(1)}, u32[]{:S(2)}, u32[]{:S(2)}) collective-permute-start(bf16[256,1024]{1,0:T(8,128)(2,1)S(1)} %get-tuple-element.196), channel_id=1, source_target_pairs={{2,0},{4,2},{6,4},{7,6},{5,7},{3,5},{1,3},{0,1},{10,8},{12,10},{14... | collective-permute-start | bytes 1572872 | tf_op jit(solution)/shard_map/ppermute | solution.py:47
  130.2 13.3 %copy-start.8 = (f32[384,1024]{1,0:T(8,128)S(1)}, f32[384,1024]{1,0:T(8,128)}, u32[]{:S(2)}) copy-start(f32[384,1024]{1,0:T(8,128)} %param.16) | copy-start | bytes 4718596
  130.2 13.2 %copy-start.9 = (f32[384,1024]{1,0:T(8,128)S(1)}, f32[384,1024]{1,0:T(8,128)}, u32[]{:S(2)}) copy-start(f32[384,1024]{1,0:T(8,128)} %param.15) | copy-start | bytes 4718596
  130.3 13.2 %copy-start.12 = (bf16[1,384,1024]{2,1,0:T(8,128)(2,1)S(1)}, bf16[1,384,1024]{2,1,0:T(8,128)(2,1)}, u32[]{:S(2)}) copy-start(bf16[1,384,1024]{2,1,0:T(8,128)(2,1)} %param.17) | copy-start | bytes 2359300
  130.3 27.4 %collective-permute-start.28 = (bf16[256,1024]{1,0:T(8,128)(2,1)S(1)}, bf16[256,1024]{1,0:T(8,128)(2,1)S(1)}, u32[]{:S(2)}, u32[]{:S(2)}) collective-permute-start(bf16[256,1024]{1,0:T(8,128)(2,1)S(1)} %get-tuple-element.197), channel_id=1, source_target_pairs={{0,2},{2,4},{4,6},{6,7},{7,5},{5,3},{3,1},{1,0},{8,10},{10,12},{12... | collective-permute-start | bytes 1572872 | tf_op jit(solution)/shard_map/ppermute | solution.py:44
  137.4 21.6 %collective-permute-start.25 = (bf16[256,1024]{1,0:T(8,128)(2,1)S(1)}, bf16[256,1024]{1,0:T(8,128)(2,1)S(1)}, u32[]{:S(2)}, u32[]{:S(2)}) collective-permute-start(bf16[256,1024]{1,0:T(8,128)(2,1)S(1)} %get-tuple-element.194), channel_id=1, source_target_pairs={{2,0},{4,2},{6,4},{7,6},{5,7},{3,5},{1,3},{0,1},{10,8},{12,10},{14... | collective-permute-start | bytes 1572872 | tf_op jit(solution)/shard_map/ppermute | solution.py:47
  138.0 21.1 %collective-permute-start.24 = (bf16[256,1024]{1,0:T(8,128)(2,1)S(1)}, bf16[256,1024]{1,0:T(8,128)(2,1)S(1)}, u32[]{:S(2)}, u32[]{:S(2)}) collective-permute-start(bf16[256,1024]{1,0:T(8,128)(2,1)S(1)} %get-tuple-element.195), channel_id=1, source_target_pairs={{0,2},{2,4},{4,6},{6,7},{7,5},{5,3},{3,1},{1,0},{8,10},{10,12},{12... | collective-permute-start | bytes 1572872 | tf_op jit(solution)/shard_map/ppermute | solution.py:44
  139.5 19.6 %collective-permute-start.27 = (bf16[256,1024]{1,0:T(8,128)(2,1)S(1)}, bf16[256,1024]{1,0:T(8,128)(2,1)S(1)}, u32[]{:S(2)}, u32[]{:S(2)}) collective-permute-start(bf16[256,1024]{1,0:T(8,128)(2,1)S(1)} %get-tuple-element.182), channel_id=1, source_target_pairs={{2,3},{3,2},{4,5},{5,4},{10,11},{11,10},{12,13},{13,12},{18,19},{1... | collective-permute-start | bytes 1572872 | tf_op jit(solution)/shard_map/ppermute | solution.py:56
  146.0 11.6 %copy-start = (bf16[1,512,1024]{2,1,0:T(8,128)(2,1)S(1)}, bf16[1,512,1024]{2,1,0:T(8,128)(2,1)}, u32[]{:S(2)}) copy-start(bf16[1,512,1024]{2,1,0:T(8,128)(2,1)} %param.12) | copy-start | bytes 3145732
  146.0 11.7 %copy-start.6 = (bf16[1,512]{1,0:T(2,128)(2,1)S(1)}, bf16[1,512]{1,0:T(2,128)(2,1)}, u32[]{:S(2)}) copy-start(bf16[1,512]{1,0:T(2,128)(2,1)} %gain.3) | copy-start | bytes 3076

commit v11 on v10

--- a/solution.py
+++ b/solution.py
@@ -67,6 +67,30 @@
     angle = positions.astype(f32)[:, None] * inverse[None, :]
     cosine, sine = jnp.cos(angle), jnp.sin(angle)
     return jnp.concatenate([cosine, cosine], axis=1), jnp.concatenate([-sine, sine], axis=1)
+
+
+def scale_kernel(weight, gain, out):
+    gains = jnp.broadcast_to(gain[...].astype(f32), (8, weight.shape[0])).T
+    out[...] = (weight[...].astype(f32) * gains[:, :1]).astype(bf16)
+
+
+def scale_rows(weight, gain):
+    shard, cols = weight.shape
+    return pl.pallas_call(
+        scale_kernel,
+        grid=(shard // HEAD,),
+        in_specs=[
+            pl.BlockSpec((HEAD, cols), lambda i: (i, 0)),
+            pl.BlockSpec((1, HEAD), lambda i: (0, i)),
+        ],
+        out_specs=pl.BlockSpec((HEAD, cols), lambda i: (i, 0)),
+        out_shape=jax.ShapeDtypeStruct((shard, cols), bf16),
+        compiler_params=pltpu.CompilerParams(vmem_limit_bytes=16 * 2**20),
+        cost_estimate=pl.CostEstimate(
+            flops=shard * cols, bytes_accessed=4 * shard * cols, transcendentals=0
+        ),
+        name="scale_rows",
+    )(weight, gain)
 
 
 def first_kernel(scale, at, x, cotangent, cosine, sine, kv_grad, inv, far, near, last):
@@ -216,7 +240,7 @@
     here = len(plan)
     done = sum(before)
     n = done + here
-    total_at = len(refs) - (8 if not finish else 9)
+    total_at = len(refs) - 9
     blocks, refs = refs[:total_at], refs[total_at:]
     if before:
         pre0, sums0, *grads0 = blocks[: 2 + len(before)]
@@ -224,7 +248,7 @@
     if finish:
         kv_out, input_grad, xs, ws, ng, pre, x_sem, w_sem, g_sem = refs
     else:
-        pre, sums, grads, xs, ws, x_sem, w_sem, g_sem = refs
+        pre, sums, grads, xs, ws, ng, x_sem, w_sem, g_sem = refs
     rows, width = x.shape
     shard = xs.shape[2]
     kvw = pre.shape[1] // 2
@@ -282,10 +306,9 @@
         grad = lax.dot_general(
             kv_grad[...], weight, (((1,), (1,)), ((), ())), preferred_element_type=f32
         )
-        if finish:
-            ng[k] = grad
-        else:
-            grads[i] = grad
+        ng[k - base] = grad
+        if not finish:
+            pltpu.make_async_copy(ng.at[i], grads.at[i], g_sem.at[i]).start()
         product = grad * normed
         for c in range(0, shard, HEAD):
             total = total + product[:, c : c + HEAD]
@@ -294,6 +317,8 @@
     total = lax.fori_loop(0, here, gather, start)
     if not finish:
         sums[...] = total
+        for i in range(here):
+            pltpu.make_async_copy(ng.at[i], grads.at[i], g_sem.at[i]).wait()
         return
     mean = jnp.sum(total, axis=1, keepdims=True) / width
     for load in loads:
@@ -353,14 +378,15 @@
             jax.ShapeDtypeStruct((rows, width), bf16),
         ]
     else:
-        out_specs = [whole] * 3
+        scratch.append(pltpu.VMEM((here, rows, shard), f32))
+        out_specs = [whole, whole, there]
         out_shape = [
             jax.ShapeDtypeStruct((rows, cols), f32),
             jax.ShapeDtypeStruct((rows, HEAD), f32),
             jax.ShapeDtypeStruct((here, rows, shard), f32),
         ]
     scratch += [pltpu.SemaphoreType.DMA((slots,)), pltpu.SemaphoreType.DMA((here,))]
-    scratch += [pltpu.SemaphoreType.DMA((max(len(before), 1),))]
+    scratch += [pltpu.SemaphoreType.DMA((max(len(before), here),))]
     return pl.pallas_call(
         functools.partial(part_kernel, plan, tuple(before), finish),
         in_specs=in_specs,
@@ -391,7 +417,7 @@
     return jnp.where(odd, theirs, mine), jnp.where(odd, mine, theirs)
 
 
-def exchange_ring(ring, own, far, near, pseudo, project):
+def exchange_ring(ring, own, far, near, pseudo, project, update):
     total = lax.psum(pseudo, "replica")
     shard, cut = own.shape[0], own.shape[0] // 2
     blocks = [own]
@@ -415,14 +441,15 @@
         from_left = ring.to_right((near[k] + from_left.astype(f32)).astype(bf16))
         from_right = ring.to_left((near[k + 1] + from_right.astype(f32)).astype(bf16))
     sums = [(from_left, from_right)]
-    return project(blocks, tuple(plan), (), (), True), sums, total
-
-
-ORDER = {"sum": (0, 1), "inner": (3, 8), "far": (0, 5), "partner0": (4, None), "partner1": (6, None), "first": (2, 4)}
+    return project(blocks, tuple(plan), (), (), True), sums, update(total)
+
+
+ORDER = {"sum": (0, 2), "inner": (3, 8), "far": (0, 3), "partner0": (4, None), "partner1": (6, None), "part0": (1, 3), "part1": (2, 5), "part2": (5, 9), "update": (3, 7)}
 CHAIN = True
-
-
-def exchange_plane(plane, own, far, near, pseudo, project):
+PAIR = 4
+
+
+def exchange_plane(plane, own, far, near, pseudo, project, update):
     shard = own.shape[0]
     at0, at1, at2, at3 = plane.at
     zero = jnp.zeros((), f32)
@@ -450,16 +477,27 @@
     def later(step, *values):
         names = [name for name, (_, end) in ORDER.items() if end == step]
         awaited = [beside[name] for name in names]
+        if step == PAIR:
+            awaited.append(partner[0])
         values, awaited = lax.optimization_barrier((after(values, sent[0]), awaited))
         beside.update(zip(names, awaited))
+        if step == PAIR:
+            partner[0] = awaited[-1]
         return values
 
     def for_partner(h):
         return pick(at1, part(near[1], h), part(near[0], h)).astype(bf16)
 
-    def first_blocks():
-        gated = after(blocks[0], sent[0])
-        return project([gated, *blocks[1:]], plan[:5], (), (), False)
+    ways = lambda flag, at: tuple((flag, at + h, *pieces[h]) for h in halves)
+    carry, before = [()], []
+
+    def part_of(plan, blocks, last=False):
+        blocks = [after(blocks[0], sent[0]), *blocks[1:]]
+        outs = project(blocks, plan, carry[0], tuple(before), last)
+        if not last:
+            carry[0] = (*outs[:2], *carry[0][2:], outs[2])
+            before.append(len(plan))
+        return outs
 
     tasks = {
         "sum": lambda: replica_halves(after(mine, sent[0]) + came, odd),
@@ -467,23 +505,29 @@
         "inner": lambda: chord(far),
         "partner0": lambda: chord(for_partner(0)),
         "partner1": lambda: chord(for_partner(1)),
-        "first": first_blocks,
+        "part0": lambda: part_of(
+            tuple(((None, k, 0, shard),) for k in range(3)), [own, *first]
+        ),
+        "part1": lambda: part_of((ways(None, 0), ways(None, 2)), by_way(two)),
+        "part2": lambda: part_of(
+            (((0, 0, 0, shard), *ways(2, 1)), ((1, 0, 0, shard), *ways(3, 3))),
+            [partner[0], *by_way(three)],
+        ),
+        "update": lambda: update(after(beside["sum"], sent[0])),
     }
+    by_way = lambda steps: [steps[h][way] for way in range(2) for h in halves]
 
     first = ring(None, own, own)
-    partner = chord(own)
+    partner = [chord(own)]
     odd = lax.axis_index("replica") % 2 == 1
     if lax.axis_size("replica") == 4:
         mine, came = replica_pairs(after(pseudo, own), odd.astype(jnp.int32))
     else:
         came = lax.psum(pseudo, "replica")
         tasks["sum"] = lambda: came
-    first, partner, far, came = lax.optimization_barrier((first, partner, far, came))
+    first, far, came = lax.optimization_barrier((first, far, came))
     two = [ring(0, *(part(side, 0) for side in first))]
     two.append(ring(1, *(part(side, 1) for side in later(1, *first))))
-    blocks = [own, *first, *(two[h][way] for way in range(2) for h in halves)]
-    plan = [((None, k, 0, shard),) for k in range(3)]
-    plan += [tuple((None, 3 + 2 * way + h, *pieces[h]) for h in halves) for way in range(2)]
     three = []
     for h in halves:
         left, right = later(2 + h, *two[h])
@@ -512,17 +556,10 @@
         six.append(ring(8 + h, to_right.astype(bf16), to_left.astype(bf16)))
     sums = [(*six[h], beside["partner%d" % h]) for h in halves]
 
-    blocks = [partner, beside["far"]] + [
-        steps[h][way] for steps in (three, four) for way in range(2) for h in halves
-    ]
-    ways = lambda flag, at: tuple((flag, at + h, *pieces[h]) for h in halves)
-    plan = (
-        ((0, 0, 0, shard), *ways(2, 2)),
-        ((1, 0, 0, shard), *ways(3, 4)),
-        ((4, 1, 0, shard), *ways(5, 6), *ways(6, 8)),
-    )
-    outs = project(blocks, plan, beside["first"], (5,), True)
-    return outs, sums, beside["sum"]
+    outs = part_of(
+        (((4, 0, 0, shard), *ways(5, 1), *ways(6, 3)),), [beside["far"], *by_way(four)], True
+    )
+    return outs, sums, beside["update"]
 
 
 def local(
@@ -538,13 +575,12 @@
     small = lax.axis_size("fsdp") == 8
     ring = Plane() if small else Ring()
     tokens_in = layer_input[0]
-    gain_shard = norm_gain[0].astype(f32)[:, None]
     weight_shard = kv_weight[0]
     cotangent = kv_cotangent[0]
     rows, width = tokens_in.shape
     shard, cols = weight_shard.shape
 
-    own = (weight_shard.astype(f32) * gain_shard).astype(bf16)
+    own = scale_rows(weight_shard, norm_gain)
     positions = (ring.me * rows + jnp.arange(rows, dtype=jnp.int32)) % SEQ_LEN
     cosine, sine = rope_tables(positions)
     scale = 1.0 / math.sqrt(rows * ring.count)
@@ -565,18 +601,23 @@
     def project(*args):
         return project_part(at, tokens_in, kv_grad, inv, cosine, sine, *args)
 
+    def update(total):
+        if isinstance(total, tuple):
+            total = jnp.concatenate(total)
+        average = total / lax.axis_size("replica")
+        momentum_new = momentum_rate * outer_momentum + average
+        global_new = global_params - outer_rate * (average + momentum_rate * momentum_new)
+        local_new = (
+            mixing_rate * local_params[0].astype(f32) + (1.0 - mixing_rate) * global_new
+        ).astype(bf16)
+        return momentum_new, global_new, local_new
+
     exchange = exchange_plane if small else exchange_ring
-    (kv_out, input_grad), sums, total = exchange(ring, own, far, near, pseudo_grad[0], project)
+    (kv_out, input_grad), sums, updated = exchange(
+        ring, own, far, near, pseudo_grad[0], project, update
+    )
+    momentum_new, global_new, local_new = updated
     weight_grad, gain_grad = last_part(last, weight_shard, norm_gain, sums)
-
-    if isinstance(total, tuple):
-        total = jnp.concatenate(total)
-    average = total / lax.axis_size("replica")
-    momentum_new = momentum_rate * outer_momentum + average
-    global_new = global_params - outer_rate * (average + momentum_rate * momentum_new)
-    local_new = (
-        mixing_rate * local_params[0].astype(f32) + (1.0 - mixing_rate) * global_new
-    ).astype(bf16)
 
     return (
         kv_out[None],

time: 161 us -> 161 us (level); the launches traced: 161 us -> 159 us
  waiting for transfers between devices: 42.2 us -> 22.8 us
  Pallas kernels: 37.9 us -> 50.9 us
  local copies, waits for them, and re-layouts: 9.72 us -> 12.8 us
    ppermute x11, waiting for transfers between devices: 36.7 us -> 14.1 us  [to_left(): return lax.ppermute(value, 'fsdp', self.left)]
    pallas_call x2 -> x4, Pallas kernels: 23.1 us -> 34.1 us  [project_part(): pl.pallas_call(functools.partial(part_kernel, plan, tuple(before), finish...]
    ppermute x11, waiting for transfers between devices: 0.28 us -> 6.3 us  [to_right(): return lax.ppermute(value, 'fsdp', self.right)]
    ppermute x5, waiting for transfers between devices: 5.24 us -> 2.41 us  [over_chord(): return lax.ppermute(value, 'fsdp', [(2, 3), (3, 2), (4, 5), (5, 4)])]
    broadcast_in_dim x1 -> x0, other arithmetic: 2.52 us -> none  [local(): local_new[None]]
    unnamed x30 -> x38, local copies, waits for them, and re-layouts: 3.47 us -> 5.46 us
    pallas_call x0 -> x1, Pallas kernels: none -> 1.96 us  [scale_rows(): pl.pallas_call(scale_kernel, grid=(shard // HEAD,), in_specs=[pl.BlockSpe...]
    convert_element_type x2 -> x1, other arithmetic: 3.23 us -> 2.49 us  [update(): local_new = (mixing_rate * local_params[0].astype(f32) + (1.0 - mixing_ra...]
  transfers between devices with their start and end apart: 30 -> 30, of which waited for: 13 -> 9; matrix products, arithmetic and copies ran while one was open for 15% -> 21% of each run, Pallas kernels for 23% -> 30%
where the time goes in v11:
time: 161 us; the launch traced here: 159 us
  Pallas kernels  50.9 us (32%)
  starting transfers between devices  43.7 us (27%)
  other arithmetic  27.2 us (17%)
  waiting for transfers between devices  22.8 us (14%)
  local copies, waits for them, and re-layouts  12.8 us (8%)
    pallas_call x4, Pallas kernels, project_part(): pl.pallas_call(functools.partial(part_kernel, plan, tuple(before), finish...  34.1 us
    ppermute x5, starting transfers between devices, over_chord(): return lax.ppermute(value, 'fsdp', [(2, 3), (3, 2), (4, 5), (5, 4)])  19.7 us
    ppermute x11, starting transfers between devices, to_right(): return lax.ppermute(value, 'fsdp', self.right)  17 us
    ppermute x11, waiting for transfers between devices, to_left(): return lax.ppermute(value, 'fsdp', self.left)  14.1 us
    pallas_call x1, Pallas kernels, first_part(): pl.pallas_call(functools.partial(first_kernel, scale), grid_spec=pltpu.Pr...  12 us
    ppermute x11, waiting for transfers between devices, to_right(): return lax.ppermute(value, 'fsdp', self.right)  6.3 us
    slice x4, local copies, waits for them, and re-layouts, part(): return value[pieces[h][0]:pieces[h][1]]  5.89 us
    unnamed x38, local copies, waits for them, and re-layouts  5.46 us
  transfers between devices with their start and end apart: 30, of which 9 were waited for; matrix products, arithmetic and copies ran while one was open for 21% of the time, Pallas kernels for 30%

profile of v11, /device:TPU:8, one launch (start us, length us, event | category | flops | bytes accessed | tf_op | source)
XLA Modules:
  0.0 158.6 jit_solution(9467092529918946413)
XLA Ops:
  0.7 1.2 copy-done.1
  2.6 2.0 %scale_rows.1.refs_0_ = bf16[512,1024]{1,0:T(8,128)(2,1)} custom-call(bf16[512,1024]{1,0:T(8,128)(2,1)S(1)} %bitcast.86, bf16[1,512]{1,0:T(2,128)(2,1)S(1)} %copy-done.9), custom_call_target="tpu_custom_call" | custom-call | flops 524288 | bytes 2097152 | tf_op jit(solution)/shard_map/scale_rows/pallas_call | solution.py:79
  4.5 1.3 constant_dynamic-slice_fusion
  6.0 2.0 %collective-permute-start = (bf16[512,1024]{1,0:T(8,128)(2,1)}, bf16[512,1024]{1,0:T(8,128)(2,1)}, u32[]{:S(2)}, u32[]{:S(2)}) collective-permute-start(bf16[512,1024]{1,0:T(8,128)(2,1)} %scale_rows.1.refs_0_), channel_id=1, source_target_pairs={{0,2},{2,4},{4,6},{6,7},{7,5},{5,3},{3,1},{1,0},{8,10},{10,12},{12... | collective-permute-start | bytes 3145736 | tf_op jit(solution)/shard_map/ppermute | solution.py:44
  8.0 3.4 %collective-permute-start.11 = (bf16[512,1024]{1,0:T(8,128)(2,1)}, bf16[512,1024]{1,0:T(8,128)(2,1)}, u32[]{:S(2)}, u32[]{:S(2)}) collective-permute-start(bf16[512,1024]{1,0:T(8,128)(2,1)} %scale_rows.1.refs_0_), channel_id=1, source_target_pairs={{2,3},{3,2},{4,5},{5,4},{10,11},{11,10},{12,13},{13,12},{18,19},{1... | collective-permute-start | bytes 3145736 | tf_op jit(solution)/shard_map/ppermute | solution.py:56
  12.5 1.5 collective-permute-start.3
  15.3 2.3 %copy-done = bf16[1,512,4096]{2,1,0:T(8,128)(2,1)S(1)} copy-done((bf16[1,512,4096]{2,1,0:T(8,128)(2,1)S(1)}, bf16[1,512,4096]{2,1,0:T(8,128)(2,1)}, u32[]{:S(2)}) %copy-start) | copy-done | bytes 4194328
  17.5 1.2 copy-done.11
  18.8 12.0 %norm_and_weight_terms.1 = (bf16[512,1024]{1,0:T(8,128)(2,1)S(1)}, f32[512,128]{1,0:T(8,128)S(1)}, bf16[512,1024]{1,0:T(8,128)(2,1)S(1)}, f32[6,512,1024]{2,1,0:T(8,128)}, f32[512,1024]{1,0:T(8,128)S(1)}) custom-call(s32[8]{0:T(128)S(1)} %compare_select_fusion.4.at, bf16[512,4096]{1,0:T(8,128)(2,1)S(1)} %bitcast.85, bf16[512,1024]{1,0:T(8,128)(2,1)S(1)} %bitcast.89, ...), custom_call_target="tpu_custom_call" | custom-call | flops 4294967296 | bytes 20971520 | tf_op jit(solution)/shard_map/norm_and_weight_terms/pallas_call | solution.py:145
  31.8 1.9 %slice.128 = bf16[256,1024]{1,0:T(8,128)(2,1)} slice(bf16[512,1024]{1,0:T(8,128)(2,1)} %collective-permute-done.refs_1_), slice={[0:256], [0:1024]} | slice | bytes 1048576 | tf_op jit(solution)/shard_map/slice | solution.py:463
  33.7 1.9 %slice.129 = bf16[256,1024]{1,0:T(8,128)(2,1)} slice(bf16[512,1024]{1,0:T(8,128)(2,1)} %collective-permute-done.1.refs_2_), slice={[0:256], [0:1024]} | slice | bytes 1048576 | tf_op jit(solution)/shard_map/slice | solution.py:463
  35.6 2.4 %add.148 = f32[192,1024]{1,0:T(8,128)} add(f32[192,1024]{1,0:T(8,128)} %dynamic-slice_add_fusion, f32[192,1024]{1,0:T(8,128)} %collective-permute-done.3) | non-fusion elementwise | flops 196608 | bytes 2359296 | tf_op jit(solution)/shard_map/add | solution.py:503
  38.0 1.7 %collective-permute-start.5 = (bf16[256,1024]{1,0:T(8,128)(2,1)}, bf16[256,1024]{1,0:T(8,128)(2,1)}, u32[]{:S(2)}, u32[]{:S(2)}) collective-permute-start(bf16[256,1024]{1,0:T(8,128)(2,1)} %slice.129), channel_id=1, source_target_pairs={{2,0},{4,2},{6,4},{7,6},{5,7},{3,5},{1,3},{0,1},{10,8},{12,10},{14... | collective-permute-start | bytes 1572872 | tf_op jit(solution)/shard_map/ppermute | solution.py:47
  40.1 2.3 %broadcast_select_fusion = bf16[512,1024]{1,0:T(8,128)(2,1)} fusion(bf16[512,1024]{1,0:T(8,128)(2,1)} %collective-permute-done.refs_1_, bf16[512,1024]{1,0:T(8,128)(2,1)} %collective-permute-done.1.refs_2_, pred[]{:T(512)} %eq.32), kind=kLoop, calls=%fused_computation.42 | loop fusion | flops 524288 | bytes 3145729 | tf_op jit(solution)/shard_map/jit(_where)/select_n | solution.py:504
  42.4 4.7 %collective-permute-start.12 = (bf16[512,1024]{1,0:T(8,128)(2,1)}, bf16[512,1024]{1,0:T(8,128)(2,1)}, u32[]{:S(2)}, u32[]{:S(2)}) collective-permute-start(bf16[512,1024]{1,0:T(8,128)(2,1)} %broadcast_select_fusion), channel_id=1, source_target_pairs={{2,3},{3,2},{4,5},{5,4},{10,11},{11,10},{12,13},{13,12},{18,19},{1... | collective-permute-start | bytes 3145736 | tf_op jit(solution)/shard_map/ppermute | solution.py:56
  49.5 3.6 %collective-permute-done.5.refs_5_ = bf16[256,1024]{1,0:T(8,128)(2,1)} collective-permute-done((bf16[256,1024]{1,0:T(8,128)(2,1)}, bf16[256,1024]{1,0:T(8,128)(2,1)}, u32[]{:S(2)}, u32[]{:S(2)}) %collective-permute-start.5) | collective-permute-done | bytes 524320 | tf_op jit(solution)/shard_map/ppermute | solution.py:47
  53.1 1.7 %collective-permute-start.7 = (bf16[256,1024]{1,0:T(8,128)(2,1)S(1)}, bf16[256,1024]{1,0:T(8,128)(2,1)S(1)}, u32[]{:S(2)}, u32[]{:S(2)}) collective-permute-start(bf16[256,1024]{1,0:T(8,128)(2,1)S(1)} %slice.130), channel_id=1, source_target_pairs={{0,2},{2,4},{4,6},{6,7},{7,5},{5,3},{3,1},{1,0},{8,10},{10,12},{12... | collective-permute-start | bytes 1572872 | tf_op jit(solution)/shard_map/ppermute | solution.py:44
  54.8 1.6 broadcast_select_fusion.5
  56.4 1.3 broadcast_select_fusion.2
  58.4 1.4 collective-permute-start.9
  59.8 8.3 %project_first.3 = (f32[512,1024]{1,0:T(8,128)}, f32[512,128]{1,0:T(8,128)S(1)}, f32[3,512,512]{2,1,0:T(8,128)}) custom-call(s32[15]{0:T(128)S(1)} %pad_add_fusion.at, bf16[512,4096]{1,0:T(8,128)(2,1)} %bitcast.81, bf16[512,1024]{1,0:T(8,128)(2,1)S(1)} %get-tuple-element.110.kv_grad, f32[512,128]{1,0:T(8,128)S(1)} %copy-done.6, ...), custom_call_target="tpu_custom_call" | custom-call | flops 3221225472 | bytes 11534336 | tf_op jit(solution)/shard_map/project_first/pallas_call | solution.py:390
  68.1 2.4 %collective-permute-done.12.refs_5_ = bf16[512,1024]{1,0:T(8,128)(2,1)} collective-permute-done((bf16[512,1024]{1,0:T(8,128)(2,1)}, bf16[512,1024]{1,0:T(8,128)(2,1)}, u32[]{:S(2)}, u32[]{:S(2)}) %collective-permute-start.12) | collective-permute-done | bytes 1048608 | tf_op jit(solution)/shard_map/ppermute | solution.py:56
  70.7 2.0 %collective-permute-start.13 = (bf16[256,1024]{1,0:T(8,128)(2,1)S(1)}, bf16[256,1024]{1,0:T(8,128)(2,1)S(1)}, u32[]{:S(2)}, u32[]{:S(2)}) collective-permute-start(bf16[256,1024]{1,0:T(8,128)(2,1)S(1)} %get-tuple-element.233), channel_id=1, source_target_pairs={{0,2},{2,4},{4,6},{6,7},{7,5},{5,3},{3,1},{1,0},{8,10},{10,12},{12... | collective-permute-start | bytes 1572872 | tf_op jit(solution)/shard_map/ppermute | solution.py:44
  72.7 2.9 %collective-permute-done.10.refs_7_ = bf16[256,1024]{1,0:T(8,128)(2,1)S(1)} collective-permute-done((bf16[256,1024]{1,0:T(8,128)(2,1)S(1)}, bf16[256,1024]{1,0:T(8,128)(2,1)S(1)}, u32[]{:S(2)}, u32[]{:S(2)}) %collective-permute-start.10) | collective-permute-done | bytes 524320 | tf_op jit(solution)/shard_map/ppermute | solution.py:47
  75.6 3.6 %collective-permute-done.9.refs_5_ = bf16[256,1024]{1,0:T(8,128)(2,1)S(1)} collective-permute-done((bf16[256,1024]{1,0:T(8,128)(2,1)S(1)}, bf16[256,1024]{1,0:T(8,128)(2,1)S(1)}, u32[]{:S(2)}, u32[]{:S(2)}) %collective-permute-start.9) | collective-permute-done | bytes 524320 | tf_op jit(solution)/shard_map/ppermute | solution.py:44
  79.2 1.9 %fusion.21 = (bf16[256,1024]{1,0:T(8,128)(2,1)S(1)}, bf16[256,1024]{1,0:T(8,128)(2,1)S(1)}) fusion(bf16[256,1024]{1,0:T(8,128)(2,1)S(1)} %collective-permute-done.10.refs_7_, f32[6,512,1024]{2,1,0:T(8,128)} %get-tuple-element.155, pred[]{:T(512)} %eq.31, pred[]{:T(512)} %eq.32, bf16[256,1024]{1,0:T(8,128)(2,1)S(1)} %collective-permute-done.9.refs_5_), kind=kLoop, calls=%fused_computation.44 | loop fusion | flops 2621440 | bytes 4194306 | tf_op jit(solution)/shard_map/jit(_where)/select_n | solution.py:542
  81.1 1.7 %collective-permute-start.18 = (bf16[256,1024]{1,0:T(8,128)(2,1)S(1)}, bf16[256,1024]{1,0:T(8,128)(2,1)S(1)}, u32[]{:S(2)}, u32[]{:S(2)}) collective-permute-start(bf16[256,1024]{1,0:T(8,128)(2,1)S(1)} %get-tuple-element.227), channel_id=1, source_target_pairs={{2,0},{4,2},{6,4},{7,6},{5,7},{3,5},{1,3},{0,1},{10,8},{12,10},{14... | collective-permute-start | bytes 1572872 | tf_op jit(solution)/shard_map/ppermute | solution.py:47
  83.2 7.8 %project_first.4 = (f32[512,1024]{1,0:T(8,128)}, f32[512,128]{1,0:T(8,128)S(1)}, f32[2,512,512]{2,1,0:T(8,128)}) custom-call(s32[15]{0:T(128)S(1)} %pad_add_fusion.at, bf16[512,4096]{1,0:T(8,128)(2,1)} %bitcast.82, bf16[512,1024]{1,0:T(8,128)(2,1)S(1)} %get-tuple-element.110.kv_grad, f32[512,128]{1,0:T(8,128)S(1)} %copy-done.6, ...), custom_call_target="tpu_custom_call" | custom-call | flops 2147483648 | bytes 10485760 | tf_op jit(solution)/shard_map/project_first/pallas_call | solution.py:390
  91.0 4.7 %collective-permute-start.23 = (bf16[512,1024]{1,0:T(8,128)(2,1)S(1)}, bf16[512,1024]{1,0:T(8,128)(2,1)S(1)}, u32[]{:S(2)}, u32[]{:S(2)}) collective-permute-start(bf16[512,1024]{1,0:T(8,128)(2,1)S(1)} %copy-done.8), channel_id=1, source_target_pairs={{2,3},{3,2},{4,5},{5,4},{10,11},{11,10},{12,13},{13,12},{18,19},{1... | collective-permute-start | bytes 3145736 | tf_op jit(solution)/shard_map/ppermute | solution.py:56
  95.7 4.8 %fusion.18 = (bf16[256,1024]{1,0:T(8,128)(2,1)}, bf16[256,1024]{1,0:T(8,128)(2,1)}, bf16[256,1024]{1,0:T(8,128)(2,1)S(1)}, bf16[256,1024]{1,0:T(8,128)(2,1)S(1)}) fusion(f32[6,512,1024]{2,1,0:T(8,128)} %get-tuple-element.155, pred[]{:T(512)} %eq.31, bf16[256,1024]{1,0:T(8,128)(2,1)S(1)} %collective-permute-done.14.refs_8_, pred[]{:T(512)} %eq.32, ...), kind=kLoop, calls=%fused_computation.39 | loop fusion | flops 3145728 | bytes 7340034 | tf_op jit(solution)/shard_map/convert_element_type | solution.py:489
  100.5 2.0 %collective-permute-start.15 = (bf16[256,1024]{1,0:T(8,128)(2,1)S(1)}, bf16[256,1024]{1,0:T(8,128)(2,1)S(1)}, u32[]{:S(2)}, u32[]{:S(2)}) collective-permute-start(bf16[256,1024]{1,0:T(8,128)(2,1)S(1)} %get-tuple-element.222), channel_id=1, source_target_pairs={{0,2},{2,4},{4,6},{6,7},{7,5},{5,3},{3,1},{1,0},{8,10},{10,12},{12... | collective-permute-start | bytes 1572872 | tf_op jit(solution)/shard_map/ppermute | solution.py:44
  102.5 1.9 %fusion.11 = (bf16[256,1024]{1,0:T(8,128)(2,1)S(1)}, bf16[256,1024]{1,0:T(8,128)(2,1)S(1)}) fusion(bf16[256,1024]{1,0:T(8,128)(2,1)S(1)} %collective-permute-done.18.refs_8_, f32[6,512,1024]{2,1,0:T(8,128)} %get-tuple-element.155, pred[]{:T(512)} %eq.34, bf16[256,1024]{1,0:T(8,128)(2,1)S(1)} %collective-permute-done.17.refs_6_, pred[]{:T(512)} %eq.33), kind=kLoop, calls=%fused_computation.24 | loop fusion | flops 2097152 | bytes 4194306 | tf_op jit(solution)/shard_map/convert_element_type | solution.py:549
  105.3 1.3 collective-permute-start.21
  106.6 2.5 %fusion.1 = (bf16[384,1024]{1,0:T(8,128)(2,1)}, f32[384,1024]{1,0:T(8,128)}, f32[384,1024]{1,0:T(8,128)}) fusion(bf16[1,384,1024]{2,1,0:T(8,128)(2,1)S(1)} %copy-done.15, f32[384,1024]{1,0:T(8,128)S(1)} %copy-done.12, f32[384,1024]{1,0:T(8,128)S(1)} %copy-done.13, f32[192,1024]{1,0:T(8,128)S(1)} %get-tuple-element.179, f32[192,1024]{1,0:T(8,128)S(1)} %get-tuple-element.178), kind=kLoop, calls=%fused_computation.3 | loop fusion | flops 4718592 | bytes 9437184 | tf_op jit(solution)/shard_map/convert_element_type | solution.py:612
  109.1 6.3 %collective-permute-done.16.refs_9_ = bf16[256,1024]{1,0:T(8,128)(2,1)S(1)} collective-permute-done((bf16[256,1024]{1,0:T(8,128)(2,1)S(1)}, bf16[256,1024]{1,0:T(8,128)(2,1)S(1)}, u32[]{:S(2)}, u32[]{:S(2)}) %collective-permute-start.16) | collective-permute-done | bytes 524320 | tf_op jit(solution)/shard_map/ppermute | solution.py:47
  115.4 1.9 %fusion.10 = (bf16[256,1024]{1,0:T(8,128)(2,1)S(1)}, bf16[256,1024]{1,0:T(8,128)(2,1)S(1)}) fusion(bf16[256,1024]{1,0:T(8,128)(2,1)S(1)} %collective-permute-done.16.refs_9_, f32[6,512,1024]{2,1,0:T(8,128)} %get-tuple-element.155, pred[]{:T(512)} %eq.34, bf16[256,1024]{1,0:T(8,128)(2,1)S(1)} %collective-permute-done.15.refs_7_, pred[]{:T(512)} %eq.33), kind=kLoop, calls=%fused_computation.22 | loop fusion | flops 2097152 | bytes 4194306 | tf_op jit(solution)/shard_map/convert_element_type | solution.py:549
  117.4 2.0 %collective-permute-start.19 = (bf16[256,1024]{1,0:T(8,128)(2,1)S(1)}, bf16[256,1024]{1,0:T(8,128)(2,1)S(1)}, u32[]{:S(2)}, u32[]{:S(2)}) collective-permute-start(bf16[256,1024]{1,0:T(8,128)(2,1)S(1)} %get-tuple-element.224), channel_id=1, source_target_pairs={{0,2},{2,4},{4,6},{6,7},{7,5},{5,3},{3,1},{1,0},{8,10},{10,12},{12... | collective-permute-start | bytes 1572872 | tf_op jit(solution)/shard_map/ppermute | solution.py:44
  119.5 8.0 %project_first.5 = (f32[512,1024]{1,0:T(8,128)}, f32[512,128]{1,0:T(8,128)S(1)}, f32[2,512,512]{2,1,0:T(8,128)}) custom-call(s32[15]{0:T(128)S(1)} %pad_add_fusion.at, bf16[512,4096]{1,0:T(8,128)(2,1)} %bitcast.83, bf16[512,1024]{1,0:T(8,128)(2,1)S(1)} %get-tuple-element.110.kv_grad, f32[512,128]{1,0:T(8,128)S(1)} %copy-done.6, ...), custom_call_target="tpu_custom_call" | custom-call | flops 2147483648 | bytes 10485760 | tf_op jit(solution)/shard_map/project_first/pallas_call | solution.py:390
  127.4 3.1 %collective-permute-start.26 = (bf16[256,1024]{1,0:T(8,128)(2,1)}, bf16[256,1024]{1,0:T(8,128)(2,1)S(1)}, u32[]{:S(2)}, u32[]{:S(2)}) collective-permute-start(bf16[256,1024]{1,0:T(8,128)(2,1)} %get-tuple-element.202), channel_id=1, source_target_pairs={{2,3},{3,2},{4,5},{5,4},{10,11},{11,10},{12,13},{13,12},{18,19},{1... | collective-permute-start | bytes 1572872 | tf_op jit(solution)/shard_map/ppermute | solution.py:56
  130.6 2.0 %fusion.5 = (bf16[256,1024]{1,0:T(8,128)(2,1)S(1)}, bf16[256,1024]{1,0:T(8,128)(2,1)S(1)}) fusion(bf16[256,1024]{1,0:T(8,128)(2,1)S(1)} %collective-permute-done.22, f32[6,512,1024]{2,1,0:T(8,128)} %get-tuple-element.155, pred[]{:T(512)} %eq.32, bf16[512,1024]{1,0:T(8,128)(2,1)S(1)} %collective-permute-done.23, pred[]{:T(512)} %eq.31, ...), kind=kLoop, calls=%fused_computation.13 | loop fusion | flops 2883584 | bytes 4718594 | tf_op jit(solution)/shard_map/convert_element_type | solution.py:556
  132.7 2.0 %collective-permute-start.28 = (bf16[256,1024]{1,0:T(8,128)(2,1)S(1)}, bf16[256,1024]{1,0:T(8,128)(2,1)S(1)}, u32[]{:S(2)}, u32[]{:S(2)}) collective-permute-start(bf16[256,1024]{1,0:T(8,128)(2,1)S(1)} %get-tuple-element.218), channel_id=1, source_target_pairs={{0,2},{2,4},{4,6},{6,7},{7,5},{5,3},{3,1},{1,0},{8,10},{10,12},{12... | collective-permute-start | bytes 1572872 | tf_op jit(solution)/shard_map/ppermute | solution.py:44
  135.0 2.6 %collective-permute-done.19 = bf16[256,1024]{1,0:T(8,128)(2,1)S(1)} collective-permute-done((bf16[256,1024]{1,0:T(8,128)(2,1)S(1)}, bf16[256,1024]{1,0:T(8,128)(2,1)S(1)}, u32[]{:S(2)}, u32[]{:S(2)}) %collective-permute-start.19) | collective-permute-done | bytes 524320 | tf_op jit(solution)/shard_map/ppermute | solution.py:44
  137.6 2.1 %fusion.9 = (bf16[256,1024]{1,0:T(8,128)(2,1)S(1)}, bf16[256,1024]{1,0:T(8,128)(2,1)S(1)}) fusion(bf16[256,1024]{1,0:T(8,128)(2,1)S(1)} %collective-permute-done.20, f32[6,512,1024]{2,1,0:T(8,128)} %get-tuple-element.155, pred[]{:T(512)} %eq.32, bf16[512,1024]{1,0:T(8,128)(2,1)S(1)} %collective-permute-done.23, pred[]{:T(512)} %eq.31, ...), kind=kLoop, calls=%fused_computation.17 | loop fusion | flops 2883584 | bytes 4718594 | tf_op jit(solution)/shard_map/convert_element_type | solution.py:556
  140.0 1.7 %collective-permute-start.24 = (bf16[256,1024]{1,0:T(8,128)(2,1)S(1)}, bf16[256,1024]{1,0:T(8,128)(2,1)S(1)}, u32[]{:S(2)}, u32[]{:S(2)}) collective-permute-start(bf16[256,1024]{1,0:T(8,128)(2,1)S(1)} %get-tuple-element.216), channel_id=1, source_target_pairs={{0,2},{2,4},{4,6},{6,7},{7,5},{5,3},{3,1},{1,0},{8,10},{10,12},{12... | collective-permute-start | bytes 1572872 | tf_op jit(solution)/shard_map/ppermute | solution.py:44
  141.8 3.9 %collective-permute-start.27 = (bf16[256,1024]{1,0:T(8,128)(2,1)S(1)}, bf16[256,1024]{1,0:T(8,128)(2,1)S(1)}, u32[]{:S(2)}, u32[]{:S(2)}) collective-permute-start(bf16[256,1024]{1,0:T(8,128)(2,1)S(1)} %copy-done.16), channel_id=1, source_target_pairs={{2,3},{3,2},{4,5},{5,4},{10,11},{11,10},{12,13},{13,12},{18,19},{1... | collective-permute-start | bytes 1572872 | tf_op jit(solution)/shard_map/ppermute | solution.py:56
  145.7 10.1 %project_last.1 = (bf16[512,1024]{1,0:T(8,128)(2,1)}, bf16[512,4096]{1,0:T(8,128)(2,1)}) custom-call(s32[15]{0:T(128)S(1)} %pad_add_fusion.at, bf16[512,4096]{1,0:T(8,128)(2,1)} %bitcast.84, bf16[512,1024]{1,0:T(8,128)(2,1)S(1)} %get-tuple-element.110.kv_grad, f32[512,128]{1,0:T(8,128)S(1)} %copy-done.6, f32[512,128]{1,0:T(8,128)S(1)} %get-tuple-element.239.cosine, ...), custom_call_target="tpu_custom_call" | custom-call | flops 1073741824 | bytes 9437184 | tf_op jit(solution)/shard_map/project_last/pallas_call | solution.py:390
  155.8 1.4 sum_of_terms.2
  157.2 1.4 sum_of_terms.3
  (85 shorter events, 9.9 us)
Async XLA Ops:
  0.6 1.2 copy-start.1
  4.5 6.9 %copy-start.14 = (f32[1,384,1024]{2,1,0:T(8,128)S(1)}, f32[1,384,1024]{2,1,0:T(8,128)}, u32[]{:S(2)}) copy-start(f32[1,384,1024]{2,1,0:T(8,128)} %param.14) | copy-start | bytes 4718596
  5.8 5.6 %collective-permute-start.2 = (f32[192,1024]{1,0:T(8,128)S(1)}, f32[192,1024]{1,0:T(8,128)S(1)}, u32[]{:S(2)}, u32[]{:S(2)}) collective-permute-start(f32[192,1024]{1,0:T(8,128)S(1)} %constant_dynamic-slice_fusion), channel_id=1, source_target_pairs={{0,8},{8,0},{16,24},{24,16},{1,9},{9,1},{17,25},{25,17},{2,10},{10... | collective-permute-start | bytes 2359304 | tf_op jit(solution)/shard_map/ppermute | solution.py:407
  5.9 25.9 %collective-permute-start.1 = (bf16[512,1024]{1,0:T(8,128)(2,1)}, bf16[512,1024]{1,0:T(8,128)(2,1)}, u32[]{:S(2)}, u32[]{:S(2)}) collective-permute-start(bf16[512,1024]{1,0:T(8,128)(2,1)} %scale_rows.1.refs_0_), channel_id=1, source_target_pairs={{2,0},{4,2},{6,4},{7,6},{5,7},{3,5},{1,3},{0,1},{10,8},{12,10},{14... | collective-permute-start | bytes 3145736 | tf_op jit(solution)/shard_map/ppermute | solution.py:47
  6.0 25.8 %collective-permute-start = (bf16[512,1024]{1,0:T(8,128)(2,1)}, bf16[512,1024]{1,0:T(8,128)(2,1)}, u32[]{:S(2)}, u32[]{:S(2)}) collective-permute-start(bf16[512,1024]{1,0:T(8,128)(2,1)} %scale_rows.1.refs_0_), channel_id=1, source_target_pairs={{0,2},{2,4},{4,6},{6,7},{7,5},{5,3},{3,1},{1,0},{8,10},{10,12},{12... | collective-permute-start | bytes 3145736 | tf_op jit(solution)/shard_map/ppermute | solution.py:44
  8.0 34.4 %collective-permute-start.11 = (bf16[512,1024]{1,0:T(8,128)(2,1)}, bf16[512,1024]{1,0:T(8,128)(2,1)}, u32[]{:S(2)}, u32[]{:S(2)}) collective-permute-start(bf16[512,1024]{1,0:T(8,128)(2,1)} %scale_rows.1.refs_0_), channel_id=1, source_target_pairs={{2,3},{3,2},{4,5},{5,4},{10,11},{11,10},{12,13},{13,12},{18,19},{1... | collective-permute-start | bytes 3145736 | tf_op jit(solution)/shard_map/ppermute | solution.py:56
  12.5 2.8 %copy-start.18 = (s32[8]{0:T(128)S(1)}, s32[8]{0:T(128)}, u32[]{:S(2)}) copy-start(s32[8]{0:T(128)} %constant.120.clone) | copy-start | bytes 100
  12.5 19.4 %collective-permute-start.3 = (f32[192,1024]{1,0:T(8,128)}, f32[192,1024]{1,0:T(8,128)}, u32[]{:S(2)}, u32[]{:S(2)}) collective-permute-start(f32[192,1024]{1,0:T(8,128)} %dynamic-slice_add_fusion), channel_id=1, source_target_pairs={{0,16},{8,24},{16,0},{24,8},{1,17},{9,25},{17,1},{25,9},{2,18},{10... | collective-permute-start | bytes 2359304 | tf_op jit(solution)/shard_map/ppermute | solution.py:407
  15.2 15.6 %copy-start.3 = (f32[512,128]{1,0:T(8,128)}, f32[512,128]{1,0:T(8,128)S(1)}, u32[]{:S(2)}) copy-start(f32[512,128]{1,0:T(8,128)S(1)} %get-tuple-element.240.sine) | copy-start | bytes 786436
  15.3 2.3 %copy-start = (bf16[1,512,4096]{2,1,0:T(8,128)(2,1)S(1)}, bf16[1,512,4096]{2,1,0:T(8,128)(2,1)}, u32[]{:S(2)}) copy-start(bf16[1,512,4096]{2,1,0:T(8,128)(2,1)} %param.10) | copy-start | bytes 12582916
  17.5 1.2 copy-start.11
  30.8 7.2 %copy-start.5 = (f32[512,128]{1,0:T(8,128)}, f32[512,128]{1,0:T(8,128)S(1)}, u32[]{:S(2)}) copy-start(f32[512,128]{1,0:T(8,128)S(1)} %get-tuple-element.111.inv) | copy-start | bytes 786436
  30.8 7.2 %copy-start.7 = (bf16[512,1024]{1,0:T(8,128)(2,1)}, bf16[512,1024]{1,0:T(8,128)(2,1)S(1)}, u32[]{:S(2)}) copy-start(bf16[512,1024]{1,0:T(8,128)(2,1)S(1)} %get-tuple-element.188) | copy-start | bytes 3145732
  37.9 16.9 %collective-permute-start.6 = (f32[192,1024]{1,0:T(8,128)}, f32[192,1024]{1,0:T(8,128)}, u32[]{:S(2)}, u32[]{:S(2)}) collective-permute-start(f32[192,1024]{1,0:T(8,128)} %add.148), channel_id=1, source_target_pairs={{0,8},{8,0},{16,24},{24,16},{1,9},{9,1},{17,25},{25,17},{2,10},{10... | collective-permute-start | bytes 2359304 | tf_op jit(solution)/shard_map/ppermute | solution.py:416
  38.0 9.1 %copy-start.17 = (s32[8]{0:T(128)S(1)}, s32[8]{0:T(128)}, u32[]{:S(2)}) copy-start(s32[8]{0:T(128)} %constant.121.clone) | copy-start | bytes 100
  38.0 15.1 %collective-permute-start.5 = (bf16[256,1024]{1,0:T(8,128)(2,1)}, bf16[256,1024]{1,0:T(8,128)(2,1)}, u32[]{:S(2)}, u32[]{:S(2)}) collective-permute-start(bf16[256,1024]{1,0:T(8,128)(2,1)} %slice.129), channel_id=1, source_target_pairs={{2,0},{4,2},{6,4},{7,6},{5,7},{3,5},{1,3},{0,1},{10,8},{12,10},{14... | collective-permute-start | bytes 1572872 | tf_op jit(solution)/shard_map/ppermute | solution.py:47
  39.7 15.1 %collective-permute-start.4 = (bf16[256,1024]{1,0:T(8,128)(2,1)}, bf16[256,1024]{1,0:T(8,128)(2,1)}, u32[]{:S(2)}, u32[]{:S(2)}) collective-permute-start(bf16[256,1024]{1,0:T(8,128)(2,1)} %slice.128), channel_id=1, source_target_pairs={{0,2},{2,4},{4,6},{6,7},{7,5},{5,3},{3,1},{1,0},{8,10},{10,12},{12... | collective-permute-start | bytes 1572872 | tf_op jit(solution)/shard_map/ppermute | solution.py:44
  42.4 28.2 %collective-permute-start.12 = (bf16[512,1024]{1,0:T(8,128)(2,1)}, bf16[512,1024]{1,0:T(8,128)(2,1)}, u32[]{:S(2)}, u32[]{:S(2)}) collective-permute-start(bf16[512,1024]{1,0:T(8,128)(2,1)} %broadcast_select_fusion), channel_id=1, source_target_pairs={{2,3},{3,2},{4,5},{5,4},{10,11},{11,10},{12,13},{13,12},{18,19},{1... | collective-permute-start | bytes 3145736 | tf_op jit(solution)/shard_map/ppermute | solution.py:56
  49.4 7.0 %copy-start.8 = (bf16[512,1024]{1,0:T(8,128)(2,1)S(1)}, bf16[512,1024]{1,0:T(8,128)(2,1)}, u32[]{:S(2)}) copy-start(bf16[512,1024]{1,0:T(8,128)(2,1)} %copy-done.7) | copy-start | bytes 3145732
  49.5 18.7 %collective-permute-start.8 = (bf16[256,1024]{1,0:T(8,128)(2,1)S(1)}, bf16[256,1024]{1,0:T(8,128)(2,1)S(1)}, u32[]{:S(2)}, u32[]{:S(2)}) collective-permute-start(bf16[256,1024]{1,0:T(8,128)(2,1)S(1)} %slice.131), channel_id=1, source_target_pairs={{2,0},{4,2},{6,4},{7,6},{5,7},{3,5},{1,3},{0,1},{10,8},{12,10},{14... | collective-permute-start | bytes 1572872 | tf_op jit(solution)/shard_map/ppermute | solution.py:47
  53.1 15.0 %collective-permute-start.7 = (bf16[256,1024]{1,0:T(8,128)(2,1)S(1)}, bf16[256,1024]{1,0:T(8,128)(2,1)S(1)}, u32[]{:S(2)}, u32[]{:S(2)}) collective-permute-start(bf16[256,1024]{1,0:T(8,128)(2,1)S(1)} %slice.130), channel_id=1, source_target_pairs={{0,2},{2,4},{4,6},{6,7},{7,5},{5,3},{3,1},{1,0},{8,10},{10,12},{12... | collective-permute-start | bytes 1572872 | tf_op jit(solution)/shard_map/ppermute | solution.py:44
  56.4 3.5 %copy-start.4 = (f32[512,128]{1,0:T(8,128)S(1)}, f32[512,128]{1,0:T(8,128)}, u32[]{:S(2)}) copy-start(f32[512,128]{1,0:T(8,128)} %copy-done.3) | copy-start | bytes 786436
  56.4 3.5 %copy-start.6 = (f32[512,128]{1,0:T(8,128)S(1)}, f32[512,128]{1,0:T(8,128)}, u32[]{:S(2)}) copy-start(f32[512,128]{1,0:T(8,128)} %copy-done.5) | copy-start | bytes 786436
  57.8 17.8 %collective-permute-start.10 = (bf16[256,1024]{1,0:T(8,128)(2,1)S(1)}, bf16[256,1024]{1,0:T(8,128)(2,1)S(1)}, u32[]{:S(2)}, u32[]{:S(2)}) collective-permute-start(bf16[256,1024]{1,0:T(8,128)(2,1)S(1)} %get-tuple-element.234), channel_id=1, source_target_pairs={{2,0},{4,2},{6,4},{7,6},{5,7},{3,5},{1,3},{0,1},{10,8},{12,10},{14... | collective-permute-start | bytes 1572872 | tf_op jit(solution)/shard_map/ppermute | solution.py:47
  58.4 20.8 %collective-permute-start.9 = (bf16[256,1024]{1,0:T(8,128)(2,1)S(1)}, bf16[256,1024]{1,0:T(8,128)(2,1)S(1)}, u32[]{:S(2)}, u32[]{:S(2)}) collective-permute-start(bf16[256,1024]{1,0:T(8,128)(2,1)S(1)} %get-tuple-element.235), channel_id=1, source_target_pairs={{0,2},{2,4},{4,6},{6,7},{7,5},{5,3},{3,1},{1,0},{8,10},{10,12},{12... | collective-permute-start | bytes 1572872 | tf_op jit(solution)/shard_map/ppermute | solution.py:44
  70.6 25.1 %collective-permute-start.14 = (bf16[256,1024]{1,0:T(8,128)(2,1)S(1)}, bf16[256,1024]{1,0:T(8,128)(2,1)S(1)}, u32[]{:S(2)}, u32[]{:S(2)}) collective-permute-start(bf16[256,1024]{1,0:T(8,128)(2,1)S(1)} %get-tuple-element.232), channel_id=1, source_target_pairs={{2,0},{4,2},{6,4},{7,6},{5,7},{3,5},{1,3},{0,1},{10,8},{12,10},{14... | collective-permute-start | bytes 1572872 | tf_op jit(solution)/shard_map/ppermute | solution.py:47
  70.7 25.0 %collective-permute-start.13 = (bf16[256,1024]{1,0:T(8,128)(2,1)S(1)}, bf16[256,1024]{1,0:T(8,128)(2,1)S(1)}, u32[]{:S(2)}, u32[]{:S(2)}) collective-permute-start(bf16[256,1024]{1,0:T(8,128)(2,1)S(1)} %get-tuple-element.233), channel_id=1, source_target_pairs={{0,2},{2,4},{4,6},{6,7},{7,5},{5,3},{3,1},{1,0},{8,10},{10,12},{12... | collective-permute-start | bytes 1572872 | tf_op jit(solution)/shard_map/ppermute | solution.py:44
  81.1 21.4 %collective-permute-start.18 = (bf16[256,1024]{1,0:T(8,128)(2,1)S(1)}, bf16[256,1024]{1,0:T(8,128)(2,1)S(1)}, u32[]{:S(2)}, u32[]{:S(2)}) collective-permute-start(bf16[256,1024]{1,0:T(8,128)(2,1)S(1)} %get-tuple-element.227), channel_id=1, source_target_pairs={{2,0},{4,2},{6,4},{7,6},{5,7},{3,5},{1,3},{0,1},{10,8},{12,10},{14... | collective-permute-start | bytes 1572872 | tf_op jit(solution)/shard_map/ppermute | solution.py:47
  82.8 19.7 %collective-permute-start.17 = (bf16[256,1024]{1,0:T(8,128)(2,1)S(1)}, bf16[256,1024]{1,0:T(8,128)(2,1)S(1)}, u32[]{:S(2)}, u32[]{:S(2)}) collective-permute-start(bf16[256,1024]{1,0:T(8,128)(2,1)S(1)} %get-tuple-element.228), channel_id=1, source_target_pairs={{0,2},{2,4},{4,6},{6,7},{7,5},{5,3},{3,1},{1,0},{8,10},{10,12},{12... | collective-permute-start | bytes 1572872 | tf_op jit(solution)/shard_map/ppermute | solution.py:44
  91.0 36.4 %collective-permute-start.23 = (bf16[512,1024]{1,0:T(8,128)(2,1)S(1)}, bf16[512,1024]{1,0:T(8,128)(2,1)S(1)}, u32[]{:S(2)}, u32[]{:S(2)}) collective-permute-start(bf16[512,1024]{1,0:T(8,128)(2,1)S(1)} %copy-done.8), channel_id=1, source_target_pairs={{2,3},{3,2},{4,5},{5,4},{10,11},{11,10},{12,13},{13,12},{18,19},{1... | collective-permute-start | bytes 3145736 | tf_op jit(solution)/shard_map/ppermute | solution.py:56
  100.5 14.9 %collective-permute-start.16 = (bf16[256,1024]{1,0:T(8,128)(2,1)S(1)}, bf16[256,1024]{1,0:T(8,128)(2,1)S(1)}, u32[]{:S(2)}, u32[]{:S(2)}) collective-permute-start(bf16[256,1024]{1,0:T(8,128)(2,1)S(1)} %get-tuple-element.221), channel_id=1, source_target_pairs={{2,0},{4,2},{6,4},{7,6},{5,7},{3,5},{1,3},{0,1},{10,8},{12,10},{14... | collective-permute-start | bytes 1572872 | tf_op jit(solution)/shard_map/ppermute | solution.py:47
  100.5 6.1 %copy-start.12 = (f32[384,1024]{1,0:T(8,128)S(1)}, f32[384,1024]{1,0:T(8,128)}, u32[]{:S(2)}) copy-start(f32[384,1024]{1,0:T(8,128)} %param.16) | copy-start | bytes 4718596
  100.5 6.1 %copy-start.13 = (f32[384,1024]{1,0:T(8,128)S(1)}, f32[384,1024]{1,0:T(8,128)}, u32[]{:S(2)}) copy-start(f32[384,1024]{1,0:T(8,128)} %param.15) | copy-start | bytes 4718596
  100.5 6.0 %copy-start.15 = (bf16[1,384,1024]{2,1,0:T(8,128)(2,1)S(1)}, bf16[1,384,1024]{2,1,0:T(8,128)(2,1)}, u32[]{:S(2)}) copy-start(bf16[1,384,1024]{2,1,0:T(8,128)(2,1)} %param.17) | copy-start | bytes 2359300
  100.5 14.9 %collective-permute-start.15 = (bf16[256,1024]{1,0:T(8,128)(2,1)S(1)}, bf16[256,1024]{1,0:T(8,128)(2,1)S(1)}, u32[]{:S(2)}, u32[]{:S(2)}) collective-permute-start(bf16[256,1024]{1,0:T(8,128)(2,1)S(1)} %get-tuple-element.222), channel_id=1, source_target_pairs={{0,2},{2,4},{4,6},{6,7},{7,5},{5,3},{3,1},{1,0},{8,10},{10,12},{12... | collective-permute-start | bytes 1572872 | tf_op jit(solution)/shard_map/ppermute | solution.py:44
  104.5 26.1 %collective-permute-start.22 = (bf16[256,1024]{1,0:T(8,128)(2,1)S(1)}, bf16[256,1024]{1,0:T(8,128)(2,1)S(1)}, u32[]{:S(2)}, u32[]{:S(2)}) collective-permute-start(bf16[256,1024]{1,0:T(8,128)(2,1)S(1)} %get-tuple-element.225), channel_id=1, source_target_pairs={{2,0},{4,2},{6,4},{7,6},{5,7},{3,5},{1,3},{0,1},{10,8},{12,10},{14... | collective-permute-start | bytes 1572872 | tf_op jit(solution)/shard_map/ppermute | solution.py:47
  105.3 25.3 %collective-permute-start.21 = (bf16[256,1024]{1,0:T(8,128)(2,1)S(1)}, bf16[256,1024]{1,0:T(8,128)(2,1)S(1)}, u32[]{:S(2)}, u32[]{:S(2)}) collective-permute-start(bf16[256,1024]{1,0:T(8,128)(2,1)S(1)} %get-tuple-element.226), channel_id=1, source_target_pairs={{0,2},{2,4},{4,6},{6,7},{7,5},{5,3},{3,1},{1,0},{8,10},{10,12},{12... | collective-permute-start | bytes 1572872 | tf_op jit(solution)/shard_map/ppermute | solution.py:44
  117.4 17.6 %collective-permute-start.20 = (bf16[256,1024]{1,0:T(8,128)(2,1)S(1)}, bf16[256,1024]{1,0:T(8,128)(2,1)S(1)}, u32[]{:S(2)}, u32[]{:S(2)}) collective-permute-start(bf16[256,1024]{1,0:T(8,128)(2,1)S(1)} %get-tuple-element.223), channel_id=1, source_target_pairs={{2,0},{4,2},{6,4},{7,6},{5,7},{3,5},{1,3},{0,1},{10,8},{12,10},{14... | collective-permute-start | bytes 1572872 | tf_op jit(solution)/shard_map/ppermute | solution.py:47
  117.4 20.1 %collective-permute-start.19 = (bf16[256,1024]{1,0:T(8,128)(2,1)S(1)}, bf16[256,1024]{1,0:T(8,128)(2,1)S(1)}, u32[]{:S(2)}, u32[]{:S(2)}) collective-permute-start(bf16[256,1024]{1,0:T(8,128)(2,1)S(1)} %get-tuple-element.224), channel_id=1, source_target_pairs={{0,2},{2,4},{4,6},{6,7},{7,5},{5,3},{3,1},{1,0},{8,10},{10,12},{12... | collective-permute-start | bytes 1572872 | tf_op jit(solution)/shard_map/ppermute | solution.py:44
  127.4 14.3 %collective-permute-start.26 = (bf16[256,1024]{1,0:T(8,128)(2,1)}, bf16[256,1024]{1,0:T(8,128)(2,1)S(1)}, u32[]{:S(2)}, u32[]{:S(2)}) collective-permute-start(bf16[256,1024]{1,0:T(8,128)(2,1)} %get-tuple-element.202), channel_id=1, source_target_pairs={{2,3},{3,2},{4,5},{5,4},{10,11},{11,10},{12,13},{13,12},{18,19},{1... | collective-permute-start | bytes 1572872 | tf_op jit(solution)/shard_map/ppermute | solution.py:56
  132.6 23.1 %collective-permute-start.29 = (bf16[256,1024]{1,0:T(8,128)(2,1)S(1)}, bf16[256,1024]{1,0:T(8,128)(2,1)S(1)}, u32[]{:S(2)}, u32[]{:S(2)}) collective-permute-start(bf16[256,1024]{1,0:T(8,128)(2,1)S(1)} %get-tuple-element.217), channel_id=1, source_target_pairs={{2,0},{4,2},{6,4},{7,6},{5,7},{3,5},{1,3},{0,1},{10,8},{12,10},{14... | collective-permute-start | bytes 1572872 | tf_op jit(solution)/shard_map/ppermute | solution.py:47
  132.7 23.1 %collective-permute-start.28 = (bf16[256,1024]{1,0:T(8,128)(2,1)S(1)}, bf16[256,1024]{1,0:T(8,128)(2,1)S(1)}, u32[]{:S(2)}, u32[]{:S(2)}) collective-permute-start(bf16[256,1024]{1,0:T(8,128)(2,1)S(1)} %get-tuple-element.218), channel_id=1, source_target_pairs={{0,2},{2,4},{4,6},{6,7},{7,5},{5,3},{3,1},{1,0},{8,10},{10,12},{12... | collective-permute-start | bytes 1572872 | tf_op jit(solution)/shard_map/ppermute | solution.py:44
  137.6 4.2 %copy-start.16 = (bf16[256,1024]{1,0:T(8,128)(2,1)S(1)}, bf16[256,1024]{1,0:T(8,128)(2,1)}, u32[]{:S(2)}) copy-start(bf16[256,1024]{1,0:T(8,128)(2,1)} %get-tuple-element.203) | copy-start | bytes 1572868
  139.7 17.5 %collective-permute-start.25 = (bf16[256,1024]{1,0:T(8,128)(2,1)S(1)}, bf16[256,1024]{1,0:T(8,128)(2,1)S(1)}, u32[]{:S(2)}, u32[]{:S(2)}) collective-permute-start(bf16[256,1024]{1,0:T(8,128)(2,1)S(1)} %get-tuple-element.215), channel_id=1, source_target_pairs={{2,0},{4,2},{6,4},{7,6},{5,7},{3,5},{1,3},{0,1},{10,8},{12,10},{14... | collective-permute-start | bytes 1572872 | tf_op jit(solution)/shard_map/ppermute | solution.py:47
  140.0 17.2 %collective-permute-start.24 = (bf16[256,1024]{1,0:T(8,128)(2,1)S(1)}, bf16[256,1024]{1,0:T(8,128)(2,1)S(1)}, u32[]{:S(2)}, u32[]{:S(2)}) collective-permute-start(bf16[256,1024]{1,0:T(8,128)(2,1)S(1)} %get-tuple-element.216), channel_id=1, source_target_pairs={{0,2},{2,4},{4,6},{6,7},{7,5},{5,3},{3,1},{1,0},{8,10},{10,12},{12... | collective-permute-start | bytes 1572872 | tf_op jit(solution)/shard_map/ppermute | solution.py:44
  141.7 14.0 %copy-start.2 = (bf16[1,512,1024]{2,1,0:T(8,128)(2,1)S(1)}, bf16[1,512,1024]{2,1,0:T(8,128)(2,1)}, u32[]{:S(2)}) copy-start(bf16[1,512,1024]{2,1,0:T(8,128)(2,1)} %param.12) | copy-start | bytes 3145732
  141.8 14.0 %copy-start.10 = (bf16[1,512]{1,0:T(2,128)(2,1)S(1)}, bf16[1,512]{1,0:T(2,128)(2,1)}, u32[]{:S(2)}) copy-start(bf16[1,512]{1,0:T(2,128)(2,1)} %gain.5) | copy-start | bytes 3076
  141.8 15.4 %collective-permute-start.27 = (bf16[256,1024]{1,0:T(8,128)(2,1)S(1)}, bf16[256,1024]{1,0:T(8,128)(2,1)S(1)}, u32[]{:S(2)}, u32[]{:S(2)}) collective-permute-start(bf16[256,1024]{1,0:T(8,128)(2,1)S(1)} %copy-done.16), channel_id=1, source_target_pairs={{2,3},{3,2},{4,5},{5,4},{10,11},{11,10},{12,13},{13,12},{18,19},{1... | collective-permute-start | bytes 1572872 | tf_op jit(solution)/shard_map/ppermute | solution.py:56
  (1 other events, 0.7 us)

commit v12 on v11

--- a/solution.py
+++ b/solution.py
@@ -206,7 +206,10 @@
             pl.BlockSpec((tile, cols), lambda i, row=row: (row(i), 0)),
             pl.BlockSpec((1, tile), lambda i, row=row: (0, row(i))),
         ]
-        specs += [pl.BlockSpec((tile, cols), lambda i: (i, 0))] * len(came)
+        for ref in came:
+            whole = ref.shape[0] == shard
+            at = row if whole else lambda i: i
+            specs.append(pl.BlockSpec((tile, cols), lambda i, at=at: (at(i), 0)))
         operands = [own, weight, gain, *came]
         if outs is not None:
             specs += [pl.BlockSpec(memory_space=pl.ANY)] * 2
@@ -236,39 +239,12 @@
     return outs
 
 
-def part_kernel(plan, before, finish, at, x, kv_grad, inv, cosine, sine, *refs):
-    here = len(plan)
-    done = sum(before)
-    n = done + here
-    total_at = len(refs) - 9
-    blocks, refs = refs[:total_at], refs[total_at:]
-    if before:
-        pre0, sums0, *grads0 = blocks[: 2 + len(before)]
-        blocks = blocks[2 + len(before) :]
-    if finish:
-        kv_out, input_grad, xs, ws, ng, pre, x_sem, w_sem, g_sem = refs
-    else:
-        pre, sums, grads, xs, ws, ng, x_sem, w_sem, g_sem = refs
-    rows, width = x.shape
-    shard = xs.shape[2]
-    kvw = pre.shape[1] // 2
-    held = range(n) if finish else range(done, n)
-    base = held[0]
-
-    def columns(k):
-        return pl.ds(pl.multiple_of(at[k] * shard, shard), shard)
-
-    def x_copy(k):
-        return pltpu.make_async_copy(x.at[:, columns(k)], xs.at[k - base], x_sem.at[k - base])
-
-    def o_copy(k):
-        return pltpu.make_async_copy(xs.at[k], input_grad.at[:, columns(k)], x_sem.at[k])
-
-    for k in range(done, n):
-        x_copy(k).start()
-        for flag, block, start, stop in plan[k - done]:
-            slot = k - done
-            copy = pltpu.make_async_copy(blocks[block], ws.at[slot, start:stop], w_sem.at[slot])
+def start_blocks(plan, at, blocks, ws, w_sem, ks):
+    shard = ws.shape[0] // len(plan)
+    for k in ks:
+        for flag, block, start, stop in plan[k]:
+            there = ws.at[k * shard + start : k * shard + stop]
+            copy = pltpu.make_async_copy(blocks[block], there, w_sem.at[k])
             if flag is None:
                 copy.start()
             else:
@@ -277,147 +253,210 @@
                 def _(copy=copy):
                     copy.start()
 
-    if before:
-        pre[...] = pre0[...]
-        start = sums0[...]
+
+def wait_block(ws, w_sem, k, shard):
+    there = ws.at[k * shard : (k + 1) * shard]
+    pltpu.make_async_copy(there, there, w_sem.at[k]).wait()
+
+
+def columns(at, k, shard):
+    return pl.ds(pl.multiple_of(at[k] * shard, shard), shard)
+
+
+def lane_sums(product):
+    total = product[:, :HEAD]
+    for c in range(HEAD, product.shape[1], HEAD):
+        total = total + product[:, c : c + HEAD]
+    return total
+
+
+def grad_of(kv_grad, weight):
+    return lax.dot_general(
+        kv_grad[...], weight, (((1,), (1,)), ((), ())), preferred_element_type=f32
+    )
+
+
+def early_kernel(plan, at, x, kv_grad, inv, *refs):
+    blocks, (sums, grads, xs, ws, ng, x_sem, w_sem, g_sem) = refs[:-8], refs[-8:]
+    n = len(plan)
+    shard = xs.shape[2]
+
+    def x_copy(k):
+        return pltpu.make_async_copy(x.at[:, columns(at, k, shard)], xs.at[k], x_sem.at[k])
+
+    def g_copy(k):
+        return pltpu.make_async_copy(ng.at[k], grads.at[k], g_sem.at[k])
+
+    for k in range(n):
+        x_copy(k).start()
+        start_blocks(plan, at, blocks, ws, w_sem, [k])
+    total = None
+    for k in range(n):
+        x_copy(k).wait()
+        wait_block(ws, w_sem, k, shard)
+        grad = grad_of(kv_grad, ws[k * shard : (k + 1) * shard, :])
+        ng[k] = grad
+        g_copy(k).start()
+        product = lane_sums(grad * (xs[k].astype(f32) * inv[:, :1]))
+        total = product if total is None else total + product
+    sums[...] = total
+    for k in range(n):
+        g_copy(k).wait()
+
+
+def late_kernel(plan, done, at, x, kv_grad, inv, cosine, sine, *refs):
+    own = 9
+    blocks, refs = refs[:-own], refs[-own:]
+    if done:
+        sums0, grads0, *blocks = blocks
+    kv_out, input_grad, xs, hs, ws, ng, x_sem, w_sem, g_sem = refs
+    n = len(plan)
+    rows, width = x.shape
+    shard = xs.shape[2]
+    cols = ws.shape[1]
+    kvw = cols // 2
+
+    def x_copy(k):
+        return pltpu.make_async_copy(x.at[:, columns(at, k, shard)], xs.at[k], x_sem.at[k])
+
+    def o_copy(k):
+        return pltpu.make_async_copy(xs.at[k], input_grad.at[:, columns(at, k, shard)], x_sem.at[k])
+
+    order = [*range(done, n), *range(done)]
+    for k in order:
+        x_copy(k).start()
+        start_blocks(plan, at, blocks, ws, w_sem, [k])
+    if done:
+        load = pltpu.make_async_copy(grads0, ng.at[:done], g_sem.at[0])
+        load.start()
+        total = sums0[...]
     else:
-        pre[...] = jnp.zeros_like(pre)
-        start = jnp.zeros((rows, HEAD), f32)
-    loads = []
-    if finish:
-        slot = 0
-        for j, count in enumerate(before):
-            loads.append(
-                pltpu.make_async_copy(grads0[j], ng.at[slot : slot + count], g_sem.at[j])
+        total = jnp.zeros((rows, HEAD), f32)
+    for k in order:
+        x_copy(k).wait()
+        normed = xs[k].astype(f32) * inv[:, :1]
+        hs[:, k * shard : (k + 1) * shard] = normed.astype(bf16)
+        if k >= done:
+            wait_block(ws, w_sem, k, shard)
+            grad = grad_of(kv_grad, ws[k * shard : (k + 1) * shard, :])
+            ng[k] = grad
+            total = total + lane_sums(grad * normed)
+    mean = jnp.sum(total, axis=1, keepdims=True) / width
+    if done:
+        load.wait()
+    for k in range(done):
+        wait_block(ws, w_sem, k, shard)
+
+    def project(i, keys):
+        tile = 2 * HEAD
+        at_column = pl.ds(pl.multiple_of(i * tile, tile), tile)
+        pre = jnp.dot(hs[...], ws[:, at_column], preferred_element_type=f32)
+        if keys:
+            turned = [pltpu.roll(pre[:, c : c + HEAD], HEAD // 2, 1) for c in (0, HEAD)]
+            pre = jnp.concatenate(
+                [
+                    pre[:, c : c + HEAD] * cosine[...] + part * sine[...]
+                    for c, part in zip((0, HEAD), turned)
+                ],
+                axis=1,
             )
-            slot += count
-        for load in loads:
-            load.start()
-        for k in range(done):
-            x_copy(k).start()
-
-    def gather(i, total):
-        k = done + i
-        x_copy(k).wait()
-        pltpu.make_async_copy(ws.at[i], ws.at[i], w_sem.at[i]).wait()
-        weight = ws[i]
-        normed = xs[k - base].astype(f32) * inv[:, :1]
-        pre[...] += jnp.dot(normed.astype(bf16), weight, preferred_element_type=f32)
-        grad = lax.dot_general(
-            kv_grad[...], weight, (((1,), (1,)), ((), ())), preferred_element_type=f32
-        )
-        ng[k - base] = grad
-        if not finish:
-            pltpu.make_async_copy(ng.at[i], grads.at[i], g_sem.at[i]).start()
-        product = grad * normed
-        for c in range(0, shard, HEAD):
-            total = total + product[:, c : c + HEAD]
-        return total
-
-    total = lax.fori_loop(0, here, gather, start)
-    if not finish:
-        sums[...] = total
-        for i in range(here):
-            pltpu.make_async_copy(ng.at[i], grads.at[i], g_sem.at[i]).wait()
-        return
-    mean = jnp.sum(total, axis=1, keepdims=True) / width
-    for load in loads:
-        load.wait()
-
-    def write(k, carry):
-        @pl.when(k < done)
-        def _():
-            x_copy(k).wait()
-
+        kv_out[:, at_column] = pre.astype(bf16)
+
+    def finish(k):
         scale = inv[:, :1]
         normed = xs[k].astype(f32) * scale
         xs[k] = (scale * (ng[k] - normed * mean)).astype(bf16)
         o_copy(k).start()
-        return carry
-
-    lax.fori_loop(0, n, write, 0)
-    for c in range(0, kvw, HEAD):
-        part = pre[:, c : c + HEAD]
-        turned = pltpu.roll(part, HEAD // 2, 1)
-        kv_out[:, c : c + HEAD] = (part * cosine[...] + turned * sine[...]).astype(bf16)
-    kv_out[:, kvw:] = pre[:, kvw:].astype(bf16)
-
-    def drain(k, carry):
-        o_copy(k).wait()
-        return carry
-
-    lax.fori_loop(0, n, drain, 0)
-
-
-def project_part(at, tokens_in, kv_grad, inv, cosine, sine, blocks, plan, carry, before, finish):
-    rows, width = tokens_in.shape
-    cols = kv_grad.shape[1]
-    here = len(plan)
-    n = sum(before) + here
+
+    lax.fori_loop(0, n, lambda k, c: (finish(k), c)[1], 0)
+    tiles = kvw // (2 * HEAD)
+    lax.fori_loop(0, tiles, lambda i, c: (project(i, True), c)[1], 0)
+    lax.fori_loop(tiles, 2 * tiles, lambda i, c: (project(i, False), c)[1], 0)
+    lax.fori_loop(0, n, lambda k, c: (o_copy(k).wait(), c)[1], 0)
+
+
+def pick_blocks(blocks, plan):
     used = sorted({entry[1] for entries in plan for entry in entries})
     plan = tuple(
         tuple((flag, used.index(block), *rest) for flag, block, *rest in entries)
         for entries in plan
     )
-    blocks = [blocks[i] for i in used]
-    shard = plan[0][0][3] if len(plan[0]) == 1 else max(entry[3] for entry in plan[0])
+    return [blocks[i] for i in used], plan
+
+
+def early_part(at, tokens_in, kv_grad, inv, blocks, plan, shard):
+    rows, width = tokens_in.shape
+    cols = kv_grad.shape[1]
+    n = len(plan)
+    blocks, plan = pick_blocks(blocks, plan)
     whole = pl.BlockSpec(memory_space=pltpu.VMEM)
     there = pl.BlockSpec(memory_space=pl.ANY)
-    in_specs = [pl.BlockSpec(memory_space=pltpu.SMEM), there] + [whole] * 4
-    in_specs += [whole, whole][: 2 if before else 0] + [there] * (len(before) + len(blocks))
-    slots = n if finish else here
-    scratch = [
-        pltpu.VMEM((slots, rows, shard), bf16),
-        pltpu.VMEM((here, shard, cols), bf16),
-    ]
-    if finish:
-        scratch += [pltpu.VMEM((n, rows, shard), f32), pltpu.VMEM((rows, cols), f32)]
-        out_specs = [whole, there]
-        out_shape = [
+    return pl.pallas_call(
+        functools.partial(early_kernel, plan),
+        in_specs=[pl.BlockSpec(memory_space=pltpu.SMEM), there, whole, whole]
+        + [there] * len(blocks),
+        out_specs=[whole, there],
+        out_shape=[
+            jax.ShapeDtypeStruct((rows, HEAD), f32),
+            jax.ShapeDtypeStruct((n, rows, shard), f32),
+        ],
+        scratch_shapes=[
+            pltpu.VMEM((n, rows, shard), bf16),
+            pltpu.VMEM((n * shard, cols), bf16),
+            pltpu.VMEM((n, rows, shard), f32),
+        ]
+        + [pltpu.SemaphoreType.DMA((n,))] * 3,
+        compiler_params=pltpu.CompilerParams(vmem_limit_bytes=40 * 2**20),
+        cost_estimate=pl.CostEstimate(
+            flops=2 * rows * shard * n * cols,
+            bytes_accessed=shard * n * (6 * rows + 2 * cols),
+            transcendentals=0,
+        ),
+        name="project_first",
+    )(at, tokens_in, kv_grad, inv, *blocks)
+
+
+def late_part(at, tokens_in, kv_grad, inv, cosine, sine, blocks, plan, shard, carry=()):
+    rows, width = tokens_in.shape
+    cols = kv_grad.shape[1]
+    n = len(plan)
+    done = carry[1].shape[0] if carry else 0
+    blocks, plan = pick_blocks(blocks, plan)
+    whole = pl.BlockSpec(memory_space=pltpu.VMEM)
+    there = pl.BlockSpec(memory_space=pl.ANY)
+    return pl.pallas_call(
+        functools.partial(late_kernel, plan, done),
+        in_specs=[pl.BlockSpec(memory_space=pltpu.SMEM), there]
+        + [whole] * 4
+        + [whole, there][: len(carry)]
+        + [there] * len(blocks),
+        out_specs=[whole, there],
+        out_shape=[
             jax.ShapeDtypeStruct((rows, cols), bf16),
             jax.ShapeDtypeStruct((rows, width), bf16),
+        ],
+        scratch_shapes=[
+            pltpu.VMEM((n, rows, shard), bf16),
+            pltpu.VMEM((rows, n * shard), bf16),
+            pltpu.VMEM((n * shard, cols), bf16),
+            pltpu.VMEM((n, rows, shard), f32),
         ]
-    else:
-        scratch.append(pltpu.VMEM((here, rows, shard), f32))
-        out_specs = [whole, whole, there]
-        out_shape = [
-            jax.ShapeDtypeStruct((rows, cols), f32),
-            jax.ShapeDtypeStruct((rows, HEAD), f32),
-            jax.ShapeDtypeStruct((here, rows, shard), f32),
-        ]
-    scratch += [pltpu.SemaphoreType.DMA((slots,)), pltpu.SemaphoreType.DMA((here,))]
-    scratch += [pltpu.SemaphoreType.DMA((max(len(before), here),))]
-    return pl.pallas_call(
-        functools.partial(part_kernel, plan, tuple(before), finish),
-        in_specs=in_specs,
-        out_specs=out_specs,
-        out_shape=out_shape,
-        scratch_shapes=scratch,
+        + [pltpu.SemaphoreType.DMA((n,))] * 3,
         compiler_params=pltpu.CompilerParams(vmem_limit_bytes=48 * 2**20),
         cost_estimate=pl.CostEstimate(
-            flops=4 * rows * shard * here * cols,
-            bytes_accessed=4 * rows * width + 2 * shard * here * cols,
+            flops=4 * rows * width * cols,
+            bytes_accessed=4 * rows * width + 2 * width * cols,
             transcendentals=0,
         ),
-        name="project_last" if finish else "project_first",
+        name="project_last",
     )(at, tokens_in, kv_grad, inv, cosine, sine, *carry, *blocks)
 
 
-def replica_pairs(value, odd):
-    swap = lambda v, step: lax.ppermute(v, "replica", [(r, r ^ step) for r in range(4)])
-    half = value.shape[0] // 2
-    mine = lax.dynamic_slice_in_dim(value, odd * half, half, 0)
-    theirs = lax.dynamic_slice_in_dim(value, (1 - odd) * half, half, 0)
-    mine = mine + swap(theirs, 1)
-    return mine, swap(mine, 2)
-
-
-def replica_halves(mine, odd):
-    theirs = lax.ppermute(mine, "replica", [(r, r ^ 1) for r in range(4)])
-    return jnp.where(odd, theirs, mine), jnp.where(odd, mine, theirs)
-
-
-def exchange_ring(ring, own, far, near, pseudo, project, update):
+def replica_swap(value, step):
+    return lax.ppermute(value, "replica", [(r, r ^ step) for r in range(4)])
+
+
+def exchange_ring(ring, own, far, near, pseudo, early, late, update):
     total = lax.psum(pseudo, "replica")
     shard, cut = own.shape[0], own.shape[0] // 2
     blocks = [own]
@@ -441,15 +480,14 @@
         from_left = ring.to_right((near[k] + from_left.astype(f32)).astype(bf16))
         from_right = ring.to_left((near[k + 1] + from_right.astype(f32)).astype(bf16))
     sums = [(from_left, from_right)]
-    return project(blocks, tuple(plan), (), (), True), sums, update(total)
-
-
-ORDER = {"sum": (0, 2), "inner": (3, 8), "far": (0, 3), "partner0": (4, None), "partner1": (6, None), "part0": (1, 3), "part1": (2, 5), "part2": (5, 9), "update": (3, 7)}
+    return late(blocks, plan), sums, update(total)
+
+
+ORDER = {"sum": (-1, 3), "pair": (-1, 3), "inner": (2, 7), "far": (1, 5), "partner": (7, None), "first": (2, 4), "update": (4, 7)}
 CHAIN = True
-PAIR = 4
-
-
-def exchange_plane(plane, own, far, near, pseudo, project, update):
+
+
+def exchange_plane(plane, own, far, near, pseudo, early, late, update):
     shard = own.shape[0]
     at0, at1, at2, at3 = plane.at
     zero = jnp.zeros((), f32)
@@ -477,55 +515,31 @@
     def later(step, *values):
         names = [name for name, (_, end) in ORDER.items() if end == step]
         awaited = [beside[name] for name in names]
-        if step == PAIR:
-            awaited.append(partner[0])
         values, awaited = lax.optimization_barrier((after(values, sent[0]), awaited))
         beside.update(zip(names, awaited))
-        if step == PAIR:
-            partner[0] = awaited[-1]
         return values
 
-    def for_partner(h):
-        return pick(at1, part(near[1], h), part(near[0], h)).astype(bf16)
-
     ways = lambda flag, at: tuple((flag, at + h, *pieces[h]) for h in halves)
-    carry, before = [()], []
-
-    def part_of(plan, blocks, last=False):
-        blocks = [after(blocks[0], sent[0]), *blocks[1:]]
-        outs = project(blocks, plan, carry[0], tuple(before), last)
-        if not last:
-            carry[0] = (*outs[:2], *carry[0][2:], outs[2])
-            before.append(len(plan))
-        return outs
-
+    by_way = lambda steps: [steps[h][way] for way in range(2) for h in halves]
+    near_plan = [((None, k, 0, shard),) for k in range(3)] + [ways(None, 3), ways(None, 5)]
     tasks = {
-        "sum": lambda: replica_halves(after(mine, sent[0]) + came, odd),
         "far": lambda: chord(pick(at2, *first)),
         "inner": lambda: chord(far),
-        "partner0": lambda: chord(for_partner(0)),
-        "partner1": lambda: chord(for_partner(1)),
-        "part0": lambda: part_of(
-            tuple(((None, k, 0, shard),) for k in range(3)), [own, *first]
-        ),
-        "part1": lambda: part_of((ways(None, 0), ways(None, 2)), by_way(two)),
-        "part2": lambda: part_of(
-            (((0, 0, 0, shard), *ways(2, 1)), ((1, 0, 0, shard), *ways(3, 3))),
-            [partner[0], *by_way(three)],
-        ),
-        "update": lambda: update(after(beside["sum"], sent[0])),
+        "partner": lambda: chord(pick(at1, near[1], near[0]).astype(bf16)),
+        "first": lambda: early([after(own, sent[0]), *first, *by_way(two)], near_plan),
+        "update": lambda: update(after((pairs, beside["sum"]), sent[0])),
     }
-    by_way = lambda steps: [steps[h][way] for way in range(2) for h in halves]
 
     first = ring(None, own, own)
-    partner = [chord(own)]
-    odd = lax.axis_index("replica") % 2 == 1
+    beside["pair"] = chord(own)
     if lax.axis_size("replica") == 4:
-        mine, came = replica_pairs(after(pseudo, own), odd.astype(jnp.int32))
+        pairs = after(pseudo, own)
+        pairs = (pairs + replica_swap(pairs, 1)).astype(bf16)
+        came = replica_swap(pairs, 2)
     else:
-        came = lax.psum(pseudo, "replica")
-        tasks["sum"] = lambda: came
-    first, far, came = lax.optimization_barrier((first, far, came))
+        pairs, came = lax.psum(pseudo, "replica"), jnp.zeros((), f32)
+    first, far, pairs = lax.optimization_barrier((first, far, pairs))
+    beside["sum"] = came
     two = [ring(0, *(part(side, 0) for side in first))]
     two.append(ring(1, *(part(side, 1) for side in later(1, *first))))
     three = []
@@ -554,12 +568,15 @@
         to_right = part(near[4], h) + wide(left) + pick(at1, over, zero)
         to_left = part(near[5], h) + wide(right) + pick(at2, over, zero)
         six.append(ring(8 + h, to_right.astype(bf16), to_left.astype(bf16)))
-    sums = [(*six[h], beside["partner%d" % h]) for h in halves]
-
-    outs = part_of(
-        (((4, 0, 0, shard), *ways(5, 1), *ways(6, 3)),), [beside["far"], *by_way(four)], True
-    )
-    return outs, sums, beside["update"]
+    sums = [(*six[h], beside["partner"]) for h in halves]
+
+    blocks = [own, *first, *by_way(two), beside["pair"], *by_way(three), beside["far"], *by_way(four)]
+    plan = near_plan + [
+        ((0, 7, 0, shard), *ways(2, 8)),
+        ((1, 7, 0, shard), *ways(3, 10)),
+        ((4, 12, 0, shard), *ways(5, 13), *ways(6, 15)),
+    ]
+    return late(blocks, plan, beside["first"]), sums, beside["update"]
 
 
 def local(
@@ -598,12 +615,15 @@
         at.append(jnp.stack(flags).astype(jnp.int32))
     at = jnp.concatenate(at)
 
-    def project(*args):
-        return project_part(at, tokens_in, kv_grad, inv, cosine, sine, *args)
+    def early(blocks, plan):
+        return early_part(at, tokens_in, kv_grad, inv, blocks, plan, shard)
+
+    def late(blocks, plan, carry=()):
+        return late_part(at, tokens_in, kv_grad, inv, cosine, sine, blocks, plan, shard, carry)
 
     def update(total):
         if isinstance(total, tuple):
-            total = jnp.concatenate(total)
+            total = total[0].astype(f32) + total[1].astype(f32)
         average = total / lax.axis_size("replica")
         momentum_new = momentum_rate * outer_momentum + average
         global_new = global_params - outer_rate * (average + momentum_rate * momentum_new)
@@ -614,7 +634,7 @@
 
     exchange = exchange_plane if small else exchange_ring
     (kv_out, input_grad), sums, updated = exchange(
-        ring, own, far, near, pseudo_grad[0], project, update
+        ring, own, far, near, pseudo_grad[0], early, late, update
     )
     momentum_new, global_new, local_new = updated
     weight_grad, gain_grad = last_part(last, weight_shard, norm_gain, sums)

time: 161 us -> 157 us (0.975)
  waiting for transfers between devices: 22.8 us -> 39.3 us
  Pallas kernels: 50.9 us -> 37.9 us
  other arithmetic: 27.2 us -> 22.4 us
  local copies, waits for them, and re-layouts: 12.8 us -> 10.9 us
    ppermute x11, waiting for transfers between devices: 14.1 us -> 33.1 us  [to_left(): return lax.ppermute(value, 'fsdp', self.left)]
    pallas_call x4 -> x2, Pallas kernels: 34.1 us -> 22.4 us  [the longest x1 16.3 us: late_part(): pl.pallas_call(functools.partial(late_kernel, plan, done), in_specs=[pl.B...]
    ppermute x11, starting transfers between devices: 5.41 us -> 13.5 us  [to_left(): return lax.ppermute(value, 'fsdp', self.left)]
    ppermute x11, starting transfers between devices: 17 us -> 10 us  [to_right(): return lax.ppermute(value, 'fsdp', self.right)]
    add x2 -> x0, other arithmetic: 3.37 us -> none  [the longest x1 2.37 us: exchange_plane(): after(mine, sent[0]) + came]
    convert_element_type x2, other arithmetic: 4.12 us -> 0.94 us  [exchange_plane(): six.append(ring(8 + h, to_right.astype(bf16), to_left.astype(bf16)))]
    ppermute x5 -> x4, starting transfers between devices: 19.7 us -> 17.1 us  [over_chord(): return lax.ppermute(value, 'fsdp', [(2, 3), (3, 2), (4, 5), (5, 4)])]
    slice x4, local copies, waits for them, and re-layouts: 5.89 us -> 3.33 us  [part(): return value[pieces[h][0]:pieces[h][1]]]
  transfers between devices with their start and end apart: 30 -> 28, of which waited for: 9 -> 15; matrix products, arithmetic and copies ran while one was open for 21% -> 17% of each run, Pallas kernels for 30% -> 22%
where the time goes in v12:
time: 157 us; the launch traced here: 154 us
  starting transfers between devices  42.2 us (27%)
  waiting for transfers between devices  39.3 us (25%)
  Pallas kernels  37.9 us (24%)
  other arithmetic  22.4 us (14%)
  local copies, waits for them, and re-layouts  10.9 us (7%)
    ppermute x11, waiting for transfers between devices, to_left(): return lax.ppermute(value, 'fsdp', self.left)  33.1 us
    ppermute x4, starting transfers between devices, over_chord(): return lax.ppermute(value, 'fsdp', [(2, 3), (3, 2), (4, 5), (5, 4)])  17.1 us
    pallas_call x1, Pallas kernels, late_part(): pl.pallas_call(functools.partial(late_kernel, plan, done), in_specs=[pl.B...  16.3 us
    ppermute x11, starting transfers between devices, to_left(): return lax.ppermute(value, 'fsdp', self.left)  13.5 us
    pallas_call x1, Pallas kernels, first_part(): pl.pallas_call(functools.partial(first_kernel, scale), grid_spec=pltpu.Pr...  12.1 us
    ppermute x11, starting transfers between devices, to_right(): return lax.ppermute(value, 'fsdp', self.right)  10 us
    unnamed x66, local copies, waits for them, and re-layouts  7.44 us
    ppermute x11, waiting for transfers between devices, to_right(): return lax.ppermute(value, 'fsdp', self.right)  6.26 us
  transfers between devices with their start and end apart: 28, of which 15 were waited for; matrix products, arithmetic and copies ran while one was open for 17% of the time, Pallas kernels for 22%

profile of v12, /device:TPU:8, one launch (start us, length us, event | category | flops | bytes accessed | tf_op | source)
XLA Modules:
  0.0 153.9 jit_solution(380580618108688730)
XLA Ops:
  0.6 1.2 copy-done
  3.5 2.0 %collective-permute-start = (bf16[512,1024]{1,0:T(8,128)(2,1)S(1)}, bf16[512,1024]{1,0:T(8,128)(2,1)S(1)}, u32[]{:S(2)}, u32[]{:S(2)}) collective-permute-start(bf16[512,1024]{1,0:T(8,128)(2,1)S(1)} %scale_rows.1.refs_0_.refs_2_), channel_id=1, source_target_pairs={{0,2},{2,4},{4,6},{6,7},{7,5},{5,3},{3,1},{1,0},{8,10},{10,12},{12... | collective-permute-start | bytes 3145736 | tf_op jit(solution)/shard_map/ppermute | solution.py:44
  5.5 3.4 %collective-permute-start.10 = (bf16[512,1024]{1,0:T(8,128)(2,1)S(1)}, bf16[512,1024]{1,0:T(8,128)(2,1)}, u32[]{:S(2)}, u32[]{:S(2)}) collective-permute-start(bf16[512,1024]{1,0:T(8,128)(2,1)S(1)} %scale_rows.1.refs_0_.refs_2_), channel_id=1, source_target_pairs={{2,3},{3,2},{4,5},{5,4},{10,11},{11,10},{12,13},{13,12},{18,19},{1... | collective-permute-start | bytes 3145736 | tf_op jit(solution)/shard_map/ppermute | solution.py:56
  8.9 1.0 fusion.23
  10.2 2.3 %copy-done.6 = bf16[1,512,4096]{2,1,0:T(8,128)(2,1)S(1)} copy-done((bf16[1,512,4096]{2,1,0:T(8,128)(2,1)S(1)}, bf16[1,512,4096]{2,1,0:T(8,128)(2,1)}, u32[]{:S(2)}) %copy-start.6) | copy-done | bytes 4194328
  12.5 12.1 %norm_and_weight_terms.1 = (bf16[512,1024]{1,0:T(8,128)(2,1)S(1)}, f32[512,128]{1,0:T(8,128)S(1)}, bf16[512,1024]{1,0:T(8,128)(2,1)S(1)}, f32[6,512,1024]{2,1,0:T(8,128)}, f32[512,1024]{1,0:T(8,128)S(1)}) custom-call(s32[8]{0:T(128)S(1)} %compare_select_fusion.4.at, bf16[512,4096]{1,0:T(8,128)(2,1)S(1)} %bitcast.79, bf16[512,1024]{1,0:T(8,128)(2,1)S(1)} %bitcast.81, ...), custom_call_target="tpu_custom_call" | custom-call | flops 4294967296 | bytes 20971520 | tf_op jit(solution)/shard_map/norm_and_weight_terms/pallas_call | solution.py:145
  24.6 1.0 copy-done.11
  25.6 3.4 %collective-permute-done.1.refs_2_.refs_4_ = bf16[512,1024]{1,0:T(8,128)(2,1)S(1)} collective-permute-done((bf16[512,1024]{1,0:T(8,128)(2,1)S(1)}, bf16[512,1024]{1,0:T(8,128)(2,1)S(1)}, u32[]{:S(2)}, u32[]{:S(2)}) %collective-permute-start.1) | collective-permute-done | bytes 1048608 | tf_op jit(solution)/shard_map/ppermute | solution.py:47
  29.0 3.7 %add_convert_fusion = bf16[384,1024]{1,0:T(8,128)(2,1)} fusion(f32[384,1024]{1,0:T(8,128)} %bitcast.10, f32[384,1024]{1,0:T(8,128)} %collective-permute-done.2), kind=kLoop, calls=%fused_computation.7 | loop fusion | flops 786432 | bytes 3932160 | tf_op jit(solution)/shard_map/convert_element_type | solution.py:537
  32.7 0.8 slice.128
  33.6 1.3 collective-permute-start.4
  34.8 1.5 collective-permute-start.9
  38.8 0.8 slice.130
  39.6 1.3 collective-permute-start.8
  40.9 1.1 broadcast_select_fusion
  42.7 6.0 %collective-permute-done.4.refs_5_.refs_7_ = bf16[256,1024]{1,0:T(8,128)(2,1)} collective-permute-done((bf16[256,1024]{1,0:T(8,128)(2,1)}, bf16[256,1024]{1,0:T(8,128)(2,1)}, u32[]{:S(2)}, u32[]{:S(2)}) %collective-permute-start.4) | collective-permute-done | bytes 524320 | tf_op jit(solution)/shard_map/ppermute | solution.py:47
  48.7 4.3 %collective-permute-start.13 = (bf16[512,1024]{1,0:T(8,128)(2,1)}, bf16[512,1024]{1,0:T(8,128)(2,1)}, u32[]{:S(2)}, u32[]{:S(2)}) collective-permute-start(bf16[512,1024]{1,0:T(8,128)(2,1)} %broadcast_select_fusion), channel_id=1, source_target_pairs={{2,3},{3,2},{4,5},{5,4},{10,11},{11,10},{12,13},{13,12},{18,19},{1... | collective-permute-start | bytes 3145736 | tf_op jit(solution)/shard_map/ppermute | solution.py:56
  53.3 1.6 %broadcast_select_fusion.2 = (bf16[256,1024]{1,0:T(8,128)(2,1)S(1)}, bf16[256,1024]{1,0:T(8,128)(2,1)S(1)}) fusion(bf16[256,1024]{1,0:T(8,128)(2,1)} %collective-permute-done.4.refs_5_.refs_7_, pred[]{:T(512)} %eq.29, bf16[512,1024]{1,0:T(8,128)(2,1)} %copy-done.9, bf16[256,1024]{1,0:T(8,128)(2,1)} %collective-permute-done.3.refs_3_.refs_5_, pred[]{:T(512)} %eq.30), kind=kLoop, calls=%fused_computation.47 | loop fusion | flops 524288 | bytes 2621442 | tf_op jit(solution)/shard_map/jit(_where)/select_n | solution.py:549
  55.4 4.5 %collective-permute-done.8.refs_6_.refs_8_ = bf16[256,1024]{1,0:T(8,128)(2,1)} collective-permute-done((bf16[256,1024]{1,0:T(8,128)(2,1)}, bf16[256,1024]{1,0:T(8,128)(2,1)}, u32[]{:S(2)}, u32[]{:S(2)}) %collective-permute-start.8) | collective-permute-done | bytes 524320 | tf_op jit(solution)/shard_map/ppermute | solution.py:47
  59.9 1.6 %collective-permute-start.5 = (bf16[256,1024]{1,0:T(8,128)(2,1)S(1)}, bf16[256,1024]{1,0:T(8,128)(2,1)S(1)}, u32[]{:S(2)}, u32[]{:S(2)}) collective-permute-start(bf16[256,1024]{1,0:T(8,128)(2,1)S(1)} %get-tuple-element.209), channel_id=1, source_target_pairs={{0,2},{2,4},{4,6},{6,7},{7,5},{5,3},{3,1},{1,0},{8,10},{10,12},{12... | collective-permute-start | bytes 1572872 | tf_op jit(solution)/shard_map/ppermute | solution.py:44
  61.5 0.8 collective-permute-done.7.refs_4_.refs_6_
  62.3 1.3 broadcast_select_fusion.1
  63.6 2.7 %collective-permute-start.12 = (bf16[256,1024]{1,0:T(8,128)(2,1)S(1)}, bf16[256,1024]{1,0:T(8,128)(2,1)S(1)}, u32[]{:S(2)}, u32[]{:S(2)}) collective-permute-start(bf16[256,1024]{1,0:T(8,128)(2,1)S(1)} %get-tuple-element.206), channel_id=1, source_target_pairs={{2,0},{4,2},{6,4},{7,6},{5,7},{3,5},{1,3},{0,1},{10,8},{12,10},{14... | collective-permute-start | bytes 1572872 | tf_op jit(solution)/shard_map/ppermute | solution.py:47
  66.3 1.2 copy-done.12
  67.6 0.9 copy-done.16
  68.5 6.0 %project_first.1 = (f32[512,128]{1,0:T(8,128)S(1)}, f32[5,512,512]{2,1,0:T(8,128)}) custom-call(s32[15]{0:T(128)S(1)} %pad_add_fusion.at, bf16[512,4096]{1,0:T(8,128)(2,1)S(1)} %bitcast.80, bf16[512,1024]{1,0:T(8,128)(2,1)S(1)} %copy-done.12, f32[512,128]{1,0:T(8,128)S(1)} %copy-done.16, bf16[512,1024]{1,0:T(8,128)(2,1)S(1)} %scale_rows.1.refs_0_.refs_2_, ...), custom_call_target="tpu_custom_call" | custom-call | flops 2684354560 | bytes 13107200 | tf_op jit(solution)/shard_map/project_first/pallas_call | solution.py:394
  74.8 5.0 %collective-permute-start.18 = (bf16[512,1024]{1,0:T(8,128)(2,1)S(1)}, bf16[512,1024]{1,0:T(8,128)(2,1)S(1)}, u32[]{:S(2)}, u32[]{:S(2)}) collective-permute-start(bf16[512,1024]{1,0:T(8,128)(2,1)S(1)} %copy-done.10), channel_id=1, source_target_pairs={{2,3},{3,2},{4,5},{5,4},{10,11},{11,10},{12,13},{13,12},{18,19},{1... | collective-permute-start | bytes 3145736 | tf_op jit(solution)/shard_map/ppermute | solution.py:56
  79.8 2.1 %fusion.20 = (bf16[256,1024]{1,0:T(8,128)(2,1)S(1)}, bf16[256,1024]{1,0:T(8,128)(2,1)S(1)}) fusion(bf16[256,1024]{1,0:T(8,128)(2,1)S(1)} %collective-permute-done.6.refs_12_, f32[6,512,1024]{2,1,0:T(8,128)} %get-tuple-element.138, pred[]{:T(512)} %eq.27, pred[]{:T(512)} %eq.28, bf16[256,1024]{1,0:T(8,128)(2,1)S(1)} %collective-permute-done.5.refs_10_), kind=kLoop, calls=%fused_computation.43 | loop fusion | flops 2621440 | bytes 4194306 | tf_op jit(solution)/shard_map/jit(_where)/select_n | solution.py:556
  82.0 2.0 %collective-permute-start.14 = (bf16[256,1024]{1,0:T(8,128)(2,1)S(1)}, bf16[256,1024]{1,0:T(8,128)(2,1)S(1)}, u32[]{:S(2)}, u32[]{:S(2)}) collective-permute-start(bf16[256,1024]{1,0:T(8,128)(2,1)S(1)} %get-tuple-element.204), channel_id=1, source_target_pairs={{0,2},{2,4},{4,6},{6,7},{7,5},{5,3},{3,1},{1,0},{8,10},{10,12},{12... | collective-permute-start | bytes 1572872 | tf_op jit(solution)/shard_map/ppermute | solution.py:44
  84.0 2.1 %collective-permute-done.11.refs_11_ = bf16[256,1024]{1,0:T(8,128)(2,1)S(1)} collective-permute-done((bf16[256,1024]{1,0:T(8,128)(2,1)S(1)}, bf16[256,1024]{1,0:T(8,128)(2,1)S(1)}, u32[]{:S(2)}, u32[]{:S(2)}) %collective-permute-start.11) | collective-permute-done | bytes 524320 | tf_op jit(solution)/shard_map/ppermute | solution.py:44
  86.0 1.9 %fusion.22 = (bf16[256,1024]{1,0:T(8,128)(2,1)S(1)}, bf16[256,1024]{1,0:T(8,128)(2,1)S(1)}) fusion(bf16[256,1024]{1,0:T(8,128)(2,1)S(1)} %collective-permute-done.12.refs_13_, f32[6,512,1024]{2,1,0:T(8,128)} %get-tuple-element.138, pred[]{:T(512)} %eq.27, pred[]{:T(512)} %eq.28, bf16[256,1024]{1,0:T(8,128)(2,1)S(1)} %collective-permute-done.11.refs_11_), kind=kLoop, calls=%fused_computation.45 | loop fusion | flops 2621440 | bytes 4194306 | tf_op jit(solution)/shard_map/jit(_where)/select_n | solution.py:556
  88.0 1.5 collective-permute-start.17
  90.1 4.2 %fusion.1 = (bf16[384,1024]{1,0:T(8,128)(2,1)}, f32[384,1024]{1,0:T(8,128)}, f32[384,1024]{1,0:T(8,128)}) fusion(bf16[1,384,1024]{2,1,0:T(8,128)(2,1)S(1)} %copy-done.24, f32[384,1024]{1,0:T(8,128)S(1)} %copy-done.22, f32[384,1024]{1,0:T(8,128)S(1)} %copy-done.23, bf16[384,1024]{1,0:T(8,128)(2,1)} %collective-permute-done.9, bf16[384,1024]{1,0:T(8,128)(2,1)S(1)} %copy-done.21), kind=kLoop, calls=%fused_computation.3 | loop fusion | flops 5505024 | bytes 9437184 | tf_op jit(solution)/shard_map/convert_element_type | solution.py:632
  94.3 2.5 %collective-permute-done.15.refs_17_ = bf16[256,1024]{1,0:T(8,128)(2,1)S(1)} collective-permute-done((bf16[256,1024]{1,0:T(8,128)(2,1)S(1)}, bf16[256,1024]{1,0:T(8,128)(2,1)S(1)}, u32[]{:S(2)}, u32[]{:S(2)}) %collective-permute-start.15) | collective-permute-done | bytes 524320 | tf_op jit(solution)/shard_map/ppermute | solution.py:47
  97.3 1.9 %fusion.12 = (bf16[256,1024]{1,0:T(8,128)(2,1)S(1)}, bf16[256,1024]{1,0:T(8,128)(2,1)S(1)}) fusion(bf16[256,1024]{1,0:T(8,128)(2,1)S(1)} %collective-permute-done.15.refs_17_, f32[6,512,1024]{2,1,0:T(8,128)} %get-tuple-element.138, pred[]{:T(512)} %eq.30, bf16[256,1024]{1,0:T(8,128)(2,1)S(1)} %collective-permute-done.14.refs_15_, pred[]{:T(512)} %eq.29), kind=kLoop, calls=%fused_computation.27 | loop fusion | flops 2097152 | bytes 4194306 | tf_op jit(solution)/shard_map/convert_element_type | solution.py:563
  99.2 1.7 %collective-permute-start.22 = (bf16[256,1024]{1,0:T(8,128)(2,1)S(1)}, bf16[256,1024]{1,0:T(8,128)(2,1)S(1)}, u32[]{:S(2)}, u32[]{:S(2)}) collective-permute-start(bf16[256,1024]{1,0:T(8,128)(2,1)S(1)} %get-tuple-element.199), channel_id=1, source_target_pairs={{2,0},{4,2},{6,4},{7,6},{5,7},{3,5},{1,3},{0,1},{10,8},{12,10},{14... | collective-permute-start | bytes 1572872 | tf_op jit(solution)/shard_map/ppermute | solution.py:47
  101.5 6.6 %collective-permute-done.17.refs_18_ = bf16[256,1024]{1,0:T(8,128)(2,1)S(1)} collective-permute-done((bf16[256,1024]{1,0:T(8,128)(2,1)S(1)}, bf16[256,1024]{1,0:T(8,128)(2,1)S(1)}, u32[]{:S(2)}, u32[]{:S(2)}) %collective-permute-start.17) | collective-permute-done | bytes 524320 | tf_op jit(solution)/shard_map/ppermute | solution.py:47
  108.5 2.1 %fusion.11 = (bf16[256,1024]{1,0:T(8,128)(2,1)S(1)}, bf16[256,1024]{1,0:T(8,128)(2,1)S(1)}) fusion(bf16[256,1024]{1,0:T(8,128)(2,1)S(1)} %collective-permute-done.17.refs_18_, f32[6,512,1024]{2,1,0:T(8,128)} %get-tuple-element.138, pred[]{:T(512)} %eq.30, bf16[256,1024]{1,0:T(8,128)(2,1)S(1)} %collective-permute-done.16.refs_16_, pred[]{:T(512)} %eq.29), kind=kLoop, calls=%fused_computation.25 | loop fusion | flops 2097152 | bytes 4194306 | tf_op jit(solution)/shard_map/convert_element_type | solution.py:563
  110.7 1.5 collective-permute-start.20
  112.9 6.3 %collective-permute-done.22 = bf16[256,1024]{1,0:T(8,128)(2,1)S(1)} collective-permute-done((bf16[256,1024]{1,0:T(8,128)(2,1)S(1)}, bf16[256,1024]{1,0:T(8,128)(2,1)S(1)}, u32[]{:S(2)}, u32[]{:S(2)}) %collective-permute-start.22) | collective-permute-done | bytes 524320 | tf_op jit(solution)/shard_map/ppermute | solution.py:47
  120.2 1.5 collective-permute-start.27
  122.3 4.5 %collective-permute-start.25 = (bf16[512,1024]{1,0:T(8,128)(2,1)S(1)}, bf16[512,1024]{1,0:T(8,128)(2,1)S(1)}, u32[]{:S(2)}, u32[]{:S(2)}) collective-permute-start(bf16[512,1024]{1,0:T(8,128)(2,1)S(1)} %fusion.10), channel_id=1, source_target_pairs={{2,3},{3,2},{4,5},{5,4},{10,11},{11,10},{12,13},{13,12},{18,19},{1... | collective-permute-start | bytes 3145736 | tf_op jit(solution)/shard_map/ppermute | solution.py:56
  126.8 3.7 %collective-permute-done.20 = bf16[256,1024]{1,0:T(8,128)(2,1)S(1)} collective-permute-done((bf16[256,1024]{1,0:T(8,128)(2,1)S(1)}, bf16[256,1024]{1,0:T(8,128)(2,1)S(1)}, u32[]{:S(2)}, u32[]{:S(2)}) %collective-permute-start.20) | collective-permute-done | bytes 524320 | tf_op jit(solution)/shard_map/ppermute | solution.py:47
  131.5 1.5 collective-permute-start.24
  133.5 16.3 %project_last.1 = (bf16[512,1024]{1,0:T(8,128)(2,1)}, bf16[512,4096]{1,0:T(8,128)(2,1)}) custom-call(s32[15]{0:T(128)S(1)} %pad_add_fusion.at, bf16[512,4096]{1,0:T(8,128)(2,1)} %bitcast.78, bf16[512,1024]{1,0:T(8,128)(2,1)} %copy-done.11, f32[512,128]{1,0:T(8,128)S(1)} %copy-done.17, f32[512,128]{1,0:T(8,128)S(1)} %get-tuple-element.213.cosine, ...), custom_call_target="tpu_custom_call" | custom-call | flops 8589934592 | bytes 16777216 | tf_op jit(solution)/shard_map/project_last/pallas_call | solution.py:427
  149.9 1.2 collective-permute-done.23.refs_0_
  151.1 1.4 sum_of_terms.2
  152.5 1.3 sum_of_terms.3
  (106 shorter events, 12.2 us)
Async XLA Ops:
  3.3 63.0 %copy-start.8 = (bf16[512,1024]{1,0:T(8,128)(2,1)}, bf16[512,1024]{1,0:T(8,128)(2,1)S(1)}, u32[]{:S(2)}) copy-start(bf16[512,1024]{1,0:T(8,128)(2,1)S(1)} %scale_rows.1.refs_0_.refs_2_) | copy-start | bytes 3145732
  3.3 25.7 %collective-permute-start.2 = (f32[384,1024]{1,0:T(8,128)}, f32[384,1024]{1,0:T(8,128)}, u32[]{:S(2)}, u32[]{:S(2)}) collective-permute-start(f32[384,1024]{1,0:T(8,128)} %bitcast.10), channel_id=1, source_target_pairs={{0,8},{8,0},{16,24},{24,16},{1,9},{9,1},{17,25},{25,17},{2,10},{10... | collective-permute-start | bytes 4718600 | tf_op jit(solution)/shard_map/ppermute | solution.py:456
  3.4 25.6 %collective-permute-start.1 = (bf16[512,1024]{1,0:T(8,128)(2,1)S(1)}, bf16[512,1024]{1,0:T(8,128)(2,1)S(1)}, u32[]{:S(2)}, u32[]{:S(2)}) collective-permute-start(bf16[512,1024]{1,0:T(8,128)(2,1)S(1)} %scale_rows.1.refs_0_.refs_2_), channel_id=1, source_target_pairs={{2,0},{4,2},{6,4},{7,6},{5,7},{3,5},{1,3},{0,1},{10,8},{12,10},{14... | collective-permute-start | bytes 3145736 | tf_op jit(solution)/shard_map/ppermute | solution.py:47
  3.5 25.5 %collective-permute-start = (bf16[512,1024]{1,0:T(8,128)(2,1)S(1)}, bf16[512,1024]{1,0:T(8,128)(2,1)S(1)}, u32[]{:S(2)}, u32[]{:S(2)}) collective-permute-start(bf16[512,1024]{1,0:T(8,128)(2,1)S(1)} %scale_rows.1.refs_0_.refs_2_), channel_id=1, source_target_pairs={{0,2},{2,4},{4,6},{6,7},{7,5},{5,3},{3,1},{1,0},{8,10},{10,12},{12... | collective-permute-start | bytes 3145736 | tf_op jit(solution)/shard_map/ppermute | solution.py:44
  5.5 36.5 %collective-permute-start.10 = (bf16[512,1024]{1,0:T(8,128)(2,1)S(1)}, bf16[512,1024]{1,0:T(8,128)(2,1)}, u32[]{:S(2)}, u32[]{:S(2)}) collective-permute-start(bf16[512,1024]{1,0:T(8,128)(2,1)S(1)} %scale_rows.1.refs_0_.refs_2_), channel_id=1, source_target_pairs={{2,3},{3,2},{4,5},{5,4},{10,11},{11,10},{12,13},{13,12},{18,19},{1... | collective-permute-start | bytes 3145736 | tf_op jit(solution)/shard_map/ppermute | solution.py:56
  10.2 14.4 %copy-start.13 = (f32[512,128]{1,0:T(8,128)}, f32[512,128]{1,0:T(8,128)S(1)}, u32[]{:S(2)}) copy-start(f32[512,128]{1,0:T(8,128)S(1)} %get-tuple-element.214.sine) | copy-start | bytes 786436
  25.6 7.2 %copy-start.15 = (f32[512,128]{1,0:T(8,128)}, f32[512,128]{1,0:T(8,128)S(1)}, u32[]{:S(2)}) copy-start(f32[512,128]{1,0:T(8,128)S(1)} %get-tuple-element.100.inv) | copy-start | bytes 786436
  29.0 37.3 %copy-start.2 = (bf16[512,1024]{1,0:T(8,128)(2,1)}, bf16[512,1024]{1,0:T(8,128)(2,1)S(1)}, u32[]{:S(2)}) copy-start(bf16[512,1024]{1,0:T(8,128)(2,1)S(1)} %collective-permute-done.1.refs_2_.refs_4_) | copy-start | bytes 3145732
  29.0 37.3 %copy-start.3 = (bf16[512,1024]{1,0:T(8,128)(2,1)}, bf16[512,1024]{1,0:T(8,128)(2,1)S(1)}, u32[]{:S(2)}) copy-start(bf16[512,1024]{1,0:T(8,128)(2,1)S(1)} %collective-permute-done.refs_1_.refs_3_) | copy-start | bytes 3145732
  33.6 15.1 %collective-permute-start.4 = (bf16[256,1024]{1,0:T(8,128)(2,1)}, bf16[256,1024]{1,0:T(8,128)(2,1)}, u32[]{:S(2)}, u32[]{:S(2)}) collective-permute-start(bf16[256,1024]{1,0:T(8,128)(2,1)} %slice.128), channel_id=1, source_target_pairs={{2,0},{4,2},{6,4},{7,6},{5,7},{3,5},{1,3},{0,1},{10,8},{12,10},{14... | collective-permute-start | bytes 1572872 | tf_op jit(solution)/shard_map/ppermute | solution.py:47
  34.8 27.5 %collective-permute-start.9 = (bf16[384,1024]{1,0:T(8,128)(2,1)}, bf16[384,1024]{1,0:T(8,128)(2,1)}, u32[]{:S(2)}, u32[]{:S(2)}) collective-permute-start(bf16[384,1024]{1,0:T(8,128)(2,1)} %add_convert_fusion), channel_id=1, source_target_pairs={{0,16},{8,24},{16,0},{24,8},{1,17},{9,25},{17,1},{25,9},{2,18},{10... | collective-permute-start | bytes 2359304 | tf_op jit(solution)/shard_map/ppermute | solution.py:456
  37.2 16.1 %collective-permute-start.3 = (bf16[256,1024]{1,0:T(8,128)(2,1)}, bf16[256,1024]{1,0:T(8,128)(2,1)}, u32[]{:S(2)}, u32[]{:S(2)}) collective-permute-start(bf16[256,1024]{1,0:T(8,128)(2,1)} %slice.127), channel_id=1, source_target_pairs={{0,2},{2,4},{4,6},{6,7},{7,5},{5,3},{3,1},{1,0},{8,10},{10,12},{12... | collective-permute-start | bytes 1572872 | tf_op jit(solution)/shard_map/ppermute | solution.py:44
  39.6 13.4 %copy-start.28 = (s32[8]{0:T(128)S(1)}, s32[8]{0:T(128)}, u32[]{:S(2)}) copy-start(s32[8]{0:T(128)} %constant.107.clone) | copy-start | bytes 100
  39.6 20.3 %collective-permute-start.8 = (bf16[256,1024]{1,0:T(8,128)(2,1)}, bf16[256,1024]{1,0:T(8,128)(2,1)}, u32[]{:S(2)}, u32[]{:S(2)}) collective-permute-start(bf16[256,1024]{1,0:T(8,128)(2,1)} %slice.130), channel_id=1, source_target_pairs={{2,0},{4,2},{6,4},{7,6},{5,7},{3,5},{1,3},{0,1},{10,8},{12,10},{14... | collective-permute-start | bytes 1572872 | tf_op jit(solution)/shard_map/ppermute | solution.py:47
  42.0 20.4 %collective-permute-start.7 = (bf16[256,1024]{1,0:T(8,128)(2,1)}, bf16[256,1024]{1,0:T(8,128)(2,1)}, u32[]{:S(2)}, u32[]{:S(2)}) collective-permute-start(bf16[256,1024]{1,0:T(8,128)(2,1)} %slice.129), channel_id=1, source_target_pairs={{0,2},{2,4},{4,6},{6,7},{7,5},{5,3},{3,1},{1,0},{8,10},{10,12},{12... | collective-permute-start | bytes 1572872 | tf_op jit(solution)/shard_map/ppermute | solution.py:44
  48.7 26.1 %collective-permute-start.13 = (bf16[512,1024]{1,0:T(8,128)(2,1)}, bf16[512,1024]{1,0:T(8,128)(2,1)}, u32[]{:S(2)}, u32[]{:S(2)}) collective-permute-start(bf16[512,1024]{1,0:T(8,128)(2,1)} %broadcast_select_fusion), channel_id=1, source_target_pairs={{2,3},{3,2},{4,5},{5,4},{10,11},{11,10},{12,13},{13,12},{18,19},{1... | collective-permute-start | bytes 3145736 | tf_op jit(solution)/shard_map/ppermute | solution.py:56
  53.2 9.1 %copy-start.10 = (bf16[512,1024]{1,0:T(8,128)(2,1)S(1)}, bf16[512,1024]{1,0:T(8,128)(2,1)}, u32[]{:S(2)}) copy-start(bf16[512,1024]{1,0:T(8,128)(2,1)} %copy-done.9) | copy-start | bytes 3145732
  53.3 13.0 %copy-start.7 = (bf16[1,512,4096]{2,1,0:T(8,128)(2,1)S(1)}, bf16[1,512,4096]{2,1,0:T(8,128)(2,1)}, u32[]{:S(2)}) copy-start(bf16[1,512,4096]{2,1,0:T(8,128)(2,1)} %param.10) | copy-start | bytes 12582916
  54.9 19.6 %collective-permute-start.6 = (bf16[256,1024]{1,0:T(8,128)(2,1)S(1)}, bf16[256,1024]{1,0:T(8,128)(2,1)S(1)}, u32[]{:S(2)}, u32[]{:S(2)}) collective-permute-start(bf16[256,1024]{1,0:T(8,128)(2,1)S(1)} %get-tuple-element.208), channel_id=1, source_target_pairs={{2,0},{4,2},{6,4},{7,6},{5,7},{3,5},{1,3},{0,1},{10,8},{12,10},{14... | collective-permute-start | bytes 1572872 | tf_op jit(solution)/shard_map/ppermute | solution.py:47
  59.9 14.9 %collective-permute-start.5 = (bf16[256,1024]{1,0:T(8,128)(2,1)S(1)}, bf16[256,1024]{1,0:T(8,128)(2,1)S(1)}, u32[]{:S(2)}, u32[]{:S(2)}) collective-permute-start(bf16[256,1024]{1,0:T(8,128)(2,1)S(1)} %get-tuple-element.209), channel_id=1, source_target_pairs={{0,2},{2,4},{4,6},{6,7},{7,5},{5,3},{3,1},{1,0},{8,10},{10,12},{12... | collective-permute-start | bytes 1572872 | tf_op jit(solution)/shard_map/ppermute | solution.py:44
  63.6 20.3 %collective-permute-start.12 = (bf16[256,1024]{1,0:T(8,128)(2,1)S(1)}, bf16[256,1024]{1,0:T(8,128)(2,1)S(1)}, u32[]{:S(2)}, u32[]{:S(2)}) collective-permute-start(bf16[256,1024]{1,0:T(8,128)(2,1)S(1)} %get-tuple-element.206), channel_id=1, source_target_pairs={{2,0},{4,2},{6,4},{7,6},{5,7},{3,5},{1,3},{0,1},{10,8},{12,10},{14... | collective-permute-start | bytes 1572872 | tf_op jit(solution)/shard_map/ppermute | solution.py:47
  66.3 19.7 %collective-permute-start.11 = (bf16[256,1024]{1,0:T(8,128)(2,1)S(1)}, bf16[256,1024]{1,0:T(8,128)(2,1)S(1)}, u32[]{:S(2)}, u32[]{:S(2)}) collective-permute-start(bf16[256,1024]{1,0:T(8,128)(2,1)S(1)} %get-tuple-element.207), channel_id=1, source_target_pairs={{0,2},{2,4},{4,6},{6,7},{7,5},{5,3},{3,1},{1,0},{8,10},{10,12},{12... | collective-permute-start | bytes 1572872 | tf_op jit(solution)/shard_map/ppermute | solution.py:44
  68.5 21.6 %copy-start.24 = (bf16[1,384,1024]{2,1,0:T(8,128)(2,1)S(1)}, bf16[1,384,1024]{2,1,0:T(8,128)(2,1)}, u32[]{:S(2)}) copy-start(bf16[1,384,1024]{2,1,0:T(8,128)(2,1)} %param.17) | copy-start | bytes 2359300
  74.8 33.7 %collective-permute-start.18 = (bf16[512,1024]{1,0:T(8,128)(2,1)S(1)}, bf16[512,1024]{1,0:T(8,128)(2,1)S(1)}, u32[]{:S(2)}, u32[]{:S(2)}) collective-permute-start(bf16[512,1024]{1,0:T(8,128)(2,1)S(1)} %copy-done.10), channel_id=1, source_target_pairs={{2,3},{3,2},{4,5},{5,4},{10,11},{11,10},{12,13},{13,12},{18,19},{1... | collective-permute-start | bytes 3145736 | tf_op jit(solution)/shard_map/ppermute | solution.py:56
  79.8 33.0 %slice-start = ((s8[12582912]{0:T(1024)(128)(4,1)}), s8[4194304]{0:T(1024)(128)(4,1)S(1)}, s32[]{:S(2)}) async-start(s8[12582912]{0:T(1024)(128)(4,1)} %bitcast.82), calls=%async_computation | async-start | bytes 8388608
  81.9 14.9 %collective-permute-start.15 = (bf16[256,1024]{1,0:T(8,128)(2,1)S(1)}, bf16[256,1024]{1,0:T(8,128)(2,1)S(1)}, u32[]{:S(2)}, u32[]{:S(2)}) collective-permute-start(bf16[256,1024]{1,0:T(8,128)(2,1)S(1)} %get-tuple-element.203), channel_id=1, source_target_pairs={{2,0},{4,2},{6,4},{7,6},{5,7},{3,5},{1,3},{0,1},{10,8},{12,10},{14... | collective-permute-start | bytes 1572872 | tf_op jit(solution)/shard_map/ppermute | solution.py:47
  81.9 8.1 %copy-start.21 = (bf16[384,1024]{1,0:T(8,128)(2,1)S(1)}, bf16[384,1024]{1,0:T(8,128)(2,1)}, u32[]{:S(2)}) copy-start(bf16[384,1024]{1,0:T(8,128)(2,1)} %add_convert_fusion) | copy-start | bytes 2359300
  82.0 8.1 %copy-start.22 = (f32[384,1024]{1,0:T(8,128)S(1)}, f32[384,1024]{1,0:T(8,128)}, u32[]{:S(2)}) copy-start(f32[384,1024]{1,0:T(8,128)} %param.16) | copy-start | bytes 4718596
  82.0 8.1 %copy-start.23 = (f32[384,1024]{1,0:T(8,128)S(1)}, f32[384,1024]{1,0:T(8,128)}, u32[]{:S(2)}) copy-start(f32[384,1024]{1,0:T(8,128)} %param.15) | copy-start | bytes 4718596
  82.0 15.3 %collective-permute-start.14 = (bf16[256,1024]{1,0:T(8,128)(2,1)S(1)}, bf16[256,1024]{1,0:T(8,128)(2,1)S(1)}, u32[]{:S(2)}, u32[]{:S(2)}) collective-permute-start(bf16[256,1024]{1,0:T(8,128)(2,1)S(1)} %get-tuple-element.204), channel_id=1, source_target_pairs={{0,2},{2,4},{4,6},{6,7},{7,5},{5,3},{3,1},{1,0},{8,10},{10,12},{12... | collective-permute-start | bytes 1572872 | tf_op jit(solution)/shard_map/ppermute | solution.py:44
  88.0 20.0 %collective-permute-start.17 = (bf16[256,1024]{1,0:T(8,128)(2,1)S(1)}, bf16[256,1024]{1,0:T(8,128)(2,1)S(1)}, u32[]{:S(2)}, u32[]{:S(2)}) collective-permute-start(bf16[256,1024]{1,0:T(8,128)(2,1)S(1)} %get-tuple-element.201), channel_id=1, source_target_pairs={{2,0},{4,2},{6,4},{7,6},{5,7},{3,5},{1,3},{0,1},{10,8},{12,10},{14... | collective-permute-start | bytes 1572872 | tf_op jit(solution)/shard_map/ppermute | solution.py:47
  89.5 23.3 %slice-start.1 = ((s8[12582912]{0:T(1024)(128)(4,1)}), s8[4194304]{0:T(1024)(128)(4,1)S(1)}, s32[]{:S(2)}) async-start(s8[12582912]{0:T(1024)(128)(4,1)} %bitcast.82), calls=%async_computation.1 | async-start | bytes 8388608
  89.5 23.3 %slice-start.2 = ((s8[12582912]{0:T(1024)(128)(4,1)}), s8[4194304]{0:T(1024)(128)(4,1)S(1)}, s32[]{:S(2)}) async-start(s8[12582912]{0:T(1024)(128)(4,1)} %bitcast.82), calls=%async_computation.2 | async-start | bytes 8388608
  89.5 19.0 %collective-permute-start.16 = (bf16[256,1024]{1,0:T(8,128)(2,1)S(1)}, bf16[256,1024]{1,0:T(8,128)(2,1)S(1)}, u32[]{:S(2)}, u32[]{:S(2)}) collective-permute-start(bf16[256,1024]{1,0:T(8,128)(2,1)S(1)} %get-tuple-element.202), channel_id=1, source_target_pairs={{0,2},{2,4},{4,6},{6,7},{7,5},{5,3},{3,1},{1,0},{8,10},{10,12},{12... | collective-permute-start | bytes 1572872 | tf_op jit(solution)/shard_map/ppermute | solution.py:44
  99.2 20.1 %collective-permute-start.22 = (bf16[256,1024]{1,0:T(8,128)(2,1)S(1)}, bf16[256,1024]{1,0:T(8,128)(2,1)S(1)}, u32[]{:S(2)}, u32[]{:S(2)}) collective-permute-start(bf16[256,1024]{1,0:T(8,128)(2,1)S(1)} %get-tuple-element.199), channel_id=1, source_target_pairs={{2,0},{4,2},{6,4},{7,6},{5,7},{3,5},{1,3},{0,1},{10,8},{12,10},{14... | collective-permute-start | bytes 1572872 | tf_op jit(solution)/shard_map/ppermute | solution.py:47
  100.9 18.9 %collective-permute-start.21 = (bf16[256,1024]{1,0:T(8,128)(2,1)S(1)}, bf16[256,1024]{1,0:T(8,128)(2,1)S(1)}, u32[]{:S(2)}, u32[]{:S(2)}) collective-permute-start(bf16[256,1024]{1,0:T(8,128)(2,1)S(1)} %get-tuple-element.200), channel_id=1, source_target_pairs={{0,2},{2,4},{4,6},{6,7},{7,5},{5,3},{3,1},{1,0},{8,10},{10,12},{12... | collective-permute-start | bytes 1572872 | tf_op jit(solution)/shard_map/ppermute | solution.py:44
  110.7 19.8 %collective-permute-start.20 = (bf16[256,1024]{1,0:T(8,128)(2,1)S(1)}, bf16[256,1024]{1,0:T(8,128)(2,1)S(1)}, u32[]{:S(2)}, u32[]{:S(2)}) collective-permute-start(bf16[256,1024]{1,0:T(8,128)(2,1)S(1)} %get-tuple-element.197), channel_id=1, source_target_pairs={{2,0},{4,2},{6,4},{7,6},{5,7},{3,5},{1,3},{0,1},{10,8},{12,10},{14... | collective-permute-start | bytes 1572872 | tf_op jit(solution)/shard_map/ppermute | solution.py:47
  112.1 18.8 %collective-permute-start.19 = (bf16[256,1024]{1,0:T(8,128)(2,1)S(1)}, bf16[256,1024]{1,0:T(8,128)(2,1)S(1)}, u32[]{:S(2)}, u32[]{:S(2)}) collective-permute-start(bf16[256,1024]{1,0:T(8,128)(2,1)S(1)} %get-tuple-element.198), channel_id=1, source_target_pairs={{0,2},{2,4},{4,6},{6,7},{7,5},{5,3},{3,1},{1,0},{8,10},{10,12},{12... | collective-permute-start | bytes 1572872 | tf_op jit(solution)/shard_map/ppermute | solution.py:44
  120.2 29.7 %collective-permute-start.27 = (bf16[256,1024]{1,0:T(8,128)(2,1)S(1)}, bf16[256,1024]{1,0:T(8,128)(2,1)S(1)}, u32[]{:S(2)}, u32[]{:S(2)}) collective-permute-start(bf16[256,1024]{1,0:T(8,128)(2,1)S(1)} %get-tuple-element.195), channel_id=1, source_target_pairs={{2,0},{4,2},{6,4},{7,6},{5,7},{3,5},{1,3},{0,1},{10,8},{12,10},{14... | collective-permute-start | bytes 1572872 | tf_op jit(solution)/shard_map/ppermute | solution.py:47
  121.7 11.8 %copy-start.14 = (f32[512,128]{1,0:T(8,128)S(1)}, f32[512,128]{1,0:T(8,128)}, u32[]{:S(2)}) copy-start(f32[512,128]{1,0:T(8,128)} %copy-done.13) | copy-start | bytes 786436
  121.7 11.8 %copy-start.17 = (f32[512,128]{1,0:T(8,128)S(1)}, f32[512,128]{1,0:T(8,128)}, u32[]{:S(2)}) copy-start(f32[512,128]{1,0:T(8,128)} %copy-done.15) | copy-start | bytes 786436
  121.7 28.2 %collective-permute-start.26 = (bf16[256,1024]{1,0:T(8,128)(2,1)S(1)}, bf16[256,1024]{1,0:T(8,128)(2,1)S(1)}, u32[]{:S(2)}, u32[]{:S(2)}) collective-permute-start(bf16[256,1024]{1,0:T(8,128)(2,1)S(1)} %get-tuple-element.196), channel_id=1, source_target_pairs={{0,2},{2,4},{4,6},{6,7},{7,5},{5,3},{3,1},{1,0},{8,10},{10,12},{12... | collective-permute-start | bytes 1572872 | tf_op jit(solution)/shard_map/ppermute | solution.py:44
  122.3 28.8 %collective-permute-start.25 = (bf16[512,1024]{1,0:T(8,128)(2,1)S(1)}, bf16[512,1024]{1,0:T(8,128)(2,1)S(1)}, u32[]{:S(2)}, u32[]{:S(2)}) collective-permute-start(bf16[512,1024]{1,0:T(8,128)(2,1)S(1)} %fusion.10), channel_id=1, source_target_pairs={{2,3},{3,2},{4,5},{5,4},{10,11},{11,10},{12,13},{13,12},{18,19},{1... | collective-permute-start | bytes 3145736 | tf_op jit(solution)/shard_map/ppermute | solution.py:56
  131.5 18.5 %collective-permute-start.24 = (bf16[256,1024]{1,0:T(8,128)(2,1)S(1)}, bf16[256,1024]{1,0:T(8,128)(2,1)S(1)}, u32[]{:S(2)}, u32[]{:S(2)}) collective-permute-start(bf16[256,1024]{1,0:T(8,128)(2,1)S(1)} %get-tuple-element.193), channel_id=1, source_target_pairs={{2,0},{4,2},{6,4},{7,6},{5,7},{3,5},{1,3},{0,1},{10,8},{12,10},{14... | collective-permute-start | bytes 1572872 | tf_op jit(solution)/shard_map/ppermute | solution.py:47
  132.9 18.2 %copy-start.1 = (bf16[1,512,1024]{2,1,0:T(8,128)(2,1)S(1)}, bf16[1,512,1024]{2,1,0:T(8,128)(2,1)}, u32[]{:S(2)}) copy-start(bf16[1,512,1024]{2,1,0:T(8,128)(2,1)} %param.12) | copy-start | bytes 3145732
  132.9 18.2 %copy-start.5 = (f32[512,1024]{1,0:T(8,128)S(1)}, f32[512,1024]{1,0:T(8,128)}, u32[]{:S(2)}) copy-start(f32[512,1024]{1,0:T(8,128)} %copy-done.4) | copy-start | bytes 6291460
  132.9 18.2 %copy-start.19 = (bf16[1,512]{1,0:T(2,128)(2,1)S(1)}, bf16[1,512]{1,0:T(2,128)(2,1)}, u32[]{:S(2)}) copy-start(bf16[1,512]{1,0:T(2,128)(2,1)} %gain.5) | copy-start | bytes 3076
  132.9 18.2 %collective-permute-start.23 = (bf16[256,1024]{1,0:T(8,128)(2,1)S(1)}, bf16[256,1024]{1,0:T(8,128)(2,1)S(1)}, u32[]{:S(2)}, u32[]{:S(2)}) collective-permute-start(bf16[256,1024]{1,0:T(8,128)(2,1)S(1)} %get-tuple-element.194), channel_id=1, source_target_pairs={{0,2},{2,4},{4,6},{6,7},{7,5},{5,3},{3,1},{1,0},{8,10},{10,12},{12... | collective-permute-start | bytes 1572872 | tf_op jit(solution)/shard_map/ppermute | solution.py:44
  (13 other events, 36.9 us)

commit v13 on v12

--- a/solution.py
+++ b/solution.py
@@ -452,12 +452,20 @@
     )(at, tokens_in, kv_grad, inv, cosine, sine, *carry, *blocks)
 
 
+def replica_pairs(value):
+    if lax.axis_size("replica") != 4:
+        return lax.psum(value, "replica"), False
+    value = value.astype(bf16)
+    return (value.astype(f32) + replica_swap(value, 1).astype(f32)).astype(bf16), True
+
+
 def replica_swap(value, step):
     return lax.ppermute(value, "replica", [(r, r ^ step) for r in range(4)])
 
 
 def exchange_ring(ring, own, far, near, pseudo, early, late, update):
-    total = lax.psum(pseudo, "replica")
+    pairs, halved = pseudo
+    total = (pairs, replica_swap(pairs, 2) if halved else jnp.zeros((), f32))
     shard, cut = own.shape[0], own.shape[0] // 2
     blocks = [own]
     from_left = from_right = own
@@ -483,7 +491,7 @@
     return late(blocks, plan), sums, update(total)
 
 
-ORDER = {"sum": (-1, 3), "pair": (-1, 3), "inner": (2, 7), "far": (1, 5), "partner": (7, None), "first": (2, 4), "update": (4, 7)}
+ORDER = {"sum": (-1, 3), "pair": (-1, 4), "inner": (4, None), "far": (1, 5), "partner": (7, None), "first": (6, 7), "update": (4, 7)}
 CHAIN = True
 
 
@@ -532,13 +540,9 @@
 
     first = ring(None, own, own)
     beside["pair"] = chord(own)
-    if lax.axis_size("replica") == 4:
-        pairs = after(pseudo, own)
-        pairs = (pairs + replica_swap(pairs, 1)).astype(bf16)
-        came = replica_swap(pairs, 2)
-    else:
-        pairs, came = lax.psum(pseudo, "replica"), jnp.zeros((), f32)
-    first, far, pairs = lax.optimization_barrier((first, far, pairs))
+    pairs, first_swap = pseudo
+    came = replica_swap(pairs, 2) if first_swap else jnp.zeros((), f32)
+    first, far = lax.optimization_barrier((first, far))
     beside["sum"] = came
     two = [ring(0, *(part(side, 0) for side in first))]
     two.append(ring(1, *(part(side, 1) for side in later(1, *first))))
@@ -601,8 +605,9 @@
     positions = (ring.me * rows + jnp.arange(rows, dtype=jnp.int32)) % SEQ_LEN
     cosine, sine = rope_tables(positions)
     scale = 1.0 / math.sqrt(rows * ring.count)
+    pairs, halved = replica_pairs(after(pseudo_grad[0], own))
     kv_grad, inv, far, near, last = first_part(
-        ring, tokens_in, cotangent, cosine, sine, shard, scale
+        ring, tokens_in, after(cotangent, pairs), cosine, sine, shard, scale
     )
     order = [0]
     for d in range(1, ring.half):
@@ -634,7 +639,7 @@
 
     exchange = exchange_plane if small else exchange_ring
     (kv_out, input_grad), sums, updated = exchange(
-        ring, own, far, near, pseudo_grad[0], early, late, update
+        ring, own, far, near, (pairs, halved), early, late, update
     )
     momentum_new, global_new, local_new = updated
     weight_grad, gain_grad = last_part(last, weight_shard, norm_gain, sums)

time: 157 us -> 155 us (0.987); the launches traced: 154 us -> 154 us
  other arithmetic: 22.4 us -> 30.1 us
  starting transfers between devices: 42.2 us -> 34.5 us
  local copies, waits for them, and re-layouts: 10.9 us -> 8.67 us
  waiting for transfers between devices: 39.3 us -> 41.5 us
    ppermute x11, waiting for transfers between devices: 6.26 us -> 23.2 us  [to_right(): return lax.ppermute(value, 'fsdp', self.right)]
    ppermute x11, waiting for transfers between devices: 33.1 us -> 18.3 us  [to_left(): return lax.ppermute(value, 'fsdp', self.left)]
    ppermute x11, starting transfers between devices: 13.5 us -> 5.94 us  [to_left(): return lax.ppermute(value, 'fsdp', self.left)]
    ppermute x4, starting transfers between devices: 17.1 us -> 10.7 us  [over_chord(): return lax.ppermute(value, 'fsdp', [(2, 3), (3, 2), (4, 5), (5, 4)])]
    ppermute x11, starting transfers between devices: 10 us -> 16.3 us  [to_right(): return lax.ppermute(value, 'fsdp', self.right)]
    convert_element_type x2, other arithmetic: 0.94 us -> 4.04 us  [exchange_plane(): six.append(ring(8 + h, to_right.astype(bf16), to_left.astype(bf16)))]
    convert_element_type x1, other arithmetic: 0.18 us -> 2.41 us  [exchange_plane(): pick(at1, near[1], near[0]).astype(bf16)]
    unnamed x66 -> x68, local copies, waits for them, and re-layouts: 7.44 us -> 6.74 us
  transfers between devices with their start and end apart: 28 -> 28, of which waited for: 15 -> 12; matrix products, arithmetic and copies ran while one was open for 17% -> 21% of each run, Pallas kernels for 22% -> 22%
where the time goes in v13:
time: 155 us; the launch traced here: 154 us
  waiting for transfers between devices  41.5 us (27%)
  Pallas kernels  37.7 us (24%)
  starting transfers between devices  34.5 us (22%)
  other arithmetic  30.1 us (19%)
  local copies, waits for them, and re-layouts  8.67 us (6%)
    ppermute x11, waiting for transfers between devices, to_right(): return lax.ppermute(value, 'fsdp', self.right)  23.2 us
    ppermute x11, waiting for transfers between devices, to_left(): return lax.ppermute(value, 'fsdp', self.left)  18.3 us
    ppermute x11, starting transfers between devices, to_right(): return lax.ppermute(value, 'fsdp', self.right)  16.3 us
    pallas_call x1, Pallas kernels, late_part(): pl.pallas_call(functools.partial(late_kernel, plan, done), in_specs=[pl.B...  16.1 us
    pallas_call x1, Pallas kernels, first_part(): pl.pallas_call(functools.partial(first_kernel, scale), grid_spec=pltpu.Pr...  12.1 us
    ppermute x4, starting transfers between devices, over_chord(): return lax.ppermute(value, 'fsdp', [(2, 3), (3, 2), (4, 5), (5, 4)])  10.7 us
    unnamed x68, local copies, waits for them, and re-layouts  6.74 us
    pallas_call x1, Pallas kernels, early_part(): pl.pallas_call(functools.partial(early_kernel, plan), in_specs=[pl.BlockS...  6.12 us
  transfers between devices with their start and end apart: 28, of which 12 were waited for; matrix products, arithmetic and copies ran while one was open for 21% of the time, Pallas kernels for 22%

profile of v13, /device:TPU:8, one launch (start us, length us, event | category | flops | bytes accessed | tf_op | source)
XLA Modules:
  0.0 153.5 jit_solution(13644019881565882568)
XLA Ops:
  0.6 1.2 copy-done
  3.3 1.6 %collective-permute-start.1 = (bf16[512,1024]{1,0:T(8,128)(2,1)S(1)}, bf16[512,1024]{1,0:T(8,128)(2,1)S(1)}, u32[]{:S(2)}, u32[]{:S(2)}) collective-permute-start(bf16[512,1024]{1,0:T(8,128)(2,1)S(1)} %scale_rows.1.refs_0_.refs_2_), channel_id=1, source_target_pairs={{0,2},{2,4},{4,6},{6,7},{7,5},{5,3},{3,1},{1,0},{8,10},{10,12},{12... | collective-permute-start | bytes 3145736 | tf_op jit(solution)/shard_map/ppermute | solution.py:44
  5.4 1.0 convert_element_type.122
  6.4 3.4 %collective-permute-start.12 = (bf16[512,1024]{1,0:T(8,128)(2,1)S(1)}, bf16[512,1024]{1,0:T(8,128)(2,1)}, u32[]{:S(2)}, u32[]{:S(2)}) collective-permute-start(bf16[512,1024]{1,0:T(8,128)(2,1)S(1)} %scale_rows.1.refs_0_.refs_2_), channel_id=1, source_target_pairs={{2,3},{3,2},{4,5},{5,4},{10,11},{11,10},{12,13},{13,12},{18,19},{1... | collective-permute-start | bytes 3145736 | tf_op jit(solution)/shard_map/ppermute | solution.py:56
  9.9 1.0 fusion.23
  11.1 3.0 %add_convert_fusion = bf16[384,1024]{1,0:T(8,128)(2,1)} fusion(bf16[384,1024]{1,0:T(8,128)(2,1)} %collective-permute-done, f32[384,1024]{1,0:T(8,128)} %bitcast.82), kind=kLoop, calls=%fused_computation.7 | loop fusion | flops 1966080 | bytes 3145728 | tf_op jit(solution)/shard_map/convert_element_type | solution.py:459
  14.1 12.1 %norm_and_weight_terms.1 = (bf16[512,1024]{1,0:T(8,128)(2,1)S(1)}, f32[512,128]{1,0:T(8,128)S(1)}, bf16[512,1024]{1,0:T(8,128)(2,1)S(1)}, f32[6,512,1024]{2,1,0:T(8,128)}, f32[512,1024]{1,0:T(8,128)S(1)}) custom-call(s32[8]{0:T(128)S(1)} %compare_select_fusion.4.at, bf16[512,4096]{1,0:T(8,128)(2,1)S(1)} %bitcast.79, bf16[512,1024]{1,0:T(8,128)(2,1)S(1)} %bitcast.81, ...), custom_call_target="tpu_custom_call" | custom-call | flops 4294967296 | bytes 20971520 | tf_op jit(solution)/shard_map/norm_and_weight_terms/pallas_call | solution.py:145
  26.2 1.3 copy-done.4
  31.1 1.6 %collective-permute-start.5 = (bf16[256,1024]{1,0:T(8,128)(2,1)}, bf16[256,1024]{1,0:T(8,128)(2,1)}, u32[]{:S(2)}, u32[]{:S(2)}) collective-permute-start(bf16[256,1024]{1,0:T(8,128)(2,1)} %slice.127), channel_id=1, source_target_pairs={{0,2},{2,4},{4,6},{6,7},{7,5},{5,3},{3,1},{1,0},{8,10},{10,12},{12... | collective-permute-start | bytes 1572872 | tf_op jit(solution)/shard_map/ppermute | solution.py:44
  33.9 1.5 collective-permute-start.7
  35.6 1.6 %collective-permute-start.3 = (bf16[256,1024]{1,0:T(8,128)(2,1)S(1)}, bf16[256,1024]{1,0:T(8,128)(2,1)S(1)}, u32[]{:S(2)}, u32[]{:S(2)}) collective-permute-start(bf16[256,1024]{1,0:T(8,128)(2,1)S(1)} %slice.129), channel_id=1, source_target_pairs={{0,2},{2,4},{4,6},{6,7},{7,5},{5,3},{3,1},{1,0},{8,10},{10,12},{12... | collective-permute-start | bytes 1572872 | tf_op jit(solution)/shard_map/ppermute | solution.py:44
  37.6 1.1 broadcast_select_fusion
  38.7 7.4 %collective-permute-done.5.refs_3_.refs_5_ = bf16[256,1024]{1,0:T(8,128)(2,1)} collective-permute-done((bf16[256,1024]{1,0:T(8,128)(2,1)}, bf16[256,1024]{1,0:T(8,128)(2,1)}, u32[]{:S(2)}, u32[]{:S(2)}) %collective-permute-start.5) | collective-permute-done | bytes 524320 | tf_op jit(solution)/shard_map/ppermute | solution.py:44
  46.2 2.4 %collective-permute-start.13 = (bf16[512,1024]{1,0:T(8,128)(2,1)}, bf16[512,1024]{1,0:T(8,128)(2,1)}, u32[]{:S(2)}, u32[]{:S(2)}) collective-permute-start(bf16[512,1024]{1,0:T(8,128)(2,1)} %broadcast_select_fusion), channel_id=1, source_target_pairs={{2,3},{3,2},{4,5},{5,4},{10,11},{11,10},{12,13},{13,12},{18,19},{1... | collective-permute-start | bytes 3145736 | tf_op jit(solution)/shard_map/ppermute | solution.py:56
  48.6 2.3 %broadcast_select_fusion.2 = (bf16[256,1024]{1,0:T(8,128)(2,1)}, bf16[256,1024]{1,0:T(8,128)(2,1)}) fusion(bf16[256,1024]{1,0:T(8,128)(2,1)} %collective-permute-done.6.refs_5_.refs_7_, pred[]{:T(512)} %eq.29, bf16[512,1024]{1,0:T(8,128)(2,1)S(1)} %copy-done.14, bf16[256,1024]{1,0:T(8,128)(2,1)} %collective-permute-done.5.refs_3_.refs_5_, pred[]{:T(512)} %eq.30), kind=kLoop, calls=%fused_computation.47 | loop fusion | flops 524288 | bytes 2621442 | tf_op jit(solution)/shard_map/jit(_where)/select_n | solution.py:553
  51.0 1.6 %collective-permute-start.10 = (bf16[256,1024]{1,0:T(8,128)(2,1)}, bf16[256,1024]{1,0:T(8,128)(2,1)}, u32[]{:S(2)}, u32[]{:S(2)}) collective-permute-start(bf16[256,1024]{1,0:T(8,128)(2,1)} %get-tuple-element.207), channel_id=1, source_target_pairs={{0,2},{2,4},{4,6},{6,7},{7,5},{5,3},{3,1},{1,0},{8,10},{10,12},{12... | collective-permute-start | bytes 1572872 | tf_op jit(solution)/shard_map/ppermute | solution.py:44
  52.5 4.8 %collective-permute-done.3.refs_4_.refs_6_ = bf16[256,1024]{1,0:T(8,128)(2,1)S(1)} collective-permute-done((bf16[256,1024]{1,0:T(8,128)(2,1)S(1)}, bf16[256,1024]{1,0:T(8,128)(2,1)S(1)}, u32[]{:S(2)}, u32[]{:S(2)}) %collective-permute-start.3) | collective-permute-done | bytes 524320 | tf_op jit(solution)/shard_map/ppermute | solution.py:44
  57.3 1.4 collective-permute-done.4.refs_6_.refs_8_
  58.7 1.2 broadcast_select_fusion.1
  61.3 1.4 collective-permute-start.9
  63.0 5.7 %collective-permute-done.10.refs_10_ = bf16[256,1024]{1,0:T(8,128)(2,1)} collective-permute-done((bf16[256,1024]{1,0:T(8,128)(2,1)}, bf16[256,1024]{1,0:T(8,128)(2,1)}, u32[]{:S(2)}, u32[]{:S(2)}) %collective-permute-start.10) | collective-permute-done | bytes 524320 | tf_op jit(solution)/shard_map/ppermute | solution.py:44
  68.6 3.8 %collective-permute-done.11.refs_12_ = bf16[256,1024]{1,0:T(8,128)(2,1)} collective-permute-done((bf16[256,1024]{1,0:T(8,128)(2,1)}, bf16[256,1024]{1,0:T(8,128)(2,1)}, u32[]{:S(2)}, u32[]{:S(2)}) %collective-permute-start.11) | collective-permute-done | bytes 524320 | tf_op jit(solution)/shard_map/ppermute | solution.py:47
  72.5 2.7 %fusion.20 = (bf16[256,1024]{1,0:T(8,128)(2,1)S(1)}, bf16[256,1024]{1,0:T(8,128)(2,1)S(1)}) fusion(bf16[256,1024]{1,0:T(8,128)(2,1)} %collective-permute-done.11.refs_12_, f32[6,512,1024]{2,1,0:T(8,128)} %get-tuple-element.132, pred[]{:T(512)} %eq.27, pred[]{:T(512)} %eq.28, bf16[256,1024]{1,0:T(8,128)(2,1)} %collective-permute-done.10.refs_10_), kind=kLoop, calls=%fused_computation.43 | loop fusion | flops 2621440 | bytes 4194306 | tf_op jit(solution)/shard_map/jit(_where)/select_n | solution.py:560
  75.2 1.6 %collective-permute-start.16 = (bf16[256,1024]{1,0:T(8,128)(2,1)S(1)}, bf16[256,1024]{1,0:T(8,128)(2,1)S(1)}, u32[]{:S(2)}, u32[]{:S(2)}) collective-permute-start(bf16[256,1024]{1,0:T(8,128)(2,1)S(1)} %get-tuple-element.202), channel_id=1, source_target_pairs={{0,2},{2,4},{4,6},{6,7},{7,5},{5,3},{3,1},{1,0},{8,10},{10,12},{12... | collective-permute-start | bytes 1572872 | tf_op jit(solution)/shard_map/ppermute | solution.py:44
  77.3 2.4 %collective-permute-start.22 = (bf16[512,1024]{1,0:T(8,128)(2,1)S(1)}, bf16[512,1024]{1,0:T(8,128)(2,1)S(1)}, u32[]{:S(2)}, u32[]{:S(2)}) collective-permute-start(bf16[512,1024]{1,0:T(8,128)(2,1)S(1)} %copy-done.15), channel_id=1, source_target_pairs={{2,3},{3,2},{4,5},{5,4},{10,11},{11,10},{12,13},{13,12},{18,19},{1... | collective-permute-start | bytes 3145736 | tf_op jit(solution)/shard_map/ppermute | solution.py:56
  79.9 3.8 %collective-permute-done.9.refs_13_ = bf16[256,1024]{1,0:T(8,128)(2,1)} collective-permute-done((bf16[256,1024]{1,0:T(8,128)(2,1)}, bf16[256,1024]{1,0:T(8,128)(2,1)}, u32[]{:S(2)}, u32[]{:S(2)}) %collective-permute-start.9) | collective-permute-done | bytes 524320 | tf_op jit(solution)/shard_map/ppermute | solution.py:47
  83.7 2.7 %fusion.22 = (bf16[256,1024]{1,0:T(8,128)(2,1)S(1)}, bf16[256,1024]{1,0:T(8,128)(2,1)S(1)}) fusion(bf16[256,1024]{1,0:T(8,128)(2,1)} %collective-permute-done.9.refs_13_, f32[6,512,1024]{2,1,0:T(8,128)} %get-tuple-element.132, pred[]{:T(512)} %eq.27, pred[]{:T(512)} %eq.28, bf16[256,1024]{1,0:T(8,128)(2,1)} %collective-permute-done.8.refs_11_), kind=kLoop, calls=%fused_computation.45 | loop fusion | flops 2621440 | bytes 4194306 | tf_op jit(solution)/shard_map/jit(_where)/select_n | solution.py:560
  86.4 1.6 %collective-permute-start.14 = (bf16[256,1024]{1,0:T(8,128)(2,1)S(1)}, bf16[256,1024]{1,0:T(8,128)(2,1)S(1)}, u32[]{:S(2)}, u32[]{:S(2)}) collective-permute-start(bf16[256,1024]{1,0:T(8,128)(2,1)S(1)} %get-tuple-element.200), channel_id=1, source_target_pairs={{0,2},{2,4},{4,6},{6,7},{7,5},{5,3},{3,1},{1,0},{8,10},{10,12},{12... | collective-permute-start | bytes 1572872 | tf_op jit(solution)/shard_map/ppermute | solution.py:44
  88.5 4.3 %fusion.1 = (bf16[384,1024]{1,0:T(8,128)(2,1)}, f32[384,1024]{1,0:T(8,128)}, f32[384,1024]{1,0:T(8,128)}) fusion(bf16[1,384,1024]{2,1,0:T(8,128)(2,1)S(1)} %copy-done.28, f32[384,1024]{1,0:T(8,128)S(1)} %copy-done.26, f32[384,1024]{1,0:T(8,128)S(1)} %copy-done.27, bf16[384,1024]{1,0:T(8,128)(2,1)} %collective-permute-done.7, bf16[384,1024]{1,0:T(8,128)(2,1)} %add_convert_fusion), kind=kLoop, calls=%fused_computation.3 | loop fusion | flops 5505024 | bytes 9437184 | tf_op jit(solution)/shard_map/convert_element_type | solution.py:637
  92.8 2.1 %collective-permute-done.17.refs_17_ = bf16[256,1024]{1,0:T(8,128)(2,1)S(1)} collective-permute-done((bf16[256,1024]{1,0:T(8,128)(2,1)S(1)}, bf16[256,1024]{1,0:T(8,128)(2,1)S(1)}, u32[]{:S(2)}, u32[]{:S(2)}) %collective-permute-start.17) | collective-permute-done | bytes 524320 | tf_op jit(solution)/shard_map/ppermute | solution.py:47
  94.8 2.1 %fusion.13 = (bf16[256,1024]{1,0:T(8,128)(2,1)S(1)}, bf16[256,1024]{1,0:T(8,128)(2,1)S(1)}) fusion(bf16[256,1024]{1,0:T(8,128)(2,1)S(1)} %collective-permute-done.17.refs_17_, f32[6,512,1024]{2,1,0:T(8,128)} %get-tuple-element.132, pred[]{:T(512)} %eq.30, bf16[256,1024]{1,0:T(8,128)(2,1)S(1)} %collective-permute-done.16.refs_15_, pred[]{:T(512)} %eq.29), kind=kLoop, calls=%fused_computation.30 | loop fusion | flops 2097152 | bytes 4194306 | tf_op jit(solution)/shard_map/convert_element_type | solution.py:567
  96.9 1.6 %collective-permute-start.20 = (bf16[256,1024]{1,0:T(8,128)(2,1)S(1)}, bf16[256,1024]{1,0:T(8,128)(2,1)S(1)}, u32[]{:S(2)}, u32[]{:S(2)}) collective-permute-start(bf16[256,1024]{1,0:T(8,128)(2,1)S(1)} %get-tuple-element.198), channel_id=1, source_target_pairs={{0,2},{2,4},{4,6},{6,7},{7,5},{5,3},{3,1},{1,0},{8,10},{10,12},{12... | collective-permute-start | bytes 1572872 | tf_op jit(solution)/shard_map/ppermute | solution.py:44
  99.0 3.2 %collective-permute-done.14.refs_16_ = bf16[256,1024]{1,0:T(8,128)(2,1)S(1)} collective-permute-done((bf16[256,1024]{1,0:T(8,128)(2,1)S(1)}, bf16[256,1024]{1,0:T(8,128)(2,1)S(1)}, u32[]{:S(2)}, u32[]{:S(2)}) %collective-permute-start.14) | collective-permute-done | bytes 524320 | tf_op jit(solution)/shard_map/ppermute | solution.py:44
  102.2 3.8 %collective-permute-done.15.refs_18_ = bf16[256,1024]{1,0:T(8,128)(2,1)S(1)} collective-permute-done((bf16[256,1024]{1,0:T(8,128)(2,1)S(1)}, bf16[256,1024]{1,0:T(8,128)(2,1)S(1)}, u32[]{:S(2)}, u32[]{:S(2)}) %collective-permute-start.15) | collective-permute-done | bytes 524320 | tf_op jit(solution)/shard_map/ppermute | solution.py:47
  106.1 6.1 %project_first.1 = (f32[512,128]{1,0:T(8,128)S(1)}, f32[5,512,512]{2,1,0:T(8,128)}) custom-call(s32[15]{0:T(128)S(1)} %pad_add_fusion.at, bf16[512,4096]{1,0:T(8,128)(2,1)S(1)} %bitcast.80, bf16[512,1024]{1,0:T(8,128)(2,1)S(1)} %copy-done.17, f32[512,128]{1,0:T(8,128)S(1)} %copy-done.21, bf16[512,1024]{1,0:T(8,128)(2,1)S(1)} %scale_rows.1.refs_0_.refs_2_, ...), custom_call_target="tpu_custom_call" | custom-call | flops 2684354560 | bytes 13107200 | tf_op jit(solution)/shard_map/project_first/pallas_call | solution.py:394
  112.3 1.9 %fusion.11 = (bf16[256,1024]{1,0:T(8,128)(2,1)S(1)}, bf16[256,1024]{1,0:T(8,128)(2,1)S(1)}) fusion(bf16[256,1024]{1,0:T(8,128)(2,1)S(1)} %collective-permute-done.15.refs_18_, f32[6,512,1024]{2,1,0:T(8,128)} %get-tuple-element.132, pred[]{:T(512)} %eq.30, bf16[256,1024]{1,0:T(8,128)(2,1)S(1)} %collective-permute-done.14.refs_16_, pred[]{:T(512)} %eq.29), kind=kLoop, calls=%fused_computation.25 | loop fusion | flops 2097152 | bytes 4194306 | tf_op jit(solution)/shard_map/convert_element_type | solution.py:567
  114.2 1.6 %collective-permute-start.18 = (bf16[256,1024]{1,0:T(8,128)(2,1)S(1)}, bf16[256,1024]{1,0:T(8,128)(2,1)S(1)}, u32[]{:S(2)}, u32[]{:S(2)}) collective-permute-start(bf16[256,1024]{1,0:T(8,128)(2,1)S(1)} %get-tuple-element.196), channel_id=1, source_target_pairs={{0,2},{2,4},{4,6},{6,7},{7,5},{5,3},{3,1},{1,0},{8,10},{10,12},{12... | collective-permute-start | bytes 1572872 | tf_op jit(solution)/shard_map/ppermute | solution.py:44
  116.3 2.4 %fusion.10 = bf16[512,1024]{1,0:T(8,128)(2,1)S(1)} fusion(f32[6,512,1024]{2,1,0:T(8,128)} %get-tuple-element.132, pred[]{:T(512)} %eq.27), kind=kLoop, calls=%fused_computation.20 | loop fusion | flops 524288 | bytes 3145729 | tf_op jit(solution)/shard_map/convert_element_type | solution.py:536
  118.7 2.5 %collective-permute-start.25 = (bf16[512,1024]{1,0:T(8,128)(2,1)S(1)}, bf16[512,1024]{1,0:T(8,128)(2,1)S(1)}, u32[]{:S(2)}, u32[]{:S(2)}) collective-permute-start(bf16[512,1024]{1,0:T(8,128)(2,1)S(1)} %fusion.10), channel_id=1, source_target_pairs={{2,3},{3,2},{4,5},{5,4},{10,11},{11,10},{12,13},{13,12},{18,19},{1... | collective-permute-start | bytes 3145736 | tf_op jit(solution)/shard_map/ppermute | solution.py:56
  121.2 2.0 %fusion.5 = (bf16[256,1024]{1,0:T(8,128)(2,1)S(1)}, bf16[256,1024]{1,0:T(8,128)(2,1)S(1)}) fusion(bf16[256,1024]{1,0:T(8,128)(2,1)S(1)} %collective-permute-done.21, f32[6,512,1024]{2,1,0:T(8,128)} %get-tuple-element.132, pred[]{:T(512)} %eq.28, bf16[512,1024]{1,0:T(8,128)(2,1)S(1)} %collective-permute-done.22, pred[]{:T(512)} %eq.27, ...), kind=kLoop, calls=%fused_computation.15 | loop fusion | flops 2883584 | bytes 4718594 | tf_op jit(solution)/shard_map/convert_element_type | solution.py:574
  123.2 1.6 %collective-permute-start.26 = (bf16[256,1024]{1,0:T(8,128)(2,1)S(1)}, bf16[256,1024]{1,0:T(8,128)(2,1)S(1)}, u32[]{:S(2)}, u32[]{:S(2)}) collective-permute-start(bf16[256,1024]{1,0:T(8,128)(2,1)S(1)} %get-tuple-element.194), channel_id=1, source_target_pairs={{0,2},{2,4},{4,6},{6,7},{7,5},{5,3},{3,1},{1,0},{8,10},{10,12},{12... | collective-permute-start | bytes 1572872 | tf_op jit(solution)/shard_map/ppermute | solution.py:44
  125.3 2.0 %collective-permute-done.18 = bf16[256,1024]{1,0:T(8,128)(2,1)S(1)} collective-permute-done((bf16[256,1024]{1,0:T(8,128)(2,1)S(1)}, bf16[256,1024]{1,0:T(8,128)(2,1)S(1)}, u32[]{:S(2)}, u32[]{:S(2)}) %collective-permute-start.18) | collective-permute-done | bytes 524320 | tf_op jit(solution)/shard_map/ppermute | solution.py:44
  127.3 3.3 %collective-permute-done.19 = bf16[256,1024]{1,0:T(8,128)(2,1)S(1)} collective-permute-done((bf16[256,1024]{1,0:T(8,128)(2,1)S(1)}, bf16[256,1024]{1,0:T(8,128)(2,1)S(1)}, u32[]{:S(2)}, u32[]{:S(2)}) %collective-permute-start.19) | collective-permute-done | bytes 524320 | tf_op jit(solution)/shard_map/ppermute | solution.py:47
  130.6 2.0 %fusion.9 = (bf16[256,1024]{1,0:T(8,128)(2,1)S(1)}, bf16[256,1024]{1,0:T(8,128)(2,1)S(1)}) fusion(bf16[256,1024]{1,0:T(8,128)(2,1)S(1)} %collective-permute-done.19, f32[6,512,1024]{2,1,0:T(8,128)} %get-tuple-element.132, pred[]{:T(512)} %eq.28, bf16[512,1024]{1,0:T(8,128)(2,1)S(1)} %collective-permute-done.22, pred[]{:T(512)} %eq.27, ...), kind=kLoop, calls=%fused_computation.19 | loop fusion | flops 2883584 | bytes 4718594 | tf_op jit(solution)/shard_map/convert_element_type | solution.py:574
  132.6 1.1 collective-permute-start.23
  134.7 16.1 %project_last.1 = (bf16[512,1024]{1,0:T(8,128)(2,1)}, bf16[512,4096]{1,0:T(8,128)(2,1)}) custom-call(s32[15]{0:T(128)S(1)} %pad_add_fusion.at, bf16[512,4096]{1,0:T(8,128)(2,1)} %bitcast.78, bf16[512,1024]{1,0:T(8,128)(2,1)} %copy-done.16, f32[512,128]{1,0:T(8,128)S(1)} %copy-done.21, f32[512,128]{1,0:T(8,128)S(1)} %get-tuple-element.211.cosine, ...), custom_call_target="tpu_custom_call" | custom-call | flops 8589934592 | bytes 16777216 | tf_op jit(solution)/shard_map/project_last/pallas_call | solution.py:427
  150.8 1.4 sum_of_terms.2
  152.2 1.3 sum_of_terms.3
  (108 shorter events, 12.5 us)
Async XLA Ops:
  3.3 102.8 %copy-start.8 = (bf16[512,1024]{1,0:T(8,128)(2,1)}, bf16[512,1024]{1,0:T(8,128)(2,1)S(1)}, u32[]{:S(2)}) copy-start(bf16[512,1024]{1,0:T(8,128)(2,1)S(1)} %scale_rows.1.refs_0_.refs_2_) | copy-start | bytes 3145732
  3.3 26.8 %collective-permute-start.1 = (bf16[512,1024]{1,0:T(8,128)(2,1)S(1)}, bf16[512,1024]{1,0:T(8,128)(2,1)S(1)}, u32[]{:S(2)}, u32[]{:S(2)}) collective-permute-start(bf16[512,1024]{1,0:T(8,128)(2,1)S(1)} %scale_rows.1.refs_0_.refs_2_), channel_id=1, source_target_pairs={{0,2},{2,4},{4,6},{6,7},{7,5},{5,3},{3,1},{1,0},{8,10},{10,12},{12... | collective-permute-start | bytes 3145736 | tf_op jit(solution)/shard_map/ppermute | solution.py:44
  4.9 25.2 %collective-permute-start.2 = (bf16[512,1024]{1,0:T(8,128)(2,1)S(1)}, bf16[512,1024]{1,0:T(8,128)(2,1)S(1)}, u32[]{:S(2)}, u32[]{:S(2)}) collective-permute-start(bf16[512,1024]{1,0:T(8,128)(2,1)S(1)} %scale_rows.1.refs_0_.refs_2_), channel_id=1, source_target_pairs={{2,0},{4,2},{6,4},{7,6},{5,7},{3,5},{1,3},{0,1},{10,8},{12,10},{14... | collective-permute-start | bytes 3145736 | tf_op jit(solution)/shard_map/ppermute | solution.py:47
  5.4 5.5 %copy-start.33 = (s32[8]{0:T(128)S(1)}, s32[8]{0:T(128)}, u32[]{:S(2)}) copy-start(s32[8]{0:T(128)} %constant.106.clone) | copy-start | bytes 100
  6.4 4.7 %collective-permute-start = (bf16[384,1024]{1,0:T(8,128)(2,1)}, bf16[384,1024]{1,0:T(8,128)(2,1)}, u32[]{:S(2)}, u32[]{:S(2)}) collective-permute-start(bf16[384,1024]{1,0:T(8,128)(2,1)} %convert_element_type.122), channel_id=1, source_target_pairs={{0,8},{8,0},{16,24},{24,16},{1,9},{9,1},{17,25},{25,17},{2,10},{10... | collective-permute-start | bytes 2359304 | tf_op jit(solution)/shard_map/ppermute | solution.py:463
  6.4 30.8 %collective-permute-start.12 = (bf16[512,1024]{1,0:T(8,128)(2,1)S(1)}, bf16[512,1024]{1,0:T(8,128)(2,1)}, u32[]{:S(2)}, u32[]{:S(2)}) collective-permute-start(bf16[512,1024]{1,0:T(8,128)(2,1)S(1)} %scale_rows.1.refs_0_.refs_2_), channel_id=1, source_target_pairs={{2,3},{3,2},{4,5},{5,4},{10,11},{11,10},{12,13},{13,12},{18,19},{1... | collective-permute-start | bytes 3145736 | tf_op jit(solution)/shard_map/ppermute | solution.py:56
  30.1 75.9 %copy-start.2 = (bf16[512,1024]{1,0:T(8,128)(2,1)}, bf16[512,1024]{1,0:T(8,128)(2,1)S(1)}, u32[]{:S(2)}) copy-start(bf16[512,1024]{1,0:T(8,128)(2,1)S(1)} %collective-permute-done.1.refs_1_.refs_3_) | copy-start | bytes 3145732
  30.1 75.9 %copy-start.3 = (bf16[512,1024]{1,0:T(8,128)(2,1)}, bf16[512,1024]{1,0:T(8,128)(2,1)S(1)}, u32[]{:S(2)}) copy-start(bf16[512,1024]{1,0:T(8,128)(2,1)S(1)} %collective-permute-done.2.refs_2_.refs_4_) | copy-start | bytes 3145732
  31.1 15.1 %collective-permute-start.5 = (bf16[256,1024]{1,0:T(8,128)(2,1)}, bf16[256,1024]{1,0:T(8,128)(2,1)}, u32[]{:S(2)}, u32[]{:S(2)}) collective-permute-start(bf16[256,1024]{1,0:T(8,128)(2,1)} %slice.127), channel_id=1, source_target_pairs={{0,2},{2,4},{4,6},{6,7},{7,5},{5,3},{3,1},{1,0},{8,10},{10,12},{12... | collective-permute-start | bytes 1572872 | tf_op jit(solution)/shard_map/ppermute | solution.py:44
  33.5 15.1 %collective-permute-start.6 = (bf16[256,1024]{1,0:T(8,128)(2,1)}, bf16[256,1024]{1,0:T(8,128)(2,1)}, u32[]{:S(2)}, u32[]{:S(2)}) collective-permute-start(bf16[256,1024]{1,0:T(8,128)(2,1)} %slice.128), channel_id=1, source_target_pairs={{2,0},{4,2},{6,4},{7,6},{5,7},{3,5},{1,3},{0,1},{10,8},{12,10},{14... | collective-permute-start | bytes 1572872 | tf_op jit(solution)/shard_map/ppermute | solution.py:47
  33.9 24.8 %collective-permute-start.7 = (bf16[384,1024]{1,0:T(8,128)(2,1)}, bf16[384,1024]{1,0:T(8,128)(2,1)}, u32[]{:S(2)}, u32[]{:S(2)}) collective-permute-start(bf16[384,1024]{1,0:T(8,128)(2,1)} %add_convert_fusion), channel_id=1, source_target_pairs={{0,16},{8,24},{16,0},{24,8},{1,17},{9,25},{17,1},{25,9},{2,18},{10... | collective-permute-start | bytes 2359304 | tf_op jit(solution)/shard_map/ppermute | solution.py:463
  35.5 13.1 %copy-start.14 = (bf16[512,1024]{1,0:T(8,128)(2,1)S(1)}, bf16[512,1024]{1,0:T(8,128)(2,1)}, u32[]{:S(2)}) copy-start(bf16[512,1024]{1,0:T(8,128)(2,1)} %copy-done.13) | copy-start | bytes 3145732
  35.6 21.7 %collective-permute-start.3 = (bf16[256,1024]{1,0:T(8,128)(2,1)S(1)}, bf16[256,1024]{1,0:T(8,128)(2,1)S(1)}, u32[]{:S(2)}, u32[]{:S(2)}) collective-permute-start(bf16[256,1024]{1,0:T(8,128)(2,1)S(1)} %slice.129), channel_id=1, source_target_pairs={{0,2},{2,4},{4,6},{6,7},{7,5},{5,3},{3,1},{1,0},{8,10},{10,12},{12... | collective-permute-start | bytes 1572872 | tf_op jit(solution)/shard_map/ppermute | solution.py:44
  37.2 21.5 %collective-permute-start.4 = (bf16[256,1024]{1,0:T(8,128)(2,1)S(1)}, bf16[256,1024]{1,0:T(8,128)(2,1)S(1)}, u32[]{:S(2)}, u32[]{:S(2)}) collective-permute-start(bf16[256,1024]{1,0:T(8,128)(2,1)S(1)} %slice.130), channel_id=1, source_target_pairs={{2,0},{4,2},{6,4},{7,6},{5,7},{3,5},{1,3},{0,1},{10,8},{12,10},{14... | collective-permute-start | bytes 1572872 | tf_op jit(solution)/shard_map/ppermute | solution.py:47
  46.2 31.1 %collective-permute-start.13 = (bf16[512,1024]{1,0:T(8,128)(2,1)}, bf16[512,1024]{1,0:T(8,128)(2,1)}, u32[]{:S(2)}, u32[]{:S(2)}) collective-permute-start(bf16[512,1024]{1,0:T(8,128)(2,1)} %broadcast_select_fusion), channel_id=1, source_target_pairs={{2,3},{3,2},{4,5},{5,4},{10,11},{11,10},{12,13},{13,12},{18,19},{1... | collective-permute-start | bytes 3145736 | tf_op jit(solution)/shard_map/ppermute | solution.py:56
  50.9 11.8 %copy-start.32 = (s32[8]{0:T(128)S(1)}, s32[8]{0:T(128)}, u32[]{:S(2)}) copy-start(s32[8]{0:T(128)} %constant.107.clone) | copy-start | bytes 100
  51.0 17.7 %collective-permute-start.10 = (bf16[256,1024]{1,0:T(8,128)(2,1)}, bf16[256,1024]{1,0:T(8,128)(2,1)}, u32[]{:S(2)}, u32[]{:S(2)}) collective-permute-start(bf16[256,1024]{1,0:T(8,128)(2,1)} %get-tuple-element.207), channel_id=1, source_target_pairs={{0,2},{2,4},{4,6},{6,7},{7,5},{5,3},{3,1},{1,0},{8,10},{10,12},{12... | collective-permute-start | bytes 1572872 | tf_op jit(solution)/shard_map/ppermute | solution.py:44
  57.3 15.2 %collective-permute-start.11 = (bf16[256,1024]{1,0:T(8,128)(2,1)}, bf16[256,1024]{1,0:T(8,128)(2,1)}, u32[]{:S(2)}, u32[]{:S(2)}) collective-permute-start(bf16[256,1024]{1,0:T(8,128)(2,1)} %get-tuple-element.206), channel_id=1, source_target_pairs={{2,0},{4,2},{6,4},{7,6},{5,7},{3,5},{1,3},{0,1},{10,8},{12,10},{14... | collective-permute-start | bytes 1572872 | tf_op jit(solution)/shard_map/ppermute | solution.py:47
  60.7 19.1 %collective-permute-start.8 = (bf16[256,1024]{1,0:T(8,128)(2,1)}, bf16[256,1024]{1,0:T(8,128)(2,1)}, u32[]{:S(2)}, u32[]{:S(2)}) collective-permute-start(bf16[256,1024]{1,0:T(8,128)(2,1)} %get-tuple-element.205), channel_id=1, source_target_pairs={{0,2},{2,4},{4,6},{6,7},{7,5},{5,3},{3,1},{1,0},{8,10},{10,12},{12... | collective-permute-start | bytes 1572872 | tf_op jit(solution)/shard_map/ppermute | solution.py:44
  61.3 22.4 %collective-permute-start.9 = (bf16[256,1024]{1,0:T(8,128)(2,1)}, bf16[256,1024]{1,0:T(8,128)(2,1)}, u32[]{:S(2)}, u32[]{:S(2)}) collective-permute-start(bf16[256,1024]{1,0:T(8,128)(2,1)} %get-tuple-element.204), channel_id=1, source_target_pairs={{2,0},{4,2},{6,4},{7,6},{5,7},{3,5},{1,3},{0,1},{10,8},{12,10},{14... | collective-permute-start | bytes 1572872 | tf_op jit(solution)/shard_map/ppermute | solution.py:47
  75.2 17.5 %collective-permute-start.16 = (bf16[256,1024]{1,0:T(8,128)(2,1)S(1)}, bf16[256,1024]{1,0:T(8,128)(2,1)S(1)}, u32[]{:S(2)}, u32[]{:S(2)}) collective-permute-start(bf16[256,1024]{1,0:T(8,128)(2,1)S(1)} %get-tuple-element.202), channel_id=1, source_target_pairs={{0,2},{2,4},{4,6},{6,7},{7,5},{5,3},{3,1},{1,0},{8,10},{10,12},{12... | collective-permute-start | bytes 1572872 | tf_op jit(solution)/shard_map/ppermute | solution.py:44
  76.9 11.6 %copy-start.26 = (f32[384,1024]{1,0:T(8,128)S(1)}, f32[384,1024]{1,0:T(8,128)}, u32[]{:S(2)}) copy-start(f32[384,1024]{1,0:T(8,128)} %param.16) | copy-start | bytes 4718596
  76.9 11.6 %copy-start.27 = (f32[384,1024]{1,0:T(8,128)S(1)}, f32[384,1024]{1,0:T(8,128)}, u32[]{:S(2)}) copy-start(f32[384,1024]{1,0:T(8,128)} %param.15) | copy-start | bytes 4718596
  76.9 11.6 %copy-start.28 = (bf16[1,384,1024]{2,1,0:T(8,128)(2,1)S(1)}, bf16[1,384,1024]{2,1,0:T(8,128)(2,1)}, u32[]{:S(2)}) copy-start(bf16[1,384,1024]{2,1,0:T(8,128)(2,1)} %param.17) | copy-start | bytes 2359300
  76.9 18.0 %collective-permute-start.17 = (bf16[256,1024]{1,0:T(8,128)(2,1)S(1)}, bf16[256,1024]{1,0:T(8,128)(2,1)S(1)}, u32[]{:S(2)}, u32[]{:S(2)}) collective-permute-start(bf16[256,1024]{1,0:T(8,128)(2,1)S(1)} %get-tuple-element.201), channel_id=1, source_target_pairs={{2,0},{4,2},{6,4},{7,6},{5,7},{3,5},{1,3},{0,1},{10,8},{12,10},{14... | collective-permute-start | bytes 1572872 | tf_op jit(solution)/shard_map/ppermute | solution.py:47
  77.3 41.4 %collective-permute-start.22 = (bf16[512,1024]{1,0:T(8,128)(2,1)S(1)}, bf16[512,1024]{1,0:T(8,128)(2,1)S(1)}, u32[]{:S(2)}, u32[]{:S(2)}) collective-permute-start(bf16[512,1024]{1,0:T(8,128)(2,1)S(1)} %copy-done.15), channel_id=1, source_target_pairs={{2,3},{3,2},{4,5},{5,4},{10,11},{11,10},{12,13},{13,12},{18,19},{1... | collective-permute-start | bytes 3145736 | tf_op jit(solution)/shard_map/ppermute | solution.py:56
  86.4 15.9 %collective-permute-start.14 = (bf16[256,1024]{1,0:T(8,128)(2,1)S(1)}, bf16[256,1024]{1,0:T(8,128)(2,1)S(1)}, u32[]{:S(2)}, u32[]{:S(2)}) collective-permute-start(bf16[256,1024]{1,0:T(8,128)(2,1)S(1)} %get-tuple-element.200), channel_id=1, source_target_pairs={{0,2},{2,4},{4,6},{6,7},{7,5},{5,3},{3,1},{1,0},{8,10},{10,12},{12... | collective-permute-start | bytes 1572872 | tf_op jit(solution)/shard_map/ppermute | solution.py:44
  88.0 18.1 %collective-permute-start.15 = (bf16[256,1024]{1,0:T(8,128)(2,1)S(1)}, bf16[256,1024]{1,0:T(8,128)(2,1)S(1)}, u32[]{:S(2)}, u32[]{:S(2)}) collective-permute-start(bf16[256,1024]{1,0:T(8,128)(2,1)S(1)} %get-tuple-element.199), channel_id=1, source_target_pairs={{2,0},{4,2},{6,4},{7,6},{5,7},{3,5},{1,3},{0,1},{10,8},{12,10},{14... | collective-permute-start | bytes 1572872 | tf_op jit(solution)/shard_map/ppermute | solution.py:47
  88.5 17.6 %copy-start.10 = (bf16[256,1024]{1,0:T(8,128)(2,1)S(1)}, bf16[256,1024]{1,0:T(8,128)(2,1)}, u32[]{:S(2)}) copy-start(bf16[256,1024]{1,0:T(8,128)(2,1)} %copy-done.9) | copy-start | bytes 1572868
  88.5 17.6 %copy-start.12 = (bf16[256,1024]{1,0:T(8,128)(2,1)S(1)}, bf16[256,1024]{1,0:T(8,128)(2,1)}, u32[]{:S(2)}) copy-start(bf16[256,1024]{1,0:T(8,128)(2,1)} %copy-done.11) | copy-start | bytes 1572868
  88.5 17.6 %copy-start.17 = (bf16[512,1024]{1,0:T(8,128)(2,1)S(1)}, bf16[512,1024]{1,0:T(8,128)(2,1)}, u32[]{:S(2)}) copy-start(bf16[512,1024]{1,0:T(8,128)(2,1)} %copy-done.16) | copy-start | bytes 3145732
  88.5 17.6 %copy-start.21 = (f32[512,128]{1,0:T(8,128)S(1)}, f32[512,128]{1,0:T(8,128)}, u32[]{:S(2)}) copy-start(f32[512,128]{1,0:T(8,128)} %copy-done.20) | copy-start | bytes 786436
  92.8 13.4 %copy-start.7 = (bf16[1,512,4096]{2,1,0:T(8,128)(2,1)S(1)}, bf16[1,512,4096]{2,1,0:T(8,128)(2,1)}, u32[]{:S(2)}) copy-start(bf16[1,512,4096]{2,1,0:T(8,128)(2,1)} %param.10) | copy-start | bytes 12582916
  96.9 24.2 %collective-permute-start.20 = (bf16[256,1024]{1,0:T(8,128)(2,1)S(1)}, bf16[256,1024]{1,0:T(8,128)(2,1)S(1)}, u32[]{:S(2)}, u32[]{:S(2)}) collective-permute-start(bf16[256,1024]{1,0:T(8,128)(2,1)S(1)} %get-tuple-element.198), channel_id=1, source_target_pairs={{0,2},{2,4},{4,6},{6,7},{7,5},{5,3},{3,1},{1,0},{8,10},{10,12},{12... | collective-permute-start | bytes 1572872 | tf_op jit(solution)/shard_map/ppermute | solution.py:44
  98.6 22.6 %collective-permute-start.21 = (bf16[256,1024]{1,0:T(8,128)(2,1)S(1)}, bf16[256,1024]{1,0:T(8,128)(2,1)S(1)}, u32[]{:S(2)}, u32[]{:S(2)}) collective-permute-start(bf16[256,1024]{1,0:T(8,128)(2,1)S(1)} %get-tuple-element.197), channel_id=1, source_target_pairs={{2,0},{4,2},{6,4},{7,6},{5,7},{3,5},{1,3},{0,1},{10,8},{12,10},{14... | collective-permute-start | bytes 1572872 | tf_op jit(solution)/shard_map/ppermute | solution.py:47
  102.2 10.0 %copy-start.30 = (bf16[256,1024]{1,0:T(8,128)(2,1)}, bf16[256,1024]{1,0:T(8,128)(2,1)S(1)}, u32[]{:S(2)}) copy-start(bf16[256,1024]{1,0:T(8,128)(2,1)S(1)} %collective-permute-done.14.refs_16_) | copy-start | bytes 1572868
  106.1 6.2 %copy-start.31 = (bf16[256,1024]{1,0:T(8,128)(2,1)}, bf16[256,1024]{1,0:T(8,128)(2,1)S(1)}, u32[]{:S(2)}) copy-start(bf16[256,1024]{1,0:T(8,128)(2,1)S(1)} %collective-permute-done.15.refs_18_) | copy-start | bytes 1572868
  114.2 13.0 %collective-permute-start.18 = (bf16[256,1024]{1,0:T(8,128)(2,1)S(1)}, bf16[256,1024]{1,0:T(8,128)(2,1)S(1)}, u32[]{:S(2)}, u32[]{:S(2)}) collective-permute-start(bf16[256,1024]{1,0:T(8,128)(2,1)S(1)} %get-tuple-element.196), channel_id=1, source_target_pairs={{0,2},{2,4},{4,6},{6,7},{7,5},{5,3},{3,1},{1,0},{8,10},{10,12},{12... | collective-permute-start | bytes 1572872 | tf_op jit(solution)/shard_map/ppermute | solution.py:44
  115.9 14.7 %collective-permute-start.19 = (bf16[256,1024]{1,0:T(8,128)(2,1)S(1)}, bf16[256,1024]{1,0:T(8,128)(2,1)S(1)}, u32[]{:S(2)}, u32[]{:S(2)}) collective-permute-start(bf16[256,1024]{1,0:T(8,128)(2,1)S(1)} %get-tuple-element.195), channel_id=1, source_target_pairs={{2,0},{4,2},{6,4},{7,6},{5,7},{3,5},{1,3},{0,1},{10,8},{12,10},{14... | collective-permute-start | bytes 1572872 | tf_op jit(solution)/shard_map/ppermute | solution.py:47
  118.7 32.1 %collective-permute-start.25 = (bf16[512,1024]{1,0:T(8,128)(2,1)S(1)}, bf16[512,1024]{1,0:T(8,128)(2,1)S(1)}, u32[]{:S(2)}, u32[]{:S(2)}) collective-permute-start(bf16[512,1024]{1,0:T(8,128)(2,1)S(1)} %fusion.10), channel_id=1, source_target_pairs={{2,3},{3,2},{4,5},{5,4},{10,11},{11,10},{12,13},{13,12},{18,19},{1... | collective-permute-start | bytes 3145736 | tf_op jit(solution)/shard_map/ppermute | solution.py:56
  123.2 27.5 %collective-permute-start.26 = (bf16[256,1024]{1,0:T(8,128)(2,1)S(1)}, bf16[256,1024]{1,0:T(8,128)(2,1)S(1)}, u32[]{:S(2)}, u32[]{:S(2)}) collective-permute-start(bf16[256,1024]{1,0:T(8,128)(2,1)S(1)} %get-tuple-element.194), channel_id=1, source_target_pairs={{0,2},{2,4},{4,6},{6,7},{7,5},{5,3},{3,1},{1,0},{8,10},{10,12},{12... | collective-permute-start | bytes 1572872 | tf_op jit(solution)/shard_map/ppermute | solution.py:44
  124.8 9.9 %copy-start.19 = (f32[512,128]{1,0:T(8,128)S(1)}, f32[512,128]{1,0:T(8,128)}, u32[]{:S(2)}) copy-start(f32[512,128]{1,0:T(8,128)} %copy-done.18) | copy-start | bytes 786436
  124.8 25.9 %collective-permute-start.27 = (bf16[256,1024]{1,0:T(8,128)(2,1)S(1)}, bf16[256,1024]{1,0:T(8,128)(2,1)S(1)}, u32[]{:S(2)}, u32[]{:S(2)}) collective-permute-start(bf16[256,1024]{1,0:T(8,128)(2,1)S(1)} %get-tuple-element.193), channel_id=1, source_target_pairs={{2,0},{4,2},{6,4},{7,6},{5,7},{3,5},{1,3},{0,1},{10,8},{12,10},{14... | collective-permute-start | bytes 1572872 | tf_op jit(solution)/shard_map/ppermute | solution.py:47
  132.6 18.2 %collective-permute-start.23 = (bf16[256,1024]{1,0:T(8,128)(2,1)S(1)}, bf16[256,1024]{1,0:T(8,128)(2,1)S(1)}, u32[]{:S(2)}, u32[]{:S(2)}) collective-permute-start(bf16[256,1024]{1,0:T(8,128)(2,1)S(1)} %get-tuple-element.192), channel_id=1, source_target_pairs={{0,2},{2,4},{4,6},{6,7},{7,5},{5,3},{3,1},{1,0},{8,10},{10,12},{12... | collective-permute-start | bytes 1572872 | tf_op jit(solution)/shard_map/ppermute | solution.py:44
  133.7 17.1 %copy-start.1 = (bf16[1,512,1024]{2,1,0:T(8,128)(2,1)S(1)}, bf16[1,512,1024]{2,1,0:T(8,128)(2,1)}, u32[]{:S(2)}) copy-start(bf16[1,512,1024]{2,1,0:T(8,128)(2,1)} %param.12) | copy-start | bytes 3145732
  133.7 17.1 %copy-start.5 = (f32[512,1024]{1,0:T(8,128)S(1)}, f32[512,1024]{1,0:T(8,128)}, u32[]{:S(2)}) copy-start(f32[512,1024]{1,0:T(8,128)} %copy-done.4) | copy-start | bytes 6291460
  133.7 17.1 %copy-start.23 = (bf16[1,512]{1,0:T(2,128)(2,1)S(1)}, bf16[1,512]{1,0:T(2,128)(2,1)}, u32[]{:S(2)}) copy-start(bf16[1,512]{1,0:T(2,128)(2,1)} %gain.5) | copy-start | bytes 3076
  133.7 17.1 %collective-permute-start.24 = (bf16[256,1024]{1,0:T(8,128)(2,1)S(1)}, bf16[256,1024]{1,0:T(8,128)(2,1)S(1)}, u32[]{:S(2)}, u32[]{:S(2)}) collective-permute-start(bf16[256,1024]{1,0:T(8,128)(2,1)S(1)} %get-tuple-element.191), channel_id=1, source_target_pairs={{2,0},{4,2},{6,4},{7,6},{5,7},{3,5},{1,3},{0,1},{10,8},{12,10},{14... | collective-permute-start | bytes 1572872 | tf_op jit(solution)/shard_map/ppermute | solution.py:47
  (14 other events, 28.2 us)

commit v14 on v13

--- a/solution.py
+++ b/solution.py
@@ -168,7 +168,7 @@
             jax.ShapeDtypeStruct((n - 2, shard, cols), f32),
             jax.ShapeDtypeStruct((shard, cols), f32),
         ],
-        compiler_params=pltpu.CompilerParams(vmem_limit_bytes=40 * 2**20),
+        compiler_params=pltpu.CompilerParams(vmem_limit_bytes=60 * 2**20),
         cost_estimate=pl.CostEstimate(
             flops=2 * rows * width * cols,
             bytes_accessed=2 * rows * width + 4 * width * cols,

time: 155 us -> 156 us (level)
  Pallas kernels: 37.7 us -> 41.7 us
  local copies, waits for them, and re-layouts: 8.67 us -> 4.71 us
    pallas_call x1, Pallas kernels: 12.1 us -> 16.1 us  [first_part(): pl.pallas_call(functools.partial(first_kernel, scale), grid_spec=pltpu.Pr...]
    unnamed x68 -> x58, local copies, waits for them, and re-layouts: 6.74 us -> 2.8 us
  transfers between devices with their start and end apart: 28 -> 28, of which waited for: 12 -> 12; matrix products, arithmetic and copies ran while one was open for 21% -> 21% of each run, Pallas kernels for 22% -> 25%
where the time goes in v14:
time: 156 us; the launch traced here: 154 us
  Pallas kernels  41.7 us (27%)
  waiting for transfers between devices  41.2 us (26%)
  starting transfers between devices  34.5 us (22%)
  other arithmetic  30.6 us (20%)
  local copies, waits for them, and re-layouts  4.71 us (3%)
    ppermute x11, waiting for transfers between devices, to_right(): return lax.ppermute(value, 'fsdp', self.right)  23.2 us
    ppermute x11, waiting for transfers between devices, to_left(): return lax.ppermute(value, 'fsdp', self.left)  18 us
    pallas_call x1, Pallas kernels, first_part(): pl.pallas_call(functools.partial(first_kernel, scale), grid_spec=pltpu.Pr...  16.1 us
    pallas_call x1, Pallas kernels, late_part(): pl.pallas_call(functools.partial(late_kernel, plan, done), in_specs=[pl.B...  16.1 us
    ppermute x11, starting transfers between devices, to_right(): return lax.ppermute(value, 'fsdp', self.right)  15.8 us
    ppermute x4, starting transfers between devices, over_chord(): return lax.ppermute(value, 'fsdp', [(2, 3), (3, 2), (4, 5), (5, 4)])  10.7 us
    ppermute x11, starting transfers between devices, to_left(): return lax.ppermute(value, 'fsdp', self.left)  6.4 us
    pallas_call x1, Pallas kernels, early_part(): pl.pallas_call(functools.partial(early_kernel, plan), in_specs=[pl.BlockS...  6.14 us
  transfers between devices with their start and end apart: 28, of which 12 were waited for; matrix products, arithmetic and copies ran while one was open for 21% of the time, Pallas kernels for 25%

profile of v14, /device:TPU:8, one launch (start us, length us, event | category | flops | bytes accessed | tf_op | source)
XLA Modules:
  0.0 153.9 jit_solution(3062919646546663326)
XLA Ops:
  0.6 1.2 copy-done
  3.3 1.6 %collective-permute-start.1 = (bf16[512,1024]{1,0:T(8,128)(2,1)S(1)}, bf16[512,1024]{1,0:T(8,128)(2,1)S(1)}, u32[]{:S(2)}, u32[]{:S(2)}) collective-permute-start(bf16[512,1024]{1,0:T(8,128)(2,1)S(1)} %scale_rows.1.refs_0_.refs_2_), channel_id=1, source_target_pairs={{0,2},{2,4},{4,6},{6,7},{7,5},{5,3},{3,1},{1,0},{8,10},{10,12},{12... | collective-permute-start | bytes 3145736 | tf_op jit(solution)/shard_map/ppermute | solution.py:44
  5.4 1.0 convert_element_type.122
  6.4 3.4 %collective-permute-start.12 = (bf16[512,1024]{1,0:T(8,128)(2,1)S(1)}, bf16[512,1024]{1,0:T(8,128)(2,1)}, u32[]{:S(2)}, u32[]{:S(2)}) collective-permute-start(bf16[512,1024]{1,0:T(8,128)(2,1)S(1)} %scale_rows.1.refs_0_.refs_2_), channel_id=1, source_target_pairs={{2,3},{3,2},{4,5},{5,4},{10,11},{11,10},{12,13},{13,12},{18,19},{1... | collective-permute-start | bytes 3145736 | tf_op jit(solution)/shard_map/ppermute | solution.py:56
  9.9 1.0 fusion.23
  11.4 1.0 pad_maximum_fusion
  12.4 2.3 %add_convert_fusion = bf16[384,1024]{1,0:T(8,128)(2,1)} fusion(bf16[384,1024]{1,0:T(8,128)(2,1)} %collective-permute-done, f32[384,1024]{1,0:T(8,128)S(1)} %bitcast.82), kind=kLoop, calls=%fused_computation.7 | loop fusion | flops 1966080 | bytes 3145728 | tf_op jit(solution)/shard_map/convert_element_type | solution.py:459
  14.7 16.1 %norm_and_weight_terms.1 = (bf16[512,1024]{1,0:T(8,128)(2,1)}, f32[512,128]{1,0:T(8,128)}, bf16[512,1024]{1,0:T(8,128)(2,1)}, f32[6,512,1024]{2,1,0:T(8,128)}, f32[512,1024]{1,0:T(8,128)}) custom-call(s32[8]{0:T(128)} %compare_select_fusion.4.at, bf16[512,4096]{1,0:T(8,128)(2,1)} %bitcast.78, bf16[512,1024]{1,0:T(8,128)(2,1)} %bitcast.84, ...), custom_call_target="tpu_custom_call" | custom-call | flops 4294967296 | bytes 20971520 | tf_op jit(solution)/shard_map/norm_and_weight_terms/pallas_call | solution.py:145
  31.8 1.6 %collective-permute-start.5 = (bf16[256,1024]{1,0:T(8,128)(2,1)}, bf16[256,1024]{1,0:T(8,128)(2,1)}, u32[]{:S(2)}, u32[]{:S(2)}) collective-permute-start(bf16[256,1024]{1,0:T(8,128)(2,1)} %slice.127), channel_id=1, source_target_pairs={{0,2},{2,4},{4,6},{6,7},{7,5},{5,3},{3,1},{1,0},{8,10},{10,12},{12... | collective-permute-start | bytes 1572872 | tf_op jit(solution)/shard_map/ppermute | solution.py:44
  34.6 1.5 collective-permute-start.7
  36.2 1.6 %collective-permute-start.3 = (bf16[256,1024]{1,0:T(8,128)(2,1)S(1)}, bf16[256,1024]{1,0:T(8,128)(2,1)S(1)}, u32[]{:S(2)}, u32[]{:S(2)}) collective-permute-start(bf16[256,1024]{1,0:T(8,128)(2,1)S(1)} %slice.129), channel_id=1, source_target_pairs={{0,2},{2,4},{4,6},{6,7},{7,5},{5,3},{3,1},{1,0},{8,10},{10,12},{12... | collective-permute-start | bytes 1572872 | tf_op jit(solution)/shard_map/ppermute | solution.py:44
  38.3 1.1 broadcast_select_fusion
  39.4 7.4 %collective-permute-done.5.refs_3_.refs_5_ = bf16[256,1024]{1,0:T(8,128)(2,1)} collective-permute-done((bf16[256,1024]{1,0:T(8,128)(2,1)}, bf16[256,1024]{1,0:T(8,128)(2,1)}, u32[]{:S(2)}, u32[]{:S(2)}) %collective-permute-start.5) | collective-permute-done | bytes 524320 | tf_op jit(solution)/shard_map/ppermute | solution.py:44
  46.8 2.4 %collective-permute-start.13 = (bf16[512,1024]{1,0:T(8,128)(2,1)}, bf16[512,1024]{1,0:T(8,128)(2,1)}, u32[]{:S(2)}, u32[]{:S(2)}) collective-permute-start(bf16[512,1024]{1,0:T(8,128)(2,1)} %broadcast_select_fusion), channel_id=1, source_target_pairs={{2,3},{3,2},{4,5},{5,4},{10,11},{11,10},{12,13},{13,12},{18,19},{1... | collective-permute-start | bytes 3145736 | tf_op jit(solution)/shard_map/ppermute | solution.py:56
  49.3 2.3 %broadcast_select_fusion.2 = (bf16[256,1024]{1,0:T(8,128)(2,1)}, bf16[256,1024]{1,0:T(8,128)(2,1)}) fusion(bf16[256,1024]{1,0:T(8,128)(2,1)} %collective-permute-done.6.refs_5_.refs_7_, pred[]{:T(512)} %eq.29, bf16[512,1024]{1,0:T(8,128)(2,1)S(1)} %copy-done.21, bf16[256,1024]{1,0:T(8,128)(2,1)} %collective-permute-done.5.refs_3_.refs_5_, pred[]{:T(512)} %eq.30), kind=kLoop, calls=%fused_computation.47 | loop fusion | flops 524288 | bytes 2621442 | tf_op jit(solution)/shard_map/jit(_where)/select_n | solution.py:553
  51.6 1.6 %collective-permute-start.10 = (bf16[256,1024]{1,0:T(8,128)(2,1)}, bf16[256,1024]{1,0:T(8,128)(2,1)}, u32[]{:S(2)}, u32[]{:S(2)}) collective-permute-start(bf16[256,1024]{1,0:T(8,128)(2,1)} %get-tuple-element.207), channel_id=1, source_target_pairs={{0,2},{2,4},{4,6},{6,7},{7,5},{5,3},{3,1},{1,0},{8,10},{10,12},{12... | collective-permute-start | bytes 1572872 | tf_op jit(solution)/shard_map/ppermute | solution.py:44
  53.2 4.8 %collective-permute-done.3.refs_4_.refs_6_ = bf16[256,1024]{1,0:T(8,128)(2,1)S(1)} collective-permute-done((bf16[256,1024]{1,0:T(8,128)(2,1)S(1)}, bf16[256,1024]{1,0:T(8,128)(2,1)S(1)}, u32[]{:S(2)}, u32[]{:S(2)}) %collective-permute-start.3) | collective-permute-done | bytes 524320 | tf_op jit(solution)/shard_map/ppermute | solution.py:44
  58.0 1.4 collective-permute-done.4.refs_6_.refs_8_
  59.4 1.2 broadcast_select_fusion.1
  62.0 1.4 collective-permute-start.9
  63.6 5.7 %collective-permute-done.10.refs_10_ = bf16[256,1024]{1,0:T(8,128)(2,1)} collective-permute-done((bf16[256,1024]{1,0:T(8,128)(2,1)}, bf16[256,1024]{1,0:T(8,128)(2,1)}, u32[]{:S(2)}, u32[]{:S(2)}) %collective-permute-start.10) | collective-permute-done | bytes 524320 | tf_op jit(solution)/shard_map/ppermute | solution.py:44
  69.3 3.8 %collective-permute-done.11.refs_12_ = bf16[256,1024]{1,0:T(8,128)(2,1)} collective-permute-done((bf16[256,1024]{1,0:T(8,128)(2,1)}, bf16[256,1024]{1,0:T(8,128)(2,1)}, u32[]{:S(2)}, u32[]{:S(2)}) %collective-permute-start.11) | collective-permute-done | bytes 524320 | tf_op jit(solution)/shard_map/ppermute | solution.py:47
  73.1 2.7 %fusion.20 = (bf16[256,1024]{1,0:T(8,128)(2,1)S(1)}, bf16[256,1024]{1,0:T(8,128)(2,1)S(1)}) fusion(bf16[256,1024]{1,0:T(8,128)(2,1)} %collective-permute-done.11.refs_12_, f32[6,512,1024]{2,1,0:T(8,128)} %get-tuple-element.132, pred[]{:T(512)} %eq.27, pred[]{:T(512)} %eq.28, bf16[256,1024]{1,0:T(8,128)(2,1)} %collective-permute-done.10.refs_10_), kind=kLoop, calls=%fused_computation.43 | loop fusion | flops 2621440 | bytes 4194306 | tf_op jit(solution)/shard_map/jit(_where)/select_n | solution.py:560
  75.9 1.6 %collective-permute-start.16 = (bf16[256,1024]{1,0:T(8,128)(2,1)S(1)}, bf16[256,1024]{1,0:T(8,128)(2,1)S(1)}, u32[]{:S(2)}, u32[]{:S(2)}) collective-permute-start(bf16[256,1024]{1,0:T(8,128)(2,1)S(1)} %get-tuple-element.202), channel_id=1, source_target_pairs={{0,2},{2,4},{4,6},{6,7},{7,5},{5,3},{3,1},{1,0},{8,10},{10,12},{12... | collective-permute-start | bytes 1572872 | tf_op jit(solution)/shard_map/ppermute | solution.py:44
  78.0 2.4 %collective-permute-start.22 = (bf16[512,1024]{1,0:T(8,128)(2,1)S(1)}, bf16[512,1024]{1,0:T(8,128)(2,1)S(1)}, u32[]{:S(2)}, u32[]{:S(2)}) collective-permute-start(bf16[512,1024]{1,0:T(8,128)(2,1)S(1)} %copy-done.22), channel_id=1, source_target_pairs={{2,3},{3,2},{4,5},{5,4},{10,11},{11,10},{12,13},{13,12},{18,19},{1... | collective-permute-start | bytes 3145736 | tf_op jit(solution)/shard_map/ppermute | solution.py:56
  80.5 3.8 %collective-permute-done.9.refs_13_ = bf16[256,1024]{1,0:T(8,128)(2,1)} collective-permute-done((bf16[256,1024]{1,0:T(8,128)(2,1)}, bf16[256,1024]{1,0:T(8,128)(2,1)}, u32[]{:S(2)}, u32[]{:S(2)}) %collective-permute-start.9) | collective-permute-done | bytes 524320 | tf_op jit(solution)/shard_map/ppermute | solution.py:47
  84.4 2.7 %fusion.22 = (bf16[256,1024]{1,0:T(8,128)(2,1)S(1)}, bf16[256,1024]{1,0:T(8,128)(2,1)S(1)}) fusion(bf16[256,1024]{1,0:T(8,128)(2,1)} %collective-permute-done.9.refs_13_, f32[6,512,1024]{2,1,0:T(8,128)} %get-tuple-element.132, pred[]{:T(512)} %eq.27, pred[]{:T(512)} %eq.28, bf16[256,1024]{1,0:T(8,128)(2,1)} %collective-permute-done.8.refs_11_), kind=kLoop, calls=%fused_computation.45 | loop fusion | flops 2621440 | bytes 4194306 | tf_op jit(solution)/shard_map/jit(_where)/select_n | solution.py:560
  87.0 1.6 %collective-permute-start.14 = (bf16[256,1024]{1,0:T(8,128)(2,1)S(1)}, bf16[256,1024]{1,0:T(8,128)(2,1)S(1)}, u32[]{:S(2)}, u32[]{:S(2)}) collective-permute-start(bf16[256,1024]{1,0:T(8,128)(2,1)S(1)} %get-tuple-element.200), channel_id=1, source_target_pairs={{0,2},{2,4},{4,6},{6,7},{7,5},{5,3},{3,1},{1,0},{8,10},{10,12},{12... | collective-permute-start | bytes 1572872 | tf_op jit(solution)/shard_map/ppermute | solution.py:44
  89.2 4.3 %fusion.1 = (bf16[384,1024]{1,0:T(8,128)(2,1)}, f32[384,1024]{1,0:T(8,128)}, f32[384,1024]{1,0:T(8,128)}) fusion(bf16[1,384,1024]{2,1,0:T(8,128)(2,1)S(1)} %copy-done.23, f32[384,1024]{1,0:T(8,128)S(1)} %copy-done.19, f32[384,1024]{1,0:T(8,128)S(1)} %copy-done.20, bf16[384,1024]{1,0:T(8,128)(2,1)} %collective-permute-done.7, bf16[384,1024]{1,0:T(8,128)(2,1)} %add_convert_fusion), kind=kLoop, calls=%fused_computation.3 | loop fusion | flops 5505024 | bytes 9437184 | tf_op jit(solution)/shard_map/convert_element_type | solution.py:637
  93.4 2.1 %collective-permute-done.17.refs_17_ = bf16[256,1024]{1,0:T(8,128)(2,1)S(1)} collective-permute-done((bf16[256,1024]{1,0:T(8,128)(2,1)S(1)}, bf16[256,1024]{1,0:T(8,128)(2,1)S(1)}, u32[]{:S(2)}, u32[]{:S(2)}) %collective-permute-start.17) | collective-permute-done | bytes 524320 | tf_op jit(solution)/shard_map/ppermute | solution.py:47
  95.5 2.1 %fusion.13 = (bf16[256,1024]{1,0:T(8,128)(2,1)S(1)}, bf16[256,1024]{1,0:T(8,128)(2,1)S(1)}) fusion(bf16[256,1024]{1,0:T(8,128)(2,1)S(1)} %collective-permute-done.17.refs_17_, f32[6,512,1024]{2,1,0:T(8,128)} %get-tuple-element.132, pred[]{:T(512)} %eq.30, bf16[256,1024]{1,0:T(8,128)(2,1)S(1)} %collective-permute-done.16.refs_15_, pred[]{:T(512)} %eq.29), kind=kLoop, calls=%fused_computation.30 | loop fusion | flops 2097152 | bytes 4194306 | tf_op jit(solution)/shard_map/convert_element_type | solution.py:567
  97.6 1.6 %collective-permute-start.20 = (bf16[256,1024]{1,0:T(8,128)(2,1)S(1)}, bf16[256,1024]{1,0:T(8,128)(2,1)S(1)}, u32[]{:S(2)}, u32[]{:S(2)}) collective-permute-start(bf16[256,1024]{1,0:T(8,128)(2,1)S(1)} %get-tuple-element.198), channel_id=1, source_target_pairs={{0,2},{2,4},{4,6},{6,7},{7,5},{5,3},{3,1},{1,0},{8,10},{10,12},{12... | collective-permute-start | bytes 1572872 | tf_op jit(solution)/shard_map/ppermute | solution.py:44
  99.7 3.2 %collective-permute-done.14.refs_16_ = bf16[256,1024]{1,0:T(8,128)(2,1)S(1)} collective-permute-done((bf16[256,1024]{1,0:T(8,128)(2,1)S(1)}, bf16[256,1024]{1,0:T(8,128)(2,1)S(1)}, u32[]{:S(2)}, u32[]{:S(2)}) %collective-permute-start.14) | collective-permute-done | bytes 524320 | tf_op jit(solution)/shard_map/ppermute | solution.py:44
  102.9 3.8 %collective-permute-done.15.refs_18_ = bf16[256,1024]{1,0:T(8,128)(2,1)S(1)} collective-permute-done((bf16[256,1024]{1,0:T(8,128)(2,1)S(1)}, bf16[256,1024]{1,0:T(8,128)(2,1)S(1)}, u32[]{:S(2)}, u32[]{:S(2)}) %collective-permute-start.15) | collective-permute-done | bytes 524320 | tf_op jit(solution)/shard_map/ppermute | solution.py:47
  106.8 6.1 %project_first.1 = (f32[512,128]{1,0:T(8,128)S(1)}, f32[5,512,512]{2,1,0:T(8,128)}) custom-call(s32[15]{0:T(128)S(1)} %pad_add_fusion.at, bf16[512,4096]{1,0:T(8,128)(2,1)S(1)} %bitcast.80, bf16[512,1024]{1,0:T(8,128)(2,1)S(1)} %copy-done.11, f32[512,128]{1,0:T(8,128)S(1)} %copy-done.14, bf16[512,1024]{1,0:T(8,128)(2,1)S(1)} %scale_rows.1.refs_0_.refs_2_, ...), custom_call_target="tpu_custom_call" | custom-call | flops 2684354560 | bytes 13107200 | tf_op jit(solution)/shard_map/project_first/pallas_call | solution.py:394
  113.0 1.9 %fusion.11 = (bf16[256,1024]{1,0:T(8,128)(2,1)S(1)}, bf16[256,1024]{1,0:T(8,128)(2,1)S(1)}) fusion(bf16[256,1024]{1,0:T(8,128)(2,1)S(1)} %collective-permute-done.15.refs_18_, f32[6,512,1024]{2,1,0:T(8,128)} %get-tuple-element.132, pred[]{:T(512)} %eq.30, bf16[256,1024]{1,0:T(8,128)(2,1)S(1)} %collective-permute-done.14.refs_16_, pred[]{:T(512)} %eq.29), kind=kLoop, calls=%fused_computation.25 | loop fusion | flops 2097152 | bytes 4194306 | tf_op jit(solution)/shard_map/convert_element_type | solution.py:567
  114.9 1.6 %collective-permute-start.18 = (bf16[256,1024]{1,0:T(8,128)(2,1)S(1)}, bf16[256,1024]{1,0:T(8,128)(2,1)S(1)}, u32[]{:S(2)}, u32[]{:S(2)}) collective-permute-start(bf16[256,1024]{1,0:T(8,128)(2,1)S(1)} %get-tuple-element.196), channel_id=1, source_target_pairs={{0,2},{2,4},{4,6},{6,7},{7,5},{5,3},{3,1},{1,0},{8,10},{10,12},{12... | collective-permute-start | bytes 1572872 | tf_op jit(solution)/shard_map/ppermute | solution.py:44
  117.0 2.4 %fusion.10 = bf16[512,1024]{1,0:T(8,128)(2,1)S(1)} fusion(f32[6,512,1024]{2,1,0:T(8,128)} %get-tuple-element.132, pred[]{:T(512)} %eq.27), kind=kLoop, calls=%fused_computation.20 | loop fusion | flops 524288 | bytes 3145729 | tf_op jit(solution)/shard_map/convert_element_type | solution.py:536
  119.4 2.4 %collective-permute-start.25 = (bf16[512,1024]{1,0:T(8,128)(2,1)S(1)}, bf16[512,1024]{1,0:T(8,128)(2,1)S(1)}, u32[]{:S(2)}, u32[]{:S(2)}) collective-permute-start(bf16[512,1024]{1,0:T(8,128)(2,1)S(1)} %fusion.10), channel_id=1, source_target_pairs={{2,3},{3,2},{4,5},{5,4},{10,11},{11,10},{12,13},{13,12},{18,19},{1... | collective-permute-start | bytes 3145736 | tf_op jit(solution)/shard_map/ppermute | solution.py:56
  121.9 2.0 %fusion.5 = (bf16[256,1024]{1,0:T(8,128)(2,1)S(1)}, bf16[256,1024]{1,0:T(8,128)(2,1)S(1)}) fusion(bf16[256,1024]{1,0:T(8,128)(2,1)S(1)} %collective-permute-done.21, f32[6,512,1024]{2,1,0:T(8,128)} %get-tuple-element.132, pred[]{:T(512)} %eq.28, bf16[512,1024]{1,0:T(8,128)(2,1)S(1)} %collective-permute-done.22, pred[]{:T(512)} %eq.27, ...), kind=kLoop, calls=%fused_computation.15 | loop fusion | flops 2883584 | bytes 4718594 | tf_op jit(solution)/shard_map/convert_element_type | solution.py:574
  123.9 1.6 %collective-permute-start.26 = (bf16[256,1024]{1,0:T(8,128)(2,1)S(1)}, bf16[256,1024]{1,0:T(8,128)(2,1)S(1)}, u32[]{:S(2)}, u32[]{:S(2)}) collective-permute-start(bf16[256,1024]{1,0:T(8,128)(2,1)S(1)} %get-tuple-element.194), channel_id=1, source_target_pairs={{0,2},{2,4},{4,6},{6,7},{7,5},{5,3},{3,1},{1,0},{8,10},{10,12},{12... | collective-permute-start | bytes 1572872 | tf_op jit(solution)/shard_map/ppermute | solution.py:44
  126.0 1.9 %collective-permute-done.18 = bf16[256,1024]{1,0:T(8,128)(2,1)S(1)} collective-permute-done((bf16[256,1024]{1,0:T(8,128)(2,1)S(1)}, bf16[256,1024]{1,0:T(8,128)(2,1)S(1)}, u32[]{:S(2)}, u32[]{:S(2)}) %collective-permute-start.18) | collective-permute-done | bytes 524320 | tf_op jit(solution)/shard_map/ppermute | solution.py:44
  127.9 3.0 %collective-permute-done.19 = bf16[256,1024]{1,0:T(8,128)(2,1)S(1)} collective-permute-done((bf16[256,1024]{1,0:T(8,128)(2,1)S(1)}, bf16[256,1024]{1,0:T(8,128)(2,1)S(1)}, u32[]{:S(2)}, u32[]{:S(2)}) %collective-permute-start.19) | collective-permute-done | bytes 524320 | tf_op jit(solution)/shard_map/ppermute | solution.py:47
  130.9 2.0 %fusion.9 = (bf16[256,1024]{1,0:T(8,128)(2,1)S(1)}, bf16[256,1024]{1,0:T(8,128)(2,1)S(1)}) fusion(bf16[256,1024]{1,0:T(8,128)(2,1)S(1)} %collective-permute-done.19, f32[6,512,1024]{2,1,0:T(8,128)} %get-tuple-element.132, pred[]{:T(512)} %eq.28, bf16[512,1024]{1,0:T(8,128)(2,1)S(1)} %collective-permute-done.22, pred[]{:T(512)} %eq.27, ...), kind=kLoop, calls=%fused_computation.19 | loop fusion | flops 2883584 | bytes 4718594 | tf_op jit(solution)/shard_map/convert_element_type | solution.py:574
  133.7 1.3 collective-permute-start.24
  135.0 16.1 %project_last.1 = (bf16[512,1024]{1,0:T(8,128)(2,1)}, bf16[512,4096]{1,0:T(8,128)(2,1)}) custom-call(s32[15]{0:T(128)S(1)} %pad_add_fusion.at, bf16[512,4096]{1,0:T(8,128)(2,1)} %bitcast.79, bf16[512,1024]{1,0:T(8,128)(2,1)} %get-tuple-element.100.kv_grad, f32[512,128]{1,0:T(8,128)S(1)} %copy-done.14, f32[512,128]{1,0:T(8,128)S(1)} %copy-done.12, ...), custom_call_target="tpu_custom_call" | custom-call | flops 8589934592 | bytes 16777216 | tf_op jit(solution)/shard_map/project_last/pallas_call | solution.py:427
  151.1 1.4 sum_of_terms.2
  152.5 1.3 sum_of_terms.3
  (98 shorter events, 10.0 us)
Async XLA Ops:
  3.3 103.4 %copy-start.6 = (bf16[512,1024]{1,0:T(8,128)(2,1)}, bf16[512,1024]{1,0:T(8,128)(2,1)S(1)}, u32[]{:S(2)}) copy-start(bf16[512,1024]{1,0:T(8,128)(2,1)S(1)} %scale_rows.1.refs_0_.refs_2_) | copy-start | bytes 3145732
  3.3 27.5 %collective-permute-start.1 = (bf16[512,1024]{1,0:T(8,128)(2,1)S(1)}, bf16[512,1024]{1,0:T(8,128)(2,1)S(1)}, u32[]{:S(2)}, u32[]{:S(2)}) collective-permute-start(bf16[512,1024]{1,0:T(8,128)(2,1)S(1)} %scale_rows.1.refs_0_.refs_2_), channel_id=1, source_target_pairs={{0,2},{2,4},{4,6},{6,7},{7,5},{5,3},{3,1},{1,0},{8,10},{10,12},{12... | collective-permute-start | bytes 3145736 | tf_op jit(solution)/shard_map/ppermute | solution.py:44
  4.9 25.9 %collective-permute-start.2 = (bf16[512,1024]{1,0:T(8,128)(2,1)S(1)}, bf16[512,1024]{1,0:T(8,128)(2,1)S(1)}, u32[]{:S(2)}, u32[]{:S(2)}) collective-permute-start(bf16[512,1024]{1,0:T(8,128)(2,1)S(1)} %scale_rows.1.refs_0_.refs_2_), channel_id=1, source_target_pairs={{2,0},{4,2},{6,4},{7,6},{5,7},{3,5},{1,3},{0,1},{10,8},{12,10},{14... | collective-permute-start | bytes 3145736 | tf_op jit(solution)/shard_map/ppermute | solution.py:47
  6.4 6.0 %collective-permute-start = (bf16[384,1024]{1,0:T(8,128)(2,1)}, bf16[384,1024]{1,0:T(8,128)(2,1)}, u32[]{:S(2)}, u32[]{:S(2)}) collective-permute-start(bf16[384,1024]{1,0:T(8,128)(2,1)} %convert_element_type.122), channel_id=1, source_target_pairs={{0,8},{8,0},{16,24},{24,16},{1,9},{9,1},{17,25},{25,17},{2,10},{10... | collective-permute-start | bytes 2359304 | tf_op jit(solution)/shard_map/ppermute | solution.py:463
  6.4 31.5 %collective-permute-start.12 = (bf16[512,1024]{1,0:T(8,128)(2,1)S(1)}, bf16[512,1024]{1,0:T(8,128)(2,1)}, u32[]{:S(2)}, u32[]{:S(2)}) collective-permute-start(bf16[512,1024]{1,0:T(8,128)(2,1)S(1)} %scale_rows.1.refs_0_.refs_2_), channel_id=1, source_target_pairs={{2,3},{3,2},{4,5},{5,4},{10,11},{11,10},{12,13},{13,12},{18,19},{1... | collective-permute-start | bytes 3145736 | tf_op jit(solution)/shard_map/ppermute | solution.py:56
  30.8 75.9 %copy-start.2 = (bf16[512,1024]{1,0:T(8,128)(2,1)}, bf16[512,1024]{1,0:T(8,128)(2,1)S(1)}, u32[]{:S(2)}) copy-start(bf16[512,1024]{1,0:T(8,128)(2,1)S(1)} %collective-permute-done.1.refs_1_.refs_3_) | copy-start | bytes 3145732
  30.8 75.9 %copy-start.3 = (bf16[512,1024]{1,0:T(8,128)(2,1)}, bf16[512,1024]{1,0:T(8,128)(2,1)S(1)}, u32[]{:S(2)}) copy-start(bf16[512,1024]{1,0:T(8,128)(2,1)S(1)} %collective-permute-done.2.refs_2_.refs_4_) | copy-start | bytes 3145732
  31.8 15.1 %collective-permute-start.5 = (bf16[256,1024]{1,0:T(8,128)(2,1)}, bf16[256,1024]{1,0:T(8,128)(2,1)}, u32[]{:S(2)}, u32[]{:S(2)}) collective-permute-start(bf16[256,1024]{1,0:T(8,128)(2,1)} %slice.127), channel_id=1, source_target_pairs={{0,2},{2,4},{4,6},{6,7},{7,5},{5,3},{3,1},{1,0},{8,10},{10,12},{12... | collective-permute-start | bytes 1572872 | tf_op jit(solution)/shard_map/ppermute | solution.py:44
  34.1 15.1 %collective-permute-start.6 = (bf16[256,1024]{1,0:T(8,128)(2,1)}, bf16[256,1024]{1,0:T(8,128)(2,1)}, u32[]{:S(2)}, u32[]{:S(2)}) collective-permute-start(bf16[256,1024]{1,0:T(8,128)(2,1)} %slice.128), channel_id=1, source_target_pairs={{2,0},{4,2},{6,4},{7,6},{5,7},{3,5},{1,3},{0,1},{10,8},{12,10},{14... | collective-permute-start | bytes 1572872 | tf_op jit(solution)/shard_map/ppermute | solution.py:47
  34.6 24.8 %collective-permute-start.7 = (bf16[384,1024]{1,0:T(8,128)(2,1)}, bf16[384,1024]{1,0:T(8,128)(2,1)}, u32[]{:S(2)}, u32[]{:S(2)}) collective-permute-start(bf16[384,1024]{1,0:T(8,128)(2,1)} %add_convert_fusion), channel_id=1, source_target_pairs={{0,16},{8,24},{16,0},{24,8},{1,17},{9,25},{17,1},{25,9},{2,18},{10... | collective-permute-start | bytes 2359304 | tf_op jit(solution)/shard_map/ppermute | solution.py:463
  36.2 13.1 %copy-start.21 = (bf16[512,1024]{1,0:T(8,128)(2,1)S(1)}, bf16[512,1024]{1,0:T(8,128)(2,1)}, u32[]{:S(2)}) copy-start(bf16[512,1024]{1,0:T(8,128)(2,1)} %get-tuple-element.171) | copy-start | bytes 3145732
  36.2 21.7 %collective-permute-start.3 = (bf16[256,1024]{1,0:T(8,128)(2,1)S(1)}, bf16[256,1024]{1,0:T(8,128)(2,1)S(1)}, u32[]{:S(2)}, u32[]{:S(2)}) collective-permute-start(bf16[256,1024]{1,0:T(8,128)(2,1)S(1)} %slice.129), channel_id=1, source_target_pairs={{0,2},{2,4},{4,6},{6,7},{7,5},{5,3},{3,1},{1,0},{8,10},{10,12},{12... | collective-permute-start | bytes 1572872 | tf_op jit(solution)/shard_map/ppermute | solution.py:44
  37.9 21.5 %collective-permute-start.4 = (bf16[256,1024]{1,0:T(8,128)(2,1)S(1)}, bf16[256,1024]{1,0:T(8,128)(2,1)S(1)}, u32[]{:S(2)}, u32[]{:S(2)}) collective-permute-start(bf16[256,1024]{1,0:T(8,128)(2,1)S(1)} %slice.130), channel_id=1, source_target_pairs={{2,0},{4,2},{6,4},{7,6},{5,7},{3,5},{1,3},{0,1},{10,8},{12,10},{14... | collective-permute-start | bytes 1572872 | tf_op jit(solution)/shard_map/ppermute | solution.py:47
  46.8 31.1 %collective-permute-start.13 = (bf16[512,1024]{1,0:T(8,128)(2,1)}, bf16[512,1024]{1,0:T(8,128)(2,1)}, u32[]{:S(2)}, u32[]{:S(2)}) collective-permute-start(bf16[512,1024]{1,0:T(8,128)(2,1)} %broadcast_select_fusion), channel_id=1, source_target_pairs={{2,3},{3,2},{4,5},{5,4},{10,11},{11,10},{12,13},{13,12},{18,19},{1... | collective-permute-start | bytes 3145736 | tf_op jit(solution)/shard_map/ppermute | solution.py:56
  51.6 11.8 %copy-start.27 = (s32[8]{0:T(128)S(1)}, s32[8]{0:T(128)}, u32[]{:S(2)}) copy-start(s32[8]{0:T(128)} %constant.107.clone) | copy-start | bytes 100
  51.6 17.7 %collective-permute-start.10 = (bf16[256,1024]{1,0:T(8,128)(2,1)}, bf16[256,1024]{1,0:T(8,128)(2,1)}, u32[]{:S(2)}, u32[]{:S(2)}) collective-permute-start(bf16[256,1024]{1,0:T(8,128)(2,1)} %get-tuple-element.207), channel_id=1, source_target_pairs={{0,2},{2,4},{4,6},{6,7},{7,5},{5,3},{3,1},{1,0},{8,10},{10,12},{12... | collective-permute-start | bytes 1572872 | tf_op jit(solution)/shard_map/ppermute | solution.py:44
  58.0 15.2 %collective-permute-start.11 = (bf16[256,1024]{1,0:T(8,128)(2,1)}, bf16[256,1024]{1,0:T(8,128)(2,1)}, u32[]{:S(2)}, u32[]{:S(2)}) collective-permute-start(bf16[256,1024]{1,0:T(8,128)(2,1)} %get-tuple-element.206), channel_id=1, source_target_pairs={{2,0},{4,2},{6,4},{7,6},{5,7},{3,5},{1,3},{0,1},{10,8},{12,10},{14... | collective-permute-start | bytes 1572872 | tf_op jit(solution)/shard_map/ppermute | solution.py:47
  61.3 19.2 %collective-permute-start.8 = (bf16[256,1024]{1,0:T(8,128)(2,1)}, bf16[256,1024]{1,0:T(8,128)(2,1)}, u32[]{:S(2)}, u32[]{:S(2)}) collective-permute-start(bf16[256,1024]{1,0:T(8,128)(2,1)} %get-tuple-element.205), channel_id=1, source_target_pairs={{0,2},{2,4},{4,6},{6,7},{7,5},{5,3},{3,1},{1,0},{8,10},{10,12},{12... | collective-permute-start | bytes 1572872 | tf_op jit(solution)/shard_map/ppermute | solution.py:44
  62.0 22.4 %collective-permute-start.9 = (bf16[256,1024]{1,0:T(8,128)(2,1)}, bf16[256,1024]{1,0:T(8,128)(2,1)}, u32[]{:S(2)}, u32[]{:S(2)}) collective-permute-start(bf16[256,1024]{1,0:T(8,128)(2,1)} %get-tuple-element.204), channel_id=1, source_target_pairs={{2,0},{4,2},{6,4},{7,6},{5,7},{3,5},{1,3},{0,1},{10,8},{12,10},{14... | collective-permute-start | bytes 1572872 | tf_op jit(solution)/shard_map/ppermute | solution.py:47
  75.9 17.5 %collective-permute-start.16 = (bf16[256,1024]{1,0:T(8,128)(2,1)S(1)}, bf16[256,1024]{1,0:T(8,128)(2,1)S(1)}, u32[]{:S(2)}, u32[]{:S(2)}) collective-permute-start(bf16[256,1024]{1,0:T(8,128)(2,1)S(1)} %get-tuple-element.202), channel_id=1, source_target_pairs={{0,2},{2,4},{4,6},{6,7},{7,5},{5,3},{3,1},{1,0},{8,10},{10,12},{12... | collective-permute-start | bytes 1572872 | tf_op jit(solution)/shard_map/ppermute | solution.py:44
  77.5 11.6 %copy-start.19 = (f32[384,1024]{1,0:T(8,128)S(1)}, f32[384,1024]{1,0:T(8,128)}, u32[]{:S(2)}) copy-start(f32[384,1024]{1,0:T(8,128)} %param.16) | copy-start | bytes 4718596
  77.5 11.6 %copy-start.20 = (f32[384,1024]{1,0:T(8,128)S(1)}, f32[384,1024]{1,0:T(8,128)}, u32[]{:S(2)}) copy-start(f32[384,1024]{1,0:T(8,128)} %param.15) | copy-start | bytes 4718596
  77.5 11.6 %copy-start.23 = (bf16[1,384,1024]{2,1,0:T(8,128)(2,1)S(1)}, bf16[1,384,1024]{2,1,0:T(8,128)(2,1)}, u32[]{:S(2)}) copy-start(bf16[1,384,1024]{2,1,0:T(8,128)(2,1)} %param.17) | copy-start | bytes 2359300
  77.5 18.0 %collective-permute-start.17 = (bf16[256,1024]{1,0:T(8,128)(2,1)S(1)}, bf16[256,1024]{1,0:T(8,128)(2,1)S(1)}, u32[]{:S(2)}, u32[]{:S(2)}) collective-permute-start(bf16[256,1024]{1,0:T(8,128)(2,1)S(1)} %get-tuple-element.201), channel_id=1, source_target_pairs={{2,0},{4,2},{6,4},{7,6},{5,7},{3,5},{1,3},{0,1},{10,8},{12,10},{14... | collective-permute-start | bytes 1572872 | tf_op jit(solution)/shard_map/ppermute | solution.py:47
  78.0 41.4 %collective-permute-start.22 = (bf16[512,1024]{1,0:T(8,128)(2,1)S(1)}, bf16[512,1024]{1,0:T(8,128)(2,1)S(1)}, u32[]{:S(2)}, u32[]{:S(2)}) collective-permute-start(bf16[512,1024]{1,0:T(8,128)(2,1)S(1)} %copy-done.22), channel_id=1, source_target_pairs={{2,3},{3,2},{4,5},{5,4},{10,11},{11,10},{12,13},{13,12},{18,19},{1... | collective-permute-start | bytes 3145736 | tf_op jit(solution)/shard_map/ppermute | solution.py:56
  87.0 15.9 %collective-permute-start.14 = (bf16[256,1024]{1,0:T(8,128)(2,1)S(1)}, bf16[256,1024]{1,0:T(8,128)(2,1)S(1)}, u32[]{:S(2)}, u32[]{:S(2)}) collective-permute-start(bf16[256,1024]{1,0:T(8,128)(2,1)S(1)} %get-tuple-element.200), channel_id=1, source_target_pairs={{0,2},{2,4},{4,6},{6,7},{7,5},{5,3},{3,1},{1,0},{8,10},{10,12},{12... | collective-permute-start | bytes 1572872 | tf_op jit(solution)/shard_map/ppermute | solution.py:44
  88.7 18.1 %collective-permute-start.15 = (bf16[256,1024]{1,0:T(8,128)(2,1)S(1)}, bf16[256,1024]{1,0:T(8,128)(2,1)S(1)}, u32[]{:S(2)}, u32[]{:S(2)}) collective-permute-start(bf16[256,1024]{1,0:T(8,128)(2,1)S(1)} %get-tuple-element.199), channel_id=1, source_target_pairs={{2,0},{4,2},{6,4},{7,6},{5,7},{3,5},{1,3},{0,1},{10,8},{12,10},{14... | collective-permute-start | bytes 1572872 | tf_op jit(solution)/shard_map/ppermute | solution.py:47
  89.1 17.6 %copy-start.8 = (bf16[256,1024]{1,0:T(8,128)(2,1)S(1)}, bf16[256,1024]{1,0:T(8,128)(2,1)}, u32[]{:S(2)}) copy-start(bf16[256,1024]{1,0:T(8,128)(2,1)} %copy-done.7) | copy-start | bytes 1572868
  89.1 17.6 %copy-start.10 = (bf16[256,1024]{1,0:T(8,128)(2,1)S(1)}, bf16[256,1024]{1,0:T(8,128)(2,1)}, u32[]{:S(2)}) copy-start(bf16[256,1024]{1,0:T(8,128)(2,1)} %copy-done.9) | copy-start | bytes 1572868
  89.1 17.6 %copy-start.11 = (bf16[512,1024]{1,0:T(8,128)(2,1)S(1)}, bf16[512,1024]{1,0:T(8,128)(2,1)}, u32[]{:S(2)}) copy-start(bf16[512,1024]{1,0:T(8,128)(2,1)} %get-tuple-element.100.kv_grad) | copy-start | bytes 3145732
  89.2 17.6 %copy-start.14 = (f32[512,128]{1,0:T(8,128)S(1)}, f32[512,128]{1,0:T(8,128)}, u32[]{:S(2)}) copy-start(f32[512,128]{1,0:T(8,128)} %get-tuple-element.101.inv) | copy-start | bytes 786436
  93.4 13.4 %copy-start.5 = (bf16[1,512,4096]{2,1,0:T(8,128)(2,1)S(1)}, bf16[1,512,4096]{2,1,0:T(8,128)(2,1)}, u32[]{:S(2)}) copy-start(bf16[1,512,4096]{2,1,0:T(8,128)(2,1)} %param.10) | copy-start | bytes 12582916
  97.6 24.2 %collective-permute-start.20 = (bf16[256,1024]{1,0:T(8,128)(2,1)S(1)}, bf16[256,1024]{1,0:T(8,128)(2,1)S(1)}, u32[]{:S(2)}, u32[]{:S(2)}) collective-permute-start(bf16[256,1024]{1,0:T(8,128)(2,1)S(1)} %get-tuple-element.198), channel_id=1, source_target_pairs={{0,2},{2,4},{4,6},{6,7},{7,5},{5,3},{3,1},{1,0},{8,10},{10,12},{12... | collective-permute-start | bytes 1572872 | tf_op jit(solution)/shard_map/ppermute | solution.py:44
  99.2 22.6 %collective-permute-start.21 = (bf16[256,1024]{1,0:T(8,128)(2,1)S(1)}, bf16[256,1024]{1,0:T(8,128)(2,1)S(1)}, u32[]{:S(2)}, u32[]{:S(2)}) collective-permute-start(bf16[256,1024]{1,0:T(8,128)(2,1)S(1)} %get-tuple-element.197), channel_id=1, source_target_pairs={{2,0},{4,2},{6,4},{7,6},{5,7},{3,5},{1,3},{0,1},{10,8},{12,10},{14... | collective-permute-start | bytes 1572872 | tf_op jit(solution)/shard_map/ppermute | solution.py:47
  102.9 10.1 %copy-start.25 = (bf16[256,1024]{1,0:T(8,128)(2,1)}, bf16[256,1024]{1,0:T(8,128)(2,1)S(1)}, u32[]{:S(2)}) copy-start(bf16[256,1024]{1,0:T(8,128)(2,1)S(1)} %collective-permute-done.14.refs_16_) | copy-start | bytes 1572868
  106.7 6.2 %copy-start.26 = (bf16[256,1024]{1,0:T(8,128)(2,1)}, bf16[256,1024]{1,0:T(8,128)(2,1)S(1)}, u32[]{:S(2)}) copy-start(bf16[256,1024]{1,0:T(8,128)(2,1)S(1)} %collective-permute-done.15.refs_18_) | copy-start | bytes 1572868
  114.9 13.0 %collective-permute-start.18 = (bf16[256,1024]{1,0:T(8,128)(2,1)S(1)}, bf16[256,1024]{1,0:T(8,128)(2,1)S(1)}, u32[]{:S(2)}, u32[]{:S(2)}) collective-permute-start(bf16[256,1024]{1,0:T(8,128)(2,1)S(1)} %get-tuple-element.196), channel_id=1, source_target_pairs={{0,2},{2,4},{4,6},{6,7},{7,5},{5,3},{3,1},{1,0},{8,10},{10,12},{12... | collective-permute-start | bytes 1572872 | tf_op jit(solution)/shard_map/ppermute | solution.py:44
  116.5 14.4 %collective-permute-start.19 = (bf16[256,1024]{1,0:T(8,128)(2,1)S(1)}, bf16[256,1024]{1,0:T(8,128)(2,1)S(1)}, u32[]{:S(2)}, u32[]{:S(2)}) collective-permute-start(bf16[256,1024]{1,0:T(8,128)(2,1)S(1)} %get-tuple-element.195), channel_id=1, source_target_pairs={{2,0},{4,2},{6,4},{7,6},{5,7},{3,5},{1,3},{0,1},{10,8},{12,10},{14... | collective-permute-start | bytes 1572872 | tf_op jit(solution)/shard_map/ppermute | solution.py:47
  119.4 31.7 %collective-permute-start.25 = (bf16[512,1024]{1,0:T(8,128)(2,1)S(1)}, bf16[512,1024]{1,0:T(8,128)(2,1)S(1)}, u32[]{:S(2)}, u32[]{:S(2)}) collective-permute-start(bf16[512,1024]{1,0:T(8,128)(2,1)S(1)} %fusion.10), channel_id=1, source_target_pairs={{2,3},{3,2},{4,5},{5,4},{10,11},{11,10},{12,13},{13,12},{18,19},{1... | collective-permute-start | bytes 3145736 | tf_op jit(solution)/shard_map/ppermute | solution.py:56
  123.9 27.2 %collective-permute-start.26 = (bf16[256,1024]{1,0:T(8,128)(2,1)S(1)}, bf16[256,1024]{1,0:T(8,128)(2,1)S(1)}, u32[]{:S(2)}, u32[]{:S(2)}) collective-permute-start(bf16[256,1024]{1,0:T(8,128)(2,1)S(1)} %get-tuple-element.194), channel_id=1, source_target_pairs={{0,2},{2,4},{4,6},{6,7},{7,5},{5,3},{3,1},{1,0},{8,10},{10,12},{12... | collective-permute-start | bytes 1572872 | tf_op jit(solution)/shard_map/ppermute | solution.py:44
  125.5 9.5 %copy-start.12 = (f32[512,128]{1,0:T(8,128)S(1)}, f32[512,128]{1,0:T(8,128)}, u32[]{:S(2)}) copy-start(f32[512,128]{1,0:T(8,128)} %get-tuple-element.211.cosine) | copy-start | bytes 786436
  125.5 9.5 %copy-start.13 = (f32[512,128]{1,0:T(8,128)S(1)}, f32[512,128]{1,0:T(8,128)}, u32[]{:S(2)}) copy-start(f32[512,128]{1,0:T(8,128)} %get-tuple-element.212.sine) | copy-start | bytes 786436
  125.5 25.6 %collective-permute-start.27 = (bf16[256,1024]{1,0:T(8,128)(2,1)S(1)}, bf16[256,1024]{1,0:T(8,128)(2,1)S(1)}, u32[]{:S(2)}, u32[]{:S(2)}) collective-permute-start(bf16[256,1024]{1,0:T(8,128)(2,1)S(1)} %get-tuple-element.193), channel_id=1, source_target_pairs={{2,0},{4,2},{6,4},{7,6},{5,7},{3,5},{1,3},{0,1},{10,8},{12,10},{14... | collective-permute-start | bytes 1572872 | tf_op jit(solution)/shard_map/ppermute | solution.py:47
  132.9 18.2 %collective-permute-start.23 = (bf16[256,1024]{1,0:T(8,128)(2,1)S(1)}, bf16[256,1024]{1,0:T(8,128)(2,1)S(1)}, u32[]{:S(2)}, u32[]{:S(2)}) collective-permute-start(bf16[256,1024]{1,0:T(8,128)(2,1)S(1)} %get-tuple-element.192), channel_id=1, source_target_pairs={{0,2},{2,4},{4,6},{6,7},{7,5},{5,3},{3,1},{1,0},{8,10},{10,12},{12... | collective-permute-start | bytes 1572872 | tf_op jit(solution)/shard_map/ppermute | solution.py:44
  133.6 17.5 %copy-start.1 = (bf16[1,512,1024]{2,1,0:T(8,128)(2,1)S(1)}, bf16[1,512,1024]{2,1,0:T(8,128)(2,1)}, u32[]{:S(2)}) copy-start(bf16[1,512,1024]{2,1,0:T(8,128)(2,1)} %param.12) | copy-start | bytes 3145732
  133.6 17.5 %copy-start.4 = (f32[512,1024]{1,0:T(8,128)S(1)}, f32[512,1024]{1,0:T(8,128)}, u32[]{:S(2)}) copy-start(f32[512,1024]{1,0:T(8,128)} %get-tuple-element.161.own) | copy-start | bytes 6291460
  133.6 17.5 %copy-start.16 = (bf16[1,512]{1,0:T(2,128)(2,1)S(1)}, bf16[1,512]{1,0:T(2,128)(2,1)}, u32[]{:S(2)}) copy-start(bf16[1,512]{1,0:T(2,128)(2,1)} %gain.5) | copy-start | bytes 3076
  133.7 17.4 %collective-permute-start.24 = (bf16[256,1024]{1,0:T(8,128)(2,1)S(1)}, bf16[256,1024]{1,0:T(8,128)(2,1)S(1)}, u32[]{:S(2)}, u32[]{:S(2)}) collective-permute-start(bf16[256,1024]{1,0:T(8,128)(2,1)S(1)} %get-tuple-element.191), channel_id=1, source_target_pairs={{2,0},{4,2},{6,4},{7,6},{5,7},{3,5},{1,3},{0,1},{10,8},{12,10},{14... | collective-permute-start | bytes 1572872 | tf_op jit(solution)/shard_map/ppermute | solution.py:47
  (9 other events, 21.7 us)

commit v15 on v14

--- a/solution.py
+++ b/solution.py
@@ -93,18 +93,32 @@
     )(weight, gain)
 
 
-def first_kernel(scale, at, x, cotangent, cosine, sine, kv_grad, inv, far, near, last):
+def first_kernel(scale, at, x_in, cotangent, cosine, sine, *refs):
+    kv_out, inv_out, far_out, near, last_out, kv_grad, inv, far, last, x, sem, x_sem = refs
     step = pl.program_id(0)
+    copies = [
+        pltpu.make_async_copy(here, there, sem.at[i])
+        for i, (here, there) in enumerate(
+            ((kv_grad, kv_out), (inv, inv_out), (far, far_out), (last, last_out))
+        )
+    ]
     width = x.shape[1]
     shard = far.shape[0]
     kvw = cotangent.shape[1] // 2
 
     @pl.when(step == 0)
     def _():
+        loads = []
+        for i, c in enumerate(range(0, width, shard)):
+            there = x.at[:, c : c + shard]
+            loads.append(pltpu.make_async_copy(x_in.at[:, c : c + shard], there, x_sem.at[i]))
+            loads[i].start()
         total = jnp.zeros((x.shape[0], HEAD), f32)
-        for c in range(0, width, HEAD):
-            part = x[:, c : c + HEAD].astype(f32)
-            total = total + part * part
+        for i, load in enumerate(loads):
+            load.wait()
+            for c in range(i * shard, (i + 1) * shard, HEAD):
+                part = x[:, c : c + HEAD].astype(f32)
+                total = total + part * part
         mean = jnp.sum(total, axis=1, keepdims=True) / width
         inv[...] = jnp.broadcast_to(lax.rsqrt(mean + epsilon), inv.shape)
         for c in range(0, kvw, HEAD):
@@ -112,6 +126,8 @@
             turned = pltpu.roll(part, HEAD // 2, 1)
             kv_grad[:, c : c + HEAD] = (part * cosine[...] - turned * sine[...]).astype(bf16)
         kv_grad[:, kvw:] = cotangent[:, kvw:]
+        copies[0].start()
+        copies[1].start()
 
     block = x[:, pl.ds(pl.multiple_of(at[step] * shard, shard), shard)]
     normed = (block.astype(f32) * inv[:, :1]).astype(bf16)
@@ -123,6 +139,7 @@
     @pl.when(step == 0)
     def _():
         far[...] = term.astype(bf16)
+        copies[2].start()
 
     @pl.when((step > 0) & (step < pl.num_programs(0) - 1))
     def _():
@@ -131,6 +148,9 @@
     @pl.when(step == pl.num_programs(0) - 1)
     def _():
         last[...] = term
+        copies[3].start()
+        for copy in copies:
+            copy.wait()
 
 
 def first_part(ring, tokens_in, cotangent, cosine, sine, shard, scale):
@@ -142,23 +162,33 @@
     order.append(0)
     n = ring.count
     fixed = lambda k, at: (0, 0)
+    there = pl.BlockSpec(memory_space=pltpu.HBM)
     return pl.pallas_call(
         functools.partial(first_kernel, scale),
         grid_spec=pltpu.PrefetchScalarGridSpec(
             num_scalar_prefetch=1,
             grid=(n,),
             in_specs=[
-                pl.BlockSpec((rows, width), fixed),
+                pl.BlockSpec(memory_space=pl.ANY),
                 pl.BlockSpec((rows, cols), fixed),
                 pl.BlockSpec((rows, HEAD), fixed),
                 pl.BlockSpec((rows, HEAD), fixed),
             ],
             out_specs=[
-                pl.BlockSpec((rows, cols), fixed),
-                pl.BlockSpec((rows, HEAD), fixed),
-                pl.BlockSpec((shard, cols), fixed),
+                there,
+                there,
+                there,
                 pl.BlockSpec((1, shard, cols), lambda k, at: (jnp.clip(k - 1, 0, n - 3), 0, 0)),
-                pl.BlockSpec((shard, cols), fixed),
+                there,
+            ],
+            scratch_shapes=[
+                pltpu.VMEM((rows, cols), bf16),
+                pltpu.VMEM((rows, HEAD), f32),
+                pltpu.VMEM((shard, cols), bf16),
+                pltpu.VMEM((shard, cols), f32),
+                pltpu.VMEM((rows, width), bf16),
+                pltpu.SemaphoreType.DMA((4,)),
+                pltpu.SemaphoreType.DMA((n,)),
             ],
         ),
         out_shape=[

time: 156 us -> 157 us (level)
  no operation moved by 1% of the time
where the time goes in v15:
time: 157 us; the launch traced here: 155 us
  Pallas kernels  42.6 us (27%)
  waiting for transfers between devices  41.5 us (26%)
  starting transfers between devices  34.5 us (22%)
  other arithmetic  30.6 us (19%)
  local copies, waits for them, and re-layouts  4.72 us (3%)
    ppermute x11, waiting for transfers between devices, to_right(): return lax.ppermute(value, 'fsdp', self.right)  23.2 us
    ppermute x11, waiting for transfers between devices, to_left(): return lax.ppermute(value, 'fsdp', self.left)  18.3 us
    pallas_call x1, Pallas kernels, first_part(): pl.pallas_call(functools.partial(first_kernel, scale), grid_spec=pltpu.Pr...  16.9 us
    pallas_call x1, Pallas kernels, late_part(): pl.pallas_call(functools.partial(late_kernel, plan, done), in_specs=[pl.B...  16.1 us
    ppermute x11, starting transfers between devices, to_right(): return lax.ppermute(value, 'fsdp', self.right)  15.5 us
    ppermute x4, starting transfers between devices, over_chord(): return lax.ppermute(value, 'fsdp', [(2, 3), (3, 2), (4, 5), (5, 4)])  10.7 us
    ppermute x11, starting transfers between devices, to_left(): return lax.ppermute(value, 'fsdp', self.left)  6.73 us
    pallas_call x1, Pallas kernels, early_part(): pl.pallas_call(functools.partial(early_kernel, plan), in_specs=[pl.BlockS...  6.14 us
  transfers between devices with their start and end apart: 28, of which 12 were waited for; matrix products, arithmetic and copies ran while one was open for 21% of the time, Pallas kernels for 25%

profile of v15, /device:TPU:8, one launch (start us, length us, event | category | flops | bytes accessed | tf_op | source)
XLA Modules:
  0.0 155.0 jit_solution(3917415666485977168)
XLA Ops:
  0.6 1.2 copy-done
  3.3 1.6 %collective-permute-start.1 = (bf16[512,1024]{1,0:T(8,128)(2,1)S(1)}, bf16[512,1024]{1,0:T(8,128)(2,1)S(1)}, u32[]{:S(2)}, u32[]{:S(2)}) collective-permute-start(bf16[512,1024]{1,0:T(8,128)(2,1)S(1)} %scale_rows.1.refs_0_.refs_2_), channel_id=1, source_target_pairs={{0,2},{2,4},{4,6},{6,7},{7,5},{5,3},{3,1},{1,0},{8,10},{10,12},{12... | collective-permute-start | bytes 3145736 | tf_op jit(solution)/shard_map/ppermute | solution.py:44
  5.4 1.0 convert_element_type.122
  6.4 3.4 %collective-permute-start.12 = (bf16[512,1024]{1,0:T(8,128)(2,1)S(1)}, bf16[512,1024]{1,0:T(8,128)(2,1)}, u32[]{:S(2)}, u32[]{:S(2)}) collective-permute-start(bf16[512,1024]{1,0:T(8,128)(2,1)S(1)} %scale_rows.1.refs_0_.refs_2_), channel_id=1, source_target_pairs={{2,3},{3,2},{4,5},{5,4},{10,11},{11,10},{12,13},{13,12},{18,19},{1... | collective-permute-start | bytes 3145736 | tf_op jit(solution)/shard_map/ppermute | solution.py:56
  9.9 1.0 fusion.23
  11.4 1.0 pad_maximum_fusion
  12.4 2.3 %add_convert_fusion = bf16[384,1024]{1,0:T(8,128)(2,1)} fusion(bf16[384,1024]{1,0:T(8,128)(2,1)} %collective-permute-done, f32[384,1024]{1,0:T(8,128)S(1)} %bitcast.82), kind=kLoop, calls=%fused_computation.7 | loop fusion | flops 1966080 | bytes 3145728 | tf_op jit(solution)/shard_map/convert_element_type | solution.py:489
  14.7 16.9 %norm_and_weight_terms.1 = (bf16[512,1024]{1,0:T(8,128)(2,1)}, f32[512,128]{1,0:T(8,128)}, bf16[512,1024]{1,0:T(8,128)(2,1)}, f32[6,512,1024]{2,1,0:T(8,128)}, f32[512,1024]{1,0:T(8,128)}) custom-call(s32[8]{0:T(128)} %compare_select_fusion.4.at, bf16[512,4096]{1,0:T(8,128)(2,1)} %bitcast.78, bf16[512,1024]{1,0:T(8,128)(2,1)} %bitcast.84, ...), custom_call_target="tpu_custom_call" | custom-call | flops 4294967296 | bytes 20971520 | tf_op jit(solution)/shard_map/norm_and_weight_terms/pallas_call | solution.py:166
  32.6 1.6 %collective-permute-start.5 = (bf16[256,1024]{1,0:T(8,128)(2,1)}, bf16[256,1024]{1,0:T(8,128)(2,1)}, u32[]{:S(2)}, u32[]{:S(2)}) collective-permute-start(bf16[256,1024]{1,0:T(8,128)(2,1)} %slice.127), channel_id=1, source_target_pairs={{0,2},{2,4},{4,6},{6,7},{7,5},{5,3},{3,1},{1,0},{8,10},{10,12},{12... | collective-permute-start | bytes 1572872 | tf_op jit(solution)/shard_map/ppermute | solution.py:44
  35.5 1.5 collective-permute-start.7
  37.1 1.6 %collective-permute-start.3 = (bf16[256,1024]{1,0:T(8,128)(2,1)S(1)}, bf16[256,1024]{1,0:T(8,128)(2,1)S(1)}, u32[]{:S(2)}, u32[]{:S(2)}) collective-permute-start(bf16[256,1024]{1,0:T(8,128)(2,1)S(1)} %slice.129), channel_id=1, source_target_pairs={{0,2},{2,4},{4,6},{6,7},{7,5},{5,3},{3,1},{1,0},{8,10},{10,12},{12... | collective-permute-start | bytes 1572872 | tf_op jit(solution)/shard_map/ppermute | solution.py:44
  39.2 1.1 broadcast_select_fusion
  40.3 7.4 %collective-permute-done.5.refs_3_.refs_5_ = bf16[256,1024]{1,0:T(8,128)(2,1)} collective-permute-done((bf16[256,1024]{1,0:T(8,128)(2,1)}, bf16[256,1024]{1,0:T(8,128)(2,1)}, u32[]{:S(2)}, u32[]{:S(2)}) %collective-permute-start.5) | collective-permute-done | bytes 524320 | tf_op jit(solution)/shard_map/ppermute | solution.py:44
  47.7 2.4 %collective-permute-start.13 = (bf16[512,1024]{1,0:T(8,128)(2,1)}, bf16[512,1024]{1,0:T(8,128)(2,1)}, u32[]{:S(2)}, u32[]{:S(2)}) collective-permute-start(bf16[512,1024]{1,0:T(8,128)(2,1)} %broadcast_select_fusion), channel_id=1, source_target_pairs={{2,3},{3,2},{4,5},{5,4},{10,11},{11,10},{12,13},{13,12},{18,19},{1... | collective-permute-start | bytes 3145736 | tf_op jit(solution)/shard_map/ppermute | solution.py:56
  50.2 2.3 %broadcast_select_fusion.2 = (bf16[256,1024]{1,0:T(8,128)(2,1)}, bf16[256,1024]{1,0:T(8,128)(2,1)}) fusion(bf16[256,1024]{1,0:T(8,128)(2,1)} %collective-permute-done.6.refs_5_.refs_7_, pred[]{:T(512)} %eq.29, bf16[512,1024]{1,0:T(8,128)(2,1)S(1)} %copy-done.21, bf16[256,1024]{1,0:T(8,128)(2,1)} %collective-permute-done.5.refs_3_.refs_5_, pred[]{:T(512)} %eq.30), kind=kLoop, calls=%fused_computation.47 | loop fusion | flops 524288 | bytes 2621442 | tf_op jit(solution)/shard_map/jit(_where)/select_n | solution.py:583
  52.5 1.6 %collective-permute-start.10 = (bf16[256,1024]{1,0:T(8,128)(2,1)}, bf16[256,1024]{1,0:T(8,128)(2,1)}, u32[]{:S(2)}, u32[]{:S(2)}) collective-permute-start(bf16[256,1024]{1,0:T(8,128)(2,1)} %get-tuple-element.207), channel_id=1, source_target_pairs={{0,2},{2,4},{4,6},{6,7},{7,5},{5,3},{3,1},{1,0},{8,10},{10,12},{12... | collective-permute-start | bytes 1572872 | tf_op jit(solution)/shard_map/ppermute | solution.py:44
  54.1 4.8 %collective-permute-done.3.refs_4_.refs_6_ = bf16[256,1024]{1,0:T(8,128)(2,1)S(1)} collective-permute-done((bf16[256,1024]{1,0:T(8,128)(2,1)S(1)}, bf16[256,1024]{1,0:T(8,128)(2,1)S(1)}, u32[]{:S(2)}, u32[]{:S(2)}) %collective-permute-start.3) | collective-permute-done | bytes 524320 | tf_op jit(solution)/shard_map/ppermute | solution.py:44
  58.8 1.4 collective-permute-done.4.refs_6_.refs_8_
  60.3 1.2 broadcast_select_fusion.1
  62.8 1.4 collective-permute-start.9
  64.5 5.7 %collective-permute-done.10.refs_10_ = bf16[256,1024]{1,0:T(8,128)(2,1)} collective-permute-done((bf16[256,1024]{1,0:T(8,128)(2,1)}, bf16[256,1024]{1,0:T(8,128)(2,1)}, u32[]{:S(2)}, u32[]{:S(2)}) %collective-permute-start.10) | collective-permute-done | bytes 524320 | tf_op jit(solution)/shard_map/ppermute | solution.py:44
  70.2 3.8 %collective-permute-done.11.refs_12_ = bf16[256,1024]{1,0:T(8,128)(2,1)} collective-permute-done((bf16[256,1024]{1,0:T(8,128)(2,1)}, bf16[256,1024]{1,0:T(8,128)(2,1)}, u32[]{:S(2)}, u32[]{:S(2)}) %collective-permute-start.11) | collective-permute-done | bytes 524320 | tf_op jit(solution)/shard_map/ppermute | solution.py:47
  74.0 2.7 %fusion.20 = (bf16[256,1024]{1,0:T(8,128)(2,1)S(1)}, bf16[256,1024]{1,0:T(8,128)(2,1)S(1)}) fusion(bf16[256,1024]{1,0:T(8,128)(2,1)} %collective-permute-done.11.refs_12_, f32[6,512,1024]{2,1,0:T(8,128)} %get-tuple-element.132, pred[]{:T(512)} %eq.27, pred[]{:T(512)} %eq.28, bf16[256,1024]{1,0:T(8,128)(2,1)} %collective-permute-done.10.refs_10_), kind=kLoop, calls=%fused_computation.43 | loop fusion | flops 2621440 | bytes 4194306 | tf_op jit(solution)/shard_map/jit(_where)/select_n | solution.py:590
  76.8 1.6 %collective-permute-start.16 = (bf16[256,1024]{1,0:T(8,128)(2,1)S(1)}, bf16[256,1024]{1,0:T(8,128)(2,1)S(1)}, u32[]{:S(2)}, u32[]{:S(2)}) collective-permute-start(bf16[256,1024]{1,0:T(8,128)(2,1)S(1)} %get-tuple-element.202), channel_id=1, source_target_pairs={{0,2},{2,4},{4,6},{6,7},{7,5},{5,3},{3,1},{1,0},{8,10},{10,12},{12... | collective-permute-start | bytes 1572872 | tf_op jit(solution)/shard_map/ppermute | solution.py:44
  78.9 2.4 %collective-permute-start.22 = (bf16[512,1024]{1,0:T(8,128)(2,1)S(1)}, bf16[512,1024]{1,0:T(8,128)(2,1)S(1)}, u32[]{:S(2)}, u32[]{:S(2)}) collective-permute-start(bf16[512,1024]{1,0:T(8,128)(2,1)S(1)} %copy-done.22), channel_id=1, source_target_pairs={{2,3},{3,2},{4,5},{5,4},{10,11},{11,10},{12,13},{13,12},{18,19},{1... | collective-permute-start | bytes 3145736 | tf_op jit(solution)/shard_map/ppermute | solution.py:56
  81.4 3.8 %collective-permute-done.9.refs_13_ = bf16[256,1024]{1,0:T(8,128)(2,1)} collective-permute-done((bf16[256,1024]{1,0:T(8,128)(2,1)}, bf16[256,1024]{1,0:T(8,128)(2,1)}, u32[]{:S(2)}, u32[]{:S(2)}) %collective-permute-start.9) | collective-permute-done | bytes 524320 | tf_op jit(solution)/shard_map/ppermute | solution.py:47
  85.2 2.7 %fusion.22 = (bf16[256,1024]{1,0:T(8,128)(2,1)S(1)}, bf16[256,1024]{1,0:T(8,128)(2,1)S(1)}) fusion(bf16[256,1024]{1,0:T(8,128)(2,1)} %collective-permute-done.9.refs_13_, f32[6,512,1024]{2,1,0:T(8,128)} %get-tuple-element.132, pred[]{:T(512)} %eq.27, pred[]{:T(512)} %eq.28, bf16[256,1024]{1,0:T(8,128)(2,1)} %collective-permute-done.8.refs_11_), kind=kLoop, calls=%fused_computation.45 | loop fusion | flops 2621440 | bytes 4194306 | tf_op jit(solution)/shard_map/jit(_where)/select_n | solution.py:590
  87.9 1.6 %collective-permute-start.14 = (bf16[256,1024]{1,0:T(8,128)(2,1)S(1)}, bf16[256,1024]{1,0:T(8,128)(2,1)S(1)}, u32[]{:S(2)}, u32[]{:S(2)}) collective-permute-start(bf16[256,1024]{1,0:T(8,128)(2,1)S(1)} %get-tuple-element.200), channel_id=1, source_target_pairs={{0,2},{2,4},{4,6},{6,7},{7,5},{5,3},{3,1},{1,0},{8,10},{10,12},{12... | collective-permute-start | bytes 1572872 | tf_op jit(solution)/shard_map/ppermute | solution.py:44
  90.0 4.3 %fusion.1 = (bf16[384,1024]{1,0:T(8,128)(2,1)}, f32[384,1024]{1,0:T(8,128)}, f32[384,1024]{1,0:T(8,128)}) fusion(bf16[1,384,1024]{2,1,0:T(8,128)(2,1)S(1)} %copy-done.23, f32[384,1024]{1,0:T(8,128)S(1)} %copy-done.19, f32[384,1024]{1,0:T(8,128)S(1)} %copy-done.20, bf16[384,1024]{1,0:T(8,128)(2,1)} %collective-permute-done.7, bf16[384,1024]{1,0:T(8,128)(2,1)} %add_convert_fusion), kind=kLoop, calls=%fused_computation.3 | loop fusion | flops 5505024 | bytes 9437184 | tf_op jit(solution)/shard_map/convert_element_type | solution.py:667
  94.3 2.1 %collective-permute-done.17.refs_17_ = bf16[256,1024]{1,0:T(8,128)(2,1)S(1)} collective-permute-done((bf16[256,1024]{1,0:T(8,128)(2,1)S(1)}, bf16[256,1024]{1,0:T(8,128)(2,1)S(1)}, u32[]{:S(2)}, u32[]{:S(2)}) %collective-permute-start.17) | collective-permute-done | bytes 524320 | tf_op jit(solution)/shard_map/ppermute | solution.py:47
  96.4 2.1 %fusion.13 = (bf16[256,1024]{1,0:T(8,128)(2,1)S(1)}, bf16[256,1024]{1,0:T(8,128)(2,1)S(1)}) fusion(bf16[256,1024]{1,0:T(8,128)(2,1)S(1)} %collective-permute-done.17.refs_17_, f32[6,512,1024]{2,1,0:T(8,128)} %get-tuple-element.132, pred[]{:T(512)} %eq.30, bf16[256,1024]{1,0:T(8,128)(2,1)S(1)} %collective-permute-done.16.refs_15_, pred[]{:T(512)} %eq.29), kind=kLoop, calls=%fused_computation.30 | loop fusion | flops 2097152 | bytes 4194306 | tf_op jit(solution)/shard_map/convert_element_type | solution.py:597
  98.5 1.6 %collective-permute-start.20 = (bf16[256,1024]{1,0:T(8,128)(2,1)S(1)}, bf16[256,1024]{1,0:T(8,128)(2,1)S(1)}, u32[]{:S(2)}, u32[]{:S(2)}) collective-permute-start(bf16[256,1024]{1,0:T(8,128)(2,1)S(1)} %get-tuple-element.198), channel_id=1, source_target_pairs={{0,2},{2,4},{4,6},{6,7},{7,5},{5,3},{3,1},{1,0},{8,10},{10,12},{12... | collective-permute-start | bytes 1572872 | tf_op jit(solution)/shard_map/ppermute | solution.py:44
  100.6 3.2 %collective-permute-done.14.refs_16_ = bf16[256,1024]{1,0:T(8,128)(2,1)S(1)} collective-permute-done((bf16[256,1024]{1,0:T(8,128)(2,1)S(1)}, bf16[256,1024]{1,0:T(8,128)(2,1)S(1)}, u32[]{:S(2)}, u32[]{:S(2)}) %collective-permute-start.14) | collective-permute-done | bytes 524320 | tf_op jit(solution)/shard_map/ppermute | solution.py:44
  103.8 3.8 %collective-permute-done.15.refs_18_ = bf16[256,1024]{1,0:T(8,128)(2,1)S(1)} collective-permute-done((bf16[256,1024]{1,0:T(8,128)(2,1)S(1)}, bf16[256,1024]{1,0:T(8,128)(2,1)S(1)}, u32[]{:S(2)}, u32[]{:S(2)}) %collective-permute-start.15) | collective-permute-done | bytes 524320 | tf_op jit(solution)/shard_map/ppermute | solution.py:47
  107.7 6.1 %project_first.1 = (f32[512,128]{1,0:T(8,128)S(1)}, f32[5,512,512]{2,1,0:T(8,128)}) custom-call(s32[15]{0:T(128)S(1)} %pad_add_fusion.at, bf16[512,4096]{1,0:T(8,128)(2,1)S(1)} %bitcast.80, bf16[512,1024]{1,0:T(8,128)(2,1)S(1)} %copy-done.11, f32[512,128]{1,0:T(8,128)S(1)} %copy-done.14, bf16[512,1024]{1,0:T(8,128)(2,1)S(1)} %scale_rows.1.refs_0_.refs_2_, ...), custom_call_target="tpu_custom_call" | custom-call | flops 2684354560 | bytes 13107200 | tf_op jit(solution)/shard_map/project_first/pallas_call | solution.py:424
  113.8 1.9 %fusion.11 = (bf16[256,1024]{1,0:T(8,128)(2,1)S(1)}, bf16[256,1024]{1,0:T(8,128)(2,1)S(1)}) fusion(bf16[256,1024]{1,0:T(8,128)(2,1)S(1)} %collective-permute-done.15.refs_18_, f32[6,512,1024]{2,1,0:T(8,128)} %get-tuple-element.132, pred[]{:T(512)} %eq.30, bf16[256,1024]{1,0:T(8,128)(2,1)S(1)} %collective-permute-done.14.refs_16_, pred[]{:T(512)} %eq.29), kind=kLoop, calls=%fused_computation.25 | loop fusion | flops 2097152 | bytes 4194306 | tf_op jit(solution)/shard_map/convert_element_type | solution.py:597
  115.8 1.6 %collective-permute-start.18 = (bf16[256,1024]{1,0:T(8,128)(2,1)S(1)}, bf16[256,1024]{1,0:T(8,128)(2,1)S(1)}, u32[]{:S(2)}, u32[]{:S(2)}) collective-permute-start(bf16[256,1024]{1,0:T(8,128)(2,1)S(1)} %get-tuple-element.196), channel_id=1, source_target_pairs={{0,2},{2,4},{4,6},{6,7},{7,5},{5,3},{3,1},{1,0},{8,10},{10,12},{12... | collective-permute-start | bytes 1572872 | tf_op jit(solution)/shard_map/ppermute | solution.py:44
  117.9 2.4 %fusion.10 = bf16[512,1024]{1,0:T(8,128)(2,1)S(1)} fusion(f32[6,512,1024]{2,1,0:T(8,128)} %get-tuple-element.132, pred[]{:T(512)} %eq.27), kind=kLoop, calls=%fused_computation.20 | loop fusion | flops 524288 | bytes 3145729 | tf_op jit(solution)/shard_map/convert_element_type | solution.py:566
  120.3 2.4 %collective-permute-start.25 = (bf16[512,1024]{1,0:T(8,128)(2,1)S(1)}, bf16[512,1024]{1,0:T(8,128)(2,1)S(1)}, u32[]{:S(2)}, u32[]{:S(2)}) collective-permute-start(bf16[512,1024]{1,0:T(8,128)(2,1)S(1)} %fusion.10), channel_id=1, source_target_pairs={{2,3},{3,2},{4,5},{5,4},{10,11},{11,10},{12,13},{13,12},{18,19},{1... | collective-permute-start | bytes 3145736 | tf_op jit(solution)/shard_map/ppermute | solution.py:56
  122.8 2.0 %fusion.5 = (bf16[256,1024]{1,0:T(8,128)(2,1)S(1)}, bf16[256,1024]{1,0:T(8,128)(2,1)S(1)}) fusion(bf16[256,1024]{1,0:T(8,128)(2,1)S(1)} %collective-permute-done.21, f32[6,512,1024]{2,1,0:T(8,128)} %get-tuple-element.132, pred[]{:T(512)} %eq.28, bf16[512,1024]{1,0:T(8,128)(2,1)S(1)} %collective-permute-done.22, pred[]{:T(512)} %eq.27, ...), kind=kLoop, calls=%fused_computation.15 | loop fusion | flops 2883584 | bytes 4718594 | tf_op jit(solution)/shard_map/convert_element_type | solution.py:604
  124.8 1.6 %collective-permute-start.26 = (bf16[256,1024]{1,0:T(8,128)(2,1)S(1)}, bf16[256,1024]{1,0:T(8,128)(2,1)S(1)}, u32[]{:S(2)}, u32[]{:S(2)}) collective-permute-start(bf16[256,1024]{1,0:T(8,128)(2,1)S(1)} %get-tuple-element.194), channel_id=1, source_target_pairs={{0,2},{2,4},{4,6},{6,7},{7,5},{5,3},{3,1},{1,0},{8,10},{10,12},{12... | collective-permute-start | bytes 1572872 | tf_op jit(solution)/shard_map/ppermute | solution.py:44
  126.9 1.9 %collective-permute-done.18 = bf16[256,1024]{1,0:T(8,128)(2,1)S(1)} collective-permute-done((bf16[256,1024]{1,0:T(8,128)(2,1)S(1)}, bf16[256,1024]{1,0:T(8,128)(2,1)S(1)}, u32[]{:S(2)}, u32[]{:S(2)}) %collective-permute-start.18) | collective-permute-done | bytes 524320 | tf_op jit(solution)/shard_map/ppermute | solution.py:44
  128.8 3.3 %collective-permute-done.19 = bf16[256,1024]{1,0:T(8,128)(2,1)S(1)} collective-permute-done((bf16[256,1024]{1,0:T(8,128)(2,1)S(1)}, bf16[256,1024]{1,0:T(8,128)(2,1)S(1)}, u32[]{:S(2)}, u32[]{:S(2)}) %collective-permute-start.19) | collective-permute-done | bytes 524320 | tf_op jit(solution)/shard_map/ppermute | solution.py:47
  132.1 2.0 %fusion.9 = (bf16[256,1024]{1,0:T(8,128)(2,1)S(1)}, bf16[256,1024]{1,0:T(8,128)(2,1)S(1)}) fusion(bf16[256,1024]{1,0:T(8,128)(2,1)S(1)} %collective-permute-done.19, f32[6,512,1024]{2,1,0:T(8,128)} %get-tuple-element.132, pred[]{:T(512)} %eq.28, bf16[512,1024]{1,0:T(8,128)(2,1)S(1)} %collective-permute-done.22, pred[]{:T(512)} %eq.27, ...), kind=kLoop, calls=%fused_computation.19 | loop fusion | flops 2883584 | bytes 4718594 | tf_op jit(solution)/shard_map/convert_element_type | solution.py:604
  134.4 1.7 %collective-permute-start.24 = (bf16[256,1024]{1,0:T(8,128)(2,1)S(1)}, bf16[256,1024]{1,0:T(8,128)(2,1)S(1)}, u32[]{:S(2)}, u32[]{:S(2)}) collective-permute-start(bf16[256,1024]{1,0:T(8,128)(2,1)S(1)} %get-tuple-element.191), channel_id=1, source_target_pairs={{2,0},{4,2},{6,4},{7,6},{5,7},{3,5},{1,3},{0,1},{10,8},{12,10},{14... | collective-permute-start | bytes 1572872 | tf_op jit(solution)/shard_map/ppermute | solution.py:47
  136.2 16.1 %project_last.1 = (bf16[512,1024]{1,0:T(8,128)(2,1)}, bf16[512,4096]{1,0:T(8,128)(2,1)}) custom-call(s32[15]{0:T(128)S(1)} %pad_add_fusion.at, bf16[512,4096]{1,0:T(8,128)(2,1)} %bitcast.79, bf16[512,1024]{1,0:T(8,128)(2,1)} %get-tuple-element.100.kv_grad, f32[512,128]{1,0:T(8,128)S(1)} %copy-done.14, f32[512,128]{1,0:T(8,128)S(1)} %copy-done.12, ...), custom_call_target="tpu_custom_call" | custom-call | flops 8589934592 | bytes 16777216 | tf_op jit(solution)/shard_map/project_last/pallas_call | solution.py:457
  152.3 1.4 sum_of_terms.2
  153.7 1.3 sum_of_terms.3
  (98 shorter events, 9.6 us)
Async XLA Ops:
  3.3 104.3 %copy-start.6 = (bf16[512,1024]{1,0:T(8,128)(2,1)}, bf16[512,1024]{1,0:T(8,128)(2,1)S(1)}, u32[]{:S(2)}) copy-start(bf16[512,1024]{1,0:T(8,128)(2,1)S(1)} %scale_rows.1.refs_0_.refs_2_) | copy-start | bytes 3145732
  3.3 28.4 %collective-permute-start.1 = (bf16[512,1024]{1,0:T(8,128)(2,1)S(1)}, bf16[512,1024]{1,0:T(8,128)(2,1)S(1)}, u32[]{:S(2)}, u32[]{:S(2)}) collective-permute-start(bf16[512,1024]{1,0:T(8,128)(2,1)S(1)} %scale_rows.1.refs_0_.refs_2_), channel_id=1, source_target_pairs={{0,2},{2,4},{4,6},{6,7},{7,5},{5,3},{3,1},{1,0},{8,10},{10,12},{12... | collective-permute-start | bytes 3145736 | tf_op jit(solution)/shard_map/ppermute | solution.py:44
  4.9 26.8 %collective-permute-start.2 = (bf16[512,1024]{1,0:T(8,128)(2,1)S(1)}, bf16[512,1024]{1,0:T(8,128)(2,1)S(1)}, u32[]{:S(2)}, u32[]{:S(2)}) collective-permute-start(bf16[512,1024]{1,0:T(8,128)(2,1)S(1)} %scale_rows.1.refs_0_.refs_2_), channel_id=1, source_target_pairs={{2,0},{4,2},{6,4},{7,6},{5,7},{3,5},{1,3},{0,1},{10,8},{12,10},{14... | collective-permute-start | bytes 3145736 | tf_op jit(solution)/shard_map/ppermute | solution.py:47
  6.4 6.0 %collective-permute-start = (bf16[384,1024]{1,0:T(8,128)(2,1)}, bf16[384,1024]{1,0:T(8,128)(2,1)}, u32[]{:S(2)}, u32[]{:S(2)}) collective-permute-start(bf16[384,1024]{1,0:T(8,128)(2,1)} %convert_element_type.122), channel_id=1, source_target_pairs={{0,8},{8,0},{16,24},{24,16},{1,9},{9,1},{17,25},{25,17},{2,10},{10... | collective-permute-start | bytes 2359304 | tf_op jit(solution)/shard_map/ppermute | solution.py:493
  6.4 32.3 %collective-permute-start.12 = (bf16[512,1024]{1,0:T(8,128)(2,1)S(1)}, bf16[512,1024]{1,0:T(8,128)(2,1)}, u32[]{:S(2)}, u32[]{:S(2)}) collective-permute-start(bf16[512,1024]{1,0:T(8,128)(2,1)S(1)} %scale_rows.1.refs_0_.refs_2_), channel_id=1, source_target_pairs={{2,3},{3,2},{4,5},{5,4},{10,11},{11,10},{12,13},{13,12},{18,19},{1... | collective-permute-start | bytes 3145736 | tf_op jit(solution)/shard_map/ppermute | solution.py:56
  31.7 75.9 %copy-start.2 = (bf16[512,1024]{1,0:T(8,128)(2,1)}, bf16[512,1024]{1,0:T(8,128)(2,1)S(1)}, u32[]{:S(2)}) copy-start(bf16[512,1024]{1,0:T(8,128)(2,1)S(1)} %collective-permute-done.1.refs_1_.refs_3_) | copy-start | bytes 3145732
  31.7 75.9 %copy-start.3 = (bf16[512,1024]{1,0:T(8,128)(2,1)}, bf16[512,1024]{1,0:T(8,128)(2,1)S(1)}, u32[]{:S(2)}) copy-start(bf16[512,1024]{1,0:T(8,128)(2,1)S(1)} %collective-permute-done.2.refs_2_.refs_4_) | copy-start | bytes 3145732
  32.6 15.1 %collective-permute-start.5 = (bf16[256,1024]{1,0:T(8,128)(2,1)}, bf16[256,1024]{1,0:T(8,128)(2,1)}, u32[]{:S(2)}, u32[]{:S(2)}) collective-permute-start(bf16[256,1024]{1,0:T(8,128)(2,1)} %slice.127), channel_id=1, source_target_pairs={{0,2},{2,4},{4,6},{6,7},{7,5},{5,3},{3,1},{1,0},{8,10},{10,12},{12... | collective-permute-start | bytes 1572872 | tf_op jit(solution)/shard_map/ppermute | solution.py:44
  35.0 15.1 %collective-permute-start.6 = (bf16[256,1024]{1,0:T(8,128)(2,1)}, bf16[256,1024]{1,0:T(8,128)(2,1)}, u32[]{:S(2)}, u32[]{:S(2)}) collective-permute-start(bf16[256,1024]{1,0:T(8,128)(2,1)} %slice.128), channel_id=1, source_target_pairs={{2,0},{4,2},{6,4},{7,6},{5,7},{3,5},{1,3},{0,1},{10,8},{12,10},{14... | collective-permute-start | bytes 1572872 | tf_op jit(solution)/shard_map/ppermute | solution.py:47
  35.5 24.8 %collective-permute-start.7 = (bf16[384,1024]{1,0:T(8,128)(2,1)}, bf16[384,1024]{1,0:T(8,128)(2,1)}, u32[]{:S(2)}, u32[]{:S(2)}) collective-permute-start(bf16[384,1024]{1,0:T(8,128)(2,1)} %add_convert_fusion), channel_id=1, source_target_pairs={{0,16},{8,24},{16,0},{24,8},{1,17},{9,25},{17,1},{25,9},{2,18},{10... | collective-permute-start | bytes 2359304 | tf_op jit(solution)/shard_map/ppermute | solution.py:493
  37.1 13.1 %copy-start.21 = (bf16[512,1024]{1,0:T(8,128)(2,1)S(1)}, bf16[512,1024]{1,0:T(8,128)(2,1)}, u32[]{:S(2)}) copy-start(bf16[512,1024]{1,0:T(8,128)(2,1)} %get-tuple-element.171) | copy-start | bytes 3145732
  37.1 21.7 %collective-permute-start.3 = (bf16[256,1024]{1,0:T(8,128)(2,1)S(1)}, bf16[256,1024]{1,0:T(8,128)(2,1)S(1)}, u32[]{:S(2)}, u32[]{:S(2)}) collective-permute-start(bf16[256,1024]{1,0:T(8,128)(2,1)S(1)} %slice.129), channel_id=1, source_target_pairs={{0,2},{2,4},{4,6},{6,7},{7,5},{5,3},{3,1},{1,0},{8,10},{10,12},{12... | collective-permute-start | bytes 1572872 | tf_op jit(solution)/shard_map/ppermute | solution.py:44
  38.7 21.5 %collective-permute-start.4 = (bf16[256,1024]{1,0:T(8,128)(2,1)S(1)}, bf16[256,1024]{1,0:T(8,128)(2,1)S(1)}, u32[]{:S(2)}, u32[]{:S(2)}) collective-permute-start(bf16[256,1024]{1,0:T(8,128)(2,1)S(1)} %slice.130), channel_id=1, source_target_pairs={{2,0},{4,2},{6,4},{7,6},{5,7},{3,5},{1,3},{0,1},{10,8},{12,10},{14... | collective-permute-start | bytes 1572872 | tf_op jit(solution)/shard_map/ppermute | solution.py:47
  47.7 31.1 %collective-permute-start.13 = (bf16[512,1024]{1,0:T(8,128)(2,1)}, bf16[512,1024]{1,0:T(8,128)(2,1)}, u32[]{:S(2)}, u32[]{:S(2)}) collective-permute-start(bf16[512,1024]{1,0:T(8,128)(2,1)} %broadcast_select_fusion), channel_id=1, source_target_pairs={{2,3},{3,2},{4,5},{5,4},{10,11},{11,10},{12,13},{13,12},{18,19},{1... | collective-permute-start | bytes 3145736 | tf_op jit(solution)/shard_map/ppermute | solution.py:56
  52.5 11.8 %copy-start.27 = (s32[8]{0:T(128)S(1)}, s32[8]{0:T(128)}, u32[]{:S(2)}) copy-start(s32[8]{0:T(128)} %constant.107.clone) | copy-start | bytes 100
  52.5 17.7 %collective-permute-start.10 = (bf16[256,1024]{1,0:T(8,128)(2,1)}, bf16[256,1024]{1,0:T(8,128)(2,1)}, u32[]{:S(2)}, u32[]{:S(2)}) collective-permute-start(bf16[256,1024]{1,0:T(8,128)(2,1)} %get-tuple-element.207), channel_id=1, source_target_pairs={{0,2},{2,4},{4,6},{6,7},{7,5},{5,3},{3,1},{1,0},{8,10},{10,12},{12... | collective-permute-start | bytes 1572872 | tf_op jit(solution)/shard_map/ppermute | solution.py:44
  58.8 15.2 %collective-permute-start.11 = (bf16[256,1024]{1,0:T(8,128)(2,1)}, bf16[256,1024]{1,0:T(8,128)(2,1)}, u32[]{:S(2)}, u32[]{:S(2)}) collective-permute-start(bf16[256,1024]{1,0:T(8,128)(2,1)} %get-tuple-element.206), channel_id=1, source_target_pairs={{2,0},{4,2},{6,4},{7,6},{5,7},{3,5},{1,3},{0,1},{10,8},{12,10},{14... | collective-permute-start | bytes 1572872 | tf_op jit(solution)/shard_map/ppermute | solution.py:47
  62.2 19.2 %collective-permute-start.8 = (bf16[256,1024]{1,0:T(8,128)(2,1)}, bf16[256,1024]{1,0:T(8,128)(2,1)}, u32[]{:S(2)}, u32[]{:S(2)}) collective-permute-start(bf16[256,1024]{1,0:T(8,128)(2,1)} %get-tuple-element.205), channel_id=1, source_target_pairs={{0,2},{2,4},{4,6},{6,7},{7,5},{5,3},{3,1},{1,0},{8,10},{10,12},{12... | collective-permute-start | bytes 1572872 | tf_op jit(solution)/shard_map/ppermute | solution.py:44
  62.8 22.4 %collective-permute-start.9 = (bf16[256,1024]{1,0:T(8,128)(2,1)}, bf16[256,1024]{1,0:T(8,128)(2,1)}, u32[]{:S(2)}, u32[]{:S(2)}) collective-permute-start(bf16[256,1024]{1,0:T(8,128)(2,1)} %get-tuple-element.204), channel_id=1, source_target_pairs={{2,0},{4,2},{6,4},{7,6},{5,7},{3,5},{1,3},{0,1},{10,8},{12,10},{14... | collective-permute-start | bytes 1572872 | tf_op jit(solution)/shard_map/ppermute | solution.py:47
  76.8 17.5 %collective-permute-start.16 = (bf16[256,1024]{1,0:T(8,128)(2,1)S(1)}, bf16[256,1024]{1,0:T(8,128)(2,1)S(1)}, u32[]{:S(2)}, u32[]{:S(2)}) collective-permute-start(bf16[256,1024]{1,0:T(8,128)(2,1)S(1)} %get-tuple-element.202), channel_id=1, source_target_pairs={{0,2},{2,4},{4,6},{6,7},{7,5},{5,3},{3,1},{1,0},{8,10},{10,12},{12... | collective-permute-start | bytes 1572872 | tf_op jit(solution)/shard_map/ppermute | solution.py:44
  78.4 11.6 %copy-start.19 = (f32[384,1024]{1,0:T(8,128)S(1)}, f32[384,1024]{1,0:T(8,128)}, u32[]{:S(2)}) copy-start(f32[384,1024]{1,0:T(8,128)} %param.16) | copy-start | bytes 4718596
  78.4 11.6 %copy-start.20 = (f32[384,1024]{1,0:T(8,128)S(1)}, f32[384,1024]{1,0:T(8,128)}, u32[]{:S(2)}) copy-start(f32[384,1024]{1,0:T(8,128)} %param.15) | copy-start | bytes 4718596
  78.4 11.6 %copy-start.23 = (bf16[1,384,1024]{2,1,0:T(8,128)(2,1)S(1)}, bf16[1,384,1024]{2,1,0:T(8,128)(2,1)}, u32[]{:S(2)}) copy-start(bf16[1,384,1024]{2,1,0:T(8,128)(2,1)} %param.17) | copy-start | bytes 2359300
  78.4 18.0 %collective-permute-start.17 = (bf16[256,1024]{1,0:T(8,128)(2,1)S(1)}, bf16[256,1024]{1,0:T(8,128)(2,1)S(1)}, u32[]{:S(2)}, u32[]{:S(2)}) collective-permute-start(bf16[256,1024]{1,0:T(8,128)(2,1)S(1)} %get-tuple-element.201), channel_id=1, source_target_pairs={{2,0},{4,2},{6,4},{7,6},{5,7},{3,5},{1,3},{0,1},{10,8},{12,10},{14... | collective-permute-start | bytes 1572872 | tf_op jit(solution)/shard_map/ppermute | solution.py:47
  78.9 41.4 %collective-permute-start.22 = (bf16[512,1024]{1,0:T(8,128)(2,1)S(1)}, bf16[512,1024]{1,0:T(8,128)(2,1)S(1)}, u32[]{:S(2)}, u32[]{:S(2)}) collective-permute-start(bf16[512,1024]{1,0:T(8,128)(2,1)S(1)} %copy-done.22), channel_id=1, source_target_pairs={{2,3},{3,2},{4,5},{5,4},{10,11},{11,10},{12,13},{13,12},{18,19},{1... | collective-permute-start | bytes 3145736 | tf_op jit(solution)/shard_map/ppermute | solution.py:56
  87.9 15.9 %collective-permute-start.14 = (bf16[256,1024]{1,0:T(8,128)(2,1)S(1)}, bf16[256,1024]{1,0:T(8,128)(2,1)S(1)}, u32[]{:S(2)}, u32[]{:S(2)}) collective-permute-start(bf16[256,1024]{1,0:T(8,128)(2,1)S(1)} %get-tuple-element.200), channel_id=1, source_target_pairs={{0,2},{2,4},{4,6},{6,7},{7,5},{5,3},{3,1},{1,0},{8,10},{10,12},{12... | collective-permute-start | bytes 1572872 | tf_op jit(solution)/shard_map/ppermute | solution.py:44
  89.6 18.1 %collective-permute-start.15 = (bf16[256,1024]{1,0:T(8,128)(2,1)S(1)}, bf16[256,1024]{1,0:T(8,128)(2,1)S(1)}, u32[]{:S(2)}, u32[]{:S(2)}) collective-permute-start(bf16[256,1024]{1,0:T(8,128)(2,1)S(1)} %get-tuple-element.199), channel_id=1, source_target_pairs={{2,0},{4,2},{6,4},{7,6},{5,7},{3,5},{1,3},{0,1},{10,8},{12,10},{14... | collective-permute-start | bytes 1572872 | tf_op jit(solution)/shard_map/ppermute | solution.py:47
  90.0 17.6 %copy-start.8 = (bf16[256,1024]{1,0:T(8,128)(2,1)S(1)}, bf16[256,1024]{1,0:T(8,128)(2,1)}, u32[]{:S(2)}) copy-start(bf16[256,1024]{1,0:T(8,128)(2,1)} %copy-done.7) | copy-start | bytes 1572868
  90.0 17.6 %copy-start.10 = (bf16[256,1024]{1,0:T(8,128)(2,1)S(1)}, bf16[256,1024]{1,0:T(8,128)(2,1)}, u32[]{:S(2)}) copy-start(bf16[256,1024]{1,0:T(8,128)(2,1)} %copy-done.9) | copy-start | bytes 1572868
  90.0 17.6 %copy-start.11 = (bf16[512,1024]{1,0:T(8,128)(2,1)S(1)}, bf16[512,1024]{1,0:T(8,128)(2,1)}, u32[]{:S(2)}) copy-start(bf16[512,1024]{1,0:T(8,128)(2,1)} %get-tuple-element.100.kv_grad) | copy-start | bytes 3145732
  90.0 17.6 %copy-start.14 = (f32[512,128]{1,0:T(8,128)S(1)}, f32[512,128]{1,0:T(8,128)}, u32[]{:S(2)}) copy-start(f32[512,128]{1,0:T(8,128)} %get-tuple-element.101.inv) | copy-start | bytes 786436
  94.3 13.4 %copy-start.5 = (bf16[1,512,4096]{2,1,0:T(8,128)(2,1)S(1)}, bf16[1,512,4096]{2,1,0:T(8,128)(2,1)}, u32[]{:S(2)}) copy-start(bf16[1,512,4096]{2,1,0:T(8,128)(2,1)} %param.10) | copy-start | bytes 12582916
  98.5 24.2 %collective-permute-start.20 = (bf16[256,1024]{1,0:T(8,128)(2,1)S(1)}, bf16[256,1024]{1,0:T(8,128)(2,1)S(1)}, u32[]{:S(2)}, u32[]{:S(2)}) collective-permute-start(bf16[256,1024]{1,0:T(8,128)(2,1)S(1)} %get-tuple-element.198), channel_id=1, source_target_pairs={{0,2},{2,4},{4,6},{6,7},{7,5},{5,3},{3,1},{1,0},{8,10},{10,12},{12... | collective-permute-start | bytes 1572872 | tf_op jit(solution)/shard_map/ppermute | solution.py:44
  100.1 22.6 %collective-permute-start.21 = (bf16[256,1024]{1,0:T(8,128)(2,1)S(1)}, bf16[256,1024]{1,0:T(8,128)(2,1)S(1)}, u32[]{:S(2)}, u32[]{:S(2)}) collective-permute-start(bf16[256,1024]{1,0:T(8,128)(2,1)S(1)} %get-tuple-element.197), channel_id=1, source_target_pairs={{2,0},{4,2},{6,4},{7,6},{5,7},{3,5},{1,3},{0,1},{10,8},{12,10},{14... | collective-permute-start | bytes 1572872 | tf_op jit(solution)/shard_map/ppermute | solution.py:47
  103.8 10.1 %copy-start.25 = (bf16[256,1024]{1,0:T(8,128)(2,1)}, bf16[256,1024]{1,0:T(8,128)(2,1)S(1)}, u32[]{:S(2)}) copy-start(bf16[256,1024]{1,0:T(8,128)(2,1)S(1)} %collective-permute-done.14.refs_16_) | copy-start | bytes 1572868
  107.6 6.2 %copy-start.26 = (bf16[256,1024]{1,0:T(8,128)(2,1)}, bf16[256,1024]{1,0:T(8,128)(2,1)S(1)}, u32[]{:S(2)}) copy-start(bf16[256,1024]{1,0:T(8,128)(2,1)S(1)} %collective-permute-done.15.refs_18_) | copy-start | bytes 1572868
  115.8 13.0 %collective-permute-start.18 = (bf16[256,1024]{1,0:T(8,128)(2,1)S(1)}, bf16[256,1024]{1,0:T(8,128)(2,1)S(1)}, u32[]{:S(2)}, u32[]{:S(2)}) collective-permute-start(bf16[256,1024]{1,0:T(8,128)(2,1)S(1)} %get-tuple-element.196), channel_id=1, source_target_pairs={{0,2},{2,4},{4,6},{6,7},{7,5},{5,3},{3,1},{1,0},{8,10},{10,12},{12... | collective-permute-start | bytes 1572872 | tf_op jit(solution)/shard_map/ppermute | solution.py:44
  117.4 14.6 %collective-permute-start.19 = (bf16[256,1024]{1,0:T(8,128)(2,1)S(1)}, bf16[256,1024]{1,0:T(8,128)(2,1)S(1)}, u32[]{:S(2)}, u32[]{:S(2)}) collective-permute-start(bf16[256,1024]{1,0:T(8,128)(2,1)S(1)} %get-tuple-element.195), channel_id=1, source_target_pairs={{2,0},{4,2},{6,4},{7,6},{5,7},{3,5},{1,3},{0,1},{10,8},{12,10},{14... | collective-permute-start | bytes 1572872 | tf_op jit(solution)/shard_map/ppermute | solution.py:47
  120.3 32.0 %collective-permute-start.25 = (bf16[512,1024]{1,0:T(8,128)(2,1)S(1)}, bf16[512,1024]{1,0:T(8,128)(2,1)S(1)}, u32[]{:S(2)}, u32[]{:S(2)}) collective-permute-start(bf16[512,1024]{1,0:T(8,128)(2,1)S(1)} %fusion.10), channel_id=1, source_target_pairs={{2,3},{3,2},{4,5},{5,4},{10,11},{11,10},{12,13},{13,12},{18,19},{1... | collective-permute-start | bytes 3145736 | tf_op jit(solution)/shard_map/ppermute | solution.py:56
  124.8 27.5 %collective-permute-start.26 = (bf16[256,1024]{1,0:T(8,128)(2,1)S(1)}, bf16[256,1024]{1,0:T(8,128)(2,1)S(1)}, u32[]{:S(2)}, u32[]{:S(2)}) collective-permute-start(bf16[256,1024]{1,0:T(8,128)(2,1)S(1)} %get-tuple-element.194), channel_id=1, source_target_pairs={{0,2},{2,4},{4,6},{6,7},{7,5},{5,3},{3,1},{1,0},{8,10},{10,12},{12... | collective-permute-start | bytes 1572872 | tf_op jit(solution)/shard_map/ppermute | solution.py:44
  126.4 9.8 %copy-start.12 = (f32[512,128]{1,0:T(8,128)S(1)}, f32[512,128]{1,0:T(8,128)}, u32[]{:S(2)}) copy-start(f32[512,128]{1,0:T(8,128)} %get-tuple-element.211.cosine) | copy-start | bytes 786436
  126.4 9.8 %copy-start.13 = (f32[512,128]{1,0:T(8,128)S(1)}, f32[512,128]{1,0:T(8,128)}, u32[]{:S(2)}) copy-start(f32[512,128]{1,0:T(8,128)} %get-tuple-element.212.sine) | copy-start | bytes 786436
  126.4 25.8 %collective-permute-start.27 = (bf16[256,1024]{1,0:T(8,128)(2,1)S(1)}, bf16[256,1024]{1,0:T(8,128)(2,1)S(1)}, u32[]{:S(2)}, u32[]{:S(2)}) collective-permute-start(bf16[256,1024]{1,0:T(8,128)(2,1)S(1)} %get-tuple-element.193), channel_id=1, source_target_pairs={{2,0},{4,2},{6,4},{7,6},{5,7},{3,5},{1,3},{0,1},{10,8},{12,10},{14... | collective-permute-start | bytes 1572872 | tf_op jit(solution)/shard_map/ppermute | solution.py:47
  134.1 18.2 %collective-permute-start.23 = (bf16[256,1024]{1,0:T(8,128)(2,1)S(1)}, bf16[256,1024]{1,0:T(8,128)(2,1)S(1)}, u32[]{:S(2)}, u32[]{:S(2)}) collective-permute-start(bf16[256,1024]{1,0:T(8,128)(2,1)S(1)} %get-tuple-element.192), channel_id=1, source_target_pairs={{0,2},{2,4},{4,6},{6,7},{7,5},{5,3},{3,1},{1,0},{8,10},{10,12},{12... | collective-permute-start | bytes 1572872 | tf_op jit(solution)/shard_map/ppermute | solution.py:44
  134.4 17.9 %copy-start.1 = (bf16[1,512,1024]{2,1,0:T(8,128)(2,1)S(1)}, bf16[1,512,1024]{2,1,0:T(8,128)(2,1)}, u32[]{:S(2)}) copy-start(bf16[1,512,1024]{2,1,0:T(8,128)(2,1)} %param.12) | copy-start | bytes 3145732
  134.4 17.9 %copy-start.4 = (f32[512,1024]{1,0:T(8,128)S(1)}, f32[512,1024]{1,0:T(8,128)}, u32[]{:S(2)}) copy-start(f32[512,1024]{1,0:T(8,128)} %get-tuple-element.161.own) | copy-start | bytes 6291460
  134.4 17.9 %copy-start.16 = (bf16[1,512]{1,0:T(2,128)(2,1)S(1)}, bf16[1,512]{1,0:T(2,128)(2,1)}, u32[]{:S(2)}) copy-start(bf16[1,512]{1,0:T(2,128)(2,1)} %gain.5) | copy-start | bytes 3076
  134.4 17.8 %collective-permute-start.24 = (bf16[256,1024]{1,0:T(8,128)(2,1)S(1)}, bf16[256,1024]{1,0:T(8,128)(2,1)S(1)}, u32[]{:S(2)}, u32[]{:S(2)}) collective-permute-start(bf16[256,1024]{1,0:T(8,128)(2,1)S(1)} %get-tuple-element.191), channel_id=1, source_target_pairs={{2,0},{4,2},{6,4},{7,6},{5,7},{3,5},{1,3},{0,1},{10,8},{12,10},{14... | collective-permute-start | bytes 1572872 | tf_op jit(solution)/shard_map/ppermute | solution.py:47
  (9 other events, 21.7 us)

commit v16 on v13

--- a/solution.py
+++ b/solution.py
@@ -491,7 +491,7 @@
     return late(blocks, plan), sums, update(total)
 
 
-ORDER = {"sum": (-1, 3), "pair": (-1, 4), "inner": (4, None), "far": (1, 5), "partner": (7, None), "first": (6, 7), "update": (4, 7)}
+ORDER = {"sum": (-1, 1), "pair": (-1, 3), "inner": (2, 7), "far": (1, 5), "partner": (7, None), "first": (2, 3), "update": (5, 9)}
 CHAIN = True
 
 

time: 155 us -> 154 us (level)
  starting transfers between devices: 34.5 us -> 40.2 us
  other arithmetic: 30.1 us -> 25.2 us
  waiting for transfers between devices: 41.5 us -> 38.5 us
    ppermute x11, waiting for transfers between devices: 23.2 us -> 1.42 us  [to_right(): return lax.ppermute(value, 'fsdp', self.right)]
    ppermute x11, waiting for transfers between devices: 18.3 us -> 35 us  [to_left(): return lax.ppermute(value, 'fsdp', self.left)]
    ppermute x4, starting transfers between devices: 10.7 us -> 15.9 us  [over_chord(): return lax.ppermute(value, 'fsdp', [(2, 3), (3, 2), (4, 5), (5, 4)])]
    ppermute x11, starting transfers between devices: 5.94 us -> 10 us  [to_left(): return lax.ppermute(value, 'fsdp', self.left)]
    ppermute x11, starting transfers between devices: 16.3 us -> 12.8 us  [to_right(): return lax.ppermute(value, 'fsdp', self.right)]
    select_n x2, other arithmetic: 3.51 us -> 1.44 us  [exchange_plane(): three.append(ring(2 + h, pick(at0, terms, left), pick(at3, terms, right)))]
    ppermute x4, waiting for transfers between devices: 0.01 us -> 2.07 us  [over_chord(): return lax.ppermute(value, 'fsdp', [(2, 3), (3, 2), (4, 5), (5, 4)])]
    unnamed x68 -> x60, local copies, waits for them, and re-layouts: 6.74 us -> 6.59 us
  transfers between devices with their start and end apart: 28 -> 28, of which waited for: 12 -> 15; matrix products, arithmetic and copies ran while one was open for 21% -> 17% of each run, Pallas kernels for 22% -> 23%
where the time goes in v16:
time: 154 us; the launch traced here: 151 us
  starting transfers between devices  40.2 us (26%)
  waiting for transfers between devices  38.5 us (25%)
  Pallas kernels  37.6 us (24%)
  other arithmetic  25.2 us (16%)
  local copies, waits for them, and re-layouts  8.42 us (5%)
    ppermute x11, waiting for transfers between devices, to_left(): return lax.ppermute(value, 'fsdp', self.left)  35 us
    pallas_call x1, Pallas kernels, late_part(): pl.pallas_call(functools.partial(late_kernel, plan, done), in_specs=[pl.B...  16 us
    ppermute x4, starting transfers between devices, over_chord(): return lax.ppermute(value, 'fsdp', [(2, 3), (3, 2), (4, 5), (5, 4)])  15.9 us
    ppermute x11, starting transfers between devices, to_right(): return lax.ppermute(value, 'fsdp', self.right)  12.8 us
    pallas_call x1, Pallas kernels, first_part(): pl.pallas_call(functools.partial(first_kernel, scale), grid_spec=pltpu.Pr...  12.1 us
    ppermute x11, starting transfers between devices, to_left(): return lax.ppermute(value, 'fsdp', self.left)  10 us
    unnamed x60, local copies, waits for them, and re-layouts  6.59 us
    pallas_call x1, Pallas kernels, early_part(): pl.pallas_call(functools.partial(early_kernel, plan), in_specs=[pl.BlockS...  6.14 us
  transfers between devices with their start and end apart: 28, of which 15 were waited for; matrix products, arithmetic and copies ran while one was open for 17% of the time, Pallas kernels for 23%

profile of v16, /device:TPU:8, one launch (start us, length us, event | category | flops | bytes accessed | tf_op | source)
XLA Modules:
  0.0 151.2 jit_solution(9515492023683806601)
XLA Ops:
  0.6 1.2 copy-done
  4.0 1.0 convert_element_type.122
  5.0 2.0 %collective-permute-start.1 = (bf16[512,1024]{1,0:T(8,128)(2,1)S(1)}, bf16[512,1024]{1,0:T(8,128)(2,1)S(1)}, u32[]{:S(2)}, u32[]{:S(2)}) collective-permute-start(bf16[512,1024]{1,0:T(8,128)(2,1)S(1)} %scale_rows.1.refs_0_.refs_2_), channel_id=1, source_target_pairs={{0,2},{2,4},{4,6},{6,7},{7,5},{5,3},{3,1},{1,0},{8,10},{10,12},{12... | collective-permute-start | bytes 3145736 | tf_op jit(solution)/shard_map/ppermute | solution.py:44
  7.0 3.4 %collective-permute-start.8 = (bf16[512,1024]{1,0:T(8,128)(2,1)S(1)}, bf16[512,1024]{1,0:T(8,128)(2,1)}, u32[]{:S(2)}, u32[]{:S(2)}) collective-permute-start(bf16[512,1024]{1,0:T(8,128)(2,1)S(1)} %scale_rows.1.refs_0_.refs_2_), channel_id=1, source_target_pairs={{2,3},{3,2},{4,5},{5,4},{10,11},{11,10},{12,13},{13,12},{18,19},{1... | collective-permute-start | bytes 3145736 | tf_op jit(solution)/shard_map/ppermute | solution.py:56
  10.4 1.0 fusion.23
  11.5 2.9 %add_convert_fusion = bf16[384,1024]{1,0:T(8,128)(2,1)} fusion(bf16[384,1024]{1,0:T(8,128)(2,1)} %collective-permute-done, f32[384,1024]{1,0:T(8,128)} %bitcast.82), kind=kLoop, calls=%fused_computation.7 | loop fusion | flops 1966080 | bytes 3145728 | tf_op jit(solution)/shard_map/convert_element_type | solution.py:459
  14.4 1.5 %collective-permute-start.3 = (bf16[384,1024]{1,0:T(8,128)(2,1)}, bf16[384,1024]{1,0:T(8,128)(2,1)}, u32[]{:S(2)}, u32[]{:S(2)}) collective-permute-start(bf16[384,1024]{1,0:T(8,128)(2,1)} %add_convert_fusion), channel_id=1, source_target_pairs={{0,16},{8,24},{16,0},{24,8},{1,17},{9,25},{17,1},{25,9},{2,18},{10... | collective-permute-start | bytes 2359304 | tf_op jit(solution)/shard_map/ppermute | solution.py:463
  16.2 12.1 %norm_and_weight_terms.1 = (bf16[512,1024]{1,0:T(8,128)(2,1)S(1)}, f32[512,128]{1,0:T(8,128)S(1)}, bf16[512,1024]{1,0:T(8,128)(2,1)S(1)}, f32[6,512,1024]{2,1,0:T(8,128)}, f32[512,1024]{1,0:T(8,128)S(1)}) custom-call(s32[8]{0:T(128)S(1)} %compare_select_fusion.4.at, bf16[512,4096]{1,0:T(8,128)(2,1)S(1)} %bitcast.79, bf16[512,1024]{1,0:T(8,128)(2,1)S(1)} %bitcast.81, ...), custom_call_target="tpu_custom_call" | custom-call | flops 4294967296 | bytes 20971520 | tf_op jit(solution)/shard_map/norm_and_weight_terms/pallas_call | solution.py:145
  28.2 1.3 copy-done.4
  29.6 1.0 copy-done.9
  30.5 1.0 copy-done.11
  32.2 0.8 slice.126
  33.0 0.8 slice.127
  33.9 2.0 %collective-permute-start.6 = (bf16[256,1024]{1,0:T(8,128)(2,1)}, bf16[256,1024]{1,0:T(8,128)(2,1)}, u32[]{:S(2)}, u32[]{:S(2)}) collective-permute-start(bf16[256,1024]{1,0:T(8,128)(2,1)} %slice.126), channel_id=1, source_target_pairs={{0,2},{2,4},{4,6},{6,7},{7,5},{5,3},{3,1},{1,0},{8,10},{10,12},{12... | collective-permute-start | bytes 1572872 | tf_op jit(solution)/shard_map/ppermute | solution.py:44
  36.3 2.0 %collective-permute-start.4 = (bf16[256,1024]{1,0:T(8,128)(2,1)S(1)}, bf16[256,1024]{1,0:T(8,128)(2,1)S(1)}, u32[]{:S(2)}, u32[]{:S(2)}) collective-permute-start(bf16[256,1024]{1,0:T(8,128)(2,1)S(1)} %slice.128), channel_id=1, source_target_pairs={{0,2},{2,4},{4,6},{6,7},{7,5},{5,3},{3,1},{1,0},{8,10},{10,12},{12... | collective-permute-start | bytes 1572872 | tf_op jit(solution)/shard_map/ppermute | solution.py:44
  38.5 10.6 %collective-permute-done.7.refs_5_.refs_7_ = bf16[256,1024]{1,0:T(8,128)(2,1)} collective-permute-done((bf16[256,1024]{1,0:T(8,128)(2,1)}, bf16[256,1024]{1,0:T(8,128)(2,1)}, u32[]{:S(2)}, u32[]{:S(2)}) %collective-permute-start.7) | collective-permute-done | bytes 524320 | tf_op jit(solution)/shard_map/ppermute | solution.py:47
  49.1 4.6 %collective-permute-start.13 = (bf16[512,1024]{1,0:T(8,128)(2,1)S(1)}, bf16[512,1024]{1,0:T(8,128)(2,1)S(1)}, u32[]{:S(2)}, u32[]{:S(2)}) collective-permute-start(bf16[512,1024]{1,0:T(8,128)(2,1)S(1)} %broadcast_select_fusion), channel_id=1, source_target_pairs={{2,3},{3,2},{4,5},{5,4},{10,11},{11,10},{12,13},{13,12},{18,19},{1... | collective-permute-start | bytes 3145736 | tf_op jit(solution)/shard_map/ppermute | solution.py:56
  53.7 1.3 broadcast_select_fusion.2
  55.1 2.0 %collective-permute-start.9 = (bf16[256,1024]{1,0:T(8,128)(2,1)S(1)}, bf16[256,1024]{1,0:T(8,128)(2,1)S(1)}, u32[]{:S(2)}, u32[]{:S(2)}) collective-permute-start(bf16[256,1024]{1,0:T(8,128)(2,1)S(1)} %get-tuple-element.209), channel_id=1, source_target_pairs={{0,2},{2,4},{4,6},{6,7},{7,5},{5,3},{3,1},{1,0},{8,10},{10,12},{12... | collective-permute-start | bytes 1572872 | tf_op jit(solution)/shard_map/ppermute | solution.py:44
  57.1 3.1 %collective-permute-done.5.refs_6_.refs_8_ = bf16[256,1024]{1,0:T(8,128)(2,1)S(1)} collective-permute-done((bf16[256,1024]{1,0:T(8,128)(2,1)S(1)}, bf16[256,1024]{1,0:T(8,128)(2,1)S(1)}, u32[]{:S(2)}, u32[]{:S(2)}) %collective-permute-start.5) | collective-permute-done | bytes 524320 | tf_op jit(solution)/shard_map/ppermute | solution.py:47
  60.3 6.1 %project_first.1 = (f32[512,128]{1,0:T(8,128)S(1)}, f32[5,512,512]{2,1,0:T(8,128)}) custom-call(s32[15]{0:T(128)S(1)} %pad_add_fusion.at, bf16[512,4096]{1,0:T(8,128)(2,1)S(1)} %bitcast.80, bf16[512,1024]{1,0:T(8,128)(2,1)S(1)} %copy-done.12, f32[512,128]{1,0:T(8,128)S(1)} %copy-done.16, bf16[512,1024]{1,0:T(8,128)(2,1)S(1)} %scale_rows.1.refs_0_.refs_2_, ...), custom_call_target="tpu_custom_call" | custom-call | flops 2684354560 | bytes 13107200 | tf_op jit(solution)/shard_map/project_first/pallas_call | solution.py:394
  66.5 1.6 %collective-permute-start.12 = (bf16[256,1024]{1,0:T(8,128)(2,1)S(1)}, bf16[256,1024]{1,0:T(8,128)(2,1)S(1)}, u32[]{:S(2)}, u32[]{:S(2)}) collective-permute-start(bf16[256,1024]{1,0:T(8,128)(2,1)S(1)} %get-tuple-element.206), channel_id=1, source_target_pairs={{2,0},{4,2},{6,4},{7,6},{5,7},{3,5},{1,3},{0,1},{10,8},{12,10},{14... | collective-permute-start | bytes 1572872 | tf_op jit(solution)/shard_map/ppermute | solution.py:47
  68.6 2.8 %collective-permute-done.10.refs_12_ = bf16[256,1024]{1,0:T(8,128)(2,1)S(1)} collective-permute-done((bf16[256,1024]{1,0:T(8,128)(2,1)S(1)}, bf16[256,1024]{1,0:T(8,128)(2,1)S(1)}, u32[]{:S(2)}, u32[]{:S(2)}) %collective-permute-start.10) | collective-permute-done | bytes 524320 | tf_op jit(solution)/shard_map/ppermute | solution.py:47
  71.5 2.1 %collective-permute-done.13.refs_14_ = bf16[512,1024]{1,0:T(8,128)(2,1)S(1)} collective-permute-done((bf16[512,1024]{1,0:T(8,128)(2,1)S(1)}, bf16[512,1024]{1,0:T(8,128)(2,1)S(1)}, u32[]{:S(2)}, u32[]{:S(2)}) %collective-permute-start.13) | collective-permute-done | bytes 1048608 | tf_op jit(solution)/shard_map/ppermute | solution.py:56
  73.5 3.6 %collective-permute-start.18 = (bf16[512,1024]{1,0:T(8,128)(2,1)S(1)}, bf16[512,1024]{1,0:T(8,128)(2,1)S(1)}, u32[]{:S(2)}, u32[]{:S(2)}) collective-permute-start(bf16[512,1024]{1,0:T(8,128)(2,1)S(1)} %copy-done.10), channel_id=1, source_target_pairs={{2,3},{3,2},{4,5},{5,4},{10,11},{11,10},{12,13},{13,12},{18,19},{1... | collective-permute-start | bytes 3145736 | tf_op jit(solution)/shard_map/ppermute | solution.py:56
  77.2 1.9 %fusion.20 = (bf16[256,1024]{1,0:T(8,128)(2,1)S(1)}, bf16[256,1024]{1,0:T(8,128)(2,1)S(1)}) fusion(bf16[256,1024]{1,0:T(8,128)(2,1)S(1)} %collective-permute-done.10.refs_12_, f32[6,512,1024]{2,1,0:T(8,128)} %get-tuple-element.139, pred[]{:T(512)} %eq.27, pred[]{:T(512)} %eq.28, bf16[256,1024]{1,0:T(8,128)(2,1)S(1)} %collective-permute-done.9.refs_10_), kind=kLoop, calls=%fused_computation.43 | loop fusion | flops 2621440 | bytes 4194306 | tf_op jit(solution)/shard_map/jit(_where)/select_n | solution.py:560
  79.2 2.0 %collective-permute-start.14 = (bf16[256,1024]{1,0:T(8,128)(2,1)S(1)}, bf16[256,1024]{1,0:T(8,128)(2,1)S(1)}, u32[]{:S(2)}, u32[]{:S(2)}) collective-permute-start(bf16[256,1024]{1,0:T(8,128)(2,1)S(1)} %get-tuple-element.204), channel_id=1, source_target_pairs={{0,2},{2,4},{4,6},{6,7},{7,5},{5,3},{3,1},{1,0},{8,10},{10,12},{12... | collective-permute-start | bytes 1572872 | tf_op jit(solution)/shard_map/ppermute | solution.py:44
  81.2 1.4 collective-permute-done.12.refs_13_
  83.0 1.9 %fusion.22 = (bf16[256,1024]{1,0:T(8,128)(2,1)S(1)}, bf16[256,1024]{1,0:T(8,128)(2,1)S(1)}) fusion(bf16[256,1024]{1,0:T(8,128)(2,1)S(1)} %collective-permute-done.12.refs_13_, f32[6,512,1024]{2,1,0:T(8,128)} %get-tuple-element.139, pred[]{:T(512)} %eq.27, pred[]{:T(512)} %eq.28, bf16[256,1024]{1,0:T(8,128)(2,1)S(1)} %collective-permute-done.11.refs_11_), kind=kLoop, calls=%fused_computation.45 | loop fusion | flops 2621440 | bytes 4194306 | tf_op jit(solution)/shard_map/jit(_where)/select_n | solution.py:560
  85.0 1.6 %collective-permute-start.17 = (bf16[256,1024]{1,0:T(8,128)(2,1)S(1)}, bf16[256,1024]{1,0:T(8,128)(2,1)S(1)}, u32[]{:S(2)}, u32[]{:S(2)}) collective-permute-start(bf16[256,1024]{1,0:T(8,128)(2,1)S(1)} %get-tuple-element.201), channel_id=1, source_target_pairs={{2,0},{4,2},{6,4},{7,6},{5,7},{3,5},{1,3},{0,1},{10,8},{12,10},{14... | collective-permute-start | bytes 1572872 | tf_op jit(solution)/shard_map/ppermute | solution.py:47
  87.1 2.4 %fusion.10 = bf16[512,1024]{1,0:T(8,128)(2,1)S(1)} fusion(f32[6,512,1024]{2,1,0:T(8,128)} %get-tuple-element.139, pred[]{:T(512)} %eq.27), kind=kLoop, calls=%fused_computation.20 | loop fusion | flops 524288 | bytes 3145729 | tf_op jit(solution)/shard_map/convert_element_type | solution.py:536
  89.5 4.6 %collective-permute-done.15.refs_17_ = bf16[256,1024]{1,0:T(8,128)(2,1)S(1)} collective-permute-done((bf16[256,1024]{1,0:T(8,128)(2,1)S(1)}, bf16[256,1024]{1,0:T(8,128)(2,1)S(1)}, u32[]{:S(2)}, u32[]{:S(2)}) %collective-permute-start.15) | collective-permute-done | bytes 524320 | tf_op jit(solution)/shard_map/ppermute | solution.py:47
  94.3 1.9 %fusion.12 = (bf16[256,1024]{1,0:T(8,128)(2,1)S(1)}, bf16[256,1024]{1,0:T(8,128)(2,1)S(1)}) fusion(bf16[256,1024]{1,0:T(8,128)(2,1)S(1)} %collective-permute-done.15.refs_17_, f32[6,512,1024]{2,1,0:T(8,128)} %get-tuple-element.139, pred[]{:T(512)} %eq.30, bf16[256,1024]{1,0:T(8,128)(2,1)S(1)} %collective-permute-done.14.refs_15_, pred[]{:T(512)} %eq.29), kind=kLoop, calls=%fused_computation.27 | loop fusion | flops 2097152 | bytes 4194306 | tf_op jit(solution)/shard_map/convert_element_type | solution.py:567
  96.2 1.6 %collective-permute-start.22 = (bf16[256,1024]{1,0:T(8,128)(2,1)S(1)}, bf16[256,1024]{1,0:T(8,128)(2,1)S(1)}, u32[]{:S(2)}, u32[]{:S(2)}) collective-permute-start(bf16[256,1024]{1,0:T(8,128)(2,1)S(1)} %get-tuple-element.199), channel_id=1, source_target_pairs={{2,0},{4,2},{6,4},{7,6},{5,7},{3,5},{1,3},{0,1},{10,8},{12,10},{14... | collective-permute-start | bytes 1572872 | tf_op jit(solution)/shard_map/ppermute | solution.py:47
  98.4 6.9 %collective-permute-done.17.refs_18_ = bf16[256,1024]{1,0:T(8,128)(2,1)S(1)} collective-permute-done((bf16[256,1024]{1,0:T(8,128)(2,1)S(1)}, bf16[256,1024]{1,0:T(8,128)(2,1)S(1)}, u32[]{:S(2)}, u32[]{:S(2)}) %collective-permute-start.17) | collective-permute-done | bytes 524320 | tf_op jit(solution)/shard_map/ppermute | solution.py:47
  105.5 2.1 %fusion.11 = (bf16[256,1024]{1,0:T(8,128)(2,1)S(1)}, bf16[256,1024]{1,0:T(8,128)(2,1)S(1)}) fusion(bf16[256,1024]{1,0:T(8,128)(2,1)S(1)} %collective-permute-done.17.refs_18_, f32[6,512,1024]{2,1,0:T(8,128)} %get-tuple-element.139, pred[]{:T(512)} %eq.30, bf16[256,1024]{1,0:T(8,128)(2,1)S(1)} %collective-permute-done.16.refs_16_, pred[]{:T(512)} %eq.29), kind=kLoop, calls=%fused_computation.25 | loop fusion | flops 2097152 | bytes 4194306 | tf_op jit(solution)/shard_map/convert_element_type | solution.py:567
  107.6 1.6 %collective-permute-start.20 = (bf16[256,1024]{1,0:T(8,128)(2,1)S(1)}, bf16[256,1024]{1,0:T(8,128)(2,1)S(1)}, u32[]{:S(2)}, u32[]{:S(2)}) collective-permute-start(bf16[256,1024]{1,0:T(8,128)(2,1)S(1)} %get-tuple-element.197), channel_id=1, source_target_pairs={{2,0},{4,2},{6,4},{7,6},{5,7},{3,5},{1,3},{0,1},{10,8},{12,10},{14... | collective-permute-start | bytes 1572872 | tf_op jit(solution)/shard_map/ppermute | solution.py:47
  109.7 4.1 %fusion.1 = (bf16[384,1024]{1,0:T(8,128)(2,1)}, f32[384,1024]{1,0:T(8,128)}, f32[384,1024]{1,0:T(8,128)}) fusion(bf16[1,384,1024]{2,1,0:T(8,128)(2,1)S(1)} %copy-done.23, f32[384,1024]{1,0:T(8,128)S(1)} %copy-done.21, f32[384,1024]{1,0:T(8,128)S(1)} %copy-done.22, bf16[384,1024]{1,0:T(8,128)(2,1)} %collective-permute-done.3, bf16[384,1024]{1,0:T(8,128)(2,1)} %add_convert_fusion), kind=kLoop, calls=%fused_computation.3 | loop fusion | flops 5505024 | bytes 9437184 | tf_op jit(solution)/shard_map/convert_element_type | solution.py:637
  113.8 2.7 %collective-permute-done.22 = bf16[256,1024]{1,0:T(8,128)(2,1)S(1)} collective-permute-done((bf16[256,1024]{1,0:T(8,128)(2,1)S(1)}, bf16[256,1024]{1,0:T(8,128)(2,1)S(1)}, u32[]{:S(2)}, u32[]{:S(2)}) %collective-permute-start.22) | collective-permute-done | bytes 524320 | tf_op jit(solution)/shard_map/ppermute | solution.py:47
  116.7 2.0 %fusion.5 = (bf16[256,1024]{1,0:T(8,128)(2,1)S(1)}, bf16[256,1024]{1,0:T(8,128)(2,1)S(1)}) fusion(bf16[256,1024]{1,0:T(8,128)(2,1)S(1)} %collective-permute-done.22, f32[6,512,1024]{2,1,0:T(8,128)} %get-tuple-element.139, pred[]{:T(512)} %eq.28, bf16[512,1024]{1,0:T(8,128)(2,1)S(1)} %collective-permute-done.18, pred[]{:T(512)} %eq.27, ...), kind=kLoop, calls=%fused_computation.15 | loop fusion | flops 2883584 | bytes 4718594 | tf_op jit(solution)/shard_map/convert_element_type | solution.py:574
  118.7 1.6 %collective-permute-start.27 = (bf16[256,1024]{1,0:T(8,128)(2,1)S(1)}, bf16[256,1024]{1,0:T(8,128)(2,1)S(1)}, u32[]{:S(2)}, u32[]{:S(2)}) collective-permute-start(bf16[256,1024]{1,0:T(8,128)(2,1)S(1)} %get-tuple-element.195), channel_id=1, source_target_pairs={{2,0},{4,2},{6,4},{7,6},{5,7},{3,5},{1,3},{0,1},{10,8},{12,10},{14... | collective-permute-start | bytes 1572872 | tf_op jit(solution)/shard_map/ppermute | solution.py:47
  120.8 4.3 %collective-permute-start.25 = (bf16[512,1024]{1,0:T(8,128)(2,1)S(1)}, bf16[512,1024]{1,0:T(8,128)(2,1)S(1)}, u32[]{:S(2)}, u32[]{:S(2)}) collective-permute-start(bf16[512,1024]{1,0:T(8,128)(2,1)S(1)} %fusion.10), channel_id=1, source_target_pairs={{2,3},{3,2},{4,5},{5,4},{10,11},{11,10},{12,13},{13,12},{18,19},{1... | collective-permute-start | bytes 3145736 | tf_op jit(solution)/shard_map/ppermute | solution.py:56
  125.1 2.7 %collective-permute-done.20 = bf16[256,1024]{1,0:T(8,128)(2,1)S(1)} collective-permute-done((bf16[256,1024]{1,0:T(8,128)(2,1)S(1)}, bf16[256,1024]{1,0:T(8,128)(2,1)S(1)}, u32[]{:S(2)}, u32[]{:S(2)}) %collective-permute-start.20) | collective-permute-done | bytes 524320 | tf_op jit(solution)/shard_map/ppermute | solution.py:47
  128.0 2.0 %fusion.9 = (bf16[256,1024]{1,0:T(8,128)(2,1)S(1)}, bf16[256,1024]{1,0:T(8,128)(2,1)S(1)}) fusion(bf16[256,1024]{1,0:T(8,128)(2,1)S(1)} %collective-permute-done.20, f32[6,512,1024]{2,1,0:T(8,128)} %get-tuple-element.139, pred[]{:T(512)} %eq.28, bf16[512,1024]{1,0:T(8,128)(2,1)S(1)} %collective-permute-done.18, pred[]{:T(512)} %eq.27, ...), kind=kLoop, calls=%fused_computation.19 | loop fusion | flops 2883584 | bytes 4718594 | tf_op jit(solution)/shard_map/convert_element_type | solution.py:574
  130.0 1.6 %collective-permute-start.24 = (bf16[256,1024]{1,0:T(8,128)(2,1)S(1)}, bf16[256,1024]{1,0:T(8,128)(2,1)S(1)}, u32[]{:S(2)}, u32[]{:S(2)}) collective-permute-start(bf16[256,1024]{1,0:T(8,128)(2,1)S(1)} %get-tuple-element.193), channel_id=1, source_target_pairs={{2,0},{4,2},{6,4},{7,6},{5,7},{3,5},{1,3},{0,1},{10,8},{12,10},{14... | collective-permute-start | bytes 1572872 | tf_op jit(solution)/shard_map/ppermute | solution.py:47
  132.1 16.0 %project_last.1 = (bf16[512,1024]{1,0:T(8,128)(2,1)}, bf16[512,4096]{1,0:T(8,128)(2,1)}) custom-call(s32[15]{0:T(128)S(1)} %pad_add_fusion.at, bf16[512,4096]{1,0:T(8,128)(2,1)} %bitcast.78, bf16[512,1024]{1,0:T(8,128)(2,1)} %copy-done.11, f32[512,128]{1,0:T(8,128)S(1)} %copy-done.16, f32[512,128]{1,0:T(8,128)S(1)} %get-tuple-element.213.cosine, ...), custom_call_target="tpu_custom_call" | custom-call | flops 8589934592 | bytes 16777216 | tf_op jit(solution)/shard_map/project_last/pallas_call | solution.py:427
  148.4 1.4 sum_of_terms.2
  149.8 1.3 sum_of_terms.3
  (100 shorter events, 8.4 us)
Async XLA Ops:
  3.3 56.9 %copy-start.8 = (bf16[512,1024]{1,0:T(8,128)(2,1)}, bf16[512,1024]{1,0:T(8,128)(2,1)S(1)}, u32[]{:S(2)}) copy-start(bf16[512,1024]{1,0:T(8,128)(2,1)S(1)} %scale_rows.1.refs_0_.refs_2_) | copy-start | bytes 3145732
  4.0 7.5 %copy-start.29 = (s32[8]{0:T(128)S(1)}, s32[8]{0:T(128)}, u32[]{:S(2)}) copy-start(s32[8]{0:T(128)} %constant.106.clone) | copy-start | bytes 100
  4.9 6.5 %collective-permute-start = (bf16[384,1024]{1,0:T(8,128)(2,1)}, bf16[384,1024]{1,0:T(8,128)(2,1)}, u32[]{:S(2)}, u32[]{:S(2)}) collective-permute-start(bf16[384,1024]{1,0:T(8,128)(2,1)} %convert_element_type.122), channel_id=1, source_target_pairs={{0,8},{8,0},{16,24},{24,16},{1,9},{9,1},{17,25},{25,17},{2,10},{10... | collective-permute-start | bytes 2359304 | tf_op jit(solution)/shard_map/ppermute | solution.py:463
  4.9 27.3 %collective-permute-start.2 = (bf16[512,1024]{1,0:T(8,128)(2,1)S(1)}, bf16[512,1024]{1,0:T(8,128)(2,1)S(1)}, u32[]{:S(2)}, u32[]{:S(2)}) collective-permute-start(bf16[512,1024]{1,0:T(8,128)(2,1)S(1)} %scale_rows.1.refs_0_.refs_2_), channel_id=1, source_target_pairs={{2,0},{4,2},{6,4},{7,6},{5,7},{3,5},{1,3},{0,1},{10,8},{12,10},{14... | collective-permute-start | bytes 3145736 | tf_op jit(solution)/shard_map/ppermute | solution.py:47
  5.0 27.3 %collective-permute-start.1 = (bf16[512,1024]{1,0:T(8,128)(2,1)S(1)}, bf16[512,1024]{1,0:T(8,128)(2,1)S(1)}, u32[]{:S(2)}, u32[]{:S(2)}) collective-permute-start(bf16[512,1024]{1,0:T(8,128)(2,1)S(1)} %scale_rows.1.refs_0_.refs_2_), channel_id=1, source_target_pairs={{0,2},{2,4},{4,6},{6,7},{7,5},{5,3},{3,1},{1,0},{8,10},{10,12},{12... | collective-permute-start | bytes 3145736 | tf_op jit(solution)/shard_map/ppermute | solution.py:44
  7.0 42.1 %collective-permute-start.8 = (bf16[512,1024]{1,0:T(8,128)(2,1)S(1)}, bf16[512,1024]{1,0:T(8,128)(2,1)}, u32[]{:S(2)}, u32[]{:S(2)}) collective-permute-start(bf16[512,1024]{1,0:T(8,128)(2,1)S(1)} %scale_rows.1.refs_0_.refs_2_), channel_id=1, source_target_pairs={{2,3},{3,2},{4,5},{5,4},{10,11},{11,10},{12,13},{13,12},{18,19},{1... | collective-permute-start | bytes 3145736 | tf_op jit(solution)/shard_map/ppermute | solution.py:56
  10.4 5.7 %copy-start.19 = (bf16[1,512,1024]{2,1,0:T(8,128)(2,1)S(1)}, bf16[1,512,1024]{2,1,0:T(8,128)(2,1)}, u32[]{:S(2)}) copy-start(bf16[1,512,1024]{2,1,0:T(8,128)(2,1)} %param.13) | copy-start | bytes 3145732
  11.5 4.7 %copy-start.6 = (bf16[1,512,4096]{2,1,0:T(8,128)(2,1)S(1)}, bf16[1,512,4096]{2,1,0:T(8,128)(2,1)}, u32[]{:S(2)}) copy-start(bf16[1,512,4096]{2,1,0:T(8,128)(2,1)} %param.10) | copy-start | bytes 12582916
  14.4 21.7 %collective-permute-start.3 = (bf16[384,1024]{1,0:T(8,128)(2,1)}, bf16[384,1024]{1,0:T(8,128)(2,1)}, u32[]{:S(2)}, u32[]{:S(2)}) collective-permute-start(bf16[384,1024]{1,0:T(8,128)(2,1)} %add_convert_fusion), channel_id=1, source_target_pairs={{0,16},{8,24},{16,0},{24,8},{1,17},{9,25},{17,1},{25,9},{2,18},{10... | collective-permute-start | bytes 2359304 | tf_op jit(solution)/shard_map/ppermute | solution.py:463
  16.2 12.1 %copy-start.13 = (f32[512,128]{1,0:T(8,128)}, f32[512,128]{1,0:T(8,128)S(1)}, u32[]{:S(2)}) copy-start(f32[512,128]{1,0:T(8,128)S(1)} %get-tuple-element.214.sine) | copy-start | bytes 786436
  32.2 3.7 %copy-start.28 = (s32[8]{0:T(128)S(1)}, s32[8]{0:T(128)}, u32[]{:S(2)}) copy-start(s32[8]{0:T(128)} %constant.107.clone) | copy-start | bytes 100
  32.2 28.0 %copy-start.2 = (bf16[512,1024]{1,0:T(8,128)(2,1)}, bf16[512,1024]{1,0:T(8,128)(2,1)S(1)}, u32[]{:S(2)}) copy-start(bf16[512,1024]{1,0:T(8,128)(2,1)S(1)} %collective-permute-done.2.refs_2_.refs_4_) | copy-start | bytes 3145732
  32.2 28.0 %copy-start.3 = (bf16[512,1024]{1,0:T(8,128)(2,1)}, bf16[512,1024]{1,0:T(8,128)(2,1)S(1)}, u32[]{:S(2)}) copy-start(bf16[512,1024]{1,0:T(8,128)(2,1)S(1)} %collective-permute-done.1.refs_1_.refs_3_) | copy-start | bytes 3145732
  33.9 15.2 %collective-permute-start.7 = (bf16[256,1024]{1,0:T(8,128)(2,1)}, bf16[256,1024]{1,0:T(8,128)(2,1)}, u32[]{:S(2)}, u32[]{:S(2)}) collective-permute-start(bf16[256,1024]{1,0:T(8,128)(2,1)} %slice.127), channel_id=1, source_target_pairs={{2,0},{4,2},{6,4},{7,6},{5,7},{3,5},{1,3},{0,1},{10,8},{12,10},{14... | collective-permute-start | bytes 1572872 | tf_op jit(solution)/shard_map/ppermute | solution.py:47
  33.9 15.2 %collective-permute-start.6 = (bf16[256,1024]{1,0:T(8,128)(2,1)}, bf16[256,1024]{1,0:T(8,128)(2,1)}, u32[]{:S(2)}, u32[]{:S(2)}) collective-permute-start(bf16[256,1024]{1,0:T(8,128)(2,1)} %slice.126), channel_id=1, source_target_pairs={{0,2},{2,4},{4,6},{6,7},{7,5},{5,3},{3,1},{1,0},{8,10},{10,12},{12... | collective-permute-start | bytes 1572872 | tf_op jit(solution)/shard_map/ppermute | solution.py:44
  36.2 24.1 %copy-start.12 = (bf16[512,1024]{1,0:T(8,128)(2,1)S(1)}, bf16[512,1024]{1,0:T(8,128)(2,1)}, u32[]{:S(2)}) copy-start(bf16[512,1024]{1,0:T(8,128)(2,1)} %copy-done.11) | copy-start | bytes 3145732
  36.2 17.5 %copy-start.10 = (bf16[512,1024]{1,0:T(8,128)(2,1)S(1)}, bf16[512,1024]{1,0:T(8,128)(2,1)}, u32[]{:S(2)}) copy-start(bf16[512,1024]{1,0:T(8,128)(2,1)} %copy-done.9) | copy-start | bytes 3145732
  36.2 23.9 %collective-permute-start.5 = (bf16[256,1024]{1,0:T(8,128)(2,1)S(1)}, bf16[256,1024]{1,0:T(8,128)(2,1)S(1)}, u32[]{:S(2)}, u32[]{:S(2)}) collective-permute-start(bf16[256,1024]{1,0:T(8,128)(2,1)S(1)} %slice.129), channel_id=1, source_target_pairs={{2,0},{4,2},{6,4},{7,6},{5,7},{3,5},{1,3},{0,1},{10,8},{12,10},{14... | collective-permute-start | bytes 1572872 | tf_op jit(solution)/shard_map/ppermute | solution.py:47
  36.3 23.9 %collective-permute-start.4 = (bf16[256,1024]{1,0:T(8,128)(2,1)S(1)}, bf16[256,1024]{1,0:T(8,128)(2,1)S(1)}, u32[]{:S(2)}, u32[]{:S(2)}) collective-permute-start(bf16[256,1024]{1,0:T(8,128)(2,1)S(1)} %slice.128), channel_id=1, source_target_pairs={{0,2},{2,4},{4,6},{6,7},{7,5},{5,3},{3,1},{1,0},{8,10},{10,12},{12... | collective-permute-start | bytes 1572872 | tf_op jit(solution)/shard_map/ppermute | solution.py:44
  38.3 21.9 %copy-start.7 = (bf16[1,512,4096]{2,1,0:T(8,128)(2,1)S(1)}, bf16[1,512,4096]{2,1,0:T(8,128)(2,1)}, u32[]{:S(2)}) copy-start(bf16[1,512,4096]{2,1,0:T(8,128)(2,1)} %param.10) | copy-start | bytes 12582916
  38.4 21.8 %copy-start.16 = (f32[512,128]{1,0:T(8,128)S(1)}, f32[512,128]{1,0:T(8,128)}, u32[]{:S(2)}) copy-start(f32[512,128]{1,0:T(8,128)} %copy-done.15) | copy-start | bytes 786436
  49.1 24.4 %collective-permute-start.13 = (bf16[512,1024]{1,0:T(8,128)(2,1)S(1)}, bf16[512,1024]{1,0:T(8,128)(2,1)S(1)}, u32[]{:S(2)}, u32[]{:S(2)}) collective-permute-start(bf16[512,1024]{1,0:T(8,128)(2,1)S(1)} %broadcast_select_fusion), channel_id=1, source_target_pairs={{2,3},{3,2},{4,5},{5,4},{10,11},{11,10},{12,13},{13,12},{18,19},{1... | collective-permute-start | bytes 3145736 | tf_op jit(solution)/shard_map/ppermute | solution.py:56
  55.0 16.4 %collective-permute-start.10 = (bf16[256,1024]{1,0:T(8,128)(2,1)S(1)}, bf16[256,1024]{1,0:T(8,128)(2,1)S(1)}, u32[]{:S(2)}, u32[]{:S(2)}) collective-permute-start(bf16[256,1024]{1,0:T(8,128)(2,1)S(1)} %get-tuple-element.208), channel_id=1, source_target_pairs={{2,0},{4,2},{6,4},{7,6},{5,7},{3,5},{1,3},{0,1},{10,8},{12,10},{14... | collective-permute-start | bytes 1572872 | tf_op jit(solution)/shard_map/ppermute | solution.py:47
  55.1 16.4 %collective-permute-start.9 = (bf16[256,1024]{1,0:T(8,128)(2,1)S(1)}, bf16[256,1024]{1,0:T(8,128)(2,1)S(1)}, u32[]{:S(2)}, u32[]{:S(2)}) collective-permute-start(bf16[256,1024]{1,0:T(8,128)(2,1)S(1)} %get-tuple-element.209), channel_id=1, source_target_pairs={{0,2},{2,4},{4,6},{6,7},{7,5},{5,3},{3,1},{1,0},{8,10},{10,12},{12... | collective-permute-start | bytes 1572872 | tf_op jit(solution)/shard_map/ppermute | solution.py:44
  66.5 16.1 %collective-permute-start.12 = (bf16[256,1024]{1,0:T(8,128)(2,1)S(1)}, bf16[256,1024]{1,0:T(8,128)(2,1)S(1)}, u32[]{:S(2)}, u32[]{:S(2)}) collective-permute-start(bf16[256,1024]{1,0:T(8,128)(2,1)S(1)} %get-tuple-element.206), channel_id=1, source_target_pairs={{2,0},{4,2},{6,4},{7,6},{5,7},{3,5},{1,3},{0,1},{10,8},{12,10},{14... | collective-permute-start | bytes 1572872 | tf_op jit(solution)/shard_map/ppermute | solution.py:47
  68.2 14.9 %collective-permute-start.11 = (bf16[256,1024]{1,0:T(8,128)(2,1)S(1)}, bf16[256,1024]{1,0:T(8,128)(2,1)S(1)}, u32[]{:S(2)}, u32[]{:S(2)}) collective-permute-start(bf16[256,1024]{1,0:T(8,128)(2,1)S(1)} %get-tuple-element.207), channel_id=1, source_target_pairs={{0,2},{2,4},{4,6},{6,7},{7,5},{5,3},{3,1},{1,0},{8,10},{10,12},{12... | collective-permute-start | bytes 1572872 | tf_op jit(solution)/shard_map/ppermute | solution.py:44
  73.5 5.6 %copy-start.27 = (bf16[512,1024]{1,0:T(8,128)(2,1)}, bf16[512,1024]{1,0:T(8,128)(2,1)S(1)}, u32[]{:S(2)}) copy-start(bf16[512,1024]{1,0:T(8,128)(2,1)S(1)} %collective-permute-done.13.refs_14_) | copy-start | bytes 3145732
  73.5 32.0 %collective-permute-start.18 = (bf16[512,1024]{1,0:T(8,128)(2,1)S(1)}, bf16[512,1024]{1,0:T(8,128)(2,1)S(1)}, u32[]{:S(2)}, u32[]{:S(2)}) collective-permute-start(bf16[512,1024]{1,0:T(8,128)(2,1)S(1)} %copy-done.10), channel_id=1, source_target_pairs={{2,3},{3,2},{4,5},{5,4},{10,11},{11,10},{12,13},{13,12},{18,19},{1... | collective-permute-start | bytes 3145736 | tf_op jit(solution)/shard_map/ppermute | solution.py:56
  79.1 14.9 %collective-permute-start.15 = (bf16[256,1024]{1,0:T(8,128)(2,1)S(1)}, bf16[256,1024]{1,0:T(8,128)(2,1)S(1)}, u32[]{:S(2)}, u32[]{:S(2)}) collective-permute-start(bf16[256,1024]{1,0:T(8,128)(2,1)S(1)} %get-tuple-element.203), channel_id=1, source_target_pairs={{2,0},{4,2},{6,4},{7,6},{5,7},{3,5},{1,3},{0,1},{10,8},{12,10},{14... | collective-permute-start | bytes 1572872 | tf_op jit(solution)/shard_map/ppermute | solution.py:47
  79.2 15.1 %collective-permute-start.14 = (bf16[256,1024]{1,0:T(8,128)(2,1)S(1)}, bf16[256,1024]{1,0:T(8,128)(2,1)S(1)}, u32[]{:S(2)}, u32[]{:S(2)}) collective-permute-start(bf16[256,1024]{1,0:T(8,128)(2,1)S(1)} %get-tuple-element.204), channel_id=1, source_target_pairs={{0,2},{2,4},{4,6},{6,7},{7,5},{5,3},{3,1},{1,0},{8,10},{10,12},{12... | collective-permute-start | bytes 1572872 | tf_op jit(solution)/shard_map/ppermute | solution.py:44
  85.0 20.3 %collective-permute-start.17 = (bf16[256,1024]{1,0:T(8,128)(2,1)S(1)}, bf16[256,1024]{1,0:T(8,128)(2,1)S(1)}, u32[]{:S(2)}, u32[]{:S(2)}) collective-permute-start(bf16[256,1024]{1,0:T(8,128)(2,1)S(1)} %get-tuple-element.201), channel_id=1, source_target_pairs={{2,0},{4,2},{6,4},{7,6},{5,7},{3,5},{1,3},{0,1},{10,8},{12,10},{14... | collective-permute-start | bytes 1572872 | tf_op jit(solution)/shard_map/ppermute | solution.py:47
  86.6 18.9 %collective-permute-start.16 = (bf16[256,1024]{1,0:T(8,128)(2,1)S(1)}, bf16[256,1024]{1,0:T(8,128)(2,1)S(1)}, u32[]{:S(2)}, u32[]{:S(2)}) collective-permute-start(bf16[256,1024]{1,0:T(8,128)(2,1)S(1)} %get-tuple-element.202), channel_id=1, source_target_pairs={{0,2},{2,4},{4,6},{6,7},{7,5},{5,3},{3,1},{1,0},{8,10},{10,12},{12... | collective-permute-start | bytes 1572872 | tf_op jit(solution)/shard_map/ppermute | solution.py:44
  96.2 20.3 %collective-permute-start.22 = (bf16[256,1024]{1,0:T(8,128)(2,1)S(1)}, bf16[256,1024]{1,0:T(8,128)(2,1)S(1)}, u32[]{:S(2)}, u32[]{:S(2)}) collective-permute-start(bf16[256,1024]{1,0:T(8,128)(2,1)S(1)} %get-tuple-element.199), channel_id=1, source_target_pairs={{2,0},{4,2},{6,4},{7,6},{5,7},{3,5},{1,3},{0,1},{10,8},{12,10},{14... | collective-permute-start | bytes 1572872 | tf_op jit(solution)/shard_map/ppermute | solution.py:47
  97.8 11.9 %copy-start.21 = (f32[384,1024]{1,0:T(8,128)S(1)}, f32[384,1024]{1,0:T(8,128)}, u32[]{:S(2)}) copy-start(f32[384,1024]{1,0:T(8,128)} %param.16) | copy-start | bytes 4718596
  97.8 11.9 %copy-start.22 = (f32[384,1024]{1,0:T(8,128)S(1)}, f32[384,1024]{1,0:T(8,128)}, u32[]{:S(2)}) copy-start(f32[384,1024]{1,0:T(8,128)} %param.15) | copy-start | bytes 4718596
  97.8 11.9 %copy-start.23 = (bf16[1,384,1024]{2,1,0:T(8,128)(2,1)S(1)}, bf16[1,384,1024]{2,1,0:T(8,128)(2,1)}, u32[]{:S(2)}) copy-start(bf16[1,384,1024]{2,1,0:T(8,128)(2,1)} %param.17) | copy-start | bytes 2359300
  97.8 18.9 %collective-permute-start.21 = (bf16[256,1024]{1,0:T(8,128)(2,1)S(1)}, bf16[256,1024]{1,0:T(8,128)(2,1)S(1)}, u32[]{:S(2)}, u32[]{:S(2)}) collective-permute-start(bf16[256,1024]{1,0:T(8,128)(2,1)S(1)} %get-tuple-element.200), channel_id=1, source_target_pairs={{0,2},{2,4},{4,6},{6,7},{7,5},{5,3},{3,1},{1,0},{8,10},{10,12},{12... | collective-permute-start | bytes 1572872 | tf_op jit(solution)/shard_map/ppermute | solution.py:44
  107.6 20.1 %collective-permute-start.20 = (bf16[256,1024]{1,0:T(8,128)(2,1)S(1)}, bf16[256,1024]{1,0:T(8,128)(2,1)S(1)}, u32[]{:S(2)}, u32[]{:S(2)}) collective-permute-start(bf16[256,1024]{1,0:T(8,128)(2,1)S(1)} %get-tuple-element.197), channel_id=1, source_target_pairs={{2,0},{4,2},{6,4},{7,6},{5,7},{3,5},{1,3},{0,1},{10,8},{12,10},{14... | collective-permute-start | bytes 1572872 | tf_op jit(solution)/shard_map/ppermute | solution.py:47
  109.2 18.7 %collective-permute-start.19 = (bf16[256,1024]{1,0:T(8,128)(2,1)S(1)}, bf16[256,1024]{1,0:T(8,128)(2,1)S(1)}, u32[]{:S(2)}, u32[]{:S(2)}) collective-permute-start(bf16[256,1024]{1,0:T(8,128)(2,1)S(1)} %get-tuple-element.198), channel_id=1, source_target_pairs={{0,2},{2,4},{4,6},{6,7},{7,5},{5,3},{3,1},{1,0},{8,10},{10,12},{12... | collective-permute-start | bytes 1572872 | tf_op jit(solution)/shard_map/ppermute | solution.py:44
  118.7 29.4 %collective-permute-start.27 = (bf16[256,1024]{1,0:T(8,128)(2,1)S(1)}, bf16[256,1024]{1,0:T(8,128)(2,1)S(1)}, u32[]{:S(2)}, u32[]{:S(2)}) collective-permute-start(bf16[256,1024]{1,0:T(8,128)(2,1)S(1)} %get-tuple-element.195), channel_id=1, source_target_pairs={{2,0},{4,2},{6,4},{7,6},{5,7},{3,5},{1,3},{0,1},{10,8},{12,10},{14... | collective-permute-start | bytes 1572872 | tf_op jit(solution)/shard_map/ppermute | solution.py:47
  120.4 27.8 %collective-permute-start.26 = (bf16[256,1024]{1,0:T(8,128)(2,1)S(1)}, bf16[256,1024]{1,0:T(8,128)(2,1)S(1)}, u32[]{:S(2)}, u32[]{:S(2)}) collective-permute-start(bf16[256,1024]{1,0:T(8,128)(2,1)S(1)} %get-tuple-element.196), channel_id=1, source_target_pairs={{0,2},{2,4},{4,6},{6,7},{7,5},{5,3},{3,1},{1,0},{8,10},{10,12},{12... | collective-permute-start | bytes 1572872 | tf_op jit(solution)/shard_map/ppermute | solution.py:44
  120.8 27.6 %collective-permute-start.25 = (bf16[512,1024]{1,0:T(8,128)(2,1)S(1)}, bf16[512,1024]{1,0:T(8,128)(2,1)S(1)}, u32[]{:S(2)}, u32[]{:S(2)}) collective-permute-start(bf16[512,1024]{1,0:T(8,128)(2,1)S(1)} %fusion.10), channel_id=1, source_target_pairs={{2,3},{3,2},{4,5},{5,4},{10,11},{11,10},{12,13},{13,12},{18,19},{1... | collective-permute-start | bytes 3145736 | tf_op jit(solution)/shard_map/ppermute | solution.py:56
  128.0 4.1 %copy-start.14 = (f32[512,128]{1,0:T(8,128)S(1)}, f32[512,128]{1,0:T(8,128)}, u32[]{:S(2)}) copy-start(f32[512,128]{1,0:T(8,128)} %copy-done.13) | copy-start | bytes 786436
  130.0 18.4 %collective-permute-start.24 = (bf16[256,1024]{1,0:T(8,128)(2,1)S(1)}, bf16[256,1024]{1,0:T(8,128)(2,1)S(1)}, u32[]{:S(2)}, u32[]{:S(2)}) collective-permute-start(bf16[256,1024]{1,0:T(8,128)(2,1)S(1)} %get-tuple-element.193), channel_id=1, source_target_pairs={{2,0},{4,2},{6,4},{7,6},{5,7},{3,5},{1,3},{0,1},{10,8},{12,10},{14... | collective-permute-start | bytes 1572872 | tf_op jit(solution)/shard_map/ppermute | solution.py:47
  131.7 16.8 %copy-start.1 = (bf16[1,512,1024]{2,1,0:T(8,128)(2,1)S(1)}, bf16[1,512,1024]{2,1,0:T(8,128)(2,1)}, u32[]{:S(2)}) copy-start(bf16[1,512,1024]{2,1,0:T(8,128)(2,1)} %param.12) | copy-start | bytes 3145732
  131.7 16.8 %copy-start.5 = (f32[512,1024]{1,0:T(8,128)S(1)}, f32[512,1024]{1,0:T(8,128)}, u32[]{:S(2)}) copy-start(f32[512,1024]{1,0:T(8,128)} %copy-done.4) | copy-start | bytes 6291460
  131.7 16.8 %copy-start.18 = (bf16[1,512]{1,0:T(2,128)(2,1)S(1)}, bf16[1,512]{1,0:T(2,128)(2,1)}, u32[]{:S(2)}) copy-start(bf16[1,512]{1,0:T(2,128)(2,1)} %gain.5) | copy-start | bytes 3076
  131.7 16.8 %collective-permute-start.23 = (bf16[256,1024]{1,0:T(8,128)(2,1)S(1)}, bf16[256,1024]{1,0:T(8,128)(2,1)S(1)}, u32[]{:S(2)}, u32[]{:S(2)}) collective-permute-start(bf16[256,1024]{1,0:T(8,128)(2,1)S(1)} %get-tuple-element.194), channel_id=1, source_target_pairs={{0,2},{2,4},{4,6},{6,7},{7,5},{5,3},{3,1},{1,0},{8,10},{10,12},{12... | collective-permute-start | bytes 1572872 | tf_op jit(solution)/shard_map/ppermute | solution.py:44
  (10 other events, 13.8 us)

commit v17 on v16

--- a/solution.py
+++ b/solution.py
@@ -491,7 +491,7 @@
     return late(blocks, plan), sums, update(total)
 
 
-ORDER = {"sum": (-1, 1), "pair": (-1, 3), "inner": (2, 7), "far": (1, 5), "partner": (7, None), "first": (2, 3), "update": (5, 9)}
+ORDER = {"sum": (-1, 1), "pair": (-1, 3), "inner": (2, 7), "far": (1, 5), "partner": (7, None), "first": (2, 4), "update": (5, 9)}
 CHAIN = True
 
 

time: 154 us -> 163 us (1.058)
  waiting for transfers between devices: 38.5 us -> 43.7 us
  other arithmetic: 25.2 us -> 29.3 us
    ppermute x4, waiting for transfers between devices: 2.07 us -> 6.11 us  [over_chord(): return lax.ppermute(value, 'fsdp', [(2, 3), (3, 2), (4, 5), (5, 4)])]
    ppermute x11, starting transfers between devices: 10 us -> 6.95 us  [to_left(): return lax.ppermute(value, 'fsdp', self.left)]
    ppermute x11, starting transfers between devices: 12.8 us -> 15.9 us  [to_right(): return lax.ppermute(value, 'fsdp', self.right)]
    select_n x2, other arithmetic: 1.44 us -> 3.71 us  [exchange_plane(): three.append(ring(2 + h, pick(at0, terms, left), pick(at3, terms, right)))]
    slice x4, local copies, waits for them, and re-layouts: 1.73 us -> 3.45 us  [part(): return value[pieces[h][0]:pieces[h][1]]]
  transfers between devices with their start and end apart: 28 -> 28, of which waited for: 15 -> 18; matrix products, arithmetic and copies ran while one was open for 17% -> 20% of each run, Pallas kernels for 23% -> 21%
where the time goes in v17:
time: 163 us; the launch traced here: 161 us
  waiting for transfers between devices  43.7 us (27%)
  starting transfers between devices  39.8 us (24%)
  Pallas kernels  37.7 us (23%)
  other arithmetic  29.3 us (18%)
  local copies, waits for them, and re-layouts  9.77 us (6%)
    ppermute x11, waiting for transfers between devices, to_left(): return lax.ppermute(value, 'fsdp', self.left)  34.1 us
    pallas_call x1, Pallas kernels, late_part(): pl.pallas_call(functools.partial(late_kernel, plan, done), in_specs=[pl.B...  16.2 us
    ppermute x11, starting transfers between devices, to_right(): return lax.ppermute(value, 'fsdp', self.right)  15.9 us
    ppermute x4, starting transfers between devices, over_chord(): return lax.ppermute(value, 'fsdp', [(2, 3), (3, 2), (4, 5), (5, 4)])  15.5 us
    pallas_call x1, Pallas kernels, first_part(): pl.pallas_call(functools.partial(first_kernel, scale), grid_spec=pltpu.Pr...  12 us
    ppermute x11, starting transfers between devices, to_left(): return lax.ppermute(value, 'fsdp', self.left)  6.95 us
    unnamed x60, local copies, waits for them, and re-layouts  6.21 us
    ppermute x4, waiting for transfers between devices, over_chord(): return lax.ppermute(value, 'fsdp', [(2, 3), (3, 2), (4, 5), (5, 4)])  6.11 us
  transfers between devices with their start and end apart: 28, of which 18 were waited for; matrix products, arithmetic and copies ran while one was open for 20% of the time, Pallas kernels for 21%

profile of v17, /device:TPU:8, one launch (start us, length us, event | category | flops | bytes accessed | tf_op | source)
XLA Modules:
  0.0 161.3 jit_solution(3755384798980440257)
XLA Ops:
  0.6 1.2 copy-done
  3.4 2.0 %collective-permute-start.1 = (bf16[512,1024]{1,0:T(8,128)(2,1)S(1)}, bf16[512,1024]{1,0:T(8,128)(2,1)S(1)}, u32[]{:S(2)}, u32[]{:S(2)}) collective-permute-start(bf16[512,1024]{1,0:T(8,128)(2,1)S(1)} %scale_rows.1.refs_0_.refs_2_), channel_id=1, source_target_pairs={{0,2},{2,4},{4,6},{6,7},{7,5},{5,3},{3,1},{1,0},{8,10},{10,12},{12... | collective-permute-start | bytes 3145736 | tf_op jit(solution)/shard_map/ppermute | solution.py:44
  5.4 1.0 convert_element_type.122
  6.4 1.0 fusion.23
  7.7 1.3 collective-permute-done
  9.0 2.8 %add_convert_fusion = bf16[384,1024]{1,0:T(8,128)(2,1)} fusion(bf16[384,1024]{1,0:T(8,128)(2,1)} %collective-permute-done, f32[384,1024]{1,0:T(8,128)} %bitcast.82), kind=kLoop, calls=%fused_computation.7 | loop fusion | flops 1966080 | bytes 3145728 | tf_op jit(solution)/shard_map/convert_element_type | solution.py:459
  11.8 1.5 collective-permute-start.5
  13.3 12.0 %norm_and_weight_terms.1 = (bf16[512,1024]{1,0:T(8,128)(2,1)S(1)}, f32[512,128]{1,0:T(8,128)S(1)}, bf16[512,1024]{1,0:T(8,128)(2,1)S(1)}, f32[6,512,1024]{2,1,0:T(8,128)}, f32[512,1024]{1,0:T(8,128)S(1)}) custom-call(s32[8]{0:T(128)S(1)} %compare_select_fusion.4.at, bf16[512,4096]{1,0:T(8,128)(2,1)S(1)} %bitcast.79, bf16[512,1024]{1,0:T(8,128)(2,1)S(1)} %bitcast.81, ...), custom_call_target="tpu_custom_call" | custom-call | flops 4294967296 | bytes 20971520 | tf_op jit(solution)/shard_map/norm_and_weight_terms/pallas_call | solution.py:145
  25.3 1.3 copy-done.4
  28.3 1.0 slice.127
  30.1 1.5 collective-permute-start.4
  32.2 4.5 %collective-permute-start.10 = (bf16[512,1024]{1,0:T(8,128)(2,1)S(1)}, bf16[512,1024]{1,0:T(8,128)(2,1)}, u32[]{:S(2)}, u32[]{:S(2)}) collective-permute-start(bf16[512,1024]{1,0:T(8,128)(2,1)S(1)} %scale_rows.1.refs_0_.refs_2_), channel_id=1, source_target_pairs={{2,3},{3,2},{4,5},{5,4},{10,11},{11,10},{12,13},{13,12},{18,19},{1... | collective-permute-start | bytes 3145736 | tf_op jit(solution)/shard_map/ppermute | solution.py:56
  36.7 7.0 %collective-permute-done.4.refs_5_.refs_7_ = bf16[256,1024]{1,0:T(8,128)(2,1)} collective-permute-done((bf16[256,1024]{1,0:T(8,128)(2,1)}, bf16[256,1024]{1,0:T(8,128)(2,1)}, u32[]{:S(2)}, u32[]{:S(2)}) %collective-permute-start.4) | collective-permute-done | bytes 524320 | tf_op jit(solution)/shard_map/ppermute | solution.py:47
  46.0 1.5 collective-permute-start.9
  48.0 2.3 %broadcast_select_fusion.2 = (bf16[256,1024]{1,0:T(8,128)(2,1)}, bf16[256,1024]{1,0:T(8,128)(2,1)}) fusion(bf16[256,1024]{1,0:T(8,128)(2,1)} %collective-permute-done.4.refs_5_.refs_7_, pred[]{:T(512)} %eq.29, bf16[512,1024]{1,0:T(8,128)(2,1)S(1)} %copy-done.10, bf16[256,1024]{1,0:T(8,128)(2,1)} %collective-permute-done.3.refs_3_.refs_5_, pred[]{:T(512)} %eq.30), kind=kLoop, calls=%fused_computation.47 | loop fusion | flops 524288 | bytes 2621442 | tf_op jit(solution)/shard_map/jit(_where)/select_n | solution.py:553
  50.3 1.3 collective-permute-start.7
  52.3 1.1 broadcast_select_fusion
  53.4 4.9 %collective-permute-done.10.refs_9_ = bf16[512,1024]{1,0:T(8,128)(2,1)} collective-permute-done((bf16[512,1024]{1,0:T(8,128)(2,1)S(1)}, bf16[512,1024]{1,0:T(8,128)(2,1)}, u32[]{:S(2)}, u32[]{:S(2)}) %collective-permute-start.10) | collective-permute-done | bytes 1048608 | tf_op jit(solution)/shard_map/ppermute | solution.py:56
  58.3 3.6 %collective-permute-start.13 = (bf16[512,1024]{1,0:T(8,128)(2,1)}, bf16[512,1024]{1,0:T(8,128)(2,1)}, u32[]{:S(2)}, u32[]{:S(2)}) collective-permute-start(bf16[512,1024]{1,0:T(8,128)(2,1)} %broadcast_select_fusion), channel_id=1, source_target_pairs={{2,3},{3,2},{4,5},{5,4},{10,11},{11,10},{12,13},{13,12},{18,19},{1... | collective-permute-start | bytes 3145736 | tf_op jit(solution)/shard_map/ppermute | solution.py:56
  62.7 6.7 %collective-permute-done.7.refs_12_ = bf16[256,1024]{1,0:T(8,128)(2,1)} collective-permute-done((bf16[256,1024]{1,0:T(8,128)(2,1)}, bf16[256,1024]{1,0:T(8,128)(2,1)}, u32[]{:S(2)}, u32[]{:S(2)}) %collective-permute-start.7) | collective-permute-done | bytes 524320 | tf_op jit(solution)/shard_map/ppermute | solution.py:47
  70.1 1.4 broadcast_select_fusion.1
  71.6 1.5 collective-permute-start.12
  73.7 2.2 %copy-done.7 = bf16[1,512,4096]{2,1,0:T(8,128)(2,1)S(1)} copy-done((bf16[1,512,4096]{2,1,0:T(8,128)(2,1)S(1)}, bf16[1,512,4096]{2,1,0:T(8,128)(2,1)}, u32[]{:S(2)}) %copy-start.7) | copy-done | bytes 4194328
  75.9 6.1 %project_first.1 = (f32[512,128]{1,0:T(8,128)S(1)}, f32[5,512,512]{2,1,0:T(8,128)}) custom-call(s32[15]{0:T(128)S(1)} %pad_add_fusion.at, bf16[512,4096]{1,0:T(8,128)(2,1)S(1)} %bitcast.80, bf16[512,1024]{1,0:T(8,128)(2,1)S(1)} %copy-done.13, f32[512,128]{1,0:T(8,128)S(1)} %copy-done.17, bf16[512,1024]{1,0:T(8,128)(2,1)S(1)} %scale_rows.1.refs_0_.refs_2_, ...), custom_call_target="tpu_custom_call" | custom-call | flops 2684354560 | bytes 13107200 | tf_op jit(solution)/shard_map/project_first/pallas_call | solution.py:394
  82.0 1.2 collective-permute-done.13.refs_14_
  83.2 3.6 %collective-permute-start.18 = (bf16[512,1024]{1,0:T(8,128)(2,1)S(1)}, bf16[512,1024]{1,0:T(8,128)(2,1)S(1)}, u32[]{:S(2)}, u32[]{:S(2)}) collective-permute-start(bf16[512,1024]{1,0:T(8,128)(2,1)S(1)} %copy-done.11), channel_id=1, source_target_pairs={{2,3},{3,2},{4,5},{5,4},{10,11},{11,10},{12,13},{13,12},{18,19},{1... | collective-permute-start | bytes 3145736 | tf_op jit(solution)/shard_map/ppermute | solution.py:56
  86.8 2.7 %fusion.20 = (bf16[256,1024]{1,0:T(8,128)(2,1)S(1)}, bf16[256,1024]{1,0:T(8,128)(2,1)S(1)}) fusion(bf16[256,1024]{1,0:T(8,128)(2,1)} %collective-permute-done.7.refs_12_, f32[6,512,1024]{2,1,0:T(8,128)} %get-tuple-element.139, pred[]{:T(512)} %eq.27, pred[]{:T(512)} %eq.28, bf16[256,1024]{1,0:T(8,128)(2,1)} %collective-permute-done.6.refs_10_), kind=kLoop, calls=%fused_computation.43 | loop fusion | flops 2621440 | bytes 4194306 | tf_op jit(solution)/shard_map/jit(_where)/select_n | solution.py:560
  89.5 2.0 %collective-permute-start.14 = (bf16[256,1024]{1,0:T(8,128)(2,1)S(1)}, bf16[256,1024]{1,0:T(8,128)(2,1)S(1)}, u32[]{:S(2)}, u32[]{:S(2)}) collective-permute-start(bf16[256,1024]{1,0:T(8,128)(2,1)S(1)} %get-tuple-element.204), channel_id=1, source_target_pairs={{0,2},{2,4},{4,6},{6,7},{7,5},{5,3},{3,1},{1,0},{8,10},{10,12},{12... | collective-permute-start | bytes 1572872 | tf_op jit(solution)/shard_map/ppermute | solution.py:44
  91.6 1.9 %fusion.22 = (bf16[256,1024]{1,0:T(8,128)(2,1)S(1)}, bf16[256,1024]{1,0:T(8,128)(2,1)S(1)}) fusion(bf16[256,1024]{1,0:T(8,128)(2,1)S(1)} %collective-permute-done.12.refs_13_, f32[6,512,1024]{2,1,0:T(8,128)} %get-tuple-element.139, pred[]{:T(512)} %eq.27, pred[]{:T(512)} %eq.28, bf16[256,1024]{1,0:T(8,128)(2,1)S(1)} %collective-permute-done.11.refs_11_), kind=kLoop, calls=%fused_computation.45 | loop fusion | flops 2621440 | bytes 4194306 | tf_op jit(solution)/shard_map/jit(_where)/select_n | solution.py:560
  93.6 2.0 %collective-permute-start.16 = (bf16[256,1024]{1,0:T(8,128)(2,1)S(1)}, bf16[256,1024]{1,0:T(8,128)(2,1)S(1)}, u32[]{:S(2)}, u32[]{:S(2)}) collective-permute-start(bf16[256,1024]{1,0:T(8,128)(2,1)S(1)} %get-tuple-element.202), channel_id=1, source_target_pairs={{0,2},{2,4},{4,6},{6,7},{7,5},{5,3},{3,1},{1,0},{8,10},{10,12},{12... | collective-permute-start | bytes 1572872 | tf_op jit(solution)/shard_map/ppermute | solution.py:44
  95.6 2.4 %fusion.10 = bf16[512,1024]{1,0:T(8,128)(2,1)S(1)} fusion(f32[6,512,1024]{2,1,0:T(8,128)} %get-tuple-element.139, pred[]{:T(512)} %eq.27), kind=kLoop, calls=%fused_computation.20 | loop fusion | flops 524288 | bytes 3145729 | tf_op jit(solution)/shard_map/convert_element_type | solution.py:536
  98.0 6.4 %collective-permute-done.15.refs_17_ = bf16[256,1024]{1,0:T(8,128)(2,1)S(1)} collective-permute-done((bf16[256,1024]{1,0:T(8,128)(2,1)S(1)}, bf16[256,1024]{1,0:T(8,128)(2,1)S(1)}, u32[]{:S(2)}, u32[]{:S(2)}) %collective-permute-start.15) | collective-permute-done | bytes 524320 | tf_op jit(solution)/shard_map/ppermute | solution.py:47
  104.4 2.0 %fusion.12 = (bf16[256,1024]{1,0:T(8,128)(2,1)S(1)}, bf16[256,1024]{1,0:T(8,128)(2,1)S(1)}) fusion(bf16[256,1024]{1,0:T(8,128)(2,1)S(1)} %collective-permute-done.15.refs_17_, f32[6,512,1024]{2,1,0:T(8,128)} %get-tuple-element.139, pred[]{:T(512)} %eq.30, bf16[256,1024]{1,0:T(8,128)(2,1)S(1)} %collective-permute-done.14.refs_15_, pred[]{:T(512)} %eq.29), kind=kLoop, calls=%fused_computation.27 | loop fusion | flops 2097152 | bytes 4194306 | tf_op jit(solution)/shard_map/convert_element_type | solution.py:567
  106.7 2.0 %collective-permute-start.21 = (bf16[256,1024]{1,0:T(8,128)(2,1)S(1)}, bf16[256,1024]{1,0:T(8,128)(2,1)S(1)}, u32[]{:S(2)}, u32[]{:S(2)}) collective-permute-start(bf16[256,1024]{1,0:T(8,128)(2,1)S(1)} %get-tuple-element.200), channel_id=1, source_target_pairs={{0,2},{2,4},{4,6},{6,7},{7,5},{5,3},{3,1},{1,0},{8,10},{10,12},{12... | collective-permute-start | bytes 1572872 | tf_op jit(solution)/shard_map/ppermute | solution.py:44
  108.7 6.9 %collective-permute-done.17.refs_18_ = bf16[256,1024]{1,0:T(8,128)(2,1)S(1)} collective-permute-done((bf16[256,1024]{1,0:T(8,128)(2,1)S(1)}, bf16[256,1024]{1,0:T(8,128)(2,1)S(1)}, u32[]{:S(2)}, u32[]{:S(2)}) %collective-permute-start.17) | collective-permute-done | bytes 524320 | tf_op jit(solution)/shard_map/ppermute | solution.py:47
  115.7 2.2 %fusion.11 = (bf16[256,1024]{1,0:T(8,128)(2,1)S(1)}, bf16[256,1024]{1,0:T(8,128)(2,1)S(1)}) fusion(bf16[256,1024]{1,0:T(8,128)(2,1)S(1)} %collective-permute-done.17.refs_18_, f32[6,512,1024]{2,1,0:T(8,128)} %get-tuple-element.139, pred[]{:T(512)} %eq.30, bf16[256,1024]{1,0:T(8,128)(2,1)S(1)} %collective-permute-done.16.refs_16_, pred[]{:T(512)} %eq.29), kind=kLoop, calls=%fused_computation.25 | loop fusion | flops 2097152 | bytes 4194306 | tf_op jit(solution)/shard_map/convert_element_type | solution.py:567
  118.1 1.9 %collective-permute-start.19 = (bf16[256,1024]{1,0:T(8,128)(2,1)S(1)}, bf16[256,1024]{1,0:T(8,128)(2,1)S(1)}, u32[]{:S(2)}, u32[]{:S(2)}) collective-permute-start(bf16[256,1024]{1,0:T(8,128)(2,1)S(1)} %get-tuple-element.198), channel_id=1, source_target_pairs={{0,2},{2,4},{4,6},{6,7},{7,5},{5,3},{3,1},{1,0},{8,10},{10,12},{12... | collective-permute-start | bytes 1572872 | tf_op jit(solution)/shard_map/ppermute | solution.py:44
  120.0 4.1 %fusion.1 = (bf16[384,1024]{1,0:T(8,128)(2,1)}, f32[384,1024]{1,0:T(8,128)}, f32[384,1024]{1,0:T(8,128)}) fusion(bf16[1,384,1024]{2,1,0:T(8,128)(2,1)S(1)} %copy-done.24, f32[384,1024]{1,0:T(8,128)S(1)} %copy-done.22, f32[384,1024]{1,0:T(8,128)S(1)} %copy-done.23, bf16[384,1024]{1,0:T(8,128)(2,1)} %collective-permute-done.5, bf16[384,1024]{1,0:T(8,128)(2,1)} %add_convert_fusion), kind=kLoop, calls=%fused_computation.3 | loop fusion | flops 5505024 | bytes 9437184 | tf_op jit(solution)/shard_map/convert_element_type | solution.py:637
  124.1 2.7 %collective-permute-done.22 = bf16[256,1024]{1,0:T(8,128)(2,1)S(1)} collective-permute-done((bf16[256,1024]{1,0:T(8,128)(2,1)S(1)}, bf16[256,1024]{1,0:T(8,128)(2,1)S(1)}, u32[]{:S(2)}, u32[]{:S(2)}) %collective-permute-start.22) | collective-permute-done | bytes 524320 | tf_op jit(solution)/shard_map/ppermute | solution.py:47
  126.9 2.0 %fusion.5 = (bf16[256,1024]{1,0:T(8,128)(2,1)S(1)}, bf16[256,1024]{1,0:T(8,128)(2,1)S(1)}) fusion(bf16[256,1024]{1,0:T(8,128)(2,1)S(1)} %collective-permute-done.22, f32[6,512,1024]{2,1,0:T(8,128)} %get-tuple-element.139, pred[]{:T(512)} %eq.28, bf16[512,1024]{1,0:T(8,128)(2,1)S(1)} %collective-permute-done.18, pred[]{:T(512)} %eq.27, ...), kind=kLoop, calls=%fused_computation.15 | loop fusion | flops 2883584 | bytes 4718594 | tf_op jit(solution)/shard_map/convert_element_type | solution.py:574
  129.2 1.8 %collective-permute-start.26 = (bf16[256,1024]{1,0:T(8,128)(2,1)S(1)}, bf16[256,1024]{1,0:T(8,128)(2,1)S(1)}, u32[]{:S(2)}, u32[]{:S(2)}) collective-permute-start(bf16[256,1024]{1,0:T(8,128)(2,1)S(1)} %get-tuple-element.196), channel_id=1, source_target_pairs={{0,2},{2,4},{4,6},{6,7},{7,5},{5,3},{3,1},{1,0},{8,10},{10,12},{12... | collective-permute-start | bytes 1572872 | tf_op jit(solution)/shard_map/ppermute | solution.py:44
  131.0 3.7 %collective-permute-start.25 = (bf16[512,1024]{1,0:T(8,128)(2,1)S(1)}, bf16[512,1024]{1,0:T(8,128)(2,1)S(1)}, u32[]{:S(2)}, u32[]{:S(2)}) collective-permute-start(bf16[512,1024]{1,0:T(8,128)(2,1)S(1)} %fusion.10), channel_id=1, source_target_pairs={{2,3},{3,2},{4,5},{5,4},{10,11},{11,10},{12,13},{13,12},{18,19},{1... | collective-permute-start | bytes 3145736 | tf_op jit(solution)/shard_map/ppermute | solution.py:56
  134.7 3.4 %collective-permute-done.20 = bf16[256,1024]{1,0:T(8,128)(2,1)S(1)} collective-permute-done((bf16[256,1024]{1,0:T(8,128)(2,1)S(1)}, bf16[256,1024]{1,0:T(8,128)(2,1)S(1)}, u32[]{:S(2)}, u32[]{:S(2)}) %collective-permute-start.20) | collective-permute-done | bytes 524320 | tf_op jit(solution)/shard_map/ppermute | solution.py:47
  138.2 2.0 %fusion.9 = (bf16[256,1024]{1,0:T(8,128)(2,1)S(1)}, bf16[256,1024]{1,0:T(8,128)(2,1)S(1)}) fusion(bf16[256,1024]{1,0:T(8,128)(2,1)S(1)} %collective-permute-done.20, f32[6,512,1024]{2,1,0:T(8,128)} %get-tuple-element.139, pred[]{:T(512)} %eq.28, bf16[512,1024]{1,0:T(8,128)(2,1)S(1)} %collective-permute-done.18, pred[]{:T(512)} %eq.27, ...), kind=kLoop, calls=%fused_computation.19 | loop fusion | flops 2883584 | bytes 4718594 | tf_op jit(solution)/shard_map/convert_element_type | solution.py:574
  140.5 1.8 %collective-permute-start.23 = (bf16[256,1024]{1,0:T(8,128)(2,1)S(1)}, bf16[256,1024]{1,0:T(8,128)(2,1)S(1)}, u32[]{:S(2)}, u32[]{:S(2)}) collective-permute-start(bf16[256,1024]{1,0:T(8,128)(2,1)S(1)} %get-tuple-element.194), channel_id=1, source_target_pairs={{0,2},{2,4},{4,6},{6,7},{7,5},{5,3},{3,1},{1,0},{8,10},{10,12},{12... | collective-permute-start | bytes 1572872 | tf_op jit(solution)/shard_map/ppermute | solution.py:44
  142.3 16.2 %project_last.1 = (bf16[512,1024]{1,0:T(8,128)(2,1)}, bf16[512,4096]{1,0:T(8,128)(2,1)}) custom-call(s32[15]{0:T(128)S(1)} %pad_add_fusion.at, bf16[512,4096]{1,0:T(8,128)(2,1)} %bitcast.78, bf16[512,1024]{1,0:T(8,128)(2,1)} %copy-done.12, f32[512,128]{1,0:T(8,128)S(1)} %copy-done.17, f32[512,128]{1,0:T(8,128)S(1)} %get-tuple-element.213.cosine, ...), custom_call_target="tpu_custom_call" | custom-call | flops 8589934592 | bytes 16777216 | tf_op jit(solution)/shard_map/project_last/pallas_call | solution.py:427
  158.6 1.4 sum_of_terms.2
  159.9 1.3 sum_of_terms.3
  (100 shorter events, 11.7 us)
Async XLA Ops:
  3.3 70.4 %copy-start.8 = (bf16[512,1024]{1,0:T(8,128)(2,1)}, bf16[512,1024]{1,0:T(8,128)(2,1)S(1)}, u32[]{:S(2)}) copy-start(bf16[512,1024]{1,0:T(8,128)(2,1)S(1)} %scale_rows.1.refs_0_.refs_2_) | copy-start | bytes 3145732
  3.3 25.0 %collective-permute-start.2 = (bf16[512,1024]{1,0:T(8,128)(2,1)S(1)}, bf16[512,1024]{1,0:T(8,128)(2,1)S(1)}, u32[]{:S(2)}, u32[]{:S(2)}) collective-permute-start(bf16[512,1024]{1,0:T(8,128)(2,1)S(1)} %scale_rows.1.refs_0_.refs_2_), channel_id=1, source_target_pairs={{2,0},{4,2},{6,4},{7,6},{5,7},{3,5},{1,3},{0,1},{10,8},{12,10},{14... | collective-permute-start | bytes 3145736 | tf_op jit(solution)/shard_map/ppermute | solution.py:47
  3.4 25.0 %collective-permute-start.1 = (bf16[512,1024]{1,0:T(8,128)(2,1)S(1)}, bf16[512,1024]{1,0:T(8,128)(2,1)S(1)}, u32[]{:S(2)}, u32[]{:S(2)}) collective-permute-start(bf16[512,1024]{1,0:T(8,128)(2,1)S(1)} %scale_rows.1.refs_0_.refs_2_), channel_id=1, source_target_pairs={{0,2},{2,4},{4,6},{6,7},{7,5},{5,3},{3,1},{1,0},{8,10},{10,12},{12... | collective-permute-start | bytes 3145736 | tf_op jit(solution)/shard_map/ppermute | solution.py:44
  6.4 2.6 %collective-permute-start = (bf16[384,1024]{1,0:T(8,128)(2,1)}, bf16[384,1024]{1,0:T(8,128)(2,1)}, u32[]{:S(2)}, u32[]{:S(2)}) collective-permute-start(bf16[384,1024]{1,0:T(8,128)(2,1)} %convert_element_type.122), channel_id=1, source_target_pairs={{0,8},{8,0},{16,24},{24,16},{1,9},{9,1},{17,25},{25,17},{2,10},{10... | collective-permute-start | bytes 2359304 | tf_op jit(solution)/shard_map/ppermute | solution.py:463
  6.4 6.9 %copy-start.20 = (bf16[1,512,1024]{2,1,0:T(8,128)(2,1)S(1)}, bf16[1,512,1024]{2,1,0:T(8,128)(2,1)}, u32[]{:S(2)}) copy-start(bf16[1,512,1024]{2,1,0:T(8,128)(2,1)} %param.13) | copy-start | bytes 3145732
  7.4 5.9 %copy-start.6 = (bf16[1,512,4096]{2,1,0:T(8,128)(2,1)S(1)}, bf16[1,512,4096]{2,1,0:T(8,128)(2,1)}, u32[]{:S(2)}) copy-start(bf16[1,512,4096]{2,1,0:T(8,128)(2,1)} %param.10) | copy-start | bytes 12582916
  7.7 5.7 %copy-start.14 = (f32[512,128]{1,0:T(8,128)}, f32[512,128]{1,0:T(8,128)S(1)}, u32[]{:S(2)}) copy-start(f32[512,128]{1,0:T(8,128)S(1)} %get-tuple-element.214.sine) | copy-start | bytes 786436
  11.8 32.5 %collective-permute-start.5 = (bf16[384,1024]{1,0:T(8,128)(2,1)}, bf16[384,1024]{1,0:T(8,128)(2,1)}, u32[]{:S(2)}, u32[]{:S(2)}) collective-permute-start(bf16[384,1024]{1,0:T(8,128)(2,1)} %add_convert_fusion), channel_id=1, source_target_pairs={{0,16},{8,24},{16,0},{24,8},{1,17},{9,25},{17,1},{25,9},{2,18},{10... | collective-permute-start | bytes 2359304 | tf_op jit(solution)/shard_map/ppermute | solution.py:463
  27.3 4.3 %copy-start.9 = (bf16[512,1024]{1,0:T(8,128)(2,1)}, bf16[512,1024]{1,0:T(8,128)(2,1)S(1)}, u32[]{:S(2)}) copy-start(bf16[512,1024]{1,0:T(8,128)(2,1)S(1)} %get-tuple-element.160) | copy-start | bytes 3145732
  27.3 4.8 %copy-start.12 = (bf16[512,1024]{1,0:T(8,128)(2,1)}, bf16[512,1024]{1,0:T(8,128)(2,1)S(1)}, u32[]{:S(2)}) copy-start(bf16[512,1024]{1,0:T(8,128)(2,1)S(1)} %get-tuple-element.101.kv_grad) | copy-start | bytes 3145732
  28.3 45.4 %copy-start.2 = (bf16[512,1024]{1,0:T(8,128)(2,1)}, bf16[512,1024]{1,0:T(8,128)(2,1)S(1)}, u32[]{:S(2)}) copy-start(bf16[512,1024]{1,0:T(8,128)(2,1)S(1)} %collective-permute-done.2.refs_2_.refs_4_) | copy-start | bytes 3145732
  28.3 45.3 %copy-start.3 = (bf16[512,1024]{1,0:T(8,128)(2,1)}, bf16[512,1024]{1,0:T(8,128)(2,1)S(1)}, u32[]{:S(2)}) copy-start(bf16[512,1024]{1,0:T(8,128)(2,1)S(1)} %collective-permute-done.1.refs_1_.refs_3_) | copy-start | bytes 3145732
  30.1 13.7 %collective-permute-start.4 = (bf16[256,1024]{1,0:T(8,128)(2,1)}, bf16[256,1024]{1,0:T(8,128)(2,1)}, u32[]{:S(2)}, u32[]{:S(2)}) collective-permute-start(bf16[256,1024]{1,0:T(8,128)(2,1)} %slice.128), channel_id=1, source_target_pairs={{2,0},{4,2},{6,4},{7,6},{5,7},{3,5},{1,3},{0,1},{10,8},{12,10},{14... | collective-permute-start | bytes 1572872 | tf_op jit(solution)/shard_map/ppermute | solution.py:47
  31.6 12.7 %collective-permute-start.3 = (bf16[256,1024]{1,0:T(8,128)(2,1)}, bf16[256,1024]{1,0:T(8,128)(2,1)}, u32[]{:S(2)}, u32[]{:S(2)}) collective-permute-start(bf16[256,1024]{1,0:T(8,128)(2,1)} %slice.127), channel_id=1, source_target_pairs={{0,2},{2,4},{4,6},{6,7},{7,5},{5,3},{3,1},{1,0},{8,10},{10,12},{12... | collective-permute-start | bytes 1572872 | tf_op jit(solution)/shard_map/ppermute | solution.py:44
  32.2 26.2 %collective-permute-start.10 = (bf16[512,1024]{1,0:T(8,128)(2,1)S(1)}, bf16[512,1024]{1,0:T(8,128)(2,1)}, u32[]{:S(2)}, u32[]{:S(2)}) collective-permute-start(bf16[512,1024]{1,0:T(8,128)(2,1)S(1)} %scale_rows.1.refs_0_.refs_2_), channel_id=1, source_target_pairs={{2,3},{3,2},{4,5},{5,4},{10,11},{11,10},{12,13},{13,12},{18,19},{1... | collective-permute-start | bytes 3145736 | tf_op jit(solution)/shard_map/ppermute | solution.py:56
  36.7 11.3 %copy-start.10 = (bf16[512,1024]{1,0:T(8,128)(2,1)S(1)}, bf16[512,1024]{1,0:T(8,128)(2,1)}, u32[]{:S(2)}) copy-start(bf16[512,1024]{1,0:T(8,128)(2,1)} %copy-done.9) | copy-start | bytes 3145732
  46.0 16.2 %collective-permute-start.9 = (bf16[256,1024]{1,0:T(8,128)(2,1)}, bf16[256,1024]{1,0:T(8,128)(2,1)}, u32[]{:S(2)}, u32[]{:S(2)}) collective-permute-start(bf16[256,1024]{1,0:T(8,128)(2,1)} %slice.130), channel_id=1, source_target_pairs={{2,0},{4,2},{6,4},{7,6},{5,7},{3,5},{1,3},{0,1},{10,8},{12,10},{14... | collective-permute-start | bytes 1572872 | tf_op jit(solution)/shard_map/ppermute | solution.py:47
  47.5 15.2 %collective-permute-start.8 = (bf16[256,1024]{1,0:T(8,128)(2,1)}, bf16[256,1024]{1,0:T(8,128)(2,1)}, u32[]{:S(2)}, u32[]{:S(2)}) collective-permute-start(bf16[256,1024]{1,0:T(8,128)(2,1)} %slice.129), channel_id=1, source_target_pairs={{0,2},{2,4},{4,6},{6,7},{7,5},{5,3},{3,1},{1,0},{8,10},{10,12},{12... | collective-permute-start | bytes 1572872 | tf_op jit(solution)/shard_map/ppermute | solution.py:44
  50.3 19.1 %collective-permute-start.7 = (bf16[256,1024]{1,0:T(8,128)(2,1)}, bf16[256,1024]{1,0:T(8,128)(2,1)}, u32[]{:S(2)}, u32[]{:S(2)}) collective-permute-start(bf16[256,1024]{1,0:T(8,128)(2,1)} %get-tuple-element.208), channel_id=1, source_target_pairs={{2,0},{4,2},{6,4},{7,6},{5,7},{3,5},{1,3},{0,1},{10,8},{12,10},{14... | collective-permute-start | bytes 1572872 | tf_op jit(solution)/shard_map/ppermute | solution.py:47
  51.6 10.5 %copy-start.28 = (s32[8]{0:T(128)S(1)}, s32[8]{0:T(128)}, u32[]{:S(2)}) copy-start(s32[8]{0:T(128)} %constant.107.clone) | copy-start | bytes 100
  51.6 18.5 %collective-permute-start.6 = (bf16[256,1024]{1,0:T(8,128)(2,1)}, bf16[256,1024]{1,0:T(8,128)(2,1)}, u32[]{:S(2)}, u32[]{:S(2)}) collective-permute-start(bf16[256,1024]{1,0:T(8,128)(2,1)} %get-tuple-element.209), channel_id=1, source_target_pairs={{0,2},{2,4},{4,6},{6,7},{7,5},{5,3},{3,1},{1,0},{8,10},{10,12},{12... | collective-permute-start | bytes 1572872 | tf_op jit(solution)/shard_map/ppermute | solution.py:44
  58.3 24.8 %collective-permute-start.13 = (bf16[512,1024]{1,0:T(8,128)(2,1)}, bf16[512,1024]{1,0:T(8,128)(2,1)}, u32[]{:S(2)}, u32[]{:S(2)}) collective-permute-start(bf16[512,1024]{1,0:T(8,128)(2,1)} %broadcast_select_fusion), channel_id=1, source_target_pairs={{2,3},{3,2},{4,5},{5,4},{10,11},{11,10},{12,13},{13,12},{18,19},{1... | collective-permute-start | bytes 3145736 | tf_op jit(solution)/shard_map/ppermute | solution.py:56
  62.1 11.6 %copy-start.13 = (bf16[512,1024]{1,0:T(8,128)(2,1)S(1)}, bf16[512,1024]{1,0:T(8,128)(2,1)}, u32[]{:S(2)}) copy-start(bf16[512,1024]{1,0:T(8,128)(2,1)} %copy-done.12) | copy-start | bytes 3145732
  62.1 11.6 %copy-start.17 = (f32[512,128]{1,0:T(8,128)S(1)}, f32[512,128]{1,0:T(8,128)}, u32[]{:S(2)}) copy-start(f32[512,128]{1,0:T(8,128)} %copy-done.16) | copy-start | bytes 786436
  71.6 20.0 %collective-permute-start.12 = (bf16[256,1024]{1,0:T(8,128)(2,1)S(1)}, bf16[256,1024]{1,0:T(8,128)(2,1)S(1)}, u32[]{:S(2)}, u32[]{:S(2)}) collective-permute-start(bf16[256,1024]{1,0:T(8,128)(2,1)S(1)} %get-tuple-element.206), channel_id=1, source_target_pairs={{2,0},{4,2},{6,4},{7,6},{5,7},{3,5},{1,3},{0,1},{10,8},{12,10},{14... | collective-permute-start | bytes 1572872 | tf_op jit(solution)/shard_map/ppermute | solution.py:47
  73.1 18.5 %collective-permute-start.11 = (bf16[256,1024]{1,0:T(8,128)(2,1)S(1)}, bf16[256,1024]{1,0:T(8,128)(2,1)S(1)}, u32[]{:S(2)}, u32[]{:S(2)}) collective-permute-start(bf16[256,1024]{1,0:T(8,128)(2,1)S(1)} %get-tuple-element.207), channel_id=1, source_target_pairs={{0,2},{2,4},{4,6},{6,7},{7,5},{5,3},{3,1},{1,0},{8,10},{10,12},{12... | collective-permute-start | bytes 1572872 | tf_op jit(solution)/shard_map/ppermute | solution.py:44
  75.9 7.3 %copy-start.11 = (bf16[512,1024]{1,0:T(8,128)(2,1)S(1)}, bf16[512,1024]{1,0:T(8,128)(2,1)}, u32[]{:S(2)}) copy-start(bf16[512,1024]{1,0:T(8,128)(2,1)} %copy-done.9) | copy-start | bytes 3145732
  83.2 32.5 %collective-permute-start.18 = (bf16[512,1024]{1,0:T(8,128)(2,1)S(1)}, bf16[512,1024]{1,0:T(8,128)(2,1)S(1)}, u32[]{:S(2)}, u32[]{:S(2)}) collective-permute-start(bf16[512,1024]{1,0:T(8,128)(2,1)S(1)} %copy-done.11), channel_id=1, source_target_pairs={{2,3},{3,2},{4,5},{5,4},{10,11},{11,10},{12,13},{13,12},{18,19},{1... | collective-permute-start | bytes 3145736 | tf_op jit(solution)/shard_map/ppermute | solution.py:56
  89.5 14.9 %collective-permute-start.15 = (bf16[256,1024]{1,0:T(8,128)(2,1)S(1)}, bf16[256,1024]{1,0:T(8,128)(2,1)S(1)}, u32[]{:S(2)}, u32[]{:S(2)}) collective-permute-start(bf16[256,1024]{1,0:T(8,128)(2,1)S(1)} %get-tuple-element.203), channel_id=1, source_target_pairs={{2,0},{4,2},{6,4},{7,6},{5,7},{3,5},{1,3},{0,1},{10,8},{12,10},{14... | collective-permute-start | bytes 1572872 | tf_op jit(solution)/shard_map/ppermute | solution.py:47
  89.5 14.9 %collective-permute-start.14 = (bf16[256,1024]{1,0:T(8,128)(2,1)S(1)}, bf16[256,1024]{1,0:T(8,128)(2,1)S(1)}, u32[]{:S(2)}, u32[]{:S(2)}) collective-permute-start(bf16[256,1024]{1,0:T(8,128)(2,1)S(1)} %get-tuple-element.204), channel_id=1, source_target_pairs={{0,2},{2,4},{4,6},{6,7},{7,5},{5,3},{3,1},{1,0},{8,10},{10,12},{12... | collective-permute-start | bytes 1572872 | tf_op jit(solution)/shard_map/ppermute | solution.py:44
  93.5 22.1 %collective-permute-start.17 = (bf16[256,1024]{1,0:T(8,128)(2,1)S(1)}, bf16[256,1024]{1,0:T(8,128)(2,1)S(1)}, u32[]{:S(2)}, u32[]{:S(2)}) collective-permute-start(bf16[256,1024]{1,0:T(8,128)(2,1)S(1)} %get-tuple-element.201), channel_id=1, source_target_pairs={{2,0},{4,2},{6,4},{7,6},{5,7},{3,5},{1,3},{0,1},{10,8},{12,10},{14... | collective-permute-start | bytes 1572872 | tf_op jit(solution)/shard_map/ppermute | solution.py:47
  93.6 22.1 %collective-permute-start.16 = (bf16[256,1024]{1,0:T(8,128)(2,1)S(1)}, bf16[256,1024]{1,0:T(8,128)(2,1)S(1)}, u32[]{:S(2)}, u32[]{:S(2)}) collective-permute-start(bf16[256,1024]{1,0:T(8,128)(2,1)S(1)} %get-tuple-element.202), channel_id=1, source_target_pairs={{0,2},{2,4},{4,6},{6,7},{7,5},{5,3},{3,1},{1,0},{8,10},{10,12},{12... | collective-permute-start | bytes 1572872 | tf_op jit(solution)/shard_map/ppermute | solution.py:44
  106.5 20.3 %collective-permute-start.22 = (bf16[256,1024]{1,0:T(8,128)(2,1)S(1)}, bf16[256,1024]{1,0:T(8,128)(2,1)S(1)}, u32[]{:S(2)}, u32[]{:S(2)}) collective-permute-start(bf16[256,1024]{1,0:T(8,128)(2,1)S(1)} %get-tuple-element.199), channel_id=1, source_target_pairs={{2,0},{4,2},{6,4},{7,6},{5,7},{3,5},{1,3},{0,1},{10,8},{12,10},{14... | collective-permute-start | bytes 1572872 | tf_op jit(solution)/shard_map/ppermute | solution.py:47
  106.7 13.3 %copy-start.22 = (f32[384,1024]{1,0:T(8,128)S(1)}, f32[384,1024]{1,0:T(8,128)}, u32[]{:S(2)}) copy-start(f32[384,1024]{1,0:T(8,128)} %param.16) | copy-start | bytes 4718596
  106.7 13.3 %copy-start.23 = (f32[384,1024]{1,0:T(8,128)S(1)}, f32[384,1024]{1,0:T(8,128)}, u32[]{:S(2)}) copy-start(f32[384,1024]{1,0:T(8,128)} %param.15) | copy-start | bytes 4718596
  106.7 13.3 %copy-start.24 = (bf16[1,384,1024]{2,1,0:T(8,128)(2,1)S(1)}, bf16[1,384,1024]{2,1,0:T(8,128)(2,1)}, u32[]{:S(2)}) copy-start(bf16[1,384,1024]{2,1,0:T(8,128)(2,1)} %param.17) | copy-start | bytes 2359300
  106.7 20.2 %collective-permute-start.21 = (bf16[256,1024]{1,0:T(8,128)(2,1)S(1)}, bf16[256,1024]{1,0:T(8,128)(2,1)S(1)}, u32[]{:S(2)}, u32[]{:S(2)}) collective-permute-start(bf16[256,1024]{1,0:T(8,128)(2,1)S(1)} %get-tuple-element.200), channel_id=1, source_target_pairs={{0,2},{2,4},{4,6},{6,7},{7,5},{5,3},{3,1},{1,0},{8,10},{10,12},{12... | collective-permute-start | bytes 1572872 | tf_op jit(solution)/shard_map/ppermute | solution.py:44
  117.9 20.2 %collective-permute-start.20 = (bf16[256,1024]{1,0:T(8,128)(2,1)S(1)}, bf16[256,1024]{1,0:T(8,128)(2,1)S(1)}, u32[]{:S(2)}, u32[]{:S(2)}) collective-permute-start(bf16[256,1024]{1,0:T(8,128)(2,1)S(1)} %get-tuple-element.197), channel_id=1, source_target_pairs={{2,0},{4,2},{6,4},{7,6},{5,7},{3,5},{1,3},{0,1},{10,8},{12,10},{14... | collective-permute-start | bytes 1572872 | tf_op jit(solution)/shard_map/ppermute | solution.py:47
  118.1 20.1 %collective-permute-start.19 = (bf16[256,1024]{1,0:T(8,128)(2,1)S(1)}, bf16[256,1024]{1,0:T(8,128)(2,1)S(1)}, u32[]{:S(2)}, u32[]{:S(2)}) collective-permute-start(bf16[256,1024]{1,0:T(8,128)(2,1)S(1)} %get-tuple-element.198), channel_id=1, source_target_pairs={{0,2},{2,4},{4,6},{6,7},{7,5},{5,3},{3,1},{1,0},{8,10},{10,12},{12... | collective-permute-start | bytes 1572872 | tf_op jit(solution)/shard_map/ppermute | solution.py:44
  128.9 29.6 %collective-permute-start.27 = (bf16[256,1024]{1,0:T(8,128)(2,1)S(1)}, bf16[256,1024]{1,0:T(8,128)(2,1)S(1)}, u32[]{:S(2)}, u32[]{:S(2)}) collective-permute-start(bf16[256,1024]{1,0:T(8,128)(2,1)S(1)} %get-tuple-element.195), channel_id=1, source_target_pairs={{2,0},{4,2},{6,4},{7,6},{5,7},{3,5},{1,3},{0,1},{10,8},{12,10},{14... | collective-permute-start | bytes 1572872 | tf_op jit(solution)/shard_map/ppermute | solution.py:47
  129.2 29.3 %collective-permute-start.26 = (bf16[256,1024]{1,0:T(8,128)(2,1)S(1)}, bf16[256,1024]{1,0:T(8,128)(2,1)S(1)}, u32[]{:S(2)}, u32[]{:S(2)}) collective-permute-start(bf16[256,1024]{1,0:T(8,128)(2,1)S(1)} %get-tuple-element.196), channel_id=1, source_target_pairs={{0,2},{2,4},{4,6},{6,7},{7,5},{5,3},{3,1},{1,0},{8,10},{10,12},{12... | collective-permute-start | bytes 1572872 | tf_op jit(solution)/shard_map/ppermute | solution.py:44
  131.0 27.5 %collective-permute-start.25 = (bf16[512,1024]{1,0:T(8,128)(2,1)S(1)}, bf16[512,1024]{1,0:T(8,128)(2,1)S(1)}, u32[]{:S(2)}, u32[]{:S(2)}) collective-permute-start(bf16[512,1024]{1,0:T(8,128)(2,1)S(1)} %fusion.10), channel_id=1, source_target_pairs={{2,3},{3,2},{4,5},{5,4},{10,11},{11,10},{12,13},{13,12},{18,19},{1... | collective-permute-start | bytes 3145736 | tf_op jit(solution)/shard_map/ppermute | solution.py:56
  138.2 4.2 %copy-start.15 = (f32[512,128]{1,0:T(8,128)S(1)}, f32[512,128]{1,0:T(8,128)}, u32[]{:S(2)}) copy-start(f32[512,128]{1,0:T(8,128)} %copy-done.14) | copy-start | bytes 786436
  140.2 18.3 %collective-permute-start.24 = (bf16[256,1024]{1,0:T(8,128)(2,1)S(1)}, bf16[256,1024]{1,0:T(8,128)(2,1)S(1)}, u32[]{:S(2)}, u32[]{:S(2)}) collective-permute-start(bf16[256,1024]{1,0:T(8,128)(2,1)S(1)} %get-tuple-element.193), channel_id=1, source_target_pairs={{2,0},{4,2},{6,4},{7,6},{5,7},{3,5},{1,3},{0,1},{10,8},{12,10},{14... | collective-permute-start | bytes 1572872 | tf_op jit(solution)/shard_map/ppermute | solution.py:47
  140.5 18.1 %copy-start.1 = (bf16[1,512,1024]{2,1,0:T(8,128)(2,1)S(1)}, bf16[1,512,1024]{2,1,0:T(8,128)(2,1)}, u32[]{:S(2)}) copy-start(bf16[1,512,1024]{2,1,0:T(8,128)(2,1)} %param.12) | copy-start | bytes 3145732
  140.5 18.1 %copy-start.5 = (f32[512,1024]{1,0:T(8,128)S(1)}, f32[512,1024]{1,0:T(8,128)}, u32[]{:S(2)}) copy-start(f32[512,1024]{1,0:T(8,128)} %copy-done.4) | copy-start | bytes 6291460
  140.5 18.1 %copy-start.19 = (bf16[1,512]{1,0:T(2,128)(2,1)S(1)}, bf16[1,512]{1,0:T(2,128)(2,1)}, u32[]{:S(2)}) copy-start(bf16[1,512]{1,0:T(2,128)(2,1)} %gain.5) | copy-start | bytes 3076
  140.5 18.0 %collective-permute-start.23 = (bf16[256,1024]{1,0:T(8,128)(2,1)S(1)}, bf16[256,1024]{1,0:T(8,128)(2,1)S(1)}, u32[]{:S(2)}, u32[]{:S(2)}) collective-permute-start(bf16[256,1024]{1,0:T(8,128)(2,1)S(1)} %get-tuple-element.194), channel_id=1, source_target_pairs={{0,2},{2,4},{4,6},{6,7},{7,5},{5,3},{3,1},{1,0},{8,10},{10,12},{12... | collective-permute-start | bytes 1572872 | tf_op jit(solution)/shard_map/ppermute | solution.py:44
  (10 other events, 16.9 us)
